TPU v7x, 32 devices: a whole 2x2x4 slice. The times are simulated.
32 devices in a mesh: tm: 8 (over z, x), rows: 4 (over y, core).
Axes of the slice: x: 2, y: 2, z: 4, core: 2. Of those that a mesh axis runs over, the one named last changes fastest.
Arguments:
- gains: float32 [8, 1024, 1024], P('tm', 'rows'), may hold values from -0.1875 to 0.1875
- spreads: float32 [8, 1024, 1024], P('tm', 'rows'), may hold values from -1 to 6, as said below
- offsets: float32 [8, 1024, 4096], P('tm', None, 'rows'), may hold values from -6 to 6
Outputs:
- composed_gain: float32 [8, 1024, 1024], P('tm', 'rows')
- composed_spread: float32 [8, 1024, 1024], P('tm', 'rows')
- composed_offset: float32 [8, 1024, 4096], P('tm', None, 'rows')
Inputs may be any that keep to these rules, and one draw needn't show every extreme that they name: `spreads`: each time step's matrix is symmetric.
All inputs are finite; a program needn't handle non-finite values.
Results may differ from a plain program's by a relative error of at most 0.0084.
Values may be sent and summed in bfloat16 or wider, within the bound.
No kernel may reach another device: no remote copies, remote signals or barrier semaphores. Data moves between devices by JAX's collectives and lax.ppermute only.
A program may use at most 64 MiB of HBM per device.

v0:
```python
import jax
import jax.numpy as jnp
from jax import lax
from jax.sharding import PartitionSpec as P

LEVELS = 3


def shifted(value, axis, steps):
    count = lax.axis_size(axis)
    first, last = (max(0, -steps), min(count, count - steps))
    return lax.ppermute(value, axis, [(source, source + steps) for source in range(first, last)])


def per_device(gains, spreads, offsets):
    gain = gains[0]
    spread = spreads[0]
    offset = offsets[0]
    size_d = gain.shape[1]
    identity = jnp.eye(size_d, dtype=jnp.bfloat16)
    for section_number in range(LEVELS):
        distance = 2**section_number
        beyond = lax.axis_index("tm") + distance >= lax.axis_size("tm")
        own_gain = gain.astype(jnp.bfloat16)
        own_spread = spread.astype(jnp.bfloat16)
        own_offset = offset.astype(jnp.bfloat16)
        own_full, spread_full = (
            lax.all_gather(own_gain, "rows", axis=0, tiled=True),
            lax.all_gather(own_spread, "rows", axis=0, tiled=True),
        )
        far_full, far_spread_full, far_offset = shifted(
            (own_full, spread_full, own_offset), "tm", -distance
        )
        far_full = jnp.where(beyond, identity, far_full)
        row_start = lax.axis_index("rows") * gain.shape[0]
        own_rows = lax.dynamic_slice_in_dim(own_full, row_start, gain.shape[0], 0)
        middle = jnp.dot(own_rows, far_spread_full, preferred_element_type=jnp.float32).astype(
            jnp.bfloat16
        )
        new_gain = jnp.dot(own_rows, far_full, preferred_element_type=jnp.float32)
        new_spread = (
            lax.dot_general(
                middle, own_full, (((1,), (1,)), ((), ())), preferred_element_type=jnp.float32
            )
            + spread
        )
        new_offset = jnp.dot(own_full, far_offset, preferred_element_type=jnp.float32) + offset
        gain, spread, offset = (new_gain, new_spread, new_offset)
    return (gain[None], spread[None], offset[None])


def solution(mesh):
    return jax.shard_map(
        per_device,
        mesh=mesh,
        in_specs=(P("tm", "rows", None), P("tm", "rows", None), P("tm", None, "rows")),
        out_specs=(P("tm", "rows", None), P("tm", "rows", None), P("tm", None, "rows")),
        check_vma=False,
    )
```

profile of v0, /device:TPU:16, one launch (start us, length us, event | category | flops | bytes accessed | tf_op | source)
XLA Modules:
  0.0 611.7 jit_solution(8365376403876940483)
XLA Ops:
  7.2 0.0 all-gather.12.cloned.1.call-start
  7.2 2.2 bitcast_convert_fusion.1
  9.5 0.0 all-gather.12.cloned.1.call-update
  9.5 0.0 all-gather.18.cloned.1.call-start
  9.5 0.9 convert_element_type.46
  10.4 0.0 all-gather.18.cloned.1.call-update
  10.4 0.0 all-gather.14.cloned.1.call-start
  10.5 23.4 %all-gather.12.cloned.1.call-done = bf16[1024,1024]{1,0:T(8,128)(2,1)} async-done(((bf16[256,1024]{1,0:T(8,128)(2,1)}), bf16[1024,1024]{1,0:T(8,128)(2,1)}) %all-gather.12.cloned.1.call-update) | async-done | bytes 2097168 | tf_op jit(solution)/shard_map/all_gather | solution.py:29
  33.8 3.3 collective-permute-start.3
  37.2 21.4 %all-gather.18.cloned.1.call-done = bf16[1,1024,1024]{2,1,0:T(8,128)(2,1)} async-done(((bf16[1,256,1024]{2,1,0:T(8,128)(2,1)}), bf16[1,1024,1024]{2,1,0:T(8,128)(2,1)}) %all-gather.18.cloned.1.call-update) | async-done | bytes 2097168 | tf_op jit(solution)/shard_map/all_gather | solution.py:28
  58.6 25.2 %collective-permute-done.3 = bf16[1024,1024]{1,0:T(8,128)(2,1)} collective-permute-done((bf16[1024,1024]{1,0:T(8,128)(2,1)}, bf16[1024,1024]{1,0:T(8,128)(2,1)}, u32[]{:S(2)}, u32[]{:S(2)}) %collective-permute-start.3) | collective-permute-done | bytes 2097184 | tf_op jit(solution)/shard_map/ppermute | solution.py:12
  83.8 4.8 fusion.46
  88.6 0.0 all-gather.14.cloned.1.call-update
  88.6 0.0 all-gather.8.cloned.1.call-start
  88.7 4.3 collective-permute-start
  93.0 45.3 %collective-permute-done = bf16[1024,1024]{1,0:T(8,128)(2,1)} collective-permute-done((bf16[1024,1024]{1,0:T(8,128)(2,1)S(1)}, bf16[1024,1024]{1,0:T(8,128)(2,1)}, u32[]{:S(2)}, u32[]{:S(2)}) %collective-permute-start) | collective-permute-done | bytes 2097184 | tf_op jit(solution)/shard_map/ppermute | solution.py:12
  138.3 3.1 fusion.20
  141.4 0.0 all-gather.8.cloned.1.call-update
  141.4 0.0 all-gather.16.cloned.1.call-start
  141.4 0.0 all-gather.14.cloned.1.call-done
  141.5 2.5 collective-permute-start.4
  143.9 2.5 bitcast_convert_fusion
  146.5 4.5 collective-permute-start.6
  151.0 13.4 %all-gather.8.cloned.1.call-done = bf16[1024,1024]{1,0:T(8,128)(2,1)} async-done(((bf16[256,1024]{1,0:T(8,128)(2,1)}), bf16[1024,1024]{1,0:T(8,128)(2,1)}) %all-gather.8.cloned.1.call-update) | async-done | bytes 2097168 | tf_op jit(solution)/shard_map/all_gather | solution.py:28
  164.4 27.9 %collective-permute-done.4 = bf16[1024,1024]{1,0:T(8,128)(2,1)} collective-permute-done((bf16[1024,1024]{1,0:T(8,128)(2,1)}, bf16[1024,1024]{1,0:T(8,128)(2,1)}, u32[]{:S(2)}, u32[]{:S(2)}) %collective-permute-start.4) | collective-permute-done | bytes 2097184 | tf_op jit(solution)/shard_map/ppermute | solution.py:12
  192.3 4.7 fusion.49
  196.9 0.0 all-gather.16.cloned.1.call-update
  197.0 0.0 all-gather.10.cloned.1.call-start
  197.0 2.5 collective-permute-start.1
  199.5 35.7 %collective-permute-done.6 = bf16[1024,1024]{1,0:T(8,128)(2,1)} collective-permute-done((bf16[1024,1024]{1,0:T(8,128)(2,1)S(1)}, bf16[1024,1024]{1,0:T(8,128)(2,1)}, u32[]{:S(2)}, u32[]{:S(2)}) %collective-permute-start.6) | collective-permute-done | bytes 2097184 | tf_op jit(solution)/shard_map/ppermute | solution.py:12
  235.2 8.7 %fusion.52 = (bf16[1024,1024]{1,0:T(8,128)(2,1)}, f32[1024,1024]{1,0:T(8,128)}) fusion(f32[1,1024,1024]{2,1,0:T(8,128)} %param.5, bf16[1024,1024]{1,0:T(8,128)(2,1)} %collective-permute-done.6, bf16[1,1024,1024]{2,1,0:T(8,128)(2,1)} %all-gather.18.cloned.1.call-done), kind=kOutput, calls=%fused_computation.44 | convolution fusion | flops 2149580800 | bytes 14680064 | tf_op jit(solution)/shard_map/dot_general | solution.py:47
  243.8 2.4 collective-permute-start.7
  246.3 35.8 %collective-permute-done.1 = bf16[1024,1024]{1,0:T(8,128)(2,1)} collective-permute-done((bf16[1024,1024]{1,0:T(8,128)(2,1)}, bf16[1024,1024]{1,0:T(8,128)(2,1)}, u32[]{:S(2)}, u32[]{:S(2)}) %collective-permute-start.1) | collective-permute-done | bytes 2097184 | tf_op jit(solution)/shard_map/ppermute | solution.py:12
  282.1 3.1 fusion.17
  285.2 0.0 all-gather.10.cloned.1.call-update
  285.3 39.6 %collective-permute-done.7 = bf16[1024,1024]{1,0:T(8,128)(2,1)} collective-permute-done((bf16[1024,1024]{1,0:T(8,128)(2,1)}, bf16[1024,1024]{1,0:T(8,128)(2,1)}, u32[]{:S(2)}, u32[]{:S(2)}) %collective-permute-start.7) | collective-permute-done | bytes 2097184 | tf_op jit(solution)/shard_map/ppermute | solution.py:12
  324.9 7.9 %fusion.53 = (bf16[1024,1024]{1,0:T(8,128)(2,1)}, f32[1024,1024]{1,0:T(8,128)}) fusion(f32[1024,1024]{1,0:T(8,128)} %get-tuple-element.8, bf16[1024,1024]{1,0:T(8,128)(2,1)S(1)} %copy-done.3, bf16[1024,1024]{1,0:T(8,128)(2,1)} %collective-permute-done.7), kind=kOutput, calls=%fused_computation.45 | convolution fusion | flops 2149580800 | bytes 14680064 | tf_op jit(solution)/shard_map/dot_general | solution.py:47
  332.8 2.5 collective-permute-start.8
  335.3 0.0 all-gather.16.cloned.1.call-done
  335.4 2.7 collective-permute-start.5
  338.1 2.7 collective-permute-start.2
  340.7 173.6 %collective-permute-done.8 = bf16[1024,1024]{1,0:T(8,128)(2,1)S(1)} collective-permute-done((bf16[1024,1024]{1,0:T(8,128)(2,1)}, bf16[1024,1024]{1,0:T(8,128)(2,1)S(1)}, u32[]{:S(2)}, u32[]{:S(2)}) %collective-permute-start.8) | collective-permute-done | bytes 2097184 | tf_op jit(solution)/shard_map/ppermute | solution.py:12
  514.3 1.4 copy-done.5
  515.7 7.9 %add_bitcast_fusion = f32[1,1024,1024]{2,1,0:T(8,128)} fusion(f32[1024,1024]{1,0:T(8,128)} %get-tuple-element.10, bf16[1024,1024]{1,0:T(8,128)(2,1)} %all-gather.10.cloned.1.call-done, bf16[1024,1024]{1,0:T(8,128)(2,1)} %copy-done.5), kind=kOutput, calls=%fused_computation.2 | convolution fusion | flops 2148532224 | bytes 12582912 | tf_op jit(solution)/shard_map/dot_general | solution.py:47
  523.7 35.6 %collective-permute-done.5 = bf16[1024,1024]{1,0:T(8,128)(2,1)} collective-permute-done((bf16[1024,1024]{1,0:T(8,128)(2,1)}, bf16[1024,1024]{1,0:T(8,128)(2,1)}, u32[]{:S(2)}, u32[]{:S(2)}) %collective-permute-start.5) | collective-permute-done | bytes 2097184 | tf_op jit(solution)/shard_map/ppermute | solution.py:12
  559.3 3.8 fusion.16
  563.1 40.0 %collective-permute-done.2 = bf16[1024,1024]{1,0:T(8,128)(2,1)} collective-permute-done((bf16[1024,1024]{1,0:T(8,128)(2,1)}, bf16[1024,1024]{1,0:T(8,128)(2,1)}, u32[]{:S(2)}, u32[]{:S(2)}) %collective-permute-start.2) | collective-permute-done | bytes 2097184 | tf_op jit(solution)/shard_map/ppermute | solution.py:12
  603.1 1.7 fusion.13
  (12 shorter events, 0.0 us)
Async XLA Ops:
  7.2 76.7 %copy-start.1 = (f32[1,256,1024]{2,1,0:T(8,128)S(1)}, f32[1,256,1024]{2,1,0:T(8,128)}, u32[]{:S(2)}) copy-start(f32[1,256,1024]{2,1,0:T(8,128)} %param.4) | copy-start | bytes 3145732
  7.2 2.4 copy-start
  7.2 26.7 %all-gather.12.cloned.1.call-start = ((), (), s32[]{:S(2)}) async-start(), calls=%async_computation.2 | async-start | bytes 2621440 | tf_op jit(solution)/shard_map/all_gather | solution.py:29
  9.5 49.1 %all-gather.18.cloned.1.call-start = ((), (), s32[]{:S(2)}) async-start(), calls=%async_computation.5 | async-start | bytes 2621440 | tf_op jit(solution)/shard_map/all_gather | solution.py:28
  10.4 131.0 %all-gather.14.cloned.1.call-start = ((), (), s32[]{:S(2)}) async-start(), calls=%async_computation.3 | async-start | bytes 2621440 | tf_op jit(solution)/shard_map/all_gather | solution.py:29
  33.8 50.0 %collective-permute-start.3 = (bf16[1024,1024]{1,0:T(8,128)(2,1)}, bf16[1024,1024]{1,0:T(8,128)(2,1)}, u32[]{:S(2)}, u32[]{:S(2)}) collective-permute-start(bf16[1024,1024]{1,0:T(8,128)(2,1)} %all-gather.12.cloned.1.call-done), channel_id=1, source_target_pairs={{4,0},{8,4},{12,8},{16,12},{20,16},{24,20},{28,24},{5,1},{9,5},{13... | collective-permute-start | bytes 6291464 | tf_op jit(solution)/shard_map/ppermute | solution.py:12
  58.6 30.1 %copy-start.2 = (bf16[1,1024,1024]{2,1,0:T(8,128)(2,1)S(1)}, bf16[1,1024,1024]{2,1,0:T(8,128)(2,1)}, u32[]{:S(2)}) copy-start(bf16[1,1024,1024]{2,1,0:T(8,128)(2,1)} %all-gather.18.cloned.1.call-done) | copy-start | bytes 6291460
  88.6 75.8 %all-gather.8.cloned.1.call-start = ((), (), s32[]{:S(2)}) async-start(), calls=%async_computation | async-start | bytes 2621440 | tf_op jit(solution)/shard_map/all_gather | solution.py:28
  88.7 49.6 %collective-permute-start = (bf16[1024,1024]{1,0:T(8,128)(2,1)S(1)}, bf16[1024,1024]{1,0:T(8,128)(2,1)}, u32[]{:S(2)}, u32[]{:S(2)}) collective-permute-start(bf16[1024,1024]{1,0:T(8,128)(2,1)S(1)} %bitcast.39), channel_id=1, source_target_pairs={{4,0},{8,4},{12,8},{16,12},{20,16},{24,20},{28,24},{5,1},{9,5},{13... | collective-permute-start | bytes 6291464 | tf_op jit(solution)/shard_map/ppermute | solution.py:12
  141.4 193.9 %all-gather.16.cloned.1.call-start = ((), (), s32[]{:S(2)}) async-start(), calls=%async_computation.4 | async-start | bytes 2621440 | tf_op jit(solution)/shard_map/all_gather | solution.py:29
  141.5 50.8 %collective-permute-start.4 = (bf16[1024,1024]{1,0:T(8,128)(2,1)}, bf16[1024,1024]{1,0:T(8,128)(2,1)}, u32[]{:S(2)}, u32[]{:S(2)}) collective-permute-start(bf16[1024,1024]{1,0:T(8,128)(2,1)} %all-gather.14.cloned.1.call-done), channel_id=1, source_target_pairs={{8,0},{12,4},{16,8},{20,12},{24,16},{28,20},{9,1},{13,5},{17,9},{2... | collective-permute-start | bytes 6291464 | tf_op jit(solution)/shard_map/ppermute | solution.py:12
  146.5 88.7 %collective-permute-start.6 = (bf16[1024,1024]{1,0:T(8,128)(2,1)S(1)}, bf16[1024,1024]{1,0:T(8,128)(2,1)}, u32[]{:S(2)}, u32[]{:S(2)}) collective-permute-start(bf16[1024,1024]{1,0:T(8,128)(2,1)S(1)} %bitcast_convert_fusion), channel_id=1, source_target_pairs={{4,0},{8,4},{12,8},{16,12},{20,16},{24,20},{28,24},{5,1},{9,5},{13... | collective-permute-start | bytes 6291464 | tf_op jit(solution)/shard_map/ppermute | solution.py:12
  197.0 141.1 %all-gather.10.cloned.1.call-start = ((), (), s32[]{:S(2)}) async-start(), calls=%async_computation.1 | async-start | bytes 2621440 | tf_op jit(solution)/shard_map/all_gather | solution.py:28
  197.0 85.1 %collective-permute-start.1 = (bf16[1024,1024]{1,0:T(8,128)(2,1)}, bf16[1024,1024]{1,0:T(8,128)(2,1)}, u32[]{:S(2)}, u32[]{:S(2)}) collective-permute-start(bf16[1024,1024]{1,0:T(8,128)(2,1)} %all-gather.8.cloned.1.call-done), channel_id=1, source_target_pairs={{8,0},{12,4},{16,8},{20,12},{24,16},{28,20},{9,1},{13,5},{17,9},{2... | collective-permute-start | bytes 6291464 | tf_op jit(solution)/shard_map/ppermute | solution.py:12
  235.1 47.0 %copy-start.3 = (bf16[1024,1024]{1,0:T(8,128)(2,1)S(1)}, bf16[1024,1024]{1,0:T(8,128)(2,1)}, u32[]{:S(2)}) copy-start(bf16[1024,1024]{1,0:T(8,128)(2,1)} %all-gather.8.cloned.1.call-done) | copy-start | bytes 6291460
  243.8 81.0 %collective-permute-start.7 = (bf16[1024,1024]{1,0:T(8,128)(2,1)}, bf16[1024,1024]{1,0:T(8,128)(2,1)}, u32[]{:S(2)}, u32[]{:S(2)}) collective-permute-start(bf16[1024,1024]{1,0:T(8,128)(2,1)} %get-tuple-element.7), channel_id=1, source_target_pairs={{8,0},{12,4},{16,8},{20,12},{24,16},{28,20},{9,1},{13,5},{17,9},{2... | collective-permute-start | bytes 6291464 | tf_op jit(solution)/shard_map/ppermute | solution.py:12
  332.8 181.6 %collective-permute-start.8 = (bf16[1024,1024]{1,0:T(8,128)(2,1)}, bf16[1024,1024]{1,0:T(8,128)(2,1)S(1)}, u32[]{:S(2)}, u32[]{:S(2)}) collective-permute-start(bf16[1024,1024]{1,0:T(8,128)(2,1)} %get-tuple-element.9), channel_id=1, source_target_pairs={{16,0},{20,4},{24,8},{28,12},{17,1},{21,5},{25,9},{29,13},{18,2},{... | collective-permute-start | bytes 6291464 | tf_op jit(solution)/shard_map/ppermute | solution.py:12
  335.4 223.9 %collective-permute-start.5 = (bf16[1024,1024]{1,0:T(8,128)(2,1)}, bf16[1024,1024]{1,0:T(8,128)(2,1)}, u32[]{:S(2)}, u32[]{:S(2)}) collective-permute-start(bf16[1024,1024]{1,0:T(8,128)(2,1)} %all-gather.16.cloned.1.call-done), channel_id=1, source_target_pairs={{16,0},{20,4},{24,8},{28,12},{17,1},{21,5},{25,9},{29,13},{18,2},{... | collective-permute-start | bytes 6291464 | tf_op jit(solution)/shard_map/ppermute | solution.py:12
  338.1 265.1 %collective-permute-start.2 = (bf16[1024,1024]{1,0:T(8,128)(2,1)}, bf16[1024,1024]{1,0:T(8,128)(2,1)}, u32[]{:S(2)}, u32[]{:S(2)}) collective-permute-start(bf16[1024,1024]{1,0:T(8,128)(2,1)} %all-gather.10.cloned.1.call-done), channel_id=1, source_target_pairs={{16,0},{20,4},{24,8},{28,12},{17,1},{21,5},{25,9},{29,13},{18,2},{... | collective-permute-start | bytes 6291464 | tf_op jit(solution)/shard_map/ppermute | solution.py:12
  514.3 1.4 copy-start.5
  515.7 43.6 %copy-start.4 = (bf16[1024,1024]{1,0:T(8,128)(2,1)S(1)}, bf16[1024,1024]{1,0:T(8,128)(2,1)}, u32[]{:S(2)}) copy-start(bf16[1024,1024]{1,0:T(8,128)(2,1)} %all-gather.10.cloned.1.call-done) | copy-start | bytes 6291460
Sparse Core Ops, SparseCore 0:
  10.2 23.6 all-gather.11
  36.0 22.5 all-gather.17
  88.7 22.5 all-gather.13
  141.5 22.8 all-gather.7
  197.1 20.7 all-gather.15
  285.4 20.7 all-gather.9
where the time goes:
time: 618 us; the launch traced here: 612 us
  waiting for transfers between devices  517 us (84%)
  matrix products  45.8 us (7%)
  starting transfers between devices  27.6 us (4%)
  between operations  14.3 us (2%)
    ppermute x9, waiting for transfers between devices, shifted(): lax.ppermute(value, axis, [(source, source + steps) for source in range(f...  459 us
    all_gather x3, waiting for transfers between devices, per_device(): lax.all_gather(own_gain, 'rows', axis=0, tiled=True)  34.8 us
    ppermute x9, starting transfers between devices, shifted(): lax.ppermute(value, axis, [(source, source + steps) for source in range(f...  27.4 us
    dot_general x3, matrix products, per_device(): jnp.dot(own_full, far_offset, preferred_element_type=jnp.float32) + offset  24.6 us
    all_gather x3, waiting for transfers between devices, per_device(): lax.all_gather(own_spread, 'rows', axis=0, tiled=True)  23.4 us
    dot_general x3, matrix products, per_device(): lax.dot_general(middle, own_full, (((1,), (1,)), ((), ())), preferred_ele...  13.3 us
  transfers between devices with their start and end apart: 15, of which 12 were waited for; matrix products, arithmetic and copies ran while one was open for 7% of the time, Pallas kernels for 0%

commit v1 on v0

v1 whole, which is shorter than its diff:
```python
import jax
import jax.numpy as jnp
from jax import lax
from jax.sharding import Mesh, PartitionSpec as P

LEVELS = 3
LOW = jnp.bfloat16
WIDE = jnp.float32


def shifted(value, axis, steps):
    count = lax.axis_size(axis)
    first, last = (max(0, -steps), min(count, count - steps))
    return lax.ppermute(value, axis, [(source, source + steps) for source in range(first, last)])


def doubling(gains, spreads, offsets):
    gain = gains[0]
    spread = spreads[0]
    offset = offsets[0]
    size_d = gain.shape[1]
    identity = jnp.eye(size_d, dtype=LOW)
    for section_number in range(LEVELS):
        distance = 2**section_number
        beyond = lax.axis_index("tm") + distance >= lax.axis_size("tm")
        own_gain = gain.astype(LOW)
        own_spread = spread.astype(LOW)
        own_offset = offset.astype(LOW)
        own_full = lax.all_gather(own_gain, "rows", axis=0, tiled=True)
        spread_full = lax.all_gather(own_spread, "rows", axis=0, tiled=True)
        far_full, far_spread_full, far_offset = shifted((own_full, spread_full, own_offset), "tm", -distance)
        far_full = jnp.where(beyond, identity, far_full)
        row_start = lax.axis_index("rows") * gain.shape[0]
        own_rows = lax.dynamic_slice_in_dim(own_full, row_start, gain.shape[0], 0)
        middle = jnp.dot(own_rows, far_spread_full, preferred_element_type=WIDE).astype(LOW)
        new_gain = jnp.dot(own_rows, far_full, preferred_element_type=WIDE)
        new_spread = (
            lax.dot_general(middle, own_full, (((1,), (1,)), ((), ())), preferred_element_type=WIDE) + spread
        )
        new_offset = jnp.dot(own_full, far_offset, preferred_element_type=WIDE) + offset
        gain, spread, offset = (new_gain, new_spread, new_offset)
    return (gain[None], spread[None], offset[None])


def swap(value, axis):
    return lax.ppermute(value, axis, [(0, 1), (1, 0)])


def mm(a, b):
    return jnp.dot(a, b, preferred_element_type=WIDE)


def mm_bt(a, b):
    return lax.dot_general(a, b, (((1,), (1,)), ((), ())), preferred_element_type=WIDE)


def mm_atbt(a, b):
    return lax.dot_general(a, b, (((0,), (1,)), ((), ())), preferred_element_type=WIDE)


GROUP = ("y", "c", "x")


def exchange(blocks):
    return lax.all_to_all(blocks, GROUP, 0, 0)


def suffix(gains, spreads, offsets):
    pairs = lax.axis_size("z")
    x, y, c, z = (lax.axis_index(name) for name in ("x", "y", "c", "z"))
    even = x == 0
    gain, spread, offset = gains[0], spreads[0], offsets[0]
    rows, size_d = gain.shape
    part = rows // 2
    half = offset.shape[1] // 2
    groups = size_d // rows
    count = 2 * groups
    chunks = 2
    width = half // chunks

    e_low = gain.astype(LOW)
    e_x, e_y = swap(e_low, "x"), swap(e_low, "y")
    e_xy = jnp.concatenate([swap(e_x[:part], "y"), swap(e_y[part:], "x")], axis=0)
    pieces = [e_low, None, e_y, None, e_x, None, e_xy, None]
    for i in range(0, 8, 2):
        pieces[i + 1] = swap(pieces[i], "c")
    me = 4 * x + 2 * y + c
    both = jnp.zeros((8, rows, size_d), LOW)
    for i, piece in enumerate(pieces):
        both = lax.dynamic_update_index_in_dim(both, piece, me ^ i, 0)
    e0, e1 = both[:4].reshape(size_d, size_d), both[4:].reshape(size_d, size_d)

    l_low = spread.astype(LOW)
    l_got = swap(jnp.where(even, l_low[part:], l_low[:part]), "x")
    l_keep = jnp.where(even, spread[:part], spread[part:])
    l1_low = jnp.where(even, l_got, l_keep.astype(LOW))
    l0 = jnp.where(even, l_keep, l_got.astype(WIDE))

    g_keep = jnp.where(even, offset[:, :half], offset[:, half:])
    g_send = jnp.where(even, offset[:, half:], offset[:, :half]).astype(LOW)
    g_got = [swap(g_send[:, i * width : (i + 1) * width], "x") for i in range(chunks)]

    a_e = mm(e0, e1).astype(LOW)
    n = mm_bt(l1_low, e0).astype(LOW)
    n = jnp.broadcast_to(n.reshape(part, groups, 1, rows), (part, groups, 2, rows))
    n = exchange(jnp.transpose(n, (1, 2, 0, 3)).reshape(count, part, rows))
    a_l_rows = mm_atbt(n.reshape(size_d, rows), e0)
    a_l = lax.dynamic_slice_in_dim(a_l_rows, x * part, part, 0) + l0

    slab = (2 * y + c) * 2 + x
    now = lax.dynamic_slice_in_dim(a_e, slab * part, part, 1)
    column = lax.broadcasted_iota(jnp.int32, (size_d, part), 1) + slab * part
    row = lax.broadcasted_iota(jnp.int32, (size_d, part), 0)
    e_far = jnp.where((z == pairs - 1) & (row == column), 1, 0).astype(LOW)
    for hop in range(pairs - 1):
        source = pairs - 1 - hop
        got = lax.ppermute(now, "z", [(source, source - 1)])
        e_far = e_far + got
        if source > 1:
            now = mm(a_e, got).astype(LOW)
    out = jnp.stack([mm(a_e, e_far).astype(LOW), mm(e1, e_far).astype(LOW)])
    out = jnp.transpose(out.reshape(2, groups, rows, part), (1, 0, 2, 3)).reshape(count, rows, part)
    out_gain = jnp.transpose(exchange(out), (1, 0, 2)).reshape(rows, size_d).astype(WIDE)

    now = a_l.astype(LOW)
    l_far = jnp.zeros((part, size_d), LOW)
    for hop in range(pairs - 1):
        source = pairs - 1 - hop
        got = lax.ppermute(now, "z", [(source, source - 1)])
        l_far = l_far + got
        if source > 1:
            n = mm_bt(got, a_e).astype(LOW)
            n = exchange(jnp.transpose(n.reshape(part, count, part), (1, 0, 2)))
            now = (mm_atbt(n.reshape(size_d, part), a_e) + a_l).astype(LOW)
    own_e = jnp.where(even, a_e, e1)
    n = jnp.stack([mm_bt(l_far, a_e).astype(LOW), mm_bt(l_far, e1).astype(LOW)])
    n = jnp.transpose(n.reshape(2, part, groups, rows), (2, 0, 1, 3)).reshape(count, part, rows)
    n = exchange(n).reshape(size_d, rows)
    out_spread = mm_atbt(n, own_e) + jnp.where(even, a_l_rows, 0) + spread

    lefts, rights = [], []
    for i in range(chunks):
        cut = slice(i * width, (i + 1) * width)
        keep = g_keep[:, cut]
        g1_low = jnp.where(even, g_got[i], keep.astype(LOW))
        g0 = jnp.where(even, keep, g_got[i].astype(WIDE))
        p = mm(e0, g1_low)
        a_g = p + g0
        now = a_g.astype(LOW)
        g_far = jnp.zeros((size_d, width), LOW)
        for hop in range(pairs - 1):
            source = pairs - 1 - hop
            got = lax.ppermute(now, "z", [(source, source - 1)])
            g_far = g_far + got
            if source > 1:
                now = (mm(a_e, got) + a_g).astype(LOW)
        o0 = mm(a_e, g_far) + p
        o1 = mm(e1, g_far)
        mine = jnp.where(even, o0, o1) + keep
        other = swap(jnp.where(even, o1, o0).astype(LOW), "x")
        lefts.append(jnp.where(even, mine, other + offset[:, cut]))
        rights.append(jnp.where(even, other + offset[:, half + i * width : half + (i + 1) * width], mine))
    out_offset = jnp.concatenate(lefts + rights, axis=1)
    return (out_gain[None], out_spread[None], out_offset[None])


def solution(mesh):
    steps, rows = mesh.shape["tm"], mesh.shape["rows"]
    if steps <= 2**LEVELS and steps % 2 == 0 and rows == 4:
        devices = mesh.devices.reshape(steps // 2, 2, 2, 2)
        mesh = Mesh(devices, ("z", "x", "y", "c"))
        by_row, by_column = P(("z", "x"), ("y", "c"), None), P(("z", "x"), None, ("y", "c"))
        body = suffix
    else:
        by_row, by_column = P("tm", "rows", None), P("tm", None, "rows")
        body = doubling
    return jax.shard_map(
        body,
        mesh=mesh,
        in_specs=(by_row, by_row, by_column),
        out_specs=(by_row, by_row, by_column),
        check_vma=False,
    )
```

time: 618 us -> 200 us (0.32)
  waiting for transfers between devices: 517 us -> 33.2 us
  local copies, waits for them, and re-layouts: 1.4 us -> 35.9 us
  starting transfers between devices: 27.6 us -> 49.7 us
  other arithmetic: 5.62 us -> 23.2 us
  between operations: 14.3 us -> 1.22 us
  matrix products: 45.8 us -> 53.2 us
    ppermute x9 -> x25, waiting for transfers between devices: 459 us -> 30.5 us  [the longest x13 23.4 us: swap(): return lax.ppermute(value, axis, [(0, 1), (1, 0)])]
    all_gather x6 -> x0, waiting for transfers between devices: 58.2 us -> none  [the longest x3 34.8 us: per_device(): lax.all_gather(own_gain, 'rows', axis=0, tiled=True)]
    all_to_all x0 -> x5, starting transfers between devices: none -> 20.8 us  [exchange(): return lax.all_to_all(blocks, GROUP, 0, 0)]
    unnamed x12 -> x50, local copies, waits for them, and re-layouts: 1.4 us -> 15.5 us
    select_n x0 -> x3, other arithmetic: none -> 8.95 us  [the longest x1 4.76 us: suffix(): lefts.append(jnp.where(even, mine, other + offset[:, cut]))]
    dot_general x9 -> x24, matrix products: 45.8 us -> 53.2 us  [the longest x15 36.8 us: mm(): return jnp.dot(a, b, preferred_element_type=WIDE)]
    dynamic_update_slice x0 -> x7, local copies, waits for them, and re-layouts: none -> 6.83 us  [suffix(): both = lax.dynamic_update_index_in_dim(both, piece, me ^ i, 0)]
    ppermute x9 -> x25, starting transfers between devices: 27.4 us -> 28.8 us  [the longest x12 19.3 us: suffix(): got = lax.ppermute(now, 'z', [(source, source - 1)])]
  transfers between devices with their start and end apart: 15 -> 30, of which waited for: 12 -> 7; matrix products, arithmetic and copies ran while one was open for 7% -> 54% of each run, Pallas kernels for 0% -> 0%
where the time goes in v1:
time: 200 us; the launch traced here: 196 us
  matrix products  53.2 us (27%)
  starting transfers between devices  49.7 us (25%)
  local copies, waits for them, and re-layouts  35.9 us (18%)
  waiting for transfers between devices  33.2 us (17%)
  other arithmetic  23.2 us (12%)
    dot_general x15, matrix products, mm(): return jnp.dot(a, b, preferred_element_type=WIDE)  36.8 us
    ppermute x13, waiting for transfers between devices, swap(): return lax.ppermute(value, axis, [(0, 1), (1, 0)])  23.4 us
    all_to_all x5, starting transfers between devices, exchange(): return lax.all_to_all(blocks, GROUP, 0, 0)  20.8 us
    ppermute x12, starting transfers between devices, suffix(): got = lax.ppermute(now, 'z', [(source, source - 1)])  19.3 us
    unnamed x50, local copies, waits for them, and re-layouts  15.5 us
    dot_general x4, matrix products, mm_atbt(): lax.dot_general(a, b, (((0,), (1,)), ((), ())), preferred_element_type=WIDE)  9.8 us
    ppermute x13, starting transfers between devices, swap(): return lax.ppermute(value, axis, [(0, 1), (1, 0)])  9.49 us
    ppermute x12, waiting for transfers between devices, suffix(): got = lax.ppermute(now, 'z', [(source, source - 1)])  7.18 us
  transfers between devices with their start and end apart: 30, of which 7 were waited for; matrix products, arithmetic and copies ran while one was open for 54% of the time, Pallas kernels for 0%

profile of v1, /device:TPU:16, one launch (start us, length us, event | category | flops | bytes accessed | tf_op | source)
XLA Modules:
  0.0 196.3 jit_solution(9264473078781926578)
XLA Ops:
  2.0 1.6 collective-permute-start.1
  3.6 1.5 collective-permute-start.3
  5.1 5.3 %copy.33 = f32[1,1024,1024]{1,2,0:T(8,128)} copy(f32[1,1024,1024]{2,1,0:T(8,128)} %param.5) | data formatting | bytes 8388608 | tf_op args[2]
  10.4 2.5 %select_convert_fusion = bf16[1024,512]{0,1:T(8,128)(2,1)S(1)} fusion(f32[1024,1024]{0,1:T(8,128)} %bitcast.126, pred[]{:T(512)S(6)} %eq.11), kind=kLoop, calls=%fused_computation.1 | loop fusion | flops 524288 | bytes 3145729 | tf_op jit(solution)/shard_map/convert_element_type | solution.py:100
  16.1 2.5 %broadcast_in_dim.52 = bf16[8,256,1024]{2,1,0:T(8,128)(2,1)} broadcast(bf16[]{:T(256)} %constant.42.clone.1), dimensions={} | broadcast | bytes 4194306 | tf_op jit(solution)/shard_map/broadcast_in_dim | solution.py:88
  19.5 4.2 %slice_select_fusion = f32[1024,512]{0,1:T(8,128)} fusion(f32[1024,1024]{0,1:T(8,128)} %bitcast.127, pred[]{:T(512)S(6)} %eq.11), kind=kLoop, calls=%fused_computation.5 | loop fusion | flops 524288 | bytes 6291457 | tf_op jit(solution)/shard_map/jit(_where)/select_n | solution.py:99
  24.9 1.9 bitcast_dynamic-update-slice_fusion.6
  27.6 3.7 %collective-permute-done.5 = bf16[128,1024]{1,0:T(8,128)(2,1)S(1)} collective-permute-done((bf16[128,1024]{1,0:T(8,128)(2,1)S(1)}, bf16[128,1024]{1,0:T(8,128)(2,1)S(1)}, u32[]{:S(2)}, u32[]{:S(2)}) %collective-permute-start.5) | collective-permute-done | bytes 262176 | tf_op jit(solution)/shard_map/ppermute | solution.py:46
  31.9 14.6 %collective-permute-done.6 = bf16[128,1024]{1,0:T(8,128)(2,1)S(1)} collective-permute-done((bf16[128,1024]{1,0:T(8,128)(2,1)S(1)}, bf16[128,1024]{1,0:T(8,128)(2,1)S(1)}, u32[]{:S(2)}, u32[]{:S(2)}) %collective-permute-start.6) | collective-permute-done | bytes 262176 | tf_op jit(solution)/shard_map/ppermute | solution.py:46
  51.2 2.7 %fusion.46 = (bf16[4,256,1024]{2,1,0:T(8,128)(2,1)S(1)}, bf16[4,256,1024]{2,1,0:T(8,128)(2,1)S(1)}) fusion(bf16[8,256,1024]{2,1,0:T(8,128)(2,1)} %bitcast_dynamic-update-slice_fusion), kind=kLoop, calls=%fused_computation.98 | loop fusion | bytes 8388608 | tf_op jit(solution)/shard_map/slice | solution.py:91
  53.9 2.3 %convolution_convert_fusion = bf16[1024,1024]{1,0:T(8,128)(2,1)S(1)} fusion(bf16[1024,1024]{1,0:T(8,128)(2,1)S(1)} %bitcast.121, bf16[1024,1024]{1,0:T(8,128)(2,1)S(1)} %bitcast.115), kind=kOutput, calls=%fused_computation.6 | convolution fusion | flops 2148532224 | bytes 6291456 | tf_op jit(solution)/shard_map/dot_general | solution.py:50
  58.0 4.2 %all-to-all-start.1 = ((bf16[8,128,256]{2,1,0:T(8,128)(2,1)}), bf16[8,128,256]{2,1,0:T(8,128)(2,1)}, u32[]{:S(2)}, u32[]{:S(2)}) async-start(bf16[8,128,256]{2,1,0:T(8,128)(2,1)} %bitcast.21), calls=%async_computation.1 | async-start | bytes 1048576 | tf_op jit(solution)/shard_map/all_to_all | solution.py:65
  62.3 1.6 collective-permute-start.8
  63.9 2.8 %fusion.28 = f32[1024,256]{0,1:T(8,128)S(1)} fusion(bf16[1024,1024]{1,0:T(8,128)(2,1)} %bitcast.123, bf16[1024,256]{0,1:T(8,128)(2,1)} %collective-permute-done.20, f32[1024,512]{0,1:T(8,128)} %slice_select_fusion, pred[]{:T(512)S(6)} %eq.11), kind=kOutput, calls=%fused_computation.56 | convolution fusion | flops 537133056 | bytes 4194305 | tf_op jit(solution)/shard_map/dot_general | solution.py:50
  66.7 4.2 %fusion.42 = (bf16[1024,256]{0,1:T(8,128)(2,1)}, f32[1024,256]{0,1:T(8,128)}, bf16[1024,256]{0,1:T(8,128)(2,1)}, f32[1024,256]{0,1:T(8,128)}, f32[1024,256]{0,1:T(8,128)}) fusion(bf16[1024,256]{0,1:T(8,128)(2,1)} %collective-permute-done.15, f32[1024,512]{0,1:T(8,128)S(1)} %copy-done.5, pred[]{:T(512)S(6)} %eq.11, f32[1024,256]{0,1:T(8,128)S(1)} %fusion.28, ...), kind=kOutput, calls=%fused_computation.95 | convolution fusion | flops 539230208 | bytes 11535360 | tf_op jit(solution)/shard_map/dot_general | solution.py:50
  75.7 3.0 %collective-permute-start.9 = (bf16[1024,128]{1,0:T(8,128)(2,1)}, bf16[1024,128]{1,0:T(8,128)(2,1)}, u32[]{:S(2)}, u32[]{:S(2)}) collective-permute-start(bf16[1024,128]{1,0:T(8,128)(2,1)} %convolution_convert_fusion.9), channel_id=1, source_target_pairs={{16,8},{17,9},{18,10},{19,11},{20,12},{21,13},{22,14},{23,15}} | collective-permute-start | bytes 786440 | tf_op jit(solution)/shard_map/ppermute | solution.py:117
  78.7 2.6 %fusion.48 = f32[256,1024]{1,0:T(8,128)S(1)} fusion(bf16[1024,256]{1,0:T(8,128)(2,1)} %bitcast.22, bf16[1024,1024]{1,0:T(8,128)(2,1)} %bitcast.124), kind=kOutput, calls=%fused_computation.100 | convolution fusion | flops 536870912 | bytes 3670016 | tf_op jit(solution)/shard_map/dot_general | solution.py:58
  83.6 4.3 %collective-permute-done.21 = bf16[1024,256]{0,1:T(8,128)(2,1)} collective-permute-done((bf16[1024,256]{0,1:T(8,128)(2,1)}, bf16[1024,256]{0,1:T(8,128)(2,1)}, u32[]{:S(2)}, u32[]{:S(2)}) %collective-permute-start.21) | collective-permute-done | bytes 524320 | tf_op jit(solution)/shard_map/ppermute | solution.py:153
  87.9 2.6 %fusion.14 = bf16[1024,256]{0,1:T(8,128)(2,1)} fusion(f32[1024,256]{0,1:T(8,128)S(1)} %copy-done.19, bf16[1024,1024]{1,0:T(8,128)(2,1)S(1)} %convolution_convert_fusion, bf16[1024,256]{0,1:T(8,128)(2,1)} %collective-permute-done.21), kind=kOutput, calls=%fused_computation.22 | convolution fusion | flops 537395200 | bytes 4194304 | tf_op jit(solution)/shard_map/dot_general | solution.py:50
  90.5 2.2 %collective-permute-start.22 = (bf16[1024,256]{0,1:T(8,128)(2,1)}, bf16[1024,256]{0,1:T(8,128)(2,1)}, u32[]{:S(2)}, u32[]{:S(2)}) collective-permute-start(bf16[1024,256]{0,1:T(8,128)(2,1)} %fusion.14), channel_id=1, source_target_pairs={{16,8},{17,9},{18,10},{19,11},{20,12},{21,13},{22,14},{23,15}} | collective-permute-start | bytes 1572872 | tf_op jit(solution)/shard_map/ppermute | solution.py:153
  92.7 2.4 %convolution_convert_fusion.8 = bf16[1024,128]{1,0:T(8,128)(2,1)} fusion(bf16[1024,1024]{1,0:T(8,128)(2,1)S(1)} %convolution_convert_fusion, bf16[1024,128]{1,0:T(8,128)(2,1)} %collective-permute-done.9), kind=kOutput, calls=%fused_computation.33 | convolution fusion | flops 268566528 | bytes 2621440 | tf_op jit(solution)/shard_map/dot_general | solution.py:50
  96.5 2.6 %collective-permute-done.16 = bf16[1024,256]{0,1:T(8,128)(2,1)} collective-permute-done((bf16[1024,256]{0,1:T(8,128)(2,1)}, bf16[1024,256]{0,1:T(8,128)(2,1)}, u32[]{:S(2)}, u32[]{:S(2)}) %collective-permute-start.16) | collective-permute-done | bytes 524320 | tf_op jit(solution)/shard_map/ppermute | solution.py:153
  99.1 2.6 %fusion.12 = bf16[1024,256]{0,1:T(8,128)(2,1)} fusion(f32[1024,256]{0,1:T(8,128)S(1)} %copy-done.17, bf16[1024,1024]{1,0:T(8,128)(2,1)S(1)} %convolution_convert_fusion, bf16[1024,256]{0,1:T(8,128)(2,1)} %collective-permute-done.16), kind=kOutput, calls=%fused_computation.20 | convolution fusion | flops 537395200 | bytes 4194304 | tf_op jit(solution)/shard_map/dot_general | solution.py:50
  101.7 2.1 %collective-permute-start.17 = (bf16[1024,256]{0,1:T(8,128)(2,1)}, bf16[1024,256]{0,1:T(8,128)(2,1)}, u32[]{:S(2)}, u32[]{:S(2)}) collective-permute-start(bf16[1024,256]{0,1:T(8,128)(2,1)} %fusion.12), channel_id=1, source_target_pairs={{16,8},{17,9},{18,10},{19,11},{20,12},{21,13},{22,14},{23,15}} | collective-permute-start | bytes 1572872 | tf_op jit(solution)/shard_map/ppermute | solution.py:153
  105.7 4.1 %all-to-all-start.2 = ((bf16[8,128,128]{2,1,0:T(8,128)(2,1)}), bf16[8,128,128]{2,1,0:T(8,128)(2,1)}, u32[]{:S(2)}, u32[]{:S(2)}) async-start(bf16[8,128,128]{2,1,0:T(8,128)(2,1)} %bitcast.134), calls=%async_computation.2 | async-start | bytes 524288 | tf_op jit(solution)/shard_map/all_to_all | solution.py:65
  113.5 2.7 %all-to-all-done.2 = bf16[8,128,128]{2,1,0:T(8,128)(2,1)} async-done(((bf16[8,128,128]{2,1,0:T(8,128)(2,1)}), bf16[8,128,128]{2,1,0:T(8,128)(2,1)}, u32[]{:S(2)}, u32[]{:S(2)}) %all-to-all-start.2) | async-done | bytes 262176 | tf_op jit(solution)/shard_map/all_to_all | solution.py:65
  116.2 4.2 %all-to-all-start = ((bf16[8,256,128]{2,1,0:T(8,128)(2,1)}), bf16[8,256,128]{2,1,0:T(8,128)(2,1)}, u32[]{:S(2)}, u32[]{:S(2)}) async-start(bf16[8,256,128]{2,1,0:T(8,128)(2,1)} %bitcast.130), calls=%async_computation | async-start | bytes 1048576 | tf_op jit(solution)/shard_map/all_to_all | solution.py:65
  120.4 2.0 %fusion.16 = bf16[128,1024]{1,0:T(8,128)(2,1)S(1)} fusion(f32[128,1024]{1,0:T(8,128)} %get-tuple-element.17, bf16[1024,128]{1,0:T(8,128)(2,1)} %bitcast.24, bf16[1024,1024]{1,0:T(8,128)(2,1)S(1)} %convolution_convert_fusion), kind=kOutput, calls=%fused_computation.35 | convolution fusion | flops 268697600 | bytes 3145728 | tf_op jit(solution)/shard_map/dot_general | solution.py:58
  123.9 2.6 %fusion.15 = bf16[1024,256]{0,1:T(8,128)(2,1)} fusion(f32[1024,256]{0,1:T(8,128)S(1)} %copy-done.20, bf16[1024,1024]{1,0:T(8,128)(2,1)S(1)} %convolution_convert_fusion, bf16[1024,256]{0,1:T(8,128)(2,1)} %collective-permute-done.22), kind=kOutput, calls=%fused_computation.23 | convolution fusion | flops 537395200 | bytes 4194304 | tf_op jit(solution)/shard_map/dot_general | solution.py:50
  128.0 2.6 %fusion.13 = bf16[1024,256]{0,1:T(8,128)(2,1)} fusion(f32[1024,256]{0,1:T(8,128)S(1)} %copy-done.18, bf16[1024,1024]{1,0:T(8,128)(2,1)S(1)} %convolution_convert_fusion, bf16[1024,256]{0,1:T(8,128)(2,1)} %collective-permute-done.17), kind=kOutput, calls=%fused_computation.21 | convolution fusion | flops 537395200 | bytes 4194304 | tf_op jit(solution)/shard_map/dot_general | solution.py:50
  134.3 4.1 %all-to-all-start.3 = ((bf16[8,128,128]{2,1,0:T(8,128)(2,1)}), bf16[8,128,128]{2,1,0:T(8,128)(2,1)}, u32[]{:S(2)}, u32[]{:S(2)}) async-start(bf16[8,128,128]{2,1,0:T(8,128)(2,1)} %bitcast.135), calls=%async_computation.3 | async-start | bytes 524288 | tf_op jit(solution)/shard_map/all_to_all | solution.py:65
  138.4 2.1 %convert_bitcast_fusion = f32[256,8,128]{2,0,1:T(8,128)} fusion(bf16[8,256,128]{2,1,0:T(8,128)(2,1)} %all-to-all-done), kind=kLoop, calls=%fused_computation.44 | loop fusion | flops 262144 | bytes 1572864 | tf_op jit(solution)/shard_map/convert_element_type | solution.py:123
  140.5 2.5 %copy.27 = f32[256,8,128]{0,2,1:T(8,128)} copy(f32[256,8,128]{2,0,1:T(8,128)} %convert_bitcast_fusion) | data formatting | bytes 2097152 | tf_op jit(solution)/shard_map/convert_element_type | solution.py:123
  143.0 2.5 %copy.38 = f32[1,256,1024]{2,1,0:T(8,128)} copy(f32[1,256,1024]{1,2,0:T(8,128)} %bitcast.129) | data formatting | bytes 2097152
  145.6 2.0 fusion.17
  148.4 2.1 %convolution_add_fusion = f32[1024,256]{0,1:T(8,128)S(1)} fusion(f32[1024,256]{0,1:T(8,128)S(1)} %fusion.28, bf16[1024,1024]{1,0:T(8,128)(2,1)S(1)} %convolution_convert_fusion, bf16[1024,256]{0,1:T(8,128)(2,1)} %collective-permute-done.23, bf16[1024,256]{0,1:T(8,128)(2,1)} %collective-permute-done.21, bf16[1024,256]{0,1:T(8,128)(2,1)} %collective-permute-done.22), kind=kOutput, calls=%fused_computation.7 | convolution fusion | flops 537657344 | bytes 5767168 | tf_op jit(solution)/shard_map/dot_general | solution.py:50
  150.5 3.8 %select_convert_fusion.1 = (bf16[1024,256]{0,1:T(8,128)(2,1)}, f32[1024,256]{0,1:T(8,128)}) fusion(f32[1024,256]{0,1:T(8,128)S(1)} %convolution_add_fusion, pred[]{:T(512)S(6)} %eq.11, bf16[1024,1024]{1,0:T(8,128)(2,1)S(1)} %bitcast.119, bf16[1024,256]{0,1:T(8,128)(2,1)} %collective-permute-done.23, bf16[1024,256]{0,1:T(8,128)(2,1)} %collective-permute-done.21, ...), kind=kOutput, calls=%fused_computation.45 | convolution fusion | flops 537657344 | bytes 6291457 | tf_op jit(solution)/shard_map/dot_general | solution.py:50
  154.3 2.0 %collective-permute-start.24 = (bf16[1024,256]{0,1:T(8,128)(2,1)}, bf16[1024,256]{0,1:T(8,128)(2,1)}, u32[]{:S(2)}, u32[]{:S(2)}) collective-permute-start(bf16[1024,256]{0,1:T(8,128)(2,1)} %get-tuple-element.33), channel_id=1, source_target_pairs={{0,4},{4,0},{1,5},{5,1},{2,6},{6,2},{3,7},{7,3},{8,12},{12,8},{9,1... | collective-permute-start | bytes 1572872 | tf_op jit(solution)/shard_map/ppermute | solution.py:46
  156.3 2.1 %convolution_add_fusion.3 = f32[1024,256]{0,1:T(8,128)S(1)} fusion(f32[1024,256]{0,1:T(8,128)S(1)} %copy-done.13, bf16[1024,1024]{1,0:T(8,128)(2,1)S(1)} %convolution_convert_fusion, bf16[1024,256]{0,1:T(8,128)(2,1)} %collective-permute-done.18, bf16[1024,256]{0,1:T(8,128)(2,1)} %collective-permute-done.16, bf16[1024,256]{0,1:T(8,128)(2,1)} %collective-permute-done.17), kind=kOutput, calls=%fused_computation.10 | convolution fusion | flops 537657344 | bytes 5767168 | tf_op jit(solution)/shard_map/dot_general | solution.py:50
  158.5 3.8 %select_convert_fusion.2 = (bf16[1024,256]{0,1:T(8,128)(2,1)}, f32[1024,256]{0,1:T(8,128)}) fusion(f32[1024,256]{0,1:T(8,128)S(1)} %convolution_add_fusion.3, pred[]{:T(512)S(6)} %eq.11, bf16[1024,1024]{1,0:T(8,128)(2,1)S(1)} %bitcast.120, bf16[1024,256]{0,1:T(8,128)(2,1)} %collective-permute-done.18, bf16[1024,256]{0,1:T(8,128)(2,1)} %collective-permute-done.16, ...), kind=kOutput, calls=%fused_computation.48 | convolution fusion | flops 537657344 | bytes 6291457 | tf_op jit(solution)/shard_map/dot_general | solution.py:50
  164.8 3.3 %convolution_convert_fusion.1 = bf16[128,1024]{1,0:T(8,128)(2,1)} fusion(bf16[1024,1024]{1,0:T(8,128)(2,1)} %bitcast.116, bf16[128,1024]{1,0:T(8,128)(2,1)} %copy-done.22, bf16[128,1024]{1,0:T(8,128)(2,1)S(1)} %collective-permute-done.12, bf16[128,1024]{1,0:T(8,128)(2,1)S(1)} %copy-done.16), kind=kOutput, calls=%fused_computation.26 | convolution fusion | flops 268828672 | bytes 3145728 | tf_op jit(solution)/shard_map/dot_general | solution.py:54
  169.3 1.8 pad_maximum_fusion.1
  171.1 4.4 %all-to-all-start.4 = ((bf16[8,128,256]{2,1,0:T(8,128)(2,1)}), bf16[8,128,256]{2,1,0:T(8,128)(2,1)}, u32[]{:S(2)}, u32[]{:S(2)}) async-start(bf16[8,128,256]{2,1,0:T(8,128)(2,1)} %bitcast.131), calls=%async_computation.4 | async-start | bytes 1048576 | tf_op jit(solution)/shard_map/all_to_all | solution.py:65
  175.5 5.1 %collective-permute-done.19 = bf16[1024,256]{0,1:T(8,128)(2,1)} collective-permute-done((bf16[1024,256]{0,1:T(8,128)(2,1)}, bf16[1024,256]{0,1:T(8,128)(2,1)}, u32[]{:S(2)}, u32[]{:S(2)}) %collective-permute-start.19) | collective-permute-done | bytes 524320 | tf_op jit(solution)/shard_map/ppermute | solution.py:46
  180.6 4.8 %fusion.20 = (f32[1024,256]{0,1:T(8,128)S(1)}, f32[1024,256]{0,1:T(8,128)S(1)}, f32[1024,256]{0,1:T(8,128)S(1)}, f32[1024,256]{0,1:T(8,128)S(1)}) fusion(bf16[1024,256]{0,1:T(8,128)(2,1)} %collective-permute-done.19, f32[1024,1024]{0,1:T(8,128)} %bitcast.128, pred[]{:T(512)S(6)} %eq.11, f32[1024,512]{0,1:T(8,128)} %slice_select_fusion, ...), kind=kLoop, calls=%fused_computation.39 | loop fusion | flops 3670016 | bytes 15728641 | tf_op jit(solution)/shard_map/jit(_where)/select_n | solution.py:161
  185.3 2.3 %maximum_bitcast_fusion = f32[1,1024,1024]{1,2,0:T(8,128)} fusion(f32[1024,256]{0,1:T(8,128)S(1)} %get-tuple-element.22, f32[1024,256]{0,1:T(8,128)S(1)} %get-tuple-element.19, f32[1024,256]{0,1:T(8,128)S(1)} %get-tuple-element.23, f32[1024,256]{0,1:T(8,128)S(1)} %get-tuple-element.18), kind=kLoop, calls=%fused_computation | loop fusion | flops 3145728 | bytes 8388608 | tf_op jit(solution)/shard_map/broadcast_in_dim | solution.py:164
  187.7 5.4 %copy.39 = f32[1,1024,1024]{2,1,0:T(8,128)} copy(f32[1,1024,1024]{1,2,0:T(8,128)} %maximum_bitcast_fusion) | data formatting | bytes 8388608
  193.1 3.2 %fusion.9 = f32[1,256,1024]{2,1,0:T(8,128)} fusion(bf16[1024,256]{1,0:T(8,128)(2,1)} %bitcast.29, bf16[1024,1024]{1,0:T(8,128)(2,1)S(1)} %convolution_convert_fusion, bf16[1024,1024]{1,0:T(8,128)(2,1)} %bitcast.117, pred[]{:T(512)S(6)} %eq.11, f32[1,256,1024]{2,1,0:T(8,128)S(1)} %copy-done.11, f32[256,1024]{1,0:T(8,128)} %copy-done.12), kind=kOutput, calls=%fused_computation.15 | convolution fusion | flops 538705920 | bytes 7864321 | tf_op jit(solution)/shard_map/dot_general | solution.py:58
  (123 shorter events, 39.7 us)
Async XLA Ops:
  1.9 23.0 %collective-permute-start = (bf16[256,1024]{1,0:T(8,128)(2,1)S(1)}, bf16[256,1024]{1,0:T(8,128)(2,1)}, u32[]{:S(2)}, u32[]{:S(2)}) collective-permute-start(bf16[256,1024]{1,0:T(8,128)(2,1)S(1)} %convert_bitcast_fusion.1), channel_id=1, source_target_pairs={{0,1},{1,0},{2,3},{3,2},{4,5},{5,4},{6,7},{7,6},{8,9},{9,8},{10,11... | collective-permute-start | bytes 1572872 | tf_op jit(solution)/shard_map/ppermute | solution.py:46
  2.0 22.3 %collective-permute-start.1 = (bf16[256,1024]{1,0:T(8,128)(2,1)S(1)}, bf16[256,1024]{1,0:T(8,128)(2,1)S(1)}, u32[]{:S(2)}, u32[]{:S(2)}) collective-permute-start(bf16[256,1024]{1,0:T(8,128)(2,1)S(1)} %convert_bitcast_fusion.1), channel_id=1, source_target_pairs={{0,2},{2,0},{1,3},{3,1},{4,6},{6,4},{5,7},{7,5},{8,10},{10,8},{9,1... | collective-permute-start | bytes 1572872 | tf_op jit(solution)/shard_map/ppermute | solution.py:46
  3.6 20.1 %collective-permute-start.3 = (bf16[256,1024]{1,0:T(8,128)(2,1)S(1)}, bf16[256,1024]{1,0:T(8,128)(2,1)S(1)}, u32[]{:S(2)}, u32[]{:S(2)}) collective-permute-start(bf16[256,1024]{1,0:T(8,128)(2,1)S(1)} %convert_bitcast_fusion.1), channel_id=1, source_target_pairs={{0,4},{4,0},{1,5},{5,1},{2,6},{6,2},{3,7},{7,3},{8,12},{12,8},{9,1... | collective-permute-start | bytes 1572872 | tf_op jit(solution)/shard_map/ppermute | solution.py:46
  10.4 5.6 %copy-start.9 = (f32[1,256,1024]{2,1,0:T(8,128)S(1)}, f32[1,256,1024]{2,1,0:T(8,128)}, u32[]{:S(2)}) copy-start(f32[1,256,1024]{2,1,0:T(8,128)} %param.4) | copy-start | bytes 3145732
  14.0 49.9 %collective-permute-start.20 = (bf16[1024,256]{0,1:T(8,128)(2,1)}, bf16[1024,256]{0,1:T(8,128)(2,1)}, u32[]{:S(2)}, u32[]{:S(2)}) collective-permute-start(bf16[1024,256]{0,1:T(8,128)(2,1)} %get-tuple-element.29), channel_id=1, source_target_pairs={{0,4},{4,0},{1,5},{5,1},{2,6},{6,2},{3,7},{7,3},{8,12},{12,8},{9,1... | collective-permute-start | bytes 1572872 | tf_op jit(solution)/shard_map/ppermute | solution.py:46
  14.5 52.2 %collective-permute-start.15 = (bf16[1024,256]{0,1:T(8,128)(2,1)}, bf16[1024,256]{0,1:T(8,128)(2,1)}, u32[]{:S(2)}, u32[]{:S(2)}) collective-permute-start(bf16[1024,256]{0,1:T(8,128)(2,1)} %get-tuple-element.28), channel_id=1, source_target_pairs={{0,4},{4,0},{1,5},{5,1},{2,6},{6,2},{3,7},{7,3},{8,12},{12,8},{9,1... | collective-permute-start | bytes 1572872 | tf_op jit(solution)/shard_map/ppermute | solution.py:46
  16.1 2.6 %copy-start.14 = (f32[1,256,1024]{2,1,0:T(8,128)S(1)}, f32[1,256,1024]{2,1,0:T(8,128)}, u32[]{:S(2)}) copy-start(f32[1,256,1024]{2,1,0:T(8,128)} %param.3) | copy-start | bytes 3145732
  23.7 7.6 %collective-permute-start.5 = (bf16[128,1024]{1,0:T(8,128)(2,1)S(1)}, bf16[128,1024]{1,0:T(8,128)(2,1)S(1)}, u32[]{:S(2)}, u32[]{:S(2)}) collective-permute-start(bf16[128,1024]{1,0:T(8,128)(2,1)S(1)} %slice.76), channel_id=1, source_target_pairs={{0,2},{2,0},{1,3},{3,1},{4,6},{6,4},{5,7},{7,5},{8,10},{10,8},{9,1... | collective-permute-start | bytes 786440 | tf_op jit(solution)/shard_map/ppermute | solution.py:46
  24.3 22.1 %collective-permute-start.6 = (bf16[128,1024]{1,0:T(8,128)(2,1)S(1)}, bf16[128,1024]{1,0:T(8,128)(2,1)S(1)}, u32[]{:S(2)}, u32[]{:S(2)}) collective-permute-start(bf16[128,1024]{1,0:T(8,128)(2,1)S(1)} %slice.77), channel_id=1, source_target_pairs={{0,4},{4,0},{1,5},{5,1},{2,6},{6,2},{3,7},{7,3},{8,12},{12,8},{9,1... | collective-permute-start | bytes 786440 | tf_op jit(solution)/shard_map/ppermute | solution.py:46
  24.9 21.5 %collective-permute-start.2 = (bf16[256,1024]{1,0:T(8,128)(2,1)S(1)}, bf16[256,1024]{1,0:T(8,128)(2,1)S(1)}, u32[]{:S(2)}, u32[]{:S(2)}) collective-permute-start(bf16[256,1024]{1,0:T(8,128)(2,1)S(1)} %collective-permute-done.1), channel_id=1, source_target_pairs={{0,1},{1,0},{2,3},{3,2},{4,5},{5,4},{6,7},{7,6},{8,9},{9,8},{10,11... | collective-permute-start | bytes 1572872 | tf_op jit(solution)/shard_map/ppermute | solution.py:46
  31.3 24.9 %collective-permute-start.11 = (bf16[128,1024]{1,0:T(8,128)(2,1)S(1)}, bf16[128,1024]{1,0:T(8,128)(2,1)S(1)}, u32[]{:S(2)}, u32[]{:S(2)}) collective-permute-start(bf16[128,1024]{1,0:T(8,128)(2,1)S(1)} %slice_select_fusion.2), channel_id=1, source_target_pairs={{0,4},{4,0},{1,5},{5,1},{2,6},{6,2},{3,7},{7,3},{8,12},{12,8},{9,1... | collective-permute-start | bytes 786440 | tf_op jit(solution)/shard_map/ppermute | solution.py:46
  46.5 2.3 %collective-permute-start.4 = (bf16[256,1024]{1,0:T(8,128)(2,1)S(1)}, bf16[256,1024]{1,0:T(8,128)(2,1)S(1)}, u32[]{:S(2)}, u32[]{:S(2)}) collective-permute-start(bf16[256,1024]{1,0:T(8,128)(2,1)S(1)} %collective-permute-done.3), channel_id=1, source_target_pairs={{0,1},{1,0},{2,3},{3,2},{4,5},{5,4},{6,7},{7,6},{8,9},{9,8},{10,11... | collective-permute-start | bytes 1572872 | tf_op jit(solution)/shard_map/ppermute | solution.py:46
  46.5 3.9 %collective-permute-start.7 = (bf16[256,1024]{1,0:T(8,128)(2,1)S(1)}, bf16[256,1024]{1,0:T(8,128)(2,1)S(1)}, u32[]{:S(2)}, u32[]{:S(2)}) collective-permute-start(bf16[256,1024]{1,0:T(8,128)(2,1)S(1)} %constant_dynamic-update-slice_fusion), channel_id=1, source_target_pairs={{0,1},{1,0},{2,3},{3,2},{4,5},{5,4},{6,7},{7,6},{8,9},{9,8},{10,11... | collective-permute-start | bytes 1572872 | tf_op jit(solution)/shard_map/ppermute | solution.py:46
  53.9 2.4 %copy-start.3 = (bf16[4,256,1024]{2,1,0:T(8,128)(2,1)}, bf16[4,256,1024]{2,1,0:T(8,128)(2,1)S(1)}, u32[]{:S(2)}) copy-start(bf16[4,256,1024]{2,1,0:T(8,128)(2,1)S(1)} %get-tuple-element.24) | copy-start | bytes 6291460
  58.0 20.7 %all-to-all-start.1 = ((bf16[8,128,256]{2,1,0:T(8,128)(2,1)}), bf16[8,128,256]{2,1,0:T(8,128)(2,1)}, u32[]{:S(2)}, u32[]{:S(2)}) async-start(bf16[8,128,256]{2,1,0:T(8,128)(2,1)} %bitcast.21), calls=%async_computation.1 | async-start | bytes 1048576 | tf_op jit(solution)/shard_map/all_to_all | solution.py:65
  62.3 4.4 %copy-start.4 = (bf16[4,256,1024]{2,1,0:T(8,128)(2,1)S(1)}, bf16[4,256,1024]{2,1,0:T(8,128)(2,1)}, u32[]{:S(2)}) copy-start(bf16[4,256,1024]{2,1,0:T(8,128)(2,1)} %copy-done.3) | copy-start | bytes 6291460
  62.3 4.4 %copy-start.5 = (f32[1024,512]{0,1:T(8,128)S(1)}, f32[1024,512]{0,1:T(8,128)}, u32[]{:S(2)}) copy-start(f32[1024,512]{0,1:T(8,128)} %slice_select_fusion) | copy-start | bytes 6291460
  62.3 11.2 %collective-permute-start.8 = (bf16[1024,128]{1,0:T(8,128)(2,1)S(1)}, bf16[1024,128]{1,0:T(8,128)(2,1)S(1)}, u32[]{:S(2)}, u32[]{:S(2)}) collective-permute-start(bf16[1024,128]{1,0:T(8,128)(2,1)S(1)} %constant_dynamic-slice_fusion), channel_id=1, source_target_pairs={{24,16},{25,17},{26,18},{27,19},{28,20},{29,21},{30,22},{31,23}} | collective-permute-start | bytes 786440 | tf_op jit(solution)/shard_map/ppermute | solution.py:117
  70.9 17.0 %collective-permute-start.21 = (bf16[1024,256]{0,1:T(8,128)(2,1)}, bf16[1024,256]{0,1:T(8,128)(2,1)}, u32[]{:S(2)}, u32[]{:S(2)}) collective-permute-start(bf16[1024,256]{0,1:T(8,128)(2,1)} %get-tuple-element.26), channel_id=1, source_target_pairs={{24,16},{25,17},{26,18},{27,19},{28,20},{29,21},{30,22},{31,23}} | collective-permute-start | bytes 1572872 | tf_op jit(solution)/shard_map/ppermute | solution.py:153
  72.2 26.9 %collective-permute-start.16 = (bf16[1024,256]{0,1:T(8,128)(2,1)}, bf16[1024,256]{0,1:T(8,128)(2,1)}, u32[]{:S(2)}, u32[]{:S(2)}) collective-permute-start(bf16[1024,256]{0,1:T(8,128)(2,1)} %get-tuple-element.12), channel_id=1, source_target_pairs={{24,16},{25,17},{26,18},{27,19},{28,20},{29,21},{30,22},{31,23}} | collective-permute-start | bytes 1572872 | tf_op jit(solution)/shard_map/ppermute | solution.py:153
  75.7 17.1 %collective-permute-start.9 = (bf16[1024,128]{1,0:T(8,128)(2,1)}, bf16[1024,128]{1,0:T(8,128)(2,1)}, u32[]{:S(2)}, u32[]{:S(2)}) collective-permute-start(bf16[1024,128]{1,0:T(8,128)(2,1)} %convolution_convert_fusion.9), channel_id=1, source_target_pairs={{16,8},{17,9},{18,10},{19,11},{20,12},{21,13},{22,14},{23,15}} | collective-permute-start | bytes 786440 | tf_op jit(solution)/shard_map/ppermute | solution.py:117
  78.7 2.6 %copy-start.10 = (f32[1,256,1024]{2,1,0:T(8,128)S(1)}, f32[1,256,1024]{2,1,0:T(8,128)}, u32[]{:S(2)}) copy-start(f32[1,256,1024]{2,1,0:T(8,128)} %param.4) | copy-start | bytes 3145732
  81.3 9.2 %copy-start.12 = (f32[256,1024]{1,0:T(8,128)}, f32[256,1024]{1,0:T(8,128)S(1)}, u32[]{:S(2)}) copy-start(f32[256,1024]{1,0:T(8,128)S(1)} %fusion.48) | copy-start | bytes 3145732
  81.3 6.6 %copy-start.19 = (f32[1024,256]{0,1:T(8,128)S(1)}, f32[1024,256]{0,1:T(8,128)}, u32[]{:S(2)}) copy-start(f32[1024,256]{0,1:T(8,128)} %get-tuple-element.27) | copy-start | bytes 3145732
  82.3 21.8 %collective-permute-start.12 = (bf16[128,1024]{1,0:T(8,128)(2,1)S(1)}, bf16[128,1024]{1,0:T(8,128)(2,1)S(1)}, u32[]{:S(2)}, u32[]{:S(2)}) collective-permute-start(bf16[128,1024]{1,0:T(8,128)(2,1)S(1)} %get-tuple-element.16), channel_id=1, source_target_pairs={{24,16},{25,17},{26,18},{27,19},{28,20},{29,21},{30,22},{31,23}} | collective-permute-start | bytes 786440 | tf_op jit(solution)/shard_map/ppermute | solution.py:129
  90.5 8.6 %copy-start.17 = (f32[1024,256]{0,1:T(8,128)S(1)}, f32[1024,256]{0,1:T(8,128)}, u32[]{:S(2)}) copy-start(f32[1024,256]{0,1:T(8,128)} %get-tuple-element.13) | copy-start | bytes 3145732
  90.5 33.4 %collective-permute-start.22 = (bf16[1024,256]{0,1:T(8,128)(2,1)}, bf16[1024,256]{0,1:T(8,128)(2,1)}, u32[]{:S(2)}, u32[]{:S(2)}) collective-permute-start(bf16[1024,256]{0,1:T(8,128)(2,1)} %fusion.14), channel_id=1, source_target_pairs={{16,8},{17,9},{18,10},{19,11},{20,12},{21,13},{22,14},{23,15}} | collective-permute-start | bytes 1572872 | tf_op jit(solution)/shard_map/ppermute | solution.py:153
  95.1 14.6 %collective-permute-start.10 = (bf16[1024,128]{1,0:T(8,128)(2,1)}, bf16[1024,128]{1,0:T(8,128)(2,1)}, u32[]{:S(2)}, u32[]{:S(2)}) collective-permute-start(bf16[1024,128]{1,0:T(8,128)(2,1)} %convolution_convert_fusion.8), channel_id=1, source_target_pairs={{8,0},{9,1},{10,2},{11,3},{12,4},{13,5},{14,6},{15,7}} | collective-permute-start | bytes 786440 | tf_op jit(solution)/shard_map/ppermute | solution.py:117
  101.7 26.2 %collective-permute-start.17 = (bf16[1024,256]{0,1:T(8,128)(2,1)}, bf16[1024,256]{0,1:T(8,128)(2,1)}, u32[]{:S(2)}, u32[]{:S(2)}) collective-permute-start(bf16[1024,256]{0,1:T(8,128)(2,1)} %fusion.12), channel_id=1, source_target_pairs={{16,8},{17,9},{18,10},{19,11},{20,12},{21,13},{22,14},{23,15}} | collective-permute-start | bytes 1572872 | tf_op jit(solution)/shard_map/ppermute | solution.py:153
  105.7 10.5 %all-to-all-start.2 = ((bf16[8,128,128]{2,1,0:T(8,128)(2,1)}), bf16[8,128,128]{2,1,0:T(8,128)(2,1)}, u32[]{:S(2)}, u32[]{:S(2)}) async-start(bf16[8,128,128]{2,1,0:T(8,128)(2,1)} %bitcast.134), calls=%async_computation.2 | async-start | bytes 524288 | tf_op jit(solution)/shard_map/all_to_all | solution.py:65
  116.2 18.2 %all-to-all-start = ((bf16[8,256,128]{2,1,0:T(8,128)(2,1)}), bf16[8,256,128]{2,1,0:T(8,128)(2,1)}, u32[]{:S(2)}, u32[]{:S(2)}) async-start(bf16[8,256,128]{2,1,0:T(8,128)(2,1)} %bitcast.130), calls=%async_computation | async-start | bytes 1048576 | tf_op jit(solution)/shard_map/all_to_all | solution.py:65
  120.4 3.5 %copy-start.20 = (f32[1024,256]{0,1:T(8,128)S(1)}, f32[1024,256]{0,1:T(8,128)}, u32[]{:S(2)}) copy-start(f32[1024,256]{0,1:T(8,128)} %get-tuple-element.27) | copy-start | bytes 3145732
  122.4 5.6 %copy-start.18 = (f32[1024,256]{0,1:T(8,128)S(1)}, f32[1024,256]{0,1:T(8,128)}, u32[]{:S(2)}) copy-start(f32[1024,256]{0,1:T(8,128)} %get-tuple-element.13) | copy-start | bytes 3145732
  122.4 9.6 %collective-permute-start.13 = (bf16[128,1024]{1,0:T(8,128)(2,1)S(1)}, bf16[128,1024]{1,0:T(8,128)(2,1)S(1)}, u32[]{:S(2)}, u32[]{:S(2)}) collective-permute-start(bf16[128,1024]{1,0:T(8,128)(2,1)S(1)} %fusion.16), channel_id=1, source_target_pairs={{16,8},{17,9},{18,10},{19,11},{20,12},{21,13},{22,14},{23,15}} | collective-permute-start | bytes 786440 | tf_op jit(solution)/shard_map/ppermute | solution.py:129
  126.5 21.9 %collective-permute-start.23 = (bf16[1024,256]{0,1:T(8,128)(2,1)}, bf16[1024,256]{0,1:T(8,128)(2,1)}, u32[]{:S(2)}, u32[]{:S(2)}) collective-permute-start(bf16[1024,256]{0,1:T(8,128)(2,1)} %fusion.15), channel_id=1, source_target_pairs={{8,0},{9,1},{10,2},{11,3},{12,4},{13,5},{14,6},{15,7}} | collective-permute-start | bytes 1572872 | tf_op jit(solution)/shard_map/ppermute | solution.py:153
  130.5 25.8 %collective-permute-start.18 = (bf16[1024,256]{0,1:T(8,128)(2,1)}, bf16[1024,256]{0,1:T(8,128)(2,1)}, u32[]{:S(2)}, u32[]{:S(2)}) collective-permute-start(bf16[1024,256]{0,1:T(8,128)(2,1)} %fusion.13), channel_id=1, source_target_pairs={{8,0},{9,1},{10,2},{11,3},{12,4},{13,5},{14,6},{15,7}} | collective-permute-start | bytes 1572872 | tf_op jit(solution)/shard_map/ppermute | solution.py:153
  134.3 11.2 %all-to-all-start.3 = ((bf16[8,128,128]{2,1,0:T(8,128)(2,1)}), bf16[8,128,128]{2,1,0:T(8,128)(2,1)}, u32[]{:S(2)}, u32[]{:S(2)}) async-start(bf16[8,128,128]{2,1,0:T(8,128)(2,1)} %bitcast.135), calls=%async_computation.3 | async-start | bytes 524288 | tf_op jit(solution)/shard_map/all_to_all | solution.py:65
  147.5 2.9 %copy-start.2 = (bf16[4,256,1024]{2,1,0:T(8,128)(2,1)S(1)}, bf16[4,256,1024]{2,1,0:T(8,128)(2,1)}, u32[]{:S(2)}) copy-start(bf16[4,256,1024]{2,1,0:T(8,128)(2,1)} %copy-done) | copy-start | bytes 6291460
  147.5 14.8 %collective-permute-start.14 = (bf16[128,1024]{1,0:T(8,128)(2,1)S(1)}, bf16[128,1024]{1,0:T(8,128)(2,1)S(1)}, u32[]{:S(2)}, u32[]{:S(2)}) collective-permute-start(bf16[128,1024]{1,0:T(8,128)(2,1)S(1)} %fusion.17), channel_id=1, source_target_pairs={{8,0},{9,1},{10,2},{11,3},{12,4},{13,5},{14,6},{15,7}} | collective-permute-start | bytes 786440 | tf_op jit(solution)/shard_map/ppermute | solution.py:129
  150.5 3.8 %copy-start.6 = (f32[1024,256]{0,1:T(8,128)}, f32[1024,256]{0,1:T(8,128)S(1)}, u32[]{:S(2)}) copy-start(f32[1024,256]{0,1:T(8,128)S(1)} %convolution_add_fusion) | copy-start | bytes 3145732
  150.5 5.8 %copy-start.13 = (f32[1024,256]{0,1:T(8,128)S(1)}, f32[1024,256]{0,1:T(8,128)}, u32[]{:S(2)}) copy-start(f32[1024,256]{0,1:T(8,128)} %get-tuple-element.30) | copy-start | bytes 3145732
  154.3 21.2 %collective-permute-start.24 = (bf16[1024,256]{0,1:T(8,128)(2,1)}, bf16[1024,256]{0,1:T(8,128)(2,1)}, u32[]{:S(2)}, u32[]{:S(2)}) collective-permute-start(bf16[1024,256]{0,1:T(8,128)(2,1)} %get-tuple-element.33), channel_id=1, source_target_pairs={{0,4},{4,0},{1,5},{5,1},{2,6},{6,2},{3,7},{7,3},{8,12},{12,8},{9,1... | collective-permute-start | bytes 1572872 | tf_op jit(solution)/shard_map/ppermute | solution.py:46
  158.5 3.8 %copy-start.8 = (f32[1024,256]{0,1:T(8,128)}, f32[1024,256]{0,1:T(8,128)S(1)}, u32[]{:S(2)}) copy-start(f32[1024,256]{0,1:T(8,128)S(1)} %convolution_add_fusion.3) | copy-start | bytes 3145732
  158.5 4.5 %copy-start.16 = (bf16[128,1024]{1,0:T(8,128)(2,1)S(1)}, bf16[128,1024]{1,0:T(8,128)(2,1)}, u32[]{:S(2)}) copy-start(bf16[128,1024]{1,0:T(8,128)(2,1)} %copy-done.15) | copy-start | bytes 786436
  162.3 18.3 %collective-permute-start.19 = (bf16[1024,256]{0,1:T(8,128)(2,1)}, bf16[1024,256]{0,1:T(8,128)(2,1)}, u32[]{:S(2)}, u32[]{:S(2)}) collective-permute-start(bf16[1024,256]{0,1:T(8,128)(2,1)} %get-tuple-element.31), channel_id=1, source_target_pairs={{0,4},{4,0},{1,5},{5,1},{2,6},{6,2},{3,7},{7,3},{8,12},{12,8},{9,1... | collective-permute-start | bytes 1572872 | tf_op jit(solution)/shard_map/ppermute | solution.py:46
  168.0 12.6 %copy-start.7 = (f32[1024,256]{0,1:T(8,128)S(1)}, f32[1024,256]{0,1:T(8,128)}, u32[]{:S(2)}) copy-start(f32[1024,256]{0,1:T(8,128)} %copy-done.6) | copy-start | bytes 3145732
  171.1 22.0 %all-to-all-start.4 = ((bf16[8,128,256]{2,1,0:T(8,128)(2,1)}), bf16[8,128,256]{2,1,0:T(8,128)(2,1)}, u32[]{:S(2)}, u32[]{:S(2)}) async-start(bf16[8,128,256]{2,1,0:T(8,128)(2,1)} %bitcast.131), calls=%async_computation.4 | async-start | bytes 1048576 | tf_op jit(solution)/shard_map/all_to_all | solution.py:65
  187.7 5.4 %copy-start.11 = (f32[1,256,1024]{2,1,0:T(8,128)S(1)}, f32[1,256,1024]{2,1,0:T(8,128)}, u32[]{:S(2)}) copy-start(f32[1,256,1024]{2,1,0:T(8,128)} %param.4) | copy-start | bytes 3145732
  (5 other events, 6.7 us)

commit v2 on v1

v2 whole, which is shorter than its diff:
```python
import jax
import jax.numpy as jnp
from jax import lax
from jax.experimental import pallas as pl
from jax.experimental.pallas import tpu as pltpu
from jax.sharding import Mesh, PartitionSpec as P

LEVELS = 3
LOW = jnp.bfloat16
WIDE = jnp.float32
SCOPED = 40 * 2**20


def shifted(value, axis, steps):
    count = lax.axis_size(axis)
    first, last = (max(0, -steps), min(count, count - steps))
    return lax.ppermute(value, axis, [(source, source + steps) for source in range(first, last)])


def doubling(gains, spreads, offsets):
    gain = gains[0]
    spread = spreads[0]
    offset = offsets[0]
    size_d = gain.shape[1]
    identity = jnp.eye(size_d, dtype=LOW)
    for section_number in range(LEVELS):
        distance = 2**section_number
        beyond = lax.axis_index("tm") + distance >= lax.axis_size("tm")
        own_gain = gain.astype(LOW)
        own_spread = spread.astype(LOW)
        own_offset = offset.astype(LOW)
        own_full = lax.all_gather(own_gain, "rows", axis=0, tiled=True)
        spread_full = lax.all_gather(own_spread, "rows", axis=0, tiled=True)
        far_full, far_spread_full, far_offset = shifted((own_full, spread_full, own_offset), "tm", -distance)
        far_full = jnp.where(beyond, identity, far_full)
        row_start = lax.axis_index("rows") * gain.shape[0]
        own_rows = lax.dynamic_slice_in_dim(own_full, row_start, gain.shape[0], 0)
        middle = jnp.dot(own_rows, far_spread_full, preferred_element_type=WIDE).astype(LOW)
        new_gain = jnp.dot(own_rows, far_full, preferred_element_type=WIDE)
        new_spread = (
            lax.dot_general(middle, own_full, (((1,), (1,)), ((), ())), preferred_element_type=WIDE) + spread
        )
        new_offset = jnp.dot(own_full, far_offset, preferred_element_type=WIDE) + offset
        gain, spread, offset = (new_gain, new_spread, new_offset)
    return (gain[None], spread[None], offset[None])


def swap(value, axis):
    return lax.ppermute(value, axis, [(0, 1), (1, 0)])


def mm(a, b):
    return jnp.dot(a, b, preferred_element_type=WIDE)


def mm_bt(a, b):
    return lax.dot_general(a, b, (((1,), (1,)), ((), ())), preferred_element_type=WIDE)


def mm_atbt(a, b):
    return lax.dot_general(a, b, (((0,), (1,)), ((), ())), preferred_element_type=WIDE)


GROUP = ("y", "c", "x")


def exchange(blocks):
    return lax.all_to_all(blocks, GROUP, 0, 0)


def call(kernel, grid, ids, ins, outs, out_shapes, operands, scratch=(), aliases={}, flops=0, bytes_accessed=0):
    return pl.pallas_call(
        kernel,
        grid_spec=pltpu.PrefetchScalarGridSpec(
            num_scalar_prefetch=1, grid=grid, in_specs=ins, out_specs=outs, scratch_shapes=list(scratch)
        ),
        out_shape=out_shapes,
        input_output_aliases=aliases,
        cost_estimate=pl.CostEstimate(flops=flops, bytes_accessed=bytes_accessed, transcendentals=0),
        compiler_params=pltpu.CompilerParams(vmem_limit_bytes=SCOPED),
    )(ids, *operands)


def whole(shape):
    return pl.BlockSpec(shape, lambda *_: (0,) * len(shape))


def pair_kernel(ids, *refs):
    pieces, (l_ref, both, pair, n_ref) = refs[:8], refs[8:]
    me = 4 * ids[0] + 2 * ids[1] + ids[2]
    rows = pieces[0].shape[0]
    for i in range(8):
        place = me ^ i
        both[place >> 2, pl.ds(pl.multiple_of((place & 3) * rows, rows), rows), :] = pieces[i][...]
    for r in range(4):
        cut = slice(r * rows, (r + 1) * rows)
        n = mm_bt(l_ref[...], both[0, cut, :]).astype(LOW)
        n_ref[2 * r] = n
        n_ref[2 * r + 1] = n
        pair[cut, :] = mm(both[0, cut, :], both[1]).astype(LOW)


def compose_kernel(ids, pair, later, half_ref, other_ref, first, second, far):
    step = pl.program_id(0)
    size = half_ref.shape[0]
    c, z = ids[2], ids[3]

    @pl.when((step == 0) & (z % 2 == 0))
    def _():
        far[pl.ds(pl.multiple_of(c * size, size), size), :] = half_ref[...]
        far[pl.ds(pl.multiple_of((1 - c) * size, size), size), :] = other_ref[...]

    @pl.when(z % 2 == 0)
    def _():
        first[...] = mm(pair[...], far[...]).astype(LOW)
        second[...] = mm(later[0], far[...]).astype(LOW)

    @pl.when(z % 2 == 1)
    def _():
        first[...] = pair[...]
        second[...] = later[0]


def gain_kernel(ids, first, second, got_a, got_b, out, far):
    x, y, c, z = ids[0], ids[1], ids[2], ids[3]
    step = pl.program_id(0)
    size, part = far.shape

    @pl.when((step == 0) & (z < 2))
    def _():
        far[...] = got_a[...] + got_b[...]

    @pl.when((step == 0) & (z >= 2))
    def _():
        slab = (2 * y + c) * 2 + x
        column = lax.broadcasted_iota(jnp.int32, (size, part), 1) + slab * part
        row = lax.broadcasted_iota(jnp.int32, (size, part), 0)
        far[...] = jnp.where(row == column, 1.0, 0.0).astype(LOW)

    out[0] = mm(first[...], far[...]).astype(LOW)
    out[1] = mm(second[...], far[...]).astype(LOW)


def widen_kernel(ids, blocks, out):
    part = blocks.shape[2]
    for s in range(blocks.shape[0]):
        out[:, s * part : (s + 1) * part] = blocks[s].astype(WIDE)


def start_kernel(ids, e0, got, keep, p_ref, now, g1):
    step = pl.program_id(0)
    even = ids[0] == 0
    rows = e0.shape[1]
    cut = pl.ds(pl.multiple_of(step * rows, rows), rows)

    @pl.when((step == 0) & even)
    def _():
        g1[...] = got[...]

    @pl.when((step == 0) & jnp.logical_not(even))
    def _():
        g1[...] = keep[...].astype(LOW)

    p = mm(e0[0], g1[...])
    p_ref[...] = p

    @pl.when(even)
    def _():
        now[...] = (p + keep[cut, :]).astype(LOW)

    @pl.when(jnp.logical_not(even))
    def _():
        now[...] = (p + got[cut, :].astype(WIDE)).astype(LOW)


def hop_kernel(ids, pair, got, own, now):
    now[...] = (mm(pair[...], got[...]) + own[...].astype(WIDE)).astype(LOW)


def last_kernel(ids, pair, later, got_a, got_b, got_c, p_ref, keep, *refs):
    out, send, far = refs[-3:]
    even = ids[0] == 0

    @pl.when(pl.program_id(0) == 0)
    def _():
        far[...] = got_a[...] + got_b[...] + got_c[...]

    @pl.when(even)
    def _():
        out[...] = mm(pair[...], far[...]) + p_ref[...] + keep[...]
        send[...] = mm(later[0], far[...]).astype(LOW)

    @pl.when(jnp.logical_not(even))
    def _():
        out[...] = mm(later[0], far[...]) + keep[...]
        send[...] = (mm(pair[...], far[...]) + p_ref[...]).astype(LOW)


def add_kernel(ids, got, keep, into, out):
    out[...] = got[...].astype(WIDE) + keep[...]


def suffix(gains, spreads, offsets):
    x, y, c, z = (lax.axis_index(name) for name in ("x", "y", "c", "z"))
    even = x == 0
    gain, spread, offset = gains[0], spreads[0], offsets[0]
    rows, size_d = gain.shape
    part = rows // 2
    half = offset.shape[1] // 2
    chunks = 2
    width = half // chunks
    ids = jnp.stack([x, y, c, z]).astype(jnp.int32)
    slab = (2 * y + c) * 2 + x
    square = jax.ShapeDtypeStruct((size_d, size_d), LOW)

    e_low = gain.astype(LOW)
    e_x, e_y = swap(e_low, "x"), swap(e_low, "y")
    e_xy = jnp.concatenate([swap(e_x[:part], "y"), swap(e_y[part:], "x")], axis=0)
    pieces = [e_low, None, e_y, None, e_x, None, e_xy, None]
    for i in range(0, 8, 2):
        pieces[i + 1] = swap(pieces[i], "c")

    l_low = spread.astype(LOW)
    l_send = jnp.where(even, l_low[part:], l_low[:part])
    g_send = jnp.where(even, offset[:, half:], offset[:, :half]).astype(LOW)
    l_send, e_x = lax.optimization_barrier((l_send, e_x))
    g_send, e_xy = lax.optimization_barrier((g_send, e_xy))
    l_got = swap(l_send, "x")
    l_keep = jnp.where(even, spread[:part], spread[part:])
    l1_low = jnp.where(even, l_got, l_keep.astype(LOW))
    l0 = jnp.where(even, l_keep, l_got.astype(WIDE))
    g_got = [swap(g_send[:, i * width : (i + 1) * width], "x") for i in range(chunks)]

    both, a_e, n = call(
        pair_kernel, (1,), ids,
        [whole((rows, size_d))] * 8 + [whole((part, size_d))],
        [whole((2, size_d, size_d)), whole((size_d, size_d)), whole((8, part, rows))],
        [jax.ShapeDtypeStruct((2, size_d, size_d), LOW), square, jax.ShapeDtypeStruct((8, part, rows), LOW)],
        pieces + [l1_low],
        flops=2 * size_d**3, bytes_accessed=20 * size_d**2,
    )
    e0, e1 = both[0], both[1]
    n = exchange(n)
    a_l_rows = mm_atbt(n.reshape(size_d, rows), e0)
    a_l = lax.dynamic_slice_in_dim(a_l_rows, x * part, part, 0) + l0

    level = [(3, 2), (1, 0)]
    hold = size_d // 2
    e_half = lax.ppermute(lax.dynamic_slice_in_dim(a_e, c * hold, hold, 0), "z", level)
    tile = pl.BlockSpec((rows, size_d), lambda i, ids: (i, 0))
    tile0 = pl.BlockSpec((1, rows, size_d), lambda i, ids: (0, i, 0))
    tile1 = pl.BlockSpec((1, rows, size_d), lambda i, ids: (1, i, 0))
    c0_e, c1_e = call(
        compose_kernel, (4,), ids,
        [tile, tile1, whole((hold, size_d)), whole((hold, size_d))],
        [tile, tile], [square, square],
        [a_e, both, e_half, swap(e_half, "c")],
        scratch=[pltpu.VMEM((size_d, size_d), LOW)],
        flops=4 * size_d**3, bytes_accessed=12 * size_d**2,
    )
    e_slab = lax.dynamic_slice_in_dim(c0_e, slab * part, part, 1)
    got_a, got_b = lax.ppermute(e_slab, "z", [(2, 1)]), lax.ppermute(e_slab, "z", [(2, 0)])
    out = call(
        gain_kernel, (4,), ids,
        [tile, tile, whole((size_d, part)), whole((size_d, part))],
        pl.BlockSpec((2, rows, part), lambda i, ids: (i, 0, 0)),
        jax.ShapeDtypeStruct((8, rows, part), LOW),
        [c0_e, c1_e, got_a, got_b],
        scratch=[pltpu.VMEM((size_d, part), LOW)],
        flops=4 * size_d**2 * part, bytes_accessed=5 * size_d**2,
    )
    out_gain = call(
        widen_kernel, (1,), ids, [whole((8, rows, part))], whole((rows, size_d)),
        jax.ShapeDtypeStruct((rows, size_d), WIDE), [exchange(out)], bytes_accessed=6 * rows * size_d,
    )

    def for_rows(slab_rows, first, second):
        n = jnp.stack([mm_bt(slab_rows, first).astype(LOW), mm_bt(slab_rows, second).astype(LOW)])
        n = jnp.transpose(n.reshape(2, part, 4, rows), (2, 0, 1, 3)).reshape(8, part, rows)
        return exchange(n).reshape(size_d, rows)

    got = lax.ppermute(a_l.astype(LOW), "z", level)
    n = mm_bt(got, a_e).astype(LOW)
    n = exchange(jnp.transpose(n.reshape(part, 8, part), (1, 0, 2)))
    b_l = (mm_atbt(n.reshape(size_d, part), a_e) + a_l).astype(LOW)
    far = lax.ppermute(b_l, "z", [(2, 1)]) + lax.ppermute(b_l, "z", [(2, 0)])
    near = for_rows(got, a_e, e1)
    out_spread = mm_atbt(near, jnp.where(even, a_e, e1)) + jnp.where(even, a_l_rows, 0) + spread
    out_spread = mm_atbt(for_rows(far, c0_e, c1_e), jnp.where(even, c0_e, c1_e)) + out_spread

    column = jax.ShapeDtypeStruct((size_d, width), LOW)
    wide_column = jax.ShapeDtypeStruct((size_d, width), WIDE)
    block = pl.BlockSpec((rows, width), lambda i, ids: (i, 0))
    all_rows = whole((size_d, width))
    out_offset = None
    full = jax.ShapeDtypeStruct(offset.shape, WIDE)
    others = []
    for i in range(chunks):
        kept = pl.BlockSpec((rows, width), lambda s, ids, i=i: (s, ids[0] * chunks + i))
        kept_all = pl.BlockSpec((size_d, width), lambda s, ids, i=i: (0, ids[0] * chunks + i))
        p, own = call(
            start_kernel, (4,), ids, [tile0, all_rows, kept_all], [block, block], [wide_column, column],
            [both, g_got[i], offset], scratch=[pltpu.VMEM((size_d, width), LOW)],
            flops=2 * size_d**2 * width, bytes_accessed=2 * size_d**2 + 12 * size_d * width,
        )
        now, gots = own, []
        for source in (3, 2, 1):
            gots.append(lax.ppermute(now, "z", [(source, source - 1)]))
            if source > 1:
                now = call(
                    hop_kernel, (4,), ids, [tile, all_rows, block], block, column, [a_e, gots[-1], own],
                    flops=2 * size_d**2 * width, bytes_accessed=2 * size_d**2 + 6 * size_d * width,
                )
        extra = [] if out_offset is None else [out_offset]
        out_offset, other = call(
            last_kernel, (4,), ids,
            [tile, tile1, all_rows, all_rows, all_rows, block, kept] + [pl.BlockSpec(memory_space=pl.ANY)] * len(extra),
            [kept, block], [full, column],
            [a_e, both] + gots + [p, offset] + extra,
            scratch=[pltpu.VMEM((size_d, width), LOW)], aliases={8: 0} if extra else {},
            flops=4 * size_d**2 * width, bytes_accessed=4 * size_d**2 + 20 * size_d * width,
        )
        others.append(swap(other, "x"))
    for i in range(chunks):
        kept = pl.BlockSpec((rows, width), lambda s, ids, i=i: (s, (1 - ids[0]) * chunks + i))
        out_offset = call(
            add_kernel, (4,), ids, [block, kept, pl.BlockSpec(memory_space=pl.ANY)], kept, full,
            [others[i], offset, out_offset], aliases={3: 0}, bytes_accessed=10 * size_d * width,
        )
    return (out_gain[None], out_spread[None], out_offset[None])


def solution(mesh):
    steps, rows = mesh.shape["tm"], mesh.shape["rows"]
    if steps == 2**LEVELS and rows == 4:
        devices = mesh.devices.reshape(steps // 2, 2, 2, 2)
        mesh = Mesh(devices, ("z", "x", "y", "c"))
        by_row, by_column = P(("z", "x"), ("y", "c"), None), P(("z", "x"), None, ("y", "c"))
        body = suffix
    else:
        by_row, by_column = P("tm", "rows", None), P("tm", None, "rows")
        body = doubling
    return jax.shard_map(
        body,
        mesh=mesh,
        in_specs=(by_row, by_row, by_column),
        out_specs=(by_row, by_row, by_column),
        check_vma=False,
    )
```

time: 200 us -> 221 us (1.10)
  Pallas kernels: 0 us -> 56.6 us
  matrix products: 53.2 us -> 17.9 us
  waiting for transfers between devices: 33.2 us -> 50 us
  other arithmetic: 23.2 us -> 11.6 us
  local copies, waits for them, and re-layouts: 35.9 us -> 31.3 us
    pallas_call x0 -> x14, Pallas kernels: none -> 56.6 us  [call(): pl.pallas_call(kernel, grid_spec=pltpu.PrefetchScalarGridSpec(num_scalar_...]
    dot_general x15 -> x0, matrix products: 36.8 us -> none  [mm(): return jnp.dot(a, b, preferred_element_type=WIDE)]
    ppermute x12, waiting for transfers between devices: 7.18 us -> 27.9 us  [the longest x1 21.1 us: suffix(): got = lax.ppermute(a_l.astype(LOW), 'z', level)]
    select_n x3 -> x2, other arithmetic: 8.95 us -> 1.14 us  [the longest x1 1.06 us: suffix(): l_send = jnp.where(even, l_low[part:], l_low[:part])]
    dynamic_update_slice x7 -> x0, local copies, waits for them, and re-layouts: 6.83 us -> none  [suffix(): both = lax.dynamic_update_index_in_dim(both, piece, me ^ i, 0)]
    another operation x4 -> x8, local copies, waits for them, and re-layouts: 2.18 us -> 6.8 us  [for_rows(): jnp.stack([mm_bt(slab_rows, first).astype(LOW), mm_bt(slab_rows, second)....]
    unnamed x50 -> x59, local copies, waits for them, and re-layouts: 15.5 us -> 19.9 us
    broadcast_in_dim x3 -> x0, local copies, waits for them, and re-layouts: 3.4 us -> none  [the longest x1 2.55 us: suffix(): both = jnp.zeros((8, rows, size_d), LOW)]
  transfers between devices with their start and end apart: 30 -> 31, of which waited for: 7 -> 8; matrix products, arithmetic and copies ran while one was open for 54% -> 18% of each run, Pallas kernels for 0% -> 25%
where the time goes in v2:
time: 221 us; the launch traced here: 219 us
  Pallas kernels  56.6 us (26%)
  starting transfers between devices  50.6 us (23%)
  waiting for transfers between devices  50 us (23%)
  local copies, waits for them, and re-layouts  31.3 us (14%)
  matrix products  17.9 us (8%)
  other arithmetic  11.6 us (5%)
    pallas_call x14, Pallas kernels, call(): pl.pallas_call(kernel, grid_spec=pltpu.PrefetchScalarGridSpec(num_scalar_...  56.6 us
    ppermute x14, waiting for transfers between devices, swap(): return lax.ppermute(value, axis, [(0, 1), (1, 0)])  22.1 us
    ppermute x1, waiting for transfers between devices, suffix(): got = lax.ppermute(a_l.astype(LOW), 'z', level)  21.1 us
    all_to_all x5, starting transfers between devices, exchange(): return lax.all_to_all(blocks, GROUP, 0, 0)  20.7 us
    unnamed x59, local copies, waits for them, and re-layouts  19.9 us
    ppermute x14, starting transfers between devices, swap(): return lax.ppermute(value, axis, [(0, 1), (1, 0)])  12.4 us
    dot_general x4, matrix products, mm_atbt(): lax.dot_general(a, b, (((0,), (1,)), ((), ())), preferred_element_type=WIDE)  10.7 us
    ppermute x6, starting transfers between devices, suffix(): gots.append(lax.ppermute(now, 'z', [(source, source - 1)]))  9.72 us
  transfers between devices with their start and end apart: 31, of which 8 were waited for; matrix products, arithmetic and copies ran while one was open for 18% of the time, Pallas kernels for 25%

profile of v2, /device:TPU:16, one launch (start us, length us, event | category | flops | bytes accessed | tf_op | source)
XLA Modules:
  0.0 219.1 jit_solution(1970297187223032081)
XLA Ops:
  1.9 1.6 collective-permute-start.3
  5.0 3.4 %fusion = bf16[1024,512]{1,0:T(8,128)(2,1)} fusion(f32[1024,1024]{1,0:T(8,128)} %bitcast.63, pred[]{:T(512)S(6)} %eq.3), kind=kLoop, calls=%fused_computation.1 | loop fusion | flops 524288 | bytes 3145729 | tf_op jit(solution)/shard_map/convert_element_type | solution.py:225
  8.4 7.3 %collective-permute-done.3.refs_4_ = bf16[256,1024]{1,0:T(8,128)(2,1)S(1)} collective-permute-done((bf16[256,1024]{1,0:T(8,128)(2,1)S(1)}, bf16[256,1024]{1,0:T(8,128)(2,1)S(1)}, u32[]{:S(2)}, u32[]{:S(2)}) %collective-permute-start.3) | collective-permute-done | bytes 524320 | tf_op jit(solution)/shard_map/ppermute | solution.py:49
  18.9 1.6 collective-permute-start.6
  22.1 1.8 collective-permute-done.5
  23.8 2.0 collective-permute-done.6
  29.9 5.2 %collective-permute-done.8 = bf16[128,1024]{1,0:T(8,128)(2,1)S(1)} collective-permute-done((bf16[128,1024]{1,0:T(8,128)(2,1)S(1)}, bf16[128,1024]{1,0:T(8,128)(2,1)S(1)}, u32[]{:S(2)}, u32[]{:S(2)}) %collective-permute-start.8) | collective-permute-done | bytes 262176 | tf_op jit(solution)/shard_map/ppermute | solution.py:49
  38.8 3.7 %shard_map.58 = (bf16[2,1024,1024]{2,1,0:T(8,128)(2,1)S(1)}, bf16[1024,1024]{1,0:T(8,128)(2,1)S(1)}, bf16[8,128,256]{2,1,0:T(8,128)(2,1)S(1)}) custom-call(s32[4]{0:T(128)S(1)} %pad_add_fusion.ids, bf16[256,1024]{1,0:T(8,128)(2,1)S(1)} %convert_bitcast_fusion.refs_0_, bf16[256,1024]{1,0:T(8,128)(2,1)S(1)} %copy-done.23, bf16[256,1024]{1,0:T(8,128)(2,1)S(1)} %copy-done.21, ...), custom_call_target="tpu_custom_call" | custom-call | flops 2147483648 | bytes 20971520 | tf_op jit(solution)/shard_map/pallas_call | solution.py:72
  42.5 2.0 copy-done.3
  45.3 4.2 %all-to-all-start.1 = ((bf16[8,128,256]{2,1,0:T(8,128)(2,1)}), bf16[8,128,256]{2,1,0:T(8,128)(2,1)}, u32[]{:S(2)}, u32[]{:S(2)}) async-start(bf16[8,128,256]{2,1,0:T(8,128)(2,1)} %copy-done.17), calls=%async_computation.1 | async-start | bytes 1048576 | tf_op jit(solution)/shard_map/all_to_all | solution.py:68
  49.5 2.2 copy-done
  51.7 2.2 copy-done.4
  53.9 3.0 %shard_map.65 = (f32[1024,256]{1,0:T(8,128)S(1)}, bf16[1024,256]{1,0:T(8,128)(2,1)}) custom-call(s32[4]{0:T(128)S(1)} %pad_add_fusion.ids, bf16[2,1024,1024]{2,1,0:T(8,128)(2,1)S(1)} %copy-done.4, bf16[1024,256]{1,0:T(8,128)(2,1)S(1)} %collective-permute-done.20.got, f32[1024,1024]{1,0:T(8,128)S(1)} %bitcast.64), custom_call_target="tpu_custom_call" | custom-call | flops 536870912 | bytes 5242880 | tf_op jit(solution)/shard_map/pallas_call | solution.py:72
  59.1 3.9 %shard_map.62 = (f32[1024,256]{1,0:T(8,128)S(1)}, bf16[1024,256]{1,0:T(8,128)(2,1)}) custom-call(s32[4]{0:T(128)S(1)} %pad_add_fusion.ids, bf16[2,1024,1024]{2,1,0:T(8,128)(2,1)S(1)} %copy-done.4, bf16[1024,256]{1,0:T(8,128)(2,1)} %collective-permute-done.16.got, f32[1024,1024]{1,0:T(8,128)S(1)} %bitcast.65), custom_call_target="tpu_custom_call" | custom-call | flops 536870912 | bytes 5242880 | tf_op jit(solution)/shard_map/pallas_call | solution.py:72
  67.7 2.6 %fusion.4 = f32[256,1024]{1,0:T(8,128)S(1)} fusion(bf16[1024,256]{1,0:T(8,128)(2,1)} %bitcast.8, bf16[2,1024,1024]{2,1,0:T(8,128)(2,1)} %copy-done.3), kind=kOutput, calls=%fused_computation.6 | convolution fusion | flops 536870912 | bytes 3670016 | tf_op jit(solution)/shard_map/dot_general | solution.py:61
  72.8 1.9 collective-permute-done.21.got.got_a
  74.7 4.3 %shard_map.66 = bf16[1024,256]{1,0:T(8,128)(2,1)} custom-call(s32[4]{0:T(128)S(1)} %pad_add_fusion.ids, bf16[1024,1024]{1,0:T(8,128)(2,1)S(1)} %get-tuple-element.19.pair, bf16[1024,256]{1,0:T(8,128)(2,1)S(1)} %collective-permute-done.21.got.got_a, bf16[1024,256]{1,0:T(8,128)(2,1)} %get-tuple-element.27.own), custom_call_target="tpu_custom_call" | custom-call | flops 536870912 | bytes 3670016 | tf_op jit(solution)/shard_map/pallas_call | solution.py:72
  79.0 2.1 collective-permute-start.22
  81.1 4.8 %collective-permute-done.17.got.got_a = bf16[1024,256]{1,0:T(8,128)(2,1)S(1)} collective-permute-done((bf16[1024,256]{1,0:T(8,128)(2,1)}, bf16[1024,256]{1,0:T(8,128)(2,1)S(1)}, u32[]{:S(2)}, u32[]{:S(2)}) %collective-permute-start.17) | collective-permute-done | bytes 524320 | tf_op jit(solution)/shard_map/ppermute | solution.py:308
  85.9 4.3 %shard_map.63 = bf16[1024,256]{1,0:T(8,128)(2,1)} custom-call(s32[4]{0:T(128)S(1)} %pad_add_fusion.ids, bf16[1024,1024]{1,0:T(8,128)(2,1)S(1)} %get-tuple-element.19.pair, bf16[1024,256]{1,0:T(8,128)(2,1)S(1)} %collective-permute-done.17.got.got_a, bf16[1024,256]{1,0:T(8,128)(2,1)} %get-tuple-element.25.own), custom_call_target="tpu_custom_call" | custom-call | flops 536870912 | bytes 3670016 | tf_op jit(solution)/shard_map/pallas_call | solution.py:72
  90.2 2.1 collective-permute-start.18
  92.3 21.1 %collective-permute-done.13 = bf16[128,1024]{1,0:T(8,128)(2,1)S(1)} collective-permute-done((bf16[128,1024]{1,0:T(8,128)(2,1)S(1)}, bf16[128,1024]{1,0:T(8,128)(2,1)S(1)}, u32[]{:S(2)}, u32[]{:S(2)}) %collective-permute-start.13) | collective-permute-done | bytes 262176 | tf_op jit(solution)/shard_map/ppermute | solution.py:282
  115.8 4.1 %all-to-all-start.2 = ((bf16[8,128,128]{2,1,0:T(8,128)(2,1)}), bf16[8,128,128]{2,1,0:T(8,128)(2,1)}, u32[]{:S(2)}, u32[]{:S(2)}) async-start(bf16[8,128,128]{2,1,0:T(8,128)(2,1)} %bitcast_bitcast_fusion), calls=%async_computation.2 | async-start | bytes 524288 | tf_op jit(solution)/shard_map/all_to_all | solution.py:68
  119.9 3.2 %fusion.21 = bf16[128,1024]{1,0:T(8,128)(2,1)} fusion(bf16[128,1024]{1,0:T(8,128)(2,1)} %copy-done.27, bf16[2,1024,1024]{2,1,0:T(8,128)(2,1)} %copy-done.3), kind=kOutput, calls=%fused_computation.20 | convolution fusion | flops 268566528 | bytes 2621440 | tf_op jit(solution)/shard_map/dot_general | solution.py:57
  124.0 1.7 copy.12
  126.9 1.8 pad_maximum_fusion.1
  128.7 4.1 %all-to-all-start.4 = ((bf16[8,128,256]{2,1,0:T(8,128)(2,1)}), bf16[8,128,256]{2,1,0:T(8,128)(2,1)}, u32[]{:S(2)}, u32[]{:S(2)}) async-start(bf16[8,128,256]{2,1,0:T(8,128)(2,1)} %bitcast.72), calls=%async_computation.4 | async-start | bytes 1048576 | tf_op jit(solution)/shard_map/all_to_all | solution.py:68
  132.8 2.0 fusion.24
  137.5 4.8 %shard_map.67 = bf16[1024,256]{1,0:T(8,128)(2,1)} custom-call(s32[4]{0:T(128)S(1)} %pad_add_fusion.ids, bf16[1024,1024]{1,0:T(8,128)(2,1)S(1)} %get-tuple-element.19.pair, bf16[1024,256]{1,0:T(8,128)(2,1)} %collective-permute-done.22.got.got_b, bf16[1024,256]{1,0:T(8,128)(2,1)} %get-tuple-element.27.own), custom_call_target="tpu_custom_call" | custom-call | flops 536870912 | bytes 3670016 | tf_op jit(solution)/shard_map/pallas_call | solution.py:72
  143.7 4.5 %shard_map.64 = bf16[1024,256]{1,0:T(8,128)(2,1)} custom-call(s32[4]{0:T(128)S(1)} %pad_add_fusion.ids, bf16[1024,1024]{1,0:T(8,128)(2,1)S(1)} %get-tuple-element.19.pair, bf16[1024,256]{1,0:T(8,128)(2,1)} %collective-permute-done.18.got.got_b, bf16[1024,256]{1,0:T(8,128)(2,1)} %get-tuple-element.25.own), custom_call_target="tpu_custom_call" | custom-call | flops 536870912 | bytes 3670016 | tf_op jit(solution)/shard_map/pallas_call | solution.py:72
  149.7 7.3 %shard_map.59 = (bf16[1024,1024]{1,0:T(8,128)(2,1)S(1)}, bf16[1024,1024]{1,0:T(8,128)(2,1)S(1)}) custom-call(s32[4]{0:T(128)S(1)} %pad_add_fusion.ids, bf16[1024,1024]{1,0:T(8,128)(2,1)S(1)} %get-tuple-element.19.pair, bf16[2,1024,1024]{2,1,0:T(8,128)(2,1)S(1)} %copy-done.5, bf16[512,1024]{1,0:T(8,128)(2,1)} %collective-permute-done.9.half_ref, ...), custom_call_target="tpu_custom_call" | custom-call | flops 4294967296 | bytes 12582912 | tf_op jit(solution)/shard_map/pallas_call | solution.py:72
  158.4 1.5 convolution_convert_fusion.1
  159.9 1.5 convolution_convert_fusion
  164.5 1.8 pad_maximum_fusion
  166.3 4.2 %all-to-all-start.3 = ((bf16[8,128,256]{2,1,0:T(8,128)(2,1)}), bf16[8,128,256]{2,1,0:T(8,128)(2,1)}, u32[]{:S(2)}, u32[]{:S(2)}) async-start(bf16[8,128,256]{2,1,0:T(8,128)(2,1)} %bitcast.71), calls=%async_computation.3 | async-start | bytes 1048576 | tf_op jit(solution)/shard_map/all_to_all | solution.py:68
  174.1 2.2 copy-done.1
  176.3 2.2 copy-done.6
  179.7 4.8 %shard_map.68 = (f32[1024,1024]{1,0:T(8,128)}, bf16[1024,256]{1,0:T(8,128)(2,1)}) custom-call(s32[4]{0:T(128)S(1)} %pad_add_fusion.ids, bf16[1024,1024]{1,0:T(8,128)(2,1)S(1)} %get-tuple-element.19.pair, bf16[2,1024,1024]{2,1,0:T(8,128)(2,1)S(1)} %copy-done.6, bf16[1024,256]{1,0:T(8,128)(2,1)S(1)} %collective-permute-done.21.got.got_a, ...), custom_call_target="tpu_custom_call" | custom-call | flops 1073741824 | bytes 9437184 | tf_op jit(solution)/shard_map/pallas_call | solution.py:72
  184.5 2.0 collective-permute-start.25
  186.6 5.1 %shard_map.69 = (f32[1024,1024]{1,0:T(8,128)}, bf16[1024,256]{1,0:T(8,128)(2,1)}) custom-call(s32[4]{0:T(128)S(1)} %pad_add_fusion.ids, bf16[1024,1024]{1,0:T(8,128)(2,1)S(1)} %get-tuple-element.19.pair, bf16[2,1024,1024]{2,1,0:T(8,128)(2,1)S(1)} %copy-done.6, ...), custom_call_target="tpu_custom_call", output_to_operand_aliasing={{0}: (8, {})} | custom-call | flops 1073741824 | bytes 9437184 | tf_op jit(solution)/shard_map/pallas_call | solution.py:72
  191.7 3.2 %shard_map.60 = bf16[8,256,128]{2,1,0:T(8,128)(2,1)} custom-call(s32[4]{0:T(128)S(1)} %pad_add_fusion.ids, bf16[1024,1024]{1,0:T(8,128)(2,1)S(1)} %copy-done.8, bf16[1024,1024]{1,0:T(8,128)(2,1)S(1)} %copy-done.11, bf16[1024,128]{1,0:T(8,128)(2,1)S(1)} %collective-permute-done.11.got_a, bf16[1024,128]{1,0:T(8,128)(2,1)S(1)} %collective-permute-done.12.got_b), custom_call_target="tpu_custom_call" | custom-call | flops 536870912 | bytes 5242880 | tf_op jit(solution)/shard_map/pallas_call | solution.py:72
  195.0 4.2 %all-to-all-start = ((bf16[8,256,128]{2,1,0:T(8,128)(2,1)}), bf16[8,256,128]{2,1,0:T(8,128)(2,1)S(1)}, u32[]{:S(2)}, u32[]{:S(2)}) async-start(bf16[8,256,128]{2,1,0:T(8,128)(2,1)} %shard_map.60), calls=%async_computation | async-start | bytes 1048576 | tf_op jit(solution)/shard_map/all_to_all | solution.py:68
  199.1 3.4 %fusion.20 = f32[256,1024]{1,0:T(8,128)S(1)} fusion(bf16[1024,256]{1,0:T(8,128)(2,1)} %bitcast.18, bf16[1024,1024]{1,0:T(8,128)(2,1)S(1)} %get-tuple-element.19.pair, pred[]{:T(512)S(6)} %eq.3, bf16[2,1024,1024]{2,1,0:T(8,128)(2,1)} %copy-done.3, f32[1,256,1024]{2,1,0:T(8,128)} %param.4, f32[256,1024]{1,0:T(8,128)} %copy-done.28), kind=kOutput, calls=%fused_computation.18 | convolution fusion | flops 538705920 | bytes 7865344 | tf_op jit(solution)/shard_map/dot_general | solution.py:61
  202.7 2.2 shard_map.70.into
  204.9 5.9 %collective-permute-done.24.got = bf16[1024,256]{1,0:T(8,128)(2,1)} collective-permute-done((bf16[1024,256]{1,0:T(8,128)(2,1)}, bf16[1024,256]{1,0:T(8,128)(2,1)}, u32[]{:S(2)}, u32[]{:S(2)}) %collective-permute-start.24) | collective-permute-done | bytes 524320 | tf_op jit(solution)/shard_map/ppermute | solution.py:49
  210.8 3.8 %shard_map.71 = f32[1024,1024]{1,0:T(8,128)} custom-call(s32[4]{0:T(128)S(1)} %pad_add_fusion.ids, bf16[1024,256]{1,0:T(8,128)(2,1)} %collective-permute-done.24.got, f32[1024,1024]{1,0:T(8,128)S(1)} %bitcast.69, f32[1024,1024]{1,0:T(8,128)} %shard_map.70.into), custom_call_target="tpu_custom_call", output_to_operand_aliasing={{}: (3, {})} | custom-call | bytes 2621440 | tf_op jit(solution)/shard_map/pallas_call | solution.py:72
  214.6 2.8 %fusion.16 = f32[1,256,1024]{2,1,0:T(8,128)} fusion(f32[256,1024]{1,0:T(8,128)S(1)} %fusion.20, bf16[1024,256]{1,0:T(8,128)(2,1)} %bitcast.14, bf16[1024,1024]{1,0:T(8,128)(2,1)S(1)} %copy-done.9, bf16[1024,1024]{1,0:T(8,128)(2,1)S(1)} %copy-done.12, pred[]{:T(512)S(6)} %eq.3), kind=kOutput, calls=%fused_computation.16 | convolution fusion | flops 538181632 | bytes 6815745 | tf_op jit(solution)/shard_map/dot_general | solution.py:61
  217.5 1.6 shard_map.61
  (119 shorter events, 44.9 us)
Async XLA Ops:
  1.9 16.0 %copy-start.24 = (f32[1,256,1024]{2,1,0:T(8,128)S(1)}, f32[1,256,1024]{2,1,0:T(8,128)}, u32[]{:S(2)}) copy-start(f32[1,256,1024]{2,1,0:T(8,128)} %param.4) | copy-start | bytes 3145732
  1.9 13.7 %collective-permute-start.3 = (bf16[256,1024]{1,0:T(8,128)(2,1)S(1)}, bf16[256,1024]{1,0:T(8,128)(2,1)S(1)}, u32[]{:S(2)}, u32[]{:S(2)}) collective-permute-start(bf16[256,1024]{1,0:T(8,128)(2,1)S(1)} %convert_bitcast_fusion.refs_0_), channel_id=1, source_target_pairs={{0,4},{4,0},{1,5},{5,1},{2,6},{6,2},{3,7},{7,3},{8,12},{12,8},{9,1... | collective-permute-start | bytes 1572872 | tf_op jit(solution)/shard_map/ppermute | solution.py:49
  3.5 15.3 %collective-permute-start.1 = (bf16[256,1024]{1,0:T(8,128)(2,1)S(1)}, bf16[256,1024]{1,0:T(8,128)(2,1)S(1)}, u32[]{:S(2)}, u32[]{:S(2)}) collective-permute-start(bf16[256,1024]{1,0:T(8,128)(2,1)S(1)} %convert_bitcast_fusion.refs_0_), channel_id=1, source_target_pairs={{0,2},{2,0},{1,3},{3,1},{4,6},{6,4},{5,7},{7,5},{8,10},{10,8},{9,1... | collective-permute-start | bytes 1572872 | tf_op jit(solution)/shard_map/ppermute | solution.py:49
  5.0 23.6 %collective-permute-start = (bf16[256,1024]{1,0:T(8,128)(2,1)S(1)}, bf16[256,1024]{1,0:T(8,128)(2,1)S(1)}, u32[]{:S(2)}, u32[]{:S(2)}) collective-permute-start(bf16[256,1024]{1,0:T(8,128)(2,1)S(1)} %convert_bitcast_fusion.refs_0_), channel_id=1, source_target_pairs={{0,1},{1,0},{2,3},{3,2},{4,5},{5,4},{6,7},{7,6},{8,9},{9,8},{10,11... | collective-permute-start | bytes 1572872 | tf_op jit(solution)/shard_map/ppermute | solution.py:49
  15.7 10.2 %copy-start.18 = (bf16[256,1024]{1,0:T(8,128)(2,1)}, bf16[256,1024]{1,0:T(8,128)(2,1)S(1)}, u32[]{:S(2)}) copy-start(bf16[256,1024]{1,0:T(8,128)(2,1)S(1)} %collective-permute-done.3.refs_4_) | copy-start | bytes 1572868
  16.4 7.4 %collective-permute-start.5 = (bf16[128,1024]{1,0:T(8,128)(2,1)}, bf16[128,1024]{1,0:T(8,128)(2,1)S(1)}, u32[]{:S(2)}, u32[]{:S(2)}) collective-permute-start(bf16[128,1024]{1,0:T(8,128)(2,1)} %slice.50), channel_id=1, source_target_pairs={{0,2},{2,0},{1,3},{3,1},{4,6},{6,4},{5,7},{7,5},{8,10},{10,8},{9,1... | collective-permute-start | bytes 786440 | tf_op jit(solution)/shard_map/ppermute | solution.py:49
  18.8 8.7 %copy-start.26 = (bf16[1024,512]{1,0:T(8,128)(2,1)S(1)}, bf16[1024,512]{1,0:T(8,128)(2,1)}, u32[]{:S(2)}) copy-start(bf16[1024,512]{1,0:T(8,128)(2,1)} %fusion) | copy-start | bytes 3145732
  18.8 9.7 %copy-start.20 = (bf16[256,1024]{1,0:T(8,128)(2,1)}, bf16[256,1024]{1,0:T(8,128)(2,1)S(1)}, u32[]{:S(2)}) copy-start(bf16[256,1024]{1,0:T(8,128)(2,1)S(1)} %collective-permute-done.1.refs_2_) | copy-start | bytes 1572868
  18.9 7.0 %collective-permute-start.6 = (bf16[128,1024]{1,0:T(8,128)(2,1)S(1)}, bf16[128,1024]{1,0:T(8,128)(2,1)S(1)}, u32[]{:S(2)}, u32[]{:S(2)}) collective-permute-start(bf16[128,1024]{1,0:T(8,128)(2,1)S(1)} %slice.51), channel_id=1, source_target_pairs={{0,4},{4,0},{1,5},{5,1},{2,6},{6,2},{3,7},{7,3},{8,12},{12,8},{9,1... | collective-permute-start | bytes 786440 | tf_op jit(solution)/shard_map/ppermute | solution.py:49
  21.5 15.2 %collective-permute-start.4 = (bf16[256,1024]{1,0:T(8,128)(2,1)S(1)}, bf16[256,1024]{1,0:T(8,128)(2,1)S(1)}, u32[]{:S(2)}, u32[]{:S(2)}) collective-permute-start(bf16[256,1024]{1,0:T(8,128)(2,1)S(1)} %collective-permute-done.3.refs_4_), channel_id=1, source_target_pairs={{0,1},{1,0},{2,3},{3,2},{4,5},{5,4},{6,7},{7,6},{8,9},{9,8},{10,11... | collective-permute-start | bytes 1572872 | tf_op jit(solution)/shard_map/ppermute | solution.py:49
  21.6 15.2 %collective-permute-start.2 = (bf16[256,1024]{1,0:T(8,128)(2,1)S(1)}, bf16[256,1024]{1,0:T(8,128)(2,1)S(1)}, u32[]{:S(2)}, u32[]{:S(2)}) collective-permute-start(bf16[256,1024]{1,0:T(8,128)(2,1)S(1)} %collective-permute-done.1.refs_2_), channel_id=1, source_target_pairs={{0,1},{1,0},{2,3},{3,2},{4,5},{5,4},{6,7},{7,6},{8,9},{9,8},{10,11... | collective-permute-start | bytes 1572872 | tf_op jit(solution)/shard_map/ppermute | solution.py:49
  25.9 10.9 %collective-permute-start.7 = (bf16[256,1024]{1,0:T(8,128)(2,1)S(1)}, bf16[256,1024]{1,0:T(8,128)(2,1)S(1)}, u32[]{:S(2)}, u32[]{:S(2)}) collective-permute-start(bf16[256,1024]{1,0:T(8,128)(2,1)S(1)} %constant_dynamic-update-slice_fusion.refs_6_), channel_id=1, source_target_pairs={{0,1},{1,0},{2,3},{3,2},{4,5},{5,4},{6,7},{7,6},{8,9},{9,8},{10,11... | collective-permute-start | bytes 1572872 | tf_op jit(solution)/shard_map/ppermute | solution.py:49
  25.9 10.8 %copy-start.19 = (bf16[256,1024]{1,0:T(8,128)(2,1)S(1)}, bf16[256,1024]{1,0:T(8,128)(2,1)}, u32[]{:S(2)}) copy-start(bf16[256,1024]{1,0:T(8,128)(2,1)} %copy-done.18) | copy-start | bytes 1572868
  26.0 9.1 %collective-permute-start.8 = (bf16[128,1024]{1,0:T(8,128)(2,1)S(1)}, bf16[128,1024]{1,0:T(8,128)(2,1)S(1)}, u32[]{:S(2)}, u32[]{:S(2)}) collective-permute-start(bf16[128,1024]{1,0:T(8,128)(2,1)S(1)} %slice_select_fusion.2), channel_id=1, source_target_pairs={{0,4},{4,0},{1,5},{5,1},{2,6},{6,2},{3,7},{7,3},{8,12},{12,8},{9,1... | collective-permute-start | bytes 786440 | tf_op jit(solution)/shard_map/ppermute | solution.py:49
  29.4 20.1 %collective-permute-start.20 = (bf16[1024,256]{1,0:T(8,128)(2,1)}, bf16[1024,256]{1,0:T(8,128)(2,1)S(1)}, u32[]{:S(2)}, u32[]{:S(2)}) collective-permute-start(bf16[1024,256]{1,0:T(8,128)(2,1)} %get-tuple-element.35), channel_id=1, source_target_pairs={{0,4},{4,0},{1,5},{5,1},{2,6},{6,2},{3,7},{7,3},{8,12},{12,8},{9,1... | collective-permute-start | bytes 1572872 | tf_op jit(solution)/shard_map/ppermute | solution.py:49
  35.1 24.0 %collective-permute-start.16 = (bf16[1024,256]{1,0:T(8,128)(2,1)}, bf16[1024,256]{1,0:T(8,128)(2,1)}, u32[]{:S(2)}, u32[]{:S(2)}) collective-permute-start(bf16[1024,256]{1,0:T(8,128)(2,1)} %get-tuple-element.36), channel_id=1, source_target_pairs={{0,4},{4,0},{1,5},{5,1},{2,6},{6,2},{3,7},{7,3},{8,12},{12,8},{9,1... | collective-permute-start | bytes 1572872 | tf_op jit(solution)/shard_map/ppermute | solution.py:49
  45.3 22.4 %all-to-all-start.1 = ((bf16[8,128,256]{2,1,0:T(8,128)(2,1)}), bf16[8,128,256]{2,1,0:T(8,128)(2,1)}, u32[]{:S(2)}, u32[]{:S(2)}) async-start(bf16[8,128,256]{2,1,0:T(8,128)(2,1)} %copy-done.17), calls=%async_computation.1 | async-start | bytes 1048576 | tf_op jit(solution)/shard_map/all_to_all | solution.py:68
  49.5 2.2 %copy-start = (f32[1,1024,1024]{2,1,0:T(8,128)S(1)}, f32[1,1024,1024]{2,1,0:T(8,128)}, u32[]{:S(2)}) copy-start(f32[1,1024,1024]{2,1,0:T(8,128)} %param.5) | copy-start | bytes 12582916
  57.8 16.8 %collective-permute-start.21 = (bf16[1024,256]{1,0:T(8,128)(2,1)}, bf16[1024,256]{1,0:T(8,128)(2,1)S(1)}, u32[]{:S(2)}, u32[]{:S(2)}) collective-permute-start(bf16[1024,256]{1,0:T(8,128)(2,1)} %get-tuple-element.27.own), channel_id=1, source_target_pairs={{24,16},{25,17},{26,18},{27,19},{28,20},{29,21},{30,22},{31,23}} | collective-permute-start | bytes 1572872 | tf_op jit(solution)/shard_map/ppermute | solution.py:308
  64.0 21.9 %collective-permute-start.17 = (bf16[1024,256]{1,0:T(8,128)(2,1)}, bf16[1024,256]{1,0:T(8,128)(2,1)S(1)}, u32[]{:S(2)}, u32[]{:S(2)}) collective-permute-start(bf16[1024,256]{1,0:T(8,128)(2,1)} %get-tuple-element.25.own), channel_id=1, source_target_pairs={{24,16},{25,17},{26,18},{27,19},{28,20},{29,21},{30,22},{31,23}} | collective-permute-start | bytes 1572872 | tf_op jit(solution)/shard_map/ppermute | solution.py:308
  66.4 48.6 %collective-permute-start.9 = (bf16[512,1024]{1,0:T(8,128)(2,1)}, bf16[512,1024]{1,0:T(8,128)(2,1)}, u32[]{:S(2)}, u32[]{:S(2)}) collective-permute-start(bf16[512,1024]{1,0:T(8,128)(2,1)} %constant_dynamic-slice_fusion.1), channel_id=1, source_target_pairs={{24,16},{8,0},{25,17},{9,1},{26,18},{10,2},{27,19},{11,3},{28,20},... | collective-permute-start | bytes 3145736 | tf_op jit(solution)/shard_map/ppermute | solution.py:249
  67.7 2.6 %copy-start.25 = (f32[1,256,1024]{2,1,0:T(8,128)S(1)}, f32[1,256,1024]{2,1,0:T(8,128)}, u32[]{:S(2)}) copy-start(f32[1,256,1024]{2,1,0:T(8,128)} %param.4) | copy-start | bytes 3145732
  71.5 42.0 %collective-permute-start.13 = (bf16[128,1024]{1,0:T(8,128)(2,1)S(1)}, bf16[128,1024]{1,0:T(8,128)(2,1)S(1)}, u32[]{:S(2)}, u32[]{:S(2)}) collective-permute-start(bf16[128,1024]{1,0:T(8,128)(2,1)S(1)} %get-tuple-element.33), channel_id=1, source_target_pairs={{24,16},{8,0},{25,17},{9,1},{26,18},{10,2},{27,19},{11,3},{28,20},... | collective-permute-start | bytes 786440 | tf_op jit(solution)/shard_map/ppermute | solution.py:282
  79.0 58.5 %collective-permute-start.22 = (bf16[1024,256]{1,0:T(8,128)(2,1)}, bf16[1024,256]{1,0:T(8,128)(2,1)}, u32[]{:S(2)}, u32[]{:S(2)}) collective-permute-start(bf16[1024,256]{1,0:T(8,128)(2,1)} %shard_map.66), channel_id=1, source_target_pairs={{16,8},{17,9},{18,10},{19,11},{20,12},{21,13},{22,14},{23,15}} | collective-permute-start | bytes 1572872 | tf_op jit(solution)/shard_map/ppermute | solution.py:308
  90.2 53.5 %collective-permute-start.18 = (bf16[1024,256]{1,0:T(8,128)(2,1)}, bf16[1024,256]{1,0:T(8,128)(2,1)}, u32[]{:S(2)}, u32[]{:S(2)}) collective-permute-start(bf16[1024,256]{1,0:T(8,128)(2,1)} %shard_map.63), channel_id=1, source_target_pairs={{16,8},{17,9},{18,10},{19,11},{20,12},{21,13},{22,14},{23,15}} | collective-permute-start | bytes 1572872 | tf_op jit(solution)/shard_map/ppermute | solution.py:308
  115.0 34.6 %collective-permute-start.10 = (bf16[512,1024]{1,0:T(8,128)(2,1)}, bf16[512,1024]{1,0:T(8,128)(2,1)}, u32[]{:S(2)}, u32[]{:S(2)}) collective-permute-start(bf16[512,1024]{1,0:T(8,128)(2,1)} %collective-permute-done.9.half_ref), channel_id=1, source_target_pairs={{0,1},{1,0},{2,3},{3,2},{4,5},{5,4},{6,7},{7,6},{8,9},{9,8},{10,11... | collective-permute-start | bytes 3145736 | tf_op jit(solution)/shard_map/ppermute | solution.py:49
  115.8 12.8 %all-to-all-start.2 = ((bf16[8,128,128]{2,1,0:T(8,128)(2,1)}), bf16[8,128,128]{2,1,0:T(8,128)(2,1)}, u32[]{:S(2)}, u32[]{:S(2)}) async-start(bf16[8,128,128]{2,1,0:T(8,128)(2,1)} %bitcast_bitcast_fusion), calls=%async_computation.2 | async-start | bytes 524288 | tf_op jit(solution)/shard_map/all_to_all | solution.py:68
  128.7 37.7 %all-to-all-start.4 = ((bf16[8,128,256]{2,1,0:T(8,128)(2,1)}), bf16[8,128,256]{2,1,0:T(8,128)(2,1)}, u32[]{:S(2)}, u32[]{:S(2)}) async-start(bf16[8,128,256]{2,1,0:T(8,128)(2,1)} %bitcast.72), calls=%async_computation.4 | async-start | bytes 1048576 | tf_op jit(solution)/shard_map/all_to_all | solution.py:68
  134.8 22.2 %collective-permute-start.14 = (bf16[128,1024]{1,0:T(8,128)(2,1)S(1)}, bf16[128,1024]{1,0:T(8,128)(2,1)S(1)}, u32[]{:S(2)}, u32[]{:S(2)}) collective-permute-start(bf16[128,1024]{1,0:T(8,128)(2,1)S(1)} %fusion.24), channel_id=1, source_target_pairs={{16,8},{17,9},{18,10},{19,11},{20,12},{21,13},{22,14},{23,15}} | collective-permute-start | bytes 786440 | tf_op jit(solution)/shard_map/ppermute | solution.py:286
  136.1 20.9 %collective-permute-start.15 = (bf16[128,1024]{1,0:T(8,128)(2,1)S(1)}, bf16[128,1024]{1,0:T(8,128)(2,1)S(1)}, u32[]{:S(2)}, u32[]{:S(2)}) collective-permute-start(bf16[128,1024]{1,0:T(8,128)(2,1)S(1)} %fusion.24), channel_id=1, source_target_pairs={{16,0},{17,1},{18,2},{19,3},{20,4},{21,5},{22,6},{23,7}} | collective-permute-start | bytes 786440 | tf_op jit(solution)/shard_map/ppermute | solution.py:286
  137.4 12.2 %copy-start.5 = (bf16[2,1024,1024]{2,1,0:T(8,128)(2,1)S(1)}, bf16[2,1024,1024]{2,1,0:T(8,128)(2,1)}, u32[]{:S(2)}) copy-start(bf16[2,1024,1024]{2,1,0:T(8,128)(2,1)} %copy-done.3) | copy-start | bytes 12582916
  142.2 31.9 %collective-permute-start.23 = (bf16[1024,256]{1,0:T(8,128)(2,1)}, bf16[1024,256]{1,0:T(8,128)(2,1)}, u32[]{:S(2)}, u32[]{:S(2)}) collective-permute-start(bf16[1024,256]{1,0:T(8,128)(2,1)} %shard_map.67), channel_id=1, source_target_pairs={{8,0},{9,1},{10,2},{11,3},{12,4},{13,5},{14,6},{15,7}} | collective-permute-start | bytes 1572872 | tf_op jit(solution)/shard_map/ppermute | solution.py:308
  148.2 38.3 %collective-permute-start.19 = (bf16[1024,256]{1,0:T(8,128)(2,1)}, bf16[1024,256]{1,0:T(8,128)(2,1)}, u32[]{:S(2)}, u32[]{:S(2)}) collective-permute-start(bf16[1024,256]{1,0:T(8,128)(2,1)} %shard_map.64), channel_id=1, source_target_pairs={{8,0},{9,1},{10,2},{11,3},{12,4},{13,5},{14,6},{15,7}} | collective-permute-start | bytes 1572872 | tf_op jit(solution)/shard_map/ppermute | solution.py:308
  157.0 2.9 %copy-start.10 = (bf16[1024,1024]{1,0:T(8,128)(2,1)}, bf16[1024,1024]{1,0:T(8,128)(2,1)S(1)}, u32[]{:S(2)}) copy-start(bf16[1024,1024]{1,0:T(8,128)(2,1)S(1)} %get-tuple-element.22.second) | copy-start | bytes 6291460
  166.3 28.6 %all-to-all-start.3 = ((bf16[8,128,256]{2,1,0:T(8,128)(2,1)}), bf16[8,128,256]{2,1,0:T(8,128)(2,1)}, u32[]{:S(2)}, u32[]{:S(2)}) async-start(bf16[8,128,256]{2,1,0:T(8,128)(2,1)} %bitcast.71), calls=%async_computation.3 | async-start | bytes 1048576 | tf_op jit(solution)/shard_map/all_to_all | solution.py:68
  171.5 20.2 %collective-permute-start.11 = (bf16[1024,128]{1,0:T(8,128)(2,1)S(1)}, bf16[1024,128]{1,0:T(8,128)(2,1)S(1)}, u32[]{:S(2)}, u32[]{:S(2)}) collective-permute-start(bf16[1024,128]{1,0:T(8,128)(2,1)S(1)} %constant_dynamic-slice_fusion), channel_id=1, source_target_pairs={{16,8},{17,9},{18,10},{19,11},{20,12},{21,13},{22,14},{23,15}} | collective-permute-start | bytes 786440 | tf_op jit(solution)/shard_map/ppermute | solution.py:262
  172.8 18.9 %collective-permute-start.12 = (bf16[1024,128]{1,0:T(8,128)(2,1)S(1)}, bf16[1024,128]{1,0:T(8,128)(2,1)S(1)}, u32[]{:S(2)}, u32[]{:S(2)}) collective-permute-start(bf16[1024,128]{1,0:T(8,128)(2,1)S(1)} %constant_dynamic-slice_fusion), channel_id=1, source_target_pairs={{16,0},{17,1},{18,2},{19,3},{20,4},{21,5},{22,6},{23,7}} | collective-permute-start | bytes 786440 | tf_op jit(solution)/shard_map/ppermute | solution.py:262
  174.1 2.2 %copy-start.1 = (f32[1,1024,1024]{2,1,0:T(8,128)S(1)}, f32[1,1024,1024]{2,1,0:T(8,128)}, u32[]{:S(2)}) copy-start(f32[1,1024,1024]{2,1,0:T(8,128)} %param.5) | copy-start | bytes 12582916
  176.3 2.2 copy-start.6
  179.7 6.8 %copy-start.14 = (f32[1024,256]{1,0:T(8,128)S(1)}, f32[1024,256]{1,0:T(8,128)}, u32[]{:S(2)}) copy-start(f32[1024,256]{1,0:T(8,128)} %copy-done.13) | copy-start | bytes 3145732
  184.5 18.0 %collective-permute-start.25 = (bf16[1024,256]{1,0:T(8,128)(2,1)}, bf16[1024,256]{1,0:T(8,128)(2,1)S(1)}, u32[]{:S(2)}, u32[]{:S(2)}) collective-permute-start(bf16[1024,256]{1,0:T(8,128)(2,1)} %get-tuple-element.31), channel_id=1, source_target_pairs={{0,4},{4,0},{1,5},{5,1},{2,6},{6,2},{3,7},{7,3},{8,12},{12,8},{9,1... | collective-permute-start | bytes 1572872 | tf_op jit(solution)/shard_map/ppermute | solution.py:49
  186.5 5.2 %copy-start.8 = (bf16[1024,1024]{1,0:T(8,128)(2,1)S(1)}, bf16[1024,1024]{1,0:T(8,128)(2,1)}, u32[]{:S(2)}) copy-start(bf16[1024,1024]{1,0:T(8,128)(2,1)} %copy-done.7) | copy-start | bytes 6291460
  186.6 5.2 %copy-start.11 = (bf16[1024,1024]{1,0:T(8,128)(2,1)S(1)}, bf16[1024,1024]{1,0:T(8,128)(2,1)}, u32[]{:S(2)}) copy-start(bf16[1024,1024]{1,0:T(8,128)(2,1)} %copy-done.10) | copy-start | bytes 6291460
  191.7 19.1 %collective-permute-start.24 = (bf16[1024,256]{1,0:T(8,128)(2,1)}, bf16[1024,256]{1,0:T(8,128)(2,1)}, u32[]{:S(2)}, u32[]{:S(2)}) collective-permute-start(bf16[1024,256]{1,0:T(8,128)(2,1)} %get-tuple-element.30), channel_id=1, source_target_pairs={{0,4},{4,0},{1,5},{5,1},{2,6},{6,2},{3,7},{7,3},{8,12},{12,8},{9,1... | collective-permute-start | bytes 1572872 | tf_op jit(solution)/shard_map/ppermute | solution.py:49
  195.0 22.5 %all-to-all-start = ((bf16[8,256,128]{2,1,0:T(8,128)(2,1)}), bf16[8,256,128]{2,1,0:T(8,128)(2,1)S(1)}, u32[]{:S(2)}, u32[]{:S(2)}) async-start(bf16[8,256,128]{2,1,0:T(8,128)(2,1)} %shard_map.60), calls=%async_computation | async-start | bytes 1048576 | tf_op jit(solution)/shard_map/all_to_all | solution.py:68
  199.1 3.6 %copy-start.2 = (f32[1,1024,1024]{2,1,0:T(8,128)S(1)}, f32[1,1024,1024]{2,1,0:T(8,128)}, u32[]{:S(2)}) copy-start(f32[1,1024,1024]{2,1,0:T(8,128)} %param.5) | copy-start | bytes 12582916
  204.9 9.7 %copy-start.9 = (bf16[1024,1024]{1,0:T(8,128)(2,1)S(1)}, bf16[1024,1024]{1,0:T(8,128)(2,1)}, u32[]{:S(2)}) copy-start(bf16[1024,1024]{1,0:T(8,128)(2,1)} %copy-done.7) | copy-start | bytes 6291460
  204.9 9.7 %copy-start.12 = (bf16[1024,1024]{1,0:T(8,128)(2,1)S(1)}, bf16[1024,1024]{1,0:T(8,128)(2,1)}, u32[]{:S(2)}) copy-start(bf16[1024,1024]{1,0:T(8,128)(2,1)} %copy-done.10) | copy-start | bytes 6291460
  (12 other events, 14.3 us)

commit v3 on v1

v3 whole, which is shorter than its diff:
```python
import jax
import jax.numpy as jnp
from jax import lax
from jax.experimental import pallas as pl
from jax.experimental.pallas import tpu as pltpu
from jax.sharding import Mesh, PartitionSpec as P

LEVELS = 3
LOW = jnp.bfloat16
WIDE = jnp.float32
MIB = 2**20


def shifted(value, axis, steps):
    count = lax.axis_size(axis)
    first, last = (max(0, -steps), min(count, count - steps))
    return lax.ppermute(value, axis, [(source, source + steps) for source in range(first, last)])


def doubling(gains, spreads, offsets):
    gain = gains[0]
    spread = spreads[0]
    offset = offsets[0]
    size_d = gain.shape[1]
    identity = jnp.eye(size_d, dtype=LOW)
    for section_number in range(LEVELS):
        distance = 2**section_number
        beyond = lax.axis_index("tm") + distance >= lax.axis_size("tm")
        own_gain = gain.astype(LOW)
        own_spread = spread.astype(LOW)
        own_offset = offset.astype(LOW)
        own_full = lax.all_gather(own_gain, "rows", axis=0, tiled=True)
        spread_full = lax.all_gather(own_spread, "rows", axis=0, tiled=True)
        far_full, far_spread_full, far_offset = shifted((own_full, spread_full, own_offset), "tm", -distance)
        far_full = jnp.where(beyond, identity, far_full)
        row_start = lax.axis_index("rows") * gain.shape[0]
        own_rows = lax.dynamic_slice_in_dim(own_full, row_start, gain.shape[0], 0)
        middle = jnp.dot(own_rows, far_spread_full, preferred_element_type=WIDE).astype(LOW)
        new_gain = jnp.dot(own_rows, far_full, preferred_element_type=WIDE)
        new_spread = (
            lax.dot_general(middle, own_full, (((1,), (1,)), ((), ())), preferred_element_type=WIDE) + spread
        )
        new_offset = jnp.dot(own_full, far_offset, preferred_element_type=WIDE) + offset
        gain, spread, offset = (new_gain, new_spread, new_offset)
    return (gain[None], spread[None], offset[None])


def swap(value, axis):
    return lax.ppermute(value, axis, [(0, 1), (1, 0)])


def mm(a, b):
    return jnp.dot(a, b, preferred_element_type=WIDE)


def mm_bt(a, b):
    return lax.dot_general(a, b, (((1,), (1,)), ((), ())), preferred_element_type=WIDE)


GROUP = ("y", "c", "x")


def exchange(blocks):
    return lax.all_to_all(blocks, GROUP, 0, 0)


def whole(shape):
    return pl.BlockSpec(shape, lambda *_: (0,) * len(shape))


def call(kernel, ids, ins, outs, operands, mib, flops=0, scratch=(), aliases={}):
    ins = [whole(operand.shape) if spec is None else spec for spec, operand in zip(ins, operands)]
    specs, shapes = [], []
    for out in outs:
        spec, shape = out if isinstance(out, tuple) else (None, out)
        specs.append(whole(shape.shape) if spec is None else spec)
        shapes.append(shape)
    moved = sum(a.size * a.dtype.itemsize for a in list(operands) + shapes)
    return pl.pallas_call(
        kernel,
        grid_spec=pltpu.PrefetchScalarGridSpec(
            num_scalar_prefetch=1, grid=(1,), in_specs=ins, out_specs=specs, scratch_shapes=list(scratch)
        ),
        out_shape=shapes,
        input_output_aliases=aliases,
        cost_estimate=pl.CostEstimate(flops=flops, bytes_accessed=moved, transcendentals=0),
        compiler_params=pltpu.CompilerParams(vmem_limit_bytes=mib * MIB),
    )(ids, *operands)


def low(*shape):
    return jax.ShapeDtypeStruct(shape, LOW)


def wide(*shape):
    return jax.ShapeDtypeStruct(shape, WIDE)


def gather_lanes(blocks, into, start, width):
    for s in range(blocks.shape[0]):
        into[:, s * width : (s + 1) * width] = blocks[s, :, start : start + width]


def pair_kernel(ids, *refs):
    pieces, (l_low, l_got, both, pair, m_ref) = refs[:8], refs[8:]
    x = ids[0]
    me = 4 * x + 2 * ids[1] + ids[2]
    rows = pieces[0].shape[0]
    part = rows // 2
    for i in range(8):
        place = me ^ i
        both[place >> 2, pl.ds(pl.multiple_of((place & 3) * rows, rows), rows), :] = pieces[i][...]

    def product(slab):
        for r in range(4):
            cut = slice(r * rows, (r + 1) * rows)
            m = mm_bt(both[0, cut, :], slab).astype(LOW)
            m_ref[2 * r] = m
            m_ref[2 * r + 1] = m

    @pl.when(x == 0)
    def _():
        product(l_got[...])

    @pl.when(x == 1)
    def _():
        product(l_low[part:, :])

    for r in range(4):
        cut = slice(r * rows, (r + 1) * rows)
        pair[cut, :] = mm(both[0, cut, :], both[1]).astype(LOW)


def spread_start_kernel(ids, blocks, e0, spread, l_got, prod, a_l, a_low, m):
    part = l_got.shape[0]
    gather_lanes(blocks, m, 0, part)
    prod[...] = mm_bt(m[...], e0[0])

    @pl.when(ids[0] == 0)
    def _():
        a_l[...] = (prod[:part, :] + spread[0, :part, :]).T

    @pl.when(ids[0] == 1)
    def _():
        a_l[...] = (prod[part:, :] + l_got[...].astype(WIDE)).T

    a_low[...] = a_l[...].astype(LOW)


def spread_hop_kernel(ids, pair, later, got, m_ref, near):
    part = got.shape[1]
    rows = 2 * part
    m = mm(pair[...], got[...]).astype(LOW)
    m_ref[...] = m
    other = mm(later[0], got[...]).astype(LOW)
    for r in range(4):
        near[2 * r] = m[r * rows : (r + 1) * rows, :]
        near[2 * r + 1] = other[r * rows : (r + 1) * rows, :]


def spread_next_kernel(ids, blocks, pair, a_l, b_l, m):
    gather_lanes(blocks, m, 0, m.shape[0])
    b_l[...] = (mm_bt(pair[...], m[...]) + a_l[...]).astype(LOW)


def near_kernel(ids, blocks, pair, later, prod, spread, out, m):
    gather_lanes(blocks, m, 0, blocks.shape[2])

    @pl.when(ids[0] == 0)
    def _():
        out[...] = mm_bt(m[...], pair[...]) + prod[...] + spread[0]

    @pl.when(ids[0] == 1)
    def _():
        out[...] = mm_bt(m[...], later[0]) + spread[0]


def compose_kernel(ids, pair, later, next_pair, first, second, slab_ref):
    part = slab_ref.shape[1]
    slab = (2 * ids[1] + ids[2]) * 2 + ids[0]

    @pl.when(ids[3] % 2 == 0)
    def _():
        first[...] = mm(pair[...], next_pair[...]).astype(LOW)
        second[...] = mm(later[0], next_pair[...]).astype(LOW)

    @pl.when(ids[3] % 2 == 1)
    def _():
        first[...] = pair[...]
        second[...] = later[0]

    slab_ref[...] = first[:, pl.ds(pl.multiple_of(slab * part, part), part)]


def far_kernel(ids, first, second, e_a, e_b, l_a, l_b, out, far):
    size, part = e_a.shape
    rows = 2 * part

    @pl.when(ids[3] < 2)
    def _():
        far[:, :part] = e_a[...] + e_b[...]

    @pl.when(ids[3] >= 2)
    def _():
        slab = (2 * ids[1] + ids[2]) * 2 + ids[0]
        column = lax.broadcasted_iota(jnp.int32, (size, part), 1) + slab * part
        row = lax.broadcasted_iota(jnp.int32, (size, part), 0)
        far[:, :part] = jnp.where(row == column, 1.0, 0.0).astype(LOW)

    far[:, part:] = l_a[...] + l_b[...]
    one = mm(first[...], far[...]).astype(LOW)
    two = mm(second[...], far[...]).astype(LOW)
    for r in range(4):
        out[2 * r] = one[r * rows : (r + 1) * rows, :]
        out[2 * r + 1] = two[r * rows : (r + 1) * rows, :]


def end_kernel(ids, blocks, first, second, near, out_gain, out_spread, m):
    part = blocks.shape[2] // 2
    gather_lanes(blocks, m, part, part)
    for s in range(blocks.shape[0]):
        out_gain[:, s * part : (s + 1) * part] = blocks[s, :, :part].astype(WIDE)

    @pl.when(ids[0] == 0)
    def _():
        out_spread[...] = mm_bt(m[...], first[...]) + near[...]

    @pl.when(ids[0] == 1)
    def _():
        out_spread[...] = mm_bt(m[...], second[...]) + near[...]


def start_kernel(ids, e0, got, keep, p_ref, now):
    @pl.when(ids[0] == 0)
    def _():
        p = mm(e0[0], got[...])
        p_ref[...] = p
        now[...] = (p + keep[...]).astype(LOW)

    @pl.when(ids[0] == 1)
    def _():
        p = mm(e0[0], keep[...].astype(LOW))
        p_ref[...] = p
        now[...] = (p + got[...].astype(WIDE)).astype(LOW)


def hop_kernel(ids, pair, got, own, now):
    now[...] = (mm(pair[...], got[...]) + own[...].astype(WIDE)).astype(LOW)


def last_kernel(ids, pair, later, got_a, got_b, got_c, p_ref, keep, *refs):
    out, send = refs[-2:]
    far = got_a[...] + got_b[...] + got_c[...]

    @pl.when(ids[0] == 0)
    def _():
        send[...] = mm(later[0], far).astype(LOW)
        out[...] = mm(pair[...], far) + p_ref[...] + keep[...]

    @pl.when(ids[0] == 1)
    def _():
        send[...] = (mm(pair[...], far) + p_ref[...]).astype(LOW)
        out[...] = mm(later[0], far) + keep[...]


def add_kernel(ids, got, keep, into, out):
    out[...] = got[...].astype(WIDE) + keep[...]


def suffix(gains, spreads, offsets):
    x, y, c, z = (lax.axis_index(name) for name in ("x", "y", "c", "z"))
    even = x == 0
    gain, offset = gains[0], offsets[0]
    rows, size_d = gain.shape
    part = rows // 2
    half = offset.shape[1] // 2
    chunks = 2
    width = half // chunks
    ids = jnp.stack([x, y, c, z]).astype(jnp.int32)
    level = [(3, 2), (1, 0)]

    e_low = gain.astype(LOW)
    e_x, e_y = swap(e_low, "x"), swap(e_low, "y")
    e_xy = jnp.concatenate([swap(e_x[:part], "y"), swap(e_y[part:], "x")], axis=0)
    pieces = [e_low, None, e_y, None, e_x, None, e_xy, None]
    for i in range(0, 8, 2):
        pieces[i + 1] = swap(pieces[i], "c")

    l_low = spreads[0].astype(LOW)
    l_send = jnp.where(even, l_low[part:], l_low[:part])
    g_send = jnp.where(even, offset[:, half:], offset[:, :half]).astype(LOW)
    l_send, e_x = lax.optimization_barrier((l_send, e_x))
    g_send, e_xy = lax.optimization_barrier((g_send, e_xy))
    l_got = swap(l_send, "x")
    g_got = [swap(g_send[:, i * width : (i + 1) * width], "x") for i in range(chunks)]

    both, a_e, m = call(
        pair_kernel, ids, [None] * 10,
        [low(2, size_d, size_d), low(size_d, size_d), low(8, rows, part)],
        pieces + [l_low, l_got], 24, flops=2 * size_d**3,
    )
    first = pl.BlockSpec((1, size_d, size_d), lambda i, ids: (0, 0, 0))
    later = pl.BlockSpec((1, size_d, size_d), lambda i, ids: (1, 0, 0))
    prod, a_l, a_low = call(
        spread_start_kernel, ids, [None, first, None, None],
        [wide(rows, size_d), wide(size_d, part), low(size_d, part)],
        [exchange(m), both, spreads, l_got], 14, flops=2 * rows * size_d**2,
        scratch=[pltpu.VMEM((rows, size_d), LOW)],
    )

    l_next = lax.ppermute(a_low, "z", level)
    quarter = lax.dynamic_slice_in_dim(a_e, (2 * y + c) * rows, rows, 0)
    e_next = lax.all_gather(lax.ppermute(quarter, "z", level), ("y", "c"), axis=0, tiled=True)
    m, near = call(
        spread_hop_kernel, ids, [None, later, None], [low(size_d, part), low(8, rows, part)],
        [a_e, both, l_next], 10, flops=4 * part * size_d**2,
    )
    (b_l,) = call(
        spread_next_kernel, ids, [None, None, None], [low(size_d, part)],
        [exchange(m.reshape(8, part, part)), a_e, a_l], 8, flops=2 * part * size_d**2,
        scratch=[pltpu.VMEM((part, size_d), LOW)],
    )
    l_far = lax.ppermute(b_l, "z", [(2, 1)]), lax.ppermute(b_l, "z", [(2, 0)])
    c0_e, c1_e, e_slab = call(
        compose_kernel, ids, [None, later, None],
        [low(size_d, size_d), low(size_d, size_d), low(size_d, part)],
        [a_e, both, e_next], 20, flops=4 * size_d**3,
    )
    e_far = lax.ppermute(e_slab, "z", [(2, 1)]), lax.ppermute(e_slab, "z", [(2, 0)])
    (near,) = call(
        near_kernel, ids, [None, None, later, None, None], [wide(rows, size_d)],
        [exchange(near), a_e, both, prod, spreads], 14, flops=2 * rows * size_d**2,
        scratch=[pltpu.VMEM((rows, size_d), LOW)],
    )

    (m,) = call(
        far_kernel, ids, [None] * 6, [low(8, rows, rows)], [c0_e, c1_e, *e_far, *l_far], 12,
        flops=4 * rows * size_d**2, scratch=[pltpu.VMEM((size_d, rows), LOW)],
    )
    out_gain, out_spread = call(
        end_kernel, ids, [None] * 4, [wide(rows, size_d), wide(rows, size_d)],
        [exchange(m), c0_e, c1_e, near], 14, flops=2 * rows * size_d**2,
        scratch=[pltpu.VMEM((rows, size_d), LOW)],
    )

    out_offset, others = None, []
    for i in range(chunks):
        kept = pl.BlockSpec((size_d, width), lambda s, ids, i=i: (0, ids[0] * chunks + i))
        p, own = call(
            start_kernel, ids, [first, None, kept], [wide(size_d, width), low(size_d, width)],
            [both, g_got[i], offset], 10, flops=2 * size_d**2 * width,
        )
        now, gots = own, []
        for source in (3, 2, 1):
            gots.append(lax.ppermute(now, "z", [(source, source - 1)]))
            if source > 1:
                (now,) = call(
                    hop_kernel, ids, [None] * 3, [low(size_d, width)], [a_e, gots[-1], own], 8,
                    flops=2 * size_d**2 * width,
                )
        extra = [] if out_offset is None else [out_offset]
        out_offset, other = call(
            last_kernel, ids, [None, later] + [None] * 4 + [kept] + [pl.BlockSpec(memory_space=pl.ANY)] * len(extra),
            [(kept, wide(*offset.shape)), low(size_d, width)],
            [a_e, both] + gots + [p, offset] + extra, 16, flops=4 * size_d**2 * width,
            aliases={8: 0} if extra else {},
        )
        others.append(swap(other, "x"))
    for i in range(chunks):
        kept = pl.BlockSpec((size_d, width), lambda s, ids, i=i: (0, (1 - ids[0]) * chunks + i))
        (out_offset,) = call(
            add_kernel, ids, [None, kept, pl.BlockSpec(memory_space=pl.ANY)], [(kept, wide(*offset.shape))],
            [others[i], offset, out_offset], 8, aliases={3: 0},
        )
    return (out_gain[None], out_spread[None], out_offset[None])


def solution(mesh):
    steps, rows = mesh.shape["tm"], mesh.shape["rows"]
    if steps == 2**LEVELS and rows == 4:
        devices = mesh.devices.reshape(steps // 2, 2, 2, 2)
        mesh = Mesh(devices, ("z", "x", "y", "c"))
        by_row, by_column = P(("z", "x"), ("y", "c"), None), P(("z", "x"), None, ("y", "c"))
        body = suffix
    else:
        by_row, by_column = P("tm", "rows", None), P("tm", None, "rows")
        body = doubling
    return jax.shard_map(
        body,
        mesh=mesh,
        in_specs=(by_row, by_row, by_column),
        out_specs=(by_row, by_row, by_column),
        check_vma=False,
    )
```

time: 200 us -> 252 us (1.26)
  the two profiles are of different devices: /device:TPU:16 before, /device:TPU:0 now
where the time goes in v3:
time: 252 us; the launch traced here: 250 us
  waiting for transfers between devices  92 us (37%)
  Pallas kernels  58.1 us (23%)
  starting transfers between devices  44.9 us (18%)
  local copies, waits for them, and re-layouts  34.5 us (14%)
  between operations  14.5 us (6%)
  other arithmetic  5.87 us (2%)
    pallas_call x18, Pallas kernels, call(): pl.pallas_call(kernel, grid_spec=pltpu.PrefetchScalarGridSpec(num_scalar_...  58.1 us
    ppermute x13, waiting for transfers between devices, swap(): return lax.ppermute(value, axis, [(0, 1), (1, 0)])  49 us
    unnamed x77, local copies, waits for them, and re-layouts  31.6 us
    all_to_all x4, starting transfers between devices, exchange(): return lax.all_to_all(blocks, GROUP, 0, 0)  15.9 us
    ppermute x1, waiting for transfers between devices, suffix(): lax.ppermute(quarter, 'z', level)  14.2 us
    ppermute x13, starting transfers between devices, swap(): return lax.ppermute(value, axis, [(0, 1), (1, 0)])  14.1 us
    ppermute x1, waiting for transfers between devices, suffix(): lax.ppermute(e_slab, 'z', [(2, 0)])  10.9 us
    ppermute x2, waiting for transfers between devices, suffix(): l_far = (lax.ppermute(b_l, 'z', [(2, 1)]), lax.ppermute(b_l, 'z', [(2, 0)]))  10.8 us
  transfers between devices with their start and end apart: 30, of which 12 were waited for; matrix products, arithmetic and copies ran while one was open for 3% of the time, Pallas kernels for 19%

profile of v3, /device:TPU:0, one launch (start us, length us, event | category | flops | bytes accessed | tf_op | source)
XLA Modules:
  0.0 249.9 jit_solution(9036828385355878863)
XLA Ops:
  8.6 3.0 %collective-permute-start.3 = (bf16[256,1024]{1,0:T(8,128)(2,1)S(1)}, bf16[256,1024]{1,0:T(8,128)(2,1)S(1)}, u32[]{:S(2)}, u32[]{:S(2)}) collective-permute-start(bf16[256,1024]{1,0:T(8,128)(2,1)S(1)} %convert_bitcast_fusion.refs_0_), channel_id=1, source_target_pairs={{0,4},{4,0},{1,5},{5,1},{2,6},{6,2},{3,7},{7,3},{8,12},{12,8},{9,1... | collective-permute-start | bytes 1572872 | tf_op jit(solution)/shard_map/ppermute | solution.py:49
  13.1 10.4 %collective-permute-done.3.refs_4_ = bf16[256,1024]{1,0:T(8,128)(2,1)S(1)} collective-permute-done((bf16[256,1024]{1,0:T(8,128)(2,1)S(1)}, bf16[256,1024]{1,0:T(8,128)(2,1)S(1)}, u32[]{:S(2)}, u32[]{:S(2)}) %collective-permute-start.3) | collective-permute-done | bytes 524320 | tf_op jit(solution)/shard_map/ppermute | solution.py:49
  23.6 1.8 collective-permute-start.5
  28.2 2.9 %collective-permute-done.5 = bf16[128,1024]{1,0:T(8,128)(2,1)S(1)} collective-permute-done((bf16[128,1024]{1,0:T(8,128)(2,1)S(1)}, bf16[128,1024]{1,0:T(8,128)(2,1)S(1)}, u32[]{:S(2)}, u32[]{:S(2)}) %collective-permute-start.5) | collective-permute-done | bytes 262176 | tf_op jit(solution)/shard_map/ppermute | solution.py:49
  31.1 2.3 collective-permute-done.6
  36.5 1.6 collective-permute-start.8
  38.1 7.1 %collective-permute-done.8.refs_9_.l_got = bf16[128,1024]{1,0:T(8,128)(2,1)S(1)} collective-permute-done((bf16[128,1024]{1,0:T(8,128)(2,1)S(1)}, bf16[128,1024]{1,0:T(8,128)(2,1)S(1)}, u32[]{:S(2)}, u32[]{:S(2)}) %collective-permute-start.8) | collective-permute-done | bytes 262176 | tf_op jit(solution)/shard_map/ppermute | solution.py:49
  49.5 5.4 %shard_map.58 = (bf16[2,1024,1024]{2,1,0:T(8,128)(2,1)S(1)}, bf16[1024,1024]{1,0:T(8,128)(2,1)S(1)}, bf16[8,256,128]{2,1,0:T(8,128)(2,1)S(1)}) custom-call(s32[4]{0:T(128)S(1)} %pad_add_fusion.ids, bf16[256,1024]{1,0:T(8,128)(2,1)S(1)} %copy-done.25, bf16[256,1024]{1,0:T(8,128)(2,1)} %collective-permute-done.refs_1_, bf16[256,1024]{1,0:T(8,128)(2,1)S(1)} %copy-done.34, ...), custom_call_target="tpu_custom_call" | custom-call | flops 2147483648 | bytes 11796480 | tf_op jit(solution)/shard_map/pallas_call | solution.py:79
  54.9 2.0 copy-done
  59.0 14.2 %collective-permute-done.9 = bf16[256,1024]{1,0:T(8,128)(2,1)} collective-permute-done((bf16[256,1024]{1,0:T(8,128)(2,1)S(1)}, bf16[256,1024]{1,0:T(8,128)(2,1)}, u32[]{:S(2)}, u32[]{:S(2)}) %collective-permute-start.9) | collective-permute-done | bytes 524320 | tf_op jit(solution)/shard_map/ppermute | solution.py:313
  73.2 2.4 fusion
  78.7 4.1 %all-to-all-start = ((bf16[8,256,128]{2,1,0:T(8,128)(2,1)}), bf16[8,256,128]{2,1,0:T(8,128)(2,1)}, u32[]{:S(2)}, u32[]{:S(2)}) async-start(bf16[8,256,128]{2,1,0:T(8,128)(2,1)} %copy-done.27), calls=%async_computation | async-start | bytes 1048576 | tf_op jit(solution)/shard_map/all_to_all | solution.py:64
  82.9 9.0 %collective-permute-done.19.got = bf16[1024,256]{1,0:T(8,128)(2,1)} collective-permute-done((bf16[1024,256]{1,0:T(8,128)(2,1)}, bf16[1024,256]{1,0:T(8,128)(2,1)}, u32[]{:S(2)}, u32[]{:S(2)}) %collective-permute-start.19) | collective-permute-done | bytes 524320 | tf_op jit(solution)/shard_map/ppermute | solution.py:49
  91.9 2.2 copy-done.1
  94.1 2.2 copy-done.7
  96.3 3.1 %shard_map.69 = (f32[1024,256]{1,0:T(8,128)S(1)}, bf16[1024,256]{1,0:T(8,128)(2,1)}) custom-call(s32[4]{0:T(128)S(1)} %pad_add_fusion.ids, bf16[2,1024,1024]{2,1,0:T(8,128)(2,1)S(1)} %copy-done.1, bf16[1024,256]{1,0:T(8,128)(2,1)} %collective-permute-done.19.got, f32[1024,1024]{1,0:T(8,128)S(1)} %bitcast.16), custom_call_target="tpu_custom_call" | custom-call | flops 536870912 | bytes 10485760 | tf_op jit(solution)/shard_map/pallas_call | solution.py:79
  103.1 3.1 %shard_map.66 = (f32[1024,256]{1,0:T(8,128)S(1)}, bf16[1024,256]{1,0:T(8,128)(2,1)}) custom-call(s32[4]{0:T(128)S(1)} %pad_add_fusion.ids, bf16[2,1024,1024]{2,1,0:T(8,128)(2,1)S(1)} %copy-done.1, bf16[1024,256]{1,0:T(8,128)(2,1)} %collective-permute-done.15.got, f32[1024,1024]{1,0:T(8,128)S(1)} %bitcast.17), custom_call_target="tpu_custom_call" | custom-call | flops 536870912 | bytes 10485760 | tf_op jit(solution)/shard_map/pallas_call | solution.py:79
  108.6 2.2 copy-done.2
  110.8 2.8 %shard_map.60 = (f32[256,1024]{1,0:T(8,128)S(1)}, f32[1024,128]{1,0:T(8,128)S(1)}, bf16[1024,128]{1,0:T(8,128)(2,1)S(1)}) custom-call(s32[4]{0:T(128)S(1)} %pad_add_fusion.ids, bf16[8,256,128]{2,1,0:T(8,128)(2,1)} %all-to-all-done.blocks, bf16[2,1024,1024]{2,1,0:T(8,128)(2,1)S(1)} %copy-done.2, f32[1,256,1024]{2,1,0:T(8,128)S(1)} %copy-done.10, ...), custom_call_target="tpu_custom_call" | custom-call | flops 536870912 | bytes 7864320 | tf_op jit(solution)/shard_map/pallas_call | solution.py:79
  114.9 7.0 %collective-permute-done.12.got = bf16[1024,128]{1,0:T(8,128)(2,1)S(1)} collective-permute-done((bf16[1024,128]{1,0:T(8,128)(2,1)S(1)}, bf16[1024,128]{1,0:T(8,128)(2,1)S(1)}, u32[]{:S(2)}, u32[]{:S(2)}) %collective-permute-start.12) | collective-permute-done | bytes 262176 | tf_op jit(solution)/shard_map/ppermute | solution.py:311
  121.9 1.8 shard_map.61
  125.2 3.4 %all-to-all-start.1 = ((bf16[8,128,128]{2,1,0:T(8,128)(2,1)}), bf16[8,128,128]{2,1,0:T(8,128)(2,1)S(1)}, u32[]{:S(2)}, u32[]{:S(2)}) async-start(bf16[8,128,128]{2,1,0:T(8,128)(2,1)} %bitcast.22), calls=%async_computation.1 | async-start | bytes 524288 | tf_op jit(solution)/shard_map/all_to_all | solution.py:64
  128.7 3.3 %shard_map.70 = bf16[1024,256]{1,0:T(8,128)(2,1)} custom-call(s32[4]{0:T(128)S(1)} %pad_add_fusion.ids, bf16[1024,1024]{1,0:T(8,128)(2,1)S(1)} %get-tuple-element.27.pair, bf16[1024,256]{1,0:T(8,128)(2,1)} %collective-permute-done.20.got.got_a, bf16[1024,256]{1,0:T(8,128)(2,1)} %get-tuple-element.43.own), custom_call_target="tpu_custom_call" | custom-call | flops 536870912 | bytes 3670016 | tf_op jit(solution)/shard_map/pallas_call | solution.py:79
  133.4 3.3 %shard_map.67 = bf16[1024,256]{1,0:T(8,128)(2,1)} custom-call(s32[4]{0:T(128)S(1)} %pad_add_fusion.ids, bf16[1024,1024]{1,0:T(8,128)(2,1)S(1)} %get-tuple-element.27.pair, bf16[1024,256]{1,0:T(8,128)(2,1)} %collective-permute-done.16.got.got_a, bf16[1024,256]{1,0:T(8,128)(2,1)} %get-tuple-element.41.own), custom_call_target="tpu_custom_call" | custom-call | flops 536870912 | bytes 3670016 | tf_op jit(solution)/shard_map/pallas_call | solution.py:79
  138.1 4.1 %all-to-all-start.3 = ((bf16[8,256,128]{2,1,0:T(8,128)(2,1)}), bf16[8,256,128]{2,1,0:T(8,128)(2,1)}, u32[]{:S(2)}, u32[]{:S(2)}) async-start(bf16[8,256,128]{2,1,0:T(8,128)(2,1)} %copy-done.26), calls=%async_computation.3 | async-start | bytes 1048576 | tf_op jit(solution)/shard_map/all_to_all | solution.py:64
  143.3 2.0 shard_map.62
  147.3 2.2 copy-done.4
  149.5 1.6 copy-done.37
  151.1 5.3 %shard_map.59 = (bf16[1024,1024]{1,0:T(8,128)(2,1)S(1)}, bf16[1024,1024]{1,0:T(8,128)(2,1)S(1)}, bf16[1024,128]{1,0:T(8,128)(2,1)S(1)}) custom-call(s32[4]{0:T(128)S(1)} %pad_add_fusion.ids, bf16[1024,1024]{1,0:T(8,128)(2,1)S(1)} %get-tuple-element.27.pair, bf16[2,1024,1024]{2,1,0:T(8,128)(2,1)S(1)} %copy-done.4, bf16[1024,1024]{1,0:T(8,128)(2,1)S(1)} %copy-done.37), custom_call_target="tpu_custom_call" | custom-call | flops 4294967296 | bytes 12845056 | tf_op jit(solution)/shard_map/pallas_call | solution.py:79
  158.4 3.3 %shard_map.71 = bf16[1024,256]{1,0:T(8,128)(2,1)} custom-call(s32[4]{0:T(128)S(1)} %pad_add_fusion.ids, bf16[1024,1024]{1,0:T(8,128)(2,1)S(1)} %get-tuple-element.27.pair, bf16[1024,256]{1,0:T(8,128)(2,1)} %collective-permute-done.21.got.got_b, bf16[1024,256]{1,0:T(8,128)(2,1)} %get-tuple-element.43.own), custom_call_target="tpu_custom_call" | custom-call | flops 536870912 | bytes 3670016 | tf_op jit(solution)/shard_map/pallas_call | solution.py:79
  162.9 3.3 %shard_map.68 = bf16[1024,256]{1,0:T(8,128)(2,1)} custom-call(s32[4]{0:T(128)S(1)} %pad_add_fusion.ids, bf16[1024,1024]{1,0:T(8,128)(2,1)S(1)} %get-tuple-element.27.pair, bf16[1024,256]{1,0:T(8,128)(2,1)} %collective-permute-done.17.got.got_b, bf16[1024,256]{1,0:T(8,128)(2,1)} %get-tuple-element.41.own), custom_call_target="tpu_custom_call" | custom-call | flops 536870912 | bytes 3670016 | tf_op jit(solution)/shard_map/pallas_call | solution.py:79
  167.5 10.8 %collective-permute-done.14.l_b = bf16[1024,128]{1,0:T(8,128)(2,1)} collective-permute-done((bf16[1024,128]{1,0:T(8,128)(2,1)}, bf16[1024,128]{1,0:T(8,128)(2,1)}, u32[]{:S(2)}, u32[]{:S(2)}) %collective-permute-start.14) | collective-permute-done | bytes 262176 | tf_op jit(solution)/shard_map/ppermute | solution.py:323
  178.3 10.9 %collective-permute-done.11.e_b = bf16[1024,128]{1,0:T(8,128)(2,1)S(1)} collective-permute-done((bf16[1024,128]{1,0:T(8,128)(2,1)S(1)}, bf16[1024,128]{1,0:T(8,128)(2,1)S(1)}, u32[]{:S(2)}, u32[]{:S(2)}) %collective-permute-start.11) | collective-permute-done | bytes 262176 | tf_op jit(solution)/shard_map/ppermute | solution.py:329
  189.2 2.8 %shard_map.63 = bf16[8,256,256]{2,1,0:T(8,128)(2,1)S(1)} custom-call(s32[4]{0:T(128)S(1)} %pad_add_fusion.ids, bf16[1024,1024]{1,0:T(8,128)(2,1)S(1)} %get-tuple-element.29.first, bf16[1024,1024]{1,0:T(8,128)(2,1)S(1)} %get-tuple-element.30.second, bf16[1024,128]{1,0:T(8,128)(2,1)S(1)} %collective-permute-done.10.e_a, ...), custom_call_target="tpu_custom_call" | custom-call | flops 1073741824 | bytes 6291456 | tf_op jit(solution)/shard_map/pallas_call | solution.py:79
  193.0 4.2 %all-to-all-start.2 = ((bf16[8,256,256]{2,1,0:T(8,128)(2,1)}), bf16[8,256,256]{2,1,0:T(8,128)(2,1)}, u32[]{:S(2)}, u32[]{:S(2)}) async-start(bf16[8,256,256]{2,1,0:T(8,128)(2,1)} %copy-done.17), calls=%async_computation.2 | async-start | bytes 2097152 | tf_op jit(solution)/shard_map/all_to_all | solution.py:64
  197.3 2.2 copy-done.5
  199.5 2.2 copy-done.8
  202.9 4.5 %shard_map.72 = (f32[1024,1024]{1,0:T(8,128)}, bf16[1024,256]{1,0:T(8,128)(2,1)S(1)}) custom-call(s32[4]{0:T(128)S(1)} %pad_add_fusion.ids, bf16[1024,1024]{1,0:T(8,128)(2,1)S(1)} %get-tuple-element.27.pair, bf16[2,1024,1024]{2,1,0:T(8,128)(2,1)S(1)} %copy-done.5, bf16[1024,256]{1,0:T(8,128)(2,1)} %collective-permute-done.20.got.got_a, ...), custom_call_target="tpu_custom_call" | custom-call | flops 1073741824 | bytes 17825792 | tf_op jit(solution)/shard_map/pallas_call | solution.py:79
  207.4 1.9 collective-permute-start.24
  209.3 4.5 %shard_map.73 = (f32[1024,1024]{1,0:T(8,128)}, bf16[1024,256]{1,0:T(8,128)(2,1)S(1)}) custom-call(s32[4]{0:T(128)S(1)} %pad_add_fusion.ids, bf16[1024,1024]{1,0:T(8,128)(2,1)S(1)} %get-tuple-element.27.pair, bf16[2,1024,1024]{2,1,0:T(8,128)(2,1)S(1)} %copy-done.5, ...), custom_call_target="tpu_custom_call", output_to_operand_aliasing={{0}: (8, {})} | custom-call | flops 1073741824 | bytes 22020096 | tf_op jit(solution)/shard_map/pallas_call | solution.py:79
  214.0 2.5 shard_map.64.near
  216.5 6.9 %collective-permute-done.24.got = bf16[1024,256]{1,0:T(8,128)(2,1)S(1)} collective-permute-done((bf16[1024,256]{1,0:T(8,128)(2,1)S(1)}, bf16[1024,256]{1,0:T(8,128)(2,1)S(1)}, u32[]{:S(2)}, u32[]{:S(2)}) %collective-permute-start.24) | collective-permute-done | bytes 524320 | tf_op jit(solution)/shard_map/ppermute | solution.py:49
  223.4 1.6 shard_map.74.into
  225.0 9.2 %collective-permute-done.23.got = bf16[1024,256]{1,0:T(8,128)(2,1)S(1)} collective-permute-done((bf16[1024,256]{1,0:T(8,128)(2,1)S(1)}, bf16[1024,256]{1,0:T(8,128)(2,1)S(1)}, u32[]{:S(2)}, u32[]{:S(2)}) %collective-permute-start.23) | collective-permute-done | bytes 524320 | tf_op jit(solution)/shard_map/ppermute | solution.py:49
  234.1 1.6 shard_map.75
  235.7 1.6 copy-done.12
  237.3 1.6 copy-done.14
  238.9 4.1 %shard_map.65 = (f32[256,1024]{1,0:T(8,128)}, f32[256,1024]{1,0:T(8,128)}) custom-call(s32[4]{0:T(128)S(1)} %pad_add_fusion.ids, bf16[8,256,256]{2,1,0:T(8,128)(2,1)} %all-to-all-done.2.blocks, bf16[1024,1024]{1,0:T(8,128)(2,1)S(1)} %copy-done.12, bf16[1024,1024]{1,0:T(8,128)(2,1)S(1)} %copy-done.14, f32[256,1024]{1,0:T(8,128)S(1)} %copy-done.16), custom_call_target="tpu_custom_call" | custom-call | flops 536870912 | bytes 8388608 | tf_op jit(solution)/shard_map/pallas_call | solution.py:79
  (119 shorter events, 40.1 us)
Async XLA Ops:
  7.2 27.4 %copy-start.10 = (f32[1,256,1024]{2,1,0:T(8,128)S(1)}, f32[1,256,1024]{2,1,0:T(8,128)}, u32[]{:S(2)}) copy-start(f32[1,256,1024]{2,1,0:T(8,128)} %spread.3) | copy-start | bytes 3145732
  7.2 140.1 %all-gather.2.cloned.1.call-start = ((), (), s32[]{:S(2)}) async-start(), calls=%async_computation.4 | async-start | bytes 2621440 | tf_op jit(solution)/shard_map/all_gather | solution.py:313
  8.6 36.7 %copy-start.24 = (bf16[256,1024]{1,0:T(8,128)(2,1)}, bf16[256,1024]{1,0:T(8,128)(2,1)S(1)}, u32[]{:S(2)}) copy-start(bf16[256,1024]{1,0:T(8,128)(2,1)S(1)} %convert_bitcast_fusion.refs_0_) | copy-start | bytes 1572868
  8.6 14.9 %collective-permute-start.3 = (bf16[256,1024]{1,0:T(8,128)(2,1)S(1)}, bf16[256,1024]{1,0:T(8,128)(2,1)S(1)}, u32[]{:S(2)}, u32[]{:S(2)}) collective-permute-start(bf16[256,1024]{1,0:T(8,128)(2,1)S(1)} %convert_bitcast_fusion.refs_0_), channel_id=1, source_target_pairs={{0,4},{4,0},{1,5},{5,1},{2,6},{6,2},{3,7},{7,3},{8,12},{12,8},{9,1... | collective-permute-start | bytes 1572872 | tf_op jit(solution)/shard_map/ppermute | solution.py:49
  11.6 13.8 %collective-permute-start.1 = (bf16[256,1024]{1,0:T(8,128)(2,1)S(1)}, bf16[256,1024]{1,0:T(8,128)(2,1)S(1)}, u32[]{:S(2)}, u32[]{:S(2)}) collective-permute-start(bf16[256,1024]{1,0:T(8,128)(2,1)S(1)} %convert_bitcast_fusion.refs_0_), channel_id=1, source_target_pairs={{0,2},{2,0},{1,3},{3,1},{4,6},{6,4},{5,7},{7,5},{8,10},{10,8},{9,1... | collective-permute-start | bytes 1572872 | tf_op jit(solution)/shard_map/ppermute | solution.py:49
  23.5 21.7 %copy-start.31 = (bf16[256,1024]{1,0:T(8,128)(2,1)}, bf16[256,1024]{1,0:T(8,128)(2,1)S(1)}, u32[]{:S(2)}) copy-start(bf16[256,1024]{1,0:T(8,128)(2,1)S(1)} %collective-permute-done.3.refs_4_) | copy-start | bytes 1572868
  23.6 7.6 %collective-permute-start.5 = (bf16[128,1024]{1,0:T(8,128)(2,1)S(1)}, bf16[128,1024]{1,0:T(8,128)(2,1)S(1)}, u32[]{:S(2)}, u32[]{:S(2)}) collective-permute-start(bf16[128,1024]{1,0:T(8,128)(2,1)S(1)} %slice.34), channel_id=1, source_target_pairs={{0,2},{2,0},{1,3},{3,1},{4,6},{6,4},{5,7},{7,5},{8,10},{10,8},{9,1... | collective-permute-start | bytes 786440 | tf_op jit(solution)/shard_map/ppermute | solution.py:49
  25.4 19.9 %copy-start.33 = (bf16[256,1024]{1,0:T(8,128)(2,1)}, bf16[256,1024]{1,0:T(8,128)(2,1)S(1)}, u32[]{:S(2)}) copy-start(bf16[256,1024]{1,0:T(8,128)(2,1)S(1)} %collective-permute-done.1.refs_2_) | copy-start | bytes 1572868
  26.2 7.2 %collective-permute-start.6 = (bf16[128,1024]{1,0:T(8,128)(2,1)}, bf16[128,1024]{1,0:T(8,128)(2,1)}, u32[]{:S(2)}, u32[]{:S(2)}) collective-permute-start(bf16[128,1024]{1,0:T(8,128)(2,1)} %slice.35), channel_id=1, source_target_pairs={{0,4},{4,0},{1,5},{5,1},{2,6},{6,2},{3,7},{7,3},{8,12},{12,8},{9,1... | collective-permute-start | bytes 786440 | tf_op jit(solution)/shard_map/ppermute | solution.py:49
  27.7 10.4 %collective-permute-start = (bf16[256,1024]{1,0:T(8,128)(2,1)S(1)}, bf16[256,1024]{1,0:T(8,128)(2,1)}, u32[]{:S(2)}, u32[]{:S(2)}) collective-permute-start(bf16[256,1024]{1,0:T(8,128)(2,1)S(1)} %convert_bitcast_fusion.refs_0_), channel_id=1, source_target_pairs={{0,1},{1,0},{2,3},{3,2},{4,5},{5,4},{6,7},{7,6},{8,9},{9,8},{10,11... | collective-permute-start | bytes 1572872 | tf_op jit(solution)/shard_map/ppermute | solution.py:49
  27.7 17.6 %collective-permute-start.4 = (bf16[256,1024]{1,0:T(8,128)(2,1)S(1)}, bf16[256,1024]{1,0:T(8,128)(2,1)}, u32[]{:S(2)}, u32[]{:S(2)}) collective-permute-start(bf16[256,1024]{1,0:T(8,128)(2,1)S(1)} %collective-permute-done.3.refs_4_), channel_id=1, source_target_pairs={{0,1},{1,0},{2,3},{3,2},{4,5},{5,4},{6,7},{7,6},{8,9},{9,8},{10,11... | collective-permute-start | bytes 1572872 | tf_op jit(solution)/shard_map/ppermute | solution.py:49
  28.2 17.1 %collective-permute-start.2 = (bf16[256,1024]{1,0:T(8,128)(2,1)S(1)}, bf16[256,1024]{1,0:T(8,128)(2,1)}, u32[]{:S(2)}, u32[]{:S(2)}) collective-permute-start(bf16[256,1024]{1,0:T(8,128)(2,1)S(1)} %collective-permute-done.1.refs_2_), channel_id=1, source_target_pairs={{0,1},{1,0},{2,3},{3,2},{4,5},{5,4},{6,7},{7,6},{8,9},{9,8},{10,11... | collective-permute-start | bytes 1572872 | tf_op jit(solution)/shard_map/ppermute | solution.py:49
  34.4 10.9 %copy-start.35 = (bf16[256,1024]{1,0:T(8,128)(2,1)}, bf16[256,1024]{1,0:T(8,128)(2,1)S(1)}, u32[]{:S(2)}) copy-start(bf16[256,1024]{1,0:T(8,128)(2,1)S(1)} %constant_dynamic-update-slice_fusion.refs_6_) | copy-start | bytes 1572868
  34.4 10.9 %collective-permute-start.7 = (bf16[256,1024]{1,0:T(8,128)(2,1)S(1)}, bf16[256,1024]{1,0:T(8,128)(2,1)}, u32[]{:S(2)}, u32[]{:S(2)}) collective-permute-start(bf16[256,1024]{1,0:T(8,128)(2,1)S(1)} %constant_dynamic-update-slice_fusion.refs_6_), channel_id=1, source_target_pairs={{0,1},{1,0},{2,3},{3,2},{4,5},{5,4},{6,7},{7,6},{8,9},{9,8},{10,11... | collective-permute-start | bytes 1572872 | tf_op jit(solution)/shard_map/ppermute | solution.py:49
  36.5 8.8 %collective-permute-start.8 = (bf16[128,1024]{1,0:T(8,128)(2,1)S(1)}, bf16[128,1024]{1,0:T(8,128)(2,1)S(1)}, u32[]{:S(2)}, u32[]{:S(2)}) collective-permute-start(bf16[128,1024]{1,0:T(8,128)(2,1)S(1)} %fusion.1), channel_id=1, source_target_pairs={{0,4},{4,0},{1,5},{5,1},{2,6},{6,2},{3,7},{7,3},{8,12},{12,8},{9,1... | collective-permute-start | bytes 786440 | tf_op jit(solution)/shard_map/ppermute | solution.py:49
  57.7 15.5 %collective-permute-start.9 = (bf16[256,1024]{1,0:T(8,128)(2,1)S(1)}, bf16[256,1024]{1,0:T(8,128)(2,1)}, u32[]{:S(2)}, u32[]{:S(2)}) collective-permute-start(bf16[256,1024]{1,0:T(8,128)(2,1)S(1)} %constant_dynamic-slice_fusion), channel_id=1, source_target_pairs={{24,16},{8,0},{25,17},{9,1},{26,18},{10,2},{27,19},{11,3},{28,20},... | collective-permute-start | bytes 1572872 | tf_op jit(solution)/shard_map/ppermute | solution.py:313
  76.7 15.2 %collective-permute-start.19 = (bf16[1024,256]{1,0:T(8,128)(2,1)}, bf16[1024,256]{1,0:T(8,128)(2,1)}, u32[]{:S(2)}, u32[]{:S(2)}) collective-permute-start(bf16[1024,256]{1,0:T(8,128)(2,1)} %get-tuple-element.49), channel_id=1, source_target_pairs={{0,4},{4,0},{1,5},{5,1},{2,6},{6,2},{3,7},{7,3},{8,12},{12,8},{9,1... | collective-permute-start | bytes 1572872 | tf_op jit(solution)/shard_map/ppermute | solution.py:49
  78.2 24.9 %collective-permute-start.15 = (bf16[1024,256]{1,0:T(8,128)(2,1)}, bf16[1024,256]{1,0:T(8,128)(2,1)}, u32[]{:S(2)}, u32[]{:S(2)}) collective-permute-start(bf16[1024,256]{1,0:T(8,128)(2,1)} %get-tuple-element.50), channel_id=1, source_target_pairs={{0,4},{4,0},{1,5},{5,1},{2,6},{6,2},{3,7},{7,3},{8,12},{12,8},{9,1... | collective-permute-start | bytes 1572872 | tf_op jit(solution)/shard_map/ppermute | solution.py:49
  78.7 29.9 %all-to-all-start = ((bf16[8,256,128]{2,1,0:T(8,128)(2,1)}), bf16[8,256,128]{2,1,0:T(8,128)(2,1)}, u32[]{:S(2)}, u32[]{:S(2)}) async-start(bf16[8,256,128]{2,1,0:T(8,128)(2,1)} %copy-done.27), calls=%async_computation | async-start | bytes 1048576 | tf_op jit(solution)/shard_map/all_to_all | solution.py:64
  91.9 2.2 copy-start.1
  94.1 2.2 copy-start.7
  100.4 28.3 %collective-permute-start.20 = (bf16[1024,256]{1,0:T(8,128)(2,1)}, bf16[1024,256]{1,0:T(8,128)(2,1)}, u32[]{:S(2)}, u32[]{:S(2)}) collective-permute-start(bf16[1024,256]{1,0:T(8,128)(2,1)} %get-tuple-element.43.own), channel_id=1, source_target_pairs={{24,16},{25,17},{26,18},{27,19},{28,20},{29,21},{30,22},{31,23}} | collective-permute-start | bytes 1572872 | tf_op jit(solution)/shard_map/ppermute | solution.py:355
  107.2 26.2 %collective-permute-start.16 = (bf16[1024,256]{1,0:T(8,128)(2,1)}, bf16[1024,256]{1,0:T(8,128)(2,1)}, u32[]{:S(2)}, u32[]{:S(2)}) collective-permute-start(bf16[1024,256]{1,0:T(8,128)(2,1)} %get-tuple-element.41.own), channel_id=1, source_target_pairs={{24,16},{25,17},{26,18},{27,19},{28,20},{29,21},{30,22},{31,23}} | collective-permute-start | bytes 1572872 | tf_op jit(solution)/shard_map/ppermute | solution.py:355
  110.8 11.1 %copy-start.3 = (bf16[2,1024,1024]{2,1,0:T(8,128)(2,1)S(1)}, bf16[2,1024,1024]{2,1,0:T(8,128)(2,1)}, u32[]{:S(2)}) copy-start(bf16[2,1024,1024]{2,1,0:T(8,128)(2,1)} %copy-done) | copy-start | bytes 12582916
  113.6 10.1 %copy-start.20 = (f32[256,1024]{1,0:T(8,128)}, f32[256,1024]{1,0:T(8,128)S(1)}, u32[]{:S(2)}) copy-start(f32[256,1024]{1,0:T(8,128)S(1)} %get-tuple-element.37.prod) | copy-start | bytes 3145732
  113.6 11.6 %copy-start.28 = (f32[1024,128]{1,0:T(8,128)}, f32[1024,128]{1,0:T(8,128)S(1)}, u32[]{:S(2)}) copy-start(f32[1024,128]{1,0:T(8,128)S(1)} %get-tuple-element.35.a_l) | copy-start | bytes 1572868
  113.6 8.3 %collective-permute-start.12 = (bf16[1024,128]{1,0:T(8,128)(2,1)S(1)}, bf16[1024,128]{1,0:T(8,128)(2,1)S(1)}, u32[]{:S(2)}, u32[]{:S(2)}) collective-permute-start(bf16[1024,128]{1,0:T(8,128)(2,1)S(1)} %get-tuple-element.33), channel_id=1, source_target_pairs={{24,16},{8,0},{25,17},{9,1},{26,18},{10,2},{27,19},{11,3},{28,20},... | collective-permute-start | bytes 786440 | tf_op jit(solution)/shard_map/ppermute | solution.py:311
  125.2 12.9 %all-to-all-start.1 = ((bf16[8,128,128]{2,1,0:T(8,128)(2,1)}), bf16[8,128,128]{2,1,0:T(8,128)(2,1)S(1)}, u32[]{:S(2)}, u32[]{:S(2)}) async-start(bf16[8,128,128]{2,1,0:T(8,128)(2,1)} %bitcast.22), calls=%async_computation.1 | async-start | bytes 524288 | tf_op jit(solution)/shard_map/all_to_all | solution.py:64
  131.9 25.2 %collective-permute-start.21 = (bf16[1024,256]{1,0:T(8,128)(2,1)}, bf16[1024,256]{1,0:T(8,128)(2,1)}, u32[]{:S(2)}, u32[]{:S(2)}) collective-permute-start(bf16[1024,256]{1,0:T(8,128)(2,1)} %shard_map.70), channel_id=1, source_target_pairs={{16,8},{17,9},{18,10},{19,11},{20,12},{21,13},{22,14},{23,15}} | collective-permute-start | bytes 1572872 | tf_op jit(solution)/shard_map/ppermute | solution.py:355
  136.6 25.0 %collective-permute-start.17 = (bf16[1024,256]{1,0:T(8,128)(2,1)}, bf16[1024,256]{1,0:T(8,128)(2,1)}, u32[]{:S(2)}, u32[]{:S(2)}) collective-permute-start(bf16[1024,256]{1,0:T(8,128)(2,1)} %shard_map.67), channel_id=1, source_target_pairs={{16,8},{17,9},{18,10},{19,11},{20,12},{21,13},{22,14},{23,15}} | collective-permute-start | bytes 1572872 | tf_op jit(solution)/shard_map/ppermute | solution.py:355
  138.1 54.9 %all-to-all-start.3 = ((bf16[8,256,128]{2,1,0:T(8,128)(2,1)}), bf16[8,256,128]{2,1,0:T(8,128)(2,1)}, u32[]{:S(2)}, u32[]{:S(2)}) async-start(bf16[8,256,128]{2,1,0:T(8,128)(2,1)} %copy-done.26), calls=%async_computation.3 | async-start | bytes 1048576 | tf_op jit(solution)/shard_map/all_to_all | solution.py:64
  145.3 20.9 %collective-permute-start.13 = (bf16[1024,128]{1,0:T(8,128)(2,1)}, bf16[1024,128]{1,0:T(8,128)(2,1)S(1)}, u32[]{:S(2)}, u32[]{:S(2)}) collective-permute-start(bf16[1024,128]{1,0:T(8,128)(2,1)} %shard_map.62), channel_id=1, source_target_pairs={{16,8},{17,9},{18,10},{19,11},{20,12},{21,13},{22,14},{23,15}} | collective-permute-start | bytes 786440 | tf_op jit(solution)/shard_map/ppermute | solution.py:323
  145.9 32.3 %collective-permute-start.14 = (bf16[1024,128]{1,0:T(8,128)(2,1)}, bf16[1024,128]{1,0:T(8,128)(2,1)}, u32[]{:S(2)}, u32[]{:S(2)}) collective-permute-start(bf16[1024,128]{1,0:T(8,128)(2,1)} %shard_map.62), channel_id=1, source_target_pairs={{16,0},{17,1},{18,2},{19,3},{20,4},{21,5},{22,6},{23,7}} | collective-permute-start | bytes 786440 | tf_op jit(solution)/shard_map/ppermute | solution.py:323
  156.4 32.9 %copy-start.11 = (bf16[1024,1024]{1,0:T(8,128)(2,1)}, bf16[1024,1024]{1,0:T(8,128)(2,1)S(1)}, u32[]{:S(2)}) copy-start(bf16[1024,1024]{1,0:T(8,128)(2,1)S(1)} %get-tuple-element.29.first) | copy-start | bytes 6291460
  156.4 32.8 %copy-start.13 = (bf16[1024,1024]{1,0:T(8,128)(2,1)}, bf16[1024,1024]{1,0:T(8,128)(2,1)S(1)}, u32[]{:S(2)}) copy-start(bf16[1024,1024]{1,0:T(8,128)(2,1)S(1)} %get-tuple-element.30.second) | copy-start | bytes 6291460
  156.4 21.9 %collective-permute-start.10 = (bf16[1024,128]{1,0:T(8,128)(2,1)S(1)}, bf16[1024,128]{1,0:T(8,128)(2,1)S(1)}, u32[]{:S(2)}, u32[]{:S(2)}) collective-permute-start(bf16[1024,128]{1,0:T(8,128)(2,1)S(1)} %get-tuple-element.31), channel_id=1, source_target_pairs={{16,8},{17,9},{18,10},{19,11},{20,12},{21,13},{22,14},{23,15}} | collective-permute-start | bytes 786440 | tf_op jit(solution)/shard_map/ppermute | solution.py:329
  157.1 32.1 %collective-permute-start.11 = (bf16[1024,128]{1,0:T(8,128)(2,1)S(1)}, bf16[1024,128]{1,0:T(8,128)(2,1)S(1)}, u32[]{:S(2)}, u32[]{:S(2)}) collective-permute-start(bf16[1024,128]{1,0:T(8,128)(2,1)S(1)} %get-tuple-element.31), channel_id=1, source_target_pairs={{16,0},{17,1},{18,2},{19,3},{20,4},{21,5},{22,6},{23,7}} | collective-permute-start | bytes 786440 | tf_op jit(solution)/shard_map/ppermute | solution.py:329
  161.6 35.6 %collective-permute-start.22 = (bf16[1024,256]{1,0:T(8,128)(2,1)}, bf16[1024,256]{1,0:T(8,128)(2,1)}, u32[]{:S(2)}, u32[]{:S(2)}) collective-permute-start(bf16[1024,256]{1,0:T(8,128)(2,1)} %shard_map.71), channel_id=1, source_target_pairs={{8,0},{9,1},{10,2},{11,3},{12,4},{13,5},{14,6},{15,7}} | collective-permute-start | bytes 1572872 | tf_op jit(solution)/shard_map/ppermute | solution.py:355
  166.2 43.1 %collective-permute-start.18 = (bf16[1024,256]{1,0:T(8,128)(2,1)}, bf16[1024,256]{1,0:T(8,128)(2,1)}, u32[]{:S(2)}, u32[]{:S(2)}) collective-permute-start(bf16[1024,256]{1,0:T(8,128)(2,1)} %shard_map.68), channel_id=1, source_target_pairs={{8,0},{9,1},{10,2},{11,3},{12,4},{13,5},{14,6},{15,7}} | collective-permute-start | bytes 1572872 | tf_op jit(solution)/shard_map/ppermute | solution.py:355
  193.0 42.7 %all-to-all-start.2 = ((bf16[8,256,256]{2,1,0:T(8,128)(2,1)}), bf16[8,256,256]{2,1,0:T(8,128)(2,1)}, u32[]{:S(2)}, u32[]{:S(2)}) async-start(bf16[8,256,256]{2,1,0:T(8,128)(2,1)} %copy-done.17), calls=%async_computation.2 | async-start | bytes 2097152 | tf_op jit(solution)/shard_map/all_to_all | solution.py:64
  197.3 2.2 copy-start.5
  202.9 6.4 %copy-start.9 = (f32[1,1024,1024]{2,1,0:T(8,128)S(1)}, f32[1,1024,1024]{2,1,0:T(8,128)}, u32[]{:S(2)}) copy-start(f32[1,1024,1024]{2,1,0:T(8,128)} %param.5) | copy-start | bytes 12582916
  202.9 6.4 %copy-start.19 = (f32[1024,256]{1,0:T(8,128)S(1)}, f32[1024,256]{1,0:T(8,128)}, u32[]{:S(2)}) copy-start(f32[1024,256]{1,0:T(8,128)} %copy-done.18) | copy-start | bytes 3145732
  207.4 16.0 %collective-permute-start.24 = (bf16[1024,256]{1,0:T(8,128)(2,1)S(1)}, bf16[1024,256]{1,0:T(8,128)(2,1)S(1)}, u32[]{:S(2)}, u32[]{:S(2)}) collective-permute-start(bf16[1024,256]{1,0:T(8,128)(2,1)S(1)} %get-tuple-element.47), channel_id=1, source_target_pairs={{0,4},{4,0},{1,5},{5,1},{2,6},{6,2},{3,7},{7,3},{8,12},{12,8},{9,1... | collective-permute-start | bytes 1572872 | tf_op jit(solution)/shard_map/ppermute | solution.py:49
  209.3 4.7 %copy-start.6 = (bf16[2,1024,1024]{2,1,0:T(8,128)(2,1)S(1)}, bf16[2,1024,1024]{2,1,0:T(8,128)(2,1)}, u32[]{:S(2)}) copy-start(bf16[2,1024,1024]{2,1,0:T(8,128)(2,1)} %copy-done) | copy-start | bytes 12582916
  209.3 4.7 %copy-start.21 = (f32[256,1024]{1,0:T(8,128)S(1)}, f32[256,1024]{1,0:T(8,128)}, u32[]{:S(2)}) copy-start(f32[256,1024]{1,0:T(8,128)} %copy-done.20) | copy-start | bytes 3145732
  213.9 20.3 %collective-permute-start.23 = (bf16[1024,256]{1,0:T(8,128)(2,1)S(1)}, bf16[1024,256]{1,0:T(8,128)(2,1)S(1)}, u32[]{:S(2)}, u32[]{:S(2)}) collective-permute-start(bf16[1024,256]{1,0:T(8,128)(2,1)S(1)} %get-tuple-element.46), channel_id=1, source_target_pairs={{0,4},{4,0},{1,5},{5,1},{2,6},{6,2},{3,7},{7,3},{8,12},{12,8},{9,1... | collective-permute-start | bytes 1572872 | tf_op jit(solution)/shard_map/ppermute | solution.py:49
  216.5 8.5 %copy-start.15 = (f32[256,1024]{1,0:T(8,128)}, f32[256,1024]{1,0:T(8,128)S(1)}, u32[]{:S(2)}) copy-start(f32[256,1024]{1,0:T(8,128)S(1)} %shard_map.64.near) | copy-start | bytes 3145732
  (20 other events, 26.6 us)
Sparse Core Ops, SparseCore 0:
  73.3 24.6 all-gather.1

commit v4 on v3

v4 whole, which is shorter than its diff:
```python
import functools
import math

import jax
import jax.numpy as jnp
from jax import lax
from jax.experimental import pallas as pl
from jax.experimental.pallas import tpu as pltpu
from jax.sharding import Mesh, PartitionSpec as P

LEVELS = 3
LOW = jnp.bfloat16
WIDE = jnp.float32
MIB = 2**20


def shifted(value, axis, steps):
    count = lax.axis_size(axis)
    first, last = (max(0, -steps), min(count, count - steps))
    return lax.ppermute(value, axis, [(source, source + steps) for source in range(first, last)])


def doubling(gains, spreads, offsets):
    gain = gains[0]
    spread = spreads[0]
    offset = offsets[0]
    size_d = gain.shape[1]
    identity = jnp.eye(size_d, dtype=LOW)
    for section_number in range(LEVELS):
        distance = 2**section_number
        beyond = lax.axis_index("tm") + distance >= lax.axis_size("tm")
        own_gain = gain.astype(LOW)
        own_spread = spread.astype(LOW)
        own_offset = offset.astype(LOW)
        own_full = lax.all_gather(own_gain, "rows", axis=0, tiled=True)
        spread_full = lax.all_gather(own_spread, "rows", axis=0, tiled=True)
        far_full, far_spread_full, far_offset = shifted((own_full, spread_full, own_offset), "tm", -distance)
        far_full = jnp.where(beyond, identity, far_full)
        row_start = lax.axis_index("rows") * gain.shape[0]
        own_rows = lax.dynamic_slice_in_dim(own_full, row_start, gain.shape[0], 0)
        middle = jnp.dot(own_rows, far_spread_full, preferred_element_type=WIDE).astype(LOW)
        new_gain = jnp.dot(own_rows, far_full, preferred_element_type=WIDE)
        new_spread = (
            lax.dot_general(middle, own_full, (((1,), (1,)), ((), ())), preferred_element_type=WIDE) + spread
        )
        new_offset = jnp.dot(own_full, far_offset, preferred_element_type=WIDE) + offset
        gain, spread, offset = (new_gain, new_spread, new_offset)
    return (gain[None], spread[None], offset[None])


def swap(value, axis):
    return lax.ppermute(value, axis, [(0, 1), (1, 0)])


def mm(a, b):
    return jnp.dot(a, b, preferred_element_type=WIDE)


def mm_bt(a, b):
    return lax.dot_general(a, b, (((1,), (1,)), ((), ())), preferred_element_type=WIDE)


GROUP = ("y", "c", "x")


def exchange(blocks):
    return lax.all_to_all(blocks, GROUP, 0, 0)


def held(*shape, dtype=LOW):
    return pltpu.VMEM(shape, dtype)


def low(*shape):
    return jax.ShapeDtypeStruct(shape, LOW)


def wide(*shape):
    return jax.ShapeDtypeStruct(shape, WIDE)


ANY = pl.BlockSpec(memory_space=pl.ANY)
VMEM = pl.BlockSpec(memory_space=pltpu.VMEM)
SMEM = pl.BlockSpec(memory_space=pltpu.SMEM)


def call(kernel, ids, operands, outs, mib, flops=0, scratch=(), aliases={}, far_in=(), far_out=()):
    moved = sum(math.prod(a.shape) * jnp.dtype(a.dtype).itemsize for a in list(operands) + list(outs))
    return pl.pallas_call(
        kernel,
        in_specs=[SMEM] + [ANY if i in far_in else VMEM for i in range(len(operands))],
        out_specs=[ANY if i in far_out else VMEM for i in range(len(outs))],
        out_shape=list(outs),
        scratch_shapes=list(scratch),
        input_output_aliases=aliases,
        cost_estimate=pl.CostEstimate(flops=flops, bytes_accessed=moved, transcendentals=0),
        compiler_params=pltpu.CompilerParams(vmem_limit_bytes=mib * MIB),
    )(ids, *operands)


def gather_lanes(blocks, into, start, width):
    for s in range(blocks.shape[0]):
        into[:, s * width : (s + 1) * width] = blocks[s, :, start : start + width]


def pair_kernel(ids, *refs):
    pieces, (both, pair, quarter) = refs[:8], refs[8:]
    group = 2 * ids[1] + ids[2]
    me = 4 * ids[0] + group
    rows = pieces[0].shape[0]
    for i in range(8):
        place = me ^ i
        both[place >> 2, pl.ds(pl.multiple_of((place & 3) * rows, rows), rows), :] = pieces[i][...]
    for r in range(4):
        cut = slice(r * rows, (r + 1) * rows)
        pair[cut, :] = mm(both[0, cut, :], both[1]).astype(LOW)
    quarter[...] = pair[pl.ds(pl.multiple_of(group * rows, rows), rows), :]


def spread_kernel(ids, both, l_low, l_got, m_ref):
    part, rows = l_got.shape[0], l_low.shape[0]

    def product(slab):
        for r in range(4):
            m = mm_bt(both[0, r * rows : (r + 1) * rows, :], slab).astype(LOW)
            m_ref[2 * r] = m
            m_ref[2 * r + 1] = m

    @pl.when(ids[0] == 0)
    def _():
        product(l_got[...])

    @pl.when(ids[0] == 1)
    def _():
        product(l_low[part:, :])


def spread_start_kernel(ids, blocks, both, spread, l_got, prod, a_l, a_low, m):
    part = l_got.shape[0]
    gather_lanes(blocks, m, 0, part)
    prod[...] = mm_bt(m[...], both[0])

    @pl.when(ids[0] == 0)
    def _():
        a_l[...] = (prod[:part, :] + spread[0, :part, :]).T

    @pl.when(ids[0] == 1)
    def _():
        a_l[...] = (prod[part:, :] + l_got[...].astype(WIDE)).T

    a_low[...] = a_l[...].astype(LOW)


def spread_hop_kernel(ids, pair, both, got, m_ref, near):
    part = got.shape[1]
    rows = 2 * part
    m = mm(pair[...], got[...]).astype(LOW)
    m_ref[...] = m
    other = mm(both[1], got[...]).astype(LOW)
    for r in range(4):
        near[2 * r] = m[r * rows : (r + 1) * rows, :]
        near[2 * r + 1] = other[r * rows : (r + 1) * rows, :]


def spread_next_kernel(ids, blocks, pair, a_l, b_l, m):
    gather_lanes(blocks, m, 0, m.shape[0])
    b_l[...] = (mm_bt(pair[...], m[...]) + a_l[...]).astype(LOW)


def near_kernel(ids, blocks, pair, both, prod, spread, out, m):
    gather_lanes(blocks, m, 0, blocks.shape[2])

    @pl.when(ids[0] == 0)
    def _():
        out[...] = mm_bt(m[...], pair[...]) + prod[...] + spread[0]

    @pl.when(ids[0] == 1)
    def _():
        out[...] = mm_bt(m[...], both[1]) + spread[0]


def compose_kernel(ids, pair, both, *refs):
    quarters, (first, second, slab_ref, following) = refs[:4], refs[4:]
    part, rows = slab_ref.shape[1], quarters[0].shape[0]
    group = 2 * ids[1] + ids[2]

    @pl.when(ids[3] % 2 == 0)
    def _():
        for i in range(4):
            following[pl.ds(pl.multiple_of((group ^ i) * rows, rows), rows), :] = quarters[i][...]
        first[...] = mm(pair[...], following[...]).astype(LOW)
        second[...] = mm(both[1], following[...]).astype(LOW)

    @pl.when(ids[3] % 2 == 1)
    def _():
        first[...] = pair[...]
        second[...] = both[1]

    slab_ref[...] = first[:, pl.ds(pl.multiple_of((2 * group + ids[0]) * part, part), part)]


def far_kernel(ids, first, second, e_a, e_b, l_a, l_b, out, far):
    size, part = e_a.shape
    rows = 2 * part

    @pl.when(ids[3] < 2)
    def _():
        far[:, :part] = e_a[...] + e_b[...]

    @pl.when(ids[3] >= 2)
    def _():
        slab = (2 * ids[1] + ids[2]) * 2 + ids[0]
        column = lax.broadcasted_iota(jnp.int32, (size, part), 1) + slab * part
        row = lax.broadcasted_iota(jnp.int32, (size, part), 0)
        far[:, :part] = jnp.where(row == column, 1.0, 0.0).astype(LOW)

    far[:, part:] = l_a[...] + l_b[...]
    one = mm(first[...], far[...]).astype(LOW)
    two = mm(second[...], far[...]).astype(LOW)
    for r in range(4):
        out[2 * r] = one[r * rows : (r + 1) * rows, :]
        out[2 * r + 1] = two[r * rows : (r + 1) * rows, :]


def end_kernel(ids, blocks, first, second, near, out_gain, out_spread, m):
    part = blocks.shape[2] // 2
    gather_lanes(blocks, m, part, part)
    for s in range(blocks.shape[0]):
        out_gain[:, s * part : (s + 1) * part] = blocks[s, :, :part].astype(WIDE)

    @pl.when(ids[0] == 0)
    def _():
        out_spread[...] = mm_bt(m[...], first[...]) + near[...]

    @pl.when(ids[0] == 1)
    def _():
        out_spread[...] = mm_bt(m[...], second[...]) + near[...]


def columns(ref, side, chunk, width):
    start = side * (ref.shape[1] // 2) + chunk * width
    return ref.at[:, pl.ds(pl.multiple_of(start, width), width)]


def start_kernel(chunk, ids, both, got, offset, p_ref, now, keep, sem):
    copy = pltpu.make_async_copy(columns(offset, ids[0], chunk, keep.shape[1]), keep, sem)
    copy.start()

    @pl.when(ids[0] == 0)
    def _():
        p_ref[...] = mm(both[0], got[...])

    copy.wait()

    @pl.when(ids[0] == 0)
    def _():
        now[...] = (p_ref[...] + keep[...]).astype(LOW)

    @pl.when(ids[0] == 1)
    def _():
        p = mm(both[0], keep[...].astype(LOW))
        p_ref[...] = p
        now[...] = (p + got[...].astype(WIDE)).astype(LOW)


def hop_kernel(ids, pair, got, own, now):
    now[...] = (mm(pair[...], got[...]) + own[...].astype(WIDE)).astype(LOW)


def last_kernel(chunk, ids, pair, both, got_a, got_b, got_c, p_ref, offset, *refs):
    out, send, keep, far, sems = refs[-5:]
    width = keep.shape[1]
    copy = pltpu.make_async_copy(columns(offset, ids[0], chunk, width), keep, sems.at[0])
    copy.start()
    far[...] = got_a[...] + got_b[...] + got_c[...]

    @pl.when(ids[0] == 0)
    def _():
        send[...] = mm(both[1], far[...]).astype(LOW)

    @pl.when(ids[0] == 1)
    def _():
        send[...] = (mm(pair[...], far[...]) + p_ref[...]).astype(LOW)

    copy.wait()

    @pl.when(ids[0] == 0)
    def _():
        keep[...] = mm(pair[...], far[...]) + p_ref[...] + keep[...]

    @pl.when(ids[0] == 1)
    def _():
        keep[...] = mm(both[1], far[...]) + keep[...]

    copy = pltpu.make_async_copy(keep, columns(out, ids[0], chunk, width), sems.at[1])
    copy.start()
    copy.wait()


def add_kernel(chunk, ids, got, offset, into, out, keep, sems):
    width = keep.shape[1]
    copy = pltpu.make_async_copy(columns(offset, 1 - ids[0], chunk, width), keep, sems.at[0])
    copy.start()
    copy.wait()
    keep[...] = got[...].astype(WIDE) + keep[...]
    copy = pltpu.make_async_copy(keep, columns(out, 1 - ids[0], chunk, width), sems.at[1])
    copy.start()
    copy.wait()


def suffix(gains, spreads, offsets):
    x, y, c, z = (lax.axis_index(name) for name in ("x", "y", "c", "z"))
    even = x == 0
    gain, offset = gains[0], offsets[0]
    rows, size_d = gain.shape
    part = rows // 2
    half = offset.shape[1] // 2
    chunks = 2
    width = half // chunks
    ids = jnp.stack([x, y, c, z]).astype(jnp.int32)
    level = [(3, 2), (1, 0)]

    e_low = gain.astype(LOW)
    e_x, e_y = swap(e_low, "x"), swap(e_low, "y")
    e_xy = swap(e_x, "y")
    pieces = [e_low, None, e_y, None, e_x, None, e_xy, None]
    for i in range(0, 8, 2):
        pieces[i + 1] = swap(pieces[i], "c")

    l_low = spreads[0].astype(LOW)
    l_send = jnp.where(even, l_low[part:], l_low[:part])
    g_send = jnp.where(even, offset[:, half:], offset[:, :half]).astype(LOW)
    l_send, g_send, e_x = lax.optimization_barrier((l_send, g_send, e_x))
    l_got = swap(l_send, "x")
    g_got = [swap(g_send[:, i * width : (i + 1) * width], "x") for i in range(chunks)]

    both, a_e, quarter = call(
        pair_kernel, ids, pieces, [held(2, size_d, size_d), held(size_d, size_d), low(rows, size_d)], 16,
        flops=2 * size_d**3,
    )
    (m,) = call(spread_kernel, ids, [both, l_low, l_got], [low(8, rows, part)], 12, flops=2 * part * size_d**2)
    prod, a_l, a_low = call(
        spread_start_kernel, ids, [exchange(m), both, spreads, l_got],
        [held(rows, size_d, dtype=WIDE), held(size_d, part, dtype=WIDE), low(size_d, part)],
        14, flops=2 * rows * size_d**2, scratch=[pltpu.VMEM((rows, size_d), LOW)],
    )

    l_next = lax.ppermute(a_low, "z", level)
    quarter = lax.ppermute(quarter, "z", level)
    quarter_y = swap(quarter, "y")
    quarters = [quarter, swap(quarter, "c"), quarter_y, swap(quarter_y, "c")]
    m, near = call(
        spread_hop_kernel, ids, [a_e, both, l_next], [low(size_d, part), low(8, rows, part)], 12,
        flops=4 * part * size_d**2,
    )
    (b_l,) = call(
        spread_next_kernel, ids, [exchange(m.reshape(8, part, part)), a_e, a_l], [low(size_d, part)], 8,
        flops=2 * part * size_d**2, scratch=[pltpu.VMEM((part, size_d), LOW)],
    )
    l_far = lax.ppermute(b_l, "z", [(2, 1)]), lax.ppermute(b_l, "z", [(2, 0)])
    c0_e, c1_e, e_slab = call(
        compose_kernel, ids, [a_e, both, *quarters],
        [held(size_d, size_d), held(size_d, size_d), low(size_d, part)], 14,
        flops=4 * size_d**3, scratch=[pltpu.VMEM((size_d, size_d), LOW)],
    )
    e_far = lax.ppermute(e_slab, "z", [(2, 1)]), lax.ppermute(e_slab, "z", [(2, 0)])
    (near,) = call(
        near_kernel, ids, [exchange(near), a_e, both, prod, spreads], [held(rows, size_d, dtype=WIDE)], 12,
        flops=2 * rows * size_d**2, scratch=[pltpu.VMEM((rows, size_d), LOW)],
    )

    (m,) = call(
        far_kernel, ids, [c0_e, c1_e, *e_far, *l_far], [low(8, rows, rows)], 12,
        flops=4 * rows * size_d**2, scratch=[pltpu.VMEM((size_d, rows), LOW)],
    )
    out_gain, out_spread = call(
        end_kernel, ids, [exchange(m), c0_e, c1_e, near], [wide(rows, size_d), wide(rows, size_d)], 14,
        flops=2 * rows * size_d**2, scratch=[pltpu.VMEM((rows, size_d), LOW)],
    )

    out_offset, others = None, []
    keep = pltpu.VMEM((size_d, width), WIDE)
    column = pltpu.VMEM((size_d, width), LOW)
    for i in range(chunks):
        p, own = call(
            functools.partial(start_kernel, i), ids, [both, g_got[i], offset],
            [held(size_d, width, dtype=WIDE), low(size_d, width)], 8, flops=2 * size_d**2 * width,
            far_in=(2,), scratch=[keep, pltpu.SemaphoreType.DMA(())],
        )
        now, gots = own, []
        for source in (3, 2, 1):
            gots.append(lax.ppermute(now, "z", [(source, source - 1)]))
            if source > 1:
                (now,) = call(
                    hop_kernel, ids, [a_e, gots[-1], own], [low(size_d, width)], 8, flops=2 * size_d**2 * width
                )
        extra = [] if out_offset is None else [out_offset]
        out_offset, other = call(
            functools.partial(last_kernel, i), ids, [a_e, both] + gots + [p, offset] + extra,
            [wide(*offset.shape), low(size_d, width)], 12, flops=4 * size_d**2 * width,
            far_in=(6, 7), far_out=(0,), aliases={8: 0} if extra else {},
            scratch=[keep, column, pltpu.SemaphoreType.DMA((2,))],
        )
        others.append(swap(other, "x"))
    for i in range(chunks):
        (out_offset,) = call(
            functools.partial(add_kernel, i), ids, [others[i], offset, out_offset], [wide(*offset.shape)], 8,
            far_in=(1, 2), far_out=(0,), aliases={3: 0}, scratch=[keep, pltpu.SemaphoreType.DMA((2,))],
        )
    return (out_gain[None], out_spread[None], out_offset[None])


def solution(mesh):
    steps, rows = mesh.shape["tm"], mesh.shape["rows"]
    if steps == 2**LEVELS and rows == 4:
        devices = mesh.devices.reshape(steps // 2, 2, 2, 2)
        mesh = Mesh(devices, ("z", "x", "y", "c"))
        by_row, by_column = P(("z", "x"), ("y", "c"), None), P(("z", "x"), None, ("y", "c"))
        body = suffix
    else:
        by_row, by_column = P("tm", "rows", None), P("tm", None, "rows")
        body = doubling
    return jax.shard_map(
        body,
        mesh=mesh,
        in_specs=(by_row, by_row, by_column),
        out_specs=(by_row, by_row, by_column),
        check_vma=False,
    )
```

time: 252 us -> 239 us (0.948)
  between operations: 14.5 us -> 1.21 us
  waiting for transfers between devices: 92 us -> 102 us
  local copies, waits for them, and re-layouts: 34.5 us -> 29.6 us
  Pallas kernels: 58.1 us -> 53.4 us
    ppermute x13 -> x15, waiting for transfers between devices: 49 us -> 64.3 us  [swap(): return lax.ppermute(value, axis, [(0, 1), (1, 0)])]
    ppermute x1, waiting for transfers between devices: 14.2 us -> 0.01 us  [suffix(): quarter = lax.ppermute(quarter, 'z', level)]
    ppermute x2, waiting for transfers between devices: 10.8 us -> 17.9 us  [suffix(): l_far = (lax.ppermute(b_l, 'z', [(2, 1)]), lax.ppermute(b_l, 'z', [(2, 0)]))]
    pallas_call x18 -> x19, Pallas kernels: 58.1 us -> 53.4 us  [call(): pl.pallas_call(kernel, in_specs=[SMEM] + [ANY if i in far_in else VMEM fo...]
    unnamed x77 -> x72, local copies, waits for them, and re-layouts: 31.6 us -> 28.5 us
    ppermute x13 -> x15, starting transfers between devices: 14.1 us -> 15 us  [swap(): return lax.ppermute(value, axis, [(0, 1), (1, 0)])]
  transfers between devices with their start and end apart: 30 -> 31, of which waited for: 12 -> 8; matrix products, arithmetic and copies ran while one was open for 3% -> 2% of each run, Pallas kernels for 19% -> 19%
where the time goes in v4:
time: 239 us; the launch traced here: 238 us
  waiting for transfers between devices  102 us (43%)
  Pallas kernels  53.4 us (22%)
  starting transfers between devices  45.9 us (19%)
  local copies, waits for them, and re-layouts  29.6 us (12%)
  other arithmetic  5.34 us (2%)
    ppermute x15, waiting for transfers between devices, swap(): return lax.ppermute(value, axis, [(0, 1), (1, 0)])  64.3 us
    pallas_call x19, Pallas kernels, call(): pl.pallas_call(kernel, in_specs=[SMEM] + [ANY if i in far_in else VMEM fo...  53.4 us
    unnamed x72, local copies, waits for them, and re-layouts  28.5 us
    ppermute x2, waiting for transfers between devices, suffix(): l_far = (lax.ppermute(b_l, 'z', [(2, 1)]), lax.ppermute(b_l, 'z', [(2, 0)]))  17.9 us
    all_to_all x4, starting transfers between devices, exchange(): return lax.all_to_all(blocks, GROUP, 0, 0)  16 us
    ppermute x15, starting transfers between devices, swap(): return lax.ppermute(value, axis, [(0, 1), (1, 0)])  15 us
    ppermute x1, waiting for transfers between devices, suffix(): lax.ppermute(e_slab, 'z', [(2, 0)])  11.1 us
    ppermute x1, waiting for transfers between devices, suffix(): l_next = lax.ppermute(a_low, 'z', level)  8.9 us
  transfers between devices with their start and end apart: 31, of which 8 were waited for; matrix products, arithmetic and copies ran while one was open for 2% of the time, Pallas kernels for 19%

profile of v4, /device:TPU:0, one launch (start us, length us, event | category | flops | bytes accessed | tf_op | source)
XLA Modules:
  0.0 237.8 jit_solution(10927476176036757966)
XLA Ops:
  1.9 3.0 %collective-permute-start.3 = (bf16[256,1024]{1,0:T(8,128)(2,1)S(1)}, bf16[256,1024]{1,0:T(8,128)(2,1)S(1)}, u32[]{:S(2)}, u32[]{:S(2)}) collective-permute-start(bf16[256,1024]{1,0:T(8,128)(2,1)S(1)} %convert_bitcast_fusion.refs_0_), channel_id=1, source_target_pairs={{0,4},{4,0},{1,5},{5,1},{2,6},{6,2},{3,7},{7,3},{8,12},{12,8},{9,1... | collective-permute-start | bytes 1572872 | tf_op jit(solution)/shard_map/ppermute | solution.py:52
  4.9 1.5 collective-permute-start.1
  6.5 10.4 %collective-permute-done.3.refs_4_ = bf16[256,1024]{1,0:T(8,128)(2,1)S(1)} collective-permute-done((bf16[256,1024]{1,0:T(8,128)(2,1)S(1)}, bf16[256,1024]{1,0:T(8,128)(2,1)S(1)}, u32[]{:S(2)}, u32[]{:S(2)}) %collective-permute-start.3) | collective-permute-done | bytes 524320 | tf_op jit(solution)/shard_map/ppermute | solution.py:52
  16.9 1.8 collective-permute-start.5
  20.6 9.3 %collective-permute-done.5.refs_6_ = bf16[256,1024]{1,0:T(8,128)(2,1)S(1)} collective-permute-done((bf16[256,1024]{1,0:T(8,128)(2,1)S(1)}, bf16[256,1024]{1,0:T(8,128)(2,1)S(1)}, u32[]{:S(2)}, u32[]{:S(2)}) %collective-permute-start.5) | collective-permute-done | bytes 524320 | tf_op jit(solution)/shard_map/ppermute | solution.py:52
  30.0 2.6 %fusion = bf16[1024,512]{1,0:T(8,128)(2,1)S(1)} fusion(f32[1024,1024]{1,0:T(8,128)} %bitcast.15, pred[]{:T(512)S(6)} %eq.3), kind=kLoop, calls=%fused_computation.1 | loop fusion | flops 524288 | bytes 3145729 | tf_op jit(solution)/shard_map/convert_element_type | solution.py:332
  36.9 4.5 %shard_map.58 = (bf16[2,1024,1024]{2,1,0:T(8,128)(2,1)S(1)}, bf16[1024,1024]{1,0:T(8,128)(2,1)S(1)}, bf16[256,1024]{1,0:T(8,128)(2,1)}) custom-call(s32[4]{0:T(128)S(1)} %pad_add_fusion.ids, bf16[256,1024]{1,0:T(8,128)(2,1)S(1)} %copy-done.25, bf16[256,1024]{1,0:T(8,128)(2,1)} %collective-permute-done.refs_1_, bf16[256,1024]{1,0:T(8,128)(2,1)S(1)} %copy-done.33, ...), custom_call_target="tpu_custom_call" | custom-call | flops 2147483648 | bytes 11010048 | tf_op jit(solution)/shard_map/pallas_call | solution.py:89
  45.9 1.4 collective-permute-start.13
  47.4 27.7 %collective-permute-done.13.l_got = bf16[128,1024]{1,0:T(8,128)(2,1)S(1)} collective-permute-done((bf16[128,1024]{1,0:T(8,128)(2,1)S(1)}, bf16[128,1024]{1,0:T(8,128)(2,1)S(1)}, u32[]{:S(2)}, u32[]{:S(2)}) %collective-permute-start.13) | collective-permute-done | bytes 262176 | tf_op jit(solution)/shard_map/ppermute | solution.py:52
  76.3 2.0 copy-done
  79.1 4.2 %all-to-all-start = ((bf16[8,256,128]{2,1,0:T(8,128)(2,1)}), bf16[8,256,128]{2,1,0:T(8,128)(2,1)}, u32[]{:S(2)}, u32[]{:S(2)}) async-start(bf16[8,256,128]{2,1,0:T(8,128)(2,1)} %copy-done.17), calls=%async_computation | async-start | bytes 1048576 | tf_op jit(solution)/shard_map/all_to_all | solution.py:67
  83.3 1.9 collective-permute-start.9
  85.2 2.2 copy-done.1
  87.4 2.2 copy-done.6
  89.6 2.9 %shard_map.70 = (f32[1024,256]{1,0:T(8,128)S(1)}, bf16[1024,256]{1,0:T(8,128)(2,1)}) custom-call(s32[4]{0:T(128)S(1)} %pad_add_fusion.ids, bf16[2,1024,1024]{2,1,0:T(8,128)(2,1)S(1)} %copy-done.1, bf16[1024,256]{1,0:T(8,128)(2,1)} %collective-permute-done.21.got, f32[1024,1024]{1,0:T(8,128)S(1)} %bitcast.16), custom_call_target="tpu_custom_call" | custom-call | flops 536870912 | bytes 10485760 | tf_op jit(solution)/shard_map/pallas_call | solution.py:89
  93.5 1.5 collective-permute-start.22
  95.0 2.9 %shard_map.67 = (f32[1024,256]{1,0:T(8,128)S(1)}, bf16[1024,256]{1,0:T(8,128)(2,1)}) custom-call(s32[4]{0:T(128)S(1)} %pad_add_fusion.ids, bf16[2,1024,1024]{2,1,0:T(8,128)(2,1)S(1)} %copy-done.1, bf16[1024,256]{1,0:T(8,128)(2,1)} %collective-permute-done.17.got, f32[1024,1024]{1,0:T(8,128)S(1)} %bitcast.17), custom_call_target="tpu_custom_call" | custom-call | flops 536870912 | bytes 10485760 | tf_op jit(solution)/shard_map/pallas_call | solution.py:89
  98.9 1.5 collective-permute-start.18
  100.3 2.2 copy-done.2
  102.5 2.2 shard_map.61
  106.6 8.9 %collective-permute-done.14.got = bf16[1024,128]{1,0:T(8,128)(2,1)S(1)} collective-permute-done((bf16[1024,128]{1,0:T(8,128)(2,1)S(1)}, bf16[1024,128]{1,0:T(8,128)(2,1)S(1)}, u32[]{:S(2)}, u32[]{:S(2)}) %collective-permute-start.14) | collective-permute-done | bytes 262176 | tf_op jit(solution)/shard_map/ppermute | solution.py:348
  115.5 1.8 shard_map.62
  118.8 3.4 %all-to-all-start.1 = ((bf16[8,128,128]{2,1,0:T(8,128)(2,1)}), bf16[8,128,128]{2,1,0:T(8,128)(2,1)S(1)}, u32[]{:S(2)}, u32[]{:S(2)}) async-start(bf16[8,128,128]{2,1,0:T(8,128)(2,1)} %bitcast.22), calls=%async_computation.1 | async-start | bytes 524288 | tf_op jit(solution)/shard_map/all_to_all | solution.py:67
  122.3 2.8 %shard_map.71 = bf16[1024,256]{1,0:T(8,128)(2,1)} custom-call(s32[4]{0:T(128)S(1)} %pad_add_fusion.ids, bf16[1024,1024]{1,0:T(8,128)(2,1)S(1)} %get-tuple-element.26.pair, bf16[1024,256]{1,0:T(8,128)(2,1)} %collective-permute-done.22.got.got_a, bf16[1024,256]{1,0:T(8,128)(2,1)} %get-tuple-element.43.own), custom_call_target="tpu_custom_call" | custom-call | flops 536870912 | bytes 3670016 | tf_op jit(solution)/shard_map/pallas_call | solution.py:89
  125.0 1.4 collective-permute-start.23
  126.5 2.7 %shard_map.68 = bf16[1024,256]{1,0:T(8,128)(2,1)} custom-call(s32[4]{0:T(128)S(1)} %pad_add_fusion.ids, bf16[1024,1024]{1,0:T(8,128)(2,1)S(1)} %get-tuple-element.26.pair, bf16[1024,256]{1,0:T(8,128)(2,1)} %collective-permute-done.18.got.got_a, bf16[1024,256]{1,0:T(8,128)(2,1)} %get-tuple-element.41.own), custom_call_target="tpu_custom_call" | custom-call | flops 536870912 | bytes 3670016 | tf_op jit(solution)/shard_map/pallas_call | solution.py:89
  129.2 1.5 collective-permute-start.19
  130.7 4.2 %all-to-all-start.3 = ((bf16[8,256,128]{2,1,0:T(8,128)(2,1)}), bf16[8,256,128]{2,1,0:T(8,128)(2,1)}, u32[]{:S(2)}, u32[]{:S(2)}) async-start(bf16[8,256,128]{2,1,0:T(8,128)(2,1)} %copy-done.26), calls=%async_computation.3 | async-start | bytes 1048576 | tf_op jit(solution)/shard_map/all_to_all | solution.py:67
  139.1 2.2 copy-done.4
  141.3 6.4 %shard_map.59 = (bf16[1024,1024]{1,0:T(8,128)(2,1)S(1)}, bf16[1024,1024]{1,0:T(8,128)(2,1)S(1)}, bf16[1024,128]{1,0:T(8,128)(2,1)S(1)}) custom-call(s32[4]{0:T(128)S(1)} %pad_add_fusion.ids, bf16[1024,1024]{1,0:T(8,128)(2,1)S(1)} %get-tuple-element.26.pair, bf16[2,1024,1024]{2,1,0:T(8,128)(2,1)S(1)} %copy-done.4, ...), custom_call_target="tpu_custom_call" | custom-call | flops 4294967296 | bytes 12845056 | tf_op jit(solution)/shard_map/pallas_call | solution.py:89
  149.8 2.7 %shard_map.72 = bf16[1024,256]{1,0:T(8,128)(2,1)} custom-call(s32[4]{0:T(128)S(1)} %pad_add_fusion.ids, bf16[1024,1024]{1,0:T(8,128)(2,1)S(1)} %get-tuple-element.26.pair, bf16[1024,256]{1,0:T(8,128)(2,1)} %collective-permute-done.23.got.got_b, bf16[1024,256]{1,0:T(8,128)(2,1)} %get-tuple-element.43.own), custom_call_target="tpu_custom_call" | custom-call | flops 536870912 | bytes 3670016 | tf_op jit(solution)/shard_map/pallas_call | solution.py:89
  153.8 2.7 %shard_map.69 = bf16[1024,256]{1,0:T(8,128)(2,1)} custom-call(s32[4]{0:T(128)S(1)} %pad_add_fusion.ids, bf16[1024,1024]{1,0:T(8,128)(2,1)S(1)} %get-tuple-element.26.pair, bf16[1024,256]{1,0:T(8,128)(2,1)} %collective-permute-done.19.got.got_b, bf16[1024,256]{1,0:T(8,128)(2,1)} %get-tuple-element.41.own), custom_call_target="tpu_custom_call" | custom-call | flops 536870912 | bytes 3670016 | tf_op jit(solution)/shard_map/pallas_call | solution.py:89
  157.8 17.9 %collective-permute-done.16.l_b = bf16[1024,128]{1,0:T(8,128)(2,1)S(1)} collective-permute-done((bf16[1024,128]{1,0:T(8,128)(2,1)S(1)}, bf16[1024,128]{1,0:T(8,128)(2,1)S(1)}, u32[]{:S(2)}, u32[]{:S(2)}) %collective-permute-start.16) | collective-permute-done | bytes 262176 | tf_op jit(solution)/shard_map/ppermute | solution.py:360
  175.7 11.1 %collective-permute-done.12.e_b = bf16[1024,128]{1,0:T(8,128)(2,1)S(1)} collective-permute-done((bf16[1024,128]{1,0:T(8,128)(2,1)S(1)}, bf16[1024,128]{1,0:T(8,128)(2,1)S(1)}, u32[]{:S(2)}, u32[]{:S(2)}) %collective-permute-start.12) | collective-permute-done | bytes 262176 | tf_op jit(solution)/shard_map/ppermute | solution.py:366
  186.8 1.9 shard_map.64
  189.7 4.3 %all-to-all-start.2 = ((bf16[8,256,256]{2,1,0:T(8,128)(2,1)}), bf16[8,256,256]{2,1,0:T(8,128)(2,1)}, u32[]{:S(2)}, u32[]{:S(2)}) async-start(bf16[8,256,256]{2,1,0:T(8,128)(2,1)} %copy-done.16), calls=%async_computation.2 | async-start | bytes 2097152 | tf_op jit(solution)/shard_map/all_to_all | solution.py:67
  194.0 2.2 copy-done.5
  196.1 2.2 copy-done.7
  199.6 4.1 %shard_map.73 = (f32[1024,1024]{1,0:T(8,128)}, bf16[1024,256]{1,0:T(8,128)(2,1)S(1)}) custom-call(s32[4]{0:T(128)S(1)} %pad_add_fusion.ids, bf16[1024,1024]{1,0:T(8,128)(2,1)S(1)} %get-tuple-element.26.pair, bf16[2,1024,1024]{2,1,0:T(8,128)(2,1)S(1)} %copy-done.5, bf16[1024,256]{1,0:T(8,128)(2,1)} %collective-permute-done.22.got.got_a, ...), custom_call_target="tpu_custom_call" | custom-call | flops 1073741824 | bytes 17825792 | tf_op jit(solution)/shard_map/pallas_call | solution.py:89
  203.7 1.9 collective-permute-start.26
  205.6 4.1 %shard_map.74 = (f32[1024,1024]{1,0:T(8,128)}, bf16[1024,256]{1,0:T(8,128)(2,1)S(1)}) custom-call(s32[4]{0:T(128)S(1)} %pad_add_fusion.ids, bf16[1024,1024]{1,0:T(8,128)(2,1)S(1)} %get-tuple-element.26.pair, bf16[2,1024,1024]{2,1,0:T(8,128)(2,1)S(1)} %copy-done.5, ...), custom_call_target="tpu_custom_call", output_to_operand_aliasing={{0}: (8, {})} | custom-call | flops 1073741824 | bytes 22020096 | tf_op jit(solution)/shard_map/pallas_call | solution.py:89
  210.0 2.1 shard_map.65.near
  212.1 7.9 %collective-permute-done.26.got = bf16[1024,256]{1,0:T(8,128)(2,1)S(1)} collective-permute-done((bf16[1024,256]{1,0:T(8,128)(2,1)S(1)}, bf16[1024,256]{1,0:T(8,128)(2,1)S(1)}, u32[]{:S(2)}, u32[]{:S(2)}) %collective-permute-start.26) | collective-permute-done | bytes 524320 | tf_op jit(solution)/shard_map/ppermute | solution.py:52
  220.0 1.8 shard_map.75.into
  221.8 8.9 %collective-permute-done.25.got = bf16[1024,256]{1,0:T(8,128)(2,1)S(1)} collective-permute-done((bf16[1024,256]{1,0:T(8,128)(2,1)S(1)}, bf16[1024,256]{1,0:T(8,128)(2,1)S(1)}, u32[]{:S(2)}, u32[]{:S(2)}) %collective-permute-start.25) | collective-permute-done | bytes 524320 | tf_op jit(solution)/shard_map/ppermute | solution.py:52
  230.8 1.8 shard_map.76
  232.6 1.6 copy-done.13
  234.2 3.6 %shard_map.66 = (f32[256,1024]{1,0:T(8,128)}, f32[256,1024]{1,0:T(8,128)}) custom-call(s32[4]{0:T(128)S(1)} %pad_add_fusion.ids, bf16[8,256,256]{2,1,0:T(8,128)(2,1)} %all-to-all-done.2.blocks, bf16[1024,1024]{1,0:T(8,128)(2,1)S(1)} %copy-done.11, bf16[1024,1024]{1,0:T(8,128)(2,1)S(1)} %copy-done.13, f32[256,1024]{1,0:T(8,128)S(1)} %copy-done.15), custom_call_target="tpu_custom_call" | custom-call | flops 536870912 | bytes 8388608 | tf_op jit(solution)/shard_map/pallas_call | solution.py:89
  (112 shorter events, 30.8 us)
Async XLA Ops:
  1.9 30.7 %copy-start.24 = (bf16[256,1024]{1,0:T(8,128)(2,1)}, bf16[256,1024]{1,0:T(8,128)(2,1)S(1)}, u32[]{:S(2)}) copy-start(bf16[256,1024]{1,0:T(8,128)(2,1)S(1)} %convert_bitcast_fusion.refs_0_) | copy-start | bytes 1572868
  1.9 14.9 %collective-permute-start.3 = (bf16[256,1024]{1,0:T(8,128)(2,1)S(1)}, bf16[256,1024]{1,0:T(8,128)(2,1)S(1)}, u32[]{:S(2)}, u32[]{:S(2)}) collective-permute-start(bf16[256,1024]{1,0:T(8,128)(2,1)S(1)} %convert_bitcast_fusion.refs_0_), channel_id=1, source_target_pairs={{0,4},{4,0},{1,5},{5,1},{2,6},{6,2},{3,7},{7,3},{8,12},{12,8},{9,1... | collective-permute-start | bytes 1572872 | tf_op jit(solution)/shard_map/ppermute | solution.py:52
  4.9 15.6 %collective-permute-start.1 = (bf16[256,1024]{1,0:T(8,128)(2,1)S(1)}, bf16[256,1024]{1,0:T(8,128)(2,1)S(1)}, u32[]{:S(2)}, u32[]{:S(2)}) collective-permute-start(bf16[256,1024]{1,0:T(8,128)(2,1)S(1)} %convert_bitcast_fusion.refs_0_), channel_id=1, source_target_pairs={{0,2},{2,0},{1,3},{3,1},{4,6},{6,4},{5,7},{7,5},{8,10},{10,8},{9,1... | collective-permute-start | bytes 1572872 | tf_op jit(solution)/shard_map/ppermute | solution.py:52
  16.9 15.8 %copy-start.30 = (bf16[256,1024]{1,0:T(8,128)(2,1)}, bf16[256,1024]{1,0:T(8,128)(2,1)S(1)}, u32[]{:S(2)}) copy-start(bf16[256,1024]{1,0:T(8,128)(2,1)S(1)} %collective-permute-done.3.refs_4_) | copy-start | bytes 1572868
  16.9 13.1 %collective-permute-start.5 = (bf16[256,1024]{1,0:T(8,128)(2,1)S(1)}, bf16[256,1024]{1,0:T(8,128)(2,1)S(1)}, u32[]{:S(2)}, u32[]{:S(2)}) collective-permute-start(bf16[256,1024]{1,0:T(8,128)(2,1)S(1)} %collective-permute-done.3.refs_4_), channel_id=1, source_target_pairs={{0,2},{2,0},{1,3},{3,1},{4,6},{6,4},{5,7},{7,5},{8,10},{10,8},{9,1... | collective-permute-start | bytes 1572872 | tf_op jit(solution)/shard_map/ppermute | solution.py:52
  18.6 14.0 %collective-permute-start = (bf16[256,1024]{1,0:T(8,128)(2,1)S(1)}, bf16[256,1024]{1,0:T(8,128)(2,1)}, u32[]{:S(2)}, u32[]{:S(2)}) collective-permute-start(bf16[256,1024]{1,0:T(8,128)(2,1)S(1)} %convert_bitcast_fusion.refs_0_), channel_id=1, source_target_pairs={{0,1},{1,0},{2,3},{3,2},{4,5},{5,4},{6,7},{7,6},{8,9},{9,8},{10,11... | collective-permute-start | bytes 1572872 | tf_op jit(solution)/shard_map/ppermute | solution.py:52
  20.0 12.6 %collective-permute-start.4 = (bf16[256,1024]{1,0:T(8,128)(2,1)S(1)}, bf16[256,1024]{1,0:T(8,128)(2,1)S(1)}, u32[]{:S(2)}, u32[]{:S(2)}) collective-permute-start(bf16[256,1024]{1,0:T(8,128)(2,1)S(1)} %collective-permute-done.3.refs_4_), channel_id=1, source_target_pairs={{0,1},{1,0},{2,3},{3,2},{4,5},{5,4},{6,7},{7,6},{8,9},{9,8},{10,11... | collective-permute-start | bytes 1572872 | tf_op jit(solution)/shard_map/ppermute | solution.py:52
  20.6 12.1 %copy-start.32 = (bf16[256,1024]{1,0:T(8,128)(2,1)}, bf16[256,1024]{1,0:T(8,128)(2,1)S(1)}, u32[]{:S(2)}) copy-start(bf16[256,1024]{1,0:T(8,128)(2,1)S(1)} %collective-permute-done.1.refs_2_) | copy-start | bytes 1572868
  20.6 12.1 %collective-permute-start.2 = (bf16[256,1024]{1,0:T(8,128)(2,1)S(1)}, bf16[256,1024]{1,0:T(8,128)(2,1)S(1)}, u32[]{:S(2)}, u32[]{:S(2)}) collective-permute-start(bf16[256,1024]{1,0:T(8,128)(2,1)S(1)} %collective-permute-done.1.refs_2_), channel_id=1, source_target_pairs={{0,1},{1,0},{2,3},{3,2},{4,5},{5,4},{6,7},{7,6},{8,9},{9,8},{10,11... | collective-permute-start | bytes 1572872 | tf_op jit(solution)/shard_map/ppermute | solution.py:52
  30.0 2.7 %copy-start.34 = (bf16[256,1024]{1,0:T(8,128)(2,1)}, bf16[256,1024]{1,0:T(8,128)(2,1)S(1)}, u32[]{:S(2)}) copy-start(bf16[256,1024]{1,0:T(8,128)(2,1)S(1)} %collective-permute-done.5.refs_6_) | copy-start | bytes 1572868
  30.0 2.7 %collective-permute-start.6 = (bf16[256,1024]{1,0:T(8,128)(2,1)S(1)}, bf16[256,1024]{1,0:T(8,128)(2,1)S(1)}, u32[]{:S(2)}, u32[]{:S(2)}) collective-permute-start(bf16[256,1024]{1,0:T(8,128)(2,1)S(1)} %collective-permute-done.5.refs_6_), channel_id=1, source_target_pairs={{0,1},{1,0},{2,3},{3,2},{4,5},{5,4},{6,7},{7,6},{8,9},{9,8},{10,11... | collective-permute-start | bytes 1572872 | tf_op jit(solution)/shard_map/ppermute | solution.py:52
  32.6 14.7 %copy-start.9 = (f32[1,256,1024]{2,1,0:T(8,128)S(1)}, f32[1,256,1024]{2,1,0:T(8,128)}, u32[]{:S(2)}) copy-start(f32[1,256,1024]{2,1,0:T(8,128)} %spread.3) | copy-start | bytes 3145732
  41.4 41.9 %collective-permute-start.7 = (bf16[256,1024]{1,0:T(8,128)(2,1)}, bf16[256,1024]{1,0:T(8,128)(2,1)}, u32[]{:S(2)}, u32[]{:S(2)}) collective-permute-start(bf16[256,1024]{1,0:T(8,128)(2,1)} %get-tuple-element.28), channel_id=1, source_target_pairs={{24,16},{8,0},{25,17},{9,1},{26,18},{10,2},{27,19},{11,3},{28,20},... | collective-permute-start | bytes 1572872 | tf_op jit(solution)/shard_map/ppermute | solution.py:349
  43.8 41.4 %collective-permute-start.21 = (bf16[1024,256]{1,0:T(8,128)(2,1)}, bf16[1024,256]{1,0:T(8,128)(2,1)}, u32[]{:S(2)}, u32[]{:S(2)}) collective-permute-start(bf16[1024,256]{1,0:T(8,128)(2,1)} %get-tuple-element.49), channel_id=1, source_target_pairs={{0,4},{4,0},{1,5},{5,1},{2,6},{6,2},{3,7},{7,3},{8,12},{12,8},{9,1... | collective-permute-start | bytes 1572872 | tf_op jit(solution)/shard_map/ppermute | solution.py:52
  45.2 49.7 %collective-permute-start.17 = (bf16[1024,256]{1,0:T(8,128)(2,1)}, bf16[1024,256]{1,0:T(8,128)(2,1)}, u32[]{:S(2)}, u32[]{:S(2)}) collective-permute-start(bf16[1024,256]{1,0:T(8,128)(2,1)} %get-tuple-element.50), channel_id=1, source_target_pairs={{0,4},{4,0},{1,5},{5,1},{2,6},{6,2},{3,7},{7,3},{8,12},{12,8},{9,1... | collective-permute-start | bytes 1572872 | tf_op jit(solution)/shard_map/ppermute | solution.py:52
  45.9 29.2 %collective-permute-start.13 = (bf16[128,1024]{1,0:T(8,128)(2,1)S(1)}, bf16[128,1024]{1,0:T(8,128)(2,1)S(1)}, u32[]{:S(2)}, u32[]{:S(2)}) collective-permute-start(bf16[128,1024]{1,0:T(8,128)(2,1)S(1)} %fusion.1), channel_id=1, source_target_pairs={{0,4},{4,0},{1,5},{5,1},{2,6},{6,2},{3,7},{7,3},{8,12},{12,8},{9,1... | collective-permute-start | bytes 786440 | tf_op jit(solution)/shard_map/ppermute | solution.py:52
  79.1 21.2 %all-to-all-start = ((bf16[8,256,128]{2,1,0:T(8,128)(2,1)}), bf16[8,256,128]{2,1,0:T(8,128)(2,1)}, u32[]{:S(2)}, u32[]{:S(2)}) async-start(bf16[8,256,128]{2,1,0:T(8,128)(2,1)} %copy-done.17), calls=%async_computation | async-start | bytes 1048576 | tf_op jit(solution)/shard_map/all_to_all | solution.py:67
  83.3 22.8 %collective-permute-start.9 = (bf16[256,1024]{1,0:T(8,128)(2,1)}, bf16[256,1024]{1,0:T(8,128)(2,1)}, u32[]{:S(2)}, u32[]{:S(2)}) collective-permute-start(bf16[256,1024]{1,0:T(8,128)(2,1)} %collective-permute-done.7.refs_0_), channel_id=1, source_target_pairs={{0,2},{2,0},{1,3},{3,1},{4,6},{6,4},{5,7},{7,5},{8,10},{10,8},{9,1... | collective-permute-start | bytes 1572872 | tf_op jit(solution)/shard_map/ppermute | solution.py:52
  93.5 28.8 %collective-permute-start.22 = (bf16[1024,256]{1,0:T(8,128)(2,1)}, bf16[1024,256]{1,0:T(8,128)(2,1)}, u32[]{:S(2)}, u32[]{:S(2)}) collective-permute-start(bf16[1024,256]{1,0:T(8,128)(2,1)} %get-tuple-element.43.own), channel_id=1, source_target_pairs={{24,16},{25,17},{26,18},{27,19},{28,20},{29,21},{30,22},{31,23}} | collective-permute-start | bytes 1572872 | tf_op jit(solution)/shard_map/ppermute | solution.py:392
  98.9 27.6 %collective-permute-start.18 = (bf16[1024,256]{1,0:T(8,128)(2,1)}, bf16[1024,256]{1,0:T(8,128)(2,1)}, u32[]{:S(2)}, u32[]{:S(2)}) collective-permute-start(bf16[1024,256]{1,0:T(8,128)(2,1)} %get-tuple-element.41.own), channel_id=1, source_target_pairs={{24,16},{25,17},{26,18},{27,19},{28,20},{29,21},{30,22},{31,23}} | collective-permute-start | bytes 1572872 | tf_op jit(solution)/shard_map/ppermute | solution.py:392
  102.5 13.0 %copy-start.3 = (bf16[2,1024,1024]{2,1,0:T(8,128)(2,1)S(1)}, bf16[2,1024,1024]{2,1,0:T(8,128)(2,1)}, u32[]{:S(2)}) copy-start(bf16[2,1024,1024]{2,1,0:T(8,128)(2,1)} %copy-done) | copy-start | bytes 12582916
  104.7 12.6 %copy-start.20 = (f32[256,1024]{1,0:T(8,128)}, f32[256,1024]{1,0:T(8,128)S(1)}, u32[]{:S(2)}) copy-start(f32[256,1024]{1,0:T(8,128)S(1)} %get-tuple-element.37.prod) | copy-start | bytes 3145732
  104.7 14.1 %copy-start.27 = (f32[1024,128]{1,0:T(8,128)}, f32[1024,128]{1,0:T(8,128)S(1)}, u32[]{:S(2)}) copy-start(f32[1024,128]{1,0:T(8,128)S(1)} %get-tuple-element.35.a_l) | copy-start | bytes 1572868
  104.7 10.8 %collective-permute-start.14 = (bf16[1024,128]{1,0:T(8,128)(2,1)S(1)}, bf16[1024,128]{1,0:T(8,128)(2,1)S(1)}, u32[]{:S(2)}, u32[]{:S(2)}) collective-permute-start(bf16[1024,128]{1,0:T(8,128)(2,1)S(1)} %get-tuple-element.33), channel_id=1, source_target_pairs={{24,16},{8,0},{25,17},{9,1},{26,18},{10,2},{27,19},{11,3},{28,20},... | collective-permute-start | bytes 786440 | tf_op jit(solution)/shard_map/ppermute | solution.py:348
  106.0 31.8 %collective-permute-start.8 = (bf16[256,1024]{1,0:T(8,128)(2,1)}, bf16[256,1024]{1,0:T(8,128)(2,1)}, u32[]{:S(2)}, u32[]{:S(2)}) collective-permute-start(bf16[256,1024]{1,0:T(8,128)(2,1)} %collective-permute-done.7.refs_0_), channel_id=1, source_target_pairs={{0,1},{1,0},{2,3},{3,2},{4,5},{5,4},{6,7},{7,6},{8,9},{9,8},{10,11... | collective-permute-start | bytes 1572872 | tf_op jit(solution)/shard_map/ppermute | solution.py:52
  106.1 33.0 %collective-permute-start.10 = (bf16[256,1024]{1,0:T(8,128)(2,1)}, bf16[256,1024]{1,0:T(8,128)(2,1)}, u32[]{:S(2)}, u32[]{:S(2)}) collective-permute-start(bf16[256,1024]{1,0:T(8,128)(2,1)} %collective-permute-done.9.refs_2_), channel_id=1, source_target_pairs={{0,1},{1,0},{2,3},{3,2},{4,5},{5,4},{6,7},{7,6},{8,9},{9,8},{10,11... | collective-permute-start | bytes 1572872 | tf_op jit(solution)/shard_map/ppermute | solution.py:52
  118.8 11.8 %all-to-all-start.1 = ((bf16[8,128,128]{2,1,0:T(8,128)(2,1)}), bf16[8,128,128]{2,1,0:T(8,128)(2,1)S(1)}, u32[]{:S(2)}, u32[]{:S(2)}) async-start(bf16[8,128,128]{2,1,0:T(8,128)(2,1)} %bitcast.22), calls=%async_computation.1 | async-start | bytes 524288 | tf_op jit(solution)/shard_map/all_to_all | solution.py:67
  125.0 23.4 %collective-permute-start.23 = (bf16[1024,256]{1,0:T(8,128)(2,1)}, bf16[1024,256]{1,0:T(8,128)(2,1)}, u32[]{:S(2)}, u32[]{:S(2)}) collective-permute-start(bf16[1024,256]{1,0:T(8,128)(2,1)} %shard_map.71), channel_id=1, source_target_pairs={{16,8},{17,9},{18,10},{19,11},{20,12},{21,13},{22,14},{23,15}} | collective-permute-start | bytes 1572872 | tf_op jit(solution)/shard_map/ppermute | solution.py:392
  129.2 23.3 %collective-permute-start.19 = (bf16[1024,256]{1,0:T(8,128)(2,1)}, bf16[1024,256]{1,0:T(8,128)(2,1)}, u32[]{:S(2)}, u32[]{:S(2)}) collective-permute-start(bf16[1024,256]{1,0:T(8,128)(2,1)} %shard_map.68), channel_id=1, source_target_pairs={{16,8},{17,9},{18,10},{19,11},{20,12},{21,13},{22,14},{23,15}} | collective-permute-start | bytes 1572872 | tf_op jit(solution)/shard_map/ppermute | solution.py:392
  130.7 59.0 %all-to-all-start.3 = ((bf16[8,256,128]{2,1,0:T(8,128)(2,1)}), bf16[8,256,128]{2,1,0:T(8,128)(2,1)}, u32[]{:S(2)}, u32[]{:S(2)}) async-start(bf16[8,256,128]{2,1,0:T(8,128)(2,1)} %copy-done.26), calls=%async_computation.3 | async-start | bytes 1048576 | tf_op jit(solution)/shard_map/all_to_all | solution.py:67
  137.1 19.4 %collective-permute-start.15 = (bf16[1024,128]{1,0:T(8,128)(2,1)S(1)}, bf16[1024,128]{1,0:T(8,128)(2,1)S(1)}, u32[]{:S(2)}, u32[]{:S(2)}) collective-permute-start(bf16[1024,128]{1,0:T(8,128)(2,1)S(1)} %shard_map.63), channel_id=1, source_target_pairs={{16,8},{17,9},{18,10},{19,11},{20,12},{21,13},{22,14},{23,15}} | collective-permute-start | bytes 786440 | tf_op jit(solution)/shard_map/ppermute | solution.py:360
  137.8 37.9 %collective-permute-start.16 = (bf16[1024,128]{1,0:T(8,128)(2,1)S(1)}, bf16[1024,128]{1,0:T(8,128)(2,1)S(1)}, u32[]{:S(2)}, u32[]{:S(2)}) collective-permute-start(bf16[1024,128]{1,0:T(8,128)(2,1)S(1)} %shard_map.63), channel_id=1, source_target_pairs={{16,0},{17,1},{18,2},{19,3},{20,4},{21,5},{22,6},{23,7}} | collective-permute-start | bytes 786440 | tf_op jit(solution)/shard_map/ppermute | solution.py:360
  139.1 2.2 copy-start.4
  147.8 39.0 %copy-start.10 = (bf16[1024,1024]{1,0:T(8,128)(2,1)}, bf16[1024,1024]{1,0:T(8,128)(2,1)S(1)}, u32[]{:S(2)}) copy-start(bf16[1024,1024]{1,0:T(8,128)(2,1)S(1)} %get-tuple-element.29.first) | copy-start | bytes 6291460
  147.8 39.0 %copy-start.12 = (bf16[1024,1024]{1,0:T(8,128)(2,1)}, bf16[1024,1024]{1,0:T(8,128)(2,1)S(1)}, u32[]{:S(2)}) copy-start(bf16[1024,1024]{1,0:T(8,128)(2,1)S(1)} %get-tuple-element.30.second) | copy-start | bytes 6291460
  147.8 28.0 %collective-permute-start.11 = (bf16[1024,128]{1,0:T(8,128)(2,1)S(1)}, bf16[1024,128]{1,0:T(8,128)(2,1)S(1)}, u32[]{:S(2)}, u32[]{:S(2)}) collective-permute-start(bf16[1024,128]{1,0:T(8,128)(2,1)S(1)} %get-tuple-element.31), channel_id=1, source_target_pairs={{16,8},{17,9},{18,10},{19,11},{20,12},{21,13},{22,14},{23,15}} | collective-permute-start | bytes 786440 | tf_op jit(solution)/shard_map/ppermute | solution.py:366
  148.5 38.3 %collective-permute-start.12 = (bf16[1024,128]{1,0:T(8,128)(2,1)S(1)}, bf16[1024,128]{1,0:T(8,128)(2,1)S(1)}, u32[]{:S(2)}, u32[]{:S(2)}) collective-permute-start(bf16[1024,128]{1,0:T(8,128)(2,1)S(1)} %get-tuple-element.31), channel_id=1, source_target_pairs={{16,0},{17,1},{18,2},{19,3},{20,4},{21,5},{22,6},{23,7}} | collective-permute-start | bytes 786440 | tf_op jit(solution)/shard_map/ppermute | solution.py:366
  152.5 41.4 %collective-permute-start.24 = (bf16[1024,256]{1,0:T(8,128)(2,1)}, bf16[1024,256]{1,0:T(8,128)(2,1)}, u32[]{:S(2)}, u32[]{:S(2)}) collective-permute-start(bf16[1024,256]{1,0:T(8,128)(2,1)} %shard_map.72), channel_id=1, source_target_pairs={{8,0},{9,1},{10,2},{11,3},{12,4},{13,5},{14,6},{15,7}} | collective-permute-start | bytes 1572872 | tf_op jit(solution)/shard_map/ppermute | solution.py:392
  156.5 49.1 %collective-permute-start.20 = (bf16[1024,256]{1,0:T(8,128)(2,1)}, bf16[1024,256]{1,0:T(8,128)(2,1)}, u32[]{:S(2)}, u32[]{:S(2)}) collective-permute-start(bf16[1024,256]{1,0:T(8,128)(2,1)} %shard_map.69), channel_id=1, source_target_pairs={{8,0},{9,1},{10,2},{11,3},{12,4},{13,5},{14,6},{15,7}} | collective-permute-start | bytes 1572872 | tf_op jit(solution)/shard_map/ppermute | solution.py:392
  189.7 42.9 %all-to-all-start.2 = ((bf16[8,256,256]{2,1,0:T(8,128)(2,1)}), bf16[8,256,256]{2,1,0:T(8,128)(2,1)}, u32[]{:S(2)}, u32[]{:S(2)}) async-start(bf16[8,256,256]{2,1,0:T(8,128)(2,1)} %copy-done.16), calls=%async_computation.2 | async-start | bytes 2097152 | tf_op jit(solution)/shard_map/all_to_all | solution.py:67
  193.9 2.2 copy-start.5
  199.5 6.1 %copy-start.19 = (f32[1024,256]{1,0:T(8,128)S(1)}, f32[1024,256]{1,0:T(8,128)}, u32[]{:S(2)}) copy-start(f32[1024,256]{1,0:T(8,128)} %copy-done.18) | copy-start | bytes 3145732
  203.7 16.3 %collective-permute-start.26 = (bf16[1024,256]{1,0:T(8,128)(2,1)S(1)}, bf16[1024,256]{1,0:T(8,128)(2,1)S(1)}, u32[]{:S(2)}, u32[]{:S(2)}) collective-permute-start(bf16[1024,256]{1,0:T(8,128)(2,1)S(1)} %get-tuple-element.47), channel_id=1, source_target_pairs={{0,4},{4,0},{1,5},{5,1},{2,6},{6,2},{3,7},{7,3},{8,12},{12,8},{9,1... | collective-permute-start | bytes 1572872 | tf_op jit(solution)/shard_map/ppermute | solution.py:52
  205.6 4.4 %copy-start.21 = (f32[256,1024]{1,0:T(8,128)S(1)}, f32[256,1024]{1,0:T(8,128)}, u32[]{:S(2)}) copy-start(f32[256,1024]{1,0:T(8,128)} %copy-done.20) | copy-start | bytes 3145732
  209.8 21.0 %collective-permute-start.25 = (bf16[1024,256]{1,0:T(8,128)(2,1)S(1)}, bf16[1024,256]{1,0:T(8,128)(2,1)S(1)}, u32[]{:S(2)}, u32[]{:S(2)}) collective-permute-start(bf16[1024,256]{1,0:T(8,128)(2,1)S(1)} %get-tuple-element.46), channel_id=1, source_target_pairs={{0,4},{4,0},{1,5},{5,1},{2,6},{6,2},{3,7},{7,3},{8,12},{12,8},{9,1... | collective-permute-start | bytes 1572872 | tf_op jit(solution)/shard_map/ppermute | solution.py:52
  210.0 10.0 %copy-start.8 = (f32[1,1024,1024]{2,1,0:T(8,128)S(1)}, f32[1,1024,1024]{2,1,0:T(8,128)}, u32[]{:S(2)}) copy-start(f32[1,1024,1024]{2,1,0:T(8,128)} %param.5) | copy-start | bytes 12582916
  212.1 9.7 %copy-start.14 = (f32[256,1024]{1,0:T(8,128)}, f32[256,1024]{1,0:T(8,128)S(1)}, u32[]{:S(2)}) copy-start(f32[256,1024]{1,0:T(8,128)S(1)} %shard_map.65.near) | copy-start | bytes 3145732
  221.8 10.8 %copy-start.11 = (bf16[1024,1024]{1,0:T(8,128)(2,1)S(1)}, bf16[1024,1024]{1,0:T(8,128)(2,1)}, u32[]{:S(2)}) copy-start(bf16[1024,1024]{1,0:T(8,128)(2,1)} %copy-done.10) | copy-start | bytes 6291460
  (19 other events, 26.0 us)

commit v5 on v4

--- a/solution.py
+++ b/solution.py
@@ -1,5 +1,4 @@
 import functools
-import math
 
 import jax
 import jax.numpy as jnp
@@ -84,18 +83,29 @@
 SMEM = pl.BlockSpec(memory_space=pltpu.SMEM)
 
 
-def call(kernel, ids, operands, outs, mib, flops=0, scratch=(), aliases={}, far_in=(), far_out=()):
-    moved = sum(math.prod(a.shape) * jnp.dtype(a.dtype).itemsize for a in list(operands) + list(outs))
-    return pl.pallas_call(
-        kernel,
-        in_specs=[SMEM] + [ANY if i in far_in else VMEM for i in range(len(operands))],
-        out_specs=[ANY if i in far_out else VMEM for i in range(len(outs))],
-        out_shape=list(outs),
-        scratch_shapes=list(scratch),
-        input_output_aliases=aliases,
-        cost_estimate=pl.CostEstimate(flops=flops, bytes_accessed=moved, transcendentals=0),
-        compiler_params=pltpu.CompilerParams(vmem_limit_bytes=mib * MIB),
-    )(ids, *operands)
+class Order:
+    def __init__(self, ids):
+        self.ids = ids
+        self.token = jnp.zeros((8, 128), jnp.int32)
+
+    def call(self, kernel, operands, outs, mib, scratch=(), aliases={}, far_in=(), far_out=()):
+        n, m = len(operands), len(outs)
+
+        def body(ids, token, *refs):
+            kernel(ids, *refs[: n + m], *refs[n + m + 1 :])
+
+        results = pl.pallas_call(
+            body,
+            in_specs=[SMEM, ANY] + [ANY if i in far_in else VMEM for i in range(n)],
+            out_specs=[ANY if i in far_out else VMEM for i in range(m)] + [ANY],
+            out_shape=list(outs) + [jax.ShapeDtypeStruct(self.token.shape, jnp.int32)],
+            scratch_shapes=list(scratch),
+            input_output_aliases={1: m} | {2 + i: o for i, o in aliases.items()},
+            cost_estimate=pl.CostEstimate(flops=1, bytes_accessed=1, transcendentals=0),
+            compiler_params=pltpu.CompilerParams(vmem_limit_bytes=mib * MIB),
+        )(self.ids, self.token, *operands)
+        self.token = results[-1]
+        return results[:-1]
 
 
 def gather_lanes(blocks, into, start, width):
@@ -104,13 +114,18 @@
 
 
 def pair_kernel(ids, *refs):
-    pieces, (both, pair, quarter) = refs[:8], refs[8:]
+    pieces, (both, pair, quarter, sems) = refs[:8], refs[8:]
     group = 2 * ids[1] + ids[2]
     me = 4 * ids[0] + group
     rows = pieces[0].shape[0]
+    copies = []
     for i in range(8):
         place = me ^ i
-        both[place >> 2, pl.ds(pl.multiple_of((place & 3) * rows, rows), rows), :] = pieces[i][...]
+        into = both.at[place >> 2, pl.ds(pl.multiple_of((place & 3) * rows, rows), rows), :]
+        copies.append(pltpu.make_async_copy(pieces[i], into, sems.at[i]))
+        copies[-1].start()
+    for copy in copies:
+        copy.wait()
     for r in range(4):
         cut = slice(r * rows, (r + 1) * rows)
         pair[cut, :] = mm(both[0, cut, :], both[1]).astype(LOW)
@@ -310,103 +325,123 @@
 
 def suffix(gains, spreads, offsets):
     x, y, c, z = (lax.axis_index(name) for name in ("x", "y", "c", "z"))
-    even = x == 0
-    gain, offset = gains[0], offsets[0]
+    gain = gains[0]
     rows, size_d = gain.shape
     part = rows // 2
-    half = offset.shape[1] // 2
     chunks = 2
+    half = offsets.shape[2] // 2
     width = half // chunks
     ids = jnp.stack([x, y, c, z]).astype(jnp.int32)
     level = [(3, 2), (1, 0)]
+    order = Order(ids)
+    in_hbm = lambda a: pltpu.with_memory_space_constraint(a, pltpu.HBM)
 
     e_low = gain.astype(LOW)
     e_x, e_y = swap(e_low, "x"), swap(e_low, "y")
+
+    l_low = spreads[0].astype(LOW)
+    l_send = lax.dynamic_slice_in_dim(l_low, (1 - x) * part, part, 0)
+    g_send = [
+        lax.dynamic_slice_in_dim(offsets[0], (1 - x) * half + i * width, width, 1).astype(LOW) for i in range(chunks)
+    ]
+    l_send, g_send[0], e_x = lax.optimization_barrier((l_send, g_send[0], e_x))
     e_xy = swap(e_x, "y")
+    l_got = swap(l_send, "x")
+    g_got = [swap(g_send[0], "x")]
+    for i in range(1, chunks):
+        g_send[i], g_got[-1] = lax.optimization_barrier((g_send[i], g_got[-1]))
+        g_got.append(swap(g_send[i], "x"))
     pieces = [e_low, None, e_y, None, e_x, None, e_xy, None]
     for i in range(0, 8, 2):
         pieces[i + 1] = swap(pieces[i], "c")
-
-    l_low = spreads[0].astype(LOW)
-    l_send = jnp.where(even, l_low[part:], l_low[:part])
-    g_send = jnp.where(even, offset[:, half:], offset[:, :half]).astype(LOW)
-    l_send, g_send, e_x = lax.optimization_barrier((l_send, g_send, e_x))
-    l_got = swap(l_send, "x")
-    g_got = [swap(g_send[:, i * width : (i + 1) * width], "x") for i in range(chunks)]
-
-    both, a_e, quarter = call(
-        pair_kernel, ids, pieces, [held(2, size_d, size_d), held(size_d, size_d), low(rows, size_d)], 16,
-        flops=2 * size_d**3,
-    )
-    (m,) = call(spread_kernel, ids, [both, l_low, l_got], [low(8, rows, part)], 12, flops=2 * part * size_d**2)
-    prod, a_l, a_low = call(
-        spread_start_kernel, ids, [exchange(m), both, spreads, l_got],
-        [held(rows, size_d, dtype=WIDE), held(size_d, part, dtype=WIDE), low(size_d, part)],
-        14, flops=2 * rows * size_d**2, scratch=[pltpu.VMEM((rows, size_d), LOW)],
-    )
-
-    l_next = lax.ppermute(a_low, "z", level)
+    offset = in_hbm(offsets[0])
+
+    keep = pltpu.VMEM((size_d, width), WIDE)
+    column = pltpu.VMEM((size_d, width), LOW)
+    slab_rows = pltpu.VMEM((rows, size_d), LOW)
+
+    def start(i):
+        return order.call(
+            functools.partial(start_kernel, i), [both, g_got[i], offset],
+            [held(size_d, width, dtype=WIDE), low(size_d, width)], 8,
+            far_in=(2,), scratch=[keep, pltpu.SemaphoreType.DMA(())],
+        )
+
+    def down(value, source):
+        return lax.ppermute(value, "z", [(source, source - 1)])
+
+    def hop(i, got):
+        return order.call(hop_kernel, [a_e, got, own[i]], [low(size_d, width)], 8)[0]
+
+    def last(i, into):
+        extra = [] if into is None else [into]
+        return order.call(
+            functools.partial(last_kernel, i), [a_e, both] + gots[i] + [p[i], offset] + extra,
+            [wide(*offset.shape), low(size_d, width)], 12,
+            far_in=(6, 7), far_out=(0,), aliases={7: 0} if extra else {},
+            scratch=[keep, column, pltpu.SemaphoreType.DMA((2,))],
+        )
+
+    def add(i, got, into):
+        return order.call(
+            functools.partial(add_kernel, i), [got, offset, into], [wide(*offset.shape)], 8,
+            far_in=(1, 2), far_out=(0,), aliases={2: 0}, scratch=[keep, pltpu.SemaphoreType.DMA((2,))],
+        )[0]
+
+    both, a_e, quarter = order.call(
+        pair_kernel, [in_hbm(piece) for piece in pieces],
+        [held(2, size_d, size_d), held(size_d, size_d), low(rows, size_d)], 16,
+        far_in=range(8), scratch=[pltpu.SemaphoreType.DMA((8,))],
+    )
     quarter = lax.ppermute(quarter, "z", level)
     quarter_y = swap(quarter, "y")
     quarters = [quarter, swap(quarter, "c"), quarter_y, swap(quarter_y, "c")]
-    m, near = call(
-        spread_hop_kernel, ids, [a_e, both, l_next], [low(size_d, part), low(8, rows, part)], 12,
-        flops=4 * part * size_d**2,
-    )
-    (b_l,) = call(
-        spread_next_kernel, ids, [exchange(m.reshape(8, part, part)), a_e, a_l], [low(size_d, part)], 8,
-        flops=2 * part * size_d**2, scratch=[pltpu.VMEM((part, size_d), LOW)],
+    (m,) = order.call(spread_kernel, [both, l_low, l_got], [low(8, rows, part)], 12)
+    m = exchange(m)
+    p, own, gots = [None] * chunks, [None] * chunks, [[] for _ in range(chunks)]
+    p[0], own[0] = start(0)
+    gots[0].append(down(own[0], 3))
+    prod, a_l, a_low = order.call(
+        spread_start_kernel, [m, both, spreads, l_got],
+        [held(rows, size_d, dtype=WIDE), held(size_d, part, dtype=WIDE), low(size_d, part)], 14, scratch=[slab_rows],
+    )
+    l_next = lax.ppermute(a_low, "z", level)
+    p[1], own[1] = start(1)
+    gots[1].append(down(own[1], 3))
+    gots[0].append(down(hop(0, gots[0][0]), 2))
+
+    m, near = order.call(spread_hop_kernel, [a_e, both, l_next], [low(size_d, part), low(8, rows, part)], 12)
+    m = exchange(m.reshape(8, part, part))
+    near = exchange(near)
+    gots[1].append(down(hop(1, gots[1][0]), 2))
+    (b_l,) = order.call(
+        spread_next_kernel, [m, a_e, a_l], [low(size_d, part)], 8, scratch=[pltpu.VMEM((part, size_d), LOW)]
     )
     l_far = lax.ppermute(b_l, "z", [(2, 1)]), lax.ppermute(b_l, "z", [(2, 0)])
-    c0_e, c1_e, e_slab = call(
-        compose_kernel, ids, [a_e, both, *quarters],
-        [held(size_d, size_d), held(size_d, size_d), low(size_d, part)], 14,
-        flops=4 * size_d**3, scratch=[pltpu.VMEM((size_d, size_d), LOW)],
+    gots[0].append(down(hop(0, gots[0][1]), 1))
+    c0_e, c1_e, e_slab = order.call(
+        compose_kernel, [a_e, both, *quarters], [held(size_d, size_d), held(size_d, size_d), low(size_d, part)], 14,
+        scratch=[pltpu.VMEM((size_d, size_d), LOW)],
     )
     e_far = lax.ppermute(e_slab, "z", [(2, 1)]), lax.ppermute(e_slab, "z", [(2, 0)])
-    (near,) = call(
-        near_kernel, ids, [exchange(near), a_e, both, prod, spreads], [held(rows, size_d, dtype=WIDE)], 12,
-        flops=2 * rows * size_d**2, scratch=[pltpu.VMEM((rows, size_d), LOW)],
-    )
-
-    (m,) = call(
-        far_kernel, ids, [c0_e, c1_e, *e_far, *l_far], [low(8, rows, rows)], 12,
-        flops=4 * rows * size_d**2, scratch=[pltpu.VMEM((size_d, rows), LOW)],
-    )
-    out_gain, out_spread = call(
-        end_kernel, ids, [exchange(m), c0_e, c1_e, near], [wide(rows, size_d), wide(rows, size_d)], 14,
-        flops=2 * rows * size_d**2, scratch=[pltpu.VMEM((rows, size_d), LOW)],
-    )
-
-    out_offset, others = None, []
-    keep = pltpu.VMEM((size_d, width), WIDE)
-    column = pltpu.VMEM((size_d, width), LOW)
-    for i in range(chunks):
-        p, own = call(
-            functools.partial(start_kernel, i), ids, [both, g_got[i], offset],
-            [held(size_d, width, dtype=WIDE), low(size_d, width)], 8, flops=2 * size_d**2 * width,
-            far_in=(2,), scratch=[keep, pltpu.SemaphoreType.DMA(())],
-        )
-        now, gots = own, []
-        for source in (3, 2, 1):
-            gots.append(lax.ppermute(now, "z", [(source, source - 1)]))
-            if source > 1:
-                (now,) = call(
-                    hop_kernel, ids, [a_e, gots[-1], own], [low(size_d, width)], 8, flops=2 * size_d**2 * width
-                )
-        extra = [] if out_offset is None else [out_offset]
-        out_offset, other = call(
-            functools.partial(last_kernel, i), ids, [a_e, both] + gots + [p, offset] + extra,
-            [wide(*offset.shape), low(size_d, width)], 12, flops=4 * size_d**2 * width,
-            far_in=(6, 7), far_out=(0,), aliases={8: 0} if extra else {},
-            scratch=[keep, column, pltpu.SemaphoreType.DMA((2,))],
-        )
-        others.append(swap(other, "x"))
-    for i in range(chunks):
-        (out_offset,) = call(
-            functools.partial(add_kernel, i), ids, [others[i], offset, out_offset], [wide(*offset.shape)], 8,
-            far_in=(1, 2), far_out=(0,), aliases={3: 0}, scratch=[keep, pltpu.SemaphoreType.DMA((2,))],
-        )
+    gots[1].append(down(hop(1, gots[1][1]), 1))
+    (near,) = order.call(
+        near_kernel, [near, a_e, both, prod, spreads], [held(rows, size_d, dtype=WIDE)], 12, scratch=[slab_rows]
+    )
+
+    out_offset, other0 = last(0, None)
+    other0 = swap(other0, "x")
+    (m,) = order.call(
+        far_kernel, [c0_e, c1_e, *e_far, *l_far], [low(8, rows, rows)], 12, scratch=[pltpu.VMEM((size_d, rows), LOW)]
+    )
+    m = exchange(m)
+    out_offset, other1 = last(1, out_offset)
+    other1 = swap(other1, "x")
+    out_offset = add(0, other0, out_offset)
+    out_gain, out_spread = order.call(
+        end_kernel, [m, c0_e, c1_e, near], [wide(rows, size_d), wide(rows, size_d)], 14, scratch=[slab_rows]
+    )
+    out_offset = add(1, other1, out_offset)
     return (out_gain[None], out_spread[None], out_offset[None])
 
 

time: 239 us -> 201 us (0.84)
  the two profiles are of different devices: /device:TPU:0 before, /device:TPU:16 now
where the time goes in v5:
time: 201 us; the launch traced here: 200 us
  Pallas kernels  60.2 us (30%)
  waiting for transfers between devices  52.3 us (26%)
  starting transfers between devices  48.1 us (24%)
  local copies, waits for them, and re-layouts  35 us (17%)
  other arithmetic  2.82 us (1%)
    pallas_call x19, Pallas kernels, call(): pl.pallas_call(body, in_specs=[SMEM, ANY] + [ANY if i in far_in else VMEM...  60.2 us
    ppermute x15, waiting for transfers between devices, swap(): return lax.ppermute(value, axis, [(0, 1), (1, 0)])  34.2 us
    unnamed x70, local copies, waits for them, and re-layouts  31.6 us
    all_to_all x4, starting transfers between devices, exchange(): return lax.all_to_all(blocks, GROUP, 0, 0)  16.3 us
    ppermute x1, waiting for transfers between devices, suffix(): l_next = lax.ppermute(a_low, 'z', level)  12.5 us
    ppermute x15, starting transfers between devices, swap(): return lax.ppermute(value, axis, [(0, 1), (1, 0)])  12.3 us
    ppermute x6, starting transfers between devices, down(): return lax.ppermute(value, 'z', [(source, source - 1)])  9.76 us
  transfers between devices with their start and end apart: 31, of which 9 were waited for; matrix products, arithmetic and copies ran while one was open for 2% of the time, Pallas kernels for 28%

profile of v5, /device:TPU:16, one launch (start us, length us, event | category | flops | bytes accessed | tf_op | source)
XLA Modules:
  0.0 199.6 jit_solution(7136341906991478401)
XLA Ops:
  1.9 1.6 collective-permute-start.3
  3.5 1.5 collective-permute-start.1
  7.1 2.6 %fusion.1 = (bf16[1024,256]{1,0:T(8,128)(2,1)}, bf16[1024,256]{1,0:T(8,128)(2,1)}) fusion(f32[1,1024,1024]{2,1,0:T(8,128)} %param.5, s32[]{:T(128)S(6)} %select_n.11, s32[]{:T(128)S(6)} %select_n.10), kind=kLoop, calls=%fused_computation.3 | loop fusion | bytes 2097160 | tf_op jit(solution)/shard_map/convert_element_type | solution.py:345
  9.8 5.9 %collective-permute-done.3.refs_4_ = bf16[256,1024]{1,0:T(8,128)(2,1)S(1)} collective-permute-done((bf16[256,1024]{1,0:T(8,128)(2,1)S(1)}, bf16[256,1024]{1,0:T(8,128)(2,1)S(1)}, u32[]{:S(2)}, u32[]{:S(2)}) %collective-permute-start.3) | collective-permute-done | bytes 524320 | tf_op jit(solution)/shard_map/ppermute | solution.py:51
  15.7 1.5 collective-permute-start.5
  17.2 1.5 collective-permute-start.8
  19.3 9.3 %collective-permute-done.5.refs_6_ = bf16[256,1024]{1,0:T(8,128)(2,1)} collective-permute-done((bf16[256,1024]{1,0:T(8,128)(2,1)S(1)}, bf16[256,1024]{1,0:T(8,128)(2,1)}, u32[]{:S(2)}, u32[]{:S(2)}) %collective-permute-start.5) | collective-permute-done | bytes 524320 | tf_op jit(solution)/shard_map/ppermute | solution.py:51
  30.8 1.5 collective-permute-start.7
  32.9 5.9 %shard_map.58 = (bf16[2,1024,1024]{2,1,0:T(8,128)(2,1)S(1)}, bf16[1024,1024]{1,0:T(8,128)(2,1)S(1)}, bf16[256,1024]{1,0:T(8,128)(2,1)}, s32[8,128]{1,0:T(8,128)S(1)}) custom-call(s32[4]{0:T(128)S(1)} %pad_add_fusion.ids, s32[8,128]{1,0:T(8,128)S(1)} %broadcast_in_dim.12.token, bf16[256,1024]{1,0:T(8,128)(2,1)} %copy-done.32, ...), custom_call_target="tpu_custom_call", output_to_operand_aliasing={{3}: (1, {})} | custom-call | flops 1 | bytes 1 | tf_op jit(solution)/shard_map/pallas_call | solution.py:97
  41.5 2.0 %copy-done = bf16[2,1024,1024]{2,1,0:T(8,128)(2,1)} copy-done((bf16[2,1024,1024]{2,1,0:T(8,128)(2,1)}, bf16[2,1024,1024]{2,1,0:T(8,128)(2,1)S(1)}, u32[]{:S(2)}) %copy-start) | copy-done | bytes 4194328
  44.3 4.1 %all-to-all-start = ((bf16[8,256,128]{2,1,0:T(8,128)(2,1)}), bf16[8,256,128]{2,1,0:T(8,128)(2,1)}, u32[]{:S(2)}, u32[]{:S(2)}) async-start(bf16[8,256,128]{2,1,0:T(8,128)(2,1)} %copy-done.28), calls=%async_computation | async-start | bytes 1048576 | tf_op jit(solution)/shard_map/all_to_all | solution.py:66
  48.5 2.2 %copy-done.1 = bf16[2,1024,1024]{2,1,0:T(8,128)(2,1)S(1)} copy-done((bf16[2,1024,1024]{2,1,0:T(8,128)(2,1)S(1)}, bf16[2,1024,1024]{2,1,0:T(8,128)(2,1)}, u32[]{:S(2)}) %copy-start.1) | copy-done | bytes 4194328
  51.7 2.7 %shard_map.60 = (f32[1024,256]{1,0:T(8,128)S(1)}, bf16[1024,256]{1,0:T(8,128)(2,1)}, s32[8,128]{1,0:T(8,128)S(1)}) custom-call(s32[4]{0:T(128)S(1)} %pad_add_fusion.ids, s32[8,128]{1,0:T(8,128)S(1)} %get-tuple-element.61.token, bf16[2,1024,1024]{2,1,0:T(8,128)(2,1)S(1)} %copy-done.1, ...), custom_call_target="tpu_custom_call", output_to_operand_aliasing={{2}: (1, {})} | custom-call | flops 1 | bytes 1 | tf_op jit(solution)/shard_map/pallas_call | solution.py:97
  57.7 2.2 %copy-done.2 = bf16[2,1024,1024]{2,1,0:T(8,128)(2,1)S(1)} copy-done((bf16[2,1024,1024]{2,1,0:T(8,128)(2,1)S(1)}, bf16[2,1024,1024]{2,1,0:T(8,128)(2,1)}, u32[]{:S(2)}) %copy-start.2) | copy-done | bytes 4194328
  59.9 2.0 %shard_map.61 = (f32[256,1024]{1,0:T(8,128)S(1)}, f32[1024,128]{1,0:T(8,128)S(1)}, bf16[1024,128]{1,0:T(8,128)(2,1)S(1)}, s32[8,128]{1,0:T(8,128)S(1)}) custom-call(s32[4]{0:T(128)S(1)} %pad_add_fusion.ids, s32[8,128]{1,0:T(8,128)S(1)} %get-tuple-element.64.token, bf16[8,256,128]{2,1,0:T(8,128)(2,1)} %all-to-all-done.refs_0_, ...), custom_call_target="tpu_custom_call", output_to_operand_aliasing={{3}: (1, {})} | custom-call | flops 1 | bytes 1 | tf_op jit(solution)/shard_map/pallas_call | solution.py:97
  63.7 3.6 %shard_map.62 = (f32[1024,256]{1,0:T(8,128)S(1)}, bf16[1024,256]{1,0:T(8,128)(2,1)}, s32[8,128]{1,0:T(8,128)S(1)}) custom-call(s32[4]{0:T(128)S(1)} %pad_add_fusion.ids, s32[8,128]{1,0:T(8,128)S(1)} %get-tuple-element.66.token, bf16[2,1024,1024]{2,1,0:T(8,128)(2,1)S(1)} %copy-done.2, ...), custom_call_target="tpu_custom_call", output_to_operand_aliasing={{2}: (1, {})} | custom-call | flops 1 | bytes 1 | tf_op jit(solution)/shard_map/pallas_call | solution.py:97
  69.5 3.3 %collective-permute-done.10.refs_1_.refs_2_ = bf16[1024,256]{1,0:T(8,128)(2,1)} collective-permute-done((bf16[1024,256]{1,0:T(8,128)(2,1)}, bf16[1024,256]{1,0:T(8,128)(2,1)}, u32[]{:S(2)}, u32[]{:S(2)}) %collective-permute-start.10) | collective-permute-done | bytes 524320 | tf_op jit(solution)/shard_map/ppermute | solution.py:371
  72.8 2.7 %shard_map.63 = (bf16[1024,256]{1,0:T(8,128)(2,1)}, s32[8,128]{1,0:T(8,128)S(1)}) custom-call(s32[4]{0:T(128)S(1)} %pad_add_fusion.ids, s32[8,128]{1,0:T(8,128)S(1)} %get-tuple-element.68.token, bf16[1024,1024]{1,0:T(8,128)(2,1)S(1)} %get-tuple-element.69.refs_0_.refs_1_, ...), custom_call_target="tpu_custom_call", output_to_operand_aliasing={{1}: (1, {})} | custom-call | flops 1 | bytes 1 | tf_op jit(solution)/shard_map/pallas_call | solution.py:97
  75.5 2.1 %collective-permute-start.13 = (bf16[1024,256]{1,0:T(8,128)(2,1)}, bf16[1024,256]{1,0:T(8,128)(2,1)}, u32[]{:S(2)}, u32[]{:S(2)}) collective-permute-start(bf16[1024,256]{1,0:T(8,128)(2,1)} %get-tuple-element.79), channel_id=1, source_target_pairs={{16,8},{17,9},{18,10},{19,11},{20,12},{21,13},{22,14},{23,15}} | collective-permute-start | bytes 1572872 | tf_op jit(solution)/shard_map/ppermute | solution.py:371
  79.0 12.5 %collective-permute-done.11.refs_2_ = bf16[1024,128]{1,0:T(8,128)(2,1)S(1)} collective-permute-done((bf16[1024,128]{1,0:T(8,128)(2,1)S(1)}, bf16[1024,128]{1,0:T(8,128)(2,1)S(1)}, u32[]{:S(2)}, u32[]{:S(2)}) %collective-permute-start.11) | collective-permute-done | bytes 262176 | tf_op jit(solution)/shard_map/ppermute | solution.py:408
  91.5 1.8 shard_map.64
  94.8 4.0 %all-to-all-start.1 = ((bf16[8,128,128]{2,1,0:T(8,128)(2,1)}), bf16[8,128,128]{2,1,0:T(8,128)(2,1)S(1)}, u32[]{:S(2)}, u32[]{:S(2)}) async-start(bf16[8,128,128]{2,1,0:T(8,128)(2,1)} %bitcast.19), calls=%async_computation.1 | async-start | bytes 524288 | tf_op jit(solution)/shard_map/all_to_all | solution.py:66
  99.4 2.7 %shard_map.65 = (bf16[1024,256]{1,0:T(8,128)(2,1)}, s32[8,128]{1,0:T(8,128)S(1)}) custom-call(s32[4]{0:T(128)S(1)} %pad_add_fusion.ids, s32[8,128]{1,0:T(8,128)S(1)} %get-tuple-element.73.token, bf16[1024,1024]{1,0:T(8,128)(2,1)S(1)} %get-tuple-element.69.refs_0_.refs_1_, ...), custom_call_target="tpu_custom_call", output_to_operand_aliasing={{1}: (1, {})} | custom-call | flops 1 | bytes 1 | tf_op jit(solution)/shard_map/pallas_call | solution.py:97
  102.1 2.1 %collective-permute-start.18 = (bf16[1024,256]{1,0:T(8,128)(2,1)}, bf16[1024,256]{1,0:T(8,128)(2,1)}, u32[]{:S(2)}, u32[]{:S(2)}) collective-permute-start(bf16[1024,256]{1,0:T(8,128)(2,1)} %get-tuple-element.83), channel_id=1, source_target_pairs={{16,8},{17,9},{18,10},{19,11},{20,12},{21,13},{22,14},{23,15}} | collective-permute-start | bytes 1572872 | tf_op jit(solution)/shard_map/ppermute | solution.py:371
  108.3 2.7 %shard_map.67 = (bf16[1024,256]{1,0:T(8,128)(2,1)}, s32[8,128]{1,0:T(8,128)S(1)}) custom-call(s32[4]{0:T(128)S(1)} %pad_add_fusion.ids, s32[8,128]{1,0:T(8,128)S(1)} %get-tuple-element.78.token, bf16[1024,1024]{1,0:T(8,128)(2,1)S(1)} %get-tuple-element.69.refs_0_.refs_1_, ...), custom_call_target="tpu_custom_call", output_to_operand_aliasing={{1}: (1, {})} | custom-call | flops 1 | bytes 1 | tf_op jit(solution)/shard_map/pallas_call | solution.py:97
  111.0 1.5 collective-permute-start.19
  112.5 4.1 %all-to-all-start.2 = ((bf16[8,256,128]{2,1,0:T(8,128)(2,1)}), bf16[8,256,128]{2,1,0:T(8,128)(2,1)}, u32[]{:S(2)}, u32[]{:S(2)}) async-start(bf16[8,256,128]{2,1,0:T(8,128)(2,1)} %copy-done.27), calls=%async_computation.2 | async-start | bytes 1048576 | tf_op jit(solution)/shard_map/all_to_all | solution.py:66
  117.9 2.0 collective-permute-start.22
  119.9 2.2 %copy-done.4 = bf16[2,1024,1024]{2,1,0:T(8,128)(2,1)S(1)} copy-done((bf16[2,1024,1024]{2,1,0:T(8,128)(2,1)S(1)}, bf16[2,1024,1024]{2,1,0:T(8,128)(2,1)}, u32[]{:S(2)}) %copy-start.4) | copy-done | bytes 4194328
  122.1 7.1 %shard_map.68 = (bf16[1024,1024]{1,0:T(8,128)(2,1)S(1)}, bf16[1024,1024]{1,0:T(8,128)(2,1)S(1)}, bf16[1024,128]{1,0:T(8,128)(2,1)}, s32[8,128]{1,0:T(8,128)S(1)}) custom-call(s32[4]{0:T(128)S(1)} %pad_add_fusion.ids, s32[8,128]{1,0:T(8,128)S(1)} %get-tuple-element.80.token, ...), custom_call_target="tpu_custom_call", output_to_operand_aliasing={{3}: (1, {})} | custom-call | flops 1 | bytes 1 | tf_op jit(solution)/shard_map/pallas_call | solution.py:97
  132.0 2.0 collective-permute-start.21
  134.0 2.0 collective-permute-start.20
  135.9 2.7 %shard_map.69 = (bf16[1024,256]{1,0:T(8,128)(2,1)}, s32[8,128]{1,0:T(8,128)S(1)}) custom-call(s32[4]{0:T(128)S(1)} %pad_add_fusion.ids, s32[8,128]{1,0:T(8,128)S(1)} %get-tuple-element.82.token, bf16[1024,1024]{1,0:T(8,128)(2,1)S(1)} %get-tuple-element.69.refs_0_.refs_1_, ...), custom_call_target="tpu_custom_call", output_to_operand_aliasing={{1}: (1, {})} | custom-call | flops 1 | bytes 1 | tf_op jit(solution)/shard_map/pallas_call | solution.py:97
  138.7 1.5 collective-permute-start.24
  140.2 2.2 %copy-done.5 = bf16[2,1024,1024]{2,1,0:T(8,128)(2,1)S(1)} copy-done((bf16[2,1024,1024]{2,1,0:T(8,128)(2,1)S(1)}, bf16[2,1024,1024]{2,1,0:T(8,128)(2,1)}, u32[]{:S(2)}) %copy-start.5) | copy-done | bytes 4194328
  143.6 2.1 %shard_map.70 = (f32[256,1024]{1,0:T(8,128)S(1)}, s32[8,128]{1,0:T(8,128)S(1)}) custom-call(s32[4]{0:T(128)S(1)} %pad_add_fusion.ids, s32[8,128]{1,0:T(8,128)S(1)} %get-tuple-element.84.token, bf16[8,256,128]{2,1,0:T(8,128)(2,1)} %all-to-all-done.2.refs_0_, ...), custom_call_target="tpu_custom_call", output_to_operand_aliasing={{1}: (1, {})} | custom-call | flops 1 | bytes 1 | tf_op jit(solution)/shard_map/pallas_call | solution.py:97
  146.6 4.7 %shard_map.71 = (f32[1024,1024]{1,0:T(8,128)}, bf16[1024,256]{1,0:T(8,128)(2,1)S(1)}, s32[8,128]{1,0:T(8,128)S(1)}) custom-call(s32[4]{0:T(128)S(1)} %pad_add_fusion.ids, s32[8,128]{1,0:T(8,128)S(1)} %get-tuple-element.87.token, bf16[1024,1024]{1,0:T(8,128)(2,1)S(1)} %get-tuple-element.69.refs_0_.refs_1_, ...), custom_call_target="tpu_custom_call", output_to_operand_aliasing={{2}: (1, {})} | custom-call | flops 1 | bytes 1 | tf_op jit(solution)/shard_map/pallas_call | solution.py:97
  151.4 2.6 %shard_map.72 = (bf16[8,256,256]{2,1,0:T(8,128)(2,1)S(1)}, s32[8,128]{1,0:T(8,128)S(1)}) custom-call(s32[4]{0:T(128)S(1)} %pad_add_fusion.ids, s32[8,128]{1,0:T(8,128)S(1)} %get-tuple-element.90.token, bf16[1024,1024]{1,0:T(8,128)(2,1)S(1)} %copy-done.9, bf16[1024,1024]{1,0:T(8,128)(2,1)S(1)} %copy-done.12, ...), custom_call_target="tpu_custom_call", output_to_operand_aliasing={{1}: (1, {})} | custom-call | flops 1 | bytes 1 | tf_op jit(solution)/shard_map/pallas_call | solution.py:97
  155.0 4.0 %all-to-all-start.3 = ((bf16[8,256,256]{2,1,0:T(8,128)(2,1)}), bf16[8,256,256]{2,1,0:T(8,128)(2,1)S(1)}, u32[]{:S(2)}, u32[]{:S(2)}) async-start(bf16[8,256,256]{2,1,0:T(8,128)(2,1)} %copy-done.18), calls=%async_computation.3 | async-start | bytes 2097152 | tf_op jit(solution)/shard_map/all_to_all | solution.py:66
  159.1 2.0 %collective-permute-start.25 = (bf16[1024,256]{1,0:T(8,128)(2,1)}, bf16[1024,256]{1,0:T(8,128)(2,1)S(1)}, u32[]{:S(2)}, u32[]{:S(2)}) collective-permute-start(bf16[1024,256]{1,0:T(8,128)(2,1)} %copy-done.30), channel_id=1, source_target_pairs={{0,4},{4,0},{1,5},{5,1},{2,6},{6,2},{3,7},{7,3},{8,12},{12,8},{9,1... | collective-permute-start | bytes 1572872 | tf_op jit(solution)/shard_map/ppermute | solution.py:51
  161.1 2.2 %copy-done.6 = bf16[2,1024,1024]{2,1,0:T(8,128)(2,1)S(1)} copy-done((bf16[2,1024,1024]{2,1,0:T(8,128)(2,1)S(1)}, bf16[2,1024,1024]{2,1,0:T(8,128)(2,1)}, u32[]{:S(2)}) %copy-start.6) | copy-done | bytes 4194328
  164.5 5.2 %shard_map.73 = (f32[1024,1024]{1,0:T(8,128)}, bf16[1024,256]{1,0:T(8,128)(2,1)}, s32[8,128]{1,0:T(8,128)S(1)}) custom-call(s32[4]{0:T(128)S(1)} %pad_add_fusion.ids, s32[8,128]{1,0:T(8,128)S(1)} %get-tuple-element.95.token, bf16[1024,1024]{1,0:T(8,128)(2,1)S(1)} %get-tuple-element.69.refs_0_.refs_1_, ...), custom_call_target="tpu_custom_call", output_to_operand_aliasing={{2}: (1, {}), {0}: (9, {})} | custom-call | flops 1 | bytes 1 | tf_op jit(solution)/shard_map/pallas_call | solution.py:97
  169.7 15.5 %collective-permute-done.25.refs_0_ = bf16[1024,256]{1,0:T(8,128)(2,1)S(1)} collective-permute-done((bf16[1024,256]{1,0:T(8,128)(2,1)}, bf16[1024,256]{1,0:T(8,128)(2,1)S(1)}, u32[]{:S(2)}, u32[]{:S(2)}) %collective-permute-start.25) | collective-permute-done | bytes 524320 | tf_op jit(solution)/shard_map/ppermute | solution.py:51
  185.3 2.9 %shard_map.74 = (f32[1024,1024]{1,0:T(8,128)}, s32[8,128]{1,0:T(8,128)S(1)}) custom-call(s32[4]{0:T(128)S(1)} %pad_add_fusion.ids, s32[8,128]{1,0:T(8,128)S(1)} %get-tuple-element.99.token, bf16[1024,256]{1,0:T(8,128)(2,1)S(1)} %collective-permute-done.25.refs_0_, f32[1024,1024]{1,0:T(8,128)} %bitcast.24, ...), custom_call_target="tpu_custom_call", output_to_operand_aliasing={{1}: (1, {}), {0}: (4, {})} | custom-call | flops 1 | bytes 1 | tf_op jit(solution)/shard_map/pallas_call | solution.py:97
  188.2 1.6 copy-done.13
  191.0 2.9 %shard_map.75 = (f32[256,1024]{1,0:T(8,128)}, f32[256,1024]{1,0:T(8,128)}, s32[8,128]{1,0:T(8,128)S(1)}) custom-call(s32[4]{0:T(128)S(1)} %pad_add_fusion.ids, s32[8,128]{1,0:T(8,128)S(1)} %get-tuple-element.102.token, bf16[8,256,256]{2,1,0:T(8,128)(2,1)S(1)} %all-to-all-done.3.refs_0_, ...), custom_call_target="tpu_custom_call", output_to_operand_aliasing={{2}: (1, {})} | custom-call | flops 1 | bytes 1 | tf_op jit(solution)/shard_map/pallas_call | solution.py:97
  193.9 2.2 %collective-permute-done.26.refs_0_ = bf16[1024,256]{1,0:T(8,128)(2,1)} collective-permute-done((bf16[1024,256]{1,0:T(8,128)(2,1)}, bf16[1024,256]{1,0:T(8,128)(2,1)}, u32[]{:S(2)}, u32[]{:S(2)}) %collective-permute-start.26) | collective-permute-done | bytes 524320 | tf_op jit(solution)/shard_map/ppermute | solution.py:51
  196.1 3.4 %shard_map.76 = (f32[1024,1024]{1,0:T(8,128)}, s32[8,128]{1,0:T(8,128)S(1)}) custom-call(s32[4]{0:T(128)S(1)} %pad_add_fusion.ids, s32[8,128]{1,0:T(8,128)S(1)} %get-tuple-element.107.token, bf16[1024,256]{1,0:T(8,128)(2,1)} %collective-permute-done.26.refs_0_, f32[1024,1024]{1,0:T(8,128)} %bitcast.25, ...), custom_call_target="tpu_custom_call", output_to_operand_aliasing={{1}: (1, {}), {0}: (4, {})} | custom-call | flops 1 | bytes 1 | tf_op jit(solution)/shard_map/pallas_call | solution.py:97
  (110 shorter events, 35.8 us)
Async XLA Ops:
  1.9 30.9 %copy-start.32 = (bf16[256,1024]{1,0:T(8,128)(2,1)}, bf16[256,1024]{1,0:T(8,128)(2,1)S(1)}, u32[]{:S(2)}) copy-start(bf16[256,1024]{1,0:T(8,128)(2,1)S(1)} %convert_bitcast_fusion.refs_0_) | copy-start | bytes 1572868
  1.9 13.7 %collective-permute-start.3 = (bf16[256,1024]{1,0:T(8,128)(2,1)S(1)}, bf16[256,1024]{1,0:T(8,128)(2,1)S(1)}, u32[]{:S(2)}, u32[]{:S(2)}) collective-permute-start(bf16[256,1024]{1,0:T(8,128)(2,1)S(1)} %convert_bitcast_fusion.refs_0_), channel_id=1, source_target_pairs={{0,4},{4,0},{1,5},{5,1},{2,6},{6,2},{3,7},{7,3},{8,12},{12,8},{9,1... | collective-permute-start | bytes 1572872 | tf_op jit(solution)/shard_map/ppermute | solution.py:51
  3.5 15.7 %collective-permute-start.1 = (bf16[256,1024]{1,0:T(8,128)(2,1)S(1)}, bf16[256,1024]{1,0:T(8,128)(2,1)S(1)}, u32[]{:S(2)}, u32[]{:S(2)}) collective-permute-start(bf16[256,1024]{1,0:T(8,128)(2,1)S(1)} %convert_bitcast_fusion.refs_0_), channel_id=1, source_target_pairs={{0,2},{2,0},{1,3},{3,1},{4,6},{6,4},{5,7},{7,5},{8,10},{10,8},{9,1... | collective-permute-start | bytes 1572872 | tf_op jit(solution)/shard_map/ppermute | solution.py:51
  5.0 35.1 %copy-start.7 = (f32[1,256,1024]{2,1,0:T(8,128)S(1)}, f32[1,256,1024]{2,1,0:T(8,128)}, u32[]{:S(2)}) copy-start(f32[1,256,1024]{2,1,0:T(8,128)} %refs_4_.1) | copy-start | bytes 3145732
  15.7 17.2 %copy-start.33 = (bf16[256,1024]{1,0:T(8,128)(2,1)}, bf16[256,1024]{1,0:T(8,128)(2,1)S(1)}, u32[]{:S(2)}) copy-start(bf16[256,1024]{1,0:T(8,128)(2,1)S(1)} %collective-permute-done.3.refs_4_) | copy-start | bytes 1572868
  15.7 12.9 %collective-permute-start.5 = (bf16[256,1024]{1,0:T(8,128)(2,1)S(1)}, bf16[256,1024]{1,0:T(8,128)(2,1)}, u32[]{:S(2)}, u32[]{:S(2)}) collective-permute-start(bf16[256,1024]{1,0:T(8,128)(2,1)S(1)} %collective-permute-done.3.refs_4_), channel_id=1, source_target_pairs={{0,2},{2,0},{1,3},{3,1},{4,6},{6,4},{5,7},{7,5},{8,10},{10,8},{9,1... | collective-permute-start | bytes 1572872 | tf_op jit(solution)/shard_map/ppermute | solution.py:51
  17.2 12.7 %collective-permute-start.8 = (bf16[1024,256]{1,0:T(8,128)(2,1)}, bf16[1024,256]{1,0:T(8,128)(2,1)S(1)}, u32[]{:S(2)}, u32[]{:S(2)}) collective-permute-start(bf16[1024,256]{1,0:T(8,128)(2,1)} %get-tuple-element.62), channel_id=1, source_target_pairs={{0,4},{4,0},{1,5},{5,1},{2,6},{6,2},{3,7},{7,3},{8,12},{12,8},{9,1... | collective-permute-start | bytes 1572872 | tf_op jit(solution)/shard_map/ppermute | solution.py:51
  18.7 13.6 %collective-permute-start = (bf16[256,1024]{1,0:T(8,128)(2,1)S(1)}, bf16[256,1024]{1,0:T(8,128)(2,1)}, u32[]{:S(2)}, u32[]{:S(2)}) collective-permute-start(bf16[256,1024]{1,0:T(8,128)(2,1)S(1)} %convert_bitcast_fusion.refs_0_), channel_id=1, source_target_pairs={{0,1},{1,0},{2,3},{3,2},{4,5},{5,4},{6,7},{7,6},{8,9},{9,8},{10,11... | collective-permute-start | bytes 1572872 | tf_op jit(solution)/shard_map/ppermute | solution.py:51
  18.7 14.1 %collective-permute-start.4 = (bf16[256,1024]{1,0:T(8,128)(2,1)S(1)}, bf16[256,1024]{1,0:T(8,128)(2,1)}, u32[]{:S(2)}, u32[]{:S(2)}) collective-permute-start(bf16[256,1024]{1,0:T(8,128)(2,1)S(1)} %collective-permute-done.3.refs_4_), channel_id=1, source_target_pairs={{0,1},{1,0},{2,3},{3,2},{4,5},{5,4},{6,7},{7,6},{8,9},{9,8},{10,11... | collective-permute-start | bytes 1572872 | tf_op jit(solution)/shard_map/ppermute | solution.py:51
  19.2 13.6 %copy-start.34 = (bf16[256,1024]{1,0:T(8,128)(2,1)}, bf16[256,1024]{1,0:T(8,128)(2,1)S(1)}, u32[]{:S(2)}) copy-start(bf16[256,1024]{1,0:T(8,128)(2,1)S(1)} %collective-permute-done.1.refs_2_) | copy-start | bytes 1572868
  19.2 13.6 %collective-permute-start.2 = (bf16[256,1024]{1,0:T(8,128)(2,1)S(1)}, bf16[256,1024]{1,0:T(8,128)(2,1)}, u32[]{:S(2)}, u32[]{:S(2)}) collective-permute-start(bf16[256,1024]{1,0:T(8,128)(2,1)S(1)} %collective-permute-done.1.refs_2_), channel_id=1, source_target_pairs={{0,1},{1,0},{2,3},{3,2},{4,5},{5,4},{6,7},{7,6},{8,9},{9,8},{10,11... | collective-permute-start | bytes 1572872 | tf_op jit(solution)/shard_map/ppermute | solution.py:51
  28.6 4.2 %collective-permute-start.6 = (bf16[256,1024]{1,0:T(8,128)(2,1)}, bf16[256,1024]{1,0:T(8,128)(2,1)}, u32[]{:S(2)}, u32[]{:S(2)}) collective-permute-start(bf16[256,1024]{1,0:T(8,128)(2,1)} %collective-permute-done.5.refs_6_), channel_id=1, source_target_pairs={{0,1},{1,0},{2,3},{3,2},{4,5},{5,4},{6,7},{7,6},{8,9},{9,8},{10,11... | collective-permute-start | bytes 1572872 | tf_op jit(solution)/shard_map/ppermute | solution.py:51
  30.8 9.5 %collective-permute-start.7 = (bf16[128,1024]{1,0:T(8,128)(2,1)}, bf16[128,1024]{1,0:T(8,128)(2,1)S(1)}, u32[]{:S(2)}, u32[]{:S(2)}) collective-permute-start(bf16[128,1024]{1,0:T(8,128)(2,1)} %dynamic-slice_bitcast_fusion), channel_id=1, source_target_pairs={{0,4},{4,0},{1,5},{5,1},{2,6},{6,2},{3,7},{7,3},{8,12},{12,8},{9,1... | collective-permute-start | bytes 786440 | tf_op jit(solution)/shard_map/ppermute | solution.py:51
  32.3 31.5 %collective-permute-start.9 = (bf16[1024,256]{1,0:T(8,128)(2,1)}, bf16[1024,256]{1,0:T(8,128)(2,1)}, u32[]{:S(2)}, u32[]{:S(2)}) collective-permute-start(bf16[1024,256]{1,0:T(8,128)(2,1)} %get-tuple-element.67), channel_id=1, source_target_pairs={{0,4},{4,0},{1,5},{5,1},{2,6},{6,2},{3,7},{7,3},{8,12},{12,8},{9,1... | collective-permute-start | bytes 1572872 | tf_op jit(solution)/shard_map/ppermute | solution.py:51
  38.8 28.5 %collective-permute-start.14 = (bf16[256,1024]{1,0:T(8,128)(2,1)}, bf16[256,1024]{1,0:T(8,128)(2,1)}, u32[]{:S(2)}, u32[]{:S(2)}) collective-permute-start(bf16[256,1024]{1,0:T(8,128)(2,1)} %get-tuple-element.81), channel_id=1, source_target_pairs={{24,16},{8,0},{25,17},{9,1},{26,18},{10,2},{27,19},{11,3},{28,20},... | collective-permute-start | bytes 1572872 | tf_op jit(solution)/shard_map/ppermute | solution.py:396
  41.5 2.0 %copy-start = (bf16[2,1024,1024]{2,1,0:T(8,128)(2,1)}, bf16[2,1024,1024]{2,1,0:T(8,128)(2,1)S(1)}, u32[]{:S(2)}) copy-start(bf16[2,1024,1024]{2,1,0:T(8,128)(2,1)S(1)} %get-tuple-element.59.refs_0_.refs_1_.refs_2_) | copy-start | bytes 12582916
  44.3 13.4 %all-to-all-start = ((bf16[8,256,128]{2,1,0:T(8,128)(2,1)}), bf16[8,256,128]{2,1,0:T(8,128)(2,1)}, u32[]{:S(2)}, u32[]{:S(2)}) async-start(bf16[8,256,128]{2,1,0:T(8,128)(2,1)} %copy-done.28), calls=%async_computation | async-start | bytes 1048576 | tf_op jit(solution)/shard_map/all_to_all | solution.py:66
  48.5 2.2 %copy-start.1 = (bf16[2,1024,1024]{2,1,0:T(8,128)(2,1)S(1)}, bf16[2,1024,1024]{2,1,0:T(8,128)(2,1)}, u32[]{:S(2)}) copy-start(bf16[2,1024,1024]{2,1,0:T(8,128)(2,1)} %copy-done) | copy-start | bytes 12582916
  55.3 17.5 %collective-permute-start.10 = (bf16[1024,256]{1,0:T(8,128)(2,1)}, bf16[1024,256]{1,0:T(8,128)(2,1)}, u32[]{:S(2)}, u32[]{:S(2)}) collective-permute-start(bf16[1024,256]{1,0:T(8,128)(2,1)} %get-tuple-element.70.refs_2_), channel_id=1, source_target_pairs={{24,16},{25,17},{26,18},{27,19},{28,20},{29,21},{30,22},{31,23}} | collective-permute-start | bytes 1572872 | tf_op jit(solution)/shard_map/ppermute | solution.py:371
  57.7 2.2 %copy-start.2 = (bf16[2,1024,1024]{2,1,0:T(8,128)(2,1)S(1)}, bf16[2,1024,1024]{2,1,0:T(8,128)(2,1)}, u32[]{:S(2)}) copy-start(bf16[2,1024,1024]{2,1,0:T(8,128)(2,1)} %copy-done) | copy-start | bytes 12582916
  63.7 27.8 %copy-start.3 = (bf16[2,1024,1024]{2,1,0:T(8,128)(2,1)S(1)}, bf16[2,1024,1024]{2,1,0:T(8,128)(2,1)}, u32[]{:S(2)}) copy-start(bf16[2,1024,1024]{2,1,0:T(8,128)(2,1)} %copy-done) | copy-start | bytes 12582916
  67.3 26.0 %copy-start.14 = (f32[1024,256]{1,0:T(8,128)}, f32[1024,256]{1,0:T(8,128)S(1)}, u32[]{:S(2)}) copy-start(f32[1024,256]{1,0:T(8,128)S(1)} %get-tuple-element.97.refs_5_) | copy-start | bytes 3145732
  67.3 31.9 %collective-permute-start.16 = (bf16[256,1024]{1,0:T(8,128)(2,1)}, bf16[256,1024]{1,0:T(8,128)(2,1)}, u32[]{:S(2)}, u32[]{:S(2)}) collective-permute-start(bf16[256,1024]{1,0:T(8,128)(2,1)} %collective-permute-done.14.refs_2_), channel_id=1, source_target_pairs={{0,2},{2,0},{1,3},{3,1},{4,6},{6,4},{5,7},{7,5},{8,10},{10,8},{9,1... | collective-permute-start | bytes 1572872 | tf_op jit(solution)/shard_map/ppermute | solution.py:51
  68.2 31.1 %collective-permute-start.12 = (bf16[1024,256]{1,0:T(8,128)(2,1)}, bf16[1024,256]{1,0:T(8,128)(2,1)}, u32[]{:S(2)}, u32[]{:S(2)}) collective-permute-start(bf16[1024,256]{1,0:T(8,128)(2,1)} %get-tuple-element.74.refs_2_), channel_id=1, source_target_pairs={{24,16},{25,17},{26,18},{27,19},{28,20},{29,21},{30,22},{31,23}} | collective-permute-start | bytes 1572872 | tf_op jit(solution)/shard_map/ppermute | solution.py:371
  75.5 32.7 %collective-permute-start.13 = (bf16[1024,256]{1,0:T(8,128)(2,1)}, bf16[1024,256]{1,0:T(8,128)(2,1)}, u32[]{:S(2)}, u32[]{:S(2)}) collective-permute-start(bf16[1024,256]{1,0:T(8,128)(2,1)} %get-tuple-element.79), channel_id=1, source_target_pairs={{16,8},{17,9},{18,10},{19,11},{20,12},{21,13},{22,14},{23,15}} | collective-permute-start | bytes 1572872 | tf_op jit(solution)/shard_map/ppermute | solution.py:371
  77.7 13.8 %collective-permute-start.11 = (bf16[1024,128]{1,0:T(8,128)(2,1)S(1)}, bf16[1024,128]{1,0:T(8,128)(2,1)S(1)}, u32[]{:S(2)}, u32[]{:S(2)}) collective-permute-start(bf16[1024,128]{1,0:T(8,128)(2,1)S(1)} %get-tuple-element.72), channel_id=1, source_target_pairs={{24,16},{8,0},{25,17},{9,1},{26,18},{10,2},{27,19},{11,3},{28,20},... | collective-permute-start | bytes 786440 | tf_op jit(solution)/shard_map/ppermute | solution.py:408
  94.8 10.4 %all-to-all-start.1 = ((bf16[8,128,128]{2,1,0:T(8,128)(2,1)}), bf16[8,128,128]{2,1,0:T(8,128)(2,1)S(1)}, u32[]{:S(2)}, u32[]{:S(2)}) async-start(bf16[8,128,128]{2,1,0:T(8,128)(2,1)} %bitcast.19), calls=%async_computation.1 | async-start | bytes 524288 | tf_op jit(solution)/shard_map/all_to_all | solution.py:66
  98.8 19.1 %collective-permute-start.15 = (bf16[256,1024]{1,0:T(8,128)(2,1)}, bf16[256,1024]{1,0:T(8,128)(2,1)}, u32[]{:S(2)}, u32[]{:S(2)}) collective-permute-start(bf16[256,1024]{1,0:T(8,128)(2,1)} %collective-permute-done.14.refs_2_), channel_id=1, source_target_pairs={{0,1},{1,0},{2,3},{3,2},{4,5},{5,4},{6,7},{7,6},{8,9},{9,8},{10,11... | collective-permute-start | bytes 1572872 | tf_op jit(solution)/shard_map/ppermute | solution.py:51
  99.3 20.6 %collective-permute-start.17 = (bf16[256,1024]{1,0:T(8,128)(2,1)}, bf16[256,1024]{1,0:T(8,128)(2,1)}, u32[]{:S(2)}, u32[]{:S(2)}) collective-permute-start(bf16[256,1024]{1,0:T(8,128)(2,1)} %collective-permute-done.16.refs_4_), channel_id=1, source_target_pairs={{0,1},{1,0},{2,3},{3,2},{4,5},{5,4},{6,7},{7,6},{8,9},{9,8},{10,11... | collective-permute-start | bytes 1572872 | tf_op jit(solution)/shard_map/ppermute | solution.py:51
  102.1 31.9 %collective-permute-start.18 = (bf16[1024,256]{1,0:T(8,128)(2,1)}, bf16[1024,256]{1,0:T(8,128)(2,1)}, u32[]{:S(2)}, u32[]{:S(2)}) collective-permute-start(bf16[1024,256]{1,0:T(8,128)(2,1)} %get-tuple-element.83), channel_id=1, source_target_pairs={{16,8},{17,9},{18,10},{19,11},{20,12},{21,13},{22,14},{23,15}} | collective-permute-start | bytes 1572872 | tf_op jit(solution)/shard_map/ppermute | solution.py:371
  111.0 27.7 %collective-permute-start.19 = (bf16[1024,256]{1,0:T(8,128)(2,1)}, bf16[1024,256]{1,0:T(8,128)(2,1)}, u32[]{:S(2)}, u32[]{:S(2)}) collective-permute-start(bf16[1024,256]{1,0:T(8,128)(2,1)} %get-tuple-element.88), channel_id=1, source_target_pairs={{8,0},{9,1},{10,2},{11,3},{12,4},{13,5},{14,6},{15,7}} | collective-permute-start | bytes 1572872 | tf_op jit(solution)/shard_map/ppermute | solution.py:371
  112.5 27.7 %all-to-all-start.2 = ((bf16[8,256,128]{2,1,0:T(8,128)(2,1)}), bf16[8,256,128]{2,1,0:T(8,128)(2,1)}, u32[]{:S(2)}, u32[]{:S(2)}) async-start(bf16[8,256,128]{2,1,0:T(8,128)(2,1)} %copy-done.27), calls=%async_computation.2 | async-start | bytes 1048576 | tf_op jit(solution)/shard_map/all_to_all | solution.py:66
  116.6 34.8 %collective-permute-start.23 = (bf16[1024,128]{1,0:T(8,128)(2,1)}, bf16[1024,128]{1,0:T(8,128)(2,1)S(1)}, u32[]{:S(2)}, u32[]{:S(2)}) collective-permute-start(bf16[1024,128]{1,0:T(8,128)(2,1)} %copy-done.31), channel_id=1, source_target_pairs={{16,0},{17,1},{18,2},{19,3},{20,4},{21,5},{22,6},{23,7}} | collective-permute-start | bytes 786440 | tf_op jit(solution)/shard_map/ppermute | solution.py:420
  117.9 33.5 %collective-permute-start.22 = (bf16[1024,128]{1,0:T(8,128)(2,1)}, bf16[1024,128]{1,0:T(8,128)(2,1)}, u32[]{:S(2)}, u32[]{:S(2)}) collective-permute-start(bf16[1024,128]{1,0:T(8,128)(2,1)} %copy-done.31), channel_id=1, source_target_pairs={{16,8},{17,9},{18,10},{19,11},{20,12},{21,13},{22,14},{23,15}} | collective-permute-start | bytes 786440 | tf_op jit(solution)/shard_map/ppermute | solution.py:420
  119.9 2.2 %copy-start.4 = (bf16[2,1024,1024]{2,1,0:T(8,128)(2,1)S(1)}, bf16[2,1024,1024]{2,1,0:T(8,128)(2,1)}, u32[]{:S(2)}) copy-start(bf16[2,1024,1024]{2,1,0:T(8,128)(2,1)} %copy-done) | copy-start | bytes 12582916
  132.0 19.4 %collective-permute-start.21 = (bf16[1024,128]{1,0:T(8,128)(2,1)}, bf16[1024,128]{1,0:T(8,128)(2,1)}, u32[]{:S(2)}, u32[]{:S(2)}) collective-permute-start(bf16[1024,128]{1,0:T(8,128)(2,1)} %get-tuple-element.93), channel_id=1, source_target_pairs={{16,0},{17,1},{18,2},{19,3},{20,4},{21,5},{22,6},{23,7}} | collective-permute-start | bytes 786440 | tf_op jit(solution)/shard_map/ppermute | solution.py:426
  134.0 17.4 %collective-permute-start.20 = (bf16[1024,128]{1,0:T(8,128)(2,1)}, bf16[1024,128]{1,0:T(8,128)(2,1)}, u32[]{:S(2)}, u32[]{:S(2)}) collective-permute-start(bf16[1024,128]{1,0:T(8,128)(2,1)} %get-tuple-element.93), channel_id=1, source_target_pairs={{16,8},{17,9},{18,10},{19,11},{20,12},{21,13},{22,14},{23,15}} | collective-permute-start | bytes 786440 | tf_op jit(solution)/shard_map/ppermute | solution.py:426
  138.7 22.4 %collective-permute-start.24 = (bf16[1024,256]{1,0:T(8,128)(2,1)}, bf16[1024,256]{1,0:T(8,128)(2,1)}, u32[]{:S(2)}, u32[]{:S(2)}) collective-permute-start(bf16[1024,256]{1,0:T(8,128)(2,1)} %get-tuple-element.96), channel_id=1, source_target_pairs={{8,0},{9,1},{10,2},{11,3},{12,4},{13,5},{14,6},{15,7}} | collective-permute-start | bytes 1572872 | tf_op jit(solution)/shard_map/ppermute | solution.py:371
  140.2 2.2 %copy-start.5 = (bf16[2,1024,1024]{2,1,0:T(8,128)(2,1)S(1)}, bf16[2,1024,1024]{2,1,0:T(8,128)(2,1)}, u32[]{:S(2)}) copy-start(bf16[2,1024,1024]{2,1,0:T(8,128)(2,1)} %copy-done) | copy-start | bytes 12582916
  143.6 3.0 %copy-start.17 = (f32[1024,256]{1,0:T(8,128)S(1)}, f32[1024,256]{1,0:T(8,128)}, u32[]{:S(2)}) copy-start(f32[1024,256]{1,0:T(8,128)} %copy-done.16) | copy-start | bytes 3145732
  146.6 4.8 %copy-start.9 = (bf16[1024,1024]{1,0:T(8,128)(2,1)S(1)}, bf16[1024,1024]{1,0:T(8,128)(2,1)}, u32[]{:S(2)}) copy-start(bf16[1024,1024]{1,0:T(8,128)(2,1)} %copy-done.8) | copy-start | bytes 6291460
  146.6 4.8 %copy-start.12 = (bf16[1024,1024]{1,0:T(8,128)(2,1)S(1)}, bf16[1024,1024]{1,0:T(8,128)(2,1)}, u32[]{:S(2)}) copy-start(bf16[1024,1024]{1,0:T(8,128)(2,1)} %copy-done.11) | copy-start | bytes 6291460
  151.4 2.7 %copy-start.30 = (bf16[1024,256]{1,0:T(8,128)(2,1)}, bf16[1024,256]{1,0:T(8,128)(2,1)S(1)}, u32[]{:S(2)}) copy-start(bf16[1024,256]{1,0:T(8,128)(2,1)S(1)} %get-tuple-element.100) | copy-start | bytes 1572868
  155.0 33.2 %all-to-all-start.3 = ((bf16[8,256,256]{2,1,0:T(8,128)(2,1)}), bf16[8,256,256]{2,1,0:T(8,128)(2,1)S(1)}, u32[]{:S(2)}, u32[]{:S(2)}) async-start(bf16[8,256,256]{2,1,0:T(8,128)(2,1)} %copy-done.18), calls=%async_computation.3 | async-start | bytes 2097152 | tf_op jit(solution)/shard_map/all_to_all | solution.py:66
  159.1 26.2 %collective-permute-start.25 = (bf16[1024,256]{1,0:T(8,128)(2,1)}, bf16[1024,256]{1,0:T(8,128)(2,1)S(1)}, u32[]{:S(2)}, u32[]{:S(2)}) collective-permute-start(bf16[1024,256]{1,0:T(8,128)(2,1)} %copy-done.30), channel_id=1, source_target_pairs={{0,4},{4,0},{1,5},{5,1},{2,6},{6,2},{3,7},{7,3},{8,12},{12,8},{9,1... | collective-permute-start | bytes 1572872 | tf_op jit(solution)/shard_map/ppermute | solution.py:51
  161.1 2.2 %copy-start.6 = (bf16[2,1024,1024]{2,1,0:T(8,128)(2,1)S(1)}, bf16[2,1024,1024]{2,1,0:T(8,128)(2,1)}, u32[]{:S(2)}) copy-start(bf16[2,1024,1024]{2,1,0:T(8,128)(2,1)} %copy-done) | copy-start | bytes 12582916
  169.6 26.5 %collective-permute-start.26 = (bf16[1024,256]{1,0:T(8,128)(2,1)}, bf16[1024,256]{1,0:T(8,128)(2,1)}, u32[]{:S(2)}, u32[]{:S(2)}) collective-permute-start(bf16[1024,256]{1,0:T(8,128)(2,1)} %get-tuple-element.108), channel_id=1, source_target_pairs={{0,4},{4,0},{1,5},{5,1},{2,6},{6,2},{3,7},{7,3},{8,12},{12,8},{9,1... | collective-permute-start | bytes 1572872 | tf_op jit(solution)/shard_map/ppermute | solution.py:51
  185.3 2.9 %copy-start.10 = (bf16[1024,1024]{1,0:T(8,128)(2,1)S(1)}, bf16[1024,1024]{1,0:T(8,128)(2,1)}, u32[]{:S(2)}) copy-start(bf16[1024,1024]{1,0:T(8,128)(2,1)} %copy-done.8) | copy-start | bytes 6291460
  (18 other events, 18.6 us)

commit v6 on v5

v6 whole, which is shorter than its diff:
```python
import functools

import jax
import jax.numpy as jnp
from jax import lax
from jax.experimental import pallas as pl
from jax.experimental.pallas import tpu as pltpu
from jax.sharding import Mesh, PartitionSpec as P

LEVELS = 3
LOW = jnp.bfloat16
WIDE = jnp.float32
MIB = 2**20


def shifted(value, axis, steps):
    count = lax.axis_size(axis)
    first, last = (max(0, -steps), min(count, count - steps))
    return lax.ppermute(value, axis, [(source, source + steps) for source in range(first, last)])


def doubling(gains, spreads, offsets):
    gain = gains[0]
    spread = spreads[0]
    offset = offsets[0]
    size_d = gain.shape[1]
    identity = jnp.eye(size_d, dtype=LOW)
    for section_number in range(LEVELS):
        distance = 2**section_number
        beyond = lax.axis_index("tm") + distance >= lax.axis_size("tm")
        own_gain = gain.astype(LOW)
        own_spread = spread.astype(LOW)
        own_offset = offset.astype(LOW)
        own_full = lax.all_gather(own_gain, "rows", axis=0, tiled=True)
        spread_full = lax.all_gather(own_spread, "rows", axis=0, tiled=True)
        far_full, far_spread_full, far_offset = shifted((own_full, spread_full, own_offset), "tm", -distance)
        far_full = jnp.where(beyond, identity, far_full)
        row_start = lax.axis_index("rows") * gain.shape[0]
        own_rows = lax.dynamic_slice_in_dim(own_full, row_start, gain.shape[0], 0)
        middle = jnp.dot(own_rows, far_spread_full, preferred_element_type=WIDE).astype(LOW)
        new_gain = jnp.dot(own_rows, far_full, preferred_element_type=WIDE)
        new_spread = (
            lax.dot_general(middle, own_full, (((1,), (1,)), ((), ())), preferred_element_type=WIDE) + spread
        )
        new_offset = jnp.dot(own_full, far_offset, preferred_element_type=WIDE) + offset
        gain, spread, offset = (new_gain, new_spread, new_offset)
    return (gain[None], spread[None], offset[None])


def swap(value, axis):
    return lax.ppermute(value, axis, [(0, 1), (1, 0)])


def mm(a, b):
    return jnp.dot(a, b, preferred_element_type=WIDE)


def mm_bt(a, b):
    return lax.dot_general(a, b, (((1,), (1,)), ((), ())), preferred_element_type=WIDE)


GROUP = ("y", "c", "x")


def exchange(blocks):
    return lax.all_to_all(blocks, GROUP, 0, 0)


def low(*shape):
    return jax.ShapeDtypeStruct(shape, LOW)


def wide(*shape):
    return jax.ShapeDtypeStruct(shape, WIDE)


ANY = pl.BlockSpec(memory_space=pl.ANY)
VMEM = pl.BlockSpec(memory_space=pltpu.VMEM)
SMEM = pl.BlockSpec(memory_space=pltpu.SMEM)


class Refs:
    pass


class Order:
    def __init__(self, ids):
        self.ids = ids
        self.token = jnp.zeros((8, 128), jnp.int32)
        self.state = {}

    def call(self, kernel, operands, outs, mib, new={}, drop=(), scratch=(), aliases={}, far_in=(), far_out=()):
        n, m, old = len(operands), len(outs), list(self.state)
        going = [name for name in old if name not in drop]

        def body(ids, token, *refs):
            at = Refs()
            for name, ref in zip(old, refs):
                setattr(at, name, ref)
            ins, refs = refs[len(old) : len(old) + n], refs[len(old) + n :]
            results, refs = refs[:m], refs[m + 1 :]
            for name, ref in zip(going, refs):
                if name.startswith("far"):
                    setattr(at, name + "_next", ref)
            refs = refs[len(going) :]
            for name, ref in zip(new, refs):
                setattr(at, name, ref)
            kernel(ids, at, *ins, *results, *refs[len(new) :])

        first = 2 + len(old)
        links = {1: m} | {first + i: o for i, o in aliases.items()}
        links |= {2 + old.index(name): m + 1 + i for i, name in enumerate(going)}
        results = pl.pallas_call(
            body,
            in_specs=[SMEM, ANY] + [VMEM] * len(old) + [ANY if i in far_in else VMEM for i in range(n)],
            out_specs=[ANY if i in far_out else VMEM for i in range(m)] + [ANY] + [VMEM] * (len(going) + len(new)),
            out_shape=list(outs)
            + [jax.ShapeDtypeStruct(self.token.shape, jnp.int32)]
            + [pltpu.VMEM(self.state[name].shape, self.state[name].dtype) for name in going]
            + [pltpu.VMEM(shape, dtype) for shape, dtype in new.values()],
            scratch_shapes=list(scratch),
            input_output_aliases=links,
            cost_estimate=pl.CostEstimate(flops=1, bytes_accessed=1, transcendentals=0),
            compiler_params=pltpu.CompilerParams(vmem_limit_bytes=mib * MIB),
        )(self.ids, self.token, *self.state.values(), *operands)
        self.token = results[m]
        self.state = dict(zip(going + list(new), results[m + 1 :]))
        return results[:m]


def gather_lanes(blocks, into, start, width):
    for s in range(blocks.shape[0]):
        into[:, s * width : (s + 1) * width] = blocks[s, :, start : start + width]


def pair_kernel(ids, at, *refs):
    pieces, (quarter, sems) = refs[:8], refs[8:]
    group = 2 * ids[1] + ids[2]
    me = 4 * ids[0] + group
    rows = pieces[0].shape[0]
    copies = []
    for i in range(8):
        place = me ^ i
        into = at.both.at[place >> 2, pl.ds(pl.multiple_of((place & 3) * rows, rows), rows), :]
        copies.append(pltpu.make_async_copy(pieces[i], into, sems.at[i]))
        copies[-1].start()
    for copy in copies:
        copy.wait()
    for r in range(4):
        cut = slice(r * rows, (r + 1) * rows)
        at.pair[cut, :] = mm(at.both[0, cut, :], at.both[1]).astype(LOW)
    quarter[...] = at.pair[pl.ds(pl.multiple_of(group * rows, rows), rows), :]


def spread_kernel(ids, at, l_low, l_got, m_ref):
    part, rows = l_got.shape[0], l_low.shape[0]

    def product(slab):
        for r in range(4):
            m = mm_bt(at.both[0, r * rows : (r + 1) * rows, :], slab).astype(LOW)
            m_ref[2 * r] = m
            m_ref[2 * r + 1] = m

    @pl.when(ids[0] == 0)
    def _():
        product(l_got[...])

    @pl.when(ids[0] == 1)
    def _():
        product(l_low[part:, :])


def spread_start_kernel(ids, at, blocks, spread, l_got, a_low, m):
    part = l_got.shape[0]
    gather_lanes(blocks, m, 0, part)
    at.prod[...] = mm_bt(m[...], at.both[0])

    @pl.when(ids[0] == 0)
    def _():
        at.slab[...] = (at.prod[:part, :] + spread[0, :part, :]).T

    @pl.when(ids[0] == 1)
    def _():
        at.slab[...] = (at.prod[part:, :] + l_got[...].astype(WIDE)).T

    a_low[...] = at.slab[...].astype(LOW)


def spread_hop_kernel(ids, at, got, m_ref, near):
    part = got.shape[1]
    rows = 2 * part
    m = mm(at.pair[...], got[...]).astype(LOW)
    m_ref[...] = m
    other = mm(at.both[1], got[...]).astype(LOW)
    for r in range(4):
        near[2 * r] = m[r * rows : (r + 1) * rows, :]
        near[2 * r + 1] = other[r * rows : (r + 1) * rows, :]


def spread_next_kernel(ids, at, blocks, b_l, m):
    gather_lanes(blocks, m, 0, m.shape[0])
    b_l[...] = (mm_bt(at.pair[...], m[...]) + at.slab[...]).astype(LOW)


def near_kernel(ids, at, blocks, spread, m):
    gather_lanes(blocks, m, 0, blocks.shape[2])

    @pl.when(ids[0] == 0)
    def _():
        at.near[...] = mm_bt(m[...], at.pair[...]) + at.prod[...] + spread[0]

    @pl.when(ids[0] == 1)
    def _():
        at.near[...] = mm_bt(m[...], at.both[1]) + spread[0]


def next_gain_kernel(ids, at, *refs):
    quarters, (slab_ref, sems) = refs[:4], refs[4:]
    part, rows = slab_ref.shape[1], quarters[0].shape[0]
    group = 2 * ids[1] + ids[2]
    copies = []
    for i in range(4):
        into = at.following.at[pl.ds(pl.multiple_of((group ^ i) * rows, rows), rows), :]
        copies.append(pltpu.make_async_copy(quarters[i], into, sems.at[i]))
        copies[-1].start()
    for copy in copies:
        copy.wait()
    slab = pl.ds(pl.multiple_of((2 * group + ids[0]) * part, part), part)
    slab_ref[...] = mm(at.pair[...], at.following[:, slab]).astype(LOW)


def far_kernel(ids, at, e_a, e_b, l_a, l_b, out, far):
    size, part = e_a.shape
    rows = 2 * part

    @pl.when(ids[3] < 2)
    def _():
        far[:, :part] = e_a[...] + e_b[...]

    @pl.when(ids[3] >= 2)
    def _():
        slab = (2 * ids[1] + ids[2]) * 2 + ids[0]
        column = lax.broadcasted_iota(jnp.int32, (size, part), 1) + slab * part
        row = lax.broadcasted_iota(jnp.int32, (size, part), 0)
        far[:, :part] = jnp.where(row == column, 1.0, 0.0).astype(LOW)

    far[:, part:] = l_a[...] + l_b[...]

    @pl.when(ids[3] % 2 == 0)
    def _():
        far[...] = mm(at.following[...], far[...]).astype(LOW)

    one = mm(at.pair[...], far[...]).astype(LOW)
    two = mm(at.both[1], far[...]).astype(LOW)
    for r in range(4):
        out[2 * r] = one[r * rows : (r + 1) * rows, :]
        out[2 * r + 1] = two[r * rows : (r + 1) * rows, :]


def end_kernel(ids, at, blocks, out_gain, out_spread, m):
    part = blocks.shape[2] // 2
    gather_lanes(blocks, m, part, part)
    for s in range(blocks.shape[0]):
        out_gain[:, s * part : (s + 1) * part] = blocks[s, :, :part].astype(WIDE)

    @pl.when(ids[3] % 2 == 0)
    def _():
        m[...] = mm_bt(m[...], at.following[...]).astype(LOW)

    @pl.when(ids[0] == 0)
    def _():
        out_spread[...] = mm_bt(m[...], at.pair[...]) + at.near[...]

    @pl.when(ids[0] == 1)
    def _():
        out_spread[...] = mm_bt(m[...], at.both[1]) + at.near[...]


def columns(ref, side, chunk, width):
    start = side * (ref.shape[1] // 2) + chunk * width
    return ref.at[:, pl.ds(pl.multiple_of(start, width), width)]


def start_kernel(chunk, ids, at, got, offset, now, keep, sem):
    copy = pltpu.make_async_copy(columns(offset, ids[0], chunk, keep.shape[1]), keep, sem)
    copy.start()
    p, own = getattr(at, f"p{chunk}"), getattr(at, f"own{chunk}")

    @pl.when(ids[0] == 0)
    def _():
        p[...] = mm(at.both[0], got[...])

    copy.wait()

    @pl.when(ids[0] == 0)
    def _():
        own[...] = (p[...] + keep[...]).astype(LOW)

    @pl.when(ids[0] == 1)
    def _():
        p[...] = mm(at.both[0], keep[...].astype(LOW))
        own[...] = (p[...] + got[...].astype(WIDE)).astype(LOW)

    now[...] = own[...]


def hop_kernel(chunk, ids, at, got, now):
    own, far = getattr(at, f"own{chunk}"), getattr(at, f"far{chunk}")
    now[...] = (mm(at.pair[...], got[...]) + own[...].astype(WIDE)).astype(LOW)
    if hasattr(at, f"far{chunk}_next"):
        getattr(at, f"far{chunk}_next")[...] = far[...] + got[...]
    else:
        far[...] = got[...]


def last_kernel(chunk, ids, at, got, offset, *refs):
    out, send, keep, far, sems = refs[-5:]
    p = getattr(at, f"p{chunk}")
    width = keep.shape[1]
    copy = pltpu.make_async_copy(columns(offset, ids[0], chunk, width), keep, sems.at[0])
    copy.start()
    far[...] = getattr(at, f"far{chunk}")[...] + got[...]

    @pl.when(ids[0] == 0)
    def _():
        send[...] = mm(at.both[1], far[...]).astype(LOW)

    @pl.when(ids[0] == 1)
    def _():
        send[...] = (mm(at.pair[...], far[...]) + p[...]).astype(LOW)

    copy.wait()

    @pl.when(ids[0] == 0)
    def _():
        keep[...] = mm(at.pair[...], far[...]) + p[...] + keep[...]

    @pl.when(ids[0] == 1)
    def _():
        keep[...] = mm(at.both[1], far[...]) + keep[...]

    copy = pltpu.make_async_copy(keep, columns(out, ids[0], chunk, width), sems.at[1])
    copy.start()
    copy.wait()


def add_kernel(chunk, ids, at, got, offset, into, out, keep, sems):
    width = keep.shape[1]
    copy = pltpu.make_async_copy(columns(offset, 1 - ids[0], chunk, width), keep, sems.at[0])
    copy.start()
    copy.wait()
    keep[...] = got[...].astype(WIDE) + keep[...]
    copy = pltpu.make_async_copy(keep, columns(out, 1 - ids[0], chunk, width), sems.at[1])
    copy.start()
    copy.wait()


def suffix(gains, spreads, offsets):
    x, y, c, z = (lax.axis_index(name) for name in ("x", "y", "c", "z"))
    gain = gains[0]
    rows, size_d = gain.shape
    part = rows // 2
    chunks = 2
    half = offsets.shape[2] // 2
    width = half // chunks
    ids = jnp.stack([x, y, c, z]).astype(jnp.int32)
    level = [(3, 2), (1, 0)]
    order = Order(ids)
    in_hbm = lambda a: pltpu.with_memory_space_constraint(a, pltpu.HBM)

    e_low = gain.astype(LOW)
    e_x, e_y = swap(e_low, "x"), swap(e_low, "y")

    l_low = spreads[0].astype(LOW)
    l_send = lax.dynamic_slice_in_dim(l_low, (1 - x) * part, part, 0)
    g_send = [
        lax.dynamic_slice_in_dim(offsets[0], (1 - x) * half + i * width, width, 1).astype(LOW) for i in range(chunks)
    ]
    l_send, g_send[0], e_x = lax.optimization_barrier((l_send, g_send[0], e_x))
    e_xy = swap(e_x, "y")
    l_got = swap(l_send, "x")
    g_got = [swap(g_send[0], "x")]
    for i in range(1, chunks):
        g_send[i], g_got[-1] = lax.optimization_barrier((g_send[i], g_got[-1]))
        g_got.append(swap(g_send[i], "x"))
    pieces = [e_low, None, e_y, None, e_x, None, e_xy, None]
    for i in range(0, 8, 2):
        pieces[i + 1] = swap(pieces[i], "c")
    offset, spread = in_hbm(offsets[0]), in_hbm(spreads)

    keep = pltpu.VMEM((size_d, width), WIDE)
    column = pltpu.VMEM((size_d, width), LOW)
    slab_rows = pltpu.VMEM((rows, size_d), LOW)

    def start(i):
        new = {f"p{i}": ((size_d, width), WIDE), f"own{i}": ((size_d, width), LOW)}
        return order.call(
            functools.partial(start_kernel, i), [g_got[i], offset], [low(size_d, width)], 10,
            new=new, far_in=(1,), scratch=[keep, pltpu.SemaphoreType.DMA(())],
        )[0]

    def down(value, source):
        return lax.ppermute(value, "z", [(source, source - 1)])

    def hop(i, got):
        known = f"far{i}" in order.state
        return order.call(
            functools.partial(hop_kernel, i), [got], [low(size_d, width)], 10,
            new={} if known else {f"far{i}": ((size_d, width), LOW)}, drop=(f"own{i}",) if known else (),
        )[0]

    def last(i, got, into):
        extra = [] if into is None else [into]
        return order.call(
            functools.partial(last_kernel, i), [got, offset] + extra,
            [wide(*offset.shape), low(size_d, width)], 12, drop=(f"p{i}", f"far{i}"),
            far_in=(1, 2), far_out=(0,), aliases={2: 0} if extra else {},
            scratch=[keep, column, pltpu.SemaphoreType.DMA((2,))],
        )

    def add(i, got, into):
        return order.call(
            functools.partial(add_kernel, i), [got, offset, into], [wide(*offset.shape)], 10,
            far_in=(1, 2), far_out=(0,), aliases={2: 0}, scratch=[keep, pltpu.SemaphoreType.DMA((2,))],
        )[0]

    square = (size_d, size_d)
    (quarter,) = order.call(
        pair_kernel, pieces, [low(rows, size_d)], 16,
        new={"both": ((2,) + square, LOW), "pair": (square, LOW)},
        far_in=range(8), scratch=[pltpu.SemaphoreType.DMA((8,))],
    )
    quarter = lax.ppermute(quarter, "z", level)
    quarter_y = swap(quarter, "y")
    quarters = [quarter, swap(quarter, "c"), quarter_y, swap(quarter_y, "c")]
    (m,) = order.call(spread_kernel, [l_low, l_got], [low(8, rows, part)], 12)
    m = exchange(m)
    got0 = down(start(0), 3)
    (a_low,) = order.call(
        spread_start_kernel, [m, spread, l_got], [low(size_d, part)], 14,
        new={"prod": ((rows, size_d), WIDE), "slab": ((size_d, part), WIDE)}, scratch=[slab_rows],
    )
    l_next = lax.ppermute(a_low, "z", level)
    got1 = down(start(1), 3)
    got0 = down(hop(0, got0), 2)

    m, near = order.call(spread_hop_kernel, [l_next], [low(size_d, part), low(8, rows, part)], 12)
    m = exchange(m.reshape(8, part, part))
    near = exchange(near)
    got1 = down(hop(1, got1), 2)
    (b_l,) = order.call(
        spread_next_kernel, [m], [low(size_d, part)], 10, drop=("slab",), scratch=[pltpu.VMEM((part, size_d), LOW)]
    )
    l_far = lax.ppermute(b_l, "z", [(2, 1)]), lax.ppermute(b_l, "z", [(2, 0)])
    (e_slab,) = order.call(
        next_gain_kernel, quarters, [low(size_d, part)], 10,
        new={"following": (square, LOW)}, far_in=range(4), scratch=[pltpu.SemaphoreType.DMA((4,))],
    )
    e_far = lax.ppermute(e_slab, "z", [(2, 1)]), lax.ppermute(e_slab, "z", [(2, 0)])
    got0 = down(hop(0, got0), 1)
    order.call(
        near_kernel, [near, spread], [], 12, new={"near": ((rows, size_d), WIDE)}, drop=("prod",), scratch=[slab_rows]
    )
    got1 = down(hop(1, got1), 1)

    out_offset, other0 = last(0, got0, None)
    other0 = swap(other0, "x")
    (m,) = order.call(
        far_kernel, [*e_far, *l_far], [low(8, rows, rows)], 12, scratch=[pltpu.VMEM((size_d, rows), LOW)]
    )
    m = exchange(m)
    out_offset, other1 = last(1, got1, out_offset)
    other1 = swap(other1, "x")
    out_offset = add(0, other0, out_offset)
    out_gain, out_spread = order.call(
        end_kernel, [m], [wide(rows, size_d), wide(rows, size_d)], 14,
        drop=("both", "pair", "following", "near"), scratch=[slab_rows],
    )
    out_offset = add(1, other1, out_offset)
    return (out_gain[None], out_spread[None], out_offset[None])


def solution(mesh):
    steps, rows = mesh.shape["tm"], mesh.shape["rows"]
    if steps == 2**LEVELS and rows == 4:
        devices = mesh.devices.reshape(steps // 2, 2, 2, 2)
        mesh = Mesh(devices, ("z", "x", "y", "c"))
        by_row, by_column = P(("z", "x"), ("y", "c"), None), P(("z", "x"), None, ("y", "c"))
        body = suffix
    else:
        by_row, by_column = P("tm", "rows", None), P("tm", None, "rows")
        body = doubling
    return jax.shard_map(
        body,
        mesh=mesh,
        in_specs=(by_row, by_row, by_column),
        out_specs=(by_row, by_row, by_column),
        check_vma=False,
    )
```

time: 201 us -> 301 us (1.50)
  local copies, waits for them, and re-layouts: 35 us -> 137 us
  waiting for transfers between devices: 52.3 us -> 48.6 us
  starting transfers between devices: 48.1 us -> 51.7 us
  Pallas kernels: 60.2 us -> 56.9 us
    unnamed x70 -> x222, local copies, waits for them, and re-layouts: 31.6 us -> 134 us
    pallas_call x19, Pallas kernels: 60.2 us -> 56.9 us  [call(): pl.pallas_call(body, in_specs=[SMEM, ANY] + [VMEM] * len(old) + [ANY if i...]
  transfers between devices with their start and end apart: 31 -> 31, of which waited for: 9 -> 8; matrix products, arithmetic and copies ran while one was open for 2% -> 1% of each run, Pallas kernels for 28% -> 18%
where the time goes in v6:
time: 301 us; the launch traced here: 298 us
  local copies, waits for them, and re-layouts  137 us (46%)
  Pallas kernels  56.9 us (19%)
  starting transfers between devices  51.7 us (17%)
  waiting for transfers between devices  48.6 us (16%)
    unnamed x222, local copies, waits for them, and re-layouts  134 us
    pallas_call x19, Pallas kernels, call(): pl.pallas_call(body, in_specs=[SMEM, ANY] + [VMEM] * len(old) + [ANY if i...  56.9 us
    ppermute x15, waiting for transfers between devices, swap(): return lax.ppermute(value, axis, [(0, 1), (1, 0)])  35.4 us
    all_to_all x4, starting transfers between devices, exchange(): return lax.all_to_all(blocks, GROUP, 0, 0)  16.6 us
    ppermute x15, starting transfers between devices, swap(): return lax.ppermute(value, axis, [(0, 1), (1, 0)])  13.2 us
    ppermute x6, starting transfers between devices, down(): return lax.ppermute(value, 'z', [(source, source - 1)])  12.1 us
    ppermute x1, waiting for transfers between devices, suffix(): l_next = lax.ppermute(a_low, 'z', level)  10.2 us
  transfers between devices with their start and end apart: 31, of which 8 were waited for; matrix products, arithmetic and copies ran while one was open for 1% of the time, Pallas kernels for 18%

profile of v6, /device:TPU:16, one launch (start us, length us, event | category | flops | bytes accessed | tf_op | source)
XLA Modules:
  0.0 297.5 jit_solution(8094121371236791433)
XLA Ops:
  5.9 2.6 fusion.1
  8.5 7.2 %collective-permute-done.3.refs_4_ = bf16[256,1024]{1,0:T(8,128)(2,1)S(1)} collective-permute-done((bf16[256,1024]{1,0:T(8,128)(2,1)S(1)}, bf16[256,1024]{1,0:T(8,128)(2,1)S(1)}, u32[]{:S(2)}, u32[]{:S(2)}) %collective-permute-start.3) | collective-permute-done | bytes 524320 | tf_op jit(solution)/shard_map/ppermute | solution.py:51
  18.6 10.0 %collective-permute-done.5.refs_6_ = bf16[256,1024]{1,0:T(8,128)(2,1)S(1)} collective-permute-done((bf16[256,1024]{1,0:T(8,128)(2,1)S(1)}, bf16[256,1024]{1,0:T(8,128)(2,1)S(1)}, u32[]{:S(2)}, u32[]{:S(2)}) %collective-permute-start.5) | collective-permute-done | bytes 524320 | tf_op jit(solution)/shard_map/ppermute | solution.py:51
  36.7 5.1 %shard_map.58 = (bf16[256,1024]{1,0:T(8,128)(2,1)}, s32[8,128]{1,0:T(8,128)S(1)}, bf16[2,1024,1024]{2,1,0:T(8,128)(2,1)S(1)}, bf16[1024,1024]{1,0:T(8,128)(2,1)S(1)}) custom-call(s32[4]{0:T(128)S(1)} %pad_add_fusion.ids, s32[8,128]{1,0:T(8,128)S(1)} %broadcast_in_dim.12.token, ...), custom_call_target="tpu_custom_call", output_to_operand_aliasing={{1}: (1, {})} | custom-call | flops 1 | bytes 1 | tf_op jit(solution)/shard_map/pallas_call | solution.py:113
  45.6 6.8 %collective-permute-done.7.refs_3_.refs_6_ = bf16[128,1024]{1,0:T(8,128)(2,1)S(1)} collective-permute-done((bf16[128,1024]{1,0:T(8,128)(2,1)S(1)}, bf16[128,1024]{1,0:T(8,128)(2,1)S(1)}, u32[]{:S(2)}, u32[]{:S(2)}) %collective-permute-start.7) | collective-permute-done | bytes 262176 | tf_op jit(solution)/shard_map/ppermute | solution.py:51
  52.4 2.0 shard_map.59
  54.4 2.0 copy-done
  56.4 4.1 %all-to-all-start = ((bf16[8,256,128]{2,1,0:T(8,128)(2,1)}), bf16[8,256,128]{2,1,0:T(8,128)(2,1)}, u32[]{:S(2)}, u32[]{:S(2)}) async-start(bf16[8,256,128]{2,1,0:T(8,128)(2,1)} %get-tuple-element.178), calls=%async_computation | async-start | bytes 1048576 | tf_op jit(solution)/shard_map/all_to_all | solution.py:66
  60.6 2.2 copy-done.1
  62.8 3.3 %shard_map.60 = (bf16[1024,256]{1,0:T(8,128)(2,1)}, s32[8,128]{1,0:T(8,128)S(1)}, bf16[2,1024,1024]{2,1,0:T(8,128)(2,1)S(1)}, bf16[1024,1024]{1,0:T(8,128)(2,1)S...) custom-call(s32[4]{0:T(128)S(1)} %pad_add_fusion.ids, ...), custom_call_target="tpu_custom_call", output_to_operand_aliasing={{1}: (1, {}), {2}: (2, {}), {3}: (3, {})} | custom-call | flops 1 | bytes 1 | tf_op jit(solution)/shard_map/pallas_call | solution.py:113
  72.2 2.2 copy-done.3
  75.4 2.4 shard_map.61
  77.8 2.0 copy-done.4
  79.8 2.2 copy-done.5
  82.0 3.2 %shard_map.62 = (bf16[1024,256]{1,0:T(8,128)(2,1)}, s32[8,128]{1,0:T(8,128)S(1)}, bf16[2,1024,1024]{2,1,0:T(8,128)(2,1)S(1)}, bf16[1024,1024]{1,0:T(8,128)(2,1)S...) custom-call(s32[4]{0:T(128)S(1)} %pad_add_fusion.ids, ...), custom_call_target="tpu_custom_call", output_to_operand_aliasing={{1}: (1, {}), {2}: (2, {}), {3}: (3, {}), {4}: (4, {}), {5}... | custom-call | flops 1 | bytes 1 | tf_op jit(solution)/shard_map/pallas_call | solution.py:113
  87.8 2.6 shard_map.63
  90.4 2.0 copy-done.6
  92.4 4.5 %collective-permute-start.17 = (bf16[1024,256]{1,0:T(8,128)(2,1)}, bf16[1024,256]{1,0:T(8,128)(2,1)}, u32[]{:S(2)}, u32[]{:S(2)}) collective-permute-start(bf16[1024,256]{1,0:T(8,128)(2,1)} %get-tuple-element.253), channel_id=1, source_target_pairs={{16,8},{17,9},{18,10},{19,11},{20,12},{21,13},{22,14},{23,15}} | collective-permute-start | bytes 1572872 | tf_op jit(solution)/shard_map/ppermute | solution.py:403
  98.2 10.2 %collective-permute-done.11.refs_9_ = bf16[1024,128]{1,0:T(8,128)(2,1)S(1)} collective-permute-done((bf16[1024,128]{1,0:T(8,128)(2,1)S(1)}, bf16[1024,128]{1,0:T(8,128)(2,1)S(1)}, u32[]{:S(2)}, u32[]{:S(2)}) %collective-permute-start.11) | collective-permute-done | bytes 262176 | tf_op jit(solution)/shard_map/ppermute | solution.py:443
  108.4 2.2 copy-done.7
  121.2 3.9 %all-to-all-start.1 = ((bf16[8,128,128]{2,1,0:T(8,128)(2,1)}), bf16[8,128,128]{2,1,0:T(8,128)(2,1)S(1)}, u32[]{:S(2)}, u32[]{:S(2)}) async-start(bf16[8,128,128]{2,1,0:T(8,128)(2,1)} %bitcast.19), calls=%async_computation.1 | async-start | bytes 524288 | tf_op jit(solution)/shard_map/all_to_all | solution.py:66
  125.0 2.2 copy-done.9
  133.8 2.6 shard_map.65
  136.4 2.0 copy-done.10
  144.4 2.1 collective-permute-start.18
  146.5 2.2 copy-done.11
  167.9 2.8 shard_map.67
  170.8 2.7 shard_map.68
  173.5 2.0 copy-done.12
  182.7 4.2 %all-to-all-start.2 = ((bf16[8,256,128]{2,1,0:T(8,128)(2,1)}), bf16[8,256,128]{2,1,0:T(8,128)(2,1)}, u32[]{:S(2)}, u32[]{:S(2)}) async-start(bf16[8,256,128]{2,1,0:T(8,128)(2,1)} %copy-done.103), calls=%async_computation.2 | async-start | bytes 1048576 | tf_op jit(solution)/shard_map/all_to_all | solution.py:66
  194.1 2.1 all-to-all-done.2.refs_9_
  196.2 2.2 copy-done.13
  205.6 2.3 shard_map.69
  212.2 2.2 copy-done.15
  217.2 2.6 shard_map.70
  219.8 2.0 copy-done.16
  225.6 2.2 copy-done.17
  230.6 4.1 %shard_map.71 = (f32[1024,1024]{1,0:T(8,128)}, bf16[1024,256]{1,0:T(8,128)(2,1)S(1)}, s32[8,128]{1,0:T(8,128)S(1)}, bf16[2,1024,1024]{2,1,0:T(8,128)(2,1)S(1)}, ...) custom-call(s32[4]{0:T(128)S(1)} %pad_add_fusion.ids, ...), custom_call_target="tpu_custom_call", output_to_operand_aliasing={{2}: (1, {}), {3}: (2, {}), {4}: (3, {}), {5}: (5, {}), {6}... | custom-call | flops 1 | bytes 1 | tf_op jit(solution)/shard_map/pallas_call | solution.py:113
  234.7 3.4 %shard_map.72 = (bf16[8,256,256]{2,1,0:T(8,128)(2,1)S(1)}, s32[8,128]{1,0:T(8,128)S(1)}, bf16[2,1024,1024]{2,1,0:T(8,128)(2,1)S(1)}, bf16[1024,1024]{1,0:T(8,128...) custom-call(s32[4]{0:T(128)S(1)} %pad_add_fusion.ids, ...), custom_call_target="tpu_custom_call", output_to_operand_aliasing={{1}: (1, {}), {2}: (2, {}), {3}: (3, {}), {4}: (4, {}), {5}... | custom-call | flops 1 | bytes 1 | tf_op jit(solution)/shard_map/pallas_call | solution.py:113
  245.3 4.4 %all-to-all-start.3 = ((bf16[8,256,256]{2,1,0:T(8,128)(2,1)}), bf16[8,256,256]{2,1,0:T(8,128)(2,1)}, u32[]{:S(2)}, u32[]{:S(2)}) async-start(bf16[8,256,256]{2,1,0:T(8,128)(2,1)} %copy-done.94), calls=%async_computation.3 | async-start | bytes 2097152 | tf_op jit(solution)/shard_map/all_to_all | solution.py:66
  251.6 2.2 copy-done.19
  257.6 4.8 %shard_map.73 = (f32[1024,1024]{1,0:T(8,128)}, bf16[1024,256]{1,0:T(8,128)(2,1)}, s32[8,128]{1,0:T(8,128)S(1)}, bf16[2,1024,1024]{2,1,0:T(8,128)(2,1)S(1)}, bf16...) custom-call(s32[4]{0:T(128)S(1)} %pad_add_fusion.ids, ...), custom_call_target="tpu_custom_call", output_to_operand_aliasing={{2}: (1, {}), {0}: (10, {}), {3}: (2, {}), {4}: (3, {}), {5... | custom-call | flops 1 | bytes 1 | tf_op jit(solution)/shard_map/pallas_call | solution.py:113
  264.6 11.2 %collective-permute-done.25.refs_4_ = bf16[1024,256]{1,0:T(8,128)(2,1)S(1)} collective-permute-done((bf16[1024,256]{1,0:T(8,128)(2,1)}, bf16[1024,256]{1,0:T(8,128)(2,1)S(1)}, u32[]{:S(2)}, u32[]{:S(2)}) %collective-permute-start.25) | collective-permute-done | bytes 524320 | tf_op jit(solution)/shard_map/ppermute | solution.py:51
  275.7 2.2 copy-done.21
  277.9 2.8 shard_map.74
  285.2 2.2 copy-done.23
  290.2 4.3 %shard_map.75 = (f32[256,1024]{1,0:T(8,128)}, f32[256,1024]{1,0:T(8,128)}, s32[8,128]{1,0:T(8,128)S(1)}) custom-call(s32[4]{0:T(128)S(1)} %pad_add_fusion.ids, s32[8,128]{1,0:T(8,128)S(1)} %get-tuple-element.311.token, bf16[2,1024,1024]{2,1,0:T(8,128)(2,1)S(1)} %copy-done.23, ...), custom_call_target="tpu_custom_call", output_to_operand_aliasing={{2}: (1, {})} | custom-call | flops 1 | bytes 1 | tf_op jit(solution)/shard_map/pallas_call | solution.py:113
  294.5 2.9 shard_map.76
  (262 shorter events, 130.7 us)
Async XLA Ops:
  0.6 4.5 %copy-start.108 = (f32[1,256,1024]{2,1,0:T(8,128)S(1)}, f32[1,256,1024]{2,1,0:T(8,128)}, u32[]{:S(2)}) copy-start(f32[1,256,1024]{2,1,0:T(8,128)} %refs_10_.1) | copy-start | bytes 3145732
  2.0 13.7 %collective-permute-start.3 = (bf16[256,1024]{1,0:T(8,128)(2,1)S(1)}, bf16[256,1024]{1,0:T(8,128)(2,1)S(1)}, u32[]{:S(2)}, u32[]{:S(2)}) collective-permute-start(bf16[256,1024]{1,0:T(8,128)(2,1)S(1)} %convert_bitcast_fusion.refs_0_), channel_id=1, source_target_pairs={{0,4},{4,0},{1,5},{5,1},{2,6},{6,2},{3,7},{7,3},{8,12},{12,8},{9,1... | collective-permute-start | bytes 1572872 | tf_op jit(solution)/shard_map/ppermute | solution.py:51
  3.6 14.2 %collective-permute-start.1 = (bf16[256,1024]{1,0:T(8,128)(2,1)S(1)}, bf16[256,1024]{1,0:T(8,128)(2,1)S(1)}, u32[]{:S(2)}, u32[]{:S(2)}) collective-permute-start(bf16[256,1024]{1,0:T(8,128)(2,1)S(1)} %convert_bitcast_fusion.refs_0_), channel_id=1, source_target_pairs={{0,2},{2,0},{1,3},{3,1},{4,6},{6,4},{5,7},{7,5},{8,10},{10,8},{9,1... | collective-permute-start | bytes 1572872 | tf_op jit(solution)/shard_map/ppermute | solution.py:51
  15.8 12.8 %collective-permute-start.5 = (bf16[256,1024]{1,0:T(8,128)(2,1)S(1)}, bf16[256,1024]{1,0:T(8,128)(2,1)S(1)}, u32[]{:S(2)}, u32[]{:S(2)}) collective-permute-start(bf16[256,1024]{1,0:T(8,128)(2,1)S(1)} %collective-permute-done.3.refs_4_), channel_id=1, source_target_pairs={{0,2},{2,0},{1,3},{3,1},{4,6},{6,4},{5,7},{7,5},{8,10},{10,8},{9,1... | collective-permute-start | bytes 1572872 | tf_op jit(solution)/shard_map/ppermute | solution.py:51
  17.3 13.7 %collective-permute-start = (bf16[256,1024]{1,0:T(8,128)(2,1)S(1)}, bf16[256,1024]{1,0:T(8,128)(2,1)S(1)}, u32[]{:S(2)}, u32[]{:S(2)}) collective-permute-start(bf16[256,1024]{1,0:T(8,128)(2,1)S(1)} %convert_bitcast_fusion.refs_0_), channel_id=1, source_target_pairs={{0,1},{1,0},{2,3},{3,2},{4,5},{5,4},{6,7},{7,6},{8,9},{9,8},{10,11... | collective-permute-start | bytes 1572872 | tf_op jit(solution)/shard_map/ppermute | solution.py:51
  17.3 14.5 %collective-permute-start.4 = (bf16[256,1024]{1,0:T(8,128)(2,1)S(1)}, bf16[256,1024]{1,0:T(8,128)(2,1)S(1)}, u32[]{:S(2)}, u32[]{:S(2)}) collective-permute-start(bf16[256,1024]{1,0:T(8,128)(2,1)S(1)} %collective-permute-done.3.refs_4_), channel_id=1, source_target_pairs={{0,1},{1,0},{2,3},{3,2},{4,5},{5,4},{6,7},{7,6},{8,9},{9,8},{10,11... | collective-permute-start | bytes 1572872 | tf_op jit(solution)/shard_map/ppermute | solution.py:51
  17.8 13.9 %collective-permute-start.2 = (bf16[256,1024]{1,0:T(8,128)(2,1)S(1)}, bf16[256,1024]{1,0:T(8,128)(2,1)}, u32[]{:S(2)}, u32[]{:S(2)}) collective-permute-start(bf16[256,1024]{1,0:T(8,128)(2,1)S(1)} %collective-permute-done.1.refs_2_), channel_id=1, source_target_pairs={{0,1},{1,0},{2,3},{3,2},{4,5},{5,4},{6,7},{7,6},{8,9},{9,8},{10,11... | collective-permute-start | bytes 1572872 | tf_op jit(solution)/shard_map/ppermute | solution.py:51
  28.6 4.0 %collective-permute-start.6 = (bf16[256,1024]{1,0:T(8,128)(2,1)S(1)}, bf16[256,1024]{1,0:T(8,128)(2,1)}, u32[]{:S(2)}, u32[]{:S(2)}) collective-permute-start(bf16[256,1024]{1,0:T(8,128)(2,1)S(1)} %collective-permute-done.5.refs_6_), channel_id=1, source_target_pairs={{0,1},{1,0},{2,3},{3,2},{4,5},{5,4},{6,7},{7,6},{8,9},{9,8},{10,11... | collective-permute-start | bytes 1572872 | tf_op jit(solution)/shard_map/ppermute | solution.py:51
  29.4 14.7 %collective-permute-start.8 = (bf16[1024,256]{1,0:T(8,128)(2,1)}, bf16[1024,256]{1,0:T(8,128)(2,1)}, u32[]{:S(2)}, u32[]{:S(2)}) collective-permute-start(bf16[1024,256]{1,0:T(8,128)(2,1)} %get-tuple-element.171), channel_id=1, source_target_pairs={{0,4},{4,0},{1,5},{5,1},{2,6},{6,2},{3,7},{7,3},{8,12},{12,8},{9,1... | collective-permute-start | bytes 1572872 | tf_op jit(solution)/shard_map/ppermute | solution.py:51
  36.7 6.4 %copy-start.110 = (bf16[128,1024]{1,0:T(8,128)(2,1)S(1)}, bf16[128,1024]{1,0:T(8,128)(2,1)}, u32[]{:S(2)}) copy-start(bf16[128,1024]{1,0:T(8,128)(2,1)} %dynamic-slice_bitcast_fusion) | copy-start | bytes 786436
  36.7 8.8 %copy-start.109 = (f32[1,256,1024]{2,1,0:T(8,128)S(1)}, f32[1,256,1024]{2,1,0:T(8,128)}, u32[]{:S(2)}) copy-start(f32[1,256,1024]{2,1,0:T(8,128)} %refs_10_.1) | copy-start | bytes 3145732
  41.8 27.1 %collective-permute-start.13 = (bf16[256,1024]{1,0:T(8,128)(2,1)}, bf16[256,1024]{1,0:T(8,128)(2,1)}, u32[]{:S(2)}, u32[]{:S(2)}) collective-permute-start(bf16[256,1024]{1,0:T(8,128)(2,1)} %get-tuple-element.241), channel_id=1, source_target_pairs={{24,16},{8,0},{25,17},{9,1},{26,18},{10,2},{27,19},{11,3},{28,20},... | collective-permute-start | bytes 1572872 | tf_op jit(solution)/shard_map/ppermute | solution.py:433
  43.2 9.2 %collective-permute-start.7 = (bf16[128,1024]{1,0:T(8,128)(2,1)S(1)}, bf16[128,1024]{1,0:T(8,128)(2,1)S(1)}, u32[]{:S(2)}, u32[]{:S(2)}) collective-permute-start(bf16[128,1024]{1,0:T(8,128)(2,1)S(1)} %copy-done.110), channel_id=1, source_target_pairs={{0,4},{4,0},{1,5},{5,1},{2,6},{6,2},{3,7},{7,3},{8,12},{12,8},{9,1... | collective-permute-start | bytes 786440 | tf_op jit(solution)/shard_map/ppermute | solution.py:51
  44.0 35.7 %collective-permute-start.9 = (bf16[1024,256]{1,0:T(8,128)(2,1)}, bf16[1024,256]{1,0:T(8,128)(2,1)}, u32[]{:S(2)}, u32[]{:S(2)}) collective-permute-start(bf16[1024,256]{1,0:T(8,128)(2,1)} %get-tuple-element.186), channel_id=1, source_target_pairs={{0,4},{4,0},{1,5},{5,1},{2,6},{6,2},{3,7},{7,3},{8,12},{12,8},{9,1... | collective-permute-start | bytes 1572872 | tf_op jit(solution)/shard_map/ppermute | solution.py:51
  56.4 15.7 %all-to-all-start = ((bf16[8,256,128]{2,1,0:T(8,128)(2,1)}), bf16[8,256,128]{2,1,0:T(8,128)(2,1)}, u32[]{:S(2)}, u32[]{:S(2)}) async-start(bf16[8,256,128]{2,1,0:T(8,128)(2,1)} %get-tuple-element.178), calls=%async_computation | async-start | bytes 1048576 | tf_op jit(solution)/shard_map/all_to_all | solution.py:66
  60.6 2.2 copy-start.1
  68.9 17.6 %collective-permute-start.15 = (bf16[256,1024]{1,0:T(8,128)(2,1)}, bf16[256,1024]{1,0:T(8,128)(2,1)}, u32[]{:S(2)}, u32[]{:S(2)}) collective-permute-start(bf16[256,1024]{1,0:T(8,128)(2,1)} %collective-permute-done.13.refs_9_), channel_id=1, source_target_pairs={{0,2},{2,0},{1,3},{3,1},{4,6},{6,4},{5,7},{7,5},{8,10},{10,8},{9,1... | collective-permute-start | bytes 1572872 | tf_op jit(solution)/shard_map/ppermute | solution.py:51
  70.8 16.9 %collective-permute-start.10 = (bf16[1024,256]{1,0:T(8,128)(2,1)}, bf16[1024,256]{1,0:T(8,128)(2,1)}, u32[]{:S(2)}, u32[]{:S(2)}) collective-permute-start(bf16[1024,256]{1,0:T(8,128)(2,1)} %get-tuple-element.196), channel_id=1, source_target_pairs={{24,16},{25,17},{26,18},{27,19},{28,20},{29,21},{30,22},{31,23}} | collective-permute-start | bytes 1572872 | tf_op jit(solution)/shard_map/ppermute | solution.py:403
  72.1 2.2 copy-start.3
  79.8 2.2 copy-start.5
  85.2 39.8 %collective-permute-start.12 = (bf16[1024,256]{1,0:T(8,128)(2,1)}, bf16[1024,256]{1,0:T(8,128)(2,1)}, u32[]{:S(2)}, u32[]{:S(2)}) collective-permute-start(bf16[1024,256]{1,0:T(8,128)(2,1)} %get-tuple-element.218), channel_id=1, source_target_pairs={{24,16},{25,17},{26,18},{27,19},{28,20},{29,21},{30,22},{31,23}} | collective-permute-start | bytes 1572872 | tf_op jit(solution)/shard_map/ppermute | solution.py:403
  86.5 76.0 %collective-permute-start.14 = (bf16[256,1024]{1,0:T(8,128)(2,1)}, bf16[256,1024]{1,0:T(8,128)(2,1)}, u32[]{:S(2)}, u32[]{:S(2)}) collective-permute-start(bf16[256,1024]{1,0:T(8,128)(2,1)} %collective-permute-done.13.refs_9_), channel_id=1, source_target_pairs={{0,1},{1,0},{2,3},{3,2},{4,5},{5,4},{6,7},{7,6},{8,9},{9,8},{10,11... | collective-permute-start | bytes 1572872 | tf_op jit(solution)/shard_map/ppermute | solution.py:51
  86.6 75.9 %collective-permute-start.16 = (bf16[256,1024]{1,0:T(8,128)(2,1)}, bf16[256,1024]{1,0:T(8,128)(2,1)}, u32[]{:S(2)}, u32[]{:S(2)}) collective-permute-start(bf16[256,1024]{1,0:T(8,128)(2,1)} %collective-permute-done.15.refs_11_), channel_id=1, source_target_pairs={{0,1},{1,0},{2,3},{3,2},{4,5},{5,4},{6,7},{7,6},{8,9},{9,8},{10,11... | collective-permute-start | bytes 1572872 | tf_op jit(solution)/shard_map/ppermute | solution.py:51
  92.4 78.4 %collective-permute-start.17 = (bf16[1024,256]{1,0:T(8,128)(2,1)}, bf16[1024,256]{1,0:T(8,128)(2,1)}, u32[]{:S(2)}, u32[]{:S(2)}) collective-permute-start(bf16[1024,256]{1,0:T(8,128)(2,1)} %get-tuple-element.253), channel_id=1, source_target_pairs={{16,8},{17,9},{18,10},{19,11},{20,12},{21,13},{22,14},{23,15}} | collective-permute-start | bytes 1572872 | tf_op jit(solution)/shard_map/ppermute | solution.py:403
  96.9 11.5 %collective-permute-start.11 = (bf16[1024,128]{1,0:T(8,128)(2,1)S(1)}, bf16[1024,128]{1,0:T(8,128)(2,1)S(1)}, u32[]{:S(2)}, u32[]{:S(2)}) collective-permute-start(bf16[1024,128]{1,0:T(8,128)(2,1)S(1)} %get-tuple-element.207), channel_id=1, source_target_pairs={{24,16},{8,0},{25,17},{9,1},{26,18},{10,2},{27,19},{11,3},{28,20},... | collective-permute-start | bytes 786440 | tf_op jit(solution)/shard_map/ppermute | solution.py:443
  108.4 2.2 copy-start.7
  121.2 25.4 %all-to-all-start.1 = ((bf16[8,128,128]{2,1,0:T(8,128)(2,1)}), bf16[8,128,128]{2,1,0:T(8,128)(2,1)S(1)}, u32[]{:S(2)}, u32[]{:S(2)}) async-start(bf16[8,128,128]{2,1,0:T(8,128)(2,1)} %bitcast.19), calls=%async_computation.1 | async-start | bytes 524288 | tf_op jit(solution)/shard_map/all_to_all | solution.py:66
  125.0 2.2 copy-start.9
  144.4 47.7 %collective-permute-start.18 = (bf16[1024,256]{1,0:T(8,128)(2,1)}, bf16[1024,256]{1,0:T(8,128)(2,1)}, u32[]{:S(2)}, u32[]{:S(2)}) collective-permute-start(bf16[1024,256]{1,0:T(8,128)(2,1)} %get-tuple-element.275), channel_id=1, source_target_pairs={{16,8},{17,9},{18,10},{19,11},{20,12},{21,13},{22,14},{23,15}} | collective-permute-start | bytes 1572872 | tf_op jit(solution)/shard_map/ppermute | solution.py:403
  146.5 2.2 copy-start.11
  170.7 2.7 copy-start.107
  181.2 42.9 %collective-permute-start.19 = (bf16[1024,256]{1,0:T(8,128)(2,1)}, bf16[1024,256]{1,0:T(8,128)(2,1)}, u32[]{:S(2)}, u32[]{:S(2)}) collective-permute-start(bf16[1024,256]{1,0:T(8,128)(2,1)} %get-tuple-element.285), channel_id=1, source_target_pairs={{8,0},{9,1},{10,2},{11,3},{12,4},{13,5},{14,6},{15,7}} | collective-permute-start | bytes 1572872 | tf_op jit(solution)/shard_map/ppermute | solution.py:403
  182.7 13.6 %all-to-all-start.2 = ((bf16[8,256,128]{2,1,0:T(8,128)(2,1)}), bf16[8,256,128]{2,1,0:T(8,128)(2,1)}, u32[]{:S(2)}, u32[]{:S(2)}) async-start(bf16[8,256,128]{2,1,0:T(8,128)(2,1)} %copy-done.103), calls=%async_computation.2 | async-start | bytes 1048576 | tf_op jit(solution)/shard_map/all_to_all | solution.py:66
  186.9 47.8 %collective-permute-start.23 = (bf16[1024,128]{1,0:T(8,128)(2,1)}, bf16[1024,128]{1,0:T(8,128)(2,1)S(1)}, u32[]{:S(2)}, u32[]{:S(2)}) collective-permute-start(bf16[1024,128]{1,0:T(8,128)(2,1)} %copy-done.106), channel_id=1, source_target_pairs={{16,0},{17,1},{18,2},{19,3},{20,4},{21,5},{22,6},{23,7}} | collective-permute-start | bytes 786440 | tf_op jit(solution)/shard_map/ppermute | solution.py:454
  188.2 46.5 %collective-permute-start.22 = (bf16[1024,128]{1,0:T(8,128)(2,1)}, bf16[1024,128]{1,0:T(8,128)(2,1)}, u32[]{:S(2)}, u32[]{:S(2)}) collective-permute-start(bf16[1024,128]{1,0:T(8,128)(2,1)} %copy-done.106), channel_id=1, source_target_pairs={{16,8},{17,9},{18,10},{19,11},{20,12},{21,13},{22,14},{23,15}} | collective-permute-start | bytes 786440 | tf_op jit(solution)/shard_map/ppermute | solution.py:454
  190.1 44.6 %collective-permute-start.21 = (bf16[1024,128]{1,0:T(8,128)(2,1)}, bf16[1024,128]{1,0:T(8,128)(2,1)}, u32[]{:S(2)}, u32[]{:S(2)}) collective-permute-start(bf16[1024,128]{1,0:T(8,128)(2,1)} %copy-done.107), channel_id=1, source_target_pairs={{16,0},{17,1},{18,2},{19,3},{20,4},{21,5},{22,6},{23,7}} | collective-permute-start | bytes 786440 | tf_op jit(solution)/shard_map/ppermute | solution.py:459
  192.1 42.6 %collective-permute-start.20 = (bf16[1024,128]{1,0:T(8,128)(2,1)}, bf16[1024,128]{1,0:T(8,128)(2,1)}, u32[]{:S(2)}, u32[]{:S(2)}) collective-permute-start(bf16[1024,128]{1,0:T(8,128)(2,1)} %copy-done.107), channel_id=1, source_target_pairs={{16,8},{17,9},{18,10},{19,11},{20,12},{21,13},{22,14},{23,15}} | collective-permute-start | bytes 786440 | tf_op jit(solution)/shard_map/ppermute | solution.py:459
  196.2 2.2 copy-start.13
  224.2 27.4 %collective-permute-start.24 = (bf16[1024,256]{1,0:T(8,128)(2,1)}, bf16[1024,256]{1,0:T(8,128)(2,1)}, u32[]{:S(2)}, u32[]{:S(2)}) collective-permute-start(bf16[1024,256]{1,0:T(8,128)(2,1)} %get-tuple-element.302), channel_id=1, source_target_pairs={{8,0},{9,1},{10,2},{11,3},{12,4},{13,5},{14,6},{15,7}} | collective-permute-start | bytes 1572872 | tf_op jit(solution)/shard_map/ppermute | solution.py:403
  225.6 2.2 copy-start.17
  234.7 3.4 %copy-start.105 = (bf16[1024,256]{1,0:T(8,128)(2,1)}, bf16[1024,256]{1,0:T(8,128)(2,1)S(1)}, u32[]{:S(2)}) copy-start(bf16[1024,256]{1,0:T(8,128)(2,1)S(1)} %get-tuple-element.309) | copy-start | bytes 1572868
  245.3 6.3 %copy-start.47 = (f32[1024,256]{1,0:T(8,128)S(1)}, f32[1024,256]{1,0:T(8,128)}, u32[]{:S(2)}) copy-start(f32[1024,256]{1,0:T(8,128)} %copy-done.46) | copy-start | bytes 3145732
  245.3 39.9 %all-to-all-start.3 = ((bf16[8,256,256]{2,1,0:T(8,128)(2,1)}), bf16[8,256,256]{2,1,0:T(8,128)(2,1)}, u32[]{:S(2)}, u32[]{:S(2)}) async-start(bf16[8,256,256]{2,1,0:T(8,128)(2,1)} %copy-done.94), calls=%async_computation.3 | async-start | bytes 2097152 | tf_op jit(solution)/shard_map/all_to_all | solution.py:66
  249.7 26.1 %collective-permute-start.25 = (bf16[1024,256]{1,0:T(8,128)(2,1)}, bf16[1024,256]{1,0:T(8,128)(2,1)S(1)}, u32[]{:S(2)}, u32[]{:S(2)}) collective-permute-start(bf16[1024,256]{1,0:T(8,128)(2,1)} %copy-done.105), channel_id=1, source_target_pairs={{0,4},{4,0},{1,5},{5,1},{2,6},{6,2},{3,7},{7,3},{8,12},{12,8},{9,1... | collective-permute-start | bytes 1572872 | tf_op jit(solution)/shard_map/ppermute | solution.py:51
  251.6 2.2 copy-start.19
  264.4 30.1 %collective-permute-start.26 = (bf16[1024,256]{1,0:T(8,128)(2,1)}, bf16[1024,256]{1,0:T(8,128)(2,1)S(1)}, u32[]{:S(2)}, u32[]{:S(2)}) collective-permute-start(bf16[1024,256]{1,0:T(8,128)(2,1)} %get-tuple-element.320), channel_id=1, source_target_pairs={{0,4},{4,0},{1,5},{5,1},{2,6},{6,2},{3,7},{7,3},{8,12},{12,8},{9,1... | collective-permute-start | bytes 1572872 | tf_op jit(solution)/shard_map/ppermute | solution.py:51
  275.7 2.2 copy-start.21
  285.2 2.2 copy-start.23
  (94 other events, 110.1 us)

commit v7 on v5

--- a/solution.py
+++ b/solution.py
@@ -66,12 +66,8 @@
     return lax.all_to_all(blocks, GROUP, 0, 0)
 
 
-def held(*shape, dtype=LOW):
-    return pltpu.VMEM(shape, dtype)
-
-
-def low(*shape):
-    return jax.ShapeDtypeStruct(shape, LOW)
+def hbm(*shape, dtype=LOW):
+    return pltpu.HBM(shape, dtype)
 
 
 def wide(*shape):
@@ -114,7 +110,7 @@
 
 
 def pair_kernel(ids, *refs):
-    pieces, (both, pair, quarter, sems) = refs[:8], refs[8:]
+    pieces, (e0, e1, pair, quarter, both, sems) = refs[:8], refs[8:]
     group = 2 * ids[1] + ids[2]
     me = 4 * ids[0] + group
     rows = pieces[0].shape[0]
@@ -126,18 +122,23 @@
         copies[-1].start()
     for copy in copies:
         copy.wait()
+    copies = [pltpu.make_async_copy(both.at[i], e, sems.at[i]) for i, e in enumerate((e0, e1))]
+    for copy in copies:
+        copy.start()
     for r in range(4):
         cut = slice(r * rows, (r + 1) * rows)
         pair[cut, :] = mm(both[0, cut, :], both[1]).astype(LOW)
     quarter[...] = pair[pl.ds(pl.multiple_of(group * rows, rows), rows), :]
-
-
-def spread_kernel(ids, both, l_low, l_got, m_ref):
+    for copy in copies:
+        copy.wait()
+
+
+def spread_kernel(ids, e0, l_low, l_got, m_ref):
     part, rows = l_got.shape[0], l_low.shape[0]
 
     def product(slab):
         for r in range(4):
-            m = mm_bt(both[0, r * rows : (r + 1) * rows, :], slab).astype(LOW)
+            m = mm_bt(e0[r * rows : (r + 1) * rows, :], slab).astype(LOW)
             m_ref[2 * r] = m
             m_ref[2 * r + 1] = m
 
@@ -150,71 +151,66 @@
         product(l_low[part:, :])
 
 
-def spread_start_kernel(ids, blocks, both, spread, l_got, prod, a_l, a_low, m):
+def spread_start_kernel(ids, e0, blocks, spread, l_got, prod, slab, a_low, m):
     part = l_got.shape[0]
     gather_lanes(blocks, m, 0, part)
-    prod[...] = mm_bt(m[...], both[0])
-
-    @pl.when(ids[0] == 0)
-    def _():
-        a_l[...] = (prod[:part, :] + spread[0, :part, :]).T
-
-    @pl.when(ids[0] == 1)
-    def _():
-        a_l[...] = (prod[part:, :] + l_got[...].astype(WIDE)).T
-
-    a_low[...] = a_l[...].astype(LOW)
-
-
-def spread_hop_kernel(ids, pair, both, got, m_ref, near):
+    prod[...] = mm_bt(m[...], e0[...])
+
+    @pl.when(ids[0] == 0)
+    def _():
+        slab[...] = (prod[:part, :] + spread[0, :part, :]).T
+
+    @pl.when(ids[0] == 1)
+    def _():
+        slab[...] = (prod[part:, :] + l_got[...].astype(WIDE)).T
+
+    a_low[...] = slab[...].astype(LOW)
+
+
+def spread_hop_kernel(ids, pair, e1, got, m_ref, near):
     part = got.shape[1]
     rows = 2 * part
     m = mm(pair[...], got[...]).astype(LOW)
     m_ref[...] = m
-    other = mm(both[1], got[...]).astype(LOW)
+    other = mm(e1[...], got[...]).astype(LOW)
     for r in range(4):
         near[2 * r] = m[r * rows : (r + 1) * rows, :]
         near[2 * r + 1] = other[r * rows : (r + 1) * rows, :]
 
 
-def spread_next_kernel(ids, blocks, pair, a_l, b_l, m):
+def spread_next_kernel(ids, pair, slab, blocks, b_l, m):
     gather_lanes(blocks, m, 0, m.shape[0])
-    b_l[...] = (mm_bt(pair[...], m[...]) + a_l[...]).astype(LOW)
-
-
-def near_kernel(ids, blocks, pair, both, prod, spread, out, m):
+    b_l[...] = (mm_bt(pair[...], m[...]) + slab[...]).astype(LOW)
+
+
+def near_kernel(ids, pair, e1, prod, blocks, spread, near, m):
     gather_lanes(blocks, m, 0, blocks.shape[2])
 
     @pl.when(ids[0] == 0)
     def _():
-        out[...] = mm_bt(m[...], pair[...]) + prod[...] + spread[0]
-
-    @pl.when(ids[0] == 1)
-    def _():
-        out[...] = mm_bt(m[...], both[1]) + spread[0]
-
-
-def compose_kernel(ids, pair, both, *refs):
-    quarters, (first, second, slab_ref, following) = refs[:4], refs[4:]
+        near[...] = mm_bt(m[...], pair[...]) + prod[...] + spread[0]
+
+    @pl.when(ids[0] == 1)
+    def _():
+        near[...] = mm_bt(m[...], e1[...]) + spread[0]
+
+
+def next_gain_kernel(ids, pair, *refs):
+    quarters, (following, slab_ref, sems) = refs[:4], refs[4:]
     part, rows = slab_ref.shape[1], quarters[0].shape[0]
     group = 2 * ids[1] + ids[2]
-
-    @pl.when(ids[3] % 2 == 0)
-    def _():
-        for i in range(4):
-            following[pl.ds(pl.multiple_of((group ^ i) * rows, rows), rows), :] = quarters[i][...]
-        first[...] = mm(pair[...], following[...]).astype(LOW)
-        second[...] = mm(both[1], following[...]).astype(LOW)
-
-    @pl.when(ids[3] % 2 == 1)
-    def _():
-        first[...] = pair[...]
-        second[...] = both[1]
-
-    slab_ref[...] = first[:, pl.ds(pl.multiple_of((2 * group + ids[0]) * part, part), part)]
-
-
-def far_kernel(ids, first, second, e_a, e_b, l_a, l_b, out, far):
+    copies = []
+    for i in range(4):
+        into = following.at[pl.ds(pl.multiple_of((group ^ i) * rows, rows), rows), :]
+        copies.append(pltpu.make_async_copy(quarters[i], into, sems.at[i]))
+        copies[-1].start()
+    for copy in copies:
+        copy.wait()
+    slab = pl.ds(pl.multiple_of((2 * group + ids[0]) * part, part), part)
+    slab_ref[...] = mm(pair[...], following[:, slab]).astype(LOW)
+
+
+def far_kernel(ids, pair, e1, following, e_a, e_b, l_a, l_b, out, far):
     size, part = e_a.shape
     rows = 2 * part
 
@@ -230,26 +226,35 @@
         far[:, :part] = jnp.where(row == column, 1.0, 0.0).astype(LOW)
 
     far[:, part:] = l_a[...] + l_b[...]
-    one = mm(first[...], far[...]).astype(LOW)
-    two = mm(second[...], far[...]).astype(LOW)
+
+    @pl.when(ids[3] % 2 == 0)
+    def _():
+        far[...] = mm(following[...], far[...]).astype(LOW)
+
+    one = mm(pair[...], far[...]).astype(LOW)
+    two = mm(e1[...], far[...]).astype(LOW)
     for r in range(4):
         out[2 * r] = one[r * rows : (r + 1) * rows, :]
         out[2 * r + 1] = two[r * rows : (r + 1) * rows, :]
 
 
-def end_kernel(ids, blocks, first, second, near, out_gain, out_spread, m):
+def end_kernel(ids, pair, e1, following, near, blocks, out_gain, out_spread, m):
     part = blocks.shape[2] // 2
     gather_lanes(blocks, m, part, part)
     for s in range(blocks.shape[0]):
         out_gain[:, s * part : (s + 1) * part] = blocks[s, :, :part].astype(WIDE)
 
-    @pl.when(ids[0] == 0)
-    def _():
-        out_spread[...] = mm_bt(m[...], first[...]) + near[...]
-
-    @pl.when(ids[0] == 1)
-    def _():
-        out_spread[...] = mm_bt(m[...], second[...]) + near[...]
+    @pl.when(ids[3] % 2 == 0)
+    def _():
+        m[...] = mm_bt(m[...], following[...]).astype(LOW)
+
+    @pl.when(ids[0] == 0)
+    def _():
+        out_spread[...] = mm_bt(m[...], pair[...]) + near[...]
+
+    @pl.when(ids[0] == 1)
+    def _():
+        out_spread[...] = mm_bt(m[...], e1[...]) + near[...]
 
 
 def columns(ref, side, chunk, width):
@@ -257,55 +262,64 @@
     return ref.at[:, pl.ds(pl.multiple_of(start, width), width)]
 
 
-def start_kernel(chunk, ids, both, got, offset, p_ref, now, keep, sem):
+def start_kernel(chunk, ids, e0, got, offset, p, own, keep, sem):
     copy = pltpu.make_async_copy(columns(offset, ids[0], chunk, keep.shape[1]), keep, sem)
     copy.start()
 
     @pl.when(ids[0] == 0)
     def _():
-        p_ref[...] = mm(both[0], got[...])
+        p[...] = mm(e0[...], got[...])
 
     copy.wait()
 
     @pl.when(ids[0] == 0)
     def _():
-        now[...] = (p_ref[...] + keep[...]).astype(LOW)
-
-    @pl.when(ids[0] == 1)
-    def _():
-        p = mm(both[0], keep[...].astype(LOW))
-        p_ref[...] = p
-        now[...] = (p + got[...].astype(WIDE)).astype(LOW)
+        own[...] = (p[...] + keep[...]).astype(LOW)
+
+    @pl.when(ids[0] == 1)
+    def _():
+        p[...] = mm(e0[...], keep[...].astype(LOW))
+        own[...] = (p[...] + got[...].astype(WIDE)).astype(LOW)
 
 
 def hop_kernel(ids, pair, got, own, now):
     now[...] = (mm(pair[...], got[...]) + own[...].astype(WIDE)).astype(LOW)
 
 
-def last_kernel(chunk, ids, pair, both, got_a, got_b, got_c, p_ref, offset, *refs):
+def last_kernel(chunk, ids, pair, e1, p, got_a, got_b, got_c, offset, *refs):
     out, send, keep, far, sems = refs[-5:]
     width = keep.shape[1]
     copy = pltpu.make_async_copy(columns(offset, ids[0], chunk, width), keep, sems.at[0])
     copy.start()
-    far[...] = got_a[...] + got_b[...] + got_c[...]
-
-    @pl.when(ids[0] == 0)
-    def _():
-        send[...] = mm(both[1], far[...]).astype(LOW)
-
-    @pl.when(ids[0] == 1)
-    def _():
-        send[...] = (mm(pair[...], far[...]) + p_ref[...]).astype(LOW)
+    for z, got in ((2, got_a), (1, got_b), (0, got_c)):
+
+        @pl.when(ids[3] == z)
+        def _():
+            load = pltpu.make_async_copy(got, far, sems.at[1])
+            load.start()
+            load.wait()
+
+    @pl.when(ids[3] == 3)
+    def _():
+        far[...] = jnp.zeros_like(far)
+
+    @pl.when(ids[0] == 0)
+    def _():
+        send[...] = mm(e1[...], far[...]).astype(LOW)
+
+    @pl.when(ids[0] == 1)
+    def _():
+        send[...] = (mm(pair[...], far[...]) + p[...]).astype(LOW)
 
     copy.wait()
 
     @pl.when(ids[0] == 0)
     def _():
-        keep[...] = mm(pair[...], far[...]) + p_ref[...] + keep[...]
-
-    @pl.when(ids[0] == 1)
-    def _():
-        keep[...] = mm(both[1], far[...]) + keep[...]
+        keep[...] = mm(pair[...], far[...]) + p[...] + keep[...]
+
+    @pl.when(ids[0] == 1)
+    def _():
+        keep[...] = mm(e1[...], far[...]) + keep[...]
 
     copy = pltpu.make_async_copy(keep, columns(out, ids[0], chunk, width), sems.at[1])
     copy.start()
@@ -354,7 +368,7 @@
     pieces = [e_low, None, e_y, None, e_x, None, e_xy, None]
     for i in range(0, 8, 2):
         pieces[i + 1] = swap(pieces[i], "c")
-    offset = in_hbm(offsets[0])
+    offset, spread = in_hbm(offsets[0]), in_hbm(spreads)
 
     keep = pltpu.VMEM((size_d, width), WIDE)
     column = pltpu.VMEM((size_d, width), LOW)
@@ -362,23 +376,22 @@
 
     def start(i):
         return order.call(
-            functools.partial(start_kernel, i), [both, g_got[i], offset],
-            [held(size_d, width, dtype=WIDE), low(size_d, width)], 8,
-            far_in=(2,), scratch=[keep, pltpu.SemaphoreType.DMA(())],
+            functools.partial(start_kernel, i), [in_hbm(e0), g_got[i], offset], [hbm(size_d, width, dtype=WIDE), hbm(size_d, width)],
+            12, far_in=(2,), scratch=[keep, pltpu.SemaphoreType.DMA(())],
         )
 
     def down(value, source):
         return lax.ppermute(value, "z", [(source, source - 1)])
 
-    def hop(i, got):
-        return order.call(hop_kernel, [a_e, got, own[i]], [low(size_d, width)], 8)[0]
-
-    def last(i, into):
+    def hop(got, own):
+        return order.call(hop_kernel, [pair, got, in_hbm(own)], [hbm(size_d, width)], 8)[0]
+
+    def last(i, p, gots, into):
         extra = [] if into is None else [into]
         return order.call(
-            functools.partial(last_kernel, i), [a_e, both] + gots[i] + [p[i], offset] + extra,
-            [wide(*offset.shape), low(size_d, width)], 12,
-            far_in=(6, 7), far_out=(0,), aliases={7: 0} if extra else {},
+            functools.partial(last_kernel, i), [pair, in_hbm(e1), in_hbm(p), *gots, offset] + extra,
+            [wide(*offset.shape), hbm(size_d, width)], 14,
+            far_in=(3, 4, 5, 6, 7), far_out=(0,), aliases={7: 0} if extra else {},
             scratch=[keep, column, pltpu.SemaphoreType.DMA((2,))],
         )
 
@@ -388,58 +401,59 @@
             far_in=(1, 2), far_out=(0,), aliases={2: 0}, scratch=[keep, pltpu.SemaphoreType.DMA((2,))],
         )[0]
 
-    both, a_e, quarter = order.call(
-        pair_kernel, [in_hbm(piece) for piece in pieces],
-        [held(2, size_d, size_d), held(size_d, size_d), low(rows, size_d)], 16,
-        far_in=range(8), scratch=[pltpu.SemaphoreType.DMA((8,))],
+    e0, e1, pair, quarter = order.call(
+        pair_kernel, pieces,
+        [hbm(size_d, size_d), hbm(size_d, size_d), pltpu.VMEM((size_d, size_d), LOW), hbm(rows, size_d)], 14,
+        far_in=range(8), far_out=(0, 1),
+        scratch=[pltpu.VMEM((2, size_d, size_d), LOW), pltpu.SemaphoreType.DMA((8,))],
     )
     quarter = lax.ppermute(quarter, "z", level)
     quarter_y = swap(quarter, "y")
     quarters = [quarter, swap(quarter, "c"), quarter_y, swap(quarter_y, "c")]
-    (m,) = order.call(spread_kernel, [both, l_low, l_got], [low(8, rows, part)], 12)
+    (m,) = order.call(spread_kernel, [in_hbm(e0), l_low, l_got], [hbm(8, rows, part)], 8)
     m = exchange(m)
-    p, own, gots = [None] * chunks, [None] * chunks, [[] for _ in range(chunks)]
-    p[0], own[0] = start(0)
-    gots[0].append(down(own[0], 3))
-    prod, a_l, a_low = order.call(
-        spread_start_kernel, [m, both, spreads, l_got],
-        [held(rows, size_d, dtype=WIDE), held(size_d, part, dtype=WIDE), low(size_d, part)], 14, scratch=[slab_rows],
+    p0, own0 = start(0)
+    gots0 = [down(own0, 3)]
+    prod, slab, a_low = order.call(
+        spread_start_kernel, [in_hbm(e0), m, spread, l_got],
+        [hbm(rows, size_d, dtype=WIDE), hbm(size_d, part, dtype=WIDE), hbm(size_d, part)], 12, scratch=[slab_rows],
     )
     l_next = lax.ppermute(a_low, "z", level)
-    p[1], own[1] = start(1)
-    gots[1].append(down(own[1], 3))
-    gots[0].append(down(hop(0, gots[0][0]), 2))
-
-    m, near = order.call(spread_hop_kernel, [a_e, both, l_next], [low(size_d, part), low(8, rows, part)], 12)
+    p1, own1 = start(1)
+    gots1 = [down(own1, 3)]
+    gots0.append(down(hop(gots0[0], own0), 2))
+
+    m, near = order.call(spread_hop_kernel, [pair, in_hbm(e1), l_next], [hbm(size_d, part), hbm(8, rows, part)], 10)
     m = exchange(m.reshape(8, part, part))
     near = exchange(near)
-    gots[1].append(down(hop(1, gots[1][0]), 2))
+    gots1.append(down(hop(gots1[0], own1), 2))
     (b_l,) = order.call(
-        spread_next_kernel, [m, a_e, a_l], [low(size_d, part)], 8, scratch=[pltpu.VMEM((part, size_d), LOW)]
+        spread_next_kernel, [pair, in_hbm(slab), m], [hbm(size_d, part)], 8, scratch=[pltpu.VMEM((part, size_d), LOW)]
     )
     l_far = lax.ppermute(b_l, "z", [(2, 1)]), lax.ppermute(b_l, "z", [(2, 0)])
-    gots[0].append(down(hop(0, gots[0][1]), 1))
-    c0_e, c1_e, e_slab = order.call(
-        compose_kernel, [a_e, both, *quarters], [held(size_d, size_d), held(size_d, size_d), low(size_d, part)], 14,
-        scratch=[pltpu.VMEM((size_d, size_d), LOW)],
+    following, e_slab = order.call(
+        next_gain_kernel, [pair, *quarters], [hbm(size_d, size_d), hbm(size_d, part)], 10,
+        far_in=(1, 2, 3, 4), scratch=[pltpu.SemaphoreType.DMA((4,))],
     )
     e_far = lax.ppermute(e_slab, "z", [(2, 1)]), lax.ppermute(e_slab, "z", [(2, 0)])
-    gots[1].append(down(hop(1, gots[1][1]), 1))
+    gots0.append(down(hop(gots0[1], own0), 1))
     (near,) = order.call(
-        near_kernel, [near, a_e, both, prod, spreads], [held(rows, size_d, dtype=WIDE)], 12, scratch=[slab_rows]
-    )
-
-    out_offset, other0 = last(0, None)
+        near_kernel, [pair, in_hbm(e1), in_hbm(prod), near, spread], [hbm(rows, size_d, dtype=WIDE)], 12, scratch=[slab_rows]
+    )
+    gots1.append(down(hop(gots1[1], own1), 1))
+
+    out_offset, other0 = last(0, p0, gots0, None)
     other0 = swap(other0, "x")
     (m,) = order.call(
-        far_kernel, [c0_e, c1_e, *e_far, *l_far], [low(8, rows, rows)], 12, scratch=[pltpu.VMEM((size_d, rows), LOW)]
+        far_kernel, [pair, in_hbm(e1), in_hbm(following), *e_far, *l_far], [hbm(8, rows, rows)], 14,
+        scratch=[pltpu.VMEM((size_d, rows), LOW)],
     )
     m = exchange(m)
-    out_offset, other1 = last(1, out_offset)
+    out_offset, other1 = last(1, p1, gots1, out_offset)
     other1 = swap(other1, "x")
     out_offset = add(0, other0, out_offset)
     out_gain, out_spread = order.call(
-        end_kernel, [m, c0_e, c1_e, near], [wide(rows, size_d), wide(rows, size_d)], 14, scratch=[slab_rows]
+        end_kernel, [pair, in_hbm(e1), in_hbm(following), in_hbm(near), m], [wide(rows, size_d), wide(rows, size_d)], 14, scratch=[slab_rows]
     )
     out_offset = add(1, other1, out_offset)
     return (out_gain[None], out_spread[None], out_offset[None])

time: 201 us -> 205 us (1.020)
  local copies, waits for them, and re-layouts: 35 us -> 11 us
  Pallas kernels: 60.2 us -> 74.5 us
  waiting for transfers between devices: 52.3 us -> 65.6 us
    unnamed x70 -> x24, local copies, waits for them, and re-layouts: 31.6 us -> 8.39 us
    pallas_call x19, Pallas kernels: 60.2 us -> 74.5 us  [call(): pl.pallas_call(body, in_specs=[SMEM, ANY] + [ANY if i in far_in else VMEM...]
    ppermute x15, waiting for transfers between devices: 34.2 us -> 44.6 us  [swap(): return lax.ppermute(value, axis, [(0, 1), (1, 0)])]
    all_to_all x4, waiting for transfers between devices: 2.19 us -> 5.81 us  [exchange(): return lax.all_to_all(blocks, GROUP, 0, 0)]
  transfers between devices with their start and end apart: 31 -> 31, of which waited for: 9 -> 13; matrix products, arithmetic and copies ran while one was open for 2% -> 2% of each run, Pallas kernels for 28% -> 35%
where the time goes in v7:
time: 205 us; the launch traced here: 202 us
  Pallas kernels  74.5 us (36%)
  waiting for transfers between devices  65.6 us (32%)
  starting transfers between devices  47.1 us (23%)
  local copies, waits for them, and re-layouts  11 us (5%)
  other arithmetic  2.73 us (1%)
    pallas_call x19, Pallas kernels, call(): pl.pallas_call(body, in_specs=[SMEM, ANY] + [ANY if i in far_in else VMEM...  74.5 us
    ppermute x15, waiting for transfers between devices, swap(): return lax.ppermute(value, axis, [(0, 1), (1, 0)])  44.6 us
    all_to_all x4, starting transfers between devices, exchange(): return lax.all_to_all(blocks, GROUP, 0, 0)  14.4 us
    ppermute x15, starting transfers between devices, swap(): return lax.ppermute(value, axis, [(0, 1), (1, 0)])  12.9 us
    ppermute x1, waiting for transfers between devices, suffix(): l_next = lax.ppermute(a_low, 'z', level)  11.1 us
    ppermute x6, starting transfers between devices, down(): return lax.ppermute(value, 'z', [(source, source - 1)])  9.96 us
    unnamed x24, local copies, waits for them, and re-layouts  8.39 us
    all_to_all x4, waiting for transfers between devices, exchange(): return lax.all_to_all(blocks, GROUP, 0, 0)  5.81 us
  transfers between devices with their start and end apart: 31, of which 13 were waited for; matrix products, arithmetic and copies ran while one was open for 2% of the time, Pallas kernels for 35%

profile of v7, /device:TPU:16, one launch (start us, length us, event | category | flops | bytes accessed | tf_op | source)
XLA Modules:
  0.0 202.1 jit_solution(2165041521346342418)
XLA Ops:
  1.9 1.6 collective-permute-start.3
  3.5 1.5 collective-permute-start.1
  6.3 2.6 %fusion.1 = (bf16[1024,256]{1,0:T(8,128)(2,1)}, bf16[1024,256]{1,0:T(8,128)(2,1)}) fusion(f32[1,1024,1024]{2,1,0:T(8,128)} %param.5, s32[]{:T(128)S(6)} %select_n.11, s32[]{:T(128)S(6)} %select_n.10), kind=kLoop, calls=%fused_computation.3 | loop fusion | bytes 2097160 | tf_op jit(solution)/shard_map/convert_element_type | solution.py:359
  9.0 6.7 %collective-permute-done.3.refs_4_ = bf16[256,1024]{1,0:T(8,128)(2,1)S(1)} collective-permute-done((bf16[256,1024]{1,0:T(8,128)(2,1)S(1)}, bf16[256,1024]{1,0:T(8,128)(2,1)S(1)}, u32[]{:S(2)}, u32[]{:S(2)}) %collective-permute-start.3) | collective-permute-done | bytes 524320 | tf_op jit(solution)/shard_map/ppermute | solution.py:51
  15.7 1.5 collective-permute-start.5
  18.5 10.0 %collective-permute-done.5.refs_6_ = bf16[256,1024]{1,0:T(8,128)(2,1)S(1)} collective-permute-done((bf16[256,1024]{1,0:T(8,128)(2,1)S(1)}, bf16[256,1024]{1,0:T(8,128)(2,1)S(1)}, u32[]{:S(2)}, u32[]{:S(2)}) %collective-permute-start.5) | collective-permute-done | bytes 524320 | tf_op jit(solution)/shard_map/ppermute | solution.py:51
  29.3 1.5 collective-permute-start.8
  36.6 5.1 %shard_map.58 = (bf16[1024,1024]{1,0:T(8,128)(2,1)}, bf16[1024,1024]{1,0:T(8,128)(2,1)}, bf16[1024,1024]{1,0:T(8,128)(2,1)S(1)}, bf16[256,1024]{1,0:T(8,128)(2,1)}, s32[8,128]{1,0:T(8,128)S(1)}) custom-call(s32[4]{0:T(128)S(1)} %pad_add_fusion.ids, s32[8,128]{1,0:T(8,128)S(1)} %broadcast_in_dim.12.token, ...), custom_call_target="tpu_custom_call", output_to_operand_aliasing={{4}: (1, {})} | custom-call | flops 1 | bytes 1 | tf_op jit(solution)/shard_map/pallas_call | solution.py:93
  43.9 1.5 collective-permute-start.9
  45.5 6.8 %collective-permute-done.7.refs_2_.refs_3_ = bf16[128,1024]{1,0:T(8,128)(2,1)S(1)} collective-permute-done((bf16[128,1024]{1,0:T(8,128)(2,1)S(1)}, bf16[128,1024]{1,0:T(8,128)(2,1)S(1)}, u32[]{:S(2)}, u32[]{:S(2)}) %collective-permute-start.7) | collective-permute-done | bytes 262176 | tf_op jit(solution)/shard_map/ppermute | solution.py:51
  52.2 3.1 %shard_map.59 = (bf16[8,256,128]{2,1,0:T(8,128)(2,1)}, s32[8,128]{1,0:T(8,128)S(1)}) custom-call(s32[4]{0:T(128)S(1)} %pad_add_fusion.ids, s32[8,128]{1,0:T(8,128)S(1)} %get-tuple-element.58.token, bf16[1024,1024]{1,0:T(8,128)(2,1)} %get-tuple-element.59.refs_0_, ...), custom_call_target="tpu_custom_call", output_to_operand_aliasing={{1}: (1, {})} | custom-call | flops 1 | bytes 1 | tf_op jit(solution)/shard_map/pallas_call | solution.py:93
  55.4 3.5 %all-to-all-start = ((bf16[8,256,128]{2,1,0:T(8,128)(2,1)}), bf16[8,256,128]{2,1,0:T(8,128)(2,1)S(1)}, u32[]{:S(2)}, u32[]{:S(2)}) async-start(bf16[8,256,128]{2,1,0:T(8,128)(2,1)} %get-tuple-element.65), calls=%async_computation | async-start | bytes 1048576 | tf_op jit(solution)/shard_map/all_to_all | solution.py:66
  58.9 4.2 %shard_map.60 = (f32[1024,256]{1,0:T(8,128)}, bf16[1024,256]{1,0:T(8,128)(2,1)}, s32[8,128]{1,0:T(8,128)S(1)}) custom-call(s32[4]{0:T(128)S(1)} %pad_add_fusion.ids, s32[8,128]{1,0:T(8,128)S(1)} %get-tuple-element.61.token, bf16[1024,1024]{1,0:T(8,128)(2,1)} %get-tuple-element.59.refs_0_, ...), custom_call_target="tpu_custom_call", output_to_operand_aliasing={{2}: (1, {})} | custom-call | flops 1 | bytes 1 | tf_op jit(solution)/shard_map/pallas_call | solution.py:93
  63.1 2.0 collective-permute-start.15
  66.4 2.4 %all-to-all-done.refs_1_ = bf16[8,256,128]{2,1,0:T(8,128)(2,1)S(1)} async-done(((bf16[8,256,128]{2,1,0:T(8,128)(2,1)}), bf16[8,256,128]{2,1,0:T(8,128)(2,1)S(1)}, u32[]{:S(2)}, u32[]{:S(2)}) %all-to-all-start) | async-done | bytes 524320 | tf_op jit(solution)/shard_map/all_to_all | solution.py:66
  68.7 4.0 %shard_map.61 = (f32[256,1024]{1,0:T(8,128)}, f32[1024,128]{1,0:T(8,128)}, bf16[1024,128]{1,0:T(8,128)(2,1)}, s32[8,128]{1,0:T(8,128)S(1)}) custom-call(s32[4]{0:T(128)S(1)} %pad_add_fusion.ids, s32[8,128]{1,0:T(8,128)S(1)} %get-tuple-element.64.token, bf16[1024,1024]{1,0:T(8,128)(2,1)} %get-tuple-element.59.refs_0_, ...), custom_call_target="tpu_custom_call", output_to_operand_aliasing={{3}: (1, {})} | custom-call | flops 1 | bytes 1 | tf_op jit(solution)/shard_map/pallas_call | solution.py:93
  72.8 4.2 %shard_map.62 = (f32[1024,256]{1,0:T(8,128)}, bf16[1024,256]{1,0:T(8,128)(2,1)}, s32[8,128]{1,0:T(8,128)S(1)}) custom-call(s32[4]{0:T(128)S(1)} %pad_add_fusion.ids, s32[8,128]{1,0:T(8,128)S(1)} %get-tuple-element.66.token, bf16[1024,1024]{1,0:T(8,128)(2,1)} %get-tuple-element.59.refs_0_, ...), custom_call_target="tpu_custom_call", output_to_operand_aliasing={{2}: (1, {})} | custom-call | flops 1 | bytes 1 | tf_op jit(solution)/shard_map/pallas_call | solution.py:93
  79.6 2.4 %collective-permute-done.10.refs_1_.refs_3_ = bf16[1024,256]{1,0:T(8,128)(2,1)S(1)} collective-permute-done((bf16[1024,256]{1,0:T(8,128)(2,1)}, bf16[1024,256]{1,0:T(8,128)(2,1)S(1)}, u32[]{:S(2)}, u32[]{:S(2)}) %collective-permute-start.10) | collective-permute-done | bytes 524320 | tf_op jit(solution)/shard_map/ppermute | solution.py:384
  81.9 2.6 %shard_map.63 = (bf16[1024,256]{1,0:T(8,128)(2,1)}, s32[8,128]{1,0:T(8,128)S(1)}) custom-call(s32[4]{0:T(128)S(1)} %pad_add_fusion.ids, s32[8,128]{1,0:T(8,128)S(1)} %get-tuple-element.68.token, bf16[1024,1024]{1,0:T(8,128)(2,1)S(1)} %get-tuple-element.69.refs_0_, ...), custom_call_target="tpu_custom_call", output_to_operand_aliasing={{1}: (1, {})} | custom-call | flops 1 | bytes 1 | tf_op jit(solution)/shard_map/pallas_call | solution.py:93
  84.5 2.4 %collective-permute-start.17 = (bf16[1024,256]{1,0:T(8,128)(2,1)}, bf16[1024,256]{1,0:T(8,128)(2,1)}, u32[]{:S(2)}, u32[]{:S(2)}) collective-permute-start(bf16[1024,256]{1,0:T(8,128)(2,1)} %get-tuple-element.82), channel_id=1, source_target_pairs={{16,8},{17,9},{18,10},{19,11},{20,12},{21,13},{22,14},{23,15}} | collective-permute-start | bytes 1572872 | tf_op jit(solution)/shard_map/ppermute | solution.py:384
  88.2 11.1 %collective-permute-done.11.refs_2_ = bf16[1024,128]{1,0:T(8,128)(2,1)S(1)} collective-permute-done((bf16[1024,128]{1,0:T(8,128)(2,1)S(1)}, bf16[1024,128]{1,0:T(8,128)(2,1)S(1)}, u32[]{:S(2)}, u32[]{:S(2)}) %collective-permute-start.11) | collective-permute-done | bytes 262176 | tf_op jit(solution)/shard_map/ppermute | solution.py:421
  99.2 3.7 %shard_map.64 = (bf16[1024,128]{1,0:T(8,128)(2,1)}, bf16[8,256,128]{2,1,0:T(8,128)(2,1)}, s32[8,128]{1,0:T(8,128)S(1)}) custom-call(s32[4]{0:T(128)S(1)} %pad_add_fusion.ids, s32[8,128]{1,0:T(8,128)S(1)} %get-tuple-element.71.token, bf16[1024,1024]{1,0:T(8,128)(2,1)S(1)} %get-tuple-element.69.refs_0_, ...), custom_call_target="tpu_custom_call", output_to_operand_aliasing={{2}: (1, {})} | custom-call | flops 1 | bytes 1 | tf_op jit(solution)/shard_map/pallas_call | solution.py:93
  103.0 3.4 %all-to-all-start.1 = ((bf16[8,128,128]{2,1,0:T(8,128)(2,1)}), bf16[8,128,128]{2,1,0:T(8,128)(2,1)S(1)}, u32[]{:S(2)}, u32[]{:S(2)}) async-start(bf16[8,128,128]{2,1,0:T(8,128)(2,1)} %bitcast.26), calls=%async_computation.1 | async-start | bytes 524288 | tf_op jit(solution)/shard_map/all_to_all | solution.py:66
  106.4 2.7 %shard_map.65 = (bf16[1024,256]{1,0:T(8,128)(2,1)}, s32[8,128]{1,0:T(8,128)S(1)}) custom-call(s32[4]{0:T(128)S(1)} %pad_add_fusion.ids, s32[8,128]{1,0:T(8,128)S(1)} %get-tuple-element.74.token, bf16[1024,1024]{1,0:T(8,128)(2,1)S(1)} %get-tuple-element.69.refs_0_, ...), custom_call_target="tpu_custom_call", output_to_operand_aliasing={{1}: (1, {})} | custom-call | flops 1 | bytes 1 | tf_op jit(solution)/shard_map/pallas_call | solution.py:93
  109.1 2.1 %collective-permute-start.18 = (bf16[1024,256]{1,0:T(8,128)(2,1)}, bf16[1024,256]{1,0:T(8,128)(2,1)}, u32[]{:S(2)}, u32[]{:S(2)}) collective-permute-start(bf16[1024,256]{1,0:T(8,128)(2,1)} %get-tuple-element.87), channel_id=1, source_target_pairs={{16,8},{17,9},{18,10},{19,11},{20,12},{21,13},{22,14},{23,15}} | collective-permute-start | bytes 1572872 | tf_op jit(solution)/shard_map/ppermute | solution.py:384
  111.2 1.5 all-to-all-done.1.refs_2_
  112.8 2.5 %shard_map.66 = (bf16[1024,128]{1,0:T(8,128)(2,1)}, s32[8,128]{1,0:T(8,128)S(1)}) custom-call(s32[4]{0:T(128)S(1)} %pad_add_fusion.ids, s32[8,128]{1,0:T(8,128)S(1)} %get-tuple-element.76.token, bf16[1024,1024]{1,0:T(8,128)(2,1)S(1)} %get-tuple-element.69.refs_0_, f32[1024,128]{1,0:T(8,128)} %get-tuple-element.77.refs_1_, ...), custom_call_target="tpu_custom_call", output_to_operand_aliasing={{1}: (1, {})} | custom-call | flops 1 | bytes 1 | tf_op jit(solution)/shard_map/pallas_call | solution.py:93
  115.2 4.1 %shard_map.67 = (bf16[1024,1024]{1,0:T(8,128)(2,1)}, bf16[1024,128]{1,0:T(8,128)(2,1)}, s32[8,128]{1,0:T(8,128)S(1)}) custom-call(s32[4]{0:T(128)S(1)} %pad_add_fusion.ids, s32[8,128]{1,0:T(8,128)S(1)} %get-tuple-element.79.token, bf16[1024,1024]{1,0:T(8,128)(2,1)S(1)} %get-tuple-element.69.refs_0_, ...), custom_call_target="tpu_custom_call", output_to_operand_aliasing={{2}: (1, {})} | custom-call | flops 1 | bytes 1 | tf_op jit(solution)/shard_map/pallas_call | solution.py:93
  119.4 2.7 %shard_map.68 = (bf16[1024,256]{1,0:T(8,128)(2,1)}, s32[8,128]{1,0:T(8,128)S(1)}) custom-call(s32[4]{0:T(128)S(1)} %pad_add_fusion.ids, s32[8,128]{1,0:T(8,128)S(1)} %get-tuple-element.81.token, bf16[1024,1024]{1,0:T(8,128)(2,1)S(1)} %get-tuple-element.69.refs_0_, ...), custom_call_target="tpu_custom_call", output_to_operand_aliasing={{1}: (1, {})} | custom-call | flops 1 | bytes 1 | tf_op jit(solution)/shard_map/pallas_call | solution.py:93
  122.1 1.5 collective-permute-start.19
  123.6 3.7 %all-to-all-start.2 = ((bf16[8,256,128]{2,1,0:T(8,128)(2,1)}), bf16[8,256,128]{2,1,0:T(8,128)(2,1)S(1)}, u32[]{:S(2)}, u32[]{:S(2)}) async-start(bf16[8,256,128]{2,1,0:T(8,128)(2,1)} %get-tuple-element.85), calls=%async_computation.2 | async-start | bytes 1048576 | tf_op jit(solution)/shard_map/all_to_all | solution.py:66
  128.5 2.0 collective-permute-start.22
  130.5 2.0 collective-permute-start.21
  132.6 2.0 collective-permute-start.20
  134.5 1.9 all-to-all-done.2.refs_3_
  136.4 4.1 %shard_map.69 = (f32[256,1024]{1,0:T(8,128)}, s32[8,128]{1,0:T(8,128)S(1)}) custom-call(s32[4]{0:T(128)S(1)} %pad_add_fusion.ids, s32[8,128]{1,0:T(8,128)S(1)} %get-tuple-element.83.token, bf16[1024,1024]{1,0:T(8,128)(2,1)S(1)} %get-tuple-element.69.refs_0_, bf16[1024,1024]{1,0:T(8,128)(2,1)} %get-tuple-element.72.refs_1_, ...), custom_call_target="tpu_custom_call", output_to_operand_aliasing={{1}: (1, {})} | custom-call | flops 1 | bytes 1 | tf_op jit(solution)/shard_map/pallas_call | solution.py:93
  140.5 2.7 %shard_map.70 = (bf16[1024,256]{1,0:T(8,128)(2,1)}, s32[8,128]{1,0:T(8,128)S(1)}) custom-call(s32[4]{0:T(128)S(1)} %pad_add_fusion.ids, s32[8,128]{1,0:T(8,128)S(1)} %get-tuple-element.86.token, bf16[1024,1024]{1,0:T(8,128)(2,1)S(1)} %get-tuple-element.69.refs_0_, ...), custom_call_target="tpu_custom_call", output_to_operand_aliasing={{1}: (1, {})} | custom-call | flops 1 | bytes 1 | tf_op jit(solution)/shard_map/pallas_call | solution.py:93
  144.7 5.7 %shard_map.71 = (f32[1024,1024]{1,0:T(8,128)}, bf16[1024,256]{1,0:T(8,128)(2,1)}, s32[8,128]{1,0:T(8,128)S(1)}) custom-call(s32[4]{0:T(128)S(1)} %pad_add_fusion.ids, s32[8,128]{1,0:T(8,128)S(1)} %get-tuple-element.88.token, bf16[1024,1024]{1,0:T(8,128)(2,1)S(1)} %get-tuple-element.69.refs_0_, ...), custom_call_target="tpu_custom_call", output_to_operand_aliasing={{2}: (1, {})} | custom-call | flops 1 | bytes 1 | tf_op jit(solution)/shard_map/pallas_call | solution.py:93
  150.4 1.7 collective-permute-done.20.refs_3_
  152.2 5.5 %shard_map.72 = (bf16[8,256,256]{2,1,0:T(8,128)(2,1)}, s32[8,128]{1,0:T(8,128)S(1)}) custom-call(s32[4]{0:T(128)S(1)} %pad_add_fusion.ids, s32[8,128]{1,0:T(8,128)S(1)} %get-tuple-element.91.token, bf16[1024,1024]{1,0:T(8,128)(2,1)S(1)} %get-tuple-element.69.refs_0_, bf16[1024,1024]{1,0:T(8,128)(2,1)} %get-tuple-element.72.refs_1_, ...), custom_call_target="tpu_custom_call", output_to_operand_aliasing={{1}: (1, {})} | custom-call | flops 1 | bytes 1 | tf_op jit(solution)/shard_map/pallas_call | solution.py:93
  157.7 3.8 %all-to-all-start.3 = ((bf16[8,256,256]{2,1,0:T(8,128)(2,1)}), bf16[8,256,256]{2,1,0:T(8,128)(2,1)S(1)}, u32[]{:S(2)}, u32[]{:S(2)}) async-start(bf16[8,256,256]{2,1,0:T(8,128)(2,1)} %get-tuple-element.104), calls=%async_computation.3 | async-start | bytes 2097152 | tf_op jit(solution)/shard_map/all_to_all | solution.py:66
  161.5 2.0 %collective-permute-start.25 = (bf16[1024,256]{1,0:T(8,128)(2,1)}, bf16[1024,256]{1,0:T(8,128)(2,1)S(1)}, u32[]{:S(2)}, u32[]{:S(2)}) collective-permute-start(bf16[1024,256]{1,0:T(8,128)(2,1)} %get-tuple-element.100), channel_id=1, source_target_pairs={{0,4},{4,0},{1,5},{5,1},{2,6},{6,2},{3,7},{7,3},{8,12},{12,8},{9,1... | collective-permute-start | bytes 1572872 | tf_op jit(solution)/shard_map/ppermute | solution.py:51
  164.6 5.7 %shard_map.73 = (f32[1024,1024]{1,0:T(8,128)}, bf16[1024,256]{1,0:T(8,128)(2,1)}, s32[8,128]{1,0:T(8,128)S(1)}) custom-call(s32[4]{0:T(128)S(1)} %pad_add_fusion.ids, s32[8,128]{1,0:T(8,128)S(1)} %get-tuple-element.95.token, bf16[1024,1024]{1,0:T(8,128)(2,1)S(1)} %get-tuple-element.69.refs_0_, ...), custom_call_target="tpu_custom_call", output_to_operand_aliasing={{2}: (1, {}), {0}: (9, {})} | custom-call | flops 1 | bytes 1 | tf_op jit(solution)/shard_map/pallas_call | solution.py:93
  170.3 17.4 %collective-permute-done.25.refs_0_ = bf16[1024,256]{1,0:T(8,128)(2,1)S(1)} collective-permute-done((bf16[1024,256]{1,0:T(8,128)(2,1)}, bf16[1024,256]{1,0:T(8,128)(2,1)S(1)}, u32[]{:S(2)}, u32[]{:S(2)}) %collective-permute-start.25) | collective-permute-done | bytes 524320 | tf_op jit(solution)/shard_map/ppermute | solution.py:51
  187.7 2.9 %shard_map.74 = (f32[1024,1024]{1,0:T(8,128)}, s32[8,128]{1,0:T(8,128)S(1)}) custom-call(s32[4]{0:T(128)S(1)} %pad_add_fusion.ids, s32[8,128]{1,0:T(8,128)S(1)} %get-tuple-element.99.token, bf16[1024,256]{1,0:T(8,128)(2,1)S(1)} %collective-permute-done.25.refs_0_, f32[1024,1024]{1,0:T(8,128)} %bitcast.23, ...), custom_call_target="tpu_custom_call", output_to_operand_aliasing={{1}: (1, {}), {0}: (4, {})} | custom-call | flops 1 | bytes 1 | tf_op jit(solution)/shard_map/pallas_call | solution.py:93
  190.6 5.6 %shard_map.75 = (f32[256,1024]{1,0:T(8,128)}, f32[256,1024]{1,0:T(8,128)}, s32[8,128]{1,0:T(8,128)S(1)}) custom-call(s32[4]{0:T(128)S(1)} %pad_add_fusion.ids, s32[8,128]{1,0:T(8,128)S(1)} %get-tuple-element.102.token, bf16[1024,1024]{1,0:T(8,128)(2,1)S(1)} %get-tuple-element.69.refs_0_, ...), custom_call_target="tpu_custom_call", output_to_operand_aliasing={{2}: (1, {})} | custom-call | flops 1 | bytes 1 | tf_op jit(solution)/shard_map/pallas_call | solution.py:93
  196.2 2.4 %collective-permute-done.26.refs_0_ = bf16[1024,256]{1,0:T(8,128)(2,1)} collective-permute-done((bf16[1024,256]{1,0:T(8,128)(2,1)}, bf16[1024,256]{1,0:T(8,128)(2,1)}, u32[]{:S(2)}, u32[]{:S(2)}) %collective-permute-start.26) | collective-permute-done | bytes 524320 | tf_op jit(solution)/shard_map/ppermute | solution.py:51
  198.6 3.4 %shard_map.76 = (f32[1024,1024]{1,0:T(8,128)}, s32[8,128]{1,0:T(8,128)S(1)}) custom-call(s32[4]{0:T(128)S(1)} %pad_add_fusion.ids, s32[8,128]{1,0:T(8,128)S(1)} %get-tuple-element.107.token, bf16[1024,256]{1,0:T(8,128)(2,1)} %collective-permute-done.26.refs_0_, f32[1024,1024]{1,0:T(8,128)} %bitcast.24, ...), custom_call_target="tpu_custom_call", output_to_operand_aliasing={{1}: (1, {}), {0}: (4, {})} | custom-call | flops 1 | bytes 1 | tf_op jit(solution)/shard_map/pallas_call | solution.py:93
  (64 shorter events, 21.8 us)
Async XLA Ops:
  1.9 13.7 %collective-permute-start.3 = (bf16[256,1024]{1,0:T(8,128)(2,1)S(1)}, bf16[256,1024]{1,0:T(8,128)(2,1)S(1)}, u32[]{:S(2)}, u32[]{:S(2)}) collective-permute-start(bf16[256,1024]{1,0:T(8,128)(2,1)S(1)} %convert_bitcast_fusion.refs_0_), channel_id=1, source_target_pairs={{0,4},{4,0},{1,5},{5,1},{2,6},{6,2},{3,7},{7,3},{8,12},{12,8},{9,1... | collective-permute-start | bytes 1572872 | tf_op jit(solution)/shard_map/ppermute | solution.py:51
  3.5 14.2 %collective-permute-start.1 = (bf16[256,1024]{1,0:T(8,128)(2,1)S(1)}, bf16[256,1024]{1,0:T(8,128)(2,1)S(1)}, u32[]{:S(2)}, u32[]{:S(2)}) collective-permute-start(bf16[256,1024]{1,0:T(8,128)(2,1)S(1)} %convert_bitcast_fusion.refs_0_), channel_id=1, source_target_pairs={{0,2},{2,0},{1,3},{3,1},{4,6},{6,4},{5,7},{7,5},{8,10},{10,8},{9,1... | collective-permute-start | bytes 1572872 | tf_op jit(solution)/shard_map/ppermute | solution.py:51
  15.7 12.8 %collective-permute-start.5 = (bf16[256,1024]{1,0:T(8,128)(2,1)S(1)}, bf16[256,1024]{1,0:T(8,128)(2,1)S(1)}, u32[]{:S(2)}, u32[]{:S(2)}) collective-permute-start(bf16[256,1024]{1,0:T(8,128)(2,1)S(1)} %collective-permute-done.3.refs_4_), channel_id=1, source_target_pairs={{0,2},{2,0},{1,3},{3,1},{4,6},{6,4},{5,7},{7,5},{8,10},{10,8},{9,1... | collective-permute-start | bytes 1572872 | tf_op jit(solution)/shard_map/ppermute | solution.py:51
  17.2 13.6 %collective-permute-start = (bf16[256,1024]{1,0:T(8,128)(2,1)S(1)}, bf16[256,1024]{1,0:T(8,128)(2,1)S(1)}, u32[]{:S(2)}, u32[]{:S(2)}) collective-permute-start(bf16[256,1024]{1,0:T(8,128)(2,1)S(1)} %convert_bitcast_fusion.refs_0_), channel_id=1, source_target_pairs={{0,1},{1,0},{2,3},{3,2},{4,5},{5,4},{6,7},{7,6},{8,9},{9,8},{10,11... | collective-permute-start | bytes 1572872 | tf_op jit(solution)/shard_map/ppermute | solution.py:51
  17.2 14.4 %collective-permute-start.4 = (bf16[256,1024]{1,0:T(8,128)(2,1)S(1)}, bf16[256,1024]{1,0:T(8,128)(2,1)S(1)}, u32[]{:S(2)}, u32[]{:S(2)}) collective-permute-start(bf16[256,1024]{1,0:T(8,128)(2,1)S(1)} %collective-permute-done.3.refs_4_), channel_id=1, source_target_pairs={{0,1},{1,0},{2,3},{3,2},{4,5},{5,4},{6,7},{7,6},{8,9},{9,8},{10,11... | collective-permute-start | bytes 1572872 | tf_op jit(solution)/shard_map/ppermute | solution.py:51
  17.7 13.9 %collective-permute-start.2 = (bf16[256,1024]{1,0:T(8,128)(2,1)S(1)}, bf16[256,1024]{1,0:T(8,128)(2,1)}, u32[]{:S(2)}, u32[]{:S(2)}) collective-permute-start(bf16[256,1024]{1,0:T(8,128)(2,1)S(1)} %collective-permute-done.1.refs_2_), channel_id=1, source_target_pairs={{0,1},{1,0},{2,3},{3,2},{4,5},{5,4},{6,7},{7,6},{8,9},{9,8},{10,11... | collective-permute-start | bytes 1572872 | tf_op jit(solution)/shard_map/ppermute | solution.py:51
  17.7 0.8 copy-start.2
  28.5 4.0 %collective-permute-start.6 = (bf16[256,1024]{1,0:T(8,128)(2,1)S(1)}, bf16[256,1024]{1,0:T(8,128)(2,1)}, u32[]{:S(2)}, u32[]{:S(2)}) collective-permute-start(bf16[256,1024]{1,0:T(8,128)(2,1)S(1)} %collective-permute-done.5.refs_6_), channel_id=1, source_target_pairs={{0,1},{1,0},{2,3},{3,2},{4,5},{5,4},{6,7},{7,6},{8,9},{9,8},{10,11... | collective-permute-start | bytes 1572872 | tf_op jit(solution)/shard_map/ppermute | solution.py:51
  28.5 0.8 copy-start.4
  29.3 14.7 %collective-permute-start.8 = (bf16[1024,256]{1,0:T(8,128)(2,1)}, bf16[1024,256]{1,0:T(8,128)(2,1)}, u32[]{:S(2)}, u32[]{:S(2)}) collective-permute-start(bf16[1024,256]{1,0:T(8,128)(2,1)} %get-tuple-element.62), channel_id=1, source_target_pairs={{0,4},{4,0},{1,5},{5,1},{2,6},{6,2},{3,7},{7,3},{8,12},{12,8},{9,1... | collective-permute-start | bytes 1572872 | tf_op jit(solution)/shard_map/ppermute | solution.py:51
  30.8 0.8 copy-start.6
  31.6 0.8 copy-start.8
  32.4 1.0 copy-start.3
  33.5 1.0 copy-start.5
  34.5 1.0 copy-start.7
  35.6 1.0 copy-start.9
  36.6 8.8 %copy-start.10 = (f32[1,256,1024]{2,1,0:T(8,128)S(1)}, f32[1,256,1024]{2,1,0:T(8,128)}, u32[]{:S(2)}) copy-start(f32[1,256,1024]{2,1,0:T(8,128)} %refs_4_.1) | copy-start | bytes 3145732
  41.7 21.3 %collective-permute-start.13 = (bf16[256,1024]{1,0:T(8,128)(2,1)}, bf16[256,1024]{1,0:T(8,128)(2,1)}, u32[]{:S(2)}, u32[]{:S(2)}) collective-permute-start(bf16[256,1024]{1,0:T(8,128)(2,1)} %get-tuple-element.80), channel_id=1, source_target_pairs={{24,16},{8,0},{25,17},{9,1},{26,18},{10,2},{27,19},{11,3},{28,20},... | collective-permute-start | bytes 1572872 | tf_op jit(solution)/shard_map/ppermute | solution.py:410
  43.0 9.2 %collective-permute-start.7 = (bf16[128,1024]{1,0:T(8,128)(2,1)S(1)}, bf16[128,1024]{1,0:T(8,128)(2,1)S(1)}, u32[]{:S(2)}, u32[]{:S(2)}) collective-permute-start(bf16[128,1024]{1,0:T(8,128)(2,1)S(1)} %dynamic-slice_bitcast_fusion), channel_id=1, source_target_pairs={{0,4},{4,0},{1,5},{5,1},{2,6},{6,2},{3,7},{7,3},{8,12},{12,8},{9,1... | collective-permute-start | bytes 786440 | tf_op jit(solution)/shard_map/ppermute | solution.py:51
  43.9 28.9 %collective-permute-start.9 = (bf16[1024,256]{1,0:T(8,128)(2,1)}, bf16[1024,256]{1,0:T(8,128)(2,1)}, u32[]{:S(2)}, u32[]{:S(2)}) collective-permute-start(bf16[1024,256]{1,0:T(8,128)(2,1)} %get-tuple-element.67), channel_id=1, source_target_pairs={{0,4},{4,0},{1,5},{5,1},{2,6},{6,2},{3,7},{7,3},{8,12},{12,8},{9,1... | collective-permute-start | bytes 1572872 | tf_op jit(solution)/shard_map/ppermute | solution.py:51
  55.4 13.4 %all-to-all-start = ((bf16[8,256,128]{2,1,0:T(8,128)(2,1)}), bf16[8,256,128]{2,1,0:T(8,128)(2,1)S(1)}, u32[]{:S(2)}, u32[]{:S(2)}) async-start(bf16[8,256,128]{2,1,0:T(8,128)(2,1)} %get-tuple-element.65), calls=%async_computation | async-start | bytes 1048576 | tf_op jit(solution)/shard_map/all_to_all | solution.py:66
  63.1 16.5 %collective-permute-start.15 = (bf16[256,1024]{1,0:T(8,128)(2,1)}, bf16[256,1024]{1,0:T(8,128)(2,1)}, u32[]{:S(2)}, u32[]{:S(2)}) collective-permute-start(bf16[256,1024]{1,0:T(8,128)(2,1)} %collective-permute-done.13.refs_1_), channel_id=1, source_target_pairs={{0,2},{2,0},{1,3},{3,1},{4,6},{6,4},{5,7},{7,5},{8,10},{10,8},{9,1... | collective-permute-start | bytes 1572872 | tf_op jit(solution)/shard_map/ppermute | solution.py:51
  65.1 16.9 %collective-permute-start.10 = (bf16[1024,256]{1,0:T(8,128)(2,1)}, bf16[1024,256]{1,0:T(8,128)(2,1)S(1)}, u32[]{:S(2)}, u32[]{:S(2)}) collective-permute-start(bf16[1024,256]{1,0:T(8,128)(2,1)} %get-tuple-element.70.refs_2_), channel_id=1, source_target_pairs={{24,16},{25,17},{26,18},{27,19},{28,20},{29,21},{30,22},{31,23}} | collective-permute-start | bytes 1572872 | tf_op jit(solution)/shard_map/ppermute | solution.py:384
  72.8 14.1 %copy-start.11 = (bf16[1024,128]{1,0:T(8,128)(2,1)S(1)}, bf16[1024,128]{1,0:T(8,128)(2,1)}, u32[]{:S(2)}) copy-start(bf16[1024,128]{1,0:T(8,128)(2,1)} %get-tuple-element.73) | copy-start | bytes 786436
  77.0 29.3 %collective-permute-start.12 = (bf16[1024,256]{1,0:T(8,128)(2,1)}, bf16[1024,256]{1,0:T(8,128)(2,1)S(1)}, u32[]{:S(2)}, u32[]{:S(2)}) collective-permute-start(bf16[1024,256]{1,0:T(8,128)(2,1)} %get-tuple-element.75.refs_2_), channel_id=1, source_target_pairs={{24,16},{25,17},{26,18},{27,19},{28,20},{29,21},{30,22},{31,23}} | collective-permute-start | bytes 1572872 | tf_op jit(solution)/shard_map/ppermute | solution.py:384
  78.3 36.9 %collective-permute-start.14 = (bf16[256,1024]{1,0:T(8,128)(2,1)}, bf16[256,1024]{1,0:T(8,128)(2,1)}, u32[]{:S(2)}, u32[]{:S(2)}) collective-permute-start(bf16[256,1024]{1,0:T(8,128)(2,1)} %collective-permute-done.13.refs_1_), channel_id=1, source_target_pairs={{0,1},{1,0},{2,3},{3,2},{4,5},{5,4},{6,7},{7,6},{8,9},{9,8},{10,11... | collective-permute-start | bytes 1572872 | tf_op jit(solution)/shard_map/ppermute | solution.py:51
  79.6 35.7 %collective-permute-start.16 = (bf16[256,1024]{1,0:T(8,128)(2,1)}, bf16[256,1024]{1,0:T(8,128)(2,1)}, u32[]{:S(2)}, u32[]{:S(2)}) collective-permute-start(bf16[256,1024]{1,0:T(8,128)(2,1)} %collective-permute-done.15.refs_3_), channel_id=1, source_target_pairs={{0,1},{1,0},{2,3},{3,2},{4,5},{5,4},{6,7},{7,6},{8,9},{9,8},{10,11... | collective-permute-start | bytes 1572872 | tf_op jit(solution)/shard_map/ppermute | solution.py:51
  84.5 34.9 %collective-permute-start.17 = (bf16[1024,256]{1,0:T(8,128)(2,1)}, bf16[1024,256]{1,0:T(8,128)(2,1)}, u32[]{:S(2)}, u32[]{:S(2)}) collective-permute-start(bf16[1024,256]{1,0:T(8,128)(2,1)} %get-tuple-element.82), channel_id=1, source_target_pairs={{16,8},{17,9},{18,10},{19,11},{20,12},{21,13},{22,14},{23,15}} | collective-permute-start | bytes 1572872 | tf_op jit(solution)/shard_map/ppermute | solution.py:384
  86.9 12.3 %collective-permute-start.11 = (bf16[1024,128]{1,0:T(8,128)(2,1)S(1)}, bf16[1024,128]{1,0:T(8,128)(2,1)S(1)}, u32[]{:S(2)}, u32[]{:S(2)}) collective-permute-start(bf16[1024,128]{1,0:T(8,128)(2,1)S(1)} %copy-done.11), channel_id=1, source_target_pairs={{24,16},{8,0},{25,17},{9,1},{26,18},{10,2},{27,19},{11,3},{28,20},... | collective-permute-start | bytes 786440 | tf_op jit(solution)/shard_map/ppermute | solution.py:421
  103.0 9.8 %all-to-all-start.1 = ((bf16[8,128,128]{2,1,0:T(8,128)(2,1)}), bf16[8,128,128]{2,1,0:T(8,128)(2,1)S(1)}, u32[]{:S(2)}, u32[]{:S(2)}) async-start(bf16[8,128,128]{2,1,0:T(8,128)(2,1)} %bitcast.26), calls=%async_computation.1 | async-start | bytes 524288 | tf_op jit(solution)/shard_map/all_to_all | solution.py:66
  106.4 13.0 %copy-start = (bf16[1024,256]{1,0:T(8,128)(2,1)}, bf16[1024,256]{1,0:T(8,128)(2,1)S(1)}, u32[]{:S(2)}) copy-start(bf16[1024,256]{1,0:T(8,128)(2,1)S(1)} %collective-permute-done.12.refs_1_.refs_3_) | copy-start | bytes 1572868
  109.1 23.4 %collective-permute-start.18 = (bf16[1024,256]{1,0:T(8,128)(2,1)}, bf16[1024,256]{1,0:T(8,128)(2,1)}, u32[]{:S(2)}, u32[]{:S(2)}) collective-permute-start(bf16[1024,256]{1,0:T(8,128)(2,1)} %get-tuple-element.87), channel_id=1, source_target_pairs={{16,8},{17,9},{18,10},{19,11},{20,12},{21,13},{22,14},{23,15}} | collective-permute-start | bytes 1572872 | tf_op jit(solution)/shard_map/ppermute | solution.py:384
  122.1 21.2 %collective-permute-start.19 = (bf16[1024,256]{1,0:T(8,128)(2,1)}, bf16[1024,256]{1,0:T(8,128)(2,1)}, u32[]{:S(2)}, u32[]{:S(2)}) collective-permute-start(bf16[1024,256]{1,0:T(8,128)(2,1)} %get-tuple-element.90), channel_id=1, source_target_pairs={{8,0},{9,1},{10,2},{11,3},{12,4},{13,5},{14,6},{15,7}} | collective-permute-start | bytes 1572872 | tf_op jit(solution)/shard_map/ppermute | solution.py:384
  123.6 12.9 %all-to-all-start.2 = ((bf16[8,256,128]{2,1,0:T(8,128)(2,1)}), bf16[8,256,128]{2,1,0:T(8,128)(2,1)S(1)}, u32[]{:S(2)}, u32[]{:S(2)}) async-start(bf16[8,256,128]{2,1,0:T(8,128)(2,1)} %get-tuple-element.85), calls=%async_computation.2 | async-start | bytes 1048576 | tf_op jit(solution)/shard_map/all_to_all | solution.py:66
  127.2 23.2 %collective-permute-start.23 = (bf16[1024,128]{1,0:T(8,128)(2,1)}, bf16[1024,128]{1,0:T(8,128)(2,1)S(1)}, u32[]{:S(2)}, u32[]{:S(2)}) collective-permute-start(bf16[1024,128]{1,0:T(8,128)(2,1)} %get-tuple-element.94), channel_id=1, source_target_pairs={{16,0},{17,1},{18,2},{19,3},{20,4},{21,5},{22,6},{23,7}} | collective-permute-start | bytes 786440 | tf_op jit(solution)/shard_map/ppermute | solution.py:433
  128.5 21.9 %collective-permute-start.22 = (bf16[1024,128]{1,0:T(8,128)(2,1)}, bf16[1024,128]{1,0:T(8,128)(2,1)}, u32[]{:S(2)}, u32[]{:S(2)}) collective-permute-start(bf16[1024,128]{1,0:T(8,128)(2,1)} %get-tuple-element.94), channel_id=1, source_target_pairs={{16,8},{17,9},{18,10},{19,11},{20,12},{21,13},{22,14},{23,15}} | collective-permute-start | bytes 786440 | tf_op jit(solution)/shard_map/ppermute | solution.py:433
  130.5 19.9 %collective-permute-start.21 = (bf16[1024,128]{1,0:T(8,128)(2,1)}, bf16[1024,128]{1,0:T(8,128)(2,1)}, u32[]{:S(2)}, u32[]{:S(2)}) collective-permute-start(bf16[1024,128]{1,0:T(8,128)(2,1)} %get-tuple-element.93), channel_id=1, source_target_pairs={{16,0},{17,1},{18,2},{19,3},{20,4},{21,5},{22,6},{23,7}} | collective-permute-start | bytes 786440 | tf_op jit(solution)/shard_map/ppermute | solution.py:438
  132.6 19.6 %collective-permute-start.20 = (bf16[1024,128]{1,0:T(8,128)(2,1)}, bf16[1024,128]{1,0:T(8,128)(2,1)}, u32[]{:S(2)}, u32[]{:S(2)}) collective-permute-start(bf16[1024,128]{1,0:T(8,128)(2,1)} %get-tuple-element.93), channel_id=1, source_target_pairs={{16,8},{17,9},{18,10},{19,11},{20,12},{21,13},{22,14},{23,15}} | collective-permute-start | bytes 786440 | tf_op jit(solution)/shard_map/ppermute | solution.py:438
  143.2 20.3 %collective-permute-start.24 = (bf16[1024,256]{1,0:T(8,128)(2,1)}, bf16[1024,256]{1,0:T(8,128)(2,1)}, u32[]{:S(2)}, u32[]{:S(2)}) collective-permute-start(bf16[1024,256]{1,0:T(8,128)(2,1)} %get-tuple-element.97), channel_id=1, source_target_pairs={{8,0},{9,1},{10,2},{11,3},{12,4},{13,5},{14,6},{15,7}} | collective-permute-start | bytes 1572872 | tf_op jit(solution)/shard_map/ppermute | solution.py:384
  157.7 32.9 %all-to-all-start.3 = ((bf16[8,256,256]{2,1,0:T(8,128)(2,1)}), bf16[8,256,256]{2,1,0:T(8,128)(2,1)S(1)}, u32[]{:S(2)}, u32[]{:S(2)}) async-start(bf16[8,256,256]{2,1,0:T(8,128)(2,1)} %get-tuple-element.104), calls=%async_computation.3 | async-start | bytes 2097152 | tf_op jit(solution)/shard_map/all_to_all | solution.py:66
  161.5 26.2 %collective-permute-start.25 = (bf16[1024,256]{1,0:T(8,128)(2,1)}, bf16[1024,256]{1,0:T(8,128)(2,1)S(1)}, u32[]{:S(2)}, u32[]{:S(2)}) collective-permute-start(bf16[1024,256]{1,0:T(8,128)(2,1)} %get-tuple-element.100), channel_id=1, source_target_pairs={{0,4},{4,0},{1,5},{5,1},{2,6},{6,2},{3,7},{7,3},{8,12},{12,8},{9,1... | collective-permute-start | bytes 1572872 | tf_op jit(solution)/shard_map/ppermute | solution.py:51
  163.5 1.0 copy-start.1
  170.2 28.4 %collective-permute-start.26 = (bf16[1024,256]{1,0:T(8,128)(2,1)}, bf16[1024,256]{1,0:T(8,128)(2,1)}, u32[]{:S(2)}, u32[]{:S(2)}) collective-permute-start(bf16[1024,256]{1,0:T(8,128)(2,1)} %get-tuple-element.108), channel_id=1, source_target_pairs={{0,4},{4,0},{1,5},{5,1},{2,6},{6,2},{3,7},{7,3},{8,12},{12,8},{9,1... | collective-permute-start | bytes 1572872 | tf_op jit(solution)/shard_map/ppermute | solution.py:51

commit v8 on v7

--- a/solution.py
+++ b/solution.py
@@ -109,16 +109,19 @@
         into[:, s * width : (s + 1) * width] = blocks[s, :, start : start + width]
 
 
-def pair_kernel(ids, *refs):
-    pieces, (e0, e1, pair, quarter, both, sems) = refs[:8], refs[8:]
+def pair_kernel(ids, three, last, three_c, last_c, e0, e1, pair, quarter, both, sems):
     group = 2 * ids[1] + ids[2]
     me = 4 * ids[0] + group
-    rows = pieces[0].shape[0]
+    rows = last.shape[0]
+    pieces = []
+    for flip, (some, other) in enumerate(((three, last), (three_c, last_c))):
+        pieces += [(some.at[i * rows : (i + 1) * rows, :], at + flip) for i, at in enumerate((0, 4, 2))]
+        pieces.append((other, 6 + flip))
     copies = []
-    for i in range(8):
-        place = me ^ i
+    for i, (piece, at) in enumerate(pieces):
+        place = me ^ at
         into = both.at[place >> 2, pl.ds(pl.multiple_of((place & 3) * rows, rows), rows), :]
-        copies.append(pltpu.make_async_copy(pieces[i], into, sems.at[i]))
+        copies.append(pltpu.make_async_copy(piece, into, sems.at[i]))
         copies[-1].start()
     for copy in copies:
         copy.wait()
@@ -178,9 +181,22 @@
         near[2 * r + 1] = other[r * rows : (r + 1) * rows, :]
 
 
-def spread_next_kernel(ids, pair, slab, blocks, b_l, m):
-    gather_lanes(blocks, m, 0, m.shape[0])
-    b_l[...] = (mm_bt(pair[...], m[...]) + slab[...]).astype(LOW)
+def next_kernel(ids, pair, slab, blocks, quarters, quarters_c, following, out, m, sems):
+    part = m.shape[0]
+    rows = 2 * part
+    group = 2 * ids[1] + ids[2]
+    copies = []
+    for i, (piece, at) in enumerate(((quarters, 0), (quarters, 2), (quarters_c, 1), (quarters_c, 3))):
+        into = following.at[pl.ds(pl.multiple_of((group ^ at) * rows, rows), rows), :]
+        cut = piece.at[(at >> 1) * rows : ((at >> 1) + 1) * rows, :]
+        copies.append(pltpu.make_async_copy(cut, into, sems.at[i]))
+        copies[-1].start()
+    gather_lanes(blocks, m, 0, part)
+    out[:, part:] = (mm_bt(pair[...], m[...]) + slab[...]).astype(LOW)
+    for copy in copies:
+        copy.wait()
+    columns_here = pl.ds(pl.multiple_of((2 * group + ids[0]) * part, part), part)
+    out[:, :part] = mm(pair[...], following[:, columns_here]).astype(LOW)
 
 
 def near_kernel(ids, pair, e1, prod, blocks, spread, near, m):
@@ -195,28 +211,10 @@
         near[...] = mm_bt(m[...], e1[...]) + spread[0]
 
 
-def next_gain_kernel(ids, pair, *refs):
-    quarters, (following, slab_ref, sems) = refs[:4], refs[4:]
-    part, rows = slab_ref.shape[1], quarters[0].shape[0]
-    group = 2 * ids[1] + ids[2]
-    copies = []
-    for i in range(4):
-        into = following.at[pl.ds(pl.multiple_of((group ^ i) * rows, rows), rows), :]
-        copies.append(pltpu.make_async_copy(quarters[i], into, sems.at[i]))
-        copies[-1].start()
-    for copy in copies:
-        copy.wait()
-    slab = pl.ds(pl.multiple_of((2 * group + ids[0]) * part, part), part)
-    slab_ref[...] = mm(pair[...], following[:, slab]).astype(LOW)
-
-
-def far_kernel(ids, pair, e1, following, e_a, e_b, l_a, l_b, out, far):
-    size, part = e_a.shape
-    rows = 2 * part
-
-    @pl.when(ids[3] < 2)
-    def _():
-        far[:, :part] = e_a[...] + e_b[...]
+def far_kernel(ids, pair, e1, following, f_a, f_b, out, far):
+    size, rows = far.shape
+    part = rows // 2
+    far[...] = f_a[...] + f_b[...]
 
     @pl.when(ids[3] >= 2)
     def _():
@@ -224,8 +222,6 @@
         column = lax.broadcasted_iota(jnp.int32, (size, part), 1) + slab * part
         row = lax.broadcasted_iota(jnp.int32, (size, part), 0)
         far[:, :part] = jnp.where(row == column, 1.0, 0.0).astype(LOW)
-
-    far[:, part:] = l_a[...] + l_b[...]
 
     @pl.when(ids[3] % 2 == 0)
     def _():
@@ -286,44 +282,56 @@
     now[...] = (mm(pair[...], got[...]) + own[...].astype(WIDE)).astype(LOW)
 
 
-def last_kernel(chunk, ids, pair, e1, p, got_a, got_b, got_c, offset, *refs):
-    out, send, keep, far, sems = refs[-5:]
+def last_kernel(chunk, ids, pair, later, p_far, got_a, got_b, got_c, offset, *refs):
+    out, send, keep, far, e1, p, sems = refs[-7:]
     width = keep.shape[1]
-    copy = pltpu.make_async_copy(columns(offset, ids[0], chunk, width), keep, sems.at[0])
-    copy.start()
     for z, got in ((2, got_a), (1, got_b), (0, got_c)):
 
         @pl.when(ids[3] == z)
         def _():
-            load = pltpu.make_async_copy(got, far, sems.at[1])
-            load.start()
-            load.wait()
+            pltpu.make_async_copy(got, far, sems.at[0]).start()
+
+    load_e1 = pltpu.make_async_copy(later, e1, sems.at[1])
+    load_e1.start()
+    load_p = pltpu.make_async_copy(p_far, p, sems.at[2])
+    load_p.start()
+    load_keep = pltpu.make_async_copy(columns(offset, ids[0], chunk, width), keep, sems.at[3])
+    load_keep.start()
 
     @pl.when(ids[3] == 3)
     def _():
         far[...] = jnp.zeros_like(far)
 
+    @pl.when(ids[3] != 3)
+    def _():
+        pltpu.make_async_copy(got_a, far, sems.at[0]).wait()
+
+    first = mm(pair[...], far[...])
+    load_p.wait()
+    p[...] = first + p[...]
+    load_keep.wait()
+    load_e1.wait()
+
+    @pl.when(ids[0] == 0)
+    def _():
+        keep[...] = p[...] + keep[...]
+
+    @pl.when(ids[0] == 1)
+    def _():
+        keep[...] = mm(e1[...], far[...]) + keep[...]
+
+    store = pltpu.make_async_copy(keep, columns(out, ids[0], chunk, width), sems.at[4])
+    store.start()
+
     @pl.when(ids[0] == 0)
     def _():
         send[...] = mm(e1[...], far[...]).astype(LOW)
 
     @pl.when(ids[0] == 1)
     def _():
-        send[...] = (mm(pair[...], far[...]) + p[...]).astype(LOW)
-
-    copy.wait()
-
-    @pl.when(ids[0] == 0)
-    def _():
-        keep[...] = mm(pair[...], far[...]) + p[...] + keep[...]
-
-    @pl.when(ids[0] == 1)
-    def _():
-        keep[...] = mm(e1[...], far[...]) + keep[...]
-
-    copy = pltpu.make_async_copy(keep, columns(out, ids[0], chunk, width), sems.at[1])
-    copy.start()
-    copy.wait()
+        send[...] = p[...].astype(LOW)
+
+    store.wait()
 
 
 def add_kernel(chunk, ids, got, offset, into, out, keep, sems):
@@ -365,9 +373,8 @@
     for i in range(1, chunks):
         g_send[i], g_got[-1] = lax.optimization_barrier((g_send[i], g_got[-1]))
         g_got.append(swap(g_send[i], "x"))
-    pieces = [e_low, None, e_y, None, e_x, None, e_xy, None]
-    for i in range(0, 8, 2):
-        pieces[i + 1] = swap(pieces[i], "c")
+    three = jnp.concatenate([e_low, e_x, e_y], axis=0)
+    pieces = [in_hbm(a) for a in (three, e_xy, swap(three, "c"), swap(e_xy, "c"))]
     offset, spread = in_hbm(offsets[0]), in_hbm(spreads)
 
     keep = pltpu.VMEM((size_d, width), WIDE)
@@ -391,8 +398,8 @@
         return order.call(
             functools.partial(last_kernel, i), [pair, in_hbm(e1), in_hbm(p), *gots, offset] + extra,
             [wide(*offset.shape), hbm(size_d, width)], 14,
-            far_in=(3, 4, 5, 6, 7), far_out=(0,), aliases={7: 0} if extra else {},
-            scratch=[keep, column, pltpu.SemaphoreType.DMA((2,))],
+            far_in=(1, 2, 3, 4, 5, 6, 7), far_out=(0,), aliases={7: 0} if extra else {},
+            scratch=[keep, column, pltpu.VMEM((size_d, size_d), LOW), keep, pltpu.SemaphoreType.DMA((5,))],
         )
 
     def add(i, got, into):
@@ -404,48 +411,46 @@
     e0, e1, pair, quarter = order.call(
         pair_kernel, pieces,
         [hbm(size_d, size_d), hbm(size_d, size_d), pltpu.VMEM((size_d, size_d), LOW), hbm(rows, size_d)], 14,
-        far_in=range(8), far_out=(0, 1),
+        far_in=range(4), far_out=(0, 1),
         scratch=[pltpu.VMEM((2, size_d, size_d), LOW), pltpu.SemaphoreType.DMA((8,))],
     )
     quarter = lax.ppermute(quarter, "z", level)
     quarter_y = swap(quarter, "y")
-    quarters = [quarter, swap(quarter, "c"), quarter_y, swap(quarter_y, "c")]
+    quarters = jnp.concatenate([quarter, quarter_y], axis=0)
+    quarters = [quarters, swap(quarters, "c")]
     (m,) = order.call(spread_kernel, [in_hbm(e0), l_low, l_got], [hbm(8, rows, part)], 8)
     m = exchange(m)
     p0, own0 = start(0)
     gots0 = [down(own0, 3)]
+    p1, own1 = start(1)
+    gots1 = [down(own1, 3)]
     prod, slab, a_low = order.call(
         spread_start_kernel, [in_hbm(e0), m, spread, l_got],
         [hbm(rows, size_d, dtype=WIDE), hbm(size_d, part, dtype=WIDE), hbm(size_d, part)], 12, scratch=[slab_rows],
     )
     l_next = lax.ppermute(a_low, "z", level)
-    p1, own1 = start(1)
-    gots1 = [down(own1, 3)]
     gots0.append(down(hop(gots0[0], own0), 2))
 
     m, near = order.call(spread_hop_kernel, [pair, in_hbm(e1), l_next], [hbm(size_d, part), hbm(8, rows, part)], 10)
     m = exchange(m.reshape(8, part, part))
     near = exchange(near)
     gots1.append(down(hop(gots1[0], own1), 2))
-    (b_l,) = order.call(
-        spread_next_kernel, [pair, in_hbm(slab), m], [hbm(size_d, part)], 8, scratch=[pltpu.VMEM((part, size_d), LOW)]
-    )
-    l_far = lax.ppermute(b_l, "z", [(2, 1)]), lax.ppermute(b_l, "z", [(2, 0)])
-    following, e_slab = order.call(
-        next_gain_kernel, [pair, *quarters], [hbm(size_d, size_d), hbm(size_d, part)], 10,
-        far_in=(1, 2, 3, 4), scratch=[pltpu.SemaphoreType.DMA((4,))],
-    )
-    e_far = lax.ppermute(e_slab, "z", [(2, 1)]), lax.ppermute(e_slab, "z", [(2, 0)])
     gots0.append(down(hop(gots0[1], own0), 1))
+    following, far_slab = order.call(
+        next_kernel, [pair, in_hbm(slab), m, *quarters], [hbm(size_d, size_d), hbm(size_d, rows)], 12,
+        far_in=(3, 4), scratch=[pltpu.VMEM((part, size_d), LOW), pltpu.SemaphoreType.DMA((4,))],
+    )
+    far = lax.ppermute(far_slab, "z", [(2, 1)]), lax.ppermute(far_slab, "z", [(2, 0)])
     (near,) = order.call(
-        near_kernel, [pair, in_hbm(e1), in_hbm(prod), near, spread], [hbm(rows, size_d, dtype=WIDE)], 12, scratch=[slab_rows]
+        near_kernel, [pair, in_hbm(e1), in_hbm(prod), near, spread], [hbm(rows, size_d, dtype=WIDE)], 12,
+        scratch=[slab_rows],
     )
     gots1.append(down(hop(gots1[1], own1), 1))
 
     out_offset, other0 = last(0, p0, gots0, None)
     other0 = swap(other0, "x")
     (m,) = order.call(
-        far_kernel, [pair, in_hbm(e1), in_hbm(following), *e_far, *l_far], [hbm(8, rows, rows)], 14,
+        far_kernel, [pair, in_hbm(e1), in_hbm(following), *far], [hbm(8, rows, rows)], 14,
         scratch=[pltpu.VMEM((size_d, rows), LOW)],
     )
     m = exchange(m)

time: 205 us -> 213 us (1.039)
  waiting for transfers between devices: 65.6 us -> 82.4 us
  local copies, waits for them, and re-layouts: 11 us -> 4.23 us
    ppermute x1, waiting for transfers between devices: 0.01 us -> 13.7 us  [suffix(): quarter = lax.ppermute(quarter, 'z', level)]
    unnamed x24 -> x9, local copies, waits for them, and re-layouts: 8.39 us -> 0.84 us
    ppermute x4 -> x2, waiting for transfers between devices: 1.76 us -> 8.51 us  [the longest x1 8.51 us: suffix(): lax.ppermute(far_slab, 'z', [(2, 1)])]
    ppermute x1, waiting for transfers between devices: 11.1 us -> 5.38 us  [suffix(): l_next = lax.ppermute(a_low, 'z', level)]
    ppermute x15 -> x12, waiting for transfers between devices: 44.6 us -> 49.5 us  [swap(): return lax.ppermute(value, axis, [(0, 1), (1, 0)])]
    ppermute x4 -> x2, starting transfers between devices: 7.29 us -> 2.64 us  [the longest x1 1.32 us: suffix(): lax.ppermute(far_slab, 'z', [(2, 0)])]
    ppermute x6, waiting for transfers between devices: 2.39 us -> 0.02 us  [down(): return lax.ppermute(value, 'z', [(source, source - 1)])]
    all_to_all x4, starting transfers between devices: 14.4 us -> 16.6 us  [exchange(): return lax.all_to_all(blocks, GROUP, 0, 0)]
  transfers between devices with their start and end apart: 31 -> 26, of which waited for: 13 -> 12; matrix products, arithmetic and copies ran while one was open for 2% -> 2% of each run, Pallas kernels for 35% -> 30%
where the time goes in v8:
time: 213 us; the launch traced here: 211 us
  waiting for transfers between devices  82.4 us (39%)
  Pallas kernels  73.1 us (34%)
  starting transfers between devices  46.1 us (22%)
  local copies, waits for them, and re-layouts  4.23 us (2%)
  other arithmetic  4.13 us (2%)
    pallas_call x18, Pallas kernels, call(): pl.pallas_call(body, in_specs=[SMEM, ANY] + [ANY if i in far_in else VMEM...  73.1 us
    ppermute x12, waiting for transfers between devices, swap(): return lax.ppermute(value, axis, [(0, 1), (1, 0)])  49.5 us
    all_to_all x4, starting transfers between devices, exchange(): return lax.all_to_all(blocks, GROUP, 0, 0)  16.6 us
    ppermute x1, waiting for transfers between devices, suffix(): quarter = lax.ppermute(quarter, 'z', level)  13.7 us
    ppermute x12, starting transfers between devices, swap(): return lax.ppermute(value, axis, [(0, 1), (1, 0)])  12.2 us
    ppermute x6, starting transfers between devices, down(): return lax.ppermute(value, 'z', [(source, source - 1)])  12 us
    ppermute x1, waiting for transfers between devices, suffix(): lax.ppermute(far_slab, 'z', [(2, 1)])  8.51 us
    ppermute x1, waiting for transfers between devices, suffix(): l_next = lax.ppermute(a_low, 'z', level)  5.38 us
  transfers between devices with their start and end apart: 26, of which 12 were waited for; matrix products, arithmetic and copies ran while one was open for 2% of the time, Pallas kernels for 30%

profile of v8, /device:TPU:16, one launch (start us, length us, event | category | flops | bytes accessed | tf_op | source)
XLA Modules:
  0.0 211.0 jit_solution(11338631456858369263)
XLA Ops:
  1.9 1.6 collective-permute-start
  3.5 1.5 collective-permute-start.1
  7.0 2.6 %fusion.1 = (bf16[1024,256]{1,0:T(8,128)(2,1)}, bf16[1024,256]{1,0:T(8,128)(2,1)}) fusion(f32[1,1024,1024]{2,1,0:T(8,128)} %param.5, s32[]{:T(128)S(6)} %select_n.11, s32[]{:T(128)S(6)} %select_n.10), kind=kLoop, calls=%fused_computation.4 | loop fusion | bytes 2097160 | tf_op jit(solution)/shard_map/convert_element_type | solution.py:367
  9.7 6.0 %collective-permute-done = bf16[256,1024]{1,0:T(8,128)(2,1)S(1)} collective-permute-done((bf16[256,1024]{1,0:T(8,128)(2,1)S(1)}, bf16[256,1024]{1,0:T(8,128)(2,1)S(1)}, u32[]{:S(2)}, u32[]{:S(2)}) %collective-permute-start) | collective-permute-done | bytes 524320 | tf_op jit(solution)/shard_map/ppermute | solution.py:51
  17.0 1.4 pad_maximum_fusion.refs_0_
  18.5 1.6 collective-permute-start.2
  20.1 12.9 %collective-permute-done.2.refs_1_ = bf16[256,1024]{1,0:T(8,128)(2,1)} collective-permute-done((bf16[256,1024]{1,0:T(8,128)(2,1)S(1)}, bf16[256,1024]{1,0:T(8,128)(2,1)}, u32[]{:S(2)}, u32[]{:S(2)}) %collective-permute-start.2) | collective-permute-done | bytes 524320 | tf_op jit(solution)/shard_map/ppermute | solution.py:51
  33.0 2.2 %collective-permute-done.4.refs_3_ = bf16[256,1024]{1,0:T(8,128)(2,1)} collective-permute-done((bf16[256,1024]{1,0:T(8,128)(2,1)}, bf16[256,1024]{1,0:T(8,128)(2,1)}, u32[]{:S(2)}, u32[]{:S(2)}) %collective-permute-start.4) | collective-permute-done | bytes 524320 | tf_op jit(solution)/shard_map/ppermute | solution.py:51
  35.2 5.9 %shard_map.58 = (bf16[1024,1024]{1,0:T(8,128)(2,1)}, bf16[1024,1024]{1,0:T(8,128)(2,1)}, bf16[1024,1024]{1,0:T(8,128)(2,1)S(1)}, bf16[256,1024]{1,0:T(8,128)(2,1)}, s32[8,128]{1,0:T(8,128)S(1)}) custom-call(s32[4]{0:T(128)S(1)} %pad_add_fusion.ids, s32[8,128]{1,0:T(8,128)S(1)} %broadcast_in_dim.12.token, ...), custom_call_target="tpu_custom_call", output_to_operand_aliasing={{4}: (1, {})} | custom-call | flops 1 | bytes 1 | tf_op jit(solution)/shard_map/pallas_call | solution.py:93
  41.1 1.3 collective-permute-start.12
  43.5 13.7 %collective-permute-done.12 = bf16[256,1024]{1,0:T(8,128)(2,1)S(1)} collective-permute-done((bf16[256,1024]{1,0:T(8,128)(2,1)}, bf16[256,1024]{1,0:T(8,128)(2,1)S(1)}, u32[]{:S(2)}, u32[]{:S(2)}) %collective-permute-start.12) | collective-permute-done | bytes 524320 | tf_op jit(solution)/shard_map/ppermute | solution.py:417
  57.2 1.5 collective-permute-start.13
  60.9 7.3 %collective-permute-done.5.refs_2_.refs_3_ = bf16[128,1024]{1,0:T(8,128)(2,1)S(1)} collective-permute-done((bf16[128,1024]{1,0:T(8,128)(2,1)}, bf16[128,1024]{1,0:T(8,128)(2,1)S(1)}, u32[]{:S(2)}, u32[]{:S(2)}) %collective-permute-start.5) | collective-permute-done | bytes 262176 | tf_op jit(solution)/shard_map/ppermute | solution.py:51
  68.2 3.1 %shard_map.59 = (bf16[8,256,128]{2,1,0:T(8,128)(2,1)}, s32[8,128]{1,0:T(8,128)S(1)}) custom-call(s32[4]{0:T(128)S(1)} %pad_add_fusion.ids, s32[8,128]{1,0:T(8,128)S(1)} %get-tuple-element.56.token, bf16[1024,1024]{1,0:T(8,128)(2,1)} %get-tuple-element.57.refs_0_, ...), custom_call_target="tpu_custom_call", output_to_operand_aliasing={{1}: (1, {})} | custom-call | flops 1 | bytes 1 | tf_op jit(solution)/shard_map/pallas_call | solution.py:93
  71.3 4.1 %shard_map.60 = (f32[1024,256]{1,0:T(8,128)}, bf16[1024,256]{1,0:T(8,128)(2,1)}, s32[8,128]{1,0:T(8,128)S(1)}) custom-call(s32[4]{0:T(128)S(1)} %pad_add_fusion.ids, s32[8,128]{1,0:T(8,128)S(1)} %get-tuple-element.59.token, bf16[1024,1024]{1,0:T(8,128)(2,1)} %get-tuple-element.57.refs_0_, ...), custom_call_target="tpu_custom_call", output_to_operand_aliasing={{2}: (1, {})} | custom-call | flops 1 | bytes 1 | tf_op jit(solution)/shard_map/pallas_call | solution.py:93
  75.4 1.3 collective-permute-start.8
  76.9 4.2 %all-to-all-start = ((bf16[8,256,128]{2,1,0:T(8,128)(2,1)}), bf16[8,256,128]{2,1,0:T(8,128)(2,1)}, u32[]{:S(2)}, u32[]{:S(2)}) async-start(bf16[8,256,128]{2,1,0:T(8,128)(2,1)} %get-tuple-element.65), calls=%async_computation | async-start | bytes 1048576 | tf_op jit(solution)/shard_map/all_to_all | solution.py:66
  81.1 4.2 %shard_map.61 = (f32[1024,256]{1,0:T(8,128)}, bf16[1024,256]{1,0:T(8,128)(2,1)}, s32[8,128]{1,0:T(8,128)S(1)}) custom-call(s32[4]{0:T(128)S(1)} %pad_add_fusion.ids, s32[8,128]{1,0:T(8,128)S(1)} %get-tuple-element.62.token, bf16[1024,1024]{1,0:T(8,128)(2,1)} %get-tuple-element.57.refs_0_, ...), custom_call_target="tpu_custom_call", output_to_operand_aliasing={{2}: (1, {})} | custom-call | flops 1 | bytes 1 | tf_op jit(solution)/shard_map/pallas_call | solution.py:93
  86.6 3.8 %all-to-all-done.refs_1_ = bf16[8,256,128]{2,1,0:T(8,128)(2,1)} async-done(((bf16[8,256,128]{2,1,0:T(8,128)(2,1)}), bf16[8,256,128]{2,1,0:T(8,128)(2,1)}, u32[]{:S(2)}, u32[]{:S(2)}) %all-to-all-start) | async-done | bytes 524320 | tf_op jit(solution)/shard_map/all_to_all | solution.py:66
  90.3 4.2 %shard_map.62 = (f32[256,1024]{1,0:T(8,128)}, f32[1024,128]{1,0:T(8,128)}, bf16[1024,128]{1,0:T(8,128)(2,1)}, s32[8,128]{1,0:T(8,128)S(1)}) custom-call(s32[4]{0:T(128)S(1)} %pad_add_fusion.ids, s32[8,128]{1,0:T(8,128)S(1)} %get-tuple-element.64.token, bf16[1024,1024]{1,0:T(8,128)(2,1)} %get-tuple-element.57.refs_0_, ...), custom_call_target="tpu_custom_call", output_to_operand_aliasing={{3}: (1, {})} | custom-call | flops 1 | bytes 1 | tf_op jit(solution)/shard_map/pallas_call | solution.py:93
  95.8 2.7 %shard_map.63 = (bf16[1024,256]{1,0:T(8,128)(2,1)}, s32[8,128]{1,0:T(8,128)S(1)}) custom-call(s32[4]{0:T(128)S(1)} %pad_add_fusion.ids, s32[8,128]{1,0:T(8,128)S(1)} %get-tuple-element.66.token, bf16[1024,1024]{1,0:T(8,128)(2,1)S(1)} %get-tuple-element.67.refs_0_, ...), custom_call_target="tpu_custom_call", output_to_operand_aliasing={{1}: (1, {})} | custom-call | flops 1 | bytes 1 | tf_op jit(solution)/shard_map/pallas_call | solution.py:93
  98.6 4.4 %collective-permute-start.11 = (bf16[1024,256]{1,0:T(8,128)(2,1)}, bf16[1024,256]{1,0:T(8,128)(2,1)}, u32[]{:S(2)}, u32[]{:S(2)}) collective-permute-start(bf16[1024,256]{1,0:T(8,128)(2,1)} %get-tuple-element.75), channel_id=1, source_target_pairs={{16,8},{17,9},{18,10},{19,11},{20,12},{21,13},{22,14},{23,15}} | collective-permute-start | bytes 1572872 | tf_op jit(solution)/shard_map/ppermute | solution.py:391
  103.0 5.4 %collective-permute-done.9.refs_2_ = bf16[1024,128]{1,0:T(8,128)(2,1)S(1)} collective-permute-done((bf16[1024,128]{1,0:T(8,128)(2,1)}, bf16[1024,128]{1,0:T(8,128)(2,1)S(1)}, u32[]{:S(2)}, u32[]{:S(2)}) %collective-permute-start.9) | collective-permute-done | bytes 262176 | tf_op jit(solution)/shard_map/ppermute | solution.py:431
  108.4 3.7 %shard_map.64 = (bf16[1024,128]{1,0:T(8,128)(2,1)}, bf16[8,256,128]{2,1,0:T(8,128)(2,1)}, s32[8,128]{1,0:T(8,128)S(1)}) custom-call(s32[4]{0:T(128)S(1)} %pad_add_fusion.ids, s32[8,128]{1,0:T(8,128)S(1)} %get-tuple-element.69.token, bf16[1024,1024]{1,0:T(8,128)(2,1)S(1)} %get-tuple-element.67.refs_0_, ...), custom_call_target="tpu_custom_call", output_to_operand_aliasing={{2}: (1, {})} | custom-call | flops 1 | bytes 1 | tf_op jit(solution)/shard_map/pallas_call | solution.py:93
  112.1 4.4 %all-to-all-start.1 = ((bf16[8,128,128]{2,1,0:T(8,128)(2,1)}), bf16[8,128,128]{2,1,0:T(8,128)(2,1)S(1)}, u32[]{:S(2)}, u32[]{:S(2)}) async-start(bf16[8,128,128]{2,1,0:T(8,128)(2,1)} %bitcast.26), calls=%async_computation.1 | async-start | bytes 524288 | tf_op jit(solution)/shard_map/all_to_all | solution.py:66
  116.5 2.7 %shard_map.65 = (bf16[1024,256]{1,0:T(8,128)(2,1)}, s32[8,128]{1,0:T(8,128)S(1)}) custom-call(s32[4]{0:T(128)S(1)} %pad_add_fusion.ids, s32[8,128]{1,0:T(8,128)S(1)} %get-tuple-element.72.token, bf16[1024,1024]{1,0:T(8,128)(2,1)S(1)} %get-tuple-element.67.refs_0_, ...), custom_call_target="tpu_custom_call", output_to_operand_aliasing={{1}: (1, {})} | custom-call | flops 1 | bytes 1 | tf_op jit(solution)/shard_map/pallas_call | solution.py:93
  119.2 2.1 %collective-permute-start.15 = (bf16[1024,256]{1,0:T(8,128)(2,1)}, bf16[1024,256]{1,0:T(8,128)(2,1)}, u32[]{:S(2)}, u32[]{:S(2)}) collective-permute-start(bf16[1024,256]{1,0:T(8,128)(2,1)} %get-tuple-element.84), channel_id=1, source_target_pairs={{16,8},{17,9},{18,10},{19,11},{20,12},{21,13},{22,14},{23,15}} | collective-permute-start | bytes 1572872 | tf_op jit(solution)/shard_map/ppermute | solution.py:391
  121.4 1.6 all-to-all-done.1.refs_2_
  123.0 4.1 %all-to-all-start.2 = ((bf16[8,256,128]{2,1,0:T(8,128)(2,1)}), bf16[8,256,128]{2,1,0:T(8,128)(2,1)}, u32[]{:S(2)}, u32[]{:S(2)}) async-start(bf16[8,256,128]{2,1,0:T(8,128)(2,1)} %get-tuple-element.82), calls=%async_computation.2 | async-start | bytes 1048576 | tf_op jit(solution)/shard_map/all_to_all | solution.py:66
  127.1 2.7 %shard_map.66 = (bf16[1024,256]{1,0:T(8,128)(2,1)}, s32[8,128]{1,0:T(8,128)S(1)}) custom-call(s32[4]{0:T(128)S(1)} %pad_add_fusion.ids, s32[8,128]{1,0:T(8,128)S(1)} %get-tuple-element.74.token, bf16[1024,1024]{1,0:T(8,128)(2,1)S(1)} %get-tuple-element.67.refs_0_, ...), custom_call_target="tpu_custom_call", output_to_operand_aliasing={{1}: (1, {})} | custom-call | flops 1 | bytes 1 | tf_op jit(solution)/shard_map/pallas_call | solution.py:93
  129.8 1.5 collective-permute-start.16
  131.3 5.1 %shard_map.67 = (bf16[1024,1024]{1,0:T(8,128)(2,1)}, bf16[1024,256]{1,0:T(8,128)(2,1)}, s32[8,128]{1,0:T(8,128)S(1)}) custom-call(s32[4]{0:T(128)S(1)} %pad_add_fusion.ids, s32[8,128]{1,0:T(8,128)S(1)} %get-tuple-element.76.token, bf16[1024,1024]{1,0:T(8,128)(2,1)S(1)} %get-tuple-element.67.refs_0_, ...), custom_call_target="tpu_custom_call", output_to_operand_aliasing={{2}: (1, {})} | custom-call | flops 1 | bytes 1 | tf_op jit(solution)/shard_map/pallas_call | solution.py:93
  136.4 1.3 collective-permute-start.18
  137.7 1.3 collective-permute-start.17
  139.0 4.3 %shard_map.68 = (f32[256,1024]{1,0:T(8,128)}, s32[8,128]{1,0:T(8,128)S(1)}) custom-call(s32[4]{0:T(128)S(1)} %pad_add_fusion.ids, s32[8,128]{1,0:T(8,128)S(1)} %get-tuple-element.80.token, bf16[1024,1024]{1,0:T(8,128)(2,1)S(1)} %get-tuple-element.67.refs_0_, bf16[1024,1024]{1,0:T(8,128)(2,1)} %get-tuple-element.70.refs_1_, ...), custom_call_target="tpu_custom_call", output_to_operand_aliasing={{1}: (1, {})} | custom-call | flops 1 | bytes 1 | tf_op jit(solution)/shard_map/pallas_call | solution.py:93
  143.3 2.7 %shard_map.69 = (bf16[1024,256]{1,0:T(8,128)(2,1)}, s32[8,128]{1,0:T(8,128)S(1)}) custom-call(s32[4]{0:T(128)S(1)} %pad_add_fusion.ids, s32[8,128]{1,0:T(8,128)S(1)} %get-tuple-element.83.token, bf16[1024,1024]{1,0:T(8,128)(2,1)S(1)} %get-tuple-element.67.refs_0_, ...), custom_call_target="tpu_custom_call", output_to_operand_aliasing={{1}: (1, {})} | custom-call | flops 1 | bytes 1 | tf_op jit(solution)/shard_map/pallas_call | solution.py:93
  146.0 1.5 collective-permute-start.19
  147.5 5.2 %shard_map.70 = (f32[1024,1024]{1,0:T(8,128)}, bf16[1024,256]{1,0:T(8,128)(2,1)}, s32[8,128]{1,0:T(8,128)S(1)}) custom-call(s32[4]{0:T(128)S(1)} %pad_add_fusion.ids, s32[8,128]{1,0:T(8,128)S(1)} %get-tuple-element.85.token, bf16[1024,1024]{1,0:T(8,128)(2,1)S(1)} %get-tuple-element.67.refs_0_, ...), custom_call_target="tpu_custom_call", output_to_operand_aliasing={{2}: (1, {})} | custom-call | flops 1 | bytes 1 | tf_op jit(solution)/shard_map/pallas_call | solution.py:93
  152.7 8.5 %collective-permute-done.17.refs_3_ = bf16[1024,256]{1,0:T(8,128)(2,1)S(1)} collective-permute-done((bf16[1024,256]{1,0:T(8,128)(2,1)}, bf16[1024,256]{1,0:T(8,128)(2,1)S(1)}, u32[]{:S(2)}, u32[]{:S(2)}) %collective-permute-start.17) | collective-permute-done | bytes 524320 | tf_op jit(solution)/shard_map/ppermute | solution.py:443
  161.2 5.3 %shard_map.71 = (bf16[8,256,256]{2,1,0:T(8,128)(2,1)}, s32[8,128]{1,0:T(8,128)S(1)}) custom-call(s32[4]{0:T(128)S(1)} %pad_add_fusion.ids, s32[8,128]{1,0:T(8,128)S(1)} %get-tuple-element.88.token, bf16[1024,1024]{1,0:T(8,128)(2,1)S(1)} %get-tuple-element.67.refs_0_, bf16[1024,1024]{1,0:T(8,128)(2,1)} %get-tuple-element.70.refs_1_, ...), custom_call_target="tpu_custom_call", output_to_operand_aliasing={{1}: (1, {})} | custom-call | flops 1 | bytes 1 | tf_op jit(solution)/shard_map/pallas_call | solution.py:93
  166.5 3.9 %all-to-all-start.3 = ((bf16[8,256,256]{2,1,0:T(8,128)(2,1)}), bf16[8,256,256]{2,1,0:T(8,128)(2,1)S(1)}, u32[]{:S(2)}, u32[]{:S(2)}) async-start(bf16[8,256,256]{2,1,0:T(8,128)(2,1)} %get-tuple-element.100), calls=%async_computation.3 | async-start | bytes 2097152 | tf_op jit(solution)/shard_map/all_to_all | solution.py:66
  170.4 2.0 collective-permute-start.20
  172.4 5.2 %shard_map.72 = (f32[1024,1024]{1,0:T(8,128)}, bf16[1024,256]{1,0:T(8,128)(2,1)}, s32[8,128]{1,0:T(8,128)S(1)}) custom-call(s32[4]{0:T(128)S(1)} %pad_add_fusion.ids, s32[8,128]{1,0:T(8,128)S(1)} %get-tuple-element.91.token, bf16[1024,1024]{1,0:T(8,128)(2,1)S(1)} %get-tuple-element.67.refs_0_, ...), custom_call_target="tpu_custom_call", output_to_operand_aliasing={{2}: (1, {}), {0}: (9, {})} | custom-call | flops 1 | bytes 1 | tf_op jit(solution)/shard_map/pallas_call | solution.py:93
  178.4 18.3 %collective-permute-done.20.refs_0_ = bf16[1024,256]{1,0:T(8,128)(2,1)S(1)} collective-permute-done((bf16[1024,256]{1,0:T(8,128)(2,1)}, bf16[1024,256]{1,0:T(8,128)(2,1)S(1)}, u32[]{:S(2)}, u32[]{:S(2)}) %collective-permute-start.20) | collective-permute-done | bytes 524320 | tf_op jit(solution)/shard_map/ppermute | solution.py:51
  196.6 2.9 %shard_map.73 = (f32[1024,1024]{1,0:T(8,128)}, s32[8,128]{1,0:T(8,128)S(1)}) custom-call(s32[4]{0:T(128)S(1)} %pad_add_fusion.ids, s32[8,128]{1,0:T(8,128)S(1)} %get-tuple-element.95.token, bf16[1024,256]{1,0:T(8,128)(2,1)S(1)} %collective-permute-done.20.refs_0_, f32[1024,1024]{1,0:T(8,128)} %bitcast.23, ...), custom_call_target="tpu_custom_call", output_to_operand_aliasing={{1}: (1, {}), {0}: (4, {})} | custom-call | flops 1 | bytes 1 | tf_op jit(solution)/shard_map/pallas_call | solution.py:93
  199.5 5.6 %shard_map.74 = (f32[256,1024]{1,0:T(8,128)}, f32[256,1024]{1,0:T(8,128)}, s32[8,128]{1,0:T(8,128)S(1)}) custom-call(s32[4]{0:T(128)S(1)} %pad_add_fusion.ids, s32[8,128]{1,0:T(8,128)S(1)} %get-tuple-element.98.token, bf16[1024,1024]{1,0:T(8,128)(2,1)S(1)} %get-tuple-element.67.refs_0_, ...), custom_call_target="tpu_custom_call", output_to_operand_aliasing={{2}: (1, {})} | custom-call | flops 1 | bytes 1 | tf_op jit(solution)/shard_map/pallas_call | solution.py:93
  205.1 2.4 %collective-permute-done.21.refs_0_ = bf16[1024,256]{1,0:T(8,128)(2,1)} collective-permute-done((bf16[1024,256]{1,0:T(8,128)(2,1)}, bf16[1024,256]{1,0:T(8,128)(2,1)}, u32[]{:S(2)}, u32[]{:S(2)}) %collective-permute-start.21) | collective-permute-done | bytes 524320 | tf_op jit(solution)/shard_map/ppermute | solution.py:51
  207.5 3.4 %shard_map.75 = (f32[1024,1024]{1,0:T(8,128)}, s32[8,128]{1,0:T(8,128)S(1)}) custom-call(s32[4]{0:T(128)S(1)} %pad_add_fusion.ids, s32[8,128]{1,0:T(8,128)S(1)} %get-tuple-element.103.token, bf16[1024,256]{1,0:T(8,128)(2,1)} %collective-permute-done.21.refs_0_, f32[1024,1024]{1,0:T(8,128)} %bitcast.24, ...), custom_call_target="tpu_custom_call", output_to_operand_aliasing={{1}: (1, {}), {0}: (4, {})} | custom-call | flops 1 | bytes 1 | tf_op jit(solution)/shard_map/pallas_call | solution.py:93
  (40 shorter events, 11.5 us)
Async XLA Ops:
  1.9 13.7 %collective-permute-start = (bf16[256,1024]{1,0:T(8,128)(2,1)S(1)}, bf16[256,1024]{1,0:T(8,128)(2,1)S(1)}, u32[]{:S(2)}, u32[]{:S(2)}) collective-permute-start(bf16[256,1024]{1,0:T(8,128)(2,1)S(1)} %convert_bitcast_fusion), channel_id=1, source_target_pairs={{0,4},{4,0},{1,5},{5,1},{2,6},{6,2},{3,7},{7,3},{8,12},{12,8},{9,1... | collective-permute-start | bytes 1572872 | tf_op jit(solution)/shard_map/ppermute | solution.py:51
  3.5 13.5 %collective-permute-start.1 = (bf16[256,1024]{1,0:T(8,128)(2,1)S(1)}, bf16[256,1024]{1,0:T(8,128)(2,1)}, u32[]{:S(2)}, u32[]{:S(2)}) collective-permute-start(bf16[256,1024]{1,0:T(8,128)(2,1)S(1)} %convert_bitcast_fusion), channel_id=1, source_target_pairs={{0,2},{2,0},{1,3},{3,1},{4,6},{6,4},{5,7},{7,5},{8,10},{10,8},{9,1... | collective-permute-start | bytes 1572872 | tf_op jit(solution)/shard_map/ppermute | solution.py:51
  15.7 0.8 copy-start.2
  16.5 43.3 %copy-start = (f32[1,256,1024]{2,1,0:T(8,128)S(1)}, f32[1,256,1024]{2,1,0:T(8,128)}, u32[]{:S(2)}) copy-start(f32[1,256,1024]{2,1,0:T(8,128)} %refs_4_.1) | copy-start | bytes 3145732
  17.0 1.5 copy-start.3
  18.4 16.8 %copy-start.1 = (bf16[768,1024]{1,0:T(8,128)(2,1)}, bf16[768,1024]{1,0:T(8,128)(2,1)S(1)}, u32[]{:S(2)}) copy-start(bf16[768,1024]{1,0:T(8,128)(2,1)S(1)} %pad_maximum_fusion.refs_0_) | copy-start | bytes 4718596
  18.4 16.8 %collective-permute-start.3 = (bf16[768,1024]{1,0:T(8,128)(2,1)S(1)}, bf16[768,1024]{1,0:T(8,128)(2,1)}, u32[]{:S(2)}, u32[]{:S(2)}) collective-permute-start(bf16[768,1024]{1,0:T(8,128)(2,1)S(1)} %pad_maximum_fusion.refs_0_), channel_id=1, source_target_pairs={{0,1},{1,0},{2,3},{3,2},{4,5},{5,4},{6,7},{7,6},{8,9},{9,8},{10,11... | collective-permute-start | bytes 4718600 | tf_op jit(solution)/shard_map/ppermute | solution.py:51
  18.5 14.4 %collective-permute-start.2 = (bf16[256,1024]{1,0:T(8,128)(2,1)S(1)}, bf16[256,1024]{1,0:T(8,128)(2,1)}, u32[]{:S(2)}, u32[]{:S(2)}) collective-permute-start(bf16[256,1024]{1,0:T(8,128)(2,1)S(1)} %copy-done.3), channel_id=1, source_target_pairs={{0,2},{2,0},{1,3},{3,1},{4,6},{6,4},{5,7},{7,5},{8,10},{10,8},{9,1... | collective-permute-start | bytes 1572872 | tf_op jit(solution)/shard_map/ppermute | solution.py:51
  32.9 2.3 %collective-permute-start.4 = (bf16[256,1024]{1,0:T(8,128)(2,1)}, bf16[256,1024]{1,0:T(8,128)(2,1)}, u32[]{:S(2)}, u32[]{:S(2)}) collective-permute-start(bf16[256,1024]{1,0:T(8,128)(2,1)} %collective-permute-done.2.refs_1_), channel_id=1, source_target_pairs={{0,1},{1,0},{2,3},{3,2},{4,5},{5,4},{6,7},{7,6},{8,9},{9,8},{10,11... | collective-permute-start | bytes 1572872 | tf_op jit(solution)/shard_map/ppermute | solution.py:51
  41.1 16.1 %collective-permute-start.12 = (bf16[256,1024]{1,0:T(8,128)(2,1)}, bf16[256,1024]{1,0:T(8,128)(2,1)S(1)}, u32[]{:S(2)}, u32[]{:S(2)}) collective-permute-start(bf16[256,1024]{1,0:T(8,128)(2,1)} %get-tuple-element.79), channel_id=1, source_target_pairs={{24,16},{8,0},{25,17},{9,1},{26,18},{10,2},{27,19},{11,3},{28,20},... | collective-permute-start | bytes 1572872 | tf_op jit(solution)/shard_map/ppermute | solution.py:417
  42.4 17.4 %collective-permute-start.6 = (bf16[1024,256]{1,0:T(8,128)(2,1)}, bf16[1024,256]{1,0:T(8,128)(2,1)S(1)}, u32[]{:S(2)}, u32[]{:S(2)}) collective-permute-start(bf16[1024,256]{1,0:T(8,128)(2,1)} %get-tuple-element.60), channel_id=1, source_target_pairs={{0,4},{4,0},{1,5},{5,1},{2,6},{6,2},{3,7},{7,3},{8,12},{12,8},{9,1... | collective-permute-start | bytes 1572872 | tf_op jit(solution)/shard_map/ppermute | solution.py:51
  57.2 19.6 %collective-permute-start.13 = (bf16[256,1024]{1,0:T(8,128)(2,1)S(1)}, bf16[256,1024]{1,0:T(8,128)(2,1)S(1)}, u32[]{:S(2)}, u32[]{:S(2)}) collective-permute-start(bf16[256,1024]{1,0:T(8,128)(2,1)S(1)} %collective-permute-done.12), channel_id=1, source_target_pairs={{0,2},{2,0},{1,3},{3,1},{4,6},{6,4},{5,7},{7,5},{8,10},{10,8},{9,1... | collective-permute-start | bytes 1572872 | tf_op jit(solution)/shard_map/ppermute | solution.py:51
  58.7 9.5 %collective-permute-start.5 = (bf16[128,1024]{1,0:T(8,128)(2,1)}, bf16[128,1024]{1,0:T(8,128)(2,1)S(1)}, u32[]{:S(2)}, u32[]{:S(2)}) collective-permute-start(bf16[128,1024]{1,0:T(8,128)(2,1)} %dynamic-slice_bitcast_fusion), channel_id=1, source_target_pairs={{0,4},{4,0},{1,5},{5,1},{2,6},{6,2},{3,7},{7,3},{8,12},{12,8},{9,1... | collective-permute-start | bytes 786440 | tf_op jit(solution)/shard_map/ppermute | solution.py:51
  59.8 21.2 %collective-permute-start.7 = (bf16[1024,256]{1,0:T(8,128)(2,1)}, bf16[1024,256]{1,0:T(8,128)(2,1)}, u32[]{:S(2)}, u32[]{:S(2)}) collective-permute-start(bf16[1024,256]{1,0:T(8,128)(2,1)} %get-tuple-element.63), channel_id=1, source_target_pairs={{0,4},{4,0},{1,5},{5,1},{2,6},{6,2},{3,7},{7,3},{8,12},{12,8},{9,1... | collective-permute-start | bytes 1572872 | tf_op jit(solution)/shard_map/ppermute | solution.py:51
  75.4 20.4 %collective-permute-start.8 = (bf16[1024,256]{1,0:T(8,128)(2,1)}, bf16[1024,256]{1,0:T(8,128)(2,1)}, u32[]{:S(2)}, u32[]{:S(2)}) collective-permute-start(bf16[1024,256]{1,0:T(8,128)(2,1)} %get-tuple-element.68.refs_2_), channel_id=1, source_target_pairs={{24,16},{25,17},{26,18},{27,19},{28,20},{29,21},{30,22},{31,23}} | collective-permute-start | bytes 1572872 | tf_op jit(solution)/shard_map/ppermute | solution.py:391
  76.8 54.5 %collective-permute-start.14 = (bf16[512,1024]{1,0:T(8,128)(2,1)S(1)}, bf16[512,1024]{1,0:T(8,128)(2,1)}, u32[]{:S(2)}, u32[]{:S(2)}) collective-permute-start(bf16[512,1024]{1,0:T(8,128)(2,1)S(1)} %constant_dynamic-update-slice_fusion.refs_3_), channel_id=1, source_target_pairs={{0,1},{1,0},{2,3},{3,2},{4,5},{5,4},{6,7},{7,6},{8,9},{9,8},{10,11... | collective-permute-start | bytes 3145736 | tf_op jit(solution)/shard_map/ppermute | solution.py:51
  76.9 13.4 %all-to-all-start = ((bf16[8,256,128]{2,1,0:T(8,128)(2,1)}), bf16[8,256,128]{2,1,0:T(8,128)(2,1)}, u32[]{:S(2)}, u32[]{:S(2)}) async-start(bf16[8,256,128]{2,1,0:T(8,128)(2,1)} %get-tuple-element.65), calls=%async_computation | async-start | bytes 1048576 | tf_op jit(solution)/shard_map/all_to_all | solution.py:66
  85.3 31.2 %collective-permute-start.10 = (bf16[1024,256]{1,0:T(8,128)(2,1)}, bf16[1024,256]{1,0:T(8,128)(2,1)}, u32[]{:S(2)}, u32[]{:S(2)}) collective-permute-start(bf16[1024,256]{1,0:T(8,128)(2,1)} %get-tuple-element.73.refs_2_), channel_id=1, source_target_pairs={{24,16},{25,17},{26,18},{27,19},{28,20},{29,21},{30,22},{31,23}} | collective-permute-start | bytes 1572872 | tf_op jit(solution)/shard_map/ppermute | solution.py:391
  94.5 13.8 %collective-permute-start.9 = (bf16[1024,128]{1,0:T(8,128)(2,1)}, bf16[1024,128]{1,0:T(8,128)(2,1)S(1)}, u32[]{:S(2)}, u32[]{:S(2)}) collective-permute-start(bf16[1024,128]{1,0:T(8,128)(2,1)} %get-tuple-element.71), channel_id=1, source_target_pairs={{24,16},{8,0},{25,17},{9,1},{26,18},{10,2},{27,19},{11,3},{28,20},... | collective-permute-start | bytes 786440 | tf_op jit(solution)/shard_map/ppermute | solution.py:431
  98.6 28.5 %collective-permute-start.11 = (bf16[1024,256]{1,0:T(8,128)(2,1)}, bf16[1024,256]{1,0:T(8,128)(2,1)}, u32[]{:S(2)}, u32[]{:S(2)}) collective-permute-start(bf16[1024,256]{1,0:T(8,128)(2,1)} %get-tuple-element.75), channel_id=1, source_target_pairs={{16,8},{17,9},{18,10},{19,11},{20,12},{21,13},{22,14},{23,15}} | collective-permute-start | bytes 1572872 | tf_op jit(solution)/shard_map/ppermute | solution.py:391
  112.1 10.9 %all-to-all-start.1 = ((bf16[8,128,128]{2,1,0:T(8,128)(2,1)}), bf16[8,128,128]{2,1,0:T(8,128)(2,1)S(1)}, u32[]{:S(2)}, u32[]{:S(2)}) async-start(bf16[8,128,128]{2,1,0:T(8,128)(2,1)} %bitcast.26), calls=%async_computation.1 | async-start | bytes 524288 | tf_op jit(solution)/shard_map/all_to_all | solution.py:66
  119.2 24.1 %collective-permute-start.15 = (bf16[1024,256]{1,0:T(8,128)(2,1)}, bf16[1024,256]{1,0:T(8,128)(2,1)}, u32[]{:S(2)}, u32[]{:S(2)}) collective-permute-start(bf16[1024,256]{1,0:T(8,128)(2,1)} %get-tuple-element.84), channel_id=1, source_target_pairs={{16,8},{17,9},{18,10},{19,11},{20,12},{21,13},{22,14},{23,15}} | collective-permute-start | bytes 1572872 | tf_op jit(solution)/shard_map/ppermute | solution.py:391
  123.0 16.1 %all-to-all-start.2 = ((bf16[8,256,128]{2,1,0:T(8,128)(2,1)}), bf16[8,256,128]{2,1,0:T(8,128)(2,1)}, u32[]{:S(2)}, u32[]{:S(2)}) async-start(bf16[8,256,128]{2,1,0:T(8,128)(2,1)} %get-tuple-element.82), calls=%async_computation.2 | async-start | bytes 1048576 | tf_op jit(solution)/shard_map/all_to_all | solution.py:66
  129.8 17.6 %collective-permute-start.16 = (bf16[1024,256]{1,0:T(8,128)(2,1)}, bf16[1024,256]{1,0:T(8,128)(2,1)}, u32[]{:S(2)}, u32[]{:S(2)}) collective-permute-start(bf16[1024,256]{1,0:T(8,128)(2,1)} %get-tuple-element.87), channel_id=1, source_target_pairs={{8,0},{9,1},{10,2},{11,3},{12,4},{13,5},{14,6},{15,7}} | collective-permute-start | bytes 1572872 | tf_op jit(solution)/shard_map/ppermute | solution.py:391
  136.4 16.4 %collective-permute-start.18 = (bf16[1024,256]{1,0:T(8,128)(2,1)}, bf16[1024,256]{1,0:T(8,128)(2,1)S(1)}, u32[]{:S(2)}, u32[]{:S(2)}) collective-permute-start(bf16[1024,256]{1,0:T(8,128)(2,1)} %get-tuple-element.90), channel_id=1, source_target_pairs={{16,0},{17,1},{18,2},{19,3},{20,4},{21,5},{22,6},{23,7}} | collective-permute-start | bytes 1572872 | tf_op jit(solution)/shard_map/ppermute | solution.py:443
  137.7 23.5 %collective-permute-start.17 = (bf16[1024,256]{1,0:T(8,128)(2,1)}, bf16[1024,256]{1,0:T(8,128)(2,1)S(1)}, u32[]{:S(2)}, u32[]{:S(2)}) collective-permute-start(bf16[1024,256]{1,0:T(8,128)(2,1)} %get-tuple-element.90), channel_id=1, source_target_pairs={{16,8},{17,9},{18,10},{19,11},{20,12},{21,13},{22,14},{23,15}} | collective-permute-start | bytes 1572872 | tf_op jit(solution)/shard_map/ppermute | solution.py:443
  146.0 26.4 %collective-permute-start.19 = (bf16[1024,256]{1,0:T(8,128)(2,1)}, bf16[1024,256]{1,0:T(8,128)(2,1)}, u32[]{:S(2)}, u32[]{:S(2)}) collective-permute-start(bf16[1024,256]{1,0:T(8,128)(2,1)} %get-tuple-element.93), channel_id=1, source_target_pairs={{8,0},{9,1},{10,2},{11,3},{12,4},{13,5},{14,6},{15,7}} | collective-permute-start | bytes 1572872 | tf_op jit(solution)/shard_map/ppermute | solution.py:391
  166.5 33.0 %all-to-all-start.3 = ((bf16[8,256,256]{2,1,0:T(8,128)(2,1)}), bf16[8,256,256]{2,1,0:T(8,128)(2,1)S(1)}, u32[]{:S(2)}, u32[]{:S(2)}) async-start(bf16[8,256,256]{2,1,0:T(8,128)(2,1)} %get-tuple-element.100), calls=%async_computation.3 | async-start | bytes 2097152 | tf_op jit(solution)/shard_map/all_to_all | solution.py:66
  170.4 26.2 %collective-permute-start.20 = (bf16[1024,256]{1,0:T(8,128)(2,1)}, bf16[1024,256]{1,0:T(8,128)(2,1)S(1)}, u32[]{:S(2)}, u32[]{:S(2)}) collective-permute-start(bf16[1024,256]{1,0:T(8,128)(2,1)} %get-tuple-element.96), channel_id=1, source_target_pairs={{0,4},{4,0},{1,5},{5,1},{2,6},{6,2},{3,7},{7,3},{8,12},{12,8},{9,1... | collective-permute-start | bytes 1572872 | tf_op jit(solution)/shard_map/ppermute | solution.py:51
  177.6 29.8 %collective-permute-start.21 = (bf16[1024,256]{1,0:T(8,128)(2,1)}, bf16[1024,256]{1,0:T(8,128)(2,1)}, u32[]{:S(2)}, u32[]{:S(2)}) collective-permute-start(bf16[1024,256]{1,0:T(8,128)(2,1)} %get-tuple-element.104), channel_id=1, source_target_pairs={{0,4},{4,0},{1,5},{5,1},{2,6},{6,2},{3,7},{7,3},{8,12},{12,8},{9,1... | collective-permute-start | bytes 1572872 | tf_op jit(solution)/shard_map/ppermute | solution.py:51

commit v9 on v8

--- a/solution.py
+++ b/solution.py
@@ -154,7 +154,7 @@
         product(l_low[part:, :])
 
 
-def spread_start_kernel(ids, e0, blocks, spread, l_got, prod, slab, a_low, m):
+def spread_start_kernel(ids, e0, blocks, spread, l_got, unused, prod, slab, a_low, m):
     part = l_got.shape[0]
     gather_lanes(blocks, m, 0, part)
     prod[...] = mm_bt(m[...], e0[...])
@@ -366,13 +366,15 @@
     g_send = [
         lax.dynamic_slice_in_dim(offsets[0], (1 - x) * half + i * width, width, 1).astype(LOW) for i in range(chunks)
     ]
-    l_send, g_send[0], e_x = lax.optimization_barrier((l_send, g_send[0], e_x))
+    tied = lax.optimization_barrier
+    l_got = swap(l_send, "x")
+    l_got, e_x = tied((l_got, e_x))
+    g_send[0], e_x = tied((g_send[0], e_x))
     e_xy = swap(e_x, "y")
-    l_got = swap(l_send, "x")
     g_got = [swap(g_send[0], "x")]
-    for i in range(1, chunks):
-        g_send[i], g_got[-1] = lax.optimization_barrier((g_send[i], g_got[-1]))
-        g_got.append(swap(g_send[i], "x"))
+    g_got[0], e_xy = tied((g_got[0], e_xy))
+    g_send[1], g_got[0] = tied((g_send[1], g_got[0]))
+    g_got.append(swap(g_send[1], "x"))
     three = jnp.concatenate([e_low, e_x, e_y], axis=0)
     pieces = [in_hbm(a) for a in (three, e_xy, swap(three, "c"), swap(e_xy, "c"))]
     offset, spread = in_hbm(offsets[0]), in_hbm(spreads)
@@ -415,32 +417,38 @@
         scratch=[pltpu.VMEM((2, size_d, size_d), LOW), pltpu.SemaphoreType.DMA((8,))],
     )
     quarter = lax.ppermute(quarter, "z", level)
-    quarter_y = swap(quarter, "y")
-    quarters = jnp.concatenate([quarter, quarter_y], axis=0)
-    quarters = [quarters, swap(quarters, "c")]
     (m,) = order.call(spread_kernel, [in_hbm(e0), l_low, l_got], [hbm(8, rows, part)], 8)
     m = exchange(m)
     p0, own0 = start(0)
     gots0 = [down(own0, 3)]
+    quarter, own0 = tied((quarter, own0))
+    quarter_y = swap(quarter, "y")
+    prod, slab, a_low = order.call(
+        spread_start_kernel, [in_hbm(e0), m, spread, l_got, g_got[1]],
+        [hbm(rows, size_d, dtype=WIDE), hbm(size_d, part, dtype=WIDE), hbm(size_d, part)], 12,
+        far_in=(4,), scratch=[slab_rows],
+    )
+    l_next = lax.ppermute(a_low, "z", level)
     p1, own1 = start(1)
     gots1 = [down(own1, 3)]
-    prod, slab, a_low = order.call(
-        spread_start_kernel, [in_hbm(e0), m, spread, l_got],
-        [hbm(rows, size_d, dtype=WIDE), hbm(size_d, part, dtype=WIDE), hbm(size_d, part)], 12, scratch=[slab_rows],
-    )
-    l_next = lax.ppermute(a_low, "z", level)
-    gots0.append(down(hop(gots0[0], own0), 2))
 
     m, near = order.call(spread_hop_kernel, [pair, in_hbm(e1), l_next], [hbm(size_d, part), hbm(8, rows, part)], 10)
     m = exchange(m.reshape(8, part, part))
-    near = exchange(near)
-    gots1.append(down(hop(gots1[0], own1), 2))
-    gots0.append(down(hop(gots0[1], own0), 1))
+    now0 = hop(gots0[0], own0)
+    gots0.append(down(now0, 2))
+    quarter_y, now0 = tied((quarter_y, now0))
+    quarters = jnp.concatenate([quarter, quarter_y], axis=0)
+    quarters = [quarters, swap(quarters, "c")]
     following, far_slab = order.call(
         next_kernel, [pair, in_hbm(slab), m, *quarters], [hbm(size_d, size_d), hbm(size_d, rows)], 12,
         far_in=(3, 4), scratch=[pltpu.VMEM((part, size_d), LOW), pltpu.SemaphoreType.DMA((4,))],
     )
     far = lax.ppermute(far_slab, "z", [(2, 1)]), lax.ppermute(far_slab, "z", [(2, 0)])
+    now1 = hop(gots1[0], own1)
+    gots1.append(down(now1, 2))
+    near, now1 = tied((near, now1))
+    near = exchange(near)
+    gots0.append(down(hop(gots0[1], own0), 1))
     (near,) = order.call(
         near_kernel, [pair, in_hbm(e1), in_hbm(prod), near, spread], [hbm(rows, size_d, dtype=WIDE)], 12,
         scratch=[slab_rows],

time: 213 us -> 204 us (0.958)
  the two profiles are of different devices: /device:TPU:16 before, /device:TPU:0 now
where the time goes in v9:
time: 204 us; the launch traced here: 202 us
  Pallas kernels  73 us (36%)
  waiting for transfers between devices  70.9 us (35%)
  starting transfers between devices  37.9 us (19%)
  blocking collectives  8.85 us (4%)
  local copies, waits for them, and re-layouts  6.47 us (3%)
  other arithmetic  4.11 us (2%)
    pallas_call x18, Pallas kernels, call(): pl.pallas_call(body, in_specs=[SMEM, ANY] + [ANY if i in far_in else VMEM...  73 us
    ppermute x12, waiting for transfers between devices, swap(): return lax.ppermute(value, axis, [(0, 1), (1, 0)])  45.5 us
    ppermute x6, waiting for transfers between devices, down(): return lax.ppermute(value, 'z', [(source, source - 1)])  13.9 us
    ppermute x12, starting transfers between devices, swap(): return lax.ppermute(value, axis, [(0, 1), (1, 0)])  13.2 us
    all_to_all x3, starting transfers between devices, exchange(): return lax.all_to_all(blocks, GROUP, 0, 0)  12.4 us
    all_to_all x1, blocking collectives, exchange(): return lax.all_to_all(blocks, GROUP, 0, 0)  8.85 us
    ppermute x6, starting transfers between devices, down(): return lax.ppermute(value, 'z', [(source, source - 1)])  6.93 us
    all_to_all x3, waiting for transfers between devices, exchange(): return lax.all_to_all(blocks, GROUP, 0, 0)  6.01 us
  transfers between devices with their start and end apart: 25, of which 11 were waited for; matrix products, arithmetic and copies ran while one was open for 3% of the time, Pallas kernels for 32%

profile of v9, /device:TPU:0, one launch (start us, length us, event | category | flops | bytes accessed | tf_op | source)
XLA Modules:
  0.0 202.3 jit_solution(2239203683495150569)
XLA Ops:
  0.6 1.3 convert_bitcast_fusion
  1.9 3.0 %collective-permute-start.1 = (bf16[256,1024]{1,0:T(8,128)(2,1)S(1)}, bf16[256,1024]{1,0:T(8,128)(2,1)S(1)}, u32[]{:S(2)}, u32[]{:S(2)}) collective-permute-start(bf16[256,1024]{1,0:T(8,128)(2,1)S(1)} %convert_bitcast_fusion), channel_id=1, source_target_pairs={{0,4},{4,0},{1,5},{5,1},{2,6},{6,2},{3,7},{7,3},{8,12},{12,8},{9,1... | collective-permute-start | bytes 1572872 | tf_op jit(solution)/shard_map/ppermute | solution.py:51
  4.9 1.5 collective-permute-start.2
  6.5 1.3 convert_element_type.27
  8.4 2.4 %fusion.1 = (bf16[1024,256]{1,0:T(8,128)(2,1)}, bf16[1024,256]{1,0:T(8,128)(2,1)S(1)}) fusion(f32[1,1024,1024]{2,1,0:T(8,128)} %param.5, s32[]{:T(128)S(6)} %select_n.11, s32[]{:T(128)S(6)} %select_n.9), kind=kLoop, calls=%fused_computation.4 | loop fusion | bytes 2097160 | tf_op jit(solution)/shard_map/convert_element_type | solution.py:367
  10.8 11.6 %collective-permute-done.refs_2_.refs_3_ = bf16[128,1024]{1,0:T(8,128)(2,1)S(1)} collective-permute-done((bf16[128,1024]{1,0:T(8,128)(2,1)S(1)}, bf16[128,1024]{1,0:T(8,128)(2,1)S(1)}, u32[]{:S(2)}, u32[]{:S(2)}) %collective-permute-start) | collective-permute-done | bytes 262176 | tf_op jit(solution)/shard_map/ppermute | solution.py:51
  22.7 1.8 collective-permute-start.3
  24.5 1.5 collective-permute-start.4
  26.1 11.0 %collective-permute-done.3.refs_1_ = bf16[1024,256]{1,0:T(8,128)(2,1)S(1)} collective-permute-done((bf16[1024,256]{1,0:T(8,128)(2,1)S(1)}, bf16[1024,256]{1,0:T(8,128)(2,1)S(1)}, u32[]{:S(2)}, u32[]{:S(2)}) %collective-permute-start.3) | collective-permute-done | bytes 524320 | tf_op jit(solution)/shard_map/ppermute | solution.py:51
  37.1 1.5 collective-permute-done.4.refs_1_
  38.6 1.8 collective-permute-done.6.refs_3_
  41.2 5.9 %shard_map.58 = (bf16[1024,1024]{1,0:T(8,128)(2,1)}, bf16[1024,1024]{1,0:T(8,128)(2,1)}, bf16[1024,1024]{1,0:T(8,128)(2,1)S(1)}, bf16[256,1024]{1,0:T(8,128)(2,1)}, s32[8,128]{1,0:T(8,128)S(1)}) custom-call(s32[4]{0:T(128)S(1)} %pad_add_fusion.ids, s32[8,128]{1,0:T(8,128)S(1)} %broadcast_in_dim.12.token, ...), custom_call_target="tpu_custom_call", output_to_operand_aliasing={{4}: (1, {})} | custom-call | flops 1 | bytes 1 | tf_op jit(solution)/shard_map/pallas_call | solution.py:93
  47.2 1.3 collective-permute-start.10
  48.9 1.3 convert_bitcast_fusion.1.refs_1_
  50.2 3.1 %shard_map.59 = (bf16[8,256,128]{2,1,0:T(8,128)(2,1)}, s32[8,128]{1,0:T(8,128)S(1)}) custom-call(s32[4]{0:T(128)S(1)} %pad_add_fusion.ids, s32[8,128]{1,0:T(8,128)S(1)} %get-tuple-element.66.token, bf16[1024,1024]{1,0:T(8,128)(2,1)} %get-tuple-element.67.refs_0_, ...), custom_call_target="tpu_custom_call", output_to_operand_aliasing={{1}: (1, {})} | custom-call | flops 1 | bytes 1 | tf_op jit(solution)/shard_map/pallas_call | solution.py:93
  53.3 4.1 %all-to-all-start = ((bf16[8,256,128]{2,1,0:T(8,128)(2,1)}), bf16[8,256,128]{2,1,0:T(8,128)(2,1)}, u32[]{:S(2)}, u32[]{:S(2)}) async-start(bf16[8,256,128]{2,1,0:T(8,128)(2,1)} %get-tuple-element.73), calls=%async_computation | async-start | bytes 1048576 | tf_op jit(solution)/shard_map/all_to_all | solution.py:66
  57.4 4.1 %shard_map.60 = (f32[1024,256]{1,0:T(8,128)}, bf16[1024,256]{1,0:T(8,128)(2,1)}, s32[8,128]{1,0:T(8,128)S(1)}) custom-call(s32[4]{0:T(128)S(1)} %pad_add_fusion.ids, s32[8,128]{1,0:T(8,128)S(1)} %get-tuple-element.69.token, bf16[1024,1024]{1,0:T(8,128)(2,1)} %get-tuple-element.67.refs_0_, ...), custom_call_target="tpu_custom_call", output_to_operand_aliasing={{2}: (1, {})} | custom-call | flops 1 | bytes 1 | tf_op jit(solution)/shard_map/pallas_call | solution.py:93
  63.4 1.5 collective-permute-start.11
  64.9 3.8 %all-to-all-done.refs_1_ = bf16[8,256,128]{2,1,0:T(8,128)(2,1)} async-done(((bf16[8,256,128]{2,1,0:T(8,128)(2,1)}), bf16[8,256,128]{2,1,0:T(8,128)(2,1)}, u32[]{:S(2)}, u32[]{:S(2)}) %all-to-all-start) | async-done | bytes 524320 | tf_op jit(solution)/shard_map/all_to_all | solution.py:66
  68.7 4.2 %shard_map.61 = (f32[256,1024]{1,0:T(8,128)}, f32[1024,128]{1,0:T(8,128)}, bf16[1024,128]{1,0:T(8,128)(2,1)}, s32[8,128]{1,0:T(8,128)S(1)}) custom-call(s32[4]{0:T(128)S(1)} %pad_add_fusion.ids, s32[8,128]{1,0:T(8,128)S(1)} %get-tuple-element.72.token, bf16[1024,1024]{1,0:T(8,128)(2,1)} %get-tuple-element.67.refs_0_, ...), custom_call_target="tpu_custom_call", output_to_operand_aliasing={{3}: (1, {})} | custom-call | flops 1 | bytes 1 | tf_op jit(solution)/shard_map/pallas_call | solution.py:93
  72.9 1.3 collective-permute-start.8
  74.2 4.1 %shard_map.62 = (f32[1024,256]{1,0:T(8,128)}, bf16[1024,256]{1,0:T(8,128)(2,1)}, s32[8,128]{1,0:T(8,128)S(1)}) custom-call(s32[4]{0:T(128)S(1)} %pad_add_fusion.ids, s32[8,128]{1,0:T(8,128)S(1)} %get-tuple-element.75.token, bf16[1024,1024]{1,0:T(8,128)(2,1)} %get-tuple-element.67.refs_0_, ...), custom_call_target="tpu_custom_call", output_to_operand_aliasing={{2}: (1, {})} | custom-call | flops 1 | bytes 1 | tf_op jit(solution)/shard_map/pallas_call | solution.py:93
  79.4 4.5 %collective-permute-done.8.refs_2_ = bf16[1024,128]{1,0:T(8,128)(2,1)S(1)} collective-permute-done((bf16[1024,128]{1,0:T(8,128)(2,1)}, bf16[1024,128]{1,0:T(8,128)(2,1)S(1)}, u32[]{:S(2)}, u32[]{:S(2)}) %collective-permute-start.8) | collective-permute-done | bytes 262176 | tf_op jit(solution)/shard_map/ppermute | solution.py:431
  83.9 3.7 %shard_map.63 = (bf16[1024,128]{1,0:T(8,128)(2,1)}, bf16[8,256,128]{2,1,0:T(8,128)(2,1)}, s32[8,128]{1,0:T(8,128)S(1)}) custom-call(s32[4]{0:T(128)S(1)} %pad_add_fusion.ids, s32[8,128]{1,0:T(8,128)S(1)} %get-tuple-element.76.token, bf16[1024,1024]{1,0:T(8,128)(2,1)S(1)} %get-tuple-element.77.refs_0_, ...), custom_call_target="tpu_custom_call", output_to_operand_aliasing={{2}: (1, {})} | custom-call | flops 1 | bytes 1 | tf_op jit(solution)/shard_map/pallas_call | solution.py:93
  87.6 2.6 %shard_map.64 = (bf16[1024,256]{1,0:T(8,128)(2,1)}, s32[8,128]{1,0:T(8,128)S(1)}) custom-call(s32[4]{0:T(128)S(1)} %pad_add_fusion.ids, s32[8,128]{1,0:T(8,128)S(1)} %get-tuple-element.80.token, bf16[1024,1024]{1,0:T(8,128)(2,1)S(1)} %get-tuple-element.77.refs_0_, ...), custom_call_target="tpu_custom_call", output_to_operand_aliasing={{1}: (1, {})} | custom-call | flops 1 | bytes 1 | tf_op jit(solution)/shard_map/pallas_call | solution.py:93
  92.1 1.5 collective-permute-start.14
  93.6 8.9 %all_to_all.20.refs_2_ = bf16[8,128,128]{2,1,0:T(8,128)(2,1)S(1)} all-to-all(bf16[8,128,128]{2,1,0:T(8,128)(2,1)S(1)} %bitcast.26), channel_id=1, replica_groups=mesh['z'=4,'x'=2,'y'=2,'c'=2] {'y','c','x'}, dimensions={0} | all-to-all | bytes 524288 | tf_op jit(solution)/shard_map/all_to_all | solution.py:66
  102.5 5.2 %shard_map.65 = (bf16[1024,1024]{1,0:T(8,128)(2,1)}, bf16[1024,256]{1,0:T(8,128)(2,1)}, s32[8,128]{1,0:T(8,128)S(1)}) custom-call(s32[4]{0:T(128)S(1)} %pad_add_fusion.ids, s32[8,128]{1,0:T(8,128)S(1)} %get-tuple-element.84.token, bf16[1024,1024]{1,0:T(8,128)(2,1)S(1)} %get-tuple-element.77.refs_0_, ...), custom_call_target="tpu_custom_call", output_to_operand_aliasing={{2}: (1, {})} | custom-call | flops 1 | bytes 1 | tf_op jit(solution)/shard_map/pallas_call | solution.py:93
  107.7 2.7 %shard_map.66 = (bf16[1024,256]{1,0:T(8,128)(2,1)}, s32[8,128]{1,0:T(8,128)S(1)}) custom-call(s32[4]{0:T(128)S(1)} %pad_add_fusion.ids, s32[8,128]{1,0:T(8,128)S(1)} %get-tuple-element.90.token, bf16[1024,1024]{1,0:T(8,128)(2,1)S(1)} %get-tuple-element.77.refs_0_, ...), custom_call_target="tpu_custom_call", output_to_operand_aliasing={{1}: (1, {})} | custom-call | flops 1 | bytes 1 | tf_op jit(solution)/shard_map/pallas_call | solution.py:93
  110.4 1.5 collective-permute-start.15
  111.9 3.7 %all-to-all-start.2 = ((bf16[8,256,128]{2,1,0:T(8,128)(2,1)}), bf16[8,256,128]{2,1,0:T(8,128)(2,1)S(1)}, u32[]{:S(2)}, u32[]{:S(2)}) async-start(bf16[8,256,128]{2,1,0:T(8,128)(2,1)} %get-tuple-element.97), calls=%async_computation.2 | async-start | bytes 1048576 | tf_op jit(solution)/shard_map/all_to_all | solution.py:66
  115.6 2.7 %shard_map.67 = (bf16[1024,256]{1,0:T(8,128)(2,1)}, s32[8,128]{1,0:T(8,128)S(1)}) custom-call(s32[4]{0:T(128)S(1)} %pad_add_fusion.ids, s32[8,128]{1,0:T(8,128)S(1)} %get-tuple-element.92.token, bf16[1024,1024]{1,0:T(8,128)(2,1)S(1)} %get-tuple-element.77.refs_0_, ...), custom_call_target="tpu_custom_call", output_to_operand_aliasing={{1}: (1, {})} | custom-call | flops 1 | bytes 1 | tf_op jit(solution)/shard_map/pallas_call | solution.py:93
  119.6 1.3 collective-permute-start.18
  120.9 1.5 collective-permute-start.17
  122.4 2.2 %all-to-all-done.2.refs_3_ = bf16[8,256,128]{2,1,0:T(8,128)(2,1)S(1)} async-done(((bf16[8,256,128]{2,1,0:T(8,128)(2,1)}), bf16[8,256,128]{2,1,0:T(8,128)(2,1)S(1)}, u32[]{:S(2)}, u32[]{:S(2)}) %all-to-all-start.2) | async-done | bytes 524320 | tf_op jit(solution)/shard_map/all_to_all | solution.py:66
  124.6 4.1 %shard_map.68 = (f32[256,1024]{1,0:T(8,128)}, s32[8,128]{1,0:T(8,128)S(1)}) custom-call(s32[4]{0:T(128)S(1)} %pad_add_fusion.ids, s32[8,128]{1,0:T(8,128)S(1)} %get-tuple-element.93.token, bf16[1024,1024]{1,0:T(8,128)(2,1)S(1)} %get-tuple-element.77.refs_0_, bf16[1024,1024]{1,0:T(8,128)(2,1)} %get-tuple-element.78.refs_1_, ...), custom_call_target="tpu_custom_call", output_to_operand_aliasing={{1}: (1, {})} | custom-call | flops 1 | bytes 1 | tf_op jit(solution)/shard_map/pallas_call | solution.py:93
  128.7 2.7 %shard_map.69 = (bf16[1024,256]{1,0:T(8,128)(2,1)}, s32[8,128]{1,0:T(8,128)S(1)}) custom-call(s32[4]{0:T(128)S(1)} %pad_add_fusion.ids, s32[8,128]{1,0:T(8,128)S(1)} %get-tuple-element.98.token, bf16[1024,1024]{1,0:T(8,128)(2,1)S(1)} %get-tuple-element.77.refs_0_, ...), custom_call_target="tpu_custom_call", output_to_operand_aliasing={{1}: (1, {})} | custom-call | flops 1 | bytes 1 | tf_op jit(solution)/shard_map/pallas_call | solution.py:93
  132.7 13.8 %collective-permute-done.16.refs_5_ = bf16[1024,256]{1,0:T(8,128)(2,1)} collective-permute-done((bf16[1024,256]{1,0:T(8,128)(2,1)}, bf16[1024,256]{1,0:T(8,128)(2,1)}, u32[]{:S(2)}, u32[]{:S(2)}) %collective-permute-start.16) | collective-permute-done | bytes 524320 | tf_op jit(solution)/shard_map/ppermute | solution.py:393
  146.5 5.2 %shard_map.70 = (f32[1024,1024]{1,0:T(8,128)}, bf16[1024,256]{1,0:T(8,128)(2,1)}, s32[8,128]{1,0:T(8,128)S(1)}) custom-call(s32[4]{0:T(128)S(1)} %pad_add_fusion.ids, s32[8,128]{1,0:T(8,128)S(1)} %get-tuple-element.99.token, bf16[1024,1024]{1,0:T(8,128)(2,1)S(1)} %get-tuple-element.77.refs_0_, ...), custom_call_target="tpu_custom_call", output_to_operand_aliasing={{2}: (1, {})} | custom-call | flops 1 | bytes 1 | tf_op jit(solution)/shard_map/pallas_call | solution.py:93
  151.7 5.5 %shard_map.71 = (bf16[8,256,256]{2,1,0:T(8,128)(2,1)}, s32[8,128]{1,0:T(8,128)S(1)}) custom-call(s32[4]{0:T(128)S(1)} %pad_add_fusion.ids, s32[8,128]{1,0:T(8,128)S(1)} %get-tuple-element.102.token, bf16[1024,1024]{1,0:T(8,128)(2,1)S(1)} %get-tuple-element.77.refs_0_, bf16[1024,1024]{1,0:T(8,128)(2,1)} %get-tuple-element.78.refs_1_, ...), custom_call_target="tpu_custom_call", output_to_operand_aliasing={{1}: (1, {})} | custom-call | flops 1 | bytes 1 | tf_op jit(solution)/shard_map/pallas_call | solution.py:93
  157.2 4.5 %all-to-all-start.3 = ((bf16[8,256,256]{2,1,0:T(8,128)(2,1)}), bf16[8,256,256]{2,1,0:T(8,128)(2,1)S(1)}, u32[]{:S(2)}, u32[]{:S(2)}) async-start(bf16[8,256,256]{2,1,0:T(8,128)(2,1)} %get-tuple-element.114), calls=%async_computation.3 | async-start | bytes 2097152 | tf_op jit(solution)/shard_map/all_to_all | solution.py:66
  161.8 2.0 collective-permute-start.20
  164.8 5.3 %shard_map.72 = (f32[1024,1024]{1,0:T(8,128)}, bf16[1024,256]{1,0:T(8,128)(2,1)}, s32[8,128]{1,0:T(8,128)S(1)}) custom-call(s32[4]{0:T(128)S(1)} %pad_add_fusion.ids, s32[8,128]{1,0:T(8,128)S(1)} %get-tuple-element.105.token, bf16[1024,1024]{1,0:T(8,128)(2,1)S(1)} %get-tuple-element.77.refs_0_, ...), custom_call_target="tpu_custom_call", output_to_operand_aliasing={{2}: (1, {}), {0}: (9, {})} | custom-call | flops 1 | bytes 1 | tf_op jit(solution)/shard_map/pallas_call | solution.py:93
  170.8 17.2 %collective-permute-done.20.refs_0_ = bf16[1024,256]{1,0:T(8,128)(2,1)S(1)} collective-permute-done((bf16[1024,256]{1,0:T(8,128)(2,1)}, bf16[1024,256]{1,0:T(8,128)(2,1)S(1)}, u32[]{:S(2)}, u32[]{:S(2)}) %collective-permute-start.20) | collective-permute-done | bytes 524320 | tf_op jit(solution)/shard_map/ppermute | solution.py:51
  188.0 2.9 %shard_map.73 = (f32[1024,1024]{1,0:T(8,128)}, s32[8,128]{1,0:T(8,128)S(1)}) custom-call(s32[4]{0:T(128)S(1)} %pad_add_fusion.ids, s32[8,128]{1,0:T(8,128)S(1)} %get-tuple-element.109.token, bf16[1024,256]{1,0:T(8,128)(2,1)S(1)} %collective-permute-done.20.refs_0_, f32[1024,1024]{1,0:T(8,128)} %bitcast.23, ...), custom_call_target="tpu_custom_call", output_to_operand_aliasing={{1}: (1, {}), {0}: (4, {})} | custom-call | flops 1 | bytes 1 | tf_op jit(solution)/shard_map/pallas_call | solution.py:93
  190.9 5.6 %shard_map.74 = (f32[256,1024]{1,0:T(8,128)}, f32[256,1024]{1,0:T(8,128)}, s32[8,128]{1,0:T(8,128)S(1)}) custom-call(s32[4]{0:T(128)S(1)} %pad_add_fusion.ids, s32[8,128]{1,0:T(8,128)S(1)} %get-tuple-element.112.token, bf16[1024,1024]{1,0:T(8,128)(2,1)S(1)} %get-tuple-element.77.refs_0_, ...), custom_call_target="tpu_custom_call", output_to_operand_aliasing={{2}: (1, {})} | custom-call | flops 1 | bytes 1 | tf_op jit(solution)/shard_map/pallas_call | solution.py:93
  196.5 2.4 %collective-permute-done.21.refs_0_ = bf16[1024,256]{1,0:T(8,128)(2,1)} collective-permute-done((bf16[1024,256]{1,0:T(8,128)(2,1)}, bf16[1024,256]{1,0:T(8,128)(2,1)}, u32[]{:S(2)}, u32[]{:S(2)}) %collective-permute-start.21) | collective-permute-done | bytes 524320 | tf_op jit(solution)/shard_map/ppermute | solution.py:51
  198.8 3.4 %shard_map.75 = (f32[1024,1024]{1,0:T(8,128)}, s32[8,128]{1,0:T(8,128)S(1)}) custom-call(s32[4]{0:T(128)S(1)} %pad_add_fusion.ids, s32[8,128]{1,0:T(8,128)S(1)} %get-tuple-element.117.token, bf16[1024,256]{1,0:T(8,128)(2,1)} %collective-permute-done.21.refs_0_, f32[1024,1024]{1,0:T(8,128)} %bitcast.24, ...), custom_call_target="tpu_custom_call", output_to_operand_aliasing={{1}: (1, {}), {0}: (4, {})} | custom-call | flops 1 | bytes 1 | tf_op jit(solution)/shard_map/pallas_call | solution.py:93
  (45 shorter events, 11.2 us)
Async XLA Ops:
  1.9 20.5 %collective-permute-start.1 = (bf16[256,1024]{1,0:T(8,128)(2,1)S(1)}, bf16[256,1024]{1,0:T(8,128)(2,1)S(1)}, u32[]{:S(2)}, u32[]{:S(2)}) collective-permute-start(bf16[256,1024]{1,0:T(8,128)(2,1)S(1)} %convert_bitcast_fusion), channel_id=1, source_target_pairs={{0,4},{4,0},{1,5},{5,1},{2,6},{6,2},{3,7},{7,3},{8,12},{12,8},{9,1... | collective-permute-start | bytes 1572872 | tf_op jit(solution)/shard_map/ppermute | solution.py:51
  4.9 17.5 %collective-permute-start.2 = (bf16[256,1024]{1,0:T(8,128)(2,1)S(1)}, bf16[256,1024]{1,0:T(8,128)(2,1)S(1)}, u32[]{:S(2)}, u32[]{:S(2)}) collective-permute-start(bf16[256,1024]{1,0:T(8,128)(2,1)S(1)} %convert_bitcast_fusion), channel_id=1, source_target_pairs={{0,2},{2,0},{1,3},{3,1},{4,6},{6,4},{5,7},{7,5},{8,10},{10,8},{9,1... | collective-permute-start | bytes 1572872 | tf_op jit(solution)/shard_map/ppermute | solution.py:51
  7.8 14.7 %collective-permute-start = (bf16[128,1024]{1,0:T(8,128)(2,1)S(1)}, bf16[128,1024]{1,0:T(8,128)(2,1)S(1)}, u32[]{:S(2)}, u32[]{:S(2)}) collective-permute-start(bf16[128,1024]{1,0:T(8,128)(2,1)S(1)} %dynamic-slice_bitcast_fusion), channel_id=1, source_target_pairs={{0,4},{4,0},{1,5},{5,1},{2,6},{6,2},{3,7},{7,3},{8,12},{12,8},{9,1... | collective-permute-start | bytes 786440 | tf_op jit(solution)/shard_map/ppermute | solution.py:51
  22.6 17.8 %copy-start.2 = (bf16[768,1024]{1,0:T(8,128)(2,1)}, bf16[768,1024]{1,0:T(8,128)(2,1)S(1)}, u32[]{:S(2)}) copy-start(bf16[768,1024]{1,0:T(8,128)(2,1)S(1)} %pad_maximum_fusion.refs_0_) | copy-start | bytes 4718596
  22.7 17.8 %collective-permute-start.5 = (bf16[768,1024]{1,0:T(8,128)(2,1)S(1)}, bf16[768,1024]{1,0:T(8,128)(2,1)}, u32[]{:S(2)}, u32[]{:S(2)}) collective-permute-start(bf16[768,1024]{1,0:T(8,128)(2,1)S(1)} %pad_maximum_fusion.refs_0_), channel_id=1, source_target_pairs={{0,1},{1,0},{2,3},{3,2},{4,5},{5,4},{6,7},{7,6},{8,9},{9,8},{10,11... | collective-permute-start | bytes 4718600 | tf_op jit(solution)/shard_map/ppermute | solution.py:51
  22.7 14.3 %collective-permute-start.3 = (bf16[1024,256]{1,0:T(8,128)(2,1)S(1)}, bf16[1024,256]{1,0:T(8,128)(2,1)S(1)}, u32[]{:S(2)}, u32[]{:S(2)}) collective-permute-start(bf16[1024,256]{1,0:T(8,128)(2,1)S(1)} %get-tuple-element.64), channel_id=1, source_target_pairs={{0,4},{4,0},{1,5},{5,1},{2,6},{6,2},{3,7},{7,3},{8,12},{12,8},{9,1... | collective-permute-start | bytes 1572872 | tf_op jit(solution)/shard_map/ppermute | solution.py:51
  24.5 14.0 %collective-permute-start.4 = (bf16[256,1024]{1,0:T(8,128)(2,1)S(1)}, bf16[256,1024]{1,0:T(8,128)(2,1)S(1)}, u32[]{:S(2)}, u32[]{:S(2)}) collective-permute-start(bf16[256,1024]{1,0:T(8,128)(2,1)S(1)} %collective-permute-done.1), channel_id=1, source_target_pairs={{0,2},{2,0},{1,3},{3,1},{4,6},{6,4},{5,7},{7,5},{8,10},{10,8},{9,1... | collective-permute-start | bytes 1572872 | tf_op jit(solution)/shard_map/ppermute | solution.py:51
  38.5 2.7 %copy-start.4 = (bf16[256,1024]{1,0:T(8,128)(2,1)}, bf16[256,1024]{1,0:T(8,128)(2,1)S(1)}, u32[]{:S(2)}) copy-start(bf16[256,1024]{1,0:T(8,128)(2,1)S(1)} %collective-permute-done.4.refs_1_) | copy-start | bytes 1572868
  38.5 1.9 collective-permute-start.6
  40.4 0.8 copy-start.5
  47.2 16.2 %collective-permute-start.10 = (bf16[256,1024]{1,0:T(8,128)(2,1)}, bf16[256,1024]{1,0:T(8,128)(2,1)}, u32[]{:S(2)}, u32[]{:S(2)}) collective-permute-start(bf16[256,1024]{1,0:T(8,128)(2,1)} %get-tuple-element.82), channel_id=1, source_target_pairs={{24,16},{8,0},{25,17},{9,1},{26,18},{10,2},{27,19},{11,3},{28,20},... | collective-permute-start | bytes 1572872 | tf_op jit(solution)/shard_map/ppermute | solution.py:419
  48.5 16.4 %collective-permute-start.7 = (bf16[1024,256]{1,0:T(8,128)(2,1)}, bf16[1024,256]{1,0:T(8,128)(2,1)S(1)}, u32[]{:S(2)}, u32[]{:S(2)}) collective-permute-start(bf16[1024,256]{1,0:T(8,128)(2,1)} %get-tuple-element.74), channel_id=1, source_target_pairs={{0,4},{4,0},{1,5},{5,1},{2,6},{6,2},{3,7},{7,3},{8,12},{12,8},{9,1... | collective-permute-start | bytes 1572872 | tf_op jit(solution)/shard_map/ppermute | solution.py:51
  53.3 15.4 %all-to-all-start = ((bf16[8,256,128]{2,1,0:T(8,128)(2,1)}), bf16[8,256,128]{2,1,0:T(8,128)(2,1)}, u32[]{:S(2)}, u32[]{:S(2)}) async-start(bf16[8,256,128]{2,1,0:T(8,128)(2,1)} %get-tuple-element.73), calls=%async_computation | async-start | bytes 1048576 | tf_op jit(solution)/shard_map/all_to_all | solution.py:66
  61.6 26.0 %collective-permute-start.9 = (bf16[1024,256]{1,0:T(8,128)(2,1)}, bf16[1024,256]{1,0:T(8,128)(2,1)S(1)}, u32[]{:S(2)}, u32[]{:S(2)}) collective-permute-start(bf16[1024,256]{1,0:T(8,128)(2,1)} %get-tuple-element.83.refs_2_), channel_id=1, source_target_pairs={{24,16},{25,17},{26,18},{27,19},{28,20},{29,21},{30,22},{31,23}} | collective-permute-start | bytes 1572872 | tf_op jit(solution)/shard_map/ppermute | solution.py:393
  63.4 26.9 %collective-permute-start.11 = (bf16[256,1024]{1,0:T(8,128)(2,1)}, bf16[256,1024]{1,0:T(8,128)(2,1)}, u32[]{:S(2)}, u32[]{:S(2)}) collective-permute-start(bf16[256,1024]{1,0:T(8,128)(2,1)} %collective-permute-done.10), channel_id=1, source_target_pairs={{0,2},{2,0},{1,3},{3,1},{4,6},{6,4},{5,7},{7,5},{8,10},{10,8},{9,1... | collective-permute-start | bytes 1572872 | tf_op jit(solution)/shard_map/ppermute | solution.py:51
  72.9 11.0 %collective-permute-start.8 = (bf16[1024,128]{1,0:T(8,128)(2,1)}, bf16[1024,128]{1,0:T(8,128)(2,1)S(1)}, u32[]{:S(2)}, u32[]{:S(2)}) collective-permute-start(bf16[1024,128]{1,0:T(8,128)(2,1)} %get-tuple-element.79), channel_id=1, source_target_pairs={{24,16},{8,0},{25,17},{9,1},{26,18},{10,2},{27,19},{11,3},{28,20},... | collective-permute-start | bytes 786440 | tf_op jit(solution)/shard_map/ppermute | solution.py:431
  87.6 3.8 %copy-start.3 = (bf16[1024,256]{1,0:T(8,128)(2,1)S(1)}, bf16[1024,256]{1,0:T(8,128)(2,1)}, u32[]{:S(2)}) copy-start(bf16[1024,256]{1,0:T(8,128)(2,1)} %get-tuple-element.91.refs_2_) | copy-start | bytes 1572868
  87.6 6.0 %copy-start.6 = (bf16[1024,128]{1,0:T(8,128)(2,1)S(1)}, bf16[1024,128]{1,0:T(8,128)(2,1)}, u32[]{:S(2)}) copy-start(bf16[1024,128]{1,0:T(8,128)(2,1)} %get-tuple-element.86) | copy-start | bytes 786436
  91.3 11.2 %collective-permute-start.12 = (bf16[512,1024]{1,0:T(8,128)(2,1)S(1)}, bf16[512,1024]{1,0:T(8,128)(2,1)S(1)}, u32[]{:S(2)}, u32[]{:S(2)}) collective-permute-start(bf16[512,1024]{1,0:T(8,128)(2,1)S(1)} %constant_dynamic-update-slice_fusion.refs_3_), channel_id=1, source_target_pairs={{0,1},{1,0},{2,3},{3,2},{4,5},{5,4},{6,7},{7,6},{8,9},{9,8},{10,11... | collective-permute-start | bytes 3145736 | tf_op jit(solution)/shard_map/ppermute | solution.py:51
  91.4 16.2 %collective-permute-start.13 = (bf16[1024,256]{1,0:T(8,128)(2,1)S(1)}, bf16[1024,256]{1,0:T(8,128)(2,1)S(1)}, u32[]{:S(2)}, u32[]{:S(2)}) collective-permute-start(bf16[1024,256]{1,0:T(8,128)(2,1)S(1)} %copy-done.3), channel_id=1, source_target_pairs={{24,16},{25,17},{26,18},{27,19},{28,20},{29,21},{30,22},{31,23}} | collective-permute-start | bytes 1572872 | tf_op jit(solution)/shard_map/ppermute | solution.py:393
  92.1 23.5 %collective-permute-start.14 = (bf16[1024,256]{1,0:T(8,128)(2,1)}, bf16[1024,256]{1,0:T(8,128)(2,1)}, u32[]{:S(2)}, u32[]{:S(2)}) collective-permute-start(bf16[1024,256]{1,0:T(8,128)(2,1)} %get-tuple-element.88), channel_id=1, source_target_pairs={{16,8},{17,9},{18,10},{19,11},{20,12},{21,13},{22,14},{23,15}} | collective-permute-start | bytes 1572872 | tf_op jit(solution)/shard_map/ppermute | solution.py:393
  107.7 4.2 %copy-start = (bf16[1024,256]{1,0:T(8,128)(2,1)}, bf16[1024,256]{1,0:T(8,128)(2,1)S(1)}, u32[]{:S(2)}) copy-start(bf16[1024,256]{1,0:T(8,128)(2,1)S(1)} %collective-permute-done.13.refs_1_.refs_3_) | copy-start | bytes 1572868
  110.4 18.2 %collective-permute-start.15 = (bf16[1024,256]{1,0:T(8,128)(2,1)}, bf16[1024,256]{1,0:T(8,128)(2,1)}, u32[]{:S(2)}, u32[]{:S(2)}) collective-permute-start(bf16[1024,256]{1,0:T(8,128)(2,1)} %get-tuple-element.96), channel_id=1, source_target_pairs={{16,8},{17,9},{18,10},{19,11},{20,12},{21,13},{22,14},{23,15}} | collective-permute-start | bytes 1572872 | tf_op jit(solution)/shard_map/ppermute | solution.py:393
  111.9 12.7 %all-to-all-start.2 = ((bf16[8,256,128]{2,1,0:T(8,128)(2,1)}), bf16[8,256,128]{2,1,0:T(8,128)(2,1)S(1)}, u32[]{:S(2)}, u32[]{:S(2)}) async-start(bf16[8,256,128]{2,1,0:T(8,128)(2,1)} %get-tuple-element.97), calls=%async_computation.2 | async-start | bytes 1048576 | tf_op jit(solution)/shard_map/all_to_all | solution.py:66
  118.3 28.2 %collective-permute-start.16 = (bf16[1024,256]{1,0:T(8,128)(2,1)}, bf16[1024,256]{1,0:T(8,128)(2,1)}, u32[]{:S(2)}, u32[]{:S(2)}) collective-permute-start(bf16[1024,256]{1,0:T(8,128)(2,1)} %get-tuple-element.101), channel_id=1, source_target_pairs={{8,0},{9,1},{10,2},{11,3},{12,4},{13,5},{14,6},{15,7}} | collective-permute-start | bytes 1572872 | tf_op jit(solution)/shard_map/ppermute | solution.py:393
  119.6 32.1 %collective-permute-start.18 = (bf16[1024,256]{1,0:T(8,128)(2,1)}, bf16[1024,256]{1,0:T(8,128)(2,1)}, u32[]{:S(2)}, u32[]{:S(2)}) collective-permute-start(bf16[1024,256]{1,0:T(8,128)(2,1)} %get-tuple-element.104), channel_id=1, source_target_pairs={{16,0},{17,1},{18,2},{19,3},{20,4},{21,5},{22,6},{23,7}} | collective-permute-start | bytes 1572872 | tf_op jit(solution)/shard_map/ppermute | solution.py:446
  120.9 30.8 %collective-permute-start.17 = (bf16[1024,256]{1,0:T(8,128)(2,1)}, bf16[1024,256]{1,0:T(8,128)(2,1)}, u32[]{:S(2)}, u32[]{:S(2)}) collective-permute-start(bf16[1024,256]{1,0:T(8,128)(2,1)} %get-tuple-element.104), channel_id=1, source_target_pairs={{16,8},{17,9},{18,10},{19,11},{20,12},{21,13},{22,14},{23,15}} | collective-permute-start | bytes 1572872 | tf_op jit(solution)/shard_map/ppermute | solution.py:446
  131.4 32.4 %collective-permute-start.19 = (bf16[1024,256]{1,0:T(8,128)(2,1)}, bf16[1024,256]{1,0:T(8,128)(2,1)}, u32[]{:S(2)}, u32[]{:S(2)}) collective-permute-start(bf16[1024,256]{1,0:T(8,128)(2,1)} %get-tuple-element.107), channel_id=1, source_target_pairs={{8,0},{9,1},{10,2},{11,3},{12,4},{13,5},{14,6},{15,7}} | collective-permute-start | bytes 1572872 | tf_op jit(solution)/shard_map/ppermute | solution.py:393
  157.2 33.6 %all-to-all-start.3 = ((bf16[8,256,256]{2,1,0:T(8,128)(2,1)}), bf16[8,256,256]{2,1,0:T(8,128)(2,1)S(1)}, u32[]{:S(2)}, u32[]{:S(2)}) async-start(bf16[8,256,256]{2,1,0:T(8,128)(2,1)} %get-tuple-element.114), calls=%async_computation.3 | async-start | bytes 2097152 | tf_op jit(solution)/shard_map/all_to_all | solution.py:66
  161.8 26.2 %collective-permute-start.20 = (bf16[1024,256]{1,0:T(8,128)(2,1)}, bf16[1024,256]{1,0:T(8,128)(2,1)S(1)}, u32[]{:S(2)}, u32[]{:S(2)}) collective-permute-start(bf16[1024,256]{1,0:T(8,128)(2,1)} %get-tuple-element.110), channel_id=1, source_target_pairs={{0,4},{4,0},{1,5},{5,1},{2,6},{6,2},{3,7},{7,3},{8,12},{12,8},{9,1... | collective-permute-start | bytes 1572872 | tf_op jit(solution)/shard_map/ppermute | solution.py:51
  163.8 1.0 copy-start.1
  170.1 28.8 %collective-permute-start.21 = (bf16[1024,256]{1,0:T(8,128)(2,1)}, bf16[1024,256]{1,0:T(8,128)(2,1)}, u32[]{:S(2)}, u32[]{:S(2)}) collective-permute-start(bf16[1024,256]{1,0:T(8,128)(2,1)} %get-tuple-element.118), channel_id=1, source_target_pairs={{0,4},{4,0},{1,5},{5,1},{2,6},{6,2},{3,7},{7,3},{8,12},{12,8},{9,1... | collective-permute-start | bytes 1572872 | tf_op jit(solution)/shard_map/ppermute | solution.py:51

commit v10 on v9

--- a/solution.py
+++ b/solution.py
@@ -199,19 +199,7 @@
     out[:, :part] = mm(pair[...], following[:, columns_here]).astype(LOW)
 
 
-def near_kernel(ids, pair, e1, prod, blocks, spread, near, m):
-    gather_lanes(blocks, m, 0, blocks.shape[2])
-
-    @pl.when(ids[0] == 0)
-    def _():
-        near[...] = mm_bt(m[...], pair[...]) + prod[...] + spread[0]
-
-    @pl.when(ids[0] == 1)
-    def _():
-        near[...] = mm_bt(m[...], e1[...]) + spread[0]
-
-
-def far_kernel(ids, pair, e1, following, f_a, f_b, out, far):
+def far_kernel(ids, pair, e1, following, f_a, f_b, unused, out, far):
     size, rows = far.shape
     part = rows // 2
     far[...] = f_a[...] + f_b[...]
@@ -234,8 +222,9 @@
         out[2 * r + 1] = two[r * rows : (r + 1) * rows, :]
 
 
-def end_kernel(ids, pair, e1, following, near, blocks, out_gain, out_spread, m):
+def end_kernel(ids, pair, e1, following, near, prod, spread, blocks, out_gain, out_spread, m, m_near):
     part = blocks.shape[2] // 2
+    gather_lanes(near, m_near, 0, part)
     gather_lanes(blocks, m, part, part)
     for s in range(blocks.shape[0]):
         out_gain[:, s * part : (s + 1) * part] = blocks[s, :, :part].astype(WIDE)
@@ -246,11 +235,13 @@
 
     @pl.when(ids[0] == 0)
     def _():
-        out_spread[...] = mm_bt(m[...], pair[...]) + near[...]
-
-    @pl.when(ids[0] == 1)
-    def _():
-        out_spread[...] = mm_bt(m[...], e1[...]) + near[...]
+        total = mm_bt(m_near[...], pair[...]) + prod[...] + spread[0]
+        out_spread[...] = mm_bt(m[...], pair[...]) + total
+
+    @pl.when(ids[0] == 1)
+    def _():
+        total = mm_bt(m_near[...], e1[...]) + spread[0]
+        out_spread[...] = mm_bt(m[...], e1[...]) + total
 
 
 def columns(ref, side, chunk, width):
@@ -280,6 +271,16 @@
 
 def hop_kernel(ids, pair, got, own, now):
     now[...] = (mm(pair[...], got[...]) + own[...].astype(WIDE)).astype(LOW)
+
+
+def hop_start_kernel(chunk, ids, pair, got_hop, own_hop, e0, got, offset, unused, now, p, own, keep, sem):
+    hop_kernel(ids, pair, got_hop, own_hop, now)
+    start_kernel(chunk, ids, e0, got, offset, p, own, keep, sem)
+
+
+def hops_kernel(ids, pair, got_a, own_a, got_b, own_b, now_a, now_b):
+    hop_kernel(ids, pair, got_a, own_a, now_a)
+    hop_kernel(ids, pair, got_b, own_b, now_b)
 
 
 def last_kernel(chunk, ids, pair, later, p_far, got_a, got_b, got_c, offset, *refs):
@@ -429,44 +430,45 @@
         far_in=(4,), scratch=[slab_rows],
     )
     l_next = lax.ppermute(a_low, "z", level)
-    p1, own1 = start(1)
+    now0, p1, own1 = order.call(
+        functools.partial(hop_start_kernel, 1), [pair, gots0[0], in_hbm(own0), in_hbm(e0), g_got[1], offset, quarter_y],
+        [hbm(size_d, width), hbm(size_d, width, dtype=WIDE), hbm(size_d, width)], 16,
+        far_in=(5, 6), scratch=[keep, pltpu.SemaphoreType.DMA(())],
+    )
+    gots0.append(down(now0, 2))
     gots1 = [down(own1, 3)]
-
     m, near = order.call(spread_hop_kernel, [pair, in_hbm(e1), l_next], [hbm(size_d, part), hbm(8, rows, part)], 10)
+    near, quarter_y = tied((near, quarter_y))
     m = exchange(m.reshape(8, part, part))
-    now0 = hop(gots0[0], own0)
-    gots0.append(down(now0, 2))
-    quarter_y, now0 = tied((quarter_y, now0))
     quarters = jnp.concatenate([quarter, quarter_y], axis=0)
     quarters = [quarters, swap(quarters, "c")]
+    now0, now1 = order.call(
+        hops_kernel, [pair, gots0[1], in_hbm(own0), gots1[0], in_hbm(own1)], [hbm(size_d, width)] * 2, 10
+    )
+    gots0.append(down(now0, 1))
+    gots1.append(down(now1, 2))
     following, far_slab = order.call(
         next_kernel, [pair, in_hbm(slab), m, *quarters], [hbm(size_d, size_d), hbm(size_d, rows)], 12,
         far_in=(3, 4), scratch=[pltpu.VMEM((part, size_d), LOW), pltpu.SemaphoreType.DMA((4,))],
     )
     far = lax.ppermute(far_slab, "z", [(2, 1)]), lax.ppermute(far_slab, "z", [(2, 0)])
-    now1 = hop(gots1[0], own1)
-    gots1.append(down(now1, 2))
-    near, now1 = tied((near, now1))
+    near, far_slab = tied((near, far_slab))
     near = exchange(near)
-    gots0.append(down(hop(gots0[1], own0), 1))
-    (near,) = order.call(
-        near_kernel, [pair, in_hbm(e1), in_hbm(prod), near, spread], [hbm(rows, size_d, dtype=WIDE)], 12,
-        scratch=[slab_rows],
-    )
-    gots1.append(down(hop(gots1[1], own1), 1))
 
     out_offset, other0 = last(0, p0, gots0, None)
     other0 = swap(other0, "x")
+    gots1.append(down(hop(gots1[1], own1), 1))
     (m,) = order.call(
-        far_kernel, [pair, in_hbm(e1), in_hbm(following), *far], [hbm(8, rows, rows)], 14,
-        scratch=[pltpu.VMEM((size_d, rows), LOW)],
+        far_kernel, [pair, in_hbm(e1), in_hbm(following), *far, near], [hbm(8, rows, rows)], 14,
+        far_in=(5,), scratch=[pltpu.VMEM((size_d, rows), LOW)],
     )
     m = exchange(m)
+    out_offset = add(0, other0, out_offset)
     out_offset, other1 = last(1, p1, gots1, out_offset)
     other1 = swap(other1, "x")
-    out_offset = add(0, other0, out_offset)
     out_gain, out_spread = order.call(
-        end_kernel, [pair, in_hbm(e1), in_hbm(following), in_hbm(near), m], [wide(rows, size_d), wide(rows, size_d)], 14, scratch=[slab_rows]
+        end_kernel, [pair, in_hbm(e1), in_hbm(following), near, in_hbm(prod), spread, m],
+        [wide(rows, size_d), wide(rows, size_d)], 18, scratch=[slab_rows, slab_rows],
     )
     out_offset = add(1, other1, out_offset)
     return (out_gain[None], out_spread[None], out_offset[None])

time: 204 us -> 192 us (0.941)
  the two profiles are of different devices: /device:TPU:0 before, /device:TPU:16 now
where the time goes in v10:
time: 192 us; the launch traced here: 189 us
  Pallas kernels  66.7 us (35%)
  waiting for transfers between devices  59.7 us (31%)
  starting transfers between devices  49.4 us (26%)
  local copies, waits for them, and re-layouts  8.28 us (4%)
  other arithmetic  4.07 us (2%)
    pallas_call x15, Pallas kernels, call(): pl.pallas_call(body, in_specs=[SMEM, ANY] + [ANY if i in far_in else VMEM...  66.7 us
    ppermute x12, waiting for transfers between devices, swap(): return lax.ppermute(value, axis, [(0, 1), (1, 0)])  29.2 us
    ppermute x6, waiting for transfers between devices, down(): return lax.ppermute(value, 'z', [(source, source - 1)])  16.2 us
    all_to_all x4, starting transfers between devices, exchange(): return lax.all_to_all(blocks, GROUP, 0, 0)  16 us
    ppermute x12, starting transfers between devices, swap(): return lax.ppermute(value, axis, [(0, 1), (1, 0)])  15.4 us
    ppermute x6, starting transfers between devices, down(): return lax.ppermute(value, 'z', [(source, source - 1)])  11.8 us
    ppermute x1, waiting for transfers between devices, suffix(): lax.ppermute(far_slab, 'z', [(2, 1)])  8.02 us
    all_to_all x4, waiting for transfers between devices, exchange(): return lax.all_to_all(blocks, GROUP, 0, 0)  6.26 us
  transfers between devices with their start and end apart: 26, of which 11 were waited for; matrix products, arithmetic and copies ran while one was open for 3% of the time, Pallas kernels for 29%

profile of v10, /device:TPU:16, one launch (start us, length us, event | category | flops | bytes accessed | tf_op | source)
XLA Modules:
  0.0 189.3 jit_solution(12315286636779554739)
XLA Ops:
  0.6 1.3 convert_bitcast_fusion
  1.9 1.6 collective-permute-start.1
  3.5 1.5 collective-permute-start.2
  5.0 1.3 convert_element_type.27
  6.9 2.5 %fusion.1 = (bf16[1024,256]{1,0:T(8,128)(2,1)}, bf16[1024,256]{1,0:T(8,128)(2,1)S(1)}) fusion(f32[1,1024,1024]{2,1,0:T(8,128)} %param.5, s32[]{:T(128)S(6)} %select_n.11, s32[]{:T(128)S(6)} %select_n.9), kind=kLoop, calls=%fused_computation.4 | loop fusion | bytes 2097160 | tf_op jit(solution)/shard_map/convert_element_type | solution.py:368
  9.4 11.9 %collective-permute-done.refs_2_.refs_3_ = bf16[128,1024]{1,0:T(8,128)(2,1)S(1)} collective-permute-done((bf16[128,1024]{1,0:T(8,128)(2,1)S(1)}, bf16[128,1024]{1,0:T(8,128)(2,1)S(1)}, u32[]{:S(2)}, u32[]{:S(2)}) %collective-permute-start) | collective-permute-done | bytes 262176 | tf_op jit(solution)/shard_map/ppermute | solution.py:51
  21.5 1.6 collective-permute-start.3
  23.1 1.5 collective-permute-start.4
  24.6 11.3 %collective-permute-done.3.refs_1_ = bf16[1024,256]{1,0:T(8,128)(2,1)S(1)} collective-permute-done((bf16[1024,256]{1,0:T(8,128)(2,1)S(1)}, bf16[1024,256]{1,0:T(8,128)(2,1)S(1)}, u32[]{:S(2)}, u32[]{:S(2)}) %collective-permute-start.3) | collective-permute-done | bytes 524320 | tf_op jit(solution)/shard_map/ppermute | solution.py:51
  37.1 1.8 collective-permute-done.6.refs_3_
  39.8 6.0 %shard_map.58 = (bf16[1024,1024]{1,0:T(8,128)(2,1)}, bf16[1024,1024]{1,0:T(8,128)(2,1)}, bf16[1024,1024]{1,0:T(8,128)(2,1)S(1)}, bf16[256,1024]{1,0:T(8,128)(2,1)}, s32[8,128]{1,0:T(8,128)S(1)}) custom-call(s32[4]{0:T(128)S(1)} %pad_add_fusion.ids, s32[8,128]{1,0:T(8,128)S(1)} %broadcast_in_dim.12.token, ...), custom_call_target="tpu_custom_call", output_to_operand_aliasing={{4}: (1, {})} | custom-call | flops 1 | bytes 1 | tf_op jit(solution)/shard_map/pallas_call | solution.py:93
  45.7 1.3 collective-permute-start.9
  48.2 1.3 convert_bitcast_fusion.1.refs_1_
  49.5 3.1 %shard_map.59 = (bf16[8,256,128]{2,1,0:T(8,128)(2,1)}, s32[8,128]{1,0:T(8,128)S(1)}) custom-call(s32[4]{0:T(128)S(1)} %pad_add_fusion.ids, s32[8,128]{1,0:T(8,128)S(1)} %get-tuple-element.63.token, bf16[1024,1024]{1,0:T(8,128)(2,1)} %get-tuple-element.64.refs_0_.refs_3_, ...), custom_call_target="tpu_custom_call", output_to_operand_aliasing={{1}: (1, {})} | custom-call | flops 1 | bytes 1 | tf_op jit(solution)/shard_map/pallas_call | solution.py:93
  52.6 3.5 %all-to-all-start = ((bf16[8,256,128]{2,1,0:T(8,128)(2,1)}), bf16[8,256,128]{2,1,0:T(8,128)(2,1)S(1)}, u32[]{:S(2)}, u32[]{:S(2)}) async-start(bf16[8,256,128]{2,1,0:T(8,128)(2,1)} %get-tuple-element.70), calls=%async_computation | async-start | bytes 1048576 | tf_op jit(solution)/shard_map/all_to_all | solution.py:66
  57.1 4.1 %shard_map.60 = (f32[1024,256]{1,0:T(8,128)}, bf16[1024,256]{1,0:T(8,128)(2,1)}, s32[8,128]{1,0:T(8,128)S(1)}) custom-call(s32[4]{0:T(128)S(1)} %pad_add_fusion.ids, s32[8,128]{1,0:T(8,128)S(1)} %get-tuple-element.66.token, bf16[1024,1024]{1,0:T(8,128)(2,1)} %get-tuple-element.64.refs_0_.refs_3_, ...), custom_call_target="tpu_custom_call", output_to_operand_aliasing={{2}: (1, {})} | custom-call | flops 1 | bytes 1 | tf_op jit(solution)/shard_map/pallas_call | solution.py:93
  61.2 1.3 collective-permute-start.8
  62.6 2.0 %collective-permute-start.10 = (bf16[256,1024]{1,0:T(8,128)(2,1)}, bf16[256,1024]{1,0:T(8,128)(2,1)}, u32[]{:S(2)}, u32[]{:S(2)}) collective-permute-start(bf16[256,1024]{1,0:T(8,128)(2,1)} %collective-permute-done.9), channel_id=1, source_target_pairs={{0,2},{2,0},{1,3},{3,1},{4,6},{6,4},{5,7},{7,5},{8,10},{10,8},{9,1... | collective-permute-start | bytes 1572872 | tf_op jit(solution)/shard_map/ppermute | solution.py:51
  64.6 2.6 %all-to-all-done.refs_1_ = bf16[8,256,128]{2,1,0:T(8,128)(2,1)S(1)} async-done(((bf16[8,256,128]{2,1,0:T(8,128)(2,1)}), bf16[8,256,128]{2,1,0:T(8,128)(2,1)S(1)}, u32[]{:S(2)}, u32[]{:S(2)}) %all-to-all-start) | async-done | bytes 524320 | tf_op jit(solution)/shard_map/all_to_all | solution.py:66
  67.1 4.1 %shard_map.61 = (f32[256,1024]{1,0:T(8,128)}, f32[1024,128]{1,0:T(8,128)}, bf16[1024,128]{1,0:T(8,128)(2,1)}, s32[8,128]{1,0:T(8,128)S(1)}) custom-call(s32[4]{0:T(128)S(1)} %pad_add_fusion.ids, s32[8,128]{1,0:T(8,128)S(1)} %get-tuple-element.69.token, bf16[1024,1024]{1,0:T(8,128)(2,1)} %get-tuple-element.64.refs_0_.refs_3_, ...), custom_call_target="tpu_custom_call", output_to_operand_aliasing={{3}: (1, {})} | custom-call | flops 1 | bytes 1 | tf_op jit(solution)/shard_map/pallas_call | solution.py:93
  73.6 5.4 %collective-permute-done.8.refs_1_.refs_3_ = bf16[1024,256]{1,0:T(8,128)(2,1)} collective-permute-done((bf16[1024,256]{1,0:T(8,128)(2,1)}, bf16[1024,256]{1,0:T(8,128)(2,1)}, u32[]{:S(2)}, u32[]{:S(2)}) %collective-permute-start.8) | collective-permute-done | bytes 524320 | tf_op jit(solution)/shard_map/ppermute | solution.py:394
  80.0 5.2 %shard_map.62 = (bf16[1024,256]{1,0:T(8,128)(2,1)}, f32[1024,256]{1,0:T(8,128)}, bf16[1024,256]{1,0:T(8,128)(2,1)}, s32[8,128]{1,0:T(8,128)S(1)}) custom-call(s32[4]{0:T(128)S(1)} %pad_add_fusion.ids, s32[8,128]{1,0:T(8,128)S(1)} %get-tuple-element.72.token, bf16[1024,1024]{1,0:T(8,128)(2,1)S(1)} %get-tuple-element.73.refs_0_, ...), custom_call_target="tpu_custom_call", output_to_operand_aliasing={{3}: (1, {})} | custom-call | flops 1 | bytes 1 | tf_op jit(solution)/shard_map/pallas_call | solution.py:93
  85.2 3.8 %shard_map.63 = (bf16[1024,128]{1,0:T(8,128)(2,1)}, bf16[8,256,128]{2,1,0:T(8,128)(2,1)}, s32[8,128]{1,0:T(8,128)S(1)}) custom-call(s32[4]{0:T(128)S(1)} %pad_add_fusion.ids, s32[8,128]{1,0:T(8,128)S(1)} %get-tuple-element.78.token, bf16[1024,1024]{1,0:T(8,128)(2,1)S(1)} %get-tuple-element.73.refs_0_, ...), custom_call_target="tpu_custom_call", output_to_operand_aliasing={{2}: (1, {})} | custom-call | flops 1 | bytes 1 | tf_op jit(solution)/shard_map/pallas_call | solution.py:93
  90.2 4.2 %collective-permute-start.12 = (bf16[1024,256]{1,0:T(8,128)(2,1)}, bf16[1024,256]{1,0:T(8,128)(2,1)}, u32[]{:S(2)}, u32[]{:S(2)}) collective-permute-start(bf16[1024,256]{1,0:T(8,128)(2,1)} %get-tuple-element.82), channel_id=1, source_target_pairs={{16,8},{17,9},{18,10},{19,11},{20,12},{21,13},{22,14},{23,15}} | collective-permute-start | bytes 1572872 | tf_op jit(solution)/shard_map/ppermute | solution.py:394
  95.7 4.1 %all-to-all-start.1 = ((bf16[8,128,128]{2,1,0:T(8,128)(2,1)}), bf16[8,128,128]{2,1,0:T(8,128)(2,1)S(1)}, u32[]{:S(2)}, u32[]{:S(2)}) async-start(bf16[8,128,128]{2,1,0:T(8,128)(2,1)} %bitcast.26), calls=%async_computation.1 | async-start | bytes 524288 | tf_op jit(solution)/shard_map/all_to_all | solution.py:66
  99.8 5.9 %collective-permute-done.12.refs_1_.refs_4_ = bf16[1024,256]{1,0:T(8,128)(2,1)} collective-permute-done((bf16[1024,256]{1,0:T(8,128)(2,1)}, bf16[1024,256]{1,0:T(8,128)(2,1)}, u32[]{:S(2)}, u32[]{:S(2)}) %collective-permute-start.12) | collective-permute-done | bytes 524320 | tf_op jit(solution)/shard_map/ppermute | solution.py:394
  105.7 4.9 %collective-permute-done.13.refs_3_ = bf16[1024,256]{1,0:T(8,128)(2,1)} collective-permute-done((bf16[1024,256]{1,0:T(8,128)(2,1)}, bf16[1024,256]{1,0:T(8,128)(2,1)}, u32[]{:S(2)}, u32[]{:S(2)}) %collective-permute-start.13) | collective-permute-done | bytes 524320 | tf_op jit(solution)/shard_map/ppermute | solution.py:394
  110.6 3.8 %shard_map.64 = (bf16[1024,256]{1,0:T(8,128)(2,1)}, bf16[1024,256]{1,0:T(8,128)(2,1)}, s32[8,128]{1,0:T(8,128)S(1)}) custom-call(s32[4]{0:T(128)S(1)} %pad_add_fusion.ids, s32[8,128]{1,0:T(8,128)S(1)} %get-tuple-element.81.token, bf16[1024,1024]{1,0:T(8,128)(2,1)S(1)} %get-tuple-element.73.refs_0_, ...), custom_call_target="tpu_custom_call", output_to_operand_aliasing={{2}: (1, {})} | custom-call | flops 1 | bytes 1 | tf_op jit(solution)/shard_map/pallas_call | solution.py:93
  114.4 1.4 collective-permute-start.15
  115.8 2.1 %collective-permute-start.16 = (bf16[1024,256]{1,0:T(8,128)(2,1)}, bf16[1024,256]{1,0:T(8,128)(2,1)}, u32[]{:S(2)}, u32[]{:S(2)}) collective-permute-start(bf16[1024,256]{1,0:T(8,128)(2,1)} %get-tuple-element.93), channel_id=1, source_target_pairs={{16,8},{17,9},{18,10},{19,11},{20,12},{21,13},{22,14},{23,15}} | collective-permute-start | bytes 1572872 | tf_op jit(solution)/shard_map/ppermute | solution.py:394
  117.9 5.0 %shard_map.65 = (bf16[1024,1024]{1,0:T(8,128)(2,1)}, bf16[1024,256]{1,0:T(8,128)(2,1)}, s32[8,128]{1,0:T(8,128)S(1)}) custom-call(s32[4]{0:T(128)S(1)} %pad_add_fusion.ids, s32[8,128]{1,0:T(8,128)S(1)} %get-tuple-element.84.token, bf16[1024,1024]{1,0:T(8,128)(2,1)S(1)} %get-tuple-element.73.refs_0_, ...), custom_call_target="tpu_custom_call", output_to_operand_aliasing={{2}: (1, {})} | custom-call | flops 1 | bytes 1 | tf_op jit(solution)/shard_map/pallas_call | solution.py:93
  123.0 1.3 collective-permute-start.18
  124.3 2.3 %collective-permute-start.17 = (bf16[1024,256]{1,0:T(8,128)(2,1)}, bf16[1024,256]{1,0:T(8,128)(2,1)}, u32[]{:S(2)}, u32[]{:S(2)}) collective-permute-start(bf16[1024,256]{1,0:T(8,128)(2,1)} %get-tuple-element.96), channel_id=1, source_target_pairs={{16,8},{17,9},{18,10},{19,11},{20,12},{21,13},{22,14},{23,15}} | collective-permute-start | bytes 1572872 | tf_op jit(solution)/shard_map/ppermute | solution.py:454
  126.6 4.2 %all-to-all-start.2 = ((bf16[8,256,128]{2,1,0:T(8,128)(2,1)}), bf16[8,256,128]{2,1,0:T(8,128)(2,1)S(1)}, u32[]{:S(2)}, u32[]{:S(2)}) async-start(bf16[8,256,128]{2,1,0:T(8,128)(2,1)} %get-tuple-element.98), calls=%async_computation.2 | async-start | bytes 1048576 | tf_op jit(solution)/shard_map/all_to_all | solution.py:66
  130.7 5.2 %shard_map.66 = (f32[1024,1024]{1,0:T(8,128)}, bf16[1024,256]{1,0:T(8,128)(2,1)}, s32[8,128]{1,0:T(8,128)S(1)}) custom-call(s32[4]{0:T(128)S(1)} %pad_add_fusion.ids, s32[8,128]{1,0:T(8,128)S(1)} %get-tuple-element.89.token, bf16[1024,1024]{1,0:T(8,128)(2,1)S(1)} %get-tuple-element.73.refs_0_, ...), custom_call_target="tpu_custom_call", output_to_operand_aliasing={{2}: (1, {})} | custom-call | flops 1 | bytes 1 | tf_op jit(solution)/shard_map/pallas_call | solution.py:93
  135.9 2.7 %collective-permute-start.19 = (bf16[1024,256]{1,0:T(8,128)(2,1)}, bf16[1024,256]{1,0:T(8,128)(2,1)}, u32[]{:S(2)}, u32[]{:S(2)}) collective-permute-start(bf16[1024,256]{1,0:T(8,128)(2,1)} %get-tuple-element.100), channel_id=1, source_target_pairs={{0,4},{4,0},{1,5},{5,1},{2,6},{6,2},{3,7},{7,3},{8,12},{12,8},{9,1... | collective-permute-start | bytes 1572872 | tf_op jit(solution)/shard_map/ppermute | solution.py:51
  138.6 2.7 %shard_map.67 = (bf16[1024,256]{1,0:T(8,128)(2,1)}, s32[8,128]{1,0:T(8,128)S(1)}) custom-call(s32[4]{0:T(128)S(1)} %pad_add_fusion.ids, s32[8,128]{1,0:T(8,128)S(1)} %get-tuple-element.92.token, bf16[1024,1024]{1,0:T(8,128)(2,1)S(1)} %get-tuple-element.73.refs_0_, ...), custom_call_target="tpu_custom_call", output_to_operand_aliasing={{1}: (1, {})} | custom-call | flops 1 | bytes 1 | tf_op jit(solution)/shard_map/pallas_call | solution.py:93
  141.3 1.5 collective-permute-start.20
  142.8 8.0 %collective-permute-done.17.refs_3_ = bf16[1024,256]{1,0:T(8,128)(2,1)} collective-permute-done((bf16[1024,256]{1,0:T(8,128)(2,1)}, bf16[1024,256]{1,0:T(8,128)(2,1)}, u32[]{:S(2)}, u32[]{:S(2)}) %collective-permute-start.17) | collective-permute-done | bytes 524320 | tf_op jit(solution)/shard_map/ppermute | solution.py:454
  150.8 5.4 %shard_map.68 = (bf16[8,256,256]{2,1,0:T(8,128)(2,1)}, s32[8,128]{1,0:T(8,128)S(1)}) custom-call(s32[4]{0:T(128)S(1)} %pad_add_fusion.ids, s32[8,128]{1,0:T(8,128)S(1)} %get-tuple-element.94.token, bf16[1024,1024]{1,0:T(8,128)(2,1)S(1)} %get-tuple-element.73.refs_0_, bf16[1024,1024]{1,0:T(8,128)(2,1)} %get-tuple-element.79.refs_1_, ...), custom_call_target="tpu_custom_call", output_to_operand_aliasing={{1}: (1, {})} | custom-call | flops 1 | bytes 1 | tf_op jit(solution)/shard_map/pallas_call | solution.py:93
  156.3 4.3 %all-to-all-start.3 = ((bf16[8,256,256]{2,1,0:T(8,128)(2,1)}), bf16[8,256,256]{2,1,0:T(8,128)(2,1)}, u32[]{:S(2)}, u32[]{:S(2)}) async-start(bf16[8,256,256]{2,1,0:T(8,128)(2,1)} %get-tuple-element.108), calls=%async_computation.3 | async-start | bytes 2097152 | tf_op jit(solution)/shard_map/all_to_all | solution.py:66
  160.5 3.4 %shard_map.69 = (f32[1024,1024]{1,0:T(8,128)}, s32[8,128]{1,0:T(8,128)S(1)}) custom-call(s32[4]{0:T(128)S(1)} %pad_add_fusion.ids, s32[8,128]{1,0:T(8,128)S(1)} %get-tuple-element.99.token, bf16[1024,256]{1,0:T(8,128)(2,1)} %collective-permute-done.19.refs_0_, f32[1024,1024]{1,0:T(8,128)} %bitcast.22, ...), custom_call_target="tpu_custom_call", output_to_operand_aliasing={{1}: (1, {}), {0}: (4, {})} | custom-call | flops 1 | bytes 1 | tf_op jit(solution)/shard_map/pallas_call | solution.py:93
  163.9 5.2 %shard_map.70 = (f32[1024,1024]{1,0:T(8,128)}, bf16[1024,256]{1,0:T(8,128)(2,1)}, s32[8,128]{1,0:T(8,128)S(1)}) custom-call(s32[4]{0:T(128)S(1)} %pad_add_fusion.ids, s32[8,128]{1,0:T(8,128)S(1)} %get-tuple-element.102.token, bf16[1024,1024]{1,0:T(8,128)(2,1)S(1)} %get-tuple-element.73.refs_0_, ...), custom_call_target="tpu_custom_call", output_to_operand_aliasing={{2}: (1, {}), {0}: (9, {})} | custom-call | flops 1 | bytes 1 | tf_op jit(solution)/shard_map/pallas_call | solution.py:93
  169.2 2.7 %collective-permute-start.21 = (bf16[1024,256]{1,0:T(8,128)(2,1)}, bf16[1024,256]{1,0:T(8,128)(2,1)S(1)}, u32[]{:S(2)}, u32[]{:S(2)}) collective-permute-start(bf16[1024,256]{1,0:T(8,128)(2,1)} %get-tuple-element.112), channel_id=1, source_target_pairs={{0,4},{4,0},{1,5},{5,1},{2,6},{6,2},{3,7},{7,3},{8,12},{12,8},{9,1... | collective-permute-start | bytes 1572872 | tf_op jit(solution)/shard_map/ppermute | solution.py:51
  171.8 3.7 %all-to-all-done.3.refs_6_ = bf16[8,256,256]{2,1,0:T(8,128)(2,1)} async-done(((bf16[8,256,256]{2,1,0:T(8,128)(2,1)}), bf16[8,256,256]{2,1,0:T(8,128)(2,1)}, u32[]{:S(2)}, u32[]{:S(2)}) %all-to-all-start.3) | async-done | bytes 1048608 | tf_op jit(solution)/shard_map/all_to_all | solution.py:66
  175.5 6.9 %shard_map.71 = (f32[256,1024]{1,0:T(8,128)}, f32[256,1024]{1,0:T(8,128)}, s32[8,128]{1,0:T(8,128)S(1)}) custom-call(s32[4]{0:T(128)S(1)} %pad_add_fusion.ids, s32[8,128]{1,0:T(8,128)S(1)} %get-tuple-element.106.token, bf16[1024,1024]{1,0:T(8,128)(2,1)S(1)} %get-tuple-element.73.refs_0_, ...), custom_call_target="tpu_custom_call", output_to_operand_aliasing={{2}: (1, {})} | custom-call | flops 1 | bytes 1 | tf_op jit(solution)/shard_map/pallas_call | solution.py:93
  182.4 3.8 %collective-permute-done.21.refs_0_ = bf16[1024,256]{1,0:T(8,128)(2,1)S(1)} collective-permute-done((bf16[1024,256]{1,0:T(8,128)(2,1)}, bf16[1024,256]{1,0:T(8,128)(2,1)S(1)}, u32[]{:S(2)}, u32[]{:S(2)}) %collective-permute-start.21) | collective-permute-done | bytes 524320 | tf_op jit(solution)/shard_map/ppermute | solution.py:51
  186.2 2.9 %shard_map.72 = (f32[1024,1024]{1,0:T(8,128)}, s32[8,128]{1,0:T(8,128)S(1)}) custom-call(s32[4]{0:T(128)S(1)} %pad_add_fusion.ids, s32[8,128]{1,0:T(8,128)S(1)} %get-tuple-element.111.token, bf16[1024,256]{1,0:T(8,128)(2,1)S(1)} %collective-permute-done.21.refs_0_, f32[1024,1024]{1,0:T(8,128)} %bitcast.24, ...), custom_call_target="tpu_custom_call", output_to_operand_aliasing={{1}: (1, {}), {0}: (4, {})} | custom-call | flops 1 | bytes 1 | tf_op jit(solution)/shard_map/pallas_call | solution.py:93
  (43 shorter events, 10.9 us)
Async XLA Ops:
  1.9 19.3 %collective-permute-start.1 = (bf16[256,1024]{1,0:T(8,128)(2,1)S(1)}, bf16[256,1024]{1,0:T(8,128)(2,1)S(1)}, u32[]{:S(2)}, u32[]{:S(2)}) collective-permute-start(bf16[256,1024]{1,0:T(8,128)(2,1)S(1)} %convert_bitcast_fusion), channel_id=1, source_target_pairs={{0,4},{4,0},{1,5},{5,1},{2,6},{6,2},{3,7},{7,3},{8,12},{12,8},{9,1... | collective-permute-start | bytes 1572872 | tf_op jit(solution)/shard_map/ppermute | solution.py:51
  3.5 17.8 %collective-permute-start.2 = (bf16[256,1024]{1,0:T(8,128)(2,1)S(1)}, bf16[256,1024]{1,0:T(8,128)(2,1)S(1)}, u32[]{:S(2)}, u32[]{:S(2)}) collective-permute-start(bf16[256,1024]{1,0:T(8,128)(2,1)S(1)} %convert_bitcast_fusion), channel_id=1, source_target_pairs={{0,2},{2,0},{1,3},{3,1},{4,6},{6,4},{5,7},{7,5},{8,10},{10,8},{9,1... | collective-permute-start | bytes 1572872 | tf_op jit(solution)/shard_map/ppermute | solution.py:51
  6.3 14.9 %collective-permute-start = (bf16[128,1024]{1,0:T(8,128)(2,1)S(1)}, bf16[128,1024]{1,0:T(8,128)(2,1)S(1)}, u32[]{:S(2)}, u32[]{:S(2)}) collective-permute-start(bf16[128,1024]{1,0:T(8,128)(2,1)S(1)} %dynamic-slice_bitcast_fusion), channel_id=1, source_target_pairs={{0,4},{4,0},{1,5},{5,1},{2,6},{6,2},{3,7},{7,3},{8,12},{12,8},{9,1... | collective-permute-start | bytes 786440 | tf_op jit(solution)/shard_map/ppermute | solution.py:51
  21.4 17.6 %copy-start.4 = (bf16[768,1024]{1,0:T(8,128)(2,1)}, bf16[768,1024]{1,0:T(8,128)(2,1)S(1)}, u32[]{:S(2)}) copy-start(bf16[768,1024]{1,0:T(8,128)(2,1)S(1)} %pad_maximum_fusion.refs_0_) | copy-start | bytes 4718596
  21.4 17.5 %collective-permute-start.5 = (bf16[768,1024]{1,0:T(8,128)(2,1)S(1)}, bf16[768,1024]{1,0:T(8,128)(2,1)}, u32[]{:S(2)}, u32[]{:S(2)}) collective-permute-start(bf16[768,1024]{1,0:T(8,128)(2,1)S(1)} %pad_maximum_fusion.refs_0_), channel_id=1, source_target_pairs={{0,1},{1,0},{2,3},{3,2},{4,5},{5,4},{6,7},{7,6},{8,9},{9,8},{10,11... | collective-permute-start | bytes 4718600 | tf_op jit(solution)/shard_map/ppermute | solution.py:51
  21.5 14.3 %collective-permute-start.3 = (bf16[1024,256]{1,0:T(8,128)(2,1)S(1)}, bf16[1024,256]{1,0:T(8,128)(2,1)S(1)}, u32[]{:S(2)}, u32[]{:S(2)}) collective-permute-start(bf16[1024,256]{1,0:T(8,128)(2,1)S(1)} %get-tuple-element.61), channel_id=1, source_target_pairs={{0,4},{4,0},{1,5},{5,1},{2,6},{6,2},{3,7},{7,3},{8,12},{12,8},{9,1... | collective-permute-start | bytes 1572872 | tf_op jit(solution)/shard_map/ppermute | solution.py:51
  23.1 14.0 %collective-permute-start.4 = (bf16[256,1024]{1,0:T(8,128)(2,1)S(1)}, bf16[256,1024]{1,0:T(8,128)(2,1)S(1)}, u32[]{:S(2)}, u32[]{:S(2)}) collective-permute-start(bf16[256,1024]{1,0:T(8,128)(2,1)S(1)} %collective-permute-done.1), channel_id=1, source_target_pairs={{0,2},{2,0},{1,3},{3,1},{4,6},{6,4},{5,7},{7,5},{8,10},{10,8},{9,1... | collective-permute-start | bytes 1572872 | tf_op jit(solution)/shard_map/ppermute | solution.py:51
  35.8 0.8 copy-start.2
  37.0 1.9 %copy-start.5 = (bf16[256,1024]{1,0:T(8,128)(2,1)}, bf16[256,1024]{1,0:T(8,128)(2,1)S(1)}, u32[]{:S(2)}) copy-start(bf16[256,1024]{1,0:T(8,128)(2,1)S(1)} %collective-permute-done.4.refs_1_) | copy-start | bytes 1572868
  37.0 1.9 %collective-permute-start.6 = (bf16[256,1024]{1,0:T(8,128)(2,1)S(1)}, bf16[256,1024]{1,0:T(8,128)(2,1)S(1)}, u32[]{:S(2)}, u32[]{:S(2)}) collective-permute-start(bf16[256,1024]{1,0:T(8,128)(2,1)S(1)} %collective-permute-done.4.refs_1_), channel_id=1, source_target_pairs={{0,1},{1,0},{2,3},{3,2},{4,5},{5,4},{6,7},{7,6},{8,9},{9,8},{10,11... | collective-permute-start | bytes 1572872 | tf_op jit(solution)/shard_map/ppermute | solution.py:51
  39.0 0.8 copy-start.6
  45.7 16.8 %collective-permute-start.9 = (bf16[256,1024]{1,0:T(8,128)(2,1)}, bf16[256,1024]{1,0:T(8,128)(2,1)}, u32[]{:S(2)}, u32[]{:S(2)}) collective-permute-start(bf16[256,1024]{1,0:T(8,128)(2,1)} %get-tuple-element.75), channel_id=1, source_target_pairs={{24,16},{8,0},{25,17},{9,1},{26,18},{10,2},{27,19},{11,3},{28,20},... | collective-permute-start | bytes 1572872 | tf_op jit(solution)/shard_map/ppermute | solution.py:420
  47.0 17.5 %collective-permute-start.7 = (bf16[1024,256]{1,0:T(8,128)(2,1)}, bf16[1024,256]{1,0:T(8,128)(2,1)S(1)}, u32[]{:S(2)}, u32[]{:S(2)}) collective-permute-start(bf16[1024,256]{1,0:T(8,128)(2,1)} %get-tuple-element.71), channel_id=1, source_target_pairs={{0,4},{4,0},{1,5},{5,1},{2,6},{6,2},{3,7},{7,3},{8,12},{12,8},{9,1... | collective-permute-start | bytes 1572872 | tf_op jit(solution)/shard_map/ppermute | solution.py:51
  52.6 14.5 %all-to-all-start = ((bf16[8,256,128]{2,1,0:T(8,128)(2,1)}), bf16[8,256,128]{2,1,0:T(8,128)(2,1)S(1)}, u32[]{:S(2)}, u32[]{:S(2)}) async-start(bf16[8,256,128]{2,1,0:T(8,128)(2,1)} %get-tuple-element.70), calls=%async_computation | async-start | bytes 1048576 | tf_op jit(solution)/shard_map/all_to_all | solution.py:66
  56.1 1.0 copy-start.3
  61.2 17.7 %collective-permute-start.8 = (bf16[1024,256]{1,0:T(8,128)(2,1)}, bf16[1024,256]{1,0:T(8,128)(2,1)}, u32[]{:S(2)}, u32[]{:S(2)}) collective-permute-start(bf16[1024,256]{1,0:T(8,128)(2,1)} %get-tuple-element.76.refs_2_), channel_id=1, source_target_pairs={{24,16},{25,17},{26,18},{27,19},{28,20},{29,21},{30,22},{31,23}} | collective-permute-start | bytes 1572872 | tf_op jit(solution)/shard_map/ppermute | solution.py:394
  62.6 16.4 %collective-permute-start.10 = (bf16[256,1024]{1,0:T(8,128)(2,1)}, bf16[256,1024]{1,0:T(8,128)(2,1)}, u32[]{:S(2)}, u32[]{:S(2)}) collective-permute-start(bf16[256,1024]{1,0:T(8,128)(2,1)} %collective-permute-done.9), channel_id=1, source_target_pairs={{0,2},{2,0},{1,3},{3,1},{4,6},{6,4},{5,7},{7,5},{8,10},{10,8},{9,1... | collective-permute-start | bytes 1572872 | tf_op jit(solution)/shard_map/ppermute | solution.py:51
  64.6 6.6 %copy-start = (bf16[1024,256]{1,0:T(8,128)(2,1)}, bf16[1024,256]{1,0:T(8,128)(2,1)S(1)}, u32[]{:S(2)}) copy-start(bf16[1024,256]{1,0:T(8,128)(2,1)S(1)} %collective-permute-done.7.refs_4_) | copy-start | bytes 1572868
  71.2 14.0 %collective-permute-start.11 = (bf16[1024,128]{1,0:T(8,128)(2,1)}, bf16[1024,128]{1,0:T(8,128)(2,1)S(1)}, u32[]{:S(2)}, u32[]{:S(2)}) collective-permute-start(bf16[1024,128]{1,0:T(8,128)(2,1)} %get-tuple-element.80), channel_id=1, source_target_pairs={{24,16},{8,0},{25,17},{9,1},{26,18},{10,2},{27,19},{11,3},{28,20},... | collective-permute-start | bytes 786440 | tf_op jit(solution)/shard_map/ppermute | solution.py:432
  79.0 1.0 copy-start.1
  90.1 27.8 %collective-permute-start.14 = (bf16[512,1024]{1,0:T(8,128)(2,1)S(1)}, bf16[512,1024]{1,0:T(8,128)(2,1)}, u32[]{:S(2)}, u32[]{:S(2)}) collective-permute-start(bf16[512,1024]{1,0:T(8,128)(2,1)S(1)} %constant_dynamic-update-slice_fusion.refs_3_), channel_id=1, source_target_pairs={{0,1},{1,0},{2,3},{3,2},{4,5},{5,4},{6,7},{7,6},{8,9},{9,8},{10,11... | collective-permute-start | bytes 3145736 | tf_op jit(solution)/shard_map/ppermute | solution.py:51
  90.2 15.5 %collective-permute-start.12 = (bf16[1024,256]{1,0:T(8,128)(2,1)}, bf16[1024,256]{1,0:T(8,128)(2,1)}, u32[]{:S(2)}, u32[]{:S(2)}) collective-permute-start(bf16[1024,256]{1,0:T(8,128)(2,1)} %get-tuple-element.82), channel_id=1, source_target_pairs={{16,8},{17,9},{18,10},{19,11},{20,12},{21,13},{22,14},{23,15}} | collective-permute-start | bytes 1572872 | tf_op jit(solution)/shard_map/ppermute | solution.py:394
  94.4 16.2 %collective-permute-start.13 = (bf16[1024,256]{1,0:T(8,128)(2,1)}, bf16[1024,256]{1,0:T(8,128)(2,1)}, u32[]{:S(2)}, u32[]{:S(2)}) collective-permute-start(bf16[1024,256]{1,0:T(8,128)(2,1)} %get-tuple-element.83.refs_4_.refs_2_), channel_id=1, source_target_pairs={{24,16},{25,17},{26,18},{27,19},{28,20},{29,21},{30,22},{31,23}} | collective-permute-start | bytes 1572872 | tf_op jit(solution)/shard_map/ppermute | solution.py:394
  95.7 22.2 %all-to-all-start.1 = ((bf16[8,128,128]{2,1,0:T(8,128)(2,1)}), bf16[8,128,128]{2,1,0:T(8,128)(2,1)S(1)}, u32[]{:S(2)}, u32[]{:S(2)}) async-start(bf16[8,128,128]{2,1,0:T(8,128)(2,1)} %bitcast.26), calls=%async_computation.1 | async-start | bytes 524288 | tf_op jit(solution)/shard_map/all_to_all | solution.py:66
  114.4 16.4 %collective-permute-start.15 = (bf16[1024,256]{1,0:T(8,128)(2,1)}, bf16[1024,256]{1,0:T(8,128)(2,1)}, u32[]{:S(2)}, u32[]{:S(2)}) collective-permute-start(bf16[1024,256]{1,0:T(8,128)(2,1)} %get-tuple-element.91), channel_id=1, source_target_pairs={{8,0},{9,1},{10,2},{11,3},{12,4},{13,5},{14,6},{15,7}} | collective-permute-start | bytes 1572872 | tf_op jit(solution)/shard_map/ppermute | solution.py:394
  115.8 22.8 %collective-permute-start.16 = (bf16[1024,256]{1,0:T(8,128)(2,1)}, bf16[1024,256]{1,0:T(8,128)(2,1)}, u32[]{:S(2)}, u32[]{:S(2)}) collective-permute-start(bf16[1024,256]{1,0:T(8,128)(2,1)} %get-tuple-element.93), channel_id=1, source_target_pairs={{16,8},{17,9},{18,10},{19,11},{20,12},{21,13},{22,14},{23,15}} | collective-permute-start | bytes 1572872 | tf_op jit(solution)/shard_map/ppermute | solution.py:394
  123.0 19.9 %collective-permute-start.18 = (bf16[1024,256]{1,0:T(8,128)(2,1)}, bf16[1024,256]{1,0:T(8,128)(2,1)S(1)}, u32[]{:S(2)}, u32[]{:S(2)}) collective-permute-start(bf16[1024,256]{1,0:T(8,128)(2,1)} %get-tuple-element.96), channel_id=1, source_target_pairs={{16,0},{17,1},{18,2},{19,3},{20,4},{21,5},{22,6},{23,7}} | collective-permute-start | bytes 1572872 | tf_op jit(solution)/shard_map/ppermute | solution.py:454
  124.3 26.5 %collective-permute-start.17 = (bf16[1024,256]{1,0:T(8,128)(2,1)}, bf16[1024,256]{1,0:T(8,128)(2,1)}, u32[]{:S(2)}, u32[]{:S(2)}) collective-permute-start(bf16[1024,256]{1,0:T(8,128)(2,1)} %get-tuple-element.96), channel_id=1, source_target_pairs={{16,8},{17,9},{18,10},{19,11},{20,12},{21,13},{22,14},{23,15}} | collective-permute-start | bytes 1572872 | tf_op jit(solution)/shard_map/ppermute | solution.py:454
  126.6 16.2 %all-to-all-start.2 = ((bf16[8,256,128]{2,1,0:T(8,128)(2,1)}), bf16[8,256,128]{2,1,0:T(8,128)(2,1)S(1)}, u32[]{:S(2)}, u32[]{:S(2)}) async-start(bf16[8,256,128]{2,1,0:T(8,128)(2,1)} %get-tuple-element.98), calls=%async_computation.2 | async-start | bytes 1048576 | tf_op jit(solution)/shard_map/all_to_all | solution.py:66
  135.9 24.6 %collective-permute-start.19 = (bf16[1024,256]{1,0:T(8,128)(2,1)}, bf16[1024,256]{1,0:T(8,128)(2,1)}, u32[]{:S(2)}, u32[]{:S(2)}) collective-permute-start(bf16[1024,256]{1,0:T(8,128)(2,1)} %get-tuple-element.100), channel_id=1, source_target_pairs={{0,4},{4,0},{1,5},{5,1},{2,6},{6,2},{3,7},{7,3},{8,12},{12,8},{9,1... | collective-permute-start | bytes 1572872 | tf_op jit(solution)/shard_map/ppermute | solution.py:51
  141.3 22.6 %collective-permute-start.20 = (bf16[1024,256]{1,0:T(8,128)(2,1)}, bf16[1024,256]{1,0:T(8,128)(2,1)}, u32[]{:S(2)}, u32[]{:S(2)}) collective-permute-start(bf16[1024,256]{1,0:T(8,128)(2,1)} %get-tuple-element.104), channel_id=1, source_target_pairs={{8,0},{9,1},{10,2},{11,3},{12,4},{13,5},{14,6},{15,7}} | collective-permute-start | bytes 1572872 | tf_op jit(solution)/shard_map/ppermute | solution.py:394
  156.3 19.3 %all-to-all-start.3 = ((bf16[8,256,256]{2,1,0:T(8,128)(2,1)}), bf16[8,256,256]{2,1,0:T(8,128)(2,1)}, u32[]{:S(2)}, u32[]{:S(2)}) async-start(bf16[8,256,256]{2,1,0:T(8,128)(2,1)} %get-tuple-element.108), calls=%async_computation.3 | async-start | bytes 2097152 | tf_op jit(solution)/shard_map/all_to_all | solution.py:66
  169.2 17.1 %collective-permute-start.21 = (bf16[1024,256]{1,0:T(8,128)(2,1)}, bf16[1024,256]{1,0:T(8,128)(2,1)S(1)}, u32[]{:S(2)}, u32[]{:S(2)}) collective-permute-start(bf16[1024,256]{1,0:T(8,128)(2,1)} %get-tuple-element.112), channel_id=1, source_target_pairs={{0,4},{4,0},{1,5},{5,1},{2,6},{6,2},{3,7},{7,3},{8,12},{12,8},{9,1... | collective-permute-start | bytes 1572872 | tf_op jit(solution)/shard_map/ppermute | solution.py:51

commit v11 on v10

--- a/solution.py
+++ b/solution.py
@@ -136,7 +136,7 @@
         copy.wait()
 
 
-def spread_kernel(ids, e0, l_low, l_got, m_ref):
+def spread_kernel(ids, e0, l_low, l_got, unused, m_ref):
     part, rows = l_got.shape[0], l_low.shape[0]
 
     def product(slab):
@@ -170,7 +170,7 @@
     a_low[...] = slab[...].astype(LOW)
 
 
-def spread_hop_kernel(ids, pair, e1, got, m_ref, near):
+def spread_hop_kernel(ids, pair, e1, got, unused, m_ref, near):
     part = got.shape[1]
     rows = 2 * part
     m = mm(pair[...], got[...]).astype(LOW)
@@ -273,7 +273,7 @@
     now[...] = (mm(pair[...], got[...]) + own[...].astype(WIDE)).astype(LOW)
 
 
-def hop_start_kernel(chunk, ids, pair, got_hop, own_hop, e0, got, offset, unused, now, p, own, keep, sem):
+def hop_start_kernel(chunk, ids, pair, got_hop, own_hop, e0, got, offset, now, p, own, keep, sem):
     hop_kernel(ids, pair, got_hop, own_hop, now)
     start_kernel(chunk, ids, e0, got, offset, p, own, keep, sem)
 
@@ -368,12 +368,11 @@
         lax.dynamic_slice_in_dim(offsets[0], (1 - x) * half + i * width, width, 1).astype(LOW) for i in range(chunks)
     ]
     tied = lax.optimization_barrier
+    l_send, g_send[0], e_x = tied((l_send, g_send[0], e_x))
+    e_xy = swap(e_x, "y")
     l_got = swap(l_send, "x")
-    l_got, e_x = tied((l_got, e_x))
-    g_send[0], e_x = tied((g_send[0], e_x))
-    e_xy = swap(e_x, "y")
     g_got = [swap(g_send[0], "x")]
-    g_got[0], e_xy = tied((g_got[0], e_xy))
+    l_got, e_xy = tied((l_got, e_xy))
     g_send[1], g_got[0] = tied((g_send[1], g_got[0]))
     g_got.append(swap(g_send[1], "x"))
     three = jnp.concatenate([e_low, e_x, e_y], axis=0)
@@ -418,7 +417,7 @@
         scratch=[pltpu.VMEM((2, size_d, size_d), LOW), pltpu.SemaphoreType.DMA((8,))],
     )
     quarter = lax.ppermute(quarter, "z", level)
-    (m,) = order.call(spread_kernel, [in_hbm(e0), l_low, l_got], [hbm(8, rows, part)], 8)
+    (m,) = order.call(spread_kernel, [in_hbm(e0), l_low, l_got, g_got[0]], [hbm(8, rows, part)], 8, far_in=(3,))
     m = exchange(m)
     p0, own0 = start(0)
     gots0 = [down(own0, 3)]
@@ -431,16 +430,18 @@
     )
     l_next = lax.ppermute(a_low, "z", level)
     now0, p1, own1 = order.call(
-        functools.partial(hop_start_kernel, 1), [pair, gots0[0], in_hbm(own0), in_hbm(e0), g_got[1], offset, quarter_y],
+        functools.partial(hop_start_kernel, 1), [pair, gots0[0], in_hbm(own0), in_hbm(e0), g_got[1], offset],
         [hbm(size_d, width), hbm(size_d, width, dtype=WIDE), hbm(size_d, width)], 16,
-        far_in=(5, 6), scratch=[keep, pltpu.SemaphoreType.DMA(())],
+        far_in=(5,), scratch=[keep, pltpu.SemaphoreType.DMA(())],
     )
     gots0.append(down(now0, 2))
     gots1 = [down(own1, 3)]
-    m, near = order.call(spread_hop_kernel, [pair, in_hbm(e1), l_next], [hbm(size_d, part), hbm(8, rows, part)], 10)
-    near, quarter_y = tied((near, quarter_y))
+    quarters = jnp.concatenate([quarter, quarter_y], axis=0)
+    m, near = order.call(
+        spread_hop_kernel, [pair, in_hbm(e1), l_next, quarters], [hbm(size_d, part), hbm(8, rows, part)], 10, far_in=(3,)
+    )
     m = exchange(m.reshape(8, part, part))
-    quarters = jnp.concatenate([quarter, quarter_y], axis=0)
+    quarters, near = tied((quarters, near))
     quarters = [quarters, swap(quarters, "c")]
     now0, now1 = order.call(
         hops_kernel, [pair, gots0[1], in_hbm(own0), gots1[0], in_hbm(own1)], [hbm(size_d, width)] * 2, 10

time: 192 us -> 189 us (0.984)
  starting transfers between devices: 49.4 us -> 45.9 us
  waiting for transfers between devices: 59.7 us -> 61.7 us
    all_to_all x4, waiting for transfers between devices: 6.26 us -> 10.9 us  [exchange(): return lax.all_to_all(blocks, GROUP, 0, 0)]
    ppermute x6, waiting for transfers between devices: 16.2 us -> 11.5 us  [down(): return lax.ppermute(value, 'z', [(source, source - 1)])]
    unnamed x15 -> x9, local copies, waits for them, and re-layouts: 4.72 us -> 2.92 us
  transfers between devices with their start and end apart: 26 -> 26, of which waited for: 11 -> 13; matrix products, arithmetic and copies ran while one was open for 3% -> 4% of each run, Pallas kernels for 29% -> 32%
where the time goes in v11:
time: 189 us; the launch traced here: 186 us
  Pallas kernels  66.6 us (35%)
  waiting for transfers between devices  61.7 us (33%)
  starting transfers between devices  45.9 us (24%)
  local copies, waits for them, and re-layouts  6.67 us (4%)
  other arithmetic  4.07 us (2%)
    pallas_call x15, Pallas kernels, call(): pl.pallas_call(body, in_specs=[SMEM, ANY] + [ANY if i in far_in else VMEM...  66.6 us
    ppermute x12, waiting for transfers between devices, swap(): return lax.ppermute(value, axis, [(0, 1), (1, 0)])  30.6 us
    all_to_all x4, starting transfers between devices, exchange(): return lax.all_to_all(blocks, GROUP, 0, 0)  15.5 us
    ppermute x12, starting transfers between devices, swap(): return lax.ppermute(value, axis, [(0, 1), (1, 0)])  13.8 us
    ppermute x6, waiting for transfers between devices, down(): return lax.ppermute(value, 'z', [(source, source - 1)])  11.5 us
    all_to_all x4, waiting for transfers between devices, exchange(): return lax.all_to_all(blocks, GROUP, 0, 0)  10.9 us
    ppermute x6, starting transfers between devices, down(): return lax.ppermute(value, 'z', [(source, source - 1)])  10.3 us
    ppermute x1, waiting for transfers between devices, suffix(): lax.ppermute(far_slab, 'z', [(2, 1)])  7.69 us
  transfers between devices with their start and end apart: 26, of which 13 were waited for; matrix products, arithmetic and copies ran while one was open for 4% of the time, Pallas kernels for 32%

profile of v11, /device:TPU:16, one launch (start us, length us, event | category | flops | bytes accessed | tf_op | source)
XLA Modules:
  0.0 186.0 jit_solution(3069609614265533323)
XLA Ops:
  0.6 1.3 convert_bitcast_fusion
  1.9 1.6 collective-permute-start
  3.5 1.5 collective-permute-start.1
  5.0 1.3 convert_element_type.25
  6.3 2.6 %fusion.1 = (bf16[1024,256]{1,0:T(8,128)(2,1)}, bf16[1024,256]{1,0:T(8,128)(2,1)}) fusion(f32[1,1024,1024]{2,1,0:T(8,128)} %param.5, s32[]{:T(128)S(6)} %select_n.11, s32[]{:T(128)S(6)} %select_n.10), kind=kLoop, calls=%fused_computation.4 | loop fusion | bytes 2097160 | tf_op jit(solution)/shard_map/convert_element_type | solution.py:368
  9.0 6.7 %collective-permute-done = bf16[256,1024]{1,0:T(8,128)(2,1)S(1)} collective-permute-done((bf16[256,1024]{1,0:T(8,128)(2,1)S(1)}, bf16[256,1024]{1,0:T(8,128)(2,1)S(1)}, u32[]{:S(2)}, u32[]{:S(2)}) %collective-permute-start) | collective-permute-done | bytes 524320 | tf_op jit(solution)/shard_map/ppermute | solution.py:51
  17.1 1.6 collective-permute-start.3
  19.2 7.8 %collective-permute-done.2.refs_2_.refs_3_ = bf16[128,1024]{1,0:T(8,128)(2,1)S(1)} collective-permute-done((bf16[128,1024]{1,0:T(8,128)(2,1)S(1)}, bf16[128,1024]{1,0:T(8,128)(2,1)S(1)}, u32[]{:S(2)}, u32[]{:S(2)}) %collective-permute-start.2) | collective-permute-done | bytes 262176 | tf_op jit(solution)/shard_map/ppermute | solution.py:51
  27.0 4.4 %collective-permute-done.3.refs_1_ = bf16[256,1024]{1,0:T(8,128)(2,1)S(1)} collective-permute-done((bf16[256,1024]{1,0:T(8,128)(2,1)S(1)}, bf16[256,1024]{1,0:T(8,128)(2,1)S(1)}, u32[]{:S(2)}, u32[]{:S(2)}) %collective-permute-start.3) | collective-permute-done | bytes 524320 | tf_op jit(solution)/shard_map/ppermute | solution.py:51
  32.0 1.4 collective-permute-done.5.refs_3_
  33.5 5.9 %shard_map.58 = (bf16[1024,1024]{1,0:T(8,128)(2,1)}, bf16[1024,1024]{1,0:T(8,128)(2,1)}, bf16[1024,1024]{1,0:T(8,128)(2,1)S(1)}, bf16[256,1024]{1,0:T(8,128)(2,1)}, s32[8,128]{1,0:T(8,128)S(1)}) custom-call(s32[4]{0:T(128)S(1)} %pad_add_fusion.ids, s32[8,128]{1,0:T(8,128)S(1)} %broadcast_in_dim.12.token, ...), custom_call_target="tpu_custom_call", output_to_operand_aliasing={{4}: (1, {})} | custom-call | flops 1 | bytes 1 | tf_op jit(solution)/shard_map/pallas_call | solution.py:93
  39.4 1.3 collective-permute-start.9
  40.7 5.2 %collective-permute-done.6.refs_3_.refs_1_ = bf16[1024,256]{1,0:T(8,128)(2,1)S(1)} collective-permute-done((bf16[1024,256]{1,0:T(8,128)(2,1)}, bf16[1024,256]{1,0:T(8,128)(2,1)S(1)}, u32[]{:S(2)}, u32[]{:S(2)}) %collective-permute-start.6) | collective-permute-done | bytes 524320 | tf_op jit(solution)/shard_map/ppermute | solution.py:51
  46.5 1.3 convert_bitcast_fusion.1.refs_1_
  47.8 3.1 %shard_map.59 = (bf16[8,256,128]{2,1,0:T(8,128)(2,1)}, s32[8,128]{1,0:T(8,128)S(1)}) custom-call(s32[4]{0:T(128)S(1)} %pad_add_fusion.ids, s32[8,128]{1,0:T(8,128)S(1)} %get-tuple-element.61.token, bf16[1024,1024]{1,0:T(8,128)(2,1)} %get-tuple-element.62.refs_0_.refs_3_, ...), custom_call_target="tpu_custom_call", output_to_operand_aliasing={{1}: (1, {})} | custom-call | flops 1 | bytes 1 | tf_op jit(solution)/shard_map/pallas_call | solution.py:93
  50.9 4.2 %shard_map.60 = (f32[1024,256]{1,0:T(8,128)}, bf16[1024,256]{1,0:T(8,128)(2,1)}, s32[8,128]{1,0:T(8,128)S(1)}) custom-call(s32[4]{0:T(128)S(1)} %pad_add_fusion.ids, s32[8,128]{1,0:T(8,128)S(1)} %get-tuple-element.66.token, bf16[1024,1024]{1,0:T(8,128)(2,1)} %get-tuple-element.62.refs_0_.refs_3_, ...), custom_call_target="tpu_custom_call", output_to_operand_aliasing={{2}: (1, {})} | custom-call | flops 1 | bytes 1 | tf_op jit(solution)/shard_map/pallas_call | solution.py:93
  55.1 1.3 collective-permute-start.8
  56.4 4.3 %all-to-all-start = ((bf16[8,256,128]{2,1,0:T(8,128)(2,1)}), bf16[8,256,128]{2,1,0:T(8,128)(2,1)}, u32[]{:S(2)}, u32[]{:S(2)}) async-start(bf16[8,256,128]{2,1,0:T(8,128)(2,1)} %get-tuple-element.68), calls=%async_computation | async-start | bytes 1048576 | tf_op jit(solution)/shard_map/all_to_all | solution.py:66
  60.7 2.0 %collective-permute-start.11 = (bf16[256,1024]{1,0:T(8,128)(2,1)}, bf16[256,1024]{1,0:T(8,128)(2,1)}, u32[]{:S(2)}, u32[]{:S(2)}) collective-permute-start(bf16[256,1024]{1,0:T(8,128)(2,1)} %collective-permute-done.9), channel_id=1, source_target_pairs={{0,2},{2,0},{1,3},{3,1},{4,6},{6,4},{5,7},{7,5},{8,10},{10,8},{9,1... | collective-permute-start | bytes 1572872 | tf_op jit(solution)/shard_map/ppermute | solution.py:51
  62.8 7.4 %all-to-all-done.refs_1_ = bf16[8,256,128]{2,1,0:T(8,128)(2,1)} async-done(((bf16[8,256,128]{2,1,0:T(8,128)(2,1)}), bf16[8,256,128]{2,1,0:T(8,128)(2,1)}, u32[]{:S(2)}, u32[]{:S(2)}) %all-to-all-start) | async-done | bytes 524320 | tf_op jit(solution)/shard_map/all_to_all | solution.py:66
  70.1 4.2 %shard_map.61 = (f32[256,1024]{1,0:T(8,128)}, f32[1024,128]{1,0:T(8,128)}, bf16[1024,128]{1,0:T(8,128)(2,1)}, s32[8,128]{1,0:T(8,128)S(1)}) custom-call(s32[4]{0:T(128)S(1)} %pad_add_fusion.ids, s32[8,128]{1,0:T(8,128)S(1)} %get-tuple-element.67.token, bf16[1024,1024]{1,0:T(8,128)(2,1)} %get-tuple-element.62.refs_0_.refs_3_, ...), custom_call_target="tpu_custom_call", output_to_operand_aliasing={{3}: (1, {})} | custom-call | flops 1 | bytes 1 | tf_op jit(solution)/shard_map/pallas_call | solution.py:93
  75.7 5.0 %shard_map.62 = (bf16[1024,256]{1,0:T(8,128)(2,1)}, f32[1024,256]{1,0:T(8,128)}, bf16[1024,256]{1,0:T(8,128)(2,1)}, s32[8,128]{1,0:T(8,128)S(1)}) custom-call(s32[4]{0:T(128)S(1)} %pad_add_fusion.ids, s32[8,128]{1,0:T(8,128)S(1)} %get-tuple-element.70.token, bf16[1024,1024]{1,0:T(8,128)(2,1)S(1)} %get-tuple-element.71.refs_0_, ...), custom_call_target="tpu_custom_call", output_to_operand_aliasing={{3}: (1, {})} | custom-call | flops 1 | bytes 1 | tf_op jit(solution)/shard_map/pallas_call | solution.py:93
  84.6 3.8 %shard_map.63 = (bf16[1024,128]{1,0:T(8,128)(2,1)}, bf16[8,256,128]{2,1,0:T(8,128)(2,1)}, s32[8,128]{1,0:T(8,128)S(1)}) custom-call(s32[4]{0:T(128)S(1)} %pad_add_fusion.ids, s32[8,128]{1,0:T(8,128)S(1)} %get-tuple-element.75.token, bf16[1024,1024]{1,0:T(8,128)(2,1)S(1)} %get-tuple-element.71.refs_0_, ...), custom_call_target="tpu_custom_call", output_to_operand_aliasing={{2}: (1, {})} | custom-call | flops 1 | bytes 1 | tf_op jit(solution)/shard_map/pallas_call | solution.py:93
  88.4 2.7 %collective-permute-start.12 = (bf16[1024,256]{1,0:T(8,128)(2,1)}, bf16[1024,256]{1,0:T(8,128)(2,1)}, u32[]{:S(2)}, u32[]{:S(2)}) collective-permute-start(bf16[1024,256]{1,0:T(8,128)(2,1)} %get-tuple-element.80), channel_id=1, source_target_pairs={{16,8},{17,9},{18,10},{19,11},{20,12},{21,13},{22,14},{23,15}} | collective-permute-start | bytes 1572872 | tf_op jit(solution)/shard_map/ppermute | solution.py:393
  92.4 3.4 %all-to-all-start.1 = ((bf16[8,128,128]{2,1,0:T(8,128)(2,1)}), bf16[8,128,128]{2,1,0:T(8,128)(2,1)S(1)}, u32[]{:S(2)}, u32[]{:S(2)}) async-start(bf16[8,128,128]{2,1,0:T(8,128)(2,1)} %bitcast.26), calls=%async_computation.1 | async-start | bytes 524288 | tf_op jit(solution)/shard_map/all_to_all | solution.py:66
  95.8 6.6 %collective-permute-done.12.refs_1_.refs_4_ = bf16[1024,256]{1,0:T(8,128)(2,1)} collective-permute-done((bf16[1024,256]{1,0:T(8,128)(2,1)}, bf16[1024,256]{1,0:T(8,128)(2,1)}, u32[]{:S(2)}, u32[]{:S(2)}) %collective-permute-start.12) | collective-permute-done | bytes 524320 | tf_op jit(solution)/shard_map/ppermute | solution.py:393
  102.4 4.9 %collective-permute-done.13.refs_3_ = bf16[1024,256]{1,0:T(8,128)(2,1)} collective-permute-done((bf16[1024,256]{1,0:T(8,128)(2,1)}, bf16[1024,256]{1,0:T(8,128)(2,1)}, u32[]{:S(2)}, u32[]{:S(2)}) %collective-permute-start.13) | collective-permute-done | bytes 524320 | tf_op jit(solution)/shard_map/ppermute | solution.py:393
  107.3 3.8 %shard_map.64 = (bf16[1024,256]{1,0:T(8,128)(2,1)}, bf16[1024,256]{1,0:T(8,128)(2,1)}, s32[8,128]{1,0:T(8,128)S(1)}) custom-call(s32[4]{0:T(128)S(1)} %pad_add_fusion.ids, s32[8,128]{1,0:T(8,128)S(1)} %get-tuple-element.79.token, bf16[1024,1024]{1,0:T(8,128)(2,1)S(1)} %get-tuple-element.71.refs_0_, ...), custom_call_target="tpu_custom_call", output_to_operand_aliasing={{2}: (1, {})} | custom-call | flops 1 | bytes 1 | tf_op jit(solution)/shard_map/pallas_call | solution.py:93
  111.1 1.5 collective-permute-start.15
  112.6 2.1 %collective-permute-start.16 = (bf16[1024,256]{1,0:T(8,128)(2,1)}, bf16[1024,256]{1,0:T(8,128)(2,1)}, u32[]{:S(2)}, u32[]{:S(2)}) collective-permute-start(bf16[1024,256]{1,0:T(8,128)(2,1)} %get-tuple-element.91), channel_id=1, source_target_pairs={{16,8},{17,9},{18,10},{19,11},{20,12},{21,13},{22,14},{23,15}} | collective-permute-start | bytes 1572872 | tf_op jit(solution)/shard_map/ppermute | solution.py:393
  114.7 5.0 %shard_map.65 = (bf16[1024,1024]{1,0:T(8,128)(2,1)}, bf16[1024,256]{1,0:T(8,128)(2,1)}, s32[8,128]{1,0:T(8,128)S(1)}) custom-call(s32[4]{0:T(128)S(1)} %pad_add_fusion.ids, s32[8,128]{1,0:T(8,128)S(1)} %get-tuple-element.82.token, bf16[1024,1024]{1,0:T(8,128)(2,1)S(1)} %get-tuple-element.71.refs_0_, ...), custom_call_target="tpu_custom_call", output_to_operand_aliasing={{2}: (1, {})} | custom-call | flops 1 | bytes 1 | tf_op jit(solution)/shard_map/pallas_call | solution.py:93
  119.8 1.3 collective-permute-start.18
  121.1 2.3 %collective-permute-start.17 = (bf16[1024,256]{1,0:T(8,128)(2,1)}, bf16[1024,256]{1,0:T(8,128)(2,1)}, u32[]{:S(2)}, u32[]{:S(2)}) collective-permute-start(bf16[1024,256]{1,0:T(8,128)(2,1)} %get-tuple-element.94), channel_id=1, source_target_pairs={{16,8},{17,9},{18,10},{19,11},{20,12},{21,13},{22,14},{23,15}} | collective-permute-start | bytes 1572872 | tf_op jit(solution)/shard_map/ppermute | solution.py:455
  123.4 3.5 %all-to-all-start.2 = ((bf16[8,256,128]{2,1,0:T(8,128)(2,1)}), bf16[8,256,128]{2,1,0:T(8,128)(2,1)S(1)}, u32[]{:S(2)}, u32[]{:S(2)}) async-start(bf16[8,256,128]{2,1,0:T(8,128)(2,1)} %get-tuple-element.96), calls=%async_computation.2 | async-start | bytes 1048576 | tf_op jit(solution)/shard_map/all_to_all | solution.py:66
  127.9 5.1 %shard_map.66 = (f32[1024,1024]{1,0:T(8,128)}, bf16[1024,256]{1,0:T(8,128)(2,1)}, s32[8,128]{1,0:T(8,128)S(1)}) custom-call(s32[4]{0:T(128)S(1)} %pad_add_fusion.ids, s32[8,128]{1,0:T(8,128)S(1)} %get-tuple-element.87.token, bf16[1024,1024]{1,0:T(8,128)(2,1)S(1)} %get-tuple-element.71.refs_0_, ...), custom_call_target="tpu_custom_call", output_to_operand_aliasing={{2}: (1, {})} | custom-call | flops 1 | bytes 1 | tf_op jit(solution)/shard_map/pallas_call | solution.py:93
  133.0 2.7 %collective-permute-start.19 = (bf16[1024,256]{1,0:T(8,128)(2,1)}, bf16[1024,256]{1,0:T(8,128)(2,1)}, u32[]{:S(2)}, u32[]{:S(2)}) collective-permute-start(bf16[1024,256]{1,0:T(8,128)(2,1)} %get-tuple-element.98), channel_id=1, source_target_pairs={{0,4},{4,0},{1,5},{5,1},{2,6},{6,2},{3,7},{7,3},{8,12},{12,8},{9,1... | collective-permute-start | bytes 1572872 | tf_op jit(solution)/shard_map/ppermute | solution.py:51
  135.8 2.7 %shard_map.67 = (bf16[1024,256]{1,0:T(8,128)(2,1)}, s32[8,128]{1,0:T(8,128)S(1)}) custom-call(s32[4]{0:T(128)S(1)} %pad_add_fusion.ids, s32[8,128]{1,0:T(8,128)S(1)} %get-tuple-element.90.token, bf16[1024,1024]{1,0:T(8,128)(2,1)S(1)} %get-tuple-element.71.refs_0_, ...), custom_call_target="tpu_custom_call", output_to_operand_aliasing={{1}: (1, {})} | custom-call | flops 1 | bytes 1 | tf_op jit(solution)/shard_map/pallas_call | solution.py:93
  138.5 1.4 collective-permute-start.20
  140.0 7.7 %collective-permute-done.17.refs_3_ = bf16[1024,256]{1,0:T(8,128)(2,1)} collective-permute-done((bf16[1024,256]{1,0:T(8,128)(2,1)}, bf16[1024,256]{1,0:T(8,128)(2,1)}, u32[]{:S(2)}, u32[]{:S(2)}) %collective-permute-start.17) | collective-permute-done | bytes 524320 | tf_op jit(solution)/shard_map/ppermute | solution.py:455
  147.7 5.4 %shard_map.68 = (bf16[8,256,256]{2,1,0:T(8,128)(2,1)}, s32[8,128]{1,0:T(8,128)S(1)}) custom-call(s32[4]{0:T(128)S(1)} %pad_add_fusion.ids, s32[8,128]{1,0:T(8,128)S(1)} %get-tuple-element.92.token, bf16[1024,1024]{1,0:T(8,128)(2,1)S(1)} %get-tuple-element.71.refs_0_, bf16[1024,1024]{1,0:T(8,128)(2,1)} %get-tuple-element.76.refs_1_, ...), custom_call_target="tpu_custom_call", output_to_operand_aliasing={{1}: (1, {})} | custom-call | flops 1 | bytes 1 | tf_op jit(solution)/shard_map/pallas_call | solution.py:93
  153.1 4.3 %all-to-all-start.3 = ((bf16[8,256,256]{2,1,0:T(8,128)(2,1)}), bf16[8,256,256]{2,1,0:T(8,128)(2,1)}, u32[]{:S(2)}, u32[]{:S(2)}) async-start(bf16[8,256,256]{2,1,0:T(8,128)(2,1)} %get-tuple-element.106), calls=%async_computation.3 | async-start | bytes 2097152 | tf_op jit(solution)/shard_map/all_to_all | solution.py:66
  157.4 3.4 %shard_map.69 = (f32[1024,1024]{1,0:T(8,128)}, s32[8,128]{1,0:T(8,128)S(1)}) custom-call(s32[4]{0:T(128)S(1)} %pad_add_fusion.ids, s32[8,128]{1,0:T(8,128)S(1)} %get-tuple-element.97.token, bf16[1024,256]{1,0:T(8,128)(2,1)} %collective-permute-done.19.refs_0_, f32[1024,1024]{1,0:T(8,128)} %bitcast.22, ...), custom_call_target="tpu_custom_call", output_to_operand_aliasing={{1}: (1, {}), {0}: (4, {})} | custom-call | flops 1 | bytes 1 | tf_op jit(solution)/shard_map/pallas_call | solution.py:93
  160.7 5.2 %shard_map.70 = (f32[1024,1024]{1,0:T(8,128)}, bf16[1024,256]{1,0:T(8,128)(2,1)}, s32[8,128]{1,0:T(8,128)S(1)}) custom-call(s32[4]{0:T(128)S(1)} %pad_add_fusion.ids, s32[8,128]{1,0:T(8,128)S(1)} %get-tuple-element.100.token, bf16[1024,1024]{1,0:T(8,128)(2,1)S(1)} %get-tuple-element.71.refs_0_, ...), custom_call_target="tpu_custom_call", output_to_operand_aliasing={{2}: (1, {}), {0}: (9, {})} | custom-call | flops 1 | bytes 1 | tf_op jit(solution)/shard_map/pallas_call | solution.py:93
  166.0 2.8 %collective-permute-start.21 = (bf16[1024,256]{1,0:T(8,128)(2,1)}, bf16[1024,256]{1,0:T(8,128)(2,1)S(1)}, u32[]{:S(2)}, u32[]{:S(2)}) collective-permute-start(bf16[1024,256]{1,0:T(8,128)(2,1)} %get-tuple-element.110), channel_id=1, source_target_pairs={{0,4},{4,0},{1,5},{5,1},{2,6},{6,2},{3,7},{7,3},{8,12},{12,8},{9,1... | collective-permute-start | bytes 1572872 | tf_op jit(solution)/shard_map/ppermute | solution.py:51
  168.7 3.5 %all-to-all-done.3.refs_6_ = bf16[8,256,256]{2,1,0:T(8,128)(2,1)} async-done(((bf16[8,256,256]{2,1,0:T(8,128)(2,1)}), bf16[8,256,256]{2,1,0:T(8,128)(2,1)}, u32[]{:S(2)}, u32[]{:S(2)}) %all-to-all-start.3) | async-done | bytes 1048608 | tf_op jit(solution)/shard_map/all_to_all | solution.py:66
  172.3 6.9 %shard_map.71 = (f32[256,1024]{1,0:T(8,128)}, f32[256,1024]{1,0:T(8,128)}, s32[8,128]{1,0:T(8,128)S(1)}) custom-call(s32[4]{0:T(128)S(1)} %pad_add_fusion.ids, s32[8,128]{1,0:T(8,128)S(1)} %get-tuple-element.104.token, bf16[1024,1024]{1,0:T(8,128)(2,1)S(1)} %get-tuple-element.71.refs_0_, ...), custom_call_target="tpu_custom_call", output_to_operand_aliasing={{2}: (1, {})} | custom-call | flops 1 | bytes 1 | tf_op jit(solution)/shard_map/pallas_call | solution.py:93
  179.1 3.8 %collective-permute-done.21.refs_0_ = bf16[1024,256]{1,0:T(8,128)(2,1)S(1)} collective-permute-done((bf16[1024,256]{1,0:T(8,128)(2,1)}, bf16[1024,256]{1,0:T(8,128)(2,1)S(1)}, u32[]{:S(2)}, u32[]{:S(2)}) %collective-permute-start.21) | collective-permute-done | bytes 524320 | tf_op jit(solution)/shard_map/ppermute | solution.py:51
  183.0 2.9 %shard_map.72 = (f32[1024,1024]{1,0:T(8,128)}, s32[8,128]{1,0:T(8,128)S(1)}) custom-call(s32[4]{0:T(128)S(1)} %pad_add_fusion.ids, s32[8,128]{1,0:T(8,128)S(1)} %get-tuple-element.109.token, bf16[1024,256]{1,0:T(8,128)(2,1)S(1)} %collective-permute-done.21.refs_0_, f32[1024,1024]{1,0:T(8,128)} %bitcast.24, ...), custom_call_target="tpu_custom_call", output_to_operand_aliasing={{1}: (1, {}), {0}: (4, {})} | custom-call | flops 1 | bytes 1 | tf_op jit(solution)/shard_map/pallas_call | solution.py:93
  (37 shorter events, 10.7 us)
Async XLA Ops:
  1.9 13.7 %collective-permute-start = (bf16[256,1024]{1,0:T(8,128)(2,1)S(1)}, bf16[256,1024]{1,0:T(8,128)(2,1)S(1)}, u32[]{:S(2)}, u32[]{:S(2)}) collective-permute-start(bf16[256,1024]{1,0:T(8,128)(2,1)S(1)} %convert_bitcast_fusion), channel_id=1, source_target_pairs={{0,4},{4,0},{1,5},{5,1},{2,6},{6,2},{3,7},{7,3},{8,12},{12,8},{9,1... | collective-permute-start | bytes 1572872 | tf_op jit(solution)/shard_map/ppermute | solution.py:51
  3.5 13.4 %collective-permute-start.1 = (bf16[256,1024]{1,0:T(8,128)(2,1)S(1)}, bf16[256,1024]{1,0:T(8,128)(2,1)S(1)}, u32[]{:S(2)}, u32[]{:S(2)}) collective-permute-start(bf16[256,1024]{1,0:T(8,128)(2,1)S(1)} %convert_bitcast_fusion), channel_id=1, source_target_pairs={{0,2},{2,0},{1,3},{3,1},{4,6},{6,4},{5,7},{7,5},{8,10},{10,8},{9,1... | collective-permute-start | bytes 1572872 | tf_op jit(solution)/shard_map/ppermute | solution.py:51
  17.0 16.5 %copy-start.2 = (bf16[768,1024]{1,0:T(8,128)(2,1)}, bf16[768,1024]{1,0:T(8,128)(2,1)S(1)}, u32[]{:S(2)}) copy-start(bf16[768,1024]{1,0:T(8,128)(2,1)S(1)} %pad_maximum_fusion.refs_0_) | copy-start | bytes 4718596
  17.0 16.5 %collective-permute-start.4 = (bf16[768,1024]{1,0:T(8,128)(2,1)S(1)}, bf16[768,1024]{1,0:T(8,128)(2,1)}, u32[]{:S(2)}, u32[]{:S(2)}) collective-permute-start(bf16[768,1024]{1,0:T(8,128)(2,1)S(1)} %pad_maximum_fusion.refs_0_), channel_id=1, source_target_pairs={{0,1},{1,0},{2,3},{3,2},{4,5},{5,4},{6,7},{7,6},{8,9},{9,8},{10,11... | collective-permute-start | bytes 4718600 | tf_op jit(solution)/shard_map/ppermute | solution.py:51
  17.1 14.3 %collective-permute-start.3 = (bf16[256,1024]{1,0:T(8,128)(2,1)S(1)}, bf16[256,1024]{1,0:T(8,128)(2,1)S(1)}, u32[]{:S(2)}, u32[]{:S(2)}) collective-permute-start(bf16[256,1024]{1,0:T(8,128)(2,1)S(1)} %collective-permute-done), channel_id=1, source_target_pairs={{0,2},{2,0},{1,3},{3,1},{4,6},{6,4},{5,7},{7,5},{8,10},{10,8},{9,1... | collective-permute-start | bytes 1572872 | tf_op jit(solution)/shard_map/ppermute | solution.py:51
  18.7 8.4 %collective-permute-start.2 = (bf16[128,1024]{1,0:T(8,128)(2,1)S(1)}, bf16[128,1024]{1,0:T(8,128)(2,1)S(1)}, u32[]{:S(2)}, u32[]{:S(2)}) collective-permute-start(bf16[128,1024]{1,0:T(8,128)(2,1)S(1)} %dynamic-slice_bitcast_fusion), channel_id=1, source_target_pairs={{0,4},{4,0},{1,5},{5,1},{2,6},{6,2},{3,7},{7,3},{8,12},{12,8},{9,1... | collective-permute-start | bytes 786440 | tf_op jit(solution)/shard_map/ppermute | solution.py:51
  31.4 2.1 %copy-start.3 = (bf16[256,1024]{1,0:T(8,128)(2,1)}, bf16[256,1024]{1,0:T(8,128)(2,1)S(1)}, u32[]{:S(2)}) copy-start(bf16[256,1024]{1,0:T(8,128)(2,1)S(1)} %collective-permute-done.3.refs_1_) | copy-start | bytes 1572868
  31.4 2.0 %collective-permute-start.5 = (bf16[256,1024]{1,0:T(8,128)(2,1)S(1)}, bf16[256,1024]{1,0:T(8,128)(2,1)}, u32[]{:S(2)}, u32[]{:S(2)}) collective-permute-start(bf16[256,1024]{1,0:T(8,128)(2,1)S(1)} %collective-permute-done.3.refs_1_), channel_id=1, source_target_pairs={{0,1},{1,0},{2,3},{3,2},{4,5},{5,4},{6,7},{7,6},{8,9},{9,8},{10,11... | collective-permute-start | bytes 1572872 | tf_op jit(solution)/shard_map/ppermute | solution.py:51
  31.4 14.5 %collective-permute-start.6 = (bf16[1024,256]{1,0:T(8,128)(2,1)}, bf16[1024,256]{1,0:T(8,128)(2,1)S(1)}, u32[]{:S(2)}, u32[]{:S(2)}) collective-permute-start(bf16[1024,256]{1,0:T(8,128)(2,1)} %get-tuple-element.64), channel_id=1, source_target_pairs={{0,4},{4,0},{1,5},{5,1},{2,6},{6,2},{3,7},{7,3},{8,12},{12,8},{9,1... | collective-permute-start | bytes 1572872 | tf_op jit(solution)/shard_map/ppermute | solution.py:51
  39.4 21.3 %collective-permute-start.9 = (bf16[256,1024]{1,0:T(8,128)(2,1)}, bf16[256,1024]{1,0:T(8,128)(2,1)}, u32[]{:S(2)}, u32[]{:S(2)}) collective-permute-start(bf16[256,1024]{1,0:T(8,128)(2,1)} %get-tuple-element.73), channel_id=1, source_target_pairs={{24,16},{8,0},{25,17},{9,1},{26,18},{10,2},{27,19},{11,3},{28,20},... | collective-permute-start | bytes 1572872 | tf_op jit(solution)/shard_map/ppermute | solution.py:419
  46.0 16.8 %collective-permute-start.7 = (bf16[1024,256]{1,0:T(8,128)(2,1)}, bf16[1024,256]{1,0:T(8,128)(2,1)S(1)}, u32[]{:S(2)}, u32[]{:S(2)}) collective-permute-start(bf16[1024,256]{1,0:T(8,128)(2,1)} %get-tuple-element.69), channel_id=1, source_target_pairs={{0,4},{4,0},{1,5},{5,1},{2,6},{6,2},{3,7},{7,3},{8,12},{12,8},{9,1... | collective-permute-start | bytes 1572872 | tf_op jit(solution)/shard_map/ppermute | solution.py:51
  55.1 20.6 %collective-permute-start.8 = (bf16[1024,256]{1,0:T(8,128)(2,1)}, bf16[1024,256]{1,0:T(8,128)(2,1)S(1)}, u32[]{:S(2)}, u32[]{:S(2)}) collective-permute-start(bf16[1024,256]{1,0:T(8,128)(2,1)} %get-tuple-element.74.refs_2_), channel_id=1, source_target_pairs={{24,16},{25,17},{26,18},{27,19},{28,20},{29,21},{30,22},{31,23}} | collective-permute-start | bytes 1572872 | tf_op jit(solution)/shard_map/ppermute | solution.py:393
  56.4 13.8 %all-to-all-start = ((bf16[8,256,128]{2,1,0:T(8,128)(2,1)}), bf16[8,256,128]{2,1,0:T(8,128)(2,1)}, u32[]{:S(2)}, u32[]{:S(2)}) async-start(bf16[8,256,128]{2,1,0:T(8,128)(2,1)} %get-tuple-element.68), calls=%async_computation | async-start | bytes 1048576 | tf_op jit(solution)/shard_map/all_to_all | solution.py:66
  60.7 21.8 %collective-permute-start.11 = (bf16[256,1024]{1,0:T(8,128)(2,1)}, bf16[256,1024]{1,0:T(8,128)(2,1)}, u32[]{:S(2)}, u32[]{:S(2)}) collective-permute-start(bf16[256,1024]{1,0:T(8,128)(2,1)} %collective-permute-done.9), channel_id=1, source_target_pairs={{0,2},{2,0},{1,3},{3,1},{4,6},{6,4},{5,7},{7,5},{8,10},{10,8},{9,1... | collective-permute-start | bytes 1572872 | tf_op jit(solution)/shard_map/ppermute | solution.py:51
  74.4 10.2 %collective-permute-start.10 = (bf16[1024,128]{1,0:T(8,128)(2,1)}, bf16[1024,128]{1,0:T(8,128)(2,1)S(1)}, u32[]{:S(2)}, u32[]{:S(2)}) collective-permute-start(bf16[1024,128]{1,0:T(8,128)(2,1)} %get-tuple-element.77), channel_id=1, source_target_pairs={{24,16},{8,0},{25,17},{9,1},{26,18},{10,2},{27,19},{11,3},{28,20},... | collective-permute-start | bytes 786440 | tf_op jit(solution)/shard_map/ppermute | solution.py:431
  80.7 0.8 copy-start
  88.4 26.3 %collective-permute-start.14 = (bf16[512,1024]{1,0:T(8,128)(2,1)S(1)}, bf16[512,1024]{1,0:T(8,128)(2,1)}, u32[]{:S(2)}, u32[]{:S(2)}) collective-permute-start(bf16[512,1024]{1,0:T(8,128)(2,1)S(1)} %constant_dynamic-update-slice_fusion.refs_3_), channel_id=1, source_target_pairs={{0,1},{1,0},{2,3},{3,2},{4,5},{5,4},{6,7},{7,6},{8,9},{9,8},{10,11... | collective-permute-start | bytes 3145736 | tf_op jit(solution)/shard_map/ppermute | solution.py:51
  88.4 14.0 %collective-permute-start.12 = (bf16[1024,256]{1,0:T(8,128)(2,1)}, bf16[1024,256]{1,0:T(8,128)(2,1)}, u32[]{:S(2)}, u32[]{:S(2)}) collective-permute-start(bf16[1024,256]{1,0:T(8,128)(2,1)} %get-tuple-element.80), channel_id=1, source_target_pairs={{16,8},{17,9},{18,10},{19,11},{20,12},{21,13},{22,14},{23,15}} | collective-permute-start | bytes 1572872 | tf_op jit(solution)/shard_map/ppermute | solution.py:393
  91.1 16.3 %collective-permute-start.13 = (bf16[1024,256]{1,0:T(8,128)(2,1)}, bf16[1024,256]{1,0:T(8,128)(2,1)}, u32[]{:S(2)}, u32[]{:S(2)}) collective-permute-start(bf16[1024,256]{1,0:T(8,128)(2,1)} %get-tuple-element.81.refs_4_.refs_2_), channel_id=1, source_target_pairs={{24,16},{25,17},{26,18},{27,19},{28,20},{29,21},{30,22},{31,23}} | collective-permute-start | bytes 1572872 | tf_op jit(solution)/shard_map/ppermute | solution.py:393
  92.4 22.3 %all-to-all-start.1 = ((bf16[8,128,128]{2,1,0:T(8,128)(2,1)}), bf16[8,128,128]{2,1,0:T(8,128)(2,1)S(1)}, u32[]{:S(2)}, u32[]{:S(2)}) async-start(bf16[8,128,128]{2,1,0:T(8,128)(2,1)} %bitcast.26), calls=%async_computation.1 | async-start | bytes 524288 | tf_op jit(solution)/shard_map/all_to_all | solution.py:66
  111.1 15.8 %collective-permute-start.15 = (bf16[1024,256]{1,0:T(8,128)(2,1)}, bf16[1024,256]{1,0:T(8,128)(2,1)}, u32[]{:S(2)}, u32[]{:S(2)}) collective-permute-start(bf16[1024,256]{1,0:T(8,128)(2,1)} %get-tuple-element.89), channel_id=1, source_target_pairs={{8,0},{9,1},{10,2},{11,3},{12,4},{13,5},{14,6},{15,7}} | collective-permute-start | bytes 1572872 | tf_op jit(solution)/shard_map/ppermute | solution.py:393
  112.6 23.2 %collective-permute-start.16 = (bf16[1024,256]{1,0:T(8,128)(2,1)}, bf16[1024,256]{1,0:T(8,128)(2,1)}, u32[]{:S(2)}, u32[]{:S(2)}) collective-permute-start(bf16[1024,256]{1,0:T(8,128)(2,1)} %get-tuple-element.91), channel_id=1, source_target_pairs={{16,8},{17,9},{18,10},{19,11},{20,12},{21,13},{22,14},{23,15}} | collective-permute-start | bytes 1572872 | tf_op jit(solution)/shard_map/ppermute | solution.py:393
  119.8 20.2 %collective-permute-start.18 = (bf16[1024,256]{1,0:T(8,128)(2,1)}, bf16[1024,256]{1,0:T(8,128)(2,1)S(1)}, u32[]{:S(2)}, u32[]{:S(2)}) collective-permute-start(bf16[1024,256]{1,0:T(8,128)(2,1)} %get-tuple-element.94), channel_id=1, source_target_pairs={{16,0},{17,1},{18,2},{19,3},{20,4},{21,5},{22,6},{23,7}} | collective-permute-start | bytes 1572872 | tf_op jit(solution)/shard_map/ppermute | solution.py:455
  121.1 26.6 %collective-permute-start.17 = (bf16[1024,256]{1,0:T(8,128)(2,1)}, bf16[1024,256]{1,0:T(8,128)(2,1)}, u32[]{:S(2)}, u32[]{:S(2)}) collective-permute-start(bf16[1024,256]{1,0:T(8,128)(2,1)} %get-tuple-element.94), channel_id=1, source_target_pairs={{16,8},{17,9},{18,10},{19,11},{20,12},{21,13},{22,14},{23,15}} | collective-permute-start | bytes 1572872 | tf_op jit(solution)/shard_map/ppermute | solution.py:455
  123.4 16.6 %all-to-all-start.2 = ((bf16[8,256,128]{2,1,0:T(8,128)(2,1)}), bf16[8,256,128]{2,1,0:T(8,128)(2,1)S(1)}, u32[]{:S(2)}, u32[]{:S(2)}) async-start(bf16[8,256,128]{2,1,0:T(8,128)(2,1)} %get-tuple-element.96), calls=%async_computation.2 | async-start | bytes 1048576 | tf_op jit(solution)/shard_map/all_to_all | solution.py:66
  126.9 1.0 copy-start.1
  133.0 24.3 %collective-permute-start.19 = (bf16[1024,256]{1,0:T(8,128)(2,1)}, bf16[1024,256]{1,0:T(8,128)(2,1)}, u32[]{:S(2)}, u32[]{:S(2)}) collective-permute-start(bf16[1024,256]{1,0:T(8,128)(2,1)} %get-tuple-element.98), channel_id=1, source_target_pairs={{0,4},{4,0},{1,5},{5,1},{2,6},{6,2},{3,7},{7,3},{8,12},{12,8},{9,1... | collective-permute-start | bytes 1572872 | tf_op jit(solution)/shard_map/ppermute | solution.py:51
  138.5 22.2 %collective-permute-start.20 = (bf16[1024,256]{1,0:T(8,128)(2,1)}, bf16[1024,256]{1,0:T(8,128)(2,1)}, u32[]{:S(2)}, u32[]{:S(2)}) collective-permute-start(bf16[1024,256]{1,0:T(8,128)(2,1)} %get-tuple-element.102), channel_id=1, source_target_pairs={{8,0},{9,1},{10,2},{11,3},{12,4},{13,5},{14,6},{15,7}} | collective-permute-start | bytes 1572872 | tf_op jit(solution)/shard_map/ppermute | solution.py:393
  153.1 19.2 %all-to-all-start.3 = ((bf16[8,256,256]{2,1,0:T(8,128)(2,1)}), bf16[8,256,256]{2,1,0:T(8,128)(2,1)}, u32[]{:S(2)}, u32[]{:S(2)}) async-start(bf16[8,256,256]{2,1,0:T(8,128)(2,1)} %get-tuple-element.106), calls=%async_computation.3 | async-start | bytes 2097152 | tf_op jit(solution)/shard_map/all_to_all | solution.py:66
  166.0 17.0 %collective-permute-start.21 = (bf16[1024,256]{1,0:T(8,128)(2,1)}, bf16[1024,256]{1,0:T(8,128)(2,1)S(1)}, u32[]{:S(2)}, u32[]{:S(2)}) collective-permute-start(bf16[1024,256]{1,0:T(8,128)(2,1)} %get-tuple-element.110), channel_id=1, source_target_pairs={{0,4},{4,0},{1,5},{5,1},{2,6},{6,2},{3,7},{7,3},{8,12},{12,8},{9,1... | collective-permute-start | bytes 1572872 | tf_op jit(solution)/shard_map/ppermute | solution.py:51

commit v12 on v11

--- a/solution.py
+++ b/solution.py
@@ -136,7 +136,7 @@
         copy.wait()
 
 
-def spread_kernel(ids, e0, l_low, l_got, unused, m_ref):
+def spread_kernel(ids, e0, l_low, l_got, m_ref):
     part, rows = l_got.shape[0], l_low.shape[0]
 
     def product(slab):
@@ -269,18 +269,32 @@
         own[...] = (p[...] + got[...].astype(WIDE)).astype(LOW)
 
 
-def hop_kernel(ids, pair, got, own, now):
+def hop_kernel(ids, pair, got, own0, own1, now):
+    product = mm(pair[...], got[...])
+
+    @pl.when(ids[3] == 1)
+    def _():
+        now[...] = (product + own0[...].astype(WIDE)).astype(LOW)
+
+    @pl.when(ids[3] != 1)
+    def _():
+        now[...] = (product + own1[...].astype(WIDE)).astype(LOW)
+
+
+def end_hop_kernel(ids, pair, got, own, now):
     now[...] = (mm(pair[...], got[...]) + own[...].astype(WIDE)).astype(LOW)
 
 
-def hop_start_kernel(chunk, ids, pair, got_hop, own_hop, e0, got, offset, now, p, own, keep, sem):
-    hop_kernel(ids, pair, got_hop, own_hop, now)
+def hop_start_kernel(chunk, ids, pair, got_hop, own_hop, e0, got, offset, wave, p, own, keep, sem):
     start_kernel(chunk, ids, e0, got, offset, p, own, keep, sem)
 
-
-def hops_kernel(ids, pair, got_a, own_a, got_b, own_b, now_a, now_b):
-    hop_kernel(ids, pair, got_a, own_a, now_a)
-    hop_kernel(ids, pair, got_b, own_b, now_b)
+    @pl.when(ids[3] == 3)
+    def _():
+        wave[...] = own[...]
+
+    @pl.when(ids[3] != 3)
+    def _():
+        end_hop_kernel(ids, pair, got_hop, own_hop, wave)
 
 
 def last_kernel(chunk, ids, pair, later, p_far, got_a, got_b, got_c, offset, *refs):
@@ -389,11 +403,8 @@
             12, far_in=(2,), scratch=[keep, pltpu.SemaphoreType.DMA(())],
         )
 
-    def down(value, source):
-        return lax.ppermute(value, "z", [(source, source - 1)])
-
-    def hop(got, own):
-        return order.call(hop_kernel, [pair, got, in_hbm(own)], [hbm(size_d, width)], 8)[0]
+    def down(value, *sources):
+        return lax.ppermute(value, "z", [(source, source - 1) for source in sources])
 
     def last(i, p, gots, into):
         extra = [] if into is None else [into]
@@ -417,37 +428,33 @@
         scratch=[pltpu.VMEM((2, size_d, size_d), LOW), pltpu.SemaphoreType.DMA((8,))],
     )
     quarter = lax.ppermute(quarter, "z", level)
-    (m,) = order.call(spread_kernel, [in_hbm(e0), l_low, l_got, g_got[0]], [hbm(8, rows, part)], 8, far_in=(3,))
-    m = exchange(m)
     p0, own0 = start(0)
-    gots0 = [down(own0, 3)]
+    wave1 = down(own0, 3)
     quarter, own0 = tied((quarter, own0))
     quarter_y = swap(quarter, "y")
+    (m,) = order.call(spread_kernel, [in_hbm(e0), l_low, l_got], [hbm(8, rows, part)], 8)
+    m = exchange(m)
     prod, slab, a_low = order.call(
         spread_start_kernel, [in_hbm(e0), m, spread, l_got, g_got[1]],
         [hbm(rows, size_d, dtype=WIDE), hbm(size_d, part, dtype=WIDE), hbm(size_d, part)], 12,
         far_in=(4,), scratch=[slab_rows],
     )
     l_next = lax.ppermute(a_low, "z", level)
-    now0, p1, own1 = order.call(
-        functools.partial(hop_start_kernel, 1), [pair, gots0[0], in_hbm(own0), in_hbm(e0), g_got[1], offset],
+    wave2, p1, own1 = order.call(
+        functools.partial(hop_start_kernel, 1), [pair, wave1, in_hbm(own0), in_hbm(e0), g_got[1], offset],
         [hbm(size_d, width), hbm(size_d, width, dtype=WIDE), hbm(size_d, width)], 16,
         far_in=(5,), scratch=[keep, pltpu.SemaphoreType.DMA(())],
     )
-    gots0.append(down(now0, 2))
-    gots1 = [down(own1, 3)]
+    wave2 = down(wave2, 3, 2)
+
     quarters = jnp.concatenate([quarter, quarter_y], axis=0)
+    quarters = [quarters, swap(quarters, "c")]
     m, near = order.call(
-        spread_hop_kernel, [pair, in_hbm(e1), l_next, quarters], [hbm(size_d, part), hbm(8, rows, part)], 10, far_in=(3,)
+        spread_hop_kernel, [pair, in_hbm(e1), l_next, quarters[1]], [hbm(size_d, part), hbm(8, rows, part)], 10, far_in=(3,)
     )
     m = exchange(m.reshape(8, part, part))
-    quarters, near = tied((quarters, near))
-    quarters = [quarters, swap(quarters, "c")]
-    now0, now1 = order.call(
-        hops_kernel, [pair, gots0[1], in_hbm(own0), gots1[0], in_hbm(own1)], [hbm(size_d, width)] * 2, 10
-    )
-    gots0.append(down(now0, 1))
-    gots1.append(down(now1, 2))
+    (wave3,) = order.call(hop_kernel, [pair, wave2, in_hbm(own0), in_hbm(own1)], [hbm(size_d, width)], 10)
+    wave3 = down(wave3, 2, 1)
     following, far_slab = order.call(
         next_kernel, [pair, in_hbm(slab), m, *quarters], [hbm(size_d, size_d), hbm(size_d, rows)], 12,
         far_in=(3, 4), scratch=[pltpu.VMEM((part, size_d), LOW), pltpu.SemaphoreType.DMA((4,))],
@@ -456,16 +463,17 @@
     near, far_slab = tied((near, far_slab))
     near = exchange(near)
 
-    out_offset, other0 = last(0, p0, gots0, None)
+    out_offset, other0 = last(0, p0, [wave1, wave2, wave3], None)
     other0 = swap(other0, "x")
-    gots1.append(down(hop(gots1[1], own1), 1))
+    (wave4,) = order.call(end_hop_kernel, [pair, wave3, in_hbm(own1)], [hbm(size_d, width)], 8)
+    wave4 = down(wave4, 1)
     (m,) = order.call(
         far_kernel, [pair, in_hbm(e1), in_hbm(following), *far, near], [hbm(8, rows, rows)], 14,
         far_in=(5,), scratch=[pltpu.VMEM((size_d, rows), LOW)],
     )
     m = exchange(m)
     out_offset = add(0, other0, out_offset)
-    out_offset, other1 = last(1, p1, gots1, out_offset)
+    out_offset, other1 = last(1, p1, [wave2, wave3, wave4], out_offset)
     other1 = swap(other1, "x")
     out_gain, out_spread = order.call(
         end_kernel, [pair, in_hbm(e1), in_hbm(following), near, in_hbm(prod), spread, m],

time: 189 us -> 205 us (1.085)
  waiting for transfers between devices: 61.7 us -> 83.4 us
  starting transfers between devices: 45.9 us -> 42 us
    ppermute x1, waiting for transfers between devices: 0.95 us -> 18 us  [suffix(): l_next = lax.ppermute(a_low, 'z', level)]
    ppermute x6 -> x4, waiting for transfers between devices: 11.5 us -> 0.01 us  [down(): lax.ppermute(value, 'z', [(source, source - 1) for source in sources])]
    ppermute x12, waiting for transfers between devices: 30.6 us -> 38.7 us  [swap(): return lax.ppermute(value, axis, [(0, 1), (1, 0)])]
    ppermute x1, waiting for transfers between devices: 0.01 us -> 5.96 us  [suffix(): quarter = lax.ppermute(quarter, 'z', level)]
    all_to_all x4, waiting for transfers between devices: 10.9 us -> 14.6 us  [exchange(): return lax.all_to_all(blocks, GROUP, 0, 0)]
    ppermute x6 -> x4, starting transfers between devices: 10.3 us -> 6.83 us  [down(): lax.ppermute(value, 'z', [(source, source - 1) for source in sources])]
  transfers between devices with their start and end apart: 26 -> 24, of which waited for: 13 -> 14; matrix products, arithmetic and copies ran while one was open for 4% -> 3% of each run, Pallas kernels for 32% -> 32%
where the time goes in v12:
time: 205 us; the launch traced here: 202 us
  waiting for transfers between devices  83.4 us (41%)
  Pallas kernels  66.7 us (33%)
  starting transfers between devices  42 us (20%)
  local copies, waits for them, and re-layouts  6.23 us (3%)
  other arithmetic  2.85 us (1%)
    pallas_call x15, Pallas kernels, call(): pl.pallas_call(body, in_specs=[SMEM, ANY] + [ANY if i in far_in else VMEM...  66.7 us
    ppermute x12, waiting for transfers between devices, swap(): return lax.ppermute(value, axis, [(0, 1), (1, 0)])  38.7 us
    ppermute x1, waiting for transfers between devices, suffix(): l_next = lax.ppermute(a_low, 'z', level)  18 us
    all_to_all x4, starting transfers between devices, exchange(): return lax.all_to_all(blocks, GROUP, 0, 0)  15.3 us
    all_to_all x4, waiting for transfers between devices, exchange(): return lax.all_to_all(blocks, GROUP, 0, 0)  14.6 us
    ppermute x12, starting transfers between devices, swap(): return lax.ppermute(value, axis, [(0, 1), (1, 0)])  13 us
    ppermute x4, starting transfers between devices, down(): lax.ppermute(value, 'z', [(source, source - 1) for source in sources])  6.83 us
    ppermute x1, waiting for transfers between devices, suffix(): lax.ppermute(far_slab, 'z', [(2, 1)])  6.16 us
  transfers between devices with their start and end apart: 24, of which 14 were waited for; matrix products, arithmetic and copies ran while one was open for 3% of the time, Pallas kernels for 32%

profile of v12, /device:TPU:16, one launch (start us, length us, event | category | flops | bytes accessed | tf_op | source)
XLA Modules:
  0.0 202.2 jit_solution(15235931077945266394)
XLA Ops:
  0.6 1.3 convert_bitcast_fusion
  1.9 1.6 collective-permute-start
  3.5 1.5 collective-permute-start.1
  5.0 1.3 convert_element_type.25
  6.3 2.7 %fusion.1 = (bf16[1024,256]{1,0:T(8,128)(2,1)}, bf16[1024,256]{1,0:T(8,128)(2,1)}) fusion(f32[1,1024,1024]{2,1,0:T(8,128)} %param.5, s32[]{:T(128)S(6)} %select_n.11, s32[]{:T(128)S(6)} %select_n.10), kind=kLoop, calls=%fused_computation.4 | loop fusion | bytes 2097160 | tf_op jit(solution)/shard_map/convert_element_type | solution.py:382
  9.0 6.6 %collective-permute-done = bf16[256,1024]{1,0:T(8,128)(2,1)S(1)} collective-permute-done((bf16[256,1024]{1,0:T(8,128)(2,1)S(1)}, bf16[256,1024]{1,0:T(8,128)(2,1)S(1)}, u32[]{:S(2)}, u32[]{:S(2)}) %collective-permute-start) | collective-permute-done | bytes 524320 | tf_op jit(solution)/shard_map/ppermute | solution.py:51
  17.1 1.6 collective-permute-start.3
  19.2 7.8 %collective-permute-done.2.refs_2_.refs_3_ = bf16[128,1024]{1,0:T(8,128)(2,1)S(1)} collective-permute-done((bf16[128,1024]{1,0:T(8,128)(2,1)S(1)}, bf16[128,1024]{1,0:T(8,128)(2,1)S(1)}, u32[]{:S(2)}, u32[]{:S(2)}) %collective-permute-start.2) | collective-permute-done | bytes 262176 | tf_op jit(solution)/shard_map/ppermute | solution.py:51
  27.0 4.4 %collective-permute-done.3.refs_1_ = bf16[256,1024]{1,0:T(8,128)(2,1)S(1)} collective-permute-done((bf16[256,1024]{1,0:T(8,128)(2,1)S(1)}, bf16[256,1024]{1,0:T(8,128)(2,1)S(1)}, u32[]{:S(2)}, u32[]{:S(2)}) %collective-permute-start.3) | collective-permute-done | bytes 524320 | tf_op jit(solution)/shard_map/ppermute | solution.py:51
  32.0 1.3 collective-permute-done.5.refs_3_
  34.1 5.9 %shard_map.58 = (bf16[1024,1024]{1,0:T(8,128)(2,1)}, bf16[1024,1024]{1,0:T(8,128)(2,1)}, bf16[1024,1024]{1,0:T(8,128)(2,1)S(1)}, bf16[256,1024]{1,0:T(8,128)(2,1)}, s32[8,128]{1,0:T(8,128)S(1)}) custom-call(s32[4]{0:T(128)S(1)} %pad_add_fusion.ids, s32[8,128]{1,0:T(8,128)S(1)} %broadcast_in_dim.12.token, ...), custom_call_target="tpu_custom_call", output_to_operand_aliasing={{4}: (1, {})} | custom-call | flops 1 | bytes 1 | tf_op jit(solution)/shard_map/pallas_call | solution.py:93
  40.1 1.3 collective-permute-start.9
  41.4 4.6 %collective-permute-done.6.refs_1_ = bf16[1024,256]{1,0:T(8,128)(2,1)S(1)} collective-permute-done((bf16[1024,256]{1,0:T(8,128)(2,1)}, bf16[1024,256]{1,0:T(8,128)(2,1)S(1)}, u32[]{:S(2)}, u32[]{:S(2)}) %collective-permute-start.6) | collective-permute-done | bytes 524320 | tf_op jit(solution)/shard_map/ppermute | solution.py:51
  46.0 4.2 %shard_map.59 = (f32[1024,256]{1,0:T(8,128)}, bf16[1024,256]{1,0:T(8,128)(2,1)}, s32[8,128]{1,0:T(8,128)S(1)}) custom-call(s32[4]{0:T(128)S(1)} %pad_add_fusion.ids, s32[8,128]{1,0:T(8,128)S(1)} %get-tuple-element.58.token, bf16[1024,1024]{1,0:T(8,128)(2,1)} %get-tuple-element.59.refs_0_.refs_3_, ...), custom_call_target="tpu_custom_call", output_to_operand_aliasing={{2}: (1, {})} | custom-call | flops 1 | bytes 1 | tf_op jit(solution)/shard_map/pallas_call | solution.py:93
  50.2 6.0 %collective-permute-done.9 = bf16[256,1024]{1,0:T(8,128)(2,1)S(1)} collective-permute-done((bf16[256,1024]{1,0:T(8,128)(2,1)}, bf16[256,1024]{1,0:T(8,128)(2,1)S(1)}, u32[]{:S(2)}, u32[]{:S(2)}) %collective-permute-start.9) | collective-permute-done | bytes 524320 | tf_op jit(solution)/shard_map/ppermute | solution.py:430
  56.1 1.5 collective-permute-start.11
  60.3 9.0 %collective-permute-done.11 = bf16[256,1024]{1,0:T(8,128)(2,1)S(1)} collective-permute-done((bf16[256,1024]{1,0:T(8,128)(2,1)S(1)}, bf16[256,1024]{1,0:T(8,128)(2,1)S(1)}, u32[]{:S(2)}, u32[]{:S(2)}) %collective-permute-start.11) | collective-permute-done | bytes 524320 | tf_op jit(solution)/shard_map/ppermute | solution.py:51
  70.2 3.1 %shard_map.60 = (bf16[8,256,128]{2,1,0:T(8,128)(2,1)}, s32[8,128]{1,0:T(8,128)S(1)}) custom-call(s32[4]{0:T(128)S(1)} %pad_add_fusion.ids, s32[8,128]{1,0:T(8,128)S(1)} %get-tuple-element.62.token, bf16[1024,1024]{1,0:T(8,128)(2,1)} %get-tuple-element.59.refs_0_.refs_3_, ...), custom_call_target="tpu_custom_call", output_to_operand_aliasing={{1}: (1, {})} | custom-call | flops 1 | bytes 1 | tf_op jit(solution)/shard_map/pallas_call | solution.py:93
  73.3 4.1 %all-to-all-start = ((bf16[8,256,128]{2,1,0:T(8,128)(2,1)}), bf16[8,256,128]{2,1,0:T(8,128)(2,1)}, u32[]{:S(2)}, u32[]{:S(2)}) async-start(bf16[8,256,128]{2,1,0:T(8,128)(2,1)} %get-tuple-element.65), calls=%async_computation | async-start | bytes 1048576 | tf_op jit(solution)/shard_map/all_to_all | solution.py:66
  77.5 9.3 %all-to-all-done.refs_1_ = bf16[8,256,128]{2,1,0:T(8,128)(2,1)} async-done(((bf16[8,256,128]{2,1,0:T(8,128)(2,1)}), bf16[8,256,128]{2,1,0:T(8,128)(2,1)}, u32[]{:S(2)}, u32[]{:S(2)}) %all-to-all-start) | async-done | bytes 524320 | tf_op jit(solution)/shard_map/all_to_all | solution.py:66
  86.7 4.2 %shard_map.61 = (f32[256,1024]{1,0:T(8,128)}, f32[1024,128]{1,0:T(8,128)}, bf16[1024,128]{1,0:T(8,128)(2,1)}, s32[8,128]{1,0:T(8,128)S(1)}) custom-call(s32[4]{0:T(128)S(1)} %pad_add_fusion.ids, s32[8,128]{1,0:T(8,128)S(1)} %get-tuple-element.64.token, bf16[1024,1024]{1,0:T(8,128)(2,1)} %get-tuple-element.59.refs_0_.refs_3_, ...), custom_call_target="tpu_custom_call", output_to_operand_aliasing={{3}: (1, {})} | custom-call | flops 1 | bytes 1 | tf_op jit(solution)/shard_map/pallas_call | solution.py:93
  91.0 5.4 %shard_map.62 = (bf16[1024,256]{1,0:T(8,128)(2,1)}, f32[1024,256]{1,0:T(8,128)}, bf16[1024,256]{1,0:T(8,128)(2,1)}, s32[8,128]{1,0:T(8,128)S(1)}) custom-call(s32[4]{0:T(128)S(1)} %pad_add_fusion.ids, s32[8,128]{1,0:T(8,128)S(1)} %get-tuple-element.67.token, bf16[1024,1024]{1,0:T(8,128)(2,1)S(1)} %get-tuple-element.68.refs_0_, ...), custom_call_target="tpu_custom_call", output_to_operand_aliasing={{3}: (1, {})} | custom-call | flops 1 | bytes 1 | tf_op jit(solution)/shard_map/pallas_call | solution.py:93
  96.4 1.9 collective-permute-start.13
  98.3 1.3 collective-permute-start.10
  99.6 18.0 %collective-permute-done.10.refs_2_ = bf16[1024,128]{1,0:T(8,128)(2,1)S(1)} collective-permute-done((bf16[1024,128]{1,0:T(8,128)(2,1)S(1)}, bf16[1024,128]{1,0:T(8,128)(2,1)S(1)}, u32[]{:S(2)}, u32[]{:S(2)}) %collective-permute-start.10) | collective-permute-done | bytes 262176 | tf_op jit(solution)/shard_map/ppermute | solution.py:442
  117.6 3.8 %shard_map.63 = (bf16[1024,128]{1,0:T(8,128)(2,1)}, bf16[8,256,128]{2,1,0:T(8,128)(2,1)}, s32[8,128]{1,0:T(8,128)S(1)}) custom-call(s32[4]{0:T(128)S(1)} %pad_add_fusion.ids, s32[8,128]{1,0:T(8,128)S(1)} %get-tuple-element.72.token, bf16[1024,1024]{1,0:T(8,128)(2,1)S(1)} %get-tuple-element.68.refs_0_, ...), custom_call_target="tpu_custom_call", output_to_operand_aliasing={{2}: (1, {})} | custom-call | flops 1 | bytes 1 | tf_op jit(solution)/shard_map/pallas_call | solution.py:93
  121.4 3.4 %all-to-all-start.1 = ((bf16[8,128,128]{2,1,0:T(8,128)(2,1)}), bf16[8,128,128]{2,1,0:T(8,128)(2,1)S(1)}, u32[]{:S(2)}, u32[]{:S(2)}) async-start(bf16[8,128,128]{2,1,0:T(8,128)(2,1)} %bitcast.26), calls=%async_computation.1 | async-start | bytes 524288 | tf_op jit(solution)/shard_map/all_to_all | solution.py:66
  124.8 2.8 %shard_map.64 = (bf16[1024,256]{1,0:T(8,128)(2,1)}, s32[8,128]{1,0:T(8,128)S(1)}) custom-call(s32[4]{0:T(128)S(1)} %pad_add_fusion.ids, s32[8,128]{1,0:T(8,128)S(1)} %get-tuple-element.76.token, bf16[1024,1024]{1,0:T(8,128)(2,1)S(1)} %get-tuple-element.68.refs_0_, ...), custom_call_target="tpu_custom_call", output_to_operand_aliasing={{1}: (1, {})} | custom-call | flops 1 | bytes 1 | tf_op jit(solution)/shard_map/pallas_call | solution.py:93
  127.6 2.1 %collective-permute-start.14 = (bf16[1024,256]{1,0:T(8,128)(2,1)}, bf16[1024,256]{1,0:T(8,128)(2,1)}, u32[]{:S(2)}, u32[]{:S(2)}) collective-permute-start(bf16[1024,256]{1,0:T(8,128)(2,1)} %get-tuple-element.84), channel_id=1, source_target_pairs={{16,8},{8,0},{17,9},{9,1},{18,10},{10,2},{19,11},{11,3},{20,12},{1... | collective-permute-start | bytes 1572872 | tf_op jit(solution)/shard_map/ppermute | solution.py:407
  129.8 1.4 all-to-all-done.1.refs_2_
  131.2 5.7 %shard_map.65 = (bf16[1024,1024]{1,0:T(8,128)(2,1)}, bf16[1024,256]{1,0:T(8,128)(2,1)}, s32[8,128]{1,0:T(8,128)S(1)}) custom-call(s32[4]{0:T(128)S(1)} %pad_add_fusion.ids, s32[8,128]{1,0:T(8,128)S(1)} %get-tuple-element.79.token, bf16[1024,1024]{1,0:T(8,128)(2,1)S(1)} %get-tuple-element.68.refs_0_, ...), custom_call_target="tpu_custom_call", output_to_operand_aliasing={{2}: (1, {})} | custom-call | flops 1 | bytes 1 | tf_op jit(solution)/shard_map/pallas_call | solution.py:93
  136.9 2.1 %collective-permute-start.16 = (bf16[1024,256]{1,0:T(8,128)(2,1)}, bf16[1024,256]{1,0:T(8,128)(2,1)}, u32[]{:S(2)}, u32[]{:S(2)}) collective-permute-start(bf16[1024,256]{1,0:T(8,128)(2,1)} %get-tuple-element.88), channel_id=1, source_target_pairs={{16,0},{17,1},{18,2},{19,3},{20,4},{21,5},{22,6},{23,7}} | collective-permute-start | bytes 1572872 | tf_op jit(solution)/shard_map/ppermute | solution.py:462
  139.0 2.1 %collective-permute-start.15 = (bf16[1024,256]{1,0:T(8,128)(2,1)}, bf16[1024,256]{1,0:T(8,128)(2,1)}, u32[]{:S(2)}, u32[]{:S(2)}) collective-permute-start(bf16[1024,256]{1,0:T(8,128)(2,1)} %get-tuple-element.88), channel_id=1, source_target_pairs={{16,8},{17,9},{18,10},{19,11},{20,12},{21,13},{22,14},{23,15}} | collective-permute-start | bytes 1572872 | tf_op jit(solution)/shard_map/ppermute | solution.py:462
  141.1 3.5 %all-to-all-start.2 = ((bf16[8,256,128]{2,1,0:T(8,128)(2,1)}), bf16[8,256,128]{2,1,0:T(8,128)(2,1)S(1)}, u32[]{:S(2)}, u32[]{:S(2)}) async-start(bf16[8,256,128]{2,1,0:T(8,128)(2,1)} %get-tuple-element.90), calls=%async_computation.2 | async-start | bytes 1048576 | tf_op jit(solution)/shard_map/all_to_all | solution.py:66
  145.7 5.1 %shard_map.66 = (f32[1024,1024]{1,0:T(8,128)}, bf16[1024,256]{1,0:T(8,128)(2,1)}, s32[8,128]{1,0:T(8,128)S(1)}) custom-call(s32[4]{0:T(128)S(1)} %pad_add_fusion.ids, s32[8,128]{1,0:T(8,128)S(1)} %get-tuple-element.82.token, bf16[1024,1024]{1,0:T(8,128)(2,1)S(1)} %get-tuple-element.68.refs_0_, ...), custom_call_target="tpu_custom_call", output_to_operand_aliasing={{2}: (1, {})} | custom-call | flops 1 | bytes 1 | tf_op jit(solution)/shard_map/pallas_call | solution.py:93
  150.7 2.6 %collective-permute-start.17 = (bf16[1024,256]{1,0:T(8,128)(2,1)}, bf16[1024,256]{1,0:T(8,128)(2,1)}, u32[]{:S(2)}, u32[]{:S(2)}) collective-permute-start(bf16[1024,256]{1,0:T(8,128)(2,1)} %get-tuple-element.92), channel_id=1, source_target_pairs={{0,4},{4,0},{1,5},{5,1},{2,6},{6,2},{3,7},{7,3},{8,12},{12,8},{9,1... | collective-permute-start | bytes 1572872 | tf_op jit(solution)/shard_map/ppermute | solution.py:51
  153.3 2.7 %shard_map.67 = (bf16[1024,256]{1,0:T(8,128)(2,1)}, s32[8,128]{1,0:T(8,128)S(1)}) custom-call(s32[4]{0:T(128)S(1)} %pad_add_fusion.ids, s32[8,128]{1,0:T(8,128)S(1)} %get-tuple-element.85.token, bf16[1024,1024]{1,0:T(8,128)(2,1)S(1)} %get-tuple-element.68.refs_0_, ...), custom_call_target="tpu_custom_call", output_to_operand_aliasing={{1}: (1, {})} | custom-call | flops 1 | bytes 1 | tf_op jit(solution)/shard_map/pallas_call | solution.py:93
  156.1 1.5 collective-permute-start.18
  157.6 6.2 %collective-permute-done.15.refs_3_ = bf16[1024,256]{1,0:T(8,128)(2,1)} collective-permute-done((bf16[1024,256]{1,0:T(8,128)(2,1)}, bf16[1024,256]{1,0:T(8,128)(2,1)}, u32[]{:S(2)}, u32[]{:S(2)}) %collective-permute-start.15) | collective-permute-done | bytes 524320 | tf_op jit(solution)/shard_map/ppermute | solution.py:462
  163.7 5.5 %shard_map.68 = (bf16[8,256,256]{2,1,0:T(8,128)(2,1)}, s32[8,128]{1,0:T(8,128)S(1)}) custom-call(s32[4]{0:T(128)S(1)} %pad_add_fusion.ids, s32[8,128]{1,0:T(8,128)S(1)} %get-tuple-element.86.token, bf16[1024,1024]{1,0:T(8,128)(2,1)S(1)} %get-tuple-element.68.refs_0_, bf16[1024,1024]{1,0:T(8,128)(2,1)} %get-tuple-element.73.refs_1_, ...), custom_call_target="tpu_custom_call", output_to_operand_aliasing={{1}: (1, {})} | custom-call | flops 1 | bytes 1 | tf_op jit(solution)/shard_map/pallas_call | solution.py:93
  169.2 4.3 %all-to-all-start.3 = ((bf16[8,256,256]{2,1,0:T(8,128)(2,1)}), bf16[8,256,256]{2,1,0:T(8,128)(2,1)}, u32[]{:S(2)}, u32[]{:S(2)}) async-start(bf16[8,256,256]{2,1,0:T(8,128)(2,1)} %get-tuple-element.100), calls=%async_computation.3 | async-start | bytes 2097152 | tf_op jit(solution)/shard_map/all_to_all | solution.py:66
  173.5 3.4 %shard_map.69 = (f32[1024,1024]{1,0:T(8,128)}, s32[8,128]{1,0:T(8,128)S(1)}) custom-call(s32[4]{0:T(128)S(1)} %pad_add_fusion.ids, s32[8,128]{1,0:T(8,128)S(1)} %get-tuple-element.91.token, bf16[1024,256]{1,0:T(8,128)(2,1)} %collective-permute-done.17.refs_0_, f32[1024,1024]{1,0:T(8,128)} %bitcast.22, ...), custom_call_target="tpu_custom_call", output_to_operand_aliasing={{1}: (1, {}), {0}: (4, {})} | custom-call | flops 1 | bytes 1 | tf_op jit(solution)/shard_map/pallas_call | solution.py:93
  176.9 5.1 %shard_map.70 = (f32[1024,1024]{1,0:T(8,128)}, bf16[1024,256]{1,0:T(8,128)(2,1)}, s32[8,128]{1,0:T(8,128)S(1)}) custom-call(s32[4]{0:T(128)S(1)} %pad_add_fusion.ids, s32[8,128]{1,0:T(8,128)S(1)} %get-tuple-element.94.token, bf16[1024,1024]{1,0:T(8,128)(2,1)S(1)} %get-tuple-element.68.refs_0_, ...), custom_call_target="tpu_custom_call", output_to_operand_aliasing={{2}: (1, {}), {0}: (9, {})} | custom-call | flops 1 | bytes 1 | tf_op jit(solution)/shard_map/pallas_call | solution.py:93
  182.0 2.6 %collective-permute-start.19 = (bf16[1024,256]{1,0:T(8,128)(2,1)}, bf16[1024,256]{1,0:T(8,128)(2,1)S(1)}, u32[]{:S(2)}, u32[]{:S(2)}) collective-permute-start(bf16[1024,256]{1,0:T(8,128)(2,1)} %get-tuple-element.104), channel_id=1, source_target_pairs={{0,4},{4,0},{1,5},{5,1},{2,6},{6,2},{3,7},{7,3},{8,12},{12,8},{9,1... | collective-permute-start | bytes 1572872 | tf_op jit(solution)/shard_map/ppermute | solution.py:51
  184.6 3.9 %all-to-all-done.3.refs_6_ = bf16[8,256,256]{2,1,0:T(8,128)(2,1)} async-done(((bf16[8,256,256]{2,1,0:T(8,128)(2,1)}), bf16[8,256,256]{2,1,0:T(8,128)(2,1)}, u32[]{:S(2)}, u32[]{:S(2)}) %all-to-all-start.3) | async-done | bytes 1048608 | tf_op jit(solution)/shard_map/all_to_all | solution.py:66
  188.5 6.9 %shard_map.71 = (f32[256,1024]{1,0:T(8,128)}, f32[256,1024]{1,0:T(8,128)}, s32[8,128]{1,0:T(8,128)S(1)}) custom-call(s32[4]{0:T(128)S(1)} %pad_add_fusion.ids, s32[8,128]{1,0:T(8,128)S(1)} %get-tuple-element.98.token, bf16[1024,1024]{1,0:T(8,128)(2,1)S(1)} %get-tuple-element.68.refs_0_, ...), custom_call_target="tpu_custom_call", output_to_operand_aliasing={{2}: (1, {})} | custom-call | flops 1 | bytes 1 | tf_op jit(solution)/shard_map/pallas_call | solution.py:93
  195.3 3.8 %collective-permute-done.19.refs_0_ = bf16[1024,256]{1,0:T(8,128)(2,1)S(1)} collective-permute-done((bf16[1024,256]{1,0:T(8,128)(2,1)}, bf16[1024,256]{1,0:T(8,128)(2,1)S(1)}, u32[]{:S(2)}, u32[]{:S(2)}) %collective-permute-start.19) | collective-permute-done | bytes 524320 | tf_op jit(solution)/shard_map/ppermute | solution.py:51
  199.1 2.9 %shard_map.72 = (f32[1024,1024]{1,0:T(8,128)}, s32[8,128]{1,0:T(8,128)S(1)}) custom-call(s32[4]{0:T(128)S(1)} %pad_add_fusion.ids, s32[8,128]{1,0:T(8,128)S(1)} %get-tuple-element.103.token, bf16[1024,256]{1,0:T(8,128)(2,1)S(1)} %collective-permute-done.19.refs_0_, f32[1024,1024]{1,0:T(8,128)} %bitcast.24, ...), custom_call_target="tpu_custom_call", output_to_operand_aliasing={{1}: (1, {}), {0}: (4, {})} | custom-call | flops 1 | bytes 1 | tf_op jit(solution)/shard_map/pallas_call | solution.py:93
  (39 shorter events, 8.0 us)
Async XLA Ops:
  1.9 13.7 %collective-permute-start = (bf16[256,1024]{1,0:T(8,128)(2,1)S(1)}, bf16[256,1024]{1,0:T(8,128)(2,1)S(1)}, u32[]{:S(2)}, u32[]{:S(2)}) collective-permute-start(bf16[256,1024]{1,0:T(8,128)(2,1)S(1)} %convert_bitcast_fusion), channel_id=1, source_target_pairs={{0,4},{4,0},{1,5},{5,1},{2,6},{6,2},{3,7},{7,3},{8,12},{12,8},{9,1... | collective-permute-start | bytes 1572872 | tf_op jit(solution)/shard_map/ppermute | solution.py:51
  3.5 13.4 %collective-permute-start.1 = (bf16[256,1024]{1,0:T(8,128)(2,1)S(1)}, bf16[256,1024]{1,0:T(8,128)(2,1)S(1)}, u32[]{:S(2)}, u32[]{:S(2)}) collective-permute-start(bf16[256,1024]{1,0:T(8,128)(2,1)S(1)} %convert_bitcast_fusion), channel_id=1, source_target_pairs={{0,2},{2,0},{1,3},{3,1},{4,6},{6,4},{5,7},{7,5},{8,10},{10,8},{9,1... | collective-permute-start | bytes 1572872 | tf_op jit(solution)/shard_map/ppermute | solution.py:51
  17.0 16.3 %copy-start.3 = (bf16[768,1024]{1,0:T(8,128)(2,1)}, bf16[768,1024]{1,0:T(8,128)(2,1)S(1)}, u32[]{:S(2)}) copy-start(bf16[768,1024]{1,0:T(8,128)(2,1)S(1)} %pad_maximum_fusion.refs_0_) | copy-start | bytes 4718596
  17.0 16.3 %collective-permute-start.4 = (bf16[768,1024]{1,0:T(8,128)(2,1)S(1)}, bf16[768,1024]{1,0:T(8,128)(2,1)}, u32[]{:S(2)}, u32[]{:S(2)}) collective-permute-start(bf16[768,1024]{1,0:T(8,128)(2,1)S(1)} %pad_maximum_fusion.refs_0_), channel_id=1, source_target_pairs={{0,1},{1,0},{2,3},{3,2},{4,5},{5,4},{6,7},{7,6},{8,9},{9,8},{10,11... | collective-permute-start | bytes 4718600 | tf_op jit(solution)/shard_map/ppermute | solution.py:51
  17.1 14.3 %collective-permute-start.3 = (bf16[256,1024]{1,0:T(8,128)(2,1)S(1)}, bf16[256,1024]{1,0:T(8,128)(2,1)S(1)}, u32[]{:S(2)}, u32[]{:S(2)}) collective-permute-start(bf16[256,1024]{1,0:T(8,128)(2,1)S(1)} %collective-permute-done), channel_id=1, source_target_pairs={{0,2},{2,0},{1,3},{3,1},{4,6},{6,4},{5,7},{7,5},{8,10},{10,8},{9,1... | collective-permute-start | bytes 1572872 | tf_op jit(solution)/shard_map/ppermute | solution.py:51
  18.7 8.4 %collective-permute-start.2 = (bf16[128,1024]{1,0:T(8,128)(2,1)S(1)}, bf16[128,1024]{1,0:T(8,128)(2,1)S(1)}, u32[]{:S(2)}, u32[]{:S(2)}) collective-permute-start(bf16[128,1024]{1,0:T(8,128)(2,1)S(1)} %dynamic-slice_bitcast_fusion), channel_id=1, source_target_pairs={{0,4},{4,0},{1,5},{5,1},{2,6},{6,2},{3,7},{7,3},{8,12},{12,8},{9,1... | collective-permute-start | bytes 786440 | tf_op jit(solution)/shard_map/ppermute | solution.py:51
  31.4 1.9 copy-start.4
  31.4 1.9 collective-permute-start.5
  31.4 14.5 %collective-permute-start.6 = (bf16[1024,256]{1,0:T(8,128)(2,1)}, bf16[1024,256]{1,0:T(8,128)(2,1)S(1)}, u32[]{:S(2)}, u32[]{:S(2)}) collective-permute-start(bf16[1024,256]{1,0:T(8,128)(2,1)} %get-tuple-element.60), channel_id=1, source_target_pairs={{0,4},{4,0},{1,5},{5,1},{2,6},{6,2},{3,7},{7,3},{8,12},{12,8},{9,1... | collective-permute-start | bytes 1572872 | tf_op jit(solution)/shard_map/ppermute | solution.py:51
  33.3 0.8 copy-start.5
  40.1 16.1 %collective-permute-start.9 = (bf16[256,1024]{1,0:T(8,128)(2,1)}, bf16[256,1024]{1,0:T(8,128)(2,1)S(1)}, u32[]{:S(2)}, u32[]{:S(2)}) collective-permute-start(bf16[256,1024]{1,0:T(8,128)(2,1)} %get-tuple-element.70), channel_id=1, source_target_pairs={{24,16},{8,0},{25,17},{9,1},{26,18},{10,2},{27,19},{11,3},{28,20},... | collective-permute-start | bytes 1572872 | tf_op jit(solution)/shard_map/ppermute | solution.py:430
  46.0 24.2 %copy-start.2 = (f32[1,256,1024]{2,1,0:T(8,128)S(1)}, f32[1,256,1024]{2,1,0:T(8,128)}, u32[]{:S(2)}) copy-start(f32[1,256,1024]{2,1,0:T(8,128)} %refs_5_.1) | copy-start | bytes 3145732
  56.1 13.1 %collective-permute-start.11 = (bf16[256,1024]{1,0:T(8,128)(2,1)S(1)}, bf16[256,1024]{1,0:T(8,128)(2,1)S(1)}, u32[]{:S(2)}, u32[]{:S(2)}) collective-permute-start(bf16[256,1024]{1,0:T(8,128)(2,1)S(1)} %collective-permute-done.9), channel_id=1, source_target_pairs={{0,2},{2,0},{1,3},{3,1},{4,6},{6,4},{5,7},{7,5},{8,10},{10,8},{9,1... | collective-permute-start | bytes 1572872 | tf_op jit(solution)/shard_map/ppermute | solution.py:51
  57.7 19.8 %collective-permute-start.7 = (bf16[1024,256]{1,0:T(8,128)(2,1)}, bf16[1024,256]{1,0:T(8,128)(2,1)S(1)}, u32[]{:S(2)}, u32[]{:S(2)}) collective-permute-start(bf16[1024,256]{1,0:T(8,128)(2,1)} %get-tuple-element.66), channel_id=1, source_target_pairs={{0,4},{4,0},{1,5},{5,1},{2,6},{6,2},{3,7},{7,3},{8,12},{12,8},{9,1... | collective-permute-start | bytes 1572872 | tf_op jit(solution)/shard_map/ppermute | solution.py:51
  58.2 32.8 %collective-permute-start.8 = (bf16[1024,256]{1,0:T(8,128)(2,1)}, bf16[1024,256]{1,0:T(8,128)(2,1)S(1)}, u32[]{:S(2)}, u32[]{:S(2)}) collective-permute-start(bf16[1024,256]{1,0:T(8,128)(2,1)} %get-tuple-element.71.refs_2_), channel_id=1, source_target_pairs={{24,16},{25,17},{26,18},{27,19},{28,20},{29,21},{30,22},{31,23}} | collective-permute-start | bytes 1572872 | tf_op jit(solution)/shard_map/ppermute | solution.py:407
  70.1 47.5 %collective-permute-start.12 = (bf16[512,1024]{1,0:T(8,128)(2,1)}, bf16[512,1024]{1,0:T(8,128)(2,1)}, u32[]{:S(2)}, u32[]{:S(2)}) collective-permute-start(bf16[512,1024]{1,0:T(8,128)(2,1)} %constant_dynamic-update-slice_fusion.refs_3_), channel_id=1, source_target_pairs={{0,1},{1,0},{2,3},{3,2},{4,5},{5,4},{6,7},{7,6},{8,9},{9,8},{10,11... | collective-permute-start | bytes 3145736 | tf_op jit(solution)/shard_map/ppermute | solution.py:51
  73.3 13.4 %all-to-all-start = ((bf16[8,256,128]{2,1,0:T(8,128)(2,1)}), bf16[8,256,128]{2,1,0:T(8,128)(2,1)}, u32[]{:S(2)}, u32[]{:S(2)}) async-start(bf16[8,256,128]{2,1,0:T(8,128)(2,1)} %get-tuple-element.65), calls=%async_computation | async-start | bytes 1048576 | tf_op jit(solution)/shard_map/all_to_all | solution.py:66
  91.0 5.4 %copy-start = (bf16[1024,256]{1,0:T(8,128)(2,1)}, bf16[1024,256]{1,0:T(8,128)(2,1)S(1)}, u32[]{:S(2)}) copy-start(bf16[1024,256]{1,0:T(8,128)(2,1)S(1)} %collective-permute-done.8.refs_1_.refs_3_) | copy-start | bytes 1572868
  91.0 7.3 %copy-start.6 = (bf16[1024,128]{1,0:T(8,128)(2,1)S(1)}, bf16[1024,128]{1,0:T(8,128)(2,1)}, u32[]{:S(2)}) copy-start(bf16[1024,128]{1,0:T(8,128)(2,1)} %get-tuple-element.74) | copy-start | bytes 786436
  96.4 28.4 %collective-permute-start.13 = (bf16[1024,256]{1,0:T(8,128)(2,1)}, bf16[1024,256]{1,0:T(8,128)(2,1)S(1)}, u32[]{:S(2)}, u32[]{:S(2)}) collective-permute-start(bf16[1024,256]{1,0:T(8,128)(2,1)} %get-tuple-element.77), channel_id=1, source_target_pairs={{24,16},{16,8},{25,17},{17,9},{26,18},{18,10},{27,19},{19,11},{28,... | collective-permute-start | bytes 1572872 | tf_op jit(solution)/shard_map/ppermute | solution.py:407
  98.3 19.3 %collective-permute-start.10 = (bf16[1024,128]{1,0:T(8,128)(2,1)S(1)}, bf16[1024,128]{1,0:T(8,128)(2,1)S(1)}, u32[]{:S(2)}, u32[]{:S(2)}) collective-permute-start(bf16[1024,128]{1,0:T(8,128)(2,1)S(1)} %copy-done.6), channel_id=1, source_target_pairs={{24,16},{8,0},{25,17},{9,1},{26,18},{10,2},{27,19},{11,3},{28,20},... | collective-permute-start | bytes 786440 | tf_op jit(solution)/shard_map/ppermute | solution.py:442
  121.4 9.8 %all-to-all-start.1 = ((bf16[8,128,128]{2,1,0:T(8,128)(2,1)}), bf16[8,128,128]{2,1,0:T(8,128)(2,1)S(1)}, u32[]{:S(2)}, u32[]{:S(2)}) async-start(bf16[8,128,128]{2,1,0:T(8,128)(2,1)} %bitcast.26), calls=%async_computation.1 | async-start | bytes 524288 | tf_op jit(solution)/shard_map/all_to_all | solution.py:66
  127.6 17.0 %collective-permute-start.14 = (bf16[1024,256]{1,0:T(8,128)(2,1)}, bf16[1024,256]{1,0:T(8,128)(2,1)}, u32[]{:S(2)}, u32[]{:S(2)}) collective-permute-start(bf16[1024,256]{1,0:T(8,128)(2,1)} %get-tuple-element.84), channel_id=1, source_target_pairs={{16,8},{8,0},{17,9},{9,1},{18,10},{10,2},{19,11},{11,3},{20,12},{1... | collective-permute-start | bytes 1572872 | tf_op jit(solution)/shard_map/ppermute | solution.py:407
  136.9 20.7 %collective-permute-start.16 = (bf16[1024,256]{1,0:T(8,128)(2,1)}, bf16[1024,256]{1,0:T(8,128)(2,1)}, u32[]{:S(2)}, u32[]{:S(2)}) collective-permute-start(bf16[1024,256]{1,0:T(8,128)(2,1)} %get-tuple-element.88), channel_id=1, source_target_pairs={{16,0},{17,1},{18,2},{19,3},{20,4},{21,5},{22,6},{23,7}} | collective-permute-start | bytes 1572872 | tf_op jit(solution)/shard_map/ppermute | solution.py:462
  139.0 24.7 %collective-permute-start.15 = (bf16[1024,256]{1,0:T(8,128)(2,1)}, bf16[1024,256]{1,0:T(8,128)(2,1)}, u32[]{:S(2)}, u32[]{:S(2)}) collective-permute-start(bf16[1024,256]{1,0:T(8,128)(2,1)} %get-tuple-element.88), channel_id=1, source_target_pairs={{16,8},{17,9},{18,10},{19,11},{20,12},{21,13},{22,14},{23,15}} | collective-permute-start | bytes 1572872 | tf_op jit(solution)/shard_map/ppermute | solution.py:462
  141.1 16.4 %all-to-all-start.2 = ((bf16[8,256,128]{2,1,0:T(8,128)(2,1)}), bf16[8,256,128]{2,1,0:T(8,128)(2,1)S(1)}, u32[]{:S(2)}, u32[]{:S(2)}) async-start(bf16[8,256,128]{2,1,0:T(8,128)(2,1)} %get-tuple-element.90), calls=%async_computation.2 | async-start | bytes 1048576 | tf_op jit(solution)/shard_map/all_to_all | solution.py:66
  144.6 1.0 copy-start.1
  150.7 22.8 %collective-permute-start.17 = (bf16[1024,256]{1,0:T(8,128)(2,1)}, bf16[1024,256]{1,0:T(8,128)(2,1)}, u32[]{:S(2)}, u32[]{:S(2)}) collective-permute-start(bf16[1024,256]{1,0:T(8,128)(2,1)} %get-tuple-element.92), channel_id=1, source_target_pairs={{0,4},{4,0},{1,5},{5,1},{2,6},{6,2},{3,7},{7,3},{8,12},{12,8},{9,1... | collective-permute-start | bytes 1572872 | tf_op jit(solution)/shard_map/ppermute | solution.py:51
  156.1 20.9 %collective-permute-start.18 = (bf16[1024,256]{1,0:T(8,128)(2,1)}, bf16[1024,256]{1,0:T(8,128)(2,1)}, u32[]{:S(2)}, u32[]{:S(2)}) collective-permute-start(bf16[1024,256]{1,0:T(8,128)(2,1)} %get-tuple-element.96), channel_id=1, source_target_pairs={{8,0},{9,1},{10,2},{11,3},{12,4},{13,5},{14,6},{15,7}} | collective-permute-start | bytes 1572872 | tf_op jit(solution)/shard_map/ppermute | solution.py:407
  169.2 19.2 %all-to-all-start.3 = ((bf16[8,256,256]{2,1,0:T(8,128)(2,1)}), bf16[8,256,256]{2,1,0:T(8,128)(2,1)}, u32[]{:S(2)}, u32[]{:S(2)}) async-start(bf16[8,256,256]{2,1,0:T(8,128)(2,1)} %get-tuple-element.100), calls=%async_computation.3 | async-start | bytes 2097152 | tf_op jit(solution)/shard_map/all_to_all | solution.py:66
  182.0 17.1 %collective-permute-start.19 = (bf16[1024,256]{1,0:T(8,128)(2,1)}, bf16[1024,256]{1,0:T(8,128)(2,1)S(1)}, u32[]{:S(2)}, u32[]{:S(2)}) collective-permute-start(bf16[1024,256]{1,0:T(8,128)(2,1)} %get-tuple-element.104), channel_id=1, source_target_pairs={{0,4},{4,0},{1,5},{5,1},{2,6},{6,2},{3,7},{7,3},{8,12},{12,8},{9,1... | collective-permute-start | bytes 1572872 | tf_op jit(solution)/shard_map/ppermute | solution.py:51

commit v13 on v12

--- a/solution.py
+++ b/solution.py
@@ -109,7 +109,7 @@
         into[:, s * width : (s + 1) * width] = blocks[s, :, start : start + width]
 
 
-def pair_kernel(ids, three, last, three_c, last_c, e0, e1, pair, quarter, both, sems):
+def pair_kernel(ids, three, last, three_c, last_c, e0, e1, pair, part_rows, both, sems):
     group = 2 * ids[1] + ids[2]
     me = 4 * ids[0] + group
     rows = last.shape[0]
@@ -131,7 +131,9 @@
     for r in range(4):
         cut = slice(r * rows, (r + 1) * rows)
         pair[cut, :] = mm(both[0, cut, :], both[1]).astype(LOW)
-    quarter[...] = pair[pl.ds(pl.multiple_of(group * rows, rows), rows), :]
+    for i in range(2):
+        here = pl.ds(pl.multiple_of((2 * i + ids[2]) * rows, rows), rows)
+        part_rows[i * rows : (i + 1) * rows, :] = pair[here, :]
     for copy in copies:
         copy.wait()
 
@@ -170,7 +172,7 @@
     a_low[...] = slab[...].astype(LOW)
 
 
-def spread_hop_kernel(ids, pair, e1, got, unused, m_ref, near):
+def spread_hop_kernel(ids, pair, e1, got, m_ref, near):
     part = got.shape[1]
     rows = 2 * part
     m = mm(pair[...], got[...]).astype(LOW)
@@ -184,11 +186,13 @@
 def next_kernel(ids, pair, slab, blocks, quarters, quarters_c, following, out, m, sems):
     part = m.shape[0]
     rows = 2 * part
-    group = 2 * ids[1] + ids[2]
+    c = ids[2]
+    group = 2 * ids[1] + c
     copies = []
-    for i, (piece, at) in enumerate(((quarters, 0), (quarters, 2), (quarters_c, 1), (quarters_c, 3))):
-        into = following.at[pl.ds(pl.multiple_of((group ^ at) * rows, rows), rows), :]
-        cut = piece.at[(at >> 1) * rows : ((at >> 1) + 1) * rows, :]
+    for i in range(4):
+        piece, at = ((quarters, c), (quarters_c, 1 - c))[i % 2]
+        into = following.at[pl.ds(pl.multiple_of((2 * (i // 2) + at) * rows, rows), rows), :]
+        cut = piece.at[(i // 2) * rows : (i // 2 + 1) * rows, :]
         copies.append(pltpu.make_async_copy(cut, into, sems.at[i]))
         copies[-1].start()
     gather_lanes(blocks, m, 0, part)
@@ -285,7 +289,7 @@
     now[...] = (mm(pair[...], got[...]) + own[...].astype(WIDE)).astype(LOW)
 
 
-def hop_start_kernel(chunk, ids, pair, got_hop, own_hop, e0, got, offset, wave, p, own, keep, sem):
+def hop_start_kernel(chunk, ids, pair, got_hop, own_hop, e0, got, offset, unused, wave, p, own, keep, sem):
     start_kernel(chunk, ids, e0, got, offset, p, own, keep, sem)
 
     @pl.when(ids[3] == 3)
@@ -421,17 +425,15 @@
             far_in=(1, 2), far_out=(0,), aliases={2: 0}, scratch=[keep, pltpu.SemaphoreType.DMA((2,))],
         )[0]
 
-    e0, e1, pair, quarter = order.call(
+    e0, e1, pair, quarters = order.call(
         pair_kernel, pieces,
-        [hbm(size_d, size_d), hbm(size_d, size_d), pltpu.VMEM((size_d, size_d), LOW), hbm(rows, size_d)], 14,
+        [hbm(size_d, size_d), hbm(size_d, size_d), pltpu.VMEM((size_d, size_d), LOW), hbm(2 * rows, size_d)], 14,
         far_in=range(4), far_out=(0, 1),
         scratch=[pltpu.VMEM((2, size_d, size_d), LOW), pltpu.SemaphoreType.DMA((8,))],
     )
-    quarter = lax.ppermute(quarter, "z", level)
+    quarters = lax.ppermute(quarters, "z", level)
     p0, own0 = start(0)
     wave1 = down(own0, 3)
-    quarter, own0 = tied((quarter, own0))
-    quarter_y = swap(quarter, "y")
     (m,) = order.call(spread_kernel, [in_hbm(e0), l_low, l_got], [hbm(8, rows, part)], 8)
     m = exchange(m)
     prod, slab, a_low = order.call(
@@ -441,18 +443,18 @@
     )
     l_next = lax.ppermute(a_low, "z", level)
     wave2, p1, own1 = order.call(
-        functools.partial(hop_start_kernel, 1), [pair, wave1, in_hbm(own0), in_hbm(e0), g_got[1], offset],
+        functools.partial(hop_start_kernel, 1), [pair, wave1, in_hbm(own0), in_hbm(e0), g_got[1], offset, quarters],
         [hbm(size_d, width), hbm(size_d, width, dtype=WIDE), hbm(size_d, width)], 16,
-        far_in=(5,), scratch=[keep, pltpu.SemaphoreType.DMA(())],
+        far_in=(5, 6), scratch=[keep, pltpu.SemaphoreType.DMA(())],
     )
     wave2 = down(wave2, 3, 2)
 
-    quarters = jnp.concatenate([quarter, quarter_y], axis=0)
+    m, near = order.call(
+        spread_hop_kernel, [pair, in_hbm(e1), l_next], [hbm(size_d, part), hbm(8, rows, part)], 10
+    )
+    m = exchange(m.reshape(8, part, part))
+    quarters, near = tied((quarters, near))
     quarters = [quarters, swap(quarters, "c")]
-    m, near = order.call(
-        spread_hop_kernel, [pair, in_hbm(e1), l_next, quarters[1]], [hbm(size_d, part), hbm(8, rows, part)], 10, far_in=(3,)
-    )
-    m = exchange(m.reshape(8, part, part))
     (wave3,) = order.call(hop_kernel, [pair, wave2, in_hbm(own0), in_hbm(own1)], [hbm(size_d, width)], 10)
     wave3 = down(wave3, 2, 1)
     following, far_slab = order.call(

time: 205 us -> 184 us (0.90)
  waiting for transfers between devices: 83.4 us -> 64.9 us
  local copies, waits for them, and re-layouts: 6.23 us -> 3.7 us
    ppermute x1, waiting for transfers between devices: 18 us -> 0.01 us  [suffix(): l_next = lax.ppermute(a_low, 'z', level)]
    ppermute x4, waiting for transfers between devices: 0.01 us -> 15.3 us  [down(): lax.ppermute(value, 'z', [(source, source - 1) for source in sources])]
    ppermute x12 -> x11, waiting for transfers between devices: 38.7 us -> 30.4 us  [swap(): return lax.ppermute(value, axis, [(0, 1), (1, 0)])]
    ppermute x1, waiting for transfers between devices: 5.96 us -> 0.01 us  [suffix(): quarters = lax.ppermute(quarters, 'z', level)]
    all_to_all x4, waiting for transfers between devices: 14.6 us -> 12 us  [exchange(): return lax.all_to_all(blocks, GROUP, 0, 0)]
    ppermute x12 -> x11, starting transfers between devices: 13 us -> 11.6 us  [swap(): return lax.ppermute(value, axis, [(0, 1), (1, 0)])]
  transfers between devices with their start and end apart: 24 -> 23, of which waited for: 14 -> 12; matrix products, arithmetic and copies ran while one was open for 3% -> 3% of each run, Pallas kernels for 32% -> 33%
where the time goes in v13:
time: 184 us; the launch traced here: 182 us
  Pallas kernels  66.4 us (36%)
  waiting for transfers between devices  64.9 us (35%)
  starting transfers between devices  41.7 us (23%)
  other arithmetic  4.08 us (2%)
  local copies, waits for them, and re-layouts  3.7 us (2%)
    pallas_call x15, Pallas kernels, call(): pl.pallas_call(body, in_specs=[SMEM, ANY] + [ANY if i in far_in else VMEM...  66.4 us
    ppermute x11, waiting for transfers between devices, swap(): return lax.ppermute(value, axis, [(0, 1), (1, 0)])  30.4 us
    all_to_all x4, starting transfers between devices, exchange(): return lax.all_to_all(blocks, GROUP, 0, 0)  15.7 us
    ppermute x4, waiting for transfers between devices, down(): lax.ppermute(value, 'z', [(source, source - 1) for source in sources])  15.3 us
    all_to_all x4, waiting for transfers between devices, exchange(): return lax.all_to_all(blocks, GROUP, 0, 0)  12 us
    ppermute x11, starting transfers between devices, swap(): return lax.ppermute(value, axis, [(0, 1), (1, 0)])  11.6 us
    ppermute x4, starting transfers between devices, down(): lax.ppermute(value, 'z', [(source, source - 1) for source in sources])  7.72 us
    ppermute x1, waiting for transfers between devices, suffix(): lax.ppermute(far_slab, 'z', [(2, 1)])  7.24 us
  transfers between devices with their start and end apart: 23, of which 12 were waited for; matrix products, arithmetic and copies ran while one was open for 3% of the time, Pallas kernels for 33%

profile of v13, /device:TPU:16, one launch (start us, length us, event | category | flops | bytes accessed | tf_op | source)
XLA Modules:
  0.0 181.8 jit_solution(548456444207197484)
XLA Ops:
  0.6 1.3 convert_bitcast_fusion
  1.9 1.6 collective-permute-start
  3.5 1.5 collective-permute-start.1
  5.0 1.3 convert_element_type.25
  6.3 2.6 %fusion.1 = (bf16[1024,256]{1,0:T(8,128)(2,1)}, bf16[1024,256]{1,0:T(8,128)(2,1)}) fusion(f32[1,1024,1024]{2,1,0:T(8,128)} %param.5, s32[]{:T(128)S(6)} %select_n.11, s32[]{:T(128)S(6)} %select_n.10), kind=kLoop, calls=%fused_computation.4 | loop fusion | bytes 2097160 | tf_op jit(solution)/shard_map/convert_element_type | solution.py:386
  9.0 6.7 %collective-permute-done = bf16[256,1024]{1,0:T(8,128)(2,1)S(1)} collective-permute-done((bf16[256,1024]{1,0:T(8,128)(2,1)S(1)}, bf16[256,1024]{1,0:T(8,128)(2,1)S(1)}, u32[]{:S(2)}, u32[]{:S(2)}) %collective-permute-start) | collective-permute-done | bytes 524320 | tf_op jit(solution)/shard_map/ppermute | solution.py:51
  15.7 1.2 collective-permute-done.1
  17.1 1.6 collective-permute-start.3
  19.2 7.8 %collective-permute-done.2.refs_2_.refs_3_ = bf16[128,1024]{1,0:T(8,128)(2,1)S(1)} collective-permute-done((bf16[128,1024]{1,0:T(8,128)(2,1)S(1)}, bf16[128,1024]{1,0:T(8,128)(2,1)S(1)}, u32[]{:S(2)}, u32[]{:S(2)}) %collective-permute-start.2) | collective-permute-done | bytes 262176 | tf_op jit(solution)/shard_map/ppermute | solution.py:51
  27.0 4.4 %collective-permute-done.3.refs_1_ = bf16[256,1024]{1,0:T(8,128)(2,1)S(1)} collective-permute-done((bf16[256,1024]{1,0:T(8,128)(2,1)S(1)}, bf16[256,1024]{1,0:T(8,128)(2,1)S(1)}, u32[]{:S(2)}, u32[]{:S(2)}) %collective-permute-start.3) | collective-permute-done | bytes 524320 | tf_op jit(solution)/shard_map/ppermute | solution.py:51
  32.0 1.4 collective-permute-done.5.refs_3_
  33.5 6.1 %shard_map.58 = (bf16[1024,1024]{1,0:T(8,128)(2,1)}, bf16[1024,1024]{1,0:T(8,128)(2,1)}, bf16[1024,1024]{1,0:T(8,128)(2,1)S(1)}, bf16[512,1024]{1,0:T(8,128)(2,1)}, s32[8,128]{1,0:T(8,128)S(1)}) custom-call(s32[4]{0:T(128)S(1)} %pad_add_fusion.ids, s32[8,128]{1,0:T(8,128)S(1)} %broadcast_in_dim.12.token, ...), custom_call_target="tpu_custom_call", output_to_operand_aliasing={{4}: (1, {})} | custom-call | flops 1 | bytes 1 | tf_op jit(solution)/shard_map/pallas_call | solution.py:93
  39.6 1.3 collective-permute-start.9
  40.9 5.0 %collective-permute-done.6.refs_1_ = bf16[1024,256]{1,0:T(8,128)(2,1)S(1)} collective-permute-done((bf16[1024,256]{1,0:T(8,128)(2,1)}, bf16[1024,256]{1,0:T(8,128)(2,1)S(1)}, u32[]{:S(2)}, u32[]{:S(2)}) %collective-permute-start.6) | collective-permute-done | bytes 524320 | tf_op jit(solution)/shard_map/ppermute | solution.py:51
  46.5 1.3 convert_bitcast_fusion.1.refs_1_
  47.8 4.2 %shard_map.59 = (f32[1024,256]{1,0:T(8,128)}, bf16[1024,256]{1,0:T(8,128)(2,1)}, s32[8,128]{1,0:T(8,128)S(1)}) custom-call(s32[4]{0:T(128)S(1)} %pad_add_fusion.ids, s32[8,128]{1,0:T(8,128)S(1)} %get-tuple-element.58.token, bf16[1024,1024]{1,0:T(8,128)(2,1)} %get-tuple-element.59.refs_0_.refs_3_, ...), custom_call_target="tpu_custom_call", output_to_operand_aliasing={{2}: (1, {})} | custom-call | flops 1 | bytes 1 | tf_op jit(solution)/shard_map/pallas_call | solution.py:93
  52.0 3.1 %shard_map.60 = (bf16[8,256,128]{2,1,0:T(8,128)(2,1)}, s32[8,128]{1,0:T(8,128)S(1)}) custom-call(s32[4]{0:T(128)S(1)} %pad_add_fusion.ids, s32[8,128]{1,0:T(8,128)S(1)} %get-tuple-element.62.token, bf16[1024,1024]{1,0:T(8,128)(2,1)} %get-tuple-element.59.refs_0_.refs_3_, ...), custom_call_target="tpu_custom_call", output_to_operand_aliasing={{1}: (1, {})} | custom-call | flops 1 | bytes 1 | tf_op jit(solution)/shard_map/pallas_call | solution.py:93
  55.1 4.3 %all-to-all-start = ((bf16[8,256,128]{2,1,0:T(8,128)(2,1)}), bf16[8,256,128]{2,1,0:T(8,128)(2,1)}, u32[]{:S(2)}, u32[]{:S(2)}) async-start(bf16[8,256,128]{2,1,0:T(8,128)(2,1)} %get-tuple-element.65), calls=%async_computation | async-start | bytes 1048576 | tf_op jit(solution)/shard_map/all_to_all | solution.py:66
  59.4 1.3 collective-permute-start.8
  60.7 8.1 %all-to-all-done.refs_1_ = bf16[8,256,128]{2,1,0:T(8,128)(2,1)} async-done(((bf16[8,256,128]{2,1,0:T(8,128)(2,1)}), bf16[8,256,128]{2,1,0:T(8,128)(2,1)}, u32[]{:S(2)}, u32[]{:S(2)}) %all-to-all-start) | async-done | bytes 524320 | tf_op jit(solution)/shard_map/all_to_all | solution.py:66
  68.8 4.2 %shard_map.61 = (f32[256,1024]{1,0:T(8,128)}, f32[1024,128]{1,0:T(8,128)}, bf16[1024,128]{1,0:T(8,128)(2,1)}, s32[8,128]{1,0:T(8,128)S(1)}) custom-call(s32[4]{0:T(128)S(1)} %pad_add_fusion.ids, s32[8,128]{1,0:T(8,128)S(1)} %get-tuple-element.64.token, bf16[1024,1024]{1,0:T(8,128)(2,1)} %get-tuple-element.59.refs_0_.refs_3_, ...), custom_call_target="tpu_custom_call", output_to_operand_aliasing={{3}: (1, {})} | custom-call | flops 1 | bytes 1 | tf_op jit(solution)/shard_map/pallas_call | solution.py:93
  73.0 1.3 collective-permute-start.10
  74.3 4.6 %collective-permute-done.8.refs_1_.refs_3_ = bf16[1024,256]{1,0:T(8,128)(2,1)S(1)} collective-permute-done((bf16[1024,256]{1,0:T(8,128)(2,1)}, bf16[1024,256]{1,0:T(8,128)(2,1)S(1)}, u32[]{:S(2)}, u32[]{:S(2)}) %collective-permute-start.8) | collective-permute-done | bytes 524320 | tf_op jit(solution)/shard_map/ppermute | solution.py:411
  78.9 5.4 %shard_map.62 = (bf16[1024,256]{1,0:T(8,128)(2,1)}, f32[1024,256]{1,0:T(8,128)}, bf16[1024,256]{1,0:T(8,128)(2,1)}, s32[8,128]{1,0:T(8,128)S(1)}) custom-call(s32[4]{0:T(128)S(1)} %pad_add_fusion.ids, s32[8,128]{1,0:T(8,128)S(1)} %get-tuple-element.67.token, bf16[1024,1024]{1,0:T(8,128)(2,1)S(1)} %get-tuple-element.68.refs_0_, ...), custom_call_target="tpu_custom_call", output_to_operand_aliasing={{3}: (1, {})} | custom-call | flops 1 | bytes 1 | tf_op jit(solution)/shard_map/pallas_call | solution.py:93
  84.3 3.8 %shard_map.63 = (bf16[1024,128]{1,0:T(8,128)(2,1)}, bf16[8,256,128]{2,1,0:T(8,128)(2,1)}, s32[8,128]{1,0:T(8,128)S(1)}) custom-call(s32[4]{0:T(128)S(1)} %pad_add_fusion.ids, s32[8,128]{1,0:T(8,128)S(1)} %get-tuple-element.71.token, bf16[1024,1024]{1,0:T(8,128)(2,1)S(1)} %get-tuple-element.68.refs_0_, ...), custom_call_target="tpu_custom_call", output_to_operand_aliasing={{2}: (1, {})} | custom-call | flops 1 | bytes 1 | tf_op jit(solution)/shard_map/pallas_call | solution.py:93
  88.1 1.9 %collective-permute-start.11 = (bf16[1024,256]{1,0:T(8,128)(2,1)S(1)}, bf16[1024,256]{1,0:T(8,128)(2,1)S(1)}, u32[]{:S(2)}, u32[]{:S(2)}) collective-permute-start(bf16[1024,256]{1,0:T(8,128)(2,1)S(1)} %copy-done.4), channel_id=1, source_target_pairs={{24,16},{16,8},{25,17},{17,9},{26,18},{18,10},{27,19},{19,11},{28,... | collective-permute-start | bytes 1572872 | tf_op jit(solution)/shard_map/ppermute | solution.py:411
  90.1 3.6 %all-to-all-start.1 = ((bf16[8,128,128]{2,1,0:T(8,128)(2,1)}), bf16[8,128,128]{2,1,0:T(8,128)(2,1)S(1)}, u32[]{:S(2)}, u32[]{:S(2)}) async-start(bf16[8,128,128]{2,1,0:T(8,128)(2,1)} %bitcast.26), calls=%async_computation.1 | async-start | bytes 524288 | tf_op jit(solution)/shard_map/all_to_all | solution.py:66
  93.7 10.7 %collective-permute-done.11.refs_1_.refs_4_.refs_3_ = bf16[1024,256]{1,0:T(8,128)(2,1)S(1)} collective-permute-done((bf16[1024,256]{1,0:T(8,128)(2,1)S(1)}, bf16[1024,256]{1,0:T(8,128)(2,1)S(1)}, u32[]{:S(2)}, u32[]{:S(2)}) %collective-permute-start.11) | collective-permute-done | bytes 524320 | tf_op jit(solution)/shard_map/ppermute | solution.py:411
  104.4 2.8 %shard_map.64 = (bf16[1024,256]{1,0:T(8,128)(2,1)}, s32[8,128]{1,0:T(8,128)S(1)}) custom-call(s32[4]{0:T(128)S(1)} %pad_add_fusion.ids, s32[8,128]{1,0:T(8,128)S(1)} %get-tuple-element.74.token, bf16[1024,1024]{1,0:T(8,128)(2,1)S(1)} %get-tuple-element.68.refs_0_, ...), custom_call_target="tpu_custom_call", output_to_operand_aliasing={{1}: (1, {})} | custom-call | flops 1 | bytes 1 | tf_op jit(solution)/shard_map/pallas_call | solution.py:93
  107.2 3.0 %collective-permute-start.13 = (bf16[1024,256]{1,0:T(8,128)(2,1)}, bf16[1024,256]{1,0:T(8,128)(2,1)}, u32[]{:S(2)}, u32[]{:S(2)}) collective-permute-start(bf16[1024,256]{1,0:T(8,128)(2,1)} %get-tuple-element.84), channel_id=1, source_target_pairs={{16,8},{8,0},{17,9},{9,1},{18,10},{10,2},{19,11},{11,3},{20,12},{1... | collective-permute-start | bytes 1572872 | tf_op jit(solution)/shard_map/ppermute | solution.py:411
  110.2 5.2 %shard_map.65 = (bf16[1024,1024]{1,0:T(8,128)(2,1)}, bf16[1024,256]{1,0:T(8,128)(2,1)}, s32[8,128]{1,0:T(8,128)S(1)}) custom-call(s32[4]{0:T(128)S(1)} %pad_add_fusion.ids, s32[8,128]{1,0:T(8,128)S(1)} %get-tuple-element.77.token, bf16[1024,1024]{1,0:T(8,128)(2,1)S(1)} %get-tuple-element.68.refs_0_, ...), custom_call_target="tpu_custom_call", output_to_operand_aliasing={{2}: (1, {})} | custom-call | flops 1 | bytes 1 | tf_op jit(solution)/shard_map/pallas_call | solution.py:93
  115.4 2.1 %collective-permute-start.15 = (bf16[1024,256]{1,0:T(8,128)(2,1)}, bf16[1024,256]{1,0:T(8,128)(2,1)}, u32[]{:S(2)}, u32[]{:S(2)}) collective-permute-start(bf16[1024,256]{1,0:T(8,128)(2,1)} %get-tuple-element.88), channel_id=1, source_target_pairs={{16,0},{17,1},{18,2},{19,3},{20,4},{21,5},{22,6},{23,7}} | collective-permute-start | bytes 1572872 | tf_op jit(solution)/shard_map/ppermute | solution.py:464
  117.5 2.1 %collective-permute-start.14 = (bf16[1024,256]{1,0:T(8,128)(2,1)}, bf16[1024,256]{1,0:T(8,128)(2,1)}, u32[]{:S(2)}, u32[]{:S(2)}) collective-permute-start(bf16[1024,256]{1,0:T(8,128)(2,1)} %get-tuple-element.88), channel_id=1, source_target_pairs={{16,8},{17,9},{18,10},{19,11},{20,12},{21,13},{22,14},{23,15}} | collective-permute-start | bytes 1572872 | tf_op jit(solution)/shard_map/ppermute | solution.py:464
  119.6 3.5 %all-to-all-start.2 = ((bf16[8,256,128]{2,1,0:T(8,128)(2,1)}), bf16[8,256,128]{2,1,0:T(8,128)(2,1)S(1)}, u32[]{:S(2)}, u32[]{:S(2)}) async-start(bf16[8,256,128]{2,1,0:T(8,128)(2,1)} %get-tuple-element.90), calls=%async_computation.2 | async-start | bytes 1048576 | tf_op jit(solution)/shard_map/all_to_all | solution.py:66
  124.2 5.1 %shard_map.66 = (f32[1024,1024]{1,0:T(8,128)}, bf16[1024,256]{1,0:T(8,128)(2,1)}, s32[8,128]{1,0:T(8,128)S(1)}) custom-call(s32[4]{0:T(128)S(1)} %pad_add_fusion.ids, s32[8,128]{1,0:T(8,128)S(1)} %get-tuple-element.82.token, bf16[1024,1024]{1,0:T(8,128)(2,1)S(1)} %get-tuple-element.68.refs_0_, ...), custom_call_target="tpu_custom_call", output_to_operand_aliasing={{2}: (1, {})} | custom-call | flops 1 | bytes 1 | tf_op jit(solution)/shard_map/pallas_call | solution.py:93
  129.3 2.7 %collective-permute-start.16 = (bf16[1024,256]{1,0:T(8,128)(2,1)}, bf16[1024,256]{1,0:T(8,128)(2,1)}, u32[]{:S(2)}, u32[]{:S(2)}) collective-permute-start(bf16[1024,256]{1,0:T(8,128)(2,1)} %get-tuple-element.92), channel_id=1, source_target_pairs={{0,4},{4,0},{1,5},{5,1},{2,6},{6,2},{3,7},{7,3},{8,12},{12,8},{9,1... | collective-permute-start | bytes 1572872 | tf_op jit(solution)/shard_map/ppermute | solution.py:51
  131.9 2.7 %shard_map.67 = (bf16[1024,256]{1,0:T(8,128)(2,1)}, s32[8,128]{1,0:T(8,128)S(1)}) custom-call(s32[4]{0:T(128)S(1)} %pad_add_fusion.ids, s32[8,128]{1,0:T(8,128)S(1)} %get-tuple-element.85.token, bf16[1024,1024]{1,0:T(8,128)(2,1)S(1)} %get-tuple-element.68.refs_0_, ...), custom_call_target="tpu_custom_call", output_to_operand_aliasing={{1}: (1, {})} | custom-call | flops 1 | bytes 1 | tf_op jit(solution)/shard_map/pallas_call | solution.py:93
  134.7 1.5 collective-permute-start.17
  136.2 7.2 %collective-permute-done.14.refs_3_ = bf16[1024,256]{1,0:T(8,128)(2,1)} collective-permute-done((bf16[1024,256]{1,0:T(8,128)(2,1)}, bf16[1024,256]{1,0:T(8,128)(2,1)}, u32[]{:S(2)}, u32[]{:S(2)}) %collective-permute-start.14) | collective-permute-done | bytes 524320 | tf_op jit(solution)/shard_map/ppermute | solution.py:464
  143.4 5.5 %shard_map.68 = (bf16[8,256,256]{2,1,0:T(8,128)(2,1)}, s32[8,128]{1,0:T(8,128)S(1)}) custom-call(s32[4]{0:T(128)S(1)} %pad_add_fusion.ids, s32[8,128]{1,0:T(8,128)S(1)} %get-tuple-element.86.token, bf16[1024,1024]{1,0:T(8,128)(2,1)S(1)} %get-tuple-element.68.refs_0_, bf16[1024,1024]{1,0:T(8,128)(2,1)} %get-tuple-element.72.refs_1_, ...), custom_call_target="tpu_custom_call", output_to_operand_aliasing={{1}: (1, {})} | custom-call | flops 1 | bytes 1 | tf_op jit(solution)/shard_map/pallas_call | solution.py:93
  148.9 4.2 %all-to-all-start.3 = ((bf16[8,256,256]{2,1,0:T(8,128)(2,1)}), bf16[8,256,256]{2,1,0:T(8,128)(2,1)}, u32[]{:S(2)}, u32[]{:S(2)}) async-start(bf16[8,256,256]{2,1,0:T(8,128)(2,1)} %get-tuple-element.100), calls=%async_computation.3 | async-start | bytes 2097152 | tf_op jit(solution)/shard_map/all_to_all | solution.py:66
  153.2 3.4 %shard_map.69 = (f32[1024,1024]{1,0:T(8,128)}, s32[8,128]{1,0:T(8,128)S(1)}) custom-call(s32[4]{0:T(128)S(1)} %pad_add_fusion.ids, s32[8,128]{1,0:T(8,128)S(1)} %get-tuple-element.91.token, bf16[1024,256]{1,0:T(8,128)(2,1)} %collective-permute-done.16.refs_0_, f32[1024,1024]{1,0:T(8,128)} %bitcast.22, ...), custom_call_target="tpu_custom_call", output_to_operand_aliasing={{1}: (1, {}), {0}: (4, {})} | custom-call | flops 1 | bytes 1 | tf_op jit(solution)/shard_map/pallas_call | solution.py:93
  156.6 5.1 %shard_map.70 = (f32[1024,1024]{1,0:T(8,128)}, bf16[1024,256]{1,0:T(8,128)(2,1)}, s32[8,128]{1,0:T(8,128)S(1)}) custom-call(s32[4]{0:T(128)S(1)} %pad_add_fusion.ids, s32[8,128]{1,0:T(8,128)S(1)} %get-tuple-element.94.token, bf16[1024,1024]{1,0:T(8,128)(2,1)S(1)} %get-tuple-element.68.refs_0_, ...), custom_call_target="tpu_custom_call", output_to_operand_aliasing={{2}: (1, {}), {0}: (9, {})} | custom-call | flops 1 | bytes 1 | tf_op jit(solution)/shard_map/pallas_call | solution.py:93
  161.6 2.6 %collective-permute-start.18 = (bf16[1024,256]{1,0:T(8,128)(2,1)}, bf16[1024,256]{1,0:T(8,128)(2,1)S(1)}, u32[]{:S(2)}, u32[]{:S(2)}) collective-permute-start(bf16[1024,256]{1,0:T(8,128)(2,1)} %get-tuple-element.104), channel_id=1, source_target_pairs={{0,4},{4,0},{1,5},{5,1},{2,6},{6,2},{3,7},{7,3},{8,12},{12,8},{9,1... | collective-permute-start | bytes 1572872 | tf_op jit(solution)/shard_map/ppermute | solution.py:51
  164.2 3.9 %all-to-all-done.3.refs_6_ = bf16[8,256,256]{2,1,0:T(8,128)(2,1)} async-done(((bf16[8,256,256]{2,1,0:T(8,128)(2,1)}), bf16[8,256,256]{2,1,0:T(8,128)(2,1)}, u32[]{:S(2)}, u32[]{:S(2)}) %all-to-all-start.3) | async-done | bytes 1048608 | tf_op jit(solution)/shard_map/all_to_all | solution.py:66
  168.1 6.9 %shard_map.71 = (f32[256,1024]{1,0:T(8,128)}, f32[256,1024]{1,0:T(8,128)}, s32[8,128]{1,0:T(8,128)S(1)}) custom-call(s32[4]{0:T(128)S(1)} %pad_add_fusion.ids, s32[8,128]{1,0:T(8,128)S(1)} %get-tuple-element.98.token, bf16[1024,1024]{1,0:T(8,128)(2,1)S(1)} %get-tuple-element.68.refs_0_, ...), custom_call_target="tpu_custom_call", output_to_operand_aliasing={{2}: (1, {})} | custom-call | flops 1 | bytes 1 | tf_op jit(solution)/shard_map/pallas_call | solution.py:93
  175.0 3.8 %collective-permute-done.18.refs_0_ = bf16[1024,256]{1,0:T(8,128)(2,1)S(1)} collective-permute-done((bf16[1024,256]{1,0:T(8,128)(2,1)}, bf16[1024,256]{1,0:T(8,128)(2,1)S(1)}, u32[]{:S(2)}, u32[]{:S(2)}) %collective-permute-start.18) | collective-permute-done | bytes 524320 | tf_op jit(solution)/shard_map/ppermute | solution.py:51
  178.8 2.9 %shard_map.72 = (f32[1024,1024]{1,0:T(8,128)}, s32[8,128]{1,0:T(8,128)S(1)}) custom-call(s32[4]{0:T(128)S(1)} %pad_add_fusion.ids, s32[8,128]{1,0:T(8,128)S(1)} %get-tuple-element.103.token, bf16[1024,256]{1,0:T(8,128)(2,1)S(1)} %collective-permute-done.18.refs_0_, f32[1024,1024]{1,0:T(8,128)} %bitcast.24, ...), custom_call_target="tpu_custom_call", output_to_operand_aliasing={{1}: (1, {}), {0}: (4, {})} | custom-call | flops 1 | bytes 1 | tf_op jit(solution)/shard_map/pallas_call | solution.py:93
  (31 shorter events, 3.0 us)
Async XLA Ops:
  1.9 13.7 %collective-permute-start = (bf16[256,1024]{1,0:T(8,128)(2,1)S(1)}, bf16[256,1024]{1,0:T(8,128)(2,1)S(1)}, u32[]{:S(2)}, u32[]{:S(2)}) collective-permute-start(bf16[256,1024]{1,0:T(8,128)(2,1)S(1)} %convert_bitcast_fusion), channel_id=1, source_target_pairs={{0,4},{4,0},{1,5},{5,1},{2,6},{6,2},{3,7},{7,3},{8,12},{12,8},{9,1... | collective-permute-start | bytes 1572872 | tf_op jit(solution)/shard_map/ppermute | solution.py:51
  3.5 13.4 %collective-permute-start.1 = (bf16[256,1024]{1,0:T(8,128)(2,1)S(1)}, bf16[256,1024]{1,0:T(8,128)(2,1)S(1)}, u32[]{:S(2)}, u32[]{:S(2)}) collective-permute-start(bf16[256,1024]{1,0:T(8,128)(2,1)S(1)} %convert_bitcast_fusion), channel_id=1, source_target_pairs={{0,2},{2,0},{1,3},{3,1},{4,6},{6,4},{5,7},{7,5},{8,10},{10,8},{9,1... | collective-permute-start | bytes 1572872 | tf_op jit(solution)/shard_map/ppermute | solution.py:51
  17.0 16.5 %copy-start.2 = (bf16[768,1024]{1,0:T(8,128)(2,1)}, bf16[768,1024]{1,0:T(8,128)(2,1)S(1)}, u32[]{:S(2)}) copy-start(bf16[768,1024]{1,0:T(8,128)(2,1)S(1)} %pad_maximum_fusion.refs_0_) | copy-start | bytes 4718596
  17.0 16.5 %collective-permute-start.4 = (bf16[768,1024]{1,0:T(8,128)(2,1)S(1)}, bf16[768,1024]{1,0:T(8,128)(2,1)}, u32[]{:S(2)}, u32[]{:S(2)}) collective-permute-start(bf16[768,1024]{1,0:T(8,128)(2,1)S(1)} %pad_maximum_fusion.refs_0_), channel_id=1, source_target_pairs={{0,1},{1,0},{2,3},{3,2},{4,5},{5,4},{6,7},{7,6},{8,9},{9,8},{10,11... | collective-permute-start | bytes 4718600 | tf_op jit(solution)/shard_map/ppermute | solution.py:51
  17.1 14.3 %collective-permute-start.3 = (bf16[256,1024]{1,0:T(8,128)(2,1)S(1)}, bf16[256,1024]{1,0:T(8,128)(2,1)S(1)}, u32[]{:S(2)}, u32[]{:S(2)}) collective-permute-start(bf16[256,1024]{1,0:T(8,128)(2,1)S(1)} %collective-permute-done), channel_id=1, source_target_pairs={{0,2},{2,0},{1,3},{3,1},{4,6},{6,4},{5,7},{7,5},{8,10},{10,8},{9,1... | collective-permute-start | bytes 1572872 | tf_op jit(solution)/shard_map/ppermute | solution.py:51
  18.7 8.4 %collective-permute-start.2 = (bf16[128,1024]{1,0:T(8,128)(2,1)S(1)}, bf16[128,1024]{1,0:T(8,128)(2,1)S(1)}, u32[]{:S(2)}, u32[]{:S(2)}) collective-permute-start(bf16[128,1024]{1,0:T(8,128)(2,1)S(1)} %dynamic-slice_bitcast_fusion), channel_id=1, source_target_pairs={{0,4},{4,0},{1,5},{5,1},{2,6},{6,2},{3,7},{7,3},{8,12},{12,8},{9,1... | collective-permute-start | bytes 786440 | tf_op jit(solution)/shard_map/ppermute | solution.py:51
  31.4 2.1 %copy-start.3 = (bf16[256,1024]{1,0:T(8,128)(2,1)}, bf16[256,1024]{1,0:T(8,128)(2,1)S(1)}, u32[]{:S(2)}) copy-start(bf16[256,1024]{1,0:T(8,128)(2,1)S(1)} %collective-permute-done.3.refs_1_) | copy-start | bytes 1572868
  31.4 2.0 %collective-permute-start.5 = (bf16[256,1024]{1,0:T(8,128)(2,1)S(1)}, bf16[256,1024]{1,0:T(8,128)(2,1)}, u32[]{:S(2)}, u32[]{:S(2)}) collective-permute-start(bf16[256,1024]{1,0:T(8,128)(2,1)S(1)} %collective-permute-done.3.refs_1_), channel_id=1, source_target_pairs={{0,1},{1,0},{2,3},{3,2},{4,5},{5,4},{6,7},{7,6},{8,9},{9,8},{10,11... | collective-permute-start | bytes 1572872 | tf_op jit(solution)/shard_map/ppermute | solution.py:51
  31.4 14.5 %collective-permute-start.6 = (bf16[1024,256]{1,0:T(8,128)(2,1)}, bf16[1024,256]{1,0:T(8,128)(2,1)S(1)}, u32[]{:S(2)}, u32[]{:S(2)}) collective-permute-start(bf16[1024,256]{1,0:T(8,128)(2,1)} %get-tuple-element.60), channel_id=1, source_target_pairs={{0,4},{4,0},{1,5},{5,1},{2,6},{6,2},{3,7},{7,3},{8,12},{12,8},{9,1... | collective-permute-start | bytes 1572872 | tf_op jit(solution)/shard_map/ppermute | solution.py:51
  39.6 39.3 %collective-permute-start.9 = (bf16[512,1024]{1,0:T(8,128)(2,1)}, bf16[512,1024]{1,0:T(8,128)(2,1)}, u32[]{:S(2)}, u32[]{:S(2)}) collective-permute-start(bf16[512,1024]{1,0:T(8,128)(2,1)} %get-tuple-element.70), channel_id=1, source_target_pairs={{24,16},{8,0},{25,17},{9,1},{26,18},{10,2},{27,19},{11,3},{28,20},... | collective-permute-start | bytes 3145736 | tf_op jit(solution)/shard_map/ppermute | solution.py:434
  46.0 14.7 %collective-permute-start.7 = (bf16[1024,256]{1,0:T(8,128)(2,1)}, bf16[1024,256]{1,0:T(8,128)(2,1)S(1)}, u32[]{:S(2)}, u32[]{:S(2)}) collective-permute-start(bf16[1024,256]{1,0:T(8,128)(2,1)} %get-tuple-element.66), channel_id=1, source_target_pairs={{0,4},{4,0},{1,5},{5,1},{2,6},{6,2},{3,7},{7,3},{8,12},{12,8},{9,1... | collective-permute-start | bytes 1572872 | tf_op jit(solution)/shard_map/ppermute | solution.py:51
  55.1 13.7 %all-to-all-start = ((bf16[8,256,128]{2,1,0:T(8,128)(2,1)}), bf16[8,256,128]{2,1,0:T(8,128)(2,1)}, u32[]{:S(2)}, u32[]{:S(2)}) async-start(bf16[8,256,128]{2,1,0:T(8,128)(2,1)} %get-tuple-element.65), calls=%async_computation | async-start | bytes 1048576 | tf_op jit(solution)/shard_map/all_to_all | solution.py:66
  59.4 19.5 %collective-permute-start.8 = (bf16[1024,256]{1,0:T(8,128)(2,1)}, bf16[1024,256]{1,0:T(8,128)(2,1)S(1)}, u32[]{:S(2)}, u32[]{:S(2)}) collective-permute-start(bf16[1024,256]{1,0:T(8,128)(2,1)} %get-tuple-element.69.refs_2_), channel_id=1, source_target_pairs={{24,16},{25,17},{26,18},{27,19},{28,20},{29,21},{30,22},{31,23}} | collective-permute-start | bytes 1572872 | tf_op jit(solution)/shard_map/ppermute | solution.py:411
  73.0 11.3 %collective-permute-start.10 = (bf16[1024,128]{1,0:T(8,128)(2,1)}, bf16[1024,128]{1,0:T(8,128)(2,1)S(1)}, u32[]{:S(2)}, u32[]{:S(2)}) collective-permute-start(bf16[1024,128]{1,0:T(8,128)(2,1)} %get-tuple-element.73), channel_id=1, source_target_pairs={{24,16},{8,0},{25,17},{9,1},{26,18},{10,2},{27,19},{11,3},{28,20},... | collective-permute-start | bytes 786440 | tf_op jit(solution)/shard_map/ppermute | solution.py:444
  78.9 5.4 %copy-start = (bf16[1024,256]{1,0:T(8,128)(2,1)}, bf16[1024,256]{1,0:T(8,128)(2,1)S(1)}, u32[]{:S(2)}) copy-start(bf16[1024,256]{1,0:T(8,128)(2,1)S(1)} %collective-permute-done.8.refs_1_.refs_3_) | copy-start | bytes 1572868
  84.3 3.9 %copy-start.4 = (bf16[1024,256]{1,0:T(8,128)(2,1)S(1)}, bf16[1024,256]{1,0:T(8,128)(2,1)}, u32[]{:S(2)}) copy-start(bf16[1024,256]{1,0:T(8,128)(2,1)} %get-tuple-element.75) | copy-start | bytes 1572868
  88.1 22.1 %collective-permute-start.12 = (bf16[512,1024]{1,0:T(8,128)(2,1)}, bf16[512,1024]{1,0:T(8,128)(2,1)}, u32[]{:S(2)}, u32[]{:S(2)}) collective-permute-start(bf16[512,1024]{1,0:T(8,128)(2,1)} %collective-permute-done.9.refs_6_.refs_3_), channel_id=1, source_target_pairs={{0,1},{1,0},{2,3},{3,2},{4,5},{5,4},{6,7},{7,6},{8,9},{9,8},{10,11... | collective-permute-start | bytes 3145736 | tf_op jit(solution)/shard_map/ppermute | solution.py:51
  88.1 16.2 %collective-permute-start.11 = (bf16[1024,256]{1,0:T(8,128)(2,1)S(1)}, bf16[1024,256]{1,0:T(8,128)(2,1)S(1)}, u32[]{:S(2)}, u32[]{:S(2)}) collective-permute-start(bf16[1024,256]{1,0:T(8,128)(2,1)S(1)} %copy-done.4), channel_id=1, source_target_pairs={{24,16},{16,8},{25,17},{17,9},{26,18},{18,10},{27,19},{19,11},{28,... | collective-permute-start | bytes 1572872 | tf_op jit(solution)/shard_map/ppermute | solution.py:411
  90.1 20.1 %all-to-all-start.1 = ((bf16[8,128,128]{2,1,0:T(8,128)(2,1)}), bf16[8,128,128]{2,1,0:T(8,128)(2,1)S(1)}, u32[]{:S(2)}, u32[]{:S(2)}) async-start(bf16[8,128,128]{2,1,0:T(8,128)(2,1)} %bitcast.26), calls=%async_computation.1 | async-start | bytes 524288 | tf_op jit(solution)/shard_map/all_to_all | solution.py:66
  107.2 16.0 %collective-permute-start.13 = (bf16[1024,256]{1,0:T(8,128)(2,1)}, bf16[1024,256]{1,0:T(8,128)(2,1)}, u32[]{:S(2)}, u32[]{:S(2)}) collective-permute-start(bf16[1024,256]{1,0:T(8,128)(2,1)} %get-tuple-element.84), channel_id=1, source_target_pairs={{16,8},{8,0},{17,9},{9,1},{18,10},{10,2},{19,11},{11,3},{20,12},{1... | collective-permute-start | bytes 1572872 | tf_op jit(solution)/shard_map/ppermute | solution.py:411
  115.4 20.7 %collective-permute-start.15 = (bf16[1024,256]{1,0:T(8,128)(2,1)}, bf16[1024,256]{1,0:T(8,128)(2,1)}, u32[]{:S(2)}, u32[]{:S(2)}) collective-permute-start(bf16[1024,256]{1,0:T(8,128)(2,1)} %get-tuple-element.88), channel_id=1, source_target_pairs={{16,0},{17,1},{18,2},{19,3},{20,4},{21,5},{22,6},{23,7}} | collective-permute-start | bytes 1572872 | tf_op jit(solution)/shard_map/ppermute | solution.py:464
  117.5 25.9 %collective-permute-start.14 = (bf16[1024,256]{1,0:T(8,128)(2,1)}, bf16[1024,256]{1,0:T(8,128)(2,1)}, u32[]{:S(2)}, u32[]{:S(2)}) collective-permute-start(bf16[1024,256]{1,0:T(8,128)(2,1)} %get-tuple-element.88), channel_id=1, source_target_pairs={{16,8},{17,9},{18,10},{19,11},{20,12},{21,13},{22,14},{23,15}} | collective-permute-start | bytes 1572872 | tf_op jit(solution)/shard_map/ppermute | solution.py:464
  119.6 16.5 %all-to-all-start.2 = ((bf16[8,256,128]{2,1,0:T(8,128)(2,1)}), bf16[8,256,128]{2,1,0:T(8,128)(2,1)S(1)}, u32[]{:S(2)}, u32[]{:S(2)}) async-start(bf16[8,256,128]{2,1,0:T(8,128)(2,1)} %get-tuple-element.90), calls=%async_computation.2 | async-start | bytes 1048576 | tf_op jit(solution)/shard_map/all_to_all | solution.py:66
  123.1 1.0 copy-start.1
  129.3 23.9 %collective-permute-start.16 = (bf16[1024,256]{1,0:T(8,128)(2,1)}, bf16[1024,256]{1,0:T(8,128)(2,1)}, u32[]{:S(2)}, u32[]{:S(2)}) collective-permute-start(bf16[1024,256]{1,0:T(8,128)(2,1)} %get-tuple-element.92), channel_id=1, source_target_pairs={{0,4},{4,0},{1,5},{5,1},{2,6},{6,2},{3,7},{7,3},{8,12},{12,8},{9,1... | collective-permute-start | bytes 1572872 | tf_op jit(solution)/shard_map/ppermute | solution.py:51
  134.7 21.9 %collective-permute-start.17 = (bf16[1024,256]{1,0:T(8,128)(2,1)}, bf16[1024,256]{1,0:T(8,128)(2,1)}, u32[]{:S(2)}, u32[]{:S(2)}) collective-permute-start(bf16[1024,256]{1,0:T(8,128)(2,1)} %get-tuple-element.96), channel_id=1, source_target_pairs={{8,0},{9,1},{10,2},{11,3},{12,4},{13,5},{14,6},{15,7}} | collective-permute-start | bytes 1572872 | tf_op jit(solution)/shard_map/ppermute | solution.py:411
  148.9 19.2 %all-to-all-start.3 = ((bf16[8,256,256]{2,1,0:T(8,128)(2,1)}), bf16[8,256,256]{2,1,0:T(8,128)(2,1)}, u32[]{:S(2)}, u32[]{:S(2)}) async-start(bf16[8,256,256]{2,1,0:T(8,128)(2,1)} %get-tuple-element.100), calls=%async_computation.3 | async-start | bytes 2097152 | tf_op jit(solution)/shard_map/all_to_all | solution.py:66
  161.6 17.1 %collective-permute-start.18 = (bf16[1024,256]{1,0:T(8,128)(2,1)}, bf16[1024,256]{1,0:T(8,128)(2,1)S(1)}, u32[]{:S(2)}, u32[]{:S(2)}) collective-permute-start(bf16[1024,256]{1,0:T(8,128)(2,1)} %get-tuple-element.104), channel_id=1, source_target_pairs={{0,4},{4,0},{1,5},{5,1},{2,6},{6,2},{3,7},{7,3},{8,12},{12,8},{9,1... | collective-permute-start | bytes 1572872 | tf_op jit(solution)/shard_map/ppermute | solution.py:51

commit v14 on v13

--- a/solution.py
+++ b/solution.py
@@ -273,7 +273,7 @@
         own[...] = (p[...] + got[...].astype(WIDE)).astype(LOW)
 
 
-def hop_kernel(ids, pair, got, own0, own1, now):
+def hop_kernel(ids, pair, got, own0, own1, unused, now):
     product = mm(pair[...], got[...])
 
     @pl.when(ids[3] == 1)
@@ -289,7 +289,7 @@
     now[...] = (mm(pair[...], got[...]) + own[...].astype(WIDE)).astype(LOW)
 
 
-def hop_start_kernel(chunk, ids, pair, got_hop, own_hop, e0, got, offset, unused, wave, p, own, keep, sem):
+def hop_start_kernel(chunk, ids, pair, got_hop, own_hop, e0, got, offset, wave, p, own, keep, sem):
     start_kernel(chunk, ids, e0, got, offset, p, own, keep, sem)
 
     @pl.when(ids[3] == 3)
@@ -394,6 +394,7 @@
     g_send[1], g_got[0] = tied((g_send[1], g_got[0]))
     g_got.append(swap(g_send[1], "x"))
     three = jnp.concatenate([e_low, e_x, e_y], axis=0)
+    three, e_xy = tied((three, e_xy))
     pieces = [in_hbm(a) for a in (three, e_xy, swap(three, "c"), swap(e_xy, "c"))]
     offset, spread = in_hbm(offsets[0]), in_hbm(spreads)
 
@@ -436,27 +437,28 @@
     wave1 = down(own0, 3)
     (m,) = order.call(spread_kernel, [in_hbm(e0), l_low, l_got], [hbm(8, rows, part)], 8)
     m = exchange(m)
+    wave2, p1, own1 = order.call(
+        functools.partial(hop_start_kernel, 1), [pair, wave1, in_hbm(own0), in_hbm(e0), g_got[1], offset],
+        [hbm(size_d, width), hbm(size_d, width, dtype=WIDE), hbm(size_d, width)], 16,
+        far_in=(5,), scratch=[keep, pltpu.SemaphoreType.DMA(())],
+    )
+    wave2 = down(wave2, 3, 2)
     prod, slab, a_low = order.call(
         spread_start_kernel, [in_hbm(e0), m, spread, l_got, g_got[1]],
         [hbm(rows, size_d, dtype=WIDE), hbm(size_d, part, dtype=WIDE), hbm(size_d, part)], 12,
         far_in=(4,), scratch=[slab_rows],
     )
     l_next = lax.ppermute(a_low, "z", level)
-    wave2, p1, own1 = order.call(
-        functools.partial(hop_start_kernel, 1), [pair, wave1, in_hbm(own0), in_hbm(e0), g_got[1], offset, quarters],
-        [hbm(size_d, width), hbm(size_d, width, dtype=WIDE), hbm(size_d, width)], 16,
-        far_in=(5, 6), scratch=[keep, pltpu.SemaphoreType.DMA(())],
-    )
-    wave2 = down(wave2, 3, 2)
-
+    (wave3,) = order.call(
+        hop_kernel, [pair, wave2, in_hbm(own0), in_hbm(own1), quarters], [hbm(size_d, width)], 10, far_in=(4,)
+    )
+    wave3 = down(wave3, 2, 1)
     m, near = order.call(
         spread_hop_kernel, [pair, in_hbm(e1), l_next], [hbm(size_d, part), hbm(8, rows, part)], 10
     )
     m = exchange(m.reshape(8, part, part))
     quarters, near = tied((quarters, near))
     quarters = [quarters, swap(quarters, "c")]
-    (wave3,) = order.call(hop_kernel, [pair, wave2, in_hbm(own0), in_hbm(own1)], [hbm(size_d, width)], 10)
-    wave3 = down(wave3, 2, 1)
     following, far_slab = order.call(
         next_kernel, [pair, in_hbm(slab), m, *quarters], [hbm(size_d, size_d), hbm(size_d, rows)], 12,
         far_in=(3, 4), scratch=[pltpu.VMEM((part, size_d), LOW), pltpu.SemaphoreType.DMA((4,))],
@@ -465,23 +467,23 @@
     near, far_slab = tied((near, far_slab))
     near = exchange(near)
 
+    (wave4,) = order.call(end_hop_kernel, [pair, wave3, in_hbm(own1)], [hbm(size_d, width)], 8)
+    wave4 = down(wave4, 1)
     out_offset, other0 = last(0, p0, [wave1, wave2, wave3], None)
     other0 = swap(other0, "x")
-    (wave4,) = order.call(end_hop_kernel, [pair, wave3, in_hbm(own1)], [hbm(size_d, width)], 8)
-    wave4 = down(wave4, 1)
+    out_offset, other1 = last(1, p1, [wave2, wave3, wave4], out_offset)
+    other1 = swap(other1, "x")
     (m,) = order.call(
         far_kernel, [pair, in_hbm(e1), in_hbm(following), *far, near], [hbm(8, rows, rows)], 14,
         far_in=(5,), scratch=[pltpu.VMEM((size_d, rows), LOW)],
     )
     m = exchange(m)
     out_offset = add(0, other0, out_offset)
-    out_offset, other1 = last(1, p1, [wave2, wave3, wave4], out_offset)
-    other1 = swap(other1, "x")
+    out_offset = add(1, other1, out_offset)
     out_gain, out_spread = order.call(
         end_kernel, [pair, in_hbm(e1), in_hbm(following), near, in_hbm(prod), spread, m],
         [wide(rows, size_d), wide(rows, size_d)], 18, scratch=[slab_rows, slab_rows],
     )
-    out_offset = add(1, other1, out_offset)
     return (out_gain[None], out_spread[None], out_offset[None])
 
 

time: 184 us -> 221 us (1.20)
  the two profiles are of different devices: /device:TPU:16 before, /device:TPU:0 now
where the time goes in v14:
time: 221 us; the launch traced here: 220 us
  waiting for transfers between devices  100 us (45%)
  Pallas kernels  65.7 us (30%)
  starting transfers between devices  34.8 us (16%)
  blocking collectives  9.78 us (4%)
  local copies, waits for them, and re-layouts  5.46 us (2%)
  other arithmetic  2.85 us (1%)
    pallas_call x15, Pallas kernels, call(): pl.pallas_call(body, in_specs=[SMEM, ANY] + [ANY if i in far_in else VMEM...  65.7 us
    ppermute x11, waiting for transfers between devices, swap(): return lax.ppermute(value, axis, [(0, 1), (1, 0)])  60.3 us
    ppermute x4, waiting for transfers between devices, down(): lax.ppermute(value, 'z', [(source, source - 1) for source in sources])  19.8 us
    ppermute x11, starting transfers between devices, swap(): return lax.ppermute(value, axis, [(0, 1), (1, 0)])  13 us
    all_to_all x3, starting transfers between devices, exchange(): return lax.all_to_all(blocks, GROUP, 0, 0)  12.4 us
    ppermute x1, waiting for transfers between devices, suffix(): lax.ppermute(far_slab, 'z', [(2, 0)])  9.91 us
    all_to_all x1, blocking collectives, exchange(): return lax.all_to_all(blocks, GROUP, 0, 0)  9.78 us
  transfers between devices with their start and end apart: 22, of which 12 were waited for; matrix products, arithmetic and copies ran while one was open for 2% of the time, Pallas kernels for 21%

profile of v14, /device:TPU:0, one launch (start us, length us, event | category | flops | bytes accessed | tf_op | source)
XLA Modules:
  0.0 219.9 jit_solution(18315006443052331710)
XLA Ops:
  0.6 1.3 convert_bitcast_fusion
  1.9 3.0 %collective-permute-start = (bf16[256,1024]{1,0:T(8,128)(2,1)S(1)}, bf16[256,1024]{1,0:T(8,128)(2,1)S(1)}, u32[]{:S(2)}, u32[]{:S(2)}) collective-permute-start(bf16[256,1024]{1,0:T(8,128)(2,1)S(1)} %convert_bitcast_fusion), channel_id=1, source_target_pairs={{0,4},{4,0},{1,5},{5,1},{2,6},{6,2},{3,7},{7,3},{8,12},{12,8},{9,1... | collective-permute-start | bytes 1572872 | tf_op jit(solution)/shard_map/ppermute | solution.py:51
  4.9 1.5 collective-permute-start.1
  6.5 1.3 convert_element_type.25
  8.5 2.6 %fusion.1 = (bf16[1024,256]{1,0:T(8,128)(2,1)}, bf16[1024,256]{1,0:T(8,128)(2,1)}) fusion(f32[1,1024,1024]{2,1,0:T(8,128)} %param.5, s32[]{:T(128)S(6)} %select_n.11, s32[]{:T(128)S(6)} %select_n.10), kind=kLoop, calls=%fused_computation.4 | loop fusion | bytes 2097160 | tf_op jit(solution)/shard_map/convert_element_type | solution.py:386
  11.1 5.8 %collective-permute-done = bf16[256,1024]{1,0:T(8,128)(2,1)S(1)} collective-permute-done((bf16[256,1024]{1,0:T(8,128)(2,1)S(1)}, bf16[256,1024]{1,0:T(8,128)(2,1)S(1)}, u32[]{:S(2)}, u32[]{:S(2)}) %collective-permute-start) | collective-permute-done | bytes 524320 | tf_op jit(solution)/shard_map/ppermute | solution.py:51
  16.9 1.8 collective-permute-start.3
  18.6 1.5 collective-permute-start.2
  20.3 5.5 %collective-permute-done.2.refs_2_.refs_3_ = bf16[128,1024]{1,0:T(8,128)(2,1)S(1)} collective-permute-done((bf16[128,1024]{1,0:T(8,128)(2,1)}, bf16[128,1024]{1,0:T(8,128)(2,1)S(1)}, u32[]{:S(2)}, u32[]{:S(2)}) %collective-permute-start.2) | collective-permute-done | bytes 262176 | tf_op jit(solution)/shard_map/ppermute | solution.py:51
  25.7 4.3 %collective-permute-done.3.refs_1_ = bf16[256,1024]{1,0:T(8,128)(2,1)} collective-permute-done((bf16[256,1024]{1,0:T(8,128)(2,1)S(1)}, bf16[256,1024]{1,0:T(8,128)(2,1)}, u32[]{:S(2)}, u32[]{:S(2)}) %collective-permute-start.3) | collective-permute-done | bytes 524320 | tf_op jit(solution)/shard_map/ppermute | solution.py:51
  30.1 1.4 collective-permute-start.6
  31.8 12.8 %collective-permute-done.6.refs_1_ = bf16[1024,256]{1,0:T(8,128)(2,1)S(1)} collective-permute-done((bf16[1024,256]{1,0:T(8,128)(2,1)}, bf16[1024,256]{1,0:T(8,128)(2,1)S(1)}, u32[]{:S(2)}, u32[]{:S(2)}) %collective-permute-start.6) | collective-permute-done | bytes 524320 | tf_op jit(solution)/shard_map/ppermute | solution.py:51
  44.6 1.4 collective-permute-start.8
  46.1 6.1 %shard_map.58 = (bf16[1024,1024]{1,0:T(8,128)(2,1)}, bf16[1024,1024]{1,0:T(8,128)(2,1)}, bf16[1024,1024]{1,0:T(8,128)(2,1)S(1)}, bf16[512,1024]{1,0:T(8,128)(2,1)}, s32[8,128]{1,0:T(8,128)S(1)}) custom-call(s32[4]{0:T(128)S(1)} %pad_add_fusion.ids, s32[8,128]{1,0:T(8,128)S(1)} %broadcast_in_dim.12.token, ...), custom_call_target="tpu_custom_call", output_to_operand_aliasing={{4}: (1, {})} | custom-call | flops 1 | bytes 1 | tf_op jit(solution)/shard_map/pallas_call | solution.py:93
  52.2 4.2 %shard_map.59 = (f32[1024,256]{1,0:T(8,128)}, bf16[1024,256]{1,0:T(8,128)(2,1)}, s32[8,128]{1,0:T(8,128)S(1)}) custom-call(s32[4]{0:T(128)S(1)} %pad_add_fusion.ids, s32[8,128]{1,0:T(8,128)S(1)} %get-tuple-element.62.token, bf16[1024,1024]{1,0:T(8,128)(2,1)} %get-tuple-element.63.refs_0_.refs_3_, ...), custom_call_target="tpu_custom_call", output_to_operand_aliasing={{2}: (1, {})} | custom-call | flops 1 | bytes 1 | tf_op jit(solution)/shard_map/pallas_call | solution.py:93
  57.2 1.3 collective-permute-start.10
  58.6 3.1 %shard_map.60 = (bf16[8,256,128]{2,1,0:T(8,128)(2,1)}, s32[8,128]{1,0:T(8,128)S(1)}) custom-call(s32[4]{0:T(128)S(1)} %pad_add_fusion.ids, s32[8,128]{1,0:T(8,128)S(1)} %get-tuple-element.66.token, bf16[1024,1024]{1,0:T(8,128)(2,1)} %get-tuple-element.63.refs_0_.refs_3_, ...), custom_call_target="tpu_custom_call", output_to_operand_aliasing={{1}: (1, {})} | custom-call | flops 1 | bytes 1 | tf_op jit(solution)/shard_map/pallas_call | solution.py:93
  61.7 4.2 %all-to-all-start = ((bf16[8,256,128]{2,1,0:T(8,128)(2,1)}), bf16[8,256,128]{2,1,0:T(8,128)(2,1)}, u32[]{:S(2)}, u32[]{:S(2)}) async-start(bf16[8,256,128]{2,1,0:T(8,128)(2,1)} %get-tuple-element.73), calls=%async_computation | async-start | bytes 1048576 | tf_op jit(solution)/shard_map/all_to_all | solution.py:66
  65.9 5.4 %shard_map.61 = (bf16[1024,256]{1,0:T(8,128)(2,1)}, f32[1024,256]{1,0:T(8,128)}, bf16[1024,256]{1,0:T(8,128)(2,1)}, s32[8,128]{1,0:T(8,128)S(1)}) custom-call(s32[4]{0:T(128)S(1)} %pad_add_fusion.ids, s32[8,128]{1,0:T(8,128)S(1)} %get-tuple-element.68.token, bf16[1024,1024]{1,0:T(8,128)(2,1)S(1)} %get-tuple-element.69.refs_0_, ...), custom_call_target="tpu_custom_call", output_to_operand_aliasing={{3}: (1, {})} | custom-call | flops 1 | bytes 1 | tf_op jit(solution)/shard_map/pallas_call | solution.py:93
  72.0 3.2 %all-to-all-done.refs_1_ = bf16[8,256,128]{2,1,0:T(8,128)(2,1)} async-done(((bf16[8,256,128]{2,1,0:T(8,128)(2,1)}), bf16[8,256,128]{2,1,0:T(8,128)(2,1)}, u32[]{:S(2)}, u32[]{:S(2)}) %all-to-all-start) | async-done | bytes 524320 | tf_op jit(solution)/shard_map/all_to_all | solution.py:66
  75.1 4.2 %shard_map.62 = (f32[256,1024]{1,0:T(8,128)}, f32[1024,128]{1,0:T(8,128)}, bf16[1024,128]{1,0:T(8,128)(2,1)}, s32[8,128]{1,0:T(8,128)S(1)}) custom-call(s32[4]{0:T(128)S(1)} %pad_add_fusion.ids, s32[8,128]{1,0:T(8,128)S(1)} %get-tuple-element.72.token, bf16[1024,1024]{1,0:T(8,128)(2,1)} %get-tuple-element.63.refs_0_.refs_3_, ...), custom_call_target="tpu_custom_call", output_to_operand_aliasing={{3}: (1, {})} | custom-call | flops 1 | bytes 1 | tf_op jit(solution)/shard_map/pallas_call | solution.py:93
  79.3 1.3 collective-permute-start.11
  80.6 3.3 %collective-permute-done.10.refs_4_.refs_3_ = bf16[512,1024]{1,0:T(8,128)(2,1)} collective-permute-done((bf16[512,1024]{1,0:T(8,128)(2,1)}, bf16[512,1024]{1,0:T(8,128)(2,1)}, u32[]{:S(2)}, u32[]{:S(2)}) %collective-permute-start.10) | collective-permute-done | bytes 1048608 | tf_op jit(solution)/shard_map/ppermute | solution.py:435
  83.9 2.8 %shard_map.63 = (bf16[1024,256]{1,0:T(8,128)(2,1)}, s32[8,128]{1,0:T(8,128)S(1)}) custom-call(s32[4]{0:T(128)S(1)} %pad_add_fusion.ids, s32[8,128]{1,0:T(8,128)S(1)} %get-tuple-element.74.token, bf16[1024,1024]{1,0:T(8,128)(2,1)S(1)} %get-tuple-element.69.refs_0_, ...), custom_call_target="tpu_custom_call", output_to_operand_aliasing={{1}: (1, {})} | custom-call | flops 1 | bytes 1 | tf_op jit(solution)/shard_map/pallas_call | solution.py:93
  86.7 3.9 %collective-permute-done.11.refs_2_ = bf16[1024,128]{1,0:T(8,128)(2,1)S(1)} collective-permute-done((bf16[1024,128]{1,0:T(8,128)(2,1)}, bf16[1024,128]{1,0:T(8,128)(2,1)S(1)}, u32[]{:S(2)}, u32[]{:S(2)}) %collective-permute-start.11) | collective-permute-done | bytes 262176 | tf_op jit(solution)/shard_map/ppermute | solution.py:451
  90.6 3.8 %shard_map.64 = (bf16[1024,128]{1,0:T(8,128)(2,1)}, bf16[8,256,128]{2,1,0:T(8,128)(2,1)}, s32[8,128]{1,0:T(8,128)S(1)}) custom-call(s32[4]{0:T(128)S(1)} %pad_add_fusion.ids, s32[8,128]{1,0:T(8,128)S(1)} %get-tuple-element.78.token, bf16[1024,1024]{1,0:T(8,128)(2,1)S(1)} %get-tuple-element.69.refs_0_, ...), custom_call_target="tpu_custom_call", output_to_operand_aliasing={{2}: (1, {})} | custom-call | flops 1 | bytes 1 | tf_op jit(solution)/shard_map/pallas_call | solution.py:93
  94.4 1.3 collective-permute-start.13
  95.7 9.8 %all_to_all.20.refs_2_ = bf16[8,128,128]{2,1,0:T(8,128)(2,1)S(1)} all-to-all(bf16[8,128,128]{2,1,0:T(8,128)(2,1)} %bitcast.26), channel_id=1, replica_groups=mesh['z'=4,'x'=2,'y'=2,'c'=2] {'y','c','x'}, dimensions={0} | all-to-all | bytes 524288 | tf_op jit(solution)/shard_map/all_to_all | solution.py:66
  105.5 5.0 %shard_map.65 = (bf16[1024,1024]{1,0:T(8,128)(2,1)}, bf16[1024,256]{1,0:T(8,128)(2,1)}, s32[8,128]{1,0:T(8,128)S(1)}) custom-call(s32[4]{0:T(128)S(1)} %pad_add_fusion.ids, s32[8,128]{1,0:T(8,128)S(1)} %get-tuple-element.81.token, bf16[1024,1024]{1,0:T(8,128)(2,1)S(1)} %get-tuple-element.69.refs_0_, ...), custom_call_target="tpu_custom_call", output_to_operand_aliasing={{2}: (1, {})} | custom-call | flops 1 | bytes 1 | tf_op jit(solution)/shard_map/pallas_call | solution.py:93
  110.5 4.0 %collective-permute-done.13.refs_1_.refs_5_.refs_4_ = bf16[1024,256]{1,0:T(8,128)(2,1)S(1)} collective-permute-done((bf16[1024,256]{1,0:T(8,128)(2,1)S(1)}, bf16[1024,256]{1,0:T(8,128)(2,1)S(1)}, u32[]{:S(2)}, u32[]{:S(2)}) %collective-permute-start.13) | collective-permute-done | bytes 524320 | tf_op jit(solution)/shard_map/ppermute | solution.py:412
  114.6 2.6 %shard_map.66 = (bf16[1024,256]{1,0:T(8,128)(2,1)}, s32[8,128]{1,0:T(8,128)S(1)}) custom-call(s32[4]{0:T(128)S(1)} %pad_add_fusion.ids, s32[8,128]{1,0:T(8,128)S(1)} %get-tuple-element.86.token, bf16[1024,1024]{1,0:T(8,128)(2,1)S(1)} %get-tuple-element.69.refs_0_, ...), custom_call_target="tpu_custom_call", output_to_operand_aliasing={{1}: (1, {})} | custom-call | flops 1 | bytes 1 | tf_op jit(solution)/shard_map/pallas_call | solution.py:93
  117.1 1.5 collective-permute-start.14
  118.6 1.5 collective-permute-start.15
  120.1 1.3 collective-permute-start.16
  121.4 4.0 %all-to-all-start.2 = ((bf16[8,256,128]{2,1,0:T(8,128)(2,1)}), bf16[8,256,128]{2,1,0:T(8,128)(2,1)S(1)}, u32[]{:S(2)}, u32[]{:S(2)}) async-start(bf16[8,256,128]{2,1,0:T(8,128)(2,1)} %get-tuple-element.98), calls=%async_computation.2 | async-start | bytes 1048576 | tf_op jit(solution)/shard_map/all_to_all | solution.py:66
  126.4 1.0 copy-done.3
  127.4 5.1 %shard_map.67 = (f32[1024,1024]{1,0:T(8,128)}, bf16[1024,256]{1,0:T(8,128)(2,1)}, s32[8,128]{1,0:T(8,128)S(1)}) custom-call(s32[4]{0:T(128)S(1)} %pad_add_fusion.ids, s32[8,128]{1,0:T(8,128)S(1)} %get-tuple-element.88.token, bf16[1024,1024]{1,0:T(8,128)(2,1)S(1)} %get-tuple-element.69.refs_0_, ...), custom_call_target="tpu_custom_call", output_to_operand_aliasing={{2}: (1, {})} | custom-call | flops 1 | bytes 1 | tf_op jit(solution)/shard_map/pallas_call | solution.py:93
  132.5 15.8 %collective-permute-done.14.refs_5_ = bf16[1024,256]{1,0:T(8,128)(2,1)} collective-permute-done((bf16[1024,256]{1,0:T(8,128)(2,1)}, bf16[1024,256]{1,0:T(8,128)(2,1)}, u32[]{:S(2)}, u32[]{:S(2)}) %collective-permute-start.14) | collective-permute-done | bytes 524320 | tf_op jit(solution)/shard_map/ppermute | solution.py:412
  148.3 5.2 %shard_map.68 = (f32[1024,1024]{1,0:T(8,128)}, bf16[1024,256]{1,0:T(8,128)(2,1)}, s32[8,128]{1,0:T(8,128)S(1)}) custom-call(s32[4]{0:T(128)S(1)} %pad_add_fusion.ids, s32[8,128]{1,0:T(8,128)S(1)} %get-tuple-element.90.token, bf16[1024,1024]{1,0:T(8,128)(2,1)S(1)} %get-tuple-element.69.refs_0_, ...), custom_call_target="tpu_custom_call", output_to_operand_aliasing={{2}: (1, {}), {0}: (9, {})} | custom-call | flops 1 | bytes 1 | tf_op jit(solution)/shard_map/pallas_call | solution.py:93
  153.6 9.9 %collective-permute-done.16.refs_4_ = bf16[1024,256]{1,0:T(8,128)(2,1)} collective-permute-done((bf16[1024,256]{1,0:T(8,128)(2,1)}, bf16[1024,256]{1,0:T(8,128)(2,1)}, u32[]{:S(2)}, u32[]{:S(2)}) %collective-permute-start.16) | collective-permute-done | bytes 524320 | tf_op jit(solution)/shard_map/ppermute | solution.py:466
  163.5 5.5 %shard_map.69 = (bf16[8,256,256]{2,1,0:T(8,128)(2,1)}, s32[8,128]{1,0:T(8,128)S(1)}) custom-call(s32[4]{0:T(128)S(1)} %pad_add_fusion.ids, s32[8,128]{1,0:T(8,128)S(1)} %get-tuple-element.94.token, bf16[1024,1024]{1,0:T(8,128)(2,1)S(1)} %get-tuple-element.69.refs_0_, bf16[1024,1024]{1,0:T(8,128)(2,1)} %get-tuple-element.79.refs_1_, ...), custom_call_target="tpu_custom_call", output_to_operand_aliasing={{1}: (1, {})} | custom-call | flops 1 | bytes 1 | tf_op jit(solution)/shard_map/pallas_call | solution.py:93
  169.0 4.2 %all-to-all-start.3 = ((bf16[8,256,256]{2,1,0:T(8,128)(2,1)}), bf16[8,256,256]{2,1,0:T(8,128)(2,1)}, u32[]{:S(2)}, u32[]{:S(2)}) async-start(bf16[8,256,256]{2,1,0:T(8,128)(2,1)} %get-tuple-element.107), calls=%async_computation.3 | async-start | bytes 2097152 | tf_op jit(solution)/shard_map/all_to_all | solution.py:66
  173.3 1.9 collective-permute-start.17
  175.4 24.0 %collective-permute-done.17.refs_0_ = bf16[1024,256]{1,0:T(8,128)(2,1)S(1)} collective-permute-done((bf16[1024,256]{1,0:T(8,128)(2,1)S(1)}, bf16[1024,256]{1,0:T(8,128)(2,1)S(1)}, u32[]{:S(2)}, u32[]{:S(2)}) %collective-permute-start.17) | collective-permute-done | bytes 524320 | tf_op jit(solution)/shard_map/ppermute | solution.py:51
  199.3 2.9 %shard_map.70 = (f32[1024,1024]{1,0:T(8,128)}, s32[8,128]{1,0:T(8,128)S(1)}) custom-call(s32[4]{0:T(128)S(1)} %pad_add_fusion.ids, s32[8,128]{1,0:T(8,128)S(1)} %get-tuple-element.99.token, bf16[1024,256]{1,0:T(8,128)(2,1)S(1)} %collective-permute-done.17.refs_0_, f32[1024,1024]{1,0:T(8,128)} %bitcast.23, ...), custom_call_target="tpu_custom_call", output_to_operand_aliasing={{1}: (1, {}), {0}: (4, {})} | custom-call | flops 1 | bytes 1 | tf_op jit(solution)/shard_map/pallas_call | solution.py:93
  202.2 7.9 %collective-permute-done.18.refs_0_ = bf16[1024,256]{1,0:T(8,128)(2,1)S(1)} collective-permute-done((bf16[1024,256]{1,0:T(8,128)(2,1)}, bf16[1024,256]{1,0:T(8,128)(2,1)S(1)}, u32[]{:S(2)}, u32[]{:S(2)}) %collective-permute-start.18) | collective-permute-done | bytes 524320 | tf_op jit(solution)/shard_map/ppermute | solution.py:51
  210.1 2.9 %shard_map.71 = (f32[1024,1024]{1,0:T(8,128)}, s32[8,128]{1,0:T(8,128)S(1)}) custom-call(s32[4]{0:T(128)S(1)} %pad_add_fusion.ids, s32[8,128]{1,0:T(8,128)S(1)} %get-tuple-element.102.token, bf16[1024,256]{1,0:T(8,128)(2,1)S(1)} %collective-permute-done.18.refs_0_, f32[1024,1024]{1,0:T(8,128)} %bitcast.24, ...), custom_call_target="tpu_custom_call", output_to_operand_aliasing={{1}: (1, {}), {0}: (4, {})} | custom-call | flops 1 | bytes 1 | tf_op jit(solution)/shard_map/pallas_call | solution.py:93
  213.0 6.9 %shard_map.72 = (f32[256,1024]{1,0:T(8,128)}, f32[256,1024]{1,0:T(8,128)}, s32[8,128]{1,0:T(8,128)S(1)}) custom-call(s32[4]{0:T(128)S(1)} %pad_add_fusion.ids, s32[8,128]{1,0:T(8,128)S(1)} %get-tuple-element.105.token, bf16[1024,1024]{1,0:T(8,128)(2,1)S(1)} %get-tuple-element.69.refs_0_, ...), custom_call_target="tpu_custom_call", output_to_operand_aliasing={{2}: (1, {})} | custom-call | flops 1 | bytes 1 | tf_op jit(solution)/shard_map/pallas_call | solution.py:93
  (36 shorter events, 3.9 us)
Async XLA Ops:
  1.9 14.9 %collective-permute-start = (bf16[256,1024]{1,0:T(8,128)(2,1)S(1)}, bf16[256,1024]{1,0:T(8,128)(2,1)S(1)}, u32[]{:S(2)}, u32[]{:S(2)}) collective-permute-start(bf16[256,1024]{1,0:T(8,128)(2,1)S(1)} %convert_bitcast_fusion), channel_id=1, source_target_pairs={{0,4},{4,0},{1,5},{5,1},{2,6},{6,2},{3,7},{7,3},{8,12},{12,8},{9,1... | collective-permute-start | bytes 1572872 | tf_op jit(solution)/shard_map/ppermute | solution.py:51
  4.9 15.2 %collective-permute-start.1 = (bf16[256,1024]{1,0:T(8,128)(2,1)S(1)}, bf16[256,1024]{1,0:T(8,128)(2,1)S(1)}, u32[]{:S(2)}, u32[]{:S(2)}) collective-permute-start(bf16[256,1024]{1,0:T(8,128)(2,1)S(1)} %convert_bitcast_fusion), channel_id=1, source_target_pairs={{0,2},{2,0},{1,3},{3,1},{4,6},{6,4},{5,7},{7,5},{8,10},{10,8},{9,1... | collective-permute-start | bytes 1572872 | tf_op jit(solution)/shard_map/ppermute | solution.py:51
  16.9 13.2 %collective-permute-start.3 = (bf16[256,1024]{1,0:T(8,128)(2,1)S(1)}, bf16[256,1024]{1,0:T(8,128)(2,1)}, u32[]{:S(2)}, u32[]{:S(2)}) collective-permute-start(bf16[256,1024]{1,0:T(8,128)(2,1)S(1)} %collective-permute-done), channel_id=1, source_target_pairs={{0,2},{2,0},{1,3},{3,1},{4,6},{6,4},{5,7},{7,5},{8,10},{10,8},{9,1... | collective-permute-start | bytes 1572872 | tf_op jit(solution)/shard_map/ppermute | solution.py:51
  18.6 7.1 %collective-permute-start.2 = (bf16[128,1024]{1,0:T(8,128)(2,1)}, bf16[128,1024]{1,0:T(8,128)(2,1)S(1)}, u32[]{:S(2)}, u32[]{:S(2)}) collective-permute-start(bf16[128,1024]{1,0:T(8,128)(2,1)} %dynamic-slice_bitcast_fusion), channel_id=1, source_target_pairs={{0,4},{4,0},{1,5},{5,1},{2,6},{6,2},{3,7},{7,3},{8,12},{12,8},{9,1... | collective-permute-start | bytes 786440 | tf_op jit(solution)/shard_map/ppermute | solution.py:51
  20.2 25.8 %copy-start.5 = (bf16[768,1024]{1,0:T(8,128)(2,1)}, bf16[768,1024]{1,0:T(8,128)(2,1)S(1)}, u32[]{:S(2)}) copy-start(bf16[768,1024]{1,0:T(8,128)(2,1)S(1)} %pad_maximum_fusion.refs_0_) | copy-start | bytes 4718596
  30.1 16.0 %collective-permute-start.4 = (bf16[768,1024]{1,0:T(8,128)(2,1)S(1)}, bf16[768,1024]{1,0:T(8,128)(2,1)}, u32[]{:S(2)}, u32[]{:S(2)}) collective-permute-start(bf16[768,1024]{1,0:T(8,128)(2,1)S(1)} %pad_maximum_fusion.refs_0_), channel_id=1, source_target_pairs={{0,1},{1,0},{2,3},{3,2},{4,5},{5,4},{6,7},{7,6},{8,9},{9,8},{10,11... | collective-permute-start | bytes 4718600 | tf_op jit(solution)/shard_map/ppermute | solution.py:51
  30.1 14.5 %collective-permute-start.6 = (bf16[1024,256]{1,0:T(8,128)(2,1)}, bf16[1024,256]{1,0:T(8,128)(2,1)S(1)}, u32[]{:S(2)}, u32[]{:S(2)}) collective-permute-start(bf16[1024,256]{1,0:T(8,128)(2,1)} %get-tuple-element.64), channel_id=1, source_target_pairs={{0,4},{4,0},{1,5},{5,1},{2,6},{6,2},{3,7},{7,3},{8,12},{12,8},{9,1... | collective-permute-start | bytes 1572872 | tf_op jit(solution)/shard_map/ppermute | solution.py:51
  31.5 14.5 %collective-permute-start.5 = (bf16[256,1024]{1,0:T(8,128)(2,1)}, bf16[256,1024]{1,0:T(8,128)(2,1)}, u32[]{:S(2)}, u32[]{:S(2)}) collective-permute-start(bf16[256,1024]{1,0:T(8,128)(2,1)} %collective-permute-done.3.refs_1_), channel_id=1, source_target_pairs={{0,1},{1,0},{2,3},{3,2},{4,5},{5,4},{6,7},{7,6},{8,9},{9,8},{10,11... | collective-permute-start | bytes 1572872 | tf_op jit(solution)/shard_map/ppermute | solution.py:51
  44.6 21.2 %collective-permute-start.8 = (bf16[1024,256]{1,0:T(8,128)(2,1)}, bf16[1024,256]{1,0:T(8,128)(2,1)S(1)}, u32[]{:S(2)}, u32[]{:S(2)}) collective-permute-start(bf16[1024,256]{1,0:T(8,128)(2,1)} %get-tuple-element.71), channel_id=1, source_target_pairs={{0,4},{4,0},{1,5},{5,1},{2,6},{6,2},{3,7},{7,3},{8,12},{12,8},{9,1... | collective-permute-start | bytes 1572872 | tf_op jit(solution)/shard_map/ppermute | solution.py:51
  52.2 6.3 %copy-start.4 = (f32[1,256,1024]{2,1,0:T(8,128)S(1)}, f32[1,256,1024]{2,1,0:T(8,128)}, u32[]{:S(2)}) copy-start(f32[1,256,1024]{2,1,0:T(8,128)} %refs_5_.1) | copy-start | bytes 3145732
  56.5 9.4 %collective-permute-start.7 = (bf16[1024,256]{1,0:T(8,128)(2,1)}, bf16[1024,256]{1,0:T(8,128)(2,1)S(1)}, u32[]{:S(2)}, u32[]{:S(2)}) collective-permute-start(bf16[1024,256]{1,0:T(8,128)(2,1)} %get-tuple-element.70.refs_2_), channel_id=1, source_target_pairs={{24,16},{25,17},{26,18},{27,19},{28,20},{29,21},{30,22},{31,23}} | collective-permute-start | bytes 1572872 | tf_op jit(solution)/shard_map/ppermute | solution.py:412
  57.2 26.7 %collective-permute-start.10 = (bf16[512,1024]{1,0:T(8,128)(2,1)}, bf16[512,1024]{1,0:T(8,128)(2,1)}, u32[]{:S(2)}, u32[]{:S(2)}) collective-permute-start(bf16[512,1024]{1,0:T(8,128)(2,1)} %get-tuple-element.77), channel_id=1, source_target_pairs={{24,16},{8,0},{25,17},{9,1},{26,18},{10,2},{27,19},{11,3},{28,20},... | collective-permute-start | bytes 3145736 | tf_op jit(solution)/shard_map/ppermute | solution.py:435
  61.7 13.4 %all-to-all-start = ((bf16[8,256,128]{2,1,0:T(8,128)(2,1)}), bf16[8,256,128]{2,1,0:T(8,128)(2,1)}, u32[]{:S(2)}, u32[]{:S(2)}) async-start(bf16[8,256,128]{2,1,0:T(8,128)(2,1)} %get-tuple-element.73), calls=%async_computation | async-start | bytes 1048576 | tf_op jit(solution)/shard_map/all_to_all | solution.py:66
  65.9 5.4 %copy-start.2 = (bf16[1024,256]{1,0:T(8,128)(2,1)}, bf16[1024,256]{1,0:T(8,128)(2,1)S(1)}, u32[]{:S(2)}) copy-start(bf16[1024,256]{1,0:T(8,128)(2,1)S(1)} %collective-permute-done.7.refs_1_.refs_3_) | copy-start | bytes 1572868
  71.3 9.3 %collective-permute-start.9 = (bf16[1024,256]{1,0:T(8,128)(2,1)}, bf16[1024,256]{1,0:T(8,128)(2,1)S(1)}, u32[]{:S(2)}, u32[]{:S(2)}) collective-permute-start(bf16[1024,256]{1,0:T(8,128)(2,1)} %get-tuple-element.75), channel_id=1, source_target_pairs={{24,16},{16,8},{25,17},{17,9},{26,18},{18,10},{27,19},{19,11},{28,... | collective-permute-start | bytes 1572872 | tf_op jit(solution)/shard_map/ppermute | solution.py:412
  79.3 11.3 %collective-permute-start.11 = (bf16[1024,128]{1,0:T(8,128)(2,1)}, bf16[1024,128]{1,0:T(8,128)(2,1)S(1)}, u32[]{:S(2)}, u32[]{:S(2)}) collective-permute-start(bf16[1024,128]{1,0:T(8,128)(2,1)} %get-tuple-element.80), channel_id=1, source_target_pairs={{24,16},{8,0},{25,17},{9,1},{26,18},{10,2},{27,19},{11,3},{28,20},... | collective-permute-start | bytes 786440 | tf_op jit(solution)/shard_map/ppermute | solution.py:451
  80.6 13.8 %copy-start = (bf16[1024,256]{1,0:T(8,128)(2,1)}, bf16[1024,256]{1,0:T(8,128)(2,1)S(1)}, u32[]{:S(2)}) copy-start(bf16[1024,256]{1,0:T(8,128)(2,1)S(1)} %collective-permute-done.9.refs_1_.refs_4_.refs_3_) | copy-start | bytes 1572868
  86.7 7.7 %copy-start.7 = (bf16[1024,256]{1,0:T(8,128)(2,1)S(1)}, bf16[1024,256]{1,0:T(8,128)(2,1)}, u32[]{:S(2)}) copy-start(bf16[1024,256]{1,0:T(8,128)(2,1)} %get-tuple-element.87) | copy-start | bytes 1572868
  94.4 11.1 %collective-permute-start.12 = (bf16[512,1024]{1,0:T(8,128)(2,1)}, bf16[512,1024]{1,0:T(8,128)(2,1)S(1)}, u32[]{:S(2)}, u32[]{:S(2)}) collective-permute-start(bf16[512,1024]{1,0:T(8,128)(2,1)} %collective-permute-done.10.refs_4_.refs_3_), channel_id=1, source_target_pairs={{0,1},{1,0},{2,3},{3,2},{4,5},{5,4},{6,7},{7,6},{8,9},{9,8},{10,11... | collective-permute-start | bytes 3145736 | tf_op jit(solution)/shard_map/ppermute | solution.py:51
  94.4 20.2 %collective-permute-start.13 = (bf16[1024,256]{1,0:T(8,128)(2,1)S(1)}, bf16[1024,256]{1,0:T(8,128)(2,1)S(1)}, u32[]{:S(2)}, u32[]{:S(2)}) collective-permute-start(bf16[1024,256]{1,0:T(8,128)(2,1)S(1)} %copy-done.7), channel_id=1, source_target_pairs={{16,8},{8,0},{17,9},{9,1},{18,10},{10,2},{19,11},{11,3},{20,12},{1... | collective-permute-start | bytes 1572872 | tf_op jit(solution)/shard_map/ppermute | solution.py:412
  117.1 31.2 %collective-permute-start.14 = (bf16[1024,256]{1,0:T(8,128)(2,1)}, bf16[1024,256]{1,0:T(8,128)(2,1)}, u32[]{:S(2)}, u32[]{:S(2)}) collective-permute-start(bf16[1024,256]{1,0:T(8,128)(2,1)} %get-tuple-element.92), channel_id=1, source_target_pairs={{8,0},{9,1},{10,2},{11,3},{12,4},{13,5},{14,6},{15,7}} | collective-permute-start | bytes 1572872 | tf_op jit(solution)/shard_map/ppermute | solution.py:412
  118.6 35.0 %collective-permute-start.15 = (bf16[1024,256]{1,0:T(8,128)(2,1)}, bf16[1024,256]{1,0:T(8,128)(2,1)}, u32[]{:S(2)}, u32[]{:S(2)}) collective-permute-start(bf16[1024,256]{1,0:T(8,128)(2,1)} %get-tuple-element.96), channel_id=1, source_target_pairs={{16,8},{17,9},{18,10},{19,11},{20,12},{21,13},{22,14},{23,15}} | collective-permute-start | bytes 1572872 | tf_op jit(solution)/shard_map/ppermute | solution.py:466
  120.1 43.4 %collective-permute-start.16 = (bf16[1024,256]{1,0:T(8,128)(2,1)}, bf16[1024,256]{1,0:T(8,128)(2,1)}, u32[]{:S(2)}, u32[]{:S(2)}) collective-permute-start(bf16[1024,256]{1,0:T(8,128)(2,1)} %get-tuple-element.96), channel_id=1, source_target_pairs={{16,0},{17,1},{18,2},{19,3},{20,4},{21,5},{22,6},{23,7}} | collective-permute-start | bytes 1572872 | tf_op jit(solution)/shard_map/ppermute | solution.py:466
  121.4 32.2 %all-to-all-start.2 = ((bf16[8,256,128]{2,1,0:T(8,128)(2,1)}), bf16[8,256,128]{2,1,0:T(8,128)(2,1)S(1)}, u32[]{:S(2)}, u32[]{:S(2)}) async-start(bf16[8,256,128]{2,1,0:T(8,128)(2,1)} %get-tuple-element.98), calls=%async_computation.2 | async-start | bytes 1048576 | tf_op jit(solution)/shard_map/all_to_all | solution.py:66
  125.3 1.0 copy-start.1
  126.4 1.0 copy-start.3
  163.5 9.8 %copy-start.6 = (bf16[1024,256]{1,0:T(8,128)(2,1)S(1)}, bf16[1024,256]{1,0:T(8,128)(2,1)}, u32[]{:S(2)}) copy-start(bf16[1024,256]{1,0:T(8,128)(2,1)} %get-tuple-element.100) | copy-start | bytes 1572868
  169.0 44.0 %all-to-all-start.3 = ((bf16[8,256,256]{2,1,0:T(8,128)(2,1)}), bf16[8,256,256]{2,1,0:T(8,128)(2,1)}, u32[]{:S(2)}, u32[]{:S(2)}) async-start(bf16[8,256,256]{2,1,0:T(8,128)(2,1)} %get-tuple-element.107), calls=%async_computation.3 | async-start | bytes 2097152 | tf_op jit(solution)/shard_map/all_to_all | solution.py:66
  173.3 26.1 %collective-permute-start.17 = (bf16[1024,256]{1,0:T(8,128)(2,1)S(1)}, bf16[1024,256]{1,0:T(8,128)(2,1)S(1)}, u32[]{:S(2)}, u32[]{:S(2)}) collective-permute-start(bf16[1024,256]{1,0:T(8,128)(2,1)S(1)} %copy-done.6), channel_id=1, source_target_pairs={{0,4},{4,0},{1,5},{5,1},{2,6},{6,2},{3,7},{7,3},{8,12},{12,8},{9,1... | collective-permute-start | bytes 1572872 | tf_op jit(solution)/shard_map/ppermute | solution.py:51
  175.2 35.0 %collective-permute-start.18 = (bf16[1024,256]{1,0:T(8,128)(2,1)}, bf16[1024,256]{1,0:T(8,128)(2,1)S(1)}, u32[]{:S(2)}, u32[]{:S(2)}) collective-permute-start(bf16[1024,256]{1,0:T(8,128)(2,1)} %get-tuple-element.103), channel_id=1, source_target_pairs={{0,4},{4,0},{1,5},{5,1},{2,6},{6,2},{3,7},{7,3},{8,12},{12,8},{9,1... | collective-permute-start | bytes 1572872 | tf_op jit(solution)/shard_map/ppermute | solution.py:51

commit v15 on v13

--- a/solution.py
+++ b/solution.py
@@ -172,7 +172,7 @@
     a_low[...] = slab[...].astype(LOW)
 
 
-def spread_hop_kernel(ids, pair, e1, got, m_ref, near):
+def spread_hop_kernel(ids, pair, e1, got, unused, m_ref, near):
     part = got.shape[1]
     rows = 2 * part
     m = mm(pair[...], got[...]).astype(LOW)
@@ -289,7 +289,7 @@
     now[...] = (mm(pair[...], got[...]) + own[...].astype(WIDE)).astype(LOW)
 
 
-def hop_start_kernel(chunk, ids, pair, got_hop, own_hop, e0, got, offset, unused, wave, p, own, keep, sem):
+def hop_start_kernel(chunk, ids, pair, got_hop, own_hop, e0, got, offset, wave, p, own, keep, sem):
     start_kernel(chunk, ids, e0, got, offset, p, own, keep, sem)
 
     @pl.when(ids[3] == 3)
@@ -436,21 +436,20 @@
     wave1 = down(own0, 3)
     (m,) = order.call(spread_kernel, [in_hbm(e0), l_low, l_got], [hbm(8, rows, part)], 8)
     m = exchange(m)
+    wave2, p1, own1 = order.call(
+        functools.partial(hop_start_kernel, 1), [pair, wave1, in_hbm(own0), in_hbm(e0), g_got[1], offset],
+        [hbm(size_d, width), hbm(size_d, width, dtype=WIDE), hbm(size_d, width)], 16,
+        far_in=(5,), scratch=[keep, pltpu.SemaphoreType.DMA(())],
+    )
+    wave2 = down(wave2, 3, 2)
     prod, slab, a_low = order.call(
         spread_start_kernel, [in_hbm(e0), m, spread, l_got, g_got[1]],
         [hbm(rows, size_d, dtype=WIDE), hbm(size_d, part, dtype=WIDE), hbm(size_d, part)], 12,
         far_in=(4,), scratch=[slab_rows],
     )
     l_next = lax.ppermute(a_low, "z", level)
-    wave2, p1, own1 = order.call(
-        functools.partial(hop_start_kernel, 1), [pair, wave1, in_hbm(own0), in_hbm(e0), g_got[1], offset, quarters],
-        [hbm(size_d, width), hbm(size_d, width, dtype=WIDE), hbm(size_d, width)], 16,
-        far_in=(5, 6), scratch=[keep, pltpu.SemaphoreType.DMA(())],
-    )
-    wave2 = down(wave2, 3, 2)
-
     m, near = order.call(
-        spread_hop_kernel, [pair, in_hbm(e1), l_next], [hbm(size_d, part), hbm(8, rows, part)], 10
+        spread_hop_kernel, [pair, in_hbm(e1), l_next, quarters], [hbm(size_d, part), hbm(8, rows, part)], 10, far_in=(3,)
     )
     m = exchange(m.reshape(8, part, part))
     quarters, near = tied((quarters, near))

time: 184 us -> 197 us (1.071)
  waiting for transfers between devices: 64.9 us -> 79.1 us
    ppermute x4, waiting for transfers between devices: 15.3 us -> 29.1 us  [down(): lax.ppermute(value, 'z', [(source, source - 1) for source in sources])]
    ppermute x1, waiting for transfers between devices: 0.01 us -> 8.31 us  [suffix(): l_next = lax.ppermute(a_low, 'z', level)]
    all_to_all x4, waiting for transfers between devices: 12 us -> 3.83 us  [exchange(): return lax.all_to_all(blocks, GROUP, 0, 0)]
  transfers between devices with their start and end apart: 23 -> 23, of which waited for: 12 -> 13; matrix products, arithmetic and copies ran while one was open for 3% -> 2% of each run, Pallas kernels for 33% -> 31%
where the time goes in v15:
time: 197 us; the launch traced here: 195 us
  waiting for transfers between devices  79.1 us (40%)
  Pallas kernels  66.6 us (34%)
  starting transfers between devices  41.6 us (21%)
  local copies, waits for them, and re-layouts  3.71 us (2%)
  other arithmetic  2.85 us (1%)
    pallas_call x15, Pallas kernels, call(): pl.pallas_call(body, in_specs=[SMEM, ANY] + [ANY if i in far_in else VMEM...  66.6 us
    ppermute x11, waiting for transfers between devices, swap(): return lax.ppermute(value, axis, [(0, 1), (1, 0)])  30.7 us
    ppermute x4, waiting for transfers between devices, down(): lax.ppermute(value, 'z', [(source, source - 1) for source in sources])  29.1 us
    all_to_all x4, starting transfers between devices, exchange(): return lax.all_to_all(blocks, GROUP, 0, 0)  15.6 us
    ppermute x11, starting transfers between devices, swap(): return lax.ppermute(value, axis, [(0, 1), (1, 0)])  11.5 us
    ppermute x1, waiting for transfers between devices, suffix(): l_next = lax.ppermute(a_low, 'z', level)  8.31 us
    ppermute x4, starting transfers between devices, down(): lax.ppermute(value, 'z', [(source, source - 1) for source in sources])  7.67 us
    ppermute x1, waiting for transfers between devices, suffix(): lax.ppermute(far_slab, 'z', [(2, 1)])  7.21 us
  transfers between devices with their start and end apart: 23, of which 13 were waited for; matrix products, arithmetic and copies ran while one was open for 2% of the time, Pallas kernels for 31%

profile of v15, /device:TPU:16, one launch (start us, length us, event | category | flops | bytes accessed | tf_op | source)
XLA Modules:
  0.0 195.0 jit_solution(13296901769846712805)
XLA Ops:
  0.6 1.3 convert_bitcast_fusion
  1.9 1.6 collective-permute-start
  3.5 1.5 collective-permute-start.1
  5.0 1.3 convert_element_type.25
  6.3 2.6 %fusion.1 = (bf16[1024,256]{1,0:T(8,128)(2,1)}, bf16[1024,256]{1,0:T(8,128)(2,1)}) fusion(f32[1,1024,1024]{2,1,0:T(8,128)} %param.5, s32[]{:T(128)S(6)} %select_n.11, s32[]{:T(128)S(6)} %select_n.10), kind=kLoop, calls=%fused_computation.4 | loop fusion | bytes 2097160 | tf_op jit(solution)/shard_map/convert_element_type | solution.py:386
  9.0 6.7 %collective-permute-done = bf16[256,1024]{1,0:T(8,128)(2,1)S(1)} collective-permute-done((bf16[256,1024]{1,0:T(8,128)(2,1)S(1)}, bf16[256,1024]{1,0:T(8,128)(2,1)S(1)}, u32[]{:S(2)}, u32[]{:S(2)}) %collective-permute-start) | collective-permute-done | bytes 524320 | tf_op jit(solution)/shard_map/ppermute | solution.py:51
  15.7 1.2 collective-permute-done.1
  17.1 1.6 collective-permute-start.3
  19.2 7.8 %collective-permute-done.2.refs_2_.refs_3_ = bf16[128,1024]{1,0:T(8,128)(2,1)S(1)} collective-permute-done((bf16[128,1024]{1,0:T(8,128)(2,1)S(1)}, bf16[128,1024]{1,0:T(8,128)(2,1)S(1)}, u32[]{:S(2)}, u32[]{:S(2)}) %collective-permute-start.2) | collective-permute-done | bytes 262176 | tf_op jit(solution)/shard_map/ppermute | solution.py:51
  27.0 4.4 %collective-permute-done.3.refs_1_ = bf16[256,1024]{1,0:T(8,128)(2,1)S(1)} collective-permute-done((bf16[256,1024]{1,0:T(8,128)(2,1)S(1)}, bf16[256,1024]{1,0:T(8,128)(2,1)S(1)}, u32[]{:S(2)}, u32[]{:S(2)}) %collective-permute-start.3) | collective-permute-done | bytes 524320 | tf_op jit(solution)/shard_map/ppermute | solution.py:51
  32.0 1.4 collective-permute-done.5.refs_3_
  33.5 6.1 %shard_map.58 = (bf16[1024,1024]{1,0:T(8,128)(2,1)}, bf16[1024,1024]{1,0:T(8,128)(2,1)}, bf16[1024,1024]{1,0:T(8,128)(2,1)S(1)}, bf16[512,1024]{1,0:T(8,128)(2,1)}, s32[8,128]{1,0:T(8,128)S(1)}) custom-call(s32[4]{0:T(128)S(1)} %pad_add_fusion.ids, s32[8,128]{1,0:T(8,128)S(1)} %broadcast_in_dim.12.token, ...), custom_call_target="tpu_custom_call", output_to_operand_aliasing={{4}: (1, {})} | custom-call | flops 1 | bytes 1 | tf_op jit(solution)/shard_map/pallas_call | solution.py:93
  39.6 1.3 collective-permute-start.10
  40.9 5.0 %collective-permute-done.6.refs_1_ = bf16[1024,256]{1,0:T(8,128)(2,1)S(1)} collective-permute-done((bf16[1024,256]{1,0:T(8,128)(2,1)}, bf16[1024,256]{1,0:T(8,128)(2,1)S(1)}, u32[]{:S(2)}, u32[]{:S(2)}) %collective-permute-start.6) | collective-permute-done | bytes 524320 | tf_op jit(solution)/shard_map/ppermute | solution.py:51
  46.5 4.2 %shard_map.59 = (f32[1024,256]{1,0:T(8,128)}, bf16[1024,256]{1,0:T(8,128)(2,1)}, s32[8,128]{1,0:T(8,128)S(1)}) custom-call(s32[4]{0:T(128)S(1)} %pad_add_fusion.ids, s32[8,128]{1,0:T(8,128)S(1)} %get-tuple-element.58.token, bf16[1024,1024]{1,0:T(8,128)(2,1)} %get-tuple-element.59.refs_0_.refs_3_, ...), custom_call_target="tpu_custom_call", output_to_operand_aliasing={{2}: (1, {})} | custom-call | flops 1 | bytes 1 | tf_op jit(solution)/shard_map/pallas_call | solution.py:93
  50.7 1.3 collective-permute-start.7
  52.1 3.1 %shard_map.60 = (bf16[8,256,128]{2,1,0:T(8,128)(2,1)}, s32[8,128]{1,0:T(8,128)S(1)}) custom-call(s32[4]{0:T(128)S(1)} %pad_add_fusion.ids, s32[8,128]{1,0:T(8,128)S(1)} %get-tuple-element.62.token, bf16[1024,1024]{1,0:T(8,128)(2,1)} %get-tuple-element.59.refs_0_.refs_3_, ...), custom_call_target="tpu_custom_call", output_to_operand_aliasing={{1}: (1, {})} | custom-call | flops 1 | bytes 1 | tf_op jit(solution)/shard_map/pallas_call | solution.py:93
  55.3 4.3 %all-to-all-start = ((bf16[8,256,128]{2,1,0:T(8,128)(2,1)}), bf16[8,256,128]{2,1,0:T(8,128)(2,1)}, u32[]{:S(2)}, u32[]{:S(2)}) async-start(bf16[8,256,128]{2,1,0:T(8,128)(2,1)} %get-tuple-element.69), calls=%async_computation | async-start | bytes 1048576 | tf_op jit(solution)/shard_map/all_to_all | solution.py:66
  59.8 18.3 %collective-permute-done.7.refs_1_.refs_3_ = bf16[1024,256]{1,0:T(8,128)(2,1)S(1)} collective-permute-done((bf16[1024,256]{1,0:T(8,128)(2,1)}, bf16[1024,256]{1,0:T(8,128)(2,1)S(1)}, u32[]{:S(2)}, u32[]{:S(2)}) %collective-permute-start.7) | collective-permute-done | bytes 524320 | tf_op jit(solution)/shard_map/ppermute | solution.py:411
  78.2 5.4 %shard_map.61 = (bf16[1024,256]{1,0:T(8,128)(2,1)}, f32[1024,256]{1,0:T(8,128)}, bf16[1024,256]{1,0:T(8,128)(2,1)}, s32[8,128]{1,0:T(8,128)S(1)}) custom-call(s32[4]{0:T(128)S(1)} %pad_add_fusion.ids, s32[8,128]{1,0:T(8,128)S(1)} %get-tuple-element.64.token, bf16[1024,1024]{1,0:T(8,128)(2,1)S(1)} %get-tuple-element.65.refs_0_, ...), custom_call_target="tpu_custom_call", output_to_operand_aliasing={{3}: (1, {})} | custom-call | flops 1 | bytes 1 | tf_op jit(solution)/shard_map/pallas_call | solution.py:93
  83.6 4.2 %shard_map.62 = (f32[256,1024]{1,0:T(8,128)}, f32[1024,128]{1,0:T(8,128)}, bf16[1024,128]{1,0:T(8,128)(2,1)}, s32[8,128]{1,0:T(8,128)S(1)}) custom-call(s32[4]{0:T(128)S(1)} %pad_add_fusion.ids, s32[8,128]{1,0:T(8,128)S(1)} %get-tuple-element.68.token, bf16[1024,1024]{1,0:T(8,128)(2,1)} %get-tuple-element.59.refs_0_.refs_3_, ...), custom_call_target="tpu_custom_call", output_to_operand_aliasing={{3}: (1, {})} | custom-call | flops 1 | bytes 1 | tf_op jit(solution)/shard_map/pallas_call | solution.py:93
  87.8 1.4 collective-permute-start.9
  89.2 8.3 %collective-permute-done.9.refs_2_ = bf16[1024,128]{1,0:T(8,128)(2,1)S(1)} collective-permute-done((bf16[1024,128]{1,0:T(8,128)(2,1)}, bf16[1024,128]{1,0:T(8,128)(2,1)S(1)}, u32[]{:S(2)}, u32[]{:S(2)}) %collective-permute-start.9) | collective-permute-done | bytes 262176 | tf_op jit(solution)/shard_map/ppermute | solution.py:450
  97.6 3.7 %shard_map.63 = (bf16[1024,128]{1,0:T(8,128)(2,1)}, bf16[8,256,128]{2,1,0:T(8,128)(2,1)}, s32[8,128]{1,0:T(8,128)S(1)}) custom-call(s32[4]{0:T(128)S(1)} %pad_add_fusion.ids, s32[8,128]{1,0:T(8,128)S(1)} %get-tuple-element.70.token, bf16[1024,1024]{1,0:T(8,128)(2,1)S(1)} %get-tuple-element.65.refs_0_, ...), custom_call_target="tpu_custom_call", output_to_operand_aliasing={{2}: (1, {})} | custom-call | flops 1 | bytes 1 | tf_op jit(solution)/shard_map/pallas_call | solution.py:93
  101.3 1.9 collective-permute-start.11
  103.2 3.5 %all-to-all-start.1 = ((bf16[8,128,128]{2,1,0:T(8,128)(2,1)}), bf16[8,128,128]{2,1,0:T(8,128)(2,1)S(1)}, u32[]{:S(2)}, u32[]{:S(2)}) async-start(bf16[8,128,128]{2,1,0:T(8,128)(2,1)} %bitcast.26), calls=%async_computation.1 | async-start | bytes 524288 | tf_op jit(solution)/shard_map/all_to_all | solution.py:66
  106.7 10.8 %collective-permute-done.11.refs_1_.refs_4_.refs_3_ = bf16[1024,256]{1,0:T(8,128)(2,1)S(1)} collective-permute-done((bf16[1024,256]{1,0:T(8,128)(2,1)S(1)}, bf16[1024,256]{1,0:T(8,128)(2,1)S(1)}, u32[]{:S(2)}, u32[]{:S(2)}) %collective-permute-start.11) | collective-permute-done | bytes 524320 | tf_op jit(solution)/shard_map/ppermute | solution.py:411
  117.5 2.8 %shard_map.64 = (bf16[1024,256]{1,0:T(8,128)(2,1)}, s32[8,128]{1,0:T(8,128)S(1)}) custom-call(s32[4]{0:T(128)S(1)} %pad_add_fusion.ids, s32[8,128]{1,0:T(8,128)S(1)} %get-tuple-element.74.token, bf16[1024,1024]{1,0:T(8,128)(2,1)S(1)} %get-tuple-element.65.refs_0_, ...), custom_call_target="tpu_custom_call", output_to_operand_aliasing={{1}: (1, {})} | custom-call | flops 1 | bytes 1 | tf_op jit(solution)/shard_map/pallas_call | solution.py:93
  120.3 3.0 %collective-permute-start.13 = (bf16[1024,256]{1,0:T(8,128)(2,1)}, bf16[1024,256]{1,0:T(8,128)(2,1)}, u32[]{:S(2)}, u32[]{:S(2)}) collective-permute-start(bf16[1024,256]{1,0:T(8,128)(2,1)} %get-tuple-element.84), channel_id=1, source_target_pairs={{16,8},{8,0},{17,9},{9,1},{18,10},{10,2},{19,11},{11,3},{20,12},{1... | collective-permute-start | bytes 1572872 | tf_op jit(solution)/shard_map/ppermute | solution.py:411
  123.3 5.2 %shard_map.65 = (bf16[1024,1024]{1,0:T(8,128)(2,1)}, bf16[1024,256]{1,0:T(8,128)(2,1)}, s32[8,128]{1,0:T(8,128)S(1)}) custom-call(s32[4]{0:T(128)S(1)} %pad_add_fusion.ids, s32[8,128]{1,0:T(8,128)S(1)} %get-tuple-element.77.token, bf16[1024,1024]{1,0:T(8,128)(2,1)S(1)} %get-tuple-element.65.refs_0_, ...), custom_call_target="tpu_custom_call", output_to_operand_aliasing={{2}: (1, {})} | custom-call | flops 1 | bytes 1 | tf_op jit(solution)/shard_map/pallas_call | solution.py:93
  128.6 2.1 %collective-permute-start.15 = (bf16[1024,256]{1,0:T(8,128)(2,1)}, bf16[1024,256]{1,0:T(8,128)(2,1)}, u32[]{:S(2)}, u32[]{:S(2)}) collective-permute-start(bf16[1024,256]{1,0:T(8,128)(2,1)} %get-tuple-element.88), channel_id=1, source_target_pairs={{16,0},{17,1},{18,2},{19,3},{20,4},{21,5},{22,6},{23,7}} | collective-permute-start | bytes 1572872 | tf_op jit(solution)/shard_map/ppermute | solution.py:463
  130.7 2.1 %collective-permute-start.14 = (bf16[1024,256]{1,0:T(8,128)(2,1)}, bf16[1024,256]{1,0:T(8,128)(2,1)}, u32[]{:S(2)}, u32[]{:S(2)}) collective-permute-start(bf16[1024,256]{1,0:T(8,128)(2,1)} %get-tuple-element.88), channel_id=1, source_target_pairs={{16,8},{17,9},{18,10},{19,11},{20,12},{21,13},{22,14},{23,15}} | collective-permute-start | bytes 1572872 | tf_op jit(solution)/shard_map/ppermute | solution.py:463
  132.8 3.5 %all-to-all-start.2 = ((bf16[8,256,128]{2,1,0:T(8,128)(2,1)}), bf16[8,256,128]{2,1,0:T(8,128)(2,1)S(1)}, u32[]{:S(2)}, u32[]{:S(2)}) async-start(bf16[8,256,128]{2,1,0:T(8,128)(2,1)} %get-tuple-element.90), calls=%async_computation.2 | async-start | bytes 1048576 | tf_op jit(solution)/shard_map/all_to_all | solution.py:66
  136.3 1.0 copy-done.1
  137.3 5.3 %shard_map.66 = (f32[1024,1024]{1,0:T(8,128)}, bf16[1024,256]{1,0:T(8,128)(2,1)}, s32[8,128]{1,0:T(8,128)S(1)}) custom-call(s32[4]{0:T(128)S(1)} %pad_add_fusion.ids, s32[8,128]{1,0:T(8,128)S(1)} %get-tuple-element.82.token, bf16[1024,1024]{1,0:T(8,128)(2,1)S(1)} %get-tuple-element.65.refs_0_, ...), custom_call_target="tpu_custom_call", output_to_operand_aliasing={{2}: (1, {})} | custom-call | flops 1 | bytes 1 | tf_op jit(solution)/shard_map/pallas_call | solution.py:93
  142.6 2.6 %collective-permute-start.16 = (bf16[1024,256]{1,0:T(8,128)(2,1)}, bf16[1024,256]{1,0:T(8,128)(2,1)}, u32[]{:S(2)}, u32[]{:S(2)}) collective-permute-start(bf16[1024,256]{1,0:T(8,128)(2,1)} %get-tuple-element.92), channel_id=1, source_target_pairs={{0,4},{4,0},{1,5},{5,1},{2,6},{6,2},{3,7},{7,3},{8,12},{12,8},{9,1... | collective-permute-start | bytes 1572872 | tf_op jit(solution)/shard_map/ppermute | solution.py:51
  145.2 2.7 %shard_map.67 = (bf16[1024,256]{1,0:T(8,128)(2,1)}, s32[8,128]{1,0:T(8,128)S(1)}) custom-call(s32[4]{0:T(128)S(1)} %pad_add_fusion.ids, s32[8,128]{1,0:T(8,128)S(1)} %get-tuple-element.85.token, bf16[1024,1024]{1,0:T(8,128)(2,1)S(1)} %get-tuple-element.65.refs_0_, ...), custom_call_target="tpu_custom_call", output_to_operand_aliasing={{1}: (1, {})} | custom-call | flops 1 | bytes 1 | tf_op jit(solution)/shard_map/pallas_call | solution.py:93
  147.9 1.5 collective-permute-start.17
  149.3 7.2 %collective-permute-done.14.refs_3_ = bf16[1024,256]{1,0:T(8,128)(2,1)} collective-permute-done((bf16[1024,256]{1,0:T(8,128)(2,1)}, bf16[1024,256]{1,0:T(8,128)(2,1)}, u32[]{:S(2)}, u32[]{:S(2)}) %collective-permute-start.14) | collective-permute-done | bytes 524320 | tf_op jit(solution)/shard_map/ppermute | solution.py:463
  156.5 5.5 %shard_map.68 = (bf16[8,256,256]{2,1,0:T(8,128)(2,1)}, s32[8,128]{1,0:T(8,128)S(1)}) custom-call(s32[4]{0:T(128)S(1)} %pad_add_fusion.ids, s32[8,128]{1,0:T(8,128)S(1)} %get-tuple-element.86.token, bf16[1024,1024]{1,0:T(8,128)(2,1)S(1)} %get-tuple-element.65.refs_0_, bf16[1024,1024]{1,0:T(8,128)(2,1)} %get-tuple-element.71.refs_1_, ...), custom_call_target="tpu_custom_call", output_to_operand_aliasing={{1}: (1, {})} | custom-call | flops 1 | bytes 1 | tf_op jit(solution)/shard_map/pallas_call | solution.py:93
  162.1 4.3 %all-to-all-start.3 = ((bf16[8,256,256]{2,1,0:T(8,128)(2,1)}), bf16[8,256,256]{2,1,0:T(8,128)(2,1)}, u32[]{:S(2)}, u32[]{:S(2)}) async-start(bf16[8,256,256]{2,1,0:T(8,128)(2,1)} %get-tuple-element.100), calls=%async_computation.3 | async-start | bytes 2097152 | tf_op jit(solution)/shard_map/all_to_all | solution.py:66
  166.3 3.4 %shard_map.69 = (f32[1024,1024]{1,0:T(8,128)}, s32[8,128]{1,0:T(8,128)S(1)}) custom-call(s32[4]{0:T(128)S(1)} %pad_add_fusion.ids, s32[8,128]{1,0:T(8,128)S(1)} %get-tuple-element.91.token, bf16[1024,256]{1,0:T(8,128)(2,1)} %collective-permute-done.16.refs_0_, f32[1024,1024]{1,0:T(8,128)} %bitcast.22, ...), custom_call_target="tpu_custom_call", output_to_operand_aliasing={{1}: (1, {}), {0}: (4, {})} | custom-call | flops 1 | bytes 1 | tf_op jit(solution)/shard_map/pallas_call | solution.py:93
  169.7 5.1 %shard_map.70 = (f32[1024,1024]{1,0:T(8,128)}, bf16[1024,256]{1,0:T(8,128)(2,1)}, s32[8,128]{1,0:T(8,128)S(1)}) custom-call(s32[4]{0:T(128)S(1)} %pad_add_fusion.ids, s32[8,128]{1,0:T(8,128)S(1)} %get-tuple-element.94.token, bf16[1024,1024]{1,0:T(8,128)(2,1)S(1)} %get-tuple-element.65.refs_0_, ...), custom_call_target="tpu_custom_call", output_to_operand_aliasing={{2}: (1, {}), {0}: (9, {})} | custom-call | flops 1 | bytes 1 | tf_op jit(solution)/shard_map/pallas_call | solution.py:93
  174.9 2.6 %collective-permute-start.18 = (bf16[1024,256]{1,0:T(8,128)(2,1)}, bf16[1024,256]{1,0:T(8,128)(2,1)S(1)}, u32[]{:S(2)}, u32[]{:S(2)}) collective-permute-start(bf16[1024,256]{1,0:T(8,128)(2,1)} %get-tuple-element.104), channel_id=1, source_target_pairs={{0,4},{4,0},{1,5},{5,1},{2,6},{6,2},{3,7},{7,3},{8,12},{12,8},{9,1... | collective-permute-start | bytes 1572872 | tf_op jit(solution)/shard_map/ppermute | solution.py:51
  177.4 3.8 %all-to-all-done.3.refs_6_ = bf16[8,256,256]{2,1,0:T(8,128)(2,1)} async-done(((bf16[8,256,256]{2,1,0:T(8,128)(2,1)}), bf16[8,256,256]{2,1,0:T(8,128)(2,1)}, u32[]{:S(2)}, u32[]{:S(2)}) %all-to-all-start.3) | async-done | bytes 1048608 | tf_op jit(solution)/shard_map/all_to_all | solution.py:66
  181.3 6.9 %shard_map.71 = (f32[256,1024]{1,0:T(8,128)}, f32[256,1024]{1,0:T(8,128)}, s32[8,128]{1,0:T(8,128)S(1)}) custom-call(s32[4]{0:T(128)S(1)} %pad_add_fusion.ids, s32[8,128]{1,0:T(8,128)S(1)} %get-tuple-element.98.token, bf16[1024,1024]{1,0:T(8,128)(2,1)S(1)} %get-tuple-element.65.refs_0_, ...), custom_call_target="tpu_custom_call", output_to_operand_aliasing={{2}: (1, {})} | custom-call | flops 1 | bytes 1 | tf_op jit(solution)/shard_map/pallas_call | solution.py:93
  188.1 3.8 %collective-permute-done.18.refs_0_ = bf16[1024,256]{1,0:T(8,128)(2,1)S(1)} collective-permute-done((bf16[1024,256]{1,0:T(8,128)(2,1)}, bf16[1024,256]{1,0:T(8,128)(2,1)S(1)}, u32[]{:S(2)}, u32[]{:S(2)}) %collective-permute-start.18) | collective-permute-done | bytes 524320 | tf_op jit(solution)/shard_map/ppermute | solution.py:51
  192.0 2.9 %shard_map.72 = (f32[1024,1024]{1,0:T(8,128)}, s32[8,128]{1,0:T(8,128)S(1)}) custom-call(s32[4]{0:T(128)S(1)} %pad_add_fusion.ids, s32[8,128]{1,0:T(8,128)S(1)} %get-tuple-element.103.token, bf16[1024,256]{1,0:T(8,128)(2,1)S(1)} %collective-permute-done.18.refs_0_, f32[1024,1024]{1,0:T(8,128)} %bitcast.24, ...), custom_call_target="tpu_custom_call", output_to_operand_aliasing={{1}: (1, {}), {0}: (4, {})} | custom-call | flops 1 | bytes 1 | tf_op jit(solution)/shard_map/pallas_call | solution.py:93
  (33 shorter events, 2.3 us)
Async XLA Ops:
  1.9 13.7 %collective-permute-start = (bf16[256,1024]{1,0:T(8,128)(2,1)S(1)}, bf16[256,1024]{1,0:T(8,128)(2,1)S(1)}, u32[]{:S(2)}, u32[]{:S(2)}) collective-permute-start(bf16[256,1024]{1,0:T(8,128)(2,1)S(1)} %convert_bitcast_fusion), channel_id=1, source_target_pairs={{0,4},{4,0},{1,5},{5,1},{2,6},{6,2},{3,7},{7,3},{8,12},{12,8},{9,1... | collective-permute-start | bytes 1572872 | tf_op jit(solution)/shard_map/ppermute | solution.py:51
  3.5 13.4 %collective-permute-start.1 = (bf16[256,1024]{1,0:T(8,128)(2,1)S(1)}, bf16[256,1024]{1,0:T(8,128)(2,1)S(1)}, u32[]{:S(2)}, u32[]{:S(2)}) collective-permute-start(bf16[256,1024]{1,0:T(8,128)(2,1)S(1)} %convert_bitcast_fusion), channel_id=1, source_target_pairs={{0,2},{2,0},{1,3},{3,1},{4,6},{6,4},{5,7},{7,5},{8,10},{10,8},{9,1... | collective-permute-start | bytes 1572872 | tf_op jit(solution)/shard_map/ppermute | solution.py:51
  17.0 16.5 %copy-start.3 = (bf16[768,1024]{1,0:T(8,128)(2,1)}, bf16[768,1024]{1,0:T(8,128)(2,1)S(1)}, u32[]{:S(2)}) copy-start(bf16[768,1024]{1,0:T(8,128)(2,1)S(1)} %pad_maximum_fusion.refs_0_) | copy-start | bytes 4718596
  17.0 16.5 %collective-permute-start.4 = (bf16[768,1024]{1,0:T(8,128)(2,1)S(1)}, bf16[768,1024]{1,0:T(8,128)(2,1)}, u32[]{:S(2)}, u32[]{:S(2)}) collective-permute-start(bf16[768,1024]{1,0:T(8,128)(2,1)S(1)} %pad_maximum_fusion.refs_0_), channel_id=1, source_target_pairs={{0,1},{1,0},{2,3},{3,2},{4,5},{5,4},{6,7},{7,6},{8,9},{9,8},{10,11... | collective-permute-start | bytes 4718600 | tf_op jit(solution)/shard_map/ppermute | solution.py:51
  17.1 14.3 %collective-permute-start.3 = (bf16[256,1024]{1,0:T(8,128)(2,1)S(1)}, bf16[256,1024]{1,0:T(8,128)(2,1)S(1)}, u32[]{:S(2)}, u32[]{:S(2)}) collective-permute-start(bf16[256,1024]{1,0:T(8,128)(2,1)S(1)} %collective-permute-done), channel_id=1, source_target_pairs={{0,2},{2,0},{1,3},{3,1},{4,6},{6,4},{5,7},{7,5},{8,10},{10,8},{9,1... | collective-permute-start | bytes 1572872 | tf_op jit(solution)/shard_map/ppermute | solution.py:51
  18.7 8.4 %collective-permute-start.2 = (bf16[128,1024]{1,0:T(8,128)(2,1)S(1)}, bf16[128,1024]{1,0:T(8,128)(2,1)S(1)}, u32[]{:S(2)}, u32[]{:S(2)}) collective-permute-start(bf16[128,1024]{1,0:T(8,128)(2,1)S(1)} %dynamic-slice_bitcast_fusion), channel_id=1, source_target_pairs={{0,4},{4,0},{1,5},{5,1},{2,6},{6,2},{3,7},{7,3},{8,12},{12,8},{9,1... | collective-permute-start | bytes 786440 | tf_op jit(solution)/shard_map/ppermute | solution.py:51
  31.4 2.1 %copy-start.4 = (bf16[256,1024]{1,0:T(8,128)(2,1)}, bf16[256,1024]{1,0:T(8,128)(2,1)S(1)}, u32[]{:S(2)}) copy-start(bf16[256,1024]{1,0:T(8,128)(2,1)S(1)} %collective-permute-done.3.refs_1_) | copy-start | bytes 1572868
  31.4 2.0 %collective-permute-start.5 = (bf16[256,1024]{1,0:T(8,128)(2,1)S(1)}, bf16[256,1024]{1,0:T(8,128)(2,1)}, u32[]{:S(2)}, u32[]{:S(2)}) collective-permute-start(bf16[256,1024]{1,0:T(8,128)(2,1)S(1)} %collective-permute-done.3.refs_1_), channel_id=1, source_target_pairs={{0,1},{1,0},{2,3},{3,2},{4,5},{5,4},{6,7},{7,6},{8,9},{9,8},{10,11... | collective-permute-start | bytes 1572872 | tf_op jit(solution)/shard_map/ppermute | solution.py:51
  31.4 14.5 %collective-permute-start.6 = (bf16[1024,256]{1,0:T(8,128)(2,1)}, bf16[1024,256]{1,0:T(8,128)(2,1)S(1)}, u32[]{:S(2)}, u32[]{:S(2)}) collective-permute-start(bf16[1024,256]{1,0:T(8,128)(2,1)} %get-tuple-element.60), channel_id=1, source_target_pairs={{0,4},{4,0},{1,5},{5,1},{2,6},{6,2},{3,7},{7,3},{8,12},{12,8},{9,1... | collective-permute-start | bytes 1572872 | tf_op jit(solution)/shard_map/ppermute | solution.py:51
  39.6 57.9 %collective-permute-start.10 = (bf16[512,1024]{1,0:T(8,128)(2,1)}, bf16[512,1024]{1,0:T(8,128)(2,1)}, u32[]{:S(2)}, u32[]{:S(2)}) collective-permute-start(bf16[512,1024]{1,0:T(8,128)(2,1)} %get-tuple-element.73), channel_id=1, source_target_pairs={{24,16},{8,0},{25,17},{9,1},{26,18},{10,2},{27,19},{11,3},{28,20},... | collective-permute-start | bytes 3145736 | tf_op jit(solution)/shard_map/ppermute | solution.py:434
  46.0 13.9 %collective-permute-start.8 = (bf16[1024,256]{1,0:T(8,128)(2,1)}, bf16[1024,256]{1,0:T(8,128)(2,1)S(1)}, u32[]{:S(2)}, u32[]{:S(2)}) collective-permute-start(bf16[1024,256]{1,0:T(8,128)(2,1)} %get-tuple-element.67), channel_id=1, source_target_pairs={{0,4},{4,0},{1,5},{5,1},{2,6},{6,2},{3,7},{7,3},{8,12},{12,8},{9,1... | collective-permute-start | bytes 1572872 | tf_op jit(solution)/shard_map/ppermute | solution.py:51
  46.5 5.5 %copy-start.2 = (f32[1,256,1024]{2,1,0:T(8,128)S(1)}, f32[1,256,1024]{2,1,0:T(8,128)}, u32[]{:S(2)}) copy-start(f32[1,256,1024]{2,1,0:T(8,128)} %refs_5_.1) | copy-start | bytes 3145732
  50.7 27.4 %collective-permute-start.7 = (bf16[1024,256]{1,0:T(8,128)(2,1)}, bf16[1024,256]{1,0:T(8,128)(2,1)S(1)}, u32[]{:S(2)}, u32[]{:S(2)}) collective-permute-start(bf16[1024,256]{1,0:T(8,128)(2,1)} %get-tuple-element.66.refs_2_), channel_id=1, source_target_pairs={{24,16},{25,17},{26,18},{27,19},{28,20},{29,21},{30,22},{31,23}} | collective-permute-start | bytes 1572872 | tf_op jit(solution)/shard_map/ppermute | solution.py:411
  55.3 28.3 %all-to-all-start = ((bf16[8,256,128]{2,1,0:T(8,128)(2,1)}), bf16[8,256,128]{2,1,0:T(8,128)(2,1)}, u32[]{:S(2)}, u32[]{:S(2)}) async-start(bf16[8,256,128]{2,1,0:T(8,128)(2,1)} %get-tuple-element.69), calls=%async_computation | async-start | bytes 1048576 | tf_op jit(solution)/shard_map/all_to_all | solution.py:66
  78.2 5.4 %copy-start = (bf16[1024,256]{1,0:T(8,128)(2,1)}, bf16[1024,256]{1,0:T(8,128)(2,1)S(1)}, u32[]{:S(2)}) copy-start(bf16[1024,256]{1,0:T(8,128)(2,1)S(1)} %collective-permute-done.7.refs_1_.refs_3_) | copy-start | bytes 1572868
  87.8 13.5 %copy-start.5 = (bf16[1024,256]{1,0:T(8,128)(2,1)S(1)}, bf16[1024,256]{1,0:T(8,128)(2,1)}, u32[]{:S(2)}) copy-start(bf16[1024,256]{1,0:T(8,128)(2,1)} %get-tuple-element.75) | copy-start | bytes 1572868
  87.8 9.7 %collective-permute-start.9 = (bf16[1024,128]{1,0:T(8,128)(2,1)}, bf16[1024,128]{1,0:T(8,128)(2,1)S(1)}, u32[]{:S(2)}, u32[]{:S(2)}) collective-permute-start(bf16[1024,128]{1,0:T(8,128)(2,1)} %get-tuple-element.72), channel_id=1, source_target_pairs={{24,16},{8,0},{25,17},{9,1},{26,18},{10,2},{27,19},{11,3},{28,20},... | collective-permute-start | bytes 786440 | tf_op jit(solution)/shard_map/ppermute | solution.py:450
  101.3 22.0 %collective-permute-start.12 = (bf16[512,1024]{1,0:T(8,128)(2,1)}, bf16[512,1024]{1,0:T(8,128)(2,1)}, u32[]{:S(2)}, u32[]{:S(2)}) collective-permute-start(bf16[512,1024]{1,0:T(8,128)(2,1)} %collective-permute-done.10.refs_3_), channel_id=1, source_target_pairs={{0,1},{1,0},{2,3},{3,2},{4,5},{5,4},{6,7},{7,6},{8,9},{9,8},{10,11... | collective-permute-start | bytes 3145736 | tf_op jit(solution)/shard_map/ppermute | solution.py:51
  101.3 16.2 %collective-permute-start.11 = (bf16[1024,256]{1,0:T(8,128)(2,1)S(1)}, bf16[1024,256]{1,0:T(8,128)(2,1)S(1)}, u32[]{:S(2)}, u32[]{:S(2)}) collective-permute-start(bf16[1024,256]{1,0:T(8,128)(2,1)S(1)} %copy-done.5), channel_id=1, source_target_pairs={{24,16},{16,8},{25,17},{17,9},{26,18},{18,10},{27,19},{19,11},{28,... | collective-permute-start | bytes 1572872 | tf_op jit(solution)/shard_map/ppermute | solution.py:411
  103.2 20.1 %all-to-all-start.1 = ((bf16[8,128,128]{2,1,0:T(8,128)(2,1)}), bf16[8,128,128]{2,1,0:T(8,128)(2,1)S(1)}, u32[]{:S(2)}, u32[]{:S(2)}) async-start(bf16[8,128,128]{2,1,0:T(8,128)(2,1)} %bitcast.26), calls=%async_computation.1 | async-start | bytes 524288 | tf_op jit(solution)/shard_map/all_to_all | solution.py:66
  120.3 15.9 %collective-permute-start.13 = (bf16[1024,256]{1,0:T(8,128)(2,1)}, bf16[1024,256]{1,0:T(8,128)(2,1)}, u32[]{:S(2)}, u32[]{:S(2)}) collective-permute-start(bf16[1024,256]{1,0:T(8,128)(2,1)} %get-tuple-element.84), channel_id=1, source_target_pairs={{16,8},{8,0},{17,9},{9,1},{18,10},{10,2},{19,11},{11,3},{20,12},{1... | collective-permute-start | bytes 1572872 | tf_op jit(solution)/shard_map/ppermute | solution.py:411
  128.6 20.8 %collective-permute-start.15 = (bf16[1024,256]{1,0:T(8,128)(2,1)}, bf16[1024,256]{1,0:T(8,128)(2,1)}, u32[]{:S(2)}, u32[]{:S(2)}) collective-permute-start(bf16[1024,256]{1,0:T(8,128)(2,1)} %get-tuple-element.88), channel_id=1, source_target_pairs={{16,0},{17,1},{18,2},{19,3},{20,4},{21,5},{22,6},{23,7}} | collective-permute-start | bytes 1572872 | tf_op jit(solution)/shard_map/ppermute | solution.py:463
  130.7 25.9 %collective-permute-start.14 = (bf16[1024,256]{1,0:T(8,128)(2,1)}, bf16[1024,256]{1,0:T(8,128)(2,1)}, u32[]{:S(2)}, u32[]{:S(2)}) collective-permute-start(bf16[1024,256]{1,0:T(8,128)(2,1)} %get-tuple-element.88), channel_id=1, source_target_pairs={{16,8},{17,9},{18,10},{19,11},{20,12},{21,13},{22,14},{23,15}} | collective-permute-start | bytes 1572872 | tf_op jit(solution)/shard_map/ppermute | solution.py:463
  132.8 16.6 %all-to-all-start.2 = ((bf16[8,256,128]{2,1,0:T(8,128)(2,1)}), bf16[8,256,128]{2,1,0:T(8,128)(2,1)S(1)}, u32[]{:S(2)}, u32[]{:S(2)}) async-start(bf16[8,256,128]{2,1,0:T(8,128)(2,1)} %get-tuple-element.90), calls=%async_computation.2 | async-start | bytes 1048576 | tf_op jit(solution)/shard_map/all_to_all | solution.py:66
  136.3 1.0 copy-start.1
  142.6 23.8 %collective-permute-start.16 = (bf16[1024,256]{1,0:T(8,128)(2,1)}, bf16[1024,256]{1,0:T(8,128)(2,1)}, u32[]{:S(2)}, u32[]{:S(2)}) collective-permute-start(bf16[1024,256]{1,0:T(8,128)(2,1)} %get-tuple-element.92), channel_id=1, source_target_pairs={{0,4},{4,0},{1,5},{5,1},{2,6},{6,2},{3,7},{7,3},{8,12},{12,8},{9,1... | collective-permute-start | bytes 1572872 | tf_op jit(solution)/shard_map/ppermute | solution.py:51
  147.9 21.8 %collective-permute-start.17 = (bf16[1024,256]{1,0:T(8,128)(2,1)}, bf16[1024,256]{1,0:T(8,128)(2,1)}, u32[]{:S(2)}, u32[]{:S(2)}) collective-permute-start(bf16[1024,256]{1,0:T(8,128)(2,1)} %get-tuple-element.96), channel_id=1, source_target_pairs={{8,0},{9,1},{10,2},{11,3},{12,4},{13,5},{14,6},{15,7}} | collective-permute-start | bytes 1572872 | tf_op jit(solution)/shard_map/ppermute | solution.py:411
  162.1 19.2 %all-to-all-start.3 = ((bf16[8,256,256]{2,1,0:T(8,128)(2,1)}), bf16[8,256,256]{2,1,0:T(8,128)(2,1)}, u32[]{:S(2)}, u32[]{:S(2)}) async-start(bf16[8,256,256]{2,1,0:T(8,128)(2,1)} %get-tuple-element.100), calls=%async_computation.3 | async-start | bytes 2097152 | tf_op jit(solution)/shard_map/all_to_all | solution.py:66
  174.9 17.1 %collective-permute-start.18 = (bf16[1024,256]{1,0:T(8,128)(2,1)}, bf16[1024,256]{1,0:T(8,128)(2,1)S(1)}, u32[]{:S(2)}, u32[]{:S(2)}) collective-permute-start(bf16[1024,256]{1,0:T(8,128)(2,1)} %get-tuple-element.104), channel_id=1, source_target_pairs={{0,4},{4,0},{1,5},{5,1},{2,6},{6,2},{3,7},{7,3},{8,12},{12,8},{9,1... | collective-permute-start | bytes 1572872 | tf_op jit(solution)/shard_map/ppermute | solution.py:51

commit v16 on v15

--- a/solution.py
+++ b/solution.py
@@ -172,7 +172,7 @@
     a_low[...] = slab[...].astype(LOW)
 
 
-def spread_hop_kernel(ids, pair, e1, got, unused, m_ref, near):
+def spread_hop_kernel(ids, pair, e1, got, unused, unused_wave, m_ref, near):
     part = got.shape[1]
     rows = 2 * part
     m = mm(pair[...], got[...]).astype(LOW)
@@ -449,7 +449,7 @@
     )
     l_next = lax.ppermute(a_low, "z", level)
     m, near = order.call(
-        spread_hop_kernel, [pair, in_hbm(e1), l_next, quarters], [hbm(size_d, part), hbm(8, rows, part)], 10, far_in=(3,)
+        spread_hop_kernel, [pair, in_hbm(e1), l_next, quarters, wave2], [hbm(size_d, part), hbm(8, rows, part)], 10, far_in=(3, 4)
     )
     m = exchange(m.reshape(8, part, part))
     quarters, near = tied((quarters, near))

time: 197 us -> 191 us (0.970)
  waiting for transfers between devices: 79.1 us -> 72.7 us
    ppermute x4, waiting for transfers between devices: 29.1 us -> 7.01 us  [down(): lax.ppermute(value, 'z', [(source, source - 1) for source in sources])]
    ppermute x1, waiting for transfers between devices: 8.31 us -> 24.4 us  [suffix(): l_next = lax.ppermute(a_low, 'z', level)]
  transfers between devices with their start and end apart: 23 -> 23, of which waited for: 13 -> 11; matrix products, arithmetic and copies ran while one was open for 2% -> 2% of each run, Pallas kernels for 31% -> 32%
where the time goes in v16:
time: 191 us; the launch traced here: 188 us
  waiting for transfers between devices  72.7 us (38%)
  Pallas kernels  66.4 us (35%)
  starting transfers between devices  41.4 us (22%)
  local copies, waits for them, and re-layouts  3.71 us (2%)
  other arithmetic  2.85 us (1%)
    pallas_call x15, Pallas kernels, call(): pl.pallas_call(body, in_specs=[SMEM, ANY] + [ANY if i in far_in else VMEM...  66.4 us
    ppermute x11, waiting for transfers between devices, swap(): return lax.ppermute(value, axis, [(0, 1), (1, 0)])  29.2 us
    ppermute x1, waiting for transfers between devices, suffix(): l_next = lax.ppermute(a_low, 'z', level)  24.4 us
    all_to_all x4, starting transfers between devices, exchange(): return lax.all_to_all(blocks, GROUP, 0, 0)  15.4 us
    ppermute x11, starting transfers between devices, swap(): return lax.ppermute(value, axis, [(0, 1), (1, 0)])  12.5 us
    ppermute x4, waiting for transfers between devices, down(): lax.ppermute(value, 'z', [(source, source - 1) for source in sources])  7.01 us
    ppermute x4, starting transfers between devices, down(): lax.ppermute(value, 'z', [(source, source - 1) for source in sources])  6.75 us
    ppermute x1, waiting for transfers between devices, suffix(): lax.ppermute(far_slab, 'z', [(2, 1)])  6.71 us
  transfers between devices with their start and end apart: 23, of which 11 were waited for; matrix products, arithmetic and copies ran while one was open for 2% of the time, Pallas kernels for 32%

profile of v16, /device:TPU:16, one launch (start us, length us, event | category | flops | bytes accessed | tf_op | source)
XLA Modules:
  0.0 188.1 jit_solution(7538137004263241637)
XLA Ops:
  0.6 1.3 convert_bitcast_fusion
  1.9 1.6 collective-permute-start
  3.5 1.5 collective-permute-start.1
  5.0 1.3 convert_element_type.25
  6.3 2.6 %fusion.1 = (bf16[1024,256]{1,0:T(8,128)(2,1)}, bf16[1024,256]{1,0:T(8,128)(2,1)}) fusion(f32[1,1024,1024]{2,1,0:T(8,128)} %param.5, s32[]{:T(128)S(6)} %select_n.11, s32[]{:T(128)S(6)} %select_n.10), kind=kLoop, calls=%fused_computation.4 | loop fusion | bytes 2097160 | tf_op jit(solution)/shard_map/convert_element_type | solution.py:386
  9.0 6.7 %collective-permute-done = bf16[256,1024]{1,0:T(8,128)(2,1)S(1)} collective-permute-done((bf16[256,1024]{1,0:T(8,128)(2,1)S(1)}, bf16[256,1024]{1,0:T(8,128)(2,1)S(1)}, u32[]{:S(2)}, u32[]{:S(2)}) %collective-permute-start) | collective-permute-done | bytes 524320 | tf_op jit(solution)/shard_map/ppermute | solution.py:51
  15.7 1.2 collective-permute-done.1
  17.1 1.6 collective-permute-start.3
  19.2 1.5 collective-permute-start.6
  20.7 7.1 %collective-permute-done.2.refs_2_.refs_3_ = bf16[128,1024]{1,0:T(8,128)(2,1)S(1)} collective-permute-done((bf16[128,1024]{1,0:T(8,128)(2,1)S(1)}, bf16[128,1024]{1,0:T(8,128)(2,1)S(1)}, u32[]{:S(2)}, u32[]{:S(2)}) %collective-permute-start.2) | collective-permute-done | bytes 262176 | tf_op jit(solution)/shard_map/ppermute | solution.py:51
  27.8 3.7 %collective-permute-done.3.refs_1_ = bf16[256,1024]{1,0:T(8,128)(2,1)} collective-permute-done((bf16[256,1024]{1,0:T(8,128)(2,1)S(1)}, bf16[256,1024]{1,0:T(8,128)(2,1)}, u32[]{:S(2)}, u32[]{:S(2)}) %collective-permute-start.3) | collective-permute-done | bytes 524320 | tf_op jit(solution)/shard_map/ppermute | solution.py:51
  31.6 6.7 %collective-permute-done.6.refs_1_ = bf16[1024,256]{1,0:T(8,128)(2,1)S(1)} collective-permute-done((bf16[1024,256]{1,0:T(8,128)(2,1)}, bf16[1024,256]{1,0:T(8,128)(2,1)S(1)}, u32[]{:S(2)}, u32[]{:S(2)}) %collective-permute-start.6) | collective-permute-done | bytes 524320 | tf_op jit(solution)/shard_map/ppermute | solution.py:51
  38.8 6.1 %shard_map.58 = (bf16[1024,1024]{1,0:T(8,128)(2,1)}, bf16[1024,1024]{1,0:T(8,128)(2,1)}, bf16[1024,1024]{1,0:T(8,128)(2,1)S(1)}, bf16[512,1024]{1,0:T(8,128)(2,1)}, s32[8,128]{1,0:T(8,128)S(1)}) custom-call(s32[4]{0:T(128)S(1)} %pad_add_fusion.ids, s32[8,128]{1,0:T(8,128)S(1)} %broadcast_in_dim.12.token, ...), custom_call_target="tpu_custom_call", output_to_operand_aliasing={{4}: (1, {})} | custom-call | flops 1 | bytes 1 | tf_op jit(solution)/shard_map/pallas_call | solution.py:93
  45.0 4.2 %shard_map.59 = (f32[1024,256]{1,0:T(8,128)}, bf16[1024,256]{1,0:T(8,128)(2,1)}, s32[8,128]{1,0:T(8,128)S(1)}) custom-call(s32[4]{0:T(128)S(1)} %pad_add_fusion.ids, s32[8,128]{1,0:T(8,128)S(1)} %get-tuple-element.58.token, bf16[1024,1024]{1,0:T(8,128)(2,1)} %get-tuple-element.59.refs_0_.refs_3_, ...), custom_call_target="tpu_custom_call", output_to_operand_aliasing={{2}: (1, {})} | custom-call | flops 1 | bytes 1 | tf_op jit(solution)/shard_map/pallas_call | solution.py:93
  49.2 1.3 collective-permute-start.7
  50.5 1.3 collective-permute-start.10
  51.9 3.1 %shard_map.60 = (bf16[8,256,128]{2,1,0:T(8,128)(2,1)}, s32[8,128]{1,0:T(8,128)S(1)}) custom-call(s32[4]{0:T(128)S(1)} %pad_add_fusion.ids, s32[8,128]{1,0:T(8,128)S(1)} %get-tuple-element.62.token, bf16[1024,1024]{1,0:T(8,128)(2,1)} %get-tuple-element.59.refs_0_.refs_3_, ...), custom_call_target="tpu_custom_call", output_to_operand_aliasing={{1}: (1, {})} | custom-call | flops 1 | bytes 1 | tf_op jit(solution)/shard_map/pallas_call | solution.py:93
  55.0 4.2 %all-to-all-start = ((bf16[8,256,128]{2,1,0:T(8,128)(2,1)}), bf16[8,256,128]{2,1,0:T(8,128)(2,1)}, u32[]{:S(2)}, u32[]{:S(2)}) async-start(bf16[8,256,128]{2,1,0:T(8,128)(2,1)} %get-tuple-element.69), calls=%async_computation | async-start | bytes 1048576 | tf_op jit(solution)/shard_map/all_to_all | solution.py:66
  59.2 7.0 %collective-permute-done.7.refs_1_.refs_3_ = bf16[1024,256]{1,0:T(8,128)(2,1)S(1)} collective-permute-done((bf16[1024,256]{1,0:T(8,128)(2,1)}, bf16[1024,256]{1,0:T(8,128)(2,1)S(1)}, u32[]{:S(2)}, u32[]{:S(2)}) %collective-permute-start.7) | collective-permute-done | bytes 524320 | tf_op jit(solution)/shard_map/ppermute | solution.py:411
  66.2 5.4 %shard_map.61 = (bf16[1024,256]{1,0:T(8,128)(2,1)}, f32[1024,256]{1,0:T(8,128)}, bf16[1024,256]{1,0:T(8,128)(2,1)}, s32[8,128]{1,0:T(8,128)S(1)}) custom-call(s32[4]{0:T(128)S(1)} %pad_add_fusion.ids, s32[8,128]{1,0:T(8,128)S(1)} %get-tuple-element.64.token, bf16[1024,1024]{1,0:T(8,128)(2,1)S(1)} %get-tuple-element.65.refs_0_, ...), custom_call_target="tpu_custom_call", output_to_operand_aliasing={{3}: (1, {})} | custom-call | flops 1 | bytes 1 | tf_op jit(solution)/shard_map/pallas_call | solution.py:93
  71.6 1.9 %collective-permute-start.11 = (bf16[1024,256]{1,0:T(8,128)(2,1)}, bf16[1024,256]{1,0:T(8,128)(2,1)S(1)}, u32[]{:S(2)}, u32[]{:S(2)}) collective-permute-start(bf16[1024,256]{1,0:T(8,128)(2,1)} %get-tuple-element.74), channel_id=1, source_target_pairs={{24,16},{16,8},{25,17},{17,9},{26,18},{18,10},{27,19},{19,11},{28,... | collective-permute-start | bytes 1572872 | tf_op jit(solution)/shard_map/ppermute | solution.py:411
  73.6 4.3 %shard_map.62 = (f32[256,1024]{1,0:T(8,128)}, f32[1024,128]{1,0:T(8,128)}, bf16[1024,128]{1,0:T(8,128)(2,1)}, s32[8,128]{1,0:T(8,128)S(1)}) custom-call(s32[4]{0:T(128)S(1)} %pad_add_fusion.ids, s32[8,128]{1,0:T(8,128)S(1)} %get-tuple-element.68.token, bf16[1024,1024]{1,0:T(8,128)(2,1)} %get-tuple-element.59.refs_0_.refs_3_, ...), custom_call_target="tpu_custom_call", output_to_operand_aliasing={{3}: (1, {})} | custom-call | flops 1 | bytes 1 | tf_op jit(solution)/shard_map/pallas_call | solution.py:93
  77.8 1.3 collective-permute-start.9
  79.1 24.4 %collective-permute-done.9.refs_2_ = bf16[1024,128]{1,0:T(8,128)(2,1)S(1)} collective-permute-done((bf16[1024,128]{1,0:T(8,128)(2,1)}, bf16[1024,128]{1,0:T(8,128)(2,1)S(1)}, u32[]{:S(2)}, u32[]{:S(2)}) %collective-permute-start.9) | collective-permute-done | bytes 262176 | tf_op jit(solution)/shard_map/ppermute | solution.py:450
  103.5 3.7 %shard_map.63 = (bf16[1024,128]{1,0:T(8,128)(2,1)}, bf16[8,256,128]{2,1,0:T(8,128)(2,1)}, s32[8,128]{1,0:T(8,128)S(1)}) custom-call(s32[4]{0:T(128)S(1)} %pad_add_fusion.ids, s32[8,128]{1,0:T(8,128)S(1)} %get-tuple-element.70.token, bf16[1024,1024]{1,0:T(8,128)(2,1)S(1)} %get-tuple-element.65.refs_0_, ...), custom_call_target="tpu_custom_call", output_to_operand_aliasing={{2}: (1, {})} | custom-call | flops 1 | bytes 1 | tf_op jit(solution)/shard_map/pallas_call | solution.py:93
  107.3 3.5 %all-to-all-start.1 = ((bf16[8,128,128]{2,1,0:T(8,128)(2,1)}), bf16[8,128,128]{2,1,0:T(8,128)(2,1)S(1)}, u32[]{:S(2)}, u32[]{:S(2)}) async-start(bf16[8,128,128]{2,1,0:T(8,128)(2,1)} %bitcast.26), calls=%async_computation.1 | async-start | bytes 524288 | tf_op jit(solution)/shard_map/all_to_all | solution.py:66
  110.7 2.8 %shard_map.64 = (bf16[1024,256]{1,0:T(8,128)(2,1)}, s32[8,128]{1,0:T(8,128)S(1)}) custom-call(s32[4]{0:T(128)S(1)} %pad_add_fusion.ids, s32[8,128]{1,0:T(8,128)S(1)} %get-tuple-element.75.token, bf16[1024,1024]{1,0:T(8,128)(2,1)S(1)} %get-tuple-element.65.refs_0_, ...), custom_call_target="tpu_custom_call", output_to_operand_aliasing={{1}: (1, {})} | custom-call | flops 1 | bytes 1 | tf_op jit(solution)/shard_map/pallas_call | solution.py:93
  113.5 2.1 %collective-permute-start.13 = (bf16[1024,256]{1,0:T(8,128)(2,1)}, bf16[1024,256]{1,0:T(8,128)(2,1)}, u32[]{:S(2)}, u32[]{:S(2)}) collective-permute-start(bf16[1024,256]{1,0:T(8,128)(2,1)} %get-tuple-element.84), channel_id=1, source_target_pairs={{16,8},{8,0},{17,9},{9,1},{18,10},{10,2},{19,11},{11,3},{20,12},{1... | collective-permute-start | bytes 1572872 | tf_op jit(solution)/shard_map/ppermute | solution.py:411
  115.6 1.6 all-to-all-done.1.refs_2_
  117.2 5.2 %shard_map.65 = (bf16[1024,1024]{1,0:T(8,128)(2,1)}, bf16[1024,256]{1,0:T(8,128)(2,1)}, s32[8,128]{1,0:T(8,128)S(1)}) custom-call(s32[4]{0:T(128)S(1)} %pad_add_fusion.ids, s32[8,128]{1,0:T(8,128)S(1)} %get-tuple-element.77.token, bf16[1024,1024]{1,0:T(8,128)(2,1)S(1)} %get-tuple-element.65.refs_0_, ...), custom_call_target="tpu_custom_call", output_to_operand_aliasing={{2}: (1, {})} | custom-call | flops 1 | bytes 1 | tf_op jit(solution)/shard_map/pallas_call | solution.py:93
  122.4 2.1 %collective-permute-start.15 = (bf16[1024,256]{1,0:T(8,128)(2,1)}, bf16[1024,256]{1,0:T(8,128)(2,1)}, u32[]{:S(2)}, u32[]{:S(2)}) collective-permute-start(bf16[1024,256]{1,0:T(8,128)(2,1)} %get-tuple-element.88), channel_id=1, source_target_pairs={{16,0},{17,1},{18,2},{19,3},{20,4},{21,5},{22,6},{23,7}} | collective-permute-start | bytes 1572872 | tf_op jit(solution)/shard_map/ppermute | solution.py:463
  124.5 2.1 %collective-permute-start.14 = (bf16[1024,256]{1,0:T(8,128)(2,1)}, bf16[1024,256]{1,0:T(8,128)(2,1)}, u32[]{:S(2)}, u32[]{:S(2)}) collective-permute-start(bf16[1024,256]{1,0:T(8,128)(2,1)} %get-tuple-element.88), channel_id=1, source_target_pairs={{16,8},{17,9},{18,10},{19,11},{20,12},{21,13},{22,14},{23,15}} | collective-permute-start | bytes 1572872 | tf_op jit(solution)/shard_map/ppermute | solution.py:463
  126.6 3.5 %all-to-all-start.2 = ((bf16[8,256,128]{2,1,0:T(8,128)(2,1)}), bf16[8,256,128]{2,1,0:T(8,128)(2,1)S(1)}, u32[]{:S(2)}, u32[]{:S(2)}) async-start(bf16[8,256,128]{2,1,0:T(8,128)(2,1)} %get-tuple-element.90), calls=%async_computation.2 | async-start | bytes 1048576 | tf_op jit(solution)/shard_map/all_to_all | solution.py:66
  130.1 1.0 copy-done.1
  131.2 5.1 %shard_map.66 = (f32[1024,1024]{1,0:T(8,128)}, bf16[1024,256]{1,0:T(8,128)(2,1)}, s32[8,128]{1,0:T(8,128)S(1)}) custom-call(s32[4]{0:T(128)S(1)} %pad_add_fusion.ids, s32[8,128]{1,0:T(8,128)S(1)} %get-tuple-element.82.token, bf16[1024,1024]{1,0:T(8,128)(2,1)S(1)} %get-tuple-element.65.refs_0_, ...), custom_call_target="tpu_custom_call", output_to_operand_aliasing={{2}: (1, {})} | custom-call | flops 1 | bytes 1 | tf_op jit(solution)/shard_map/pallas_call | solution.py:93
  136.3 2.6 %collective-permute-start.16 = (bf16[1024,256]{1,0:T(8,128)(2,1)}, bf16[1024,256]{1,0:T(8,128)(2,1)}, u32[]{:S(2)}, u32[]{:S(2)}) collective-permute-start(bf16[1024,256]{1,0:T(8,128)(2,1)} %get-tuple-element.92), channel_id=1, source_target_pairs={{0,4},{4,0},{1,5},{5,1},{2,6},{6,2},{3,7},{7,3},{8,12},{12,8},{9,1... | collective-permute-start | bytes 1572872 | tf_op jit(solution)/shard_map/ppermute | solution.py:51
  138.8 2.7 %shard_map.67 = (bf16[1024,256]{1,0:T(8,128)(2,1)}, s32[8,128]{1,0:T(8,128)S(1)}) custom-call(s32[4]{0:T(128)S(1)} %pad_add_fusion.ids, s32[8,128]{1,0:T(8,128)S(1)} %get-tuple-element.85.token, bf16[1024,1024]{1,0:T(8,128)(2,1)S(1)} %get-tuple-element.65.refs_0_, ...), custom_call_target="tpu_custom_call", output_to_operand_aliasing={{1}: (1, {})} | custom-call | flops 1 | bytes 1 | tf_op jit(solution)/shard_map/pallas_call | solution.py:93
  141.5 1.5 collective-permute-start.17
  143.0 6.7 %collective-permute-done.14.refs_3_ = bf16[1024,256]{1,0:T(8,128)(2,1)} collective-permute-done((bf16[1024,256]{1,0:T(8,128)(2,1)}, bf16[1024,256]{1,0:T(8,128)(2,1)}, u32[]{:S(2)}, u32[]{:S(2)}) %collective-permute-start.14) | collective-permute-done | bytes 524320 | tf_op jit(solution)/shard_map/ppermute | solution.py:463
  149.7 5.5 %shard_map.68 = (bf16[8,256,256]{2,1,0:T(8,128)(2,1)}, s32[8,128]{1,0:T(8,128)S(1)}) custom-call(s32[4]{0:T(128)S(1)} %pad_add_fusion.ids, s32[8,128]{1,0:T(8,128)S(1)} %get-tuple-element.86.token, bf16[1024,1024]{1,0:T(8,128)(2,1)S(1)} %get-tuple-element.65.refs_0_, bf16[1024,1024]{1,0:T(8,128)(2,1)} %get-tuple-element.71.refs_1_, ...), custom_call_target="tpu_custom_call", output_to_operand_aliasing={{1}: (1, {})} | custom-call | flops 1 | bytes 1 | tf_op jit(solution)/shard_map/pallas_call | solution.py:93
  155.2 4.2 %all-to-all-start.3 = ((bf16[8,256,256]{2,1,0:T(8,128)(2,1)}), bf16[8,256,256]{2,1,0:T(8,128)(2,1)}, u32[]{:S(2)}, u32[]{:S(2)}) async-start(bf16[8,256,256]{2,1,0:T(8,128)(2,1)} %get-tuple-element.100), calls=%async_computation.3 | async-start | bytes 2097152 | tf_op jit(solution)/shard_map/all_to_all | solution.py:66
  159.5 3.4 %shard_map.69 = (f32[1024,1024]{1,0:T(8,128)}, s32[8,128]{1,0:T(8,128)S(1)}) custom-call(s32[4]{0:T(128)S(1)} %pad_add_fusion.ids, s32[8,128]{1,0:T(8,128)S(1)} %get-tuple-element.91.token, bf16[1024,256]{1,0:T(8,128)(2,1)} %collective-permute-done.16.refs_0_, f32[1024,1024]{1,0:T(8,128)} %bitcast.22, ...), custom_call_target="tpu_custom_call", output_to_operand_aliasing={{1}: (1, {}), {0}: (4, {})} | custom-call | flops 1 | bytes 1 | tf_op jit(solution)/shard_map/pallas_call | solution.py:93
  162.9 5.1 %shard_map.70 = (f32[1024,1024]{1,0:T(8,128)}, bf16[1024,256]{1,0:T(8,128)(2,1)}, s32[8,128]{1,0:T(8,128)S(1)}) custom-call(s32[4]{0:T(128)S(1)} %pad_add_fusion.ids, s32[8,128]{1,0:T(8,128)S(1)} %get-tuple-element.94.token, bf16[1024,1024]{1,0:T(8,128)(2,1)S(1)} %get-tuple-element.65.refs_0_, ...), custom_call_target="tpu_custom_call", output_to_operand_aliasing={{2}: (1, {}), {0}: (9, {})} | custom-call | flops 1 | bytes 1 | tf_op jit(solution)/shard_map/pallas_call | solution.py:93
  168.0 2.7 %collective-permute-start.18 = (bf16[1024,256]{1,0:T(8,128)(2,1)}, bf16[1024,256]{1,0:T(8,128)(2,1)S(1)}, u32[]{:S(2)}, u32[]{:S(2)}) collective-permute-start(bf16[1024,256]{1,0:T(8,128)(2,1)} %get-tuple-element.104), channel_id=1, source_target_pairs={{0,4},{4,0},{1,5},{5,1},{2,6},{6,2},{3,7},{7,3},{8,12},{12,8},{9,1... | collective-permute-start | bytes 1572872 | tf_op jit(solution)/shard_map/ppermute | solution.py:51
  170.7 3.8 %all-to-all-done.3.refs_6_ = bf16[8,256,256]{2,1,0:T(8,128)(2,1)} async-done(((bf16[8,256,256]{2,1,0:T(8,128)(2,1)}), bf16[8,256,256]{2,1,0:T(8,128)(2,1)}, u32[]{:S(2)}, u32[]{:S(2)}) %all-to-all-start.3) | async-done | bytes 1048608 | tf_op jit(solution)/shard_map/all_to_all | solution.py:66
  174.4 6.9 %shard_map.71 = (f32[256,1024]{1,0:T(8,128)}, f32[256,1024]{1,0:T(8,128)}, s32[8,128]{1,0:T(8,128)S(1)}) custom-call(s32[4]{0:T(128)S(1)} %pad_add_fusion.ids, s32[8,128]{1,0:T(8,128)S(1)} %get-tuple-element.98.token, bf16[1024,1024]{1,0:T(8,128)(2,1)S(1)} %get-tuple-element.65.refs_0_, ...), custom_call_target="tpu_custom_call", output_to_operand_aliasing={{2}: (1, {})} | custom-call | flops 1 | bytes 1 | tf_op jit(solution)/shard_map/pallas_call | solution.py:93
  181.3 3.8 %collective-permute-done.18.refs_0_ = bf16[1024,256]{1,0:T(8,128)(2,1)S(1)} collective-permute-done((bf16[1024,256]{1,0:T(8,128)(2,1)}, bf16[1024,256]{1,0:T(8,128)(2,1)S(1)}, u32[]{:S(2)}, u32[]{:S(2)}) %collective-permute-start.18) | collective-permute-done | bytes 524320 | tf_op jit(solution)/shard_map/ppermute | solution.py:51
  185.1 2.9 %shard_map.72 = (f32[1024,1024]{1,0:T(8,128)}, s32[8,128]{1,0:T(8,128)S(1)}) custom-call(s32[4]{0:T(128)S(1)} %pad_add_fusion.ids, s32[8,128]{1,0:T(8,128)S(1)} %get-tuple-element.103.token, bf16[1024,256]{1,0:T(8,128)(2,1)S(1)} %collective-permute-done.18.refs_0_, f32[1024,1024]{1,0:T(8,128)} %bitcast.24, ...), custom_call_target="tpu_custom_call", output_to_operand_aliasing={{1}: (1, {}), {0}: (4, {})} | custom-call | flops 1 | bytes 1 | tf_op jit(solution)/shard_map/pallas_call | solution.py:93
  (29 shorter events, 1.5 us)
Async XLA Ops:
  1.9 13.7 %collective-permute-start = (bf16[256,1024]{1,0:T(8,128)(2,1)S(1)}, bf16[256,1024]{1,0:T(8,128)(2,1)S(1)}, u32[]{:S(2)}, u32[]{:S(2)}) collective-permute-start(bf16[256,1024]{1,0:T(8,128)(2,1)S(1)} %convert_bitcast_fusion), channel_id=1, source_target_pairs={{0,4},{4,0},{1,5},{5,1},{2,6},{6,2},{3,7},{7,3},{8,12},{12,8},{9,1... | collective-permute-start | bytes 1572872 | tf_op jit(solution)/shard_map/ppermute | solution.py:51
  3.5 13.4 %collective-permute-start.1 = (bf16[256,1024]{1,0:T(8,128)(2,1)S(1)}, bf16[256,1024]{1,0:T(8,128)(2,1)S(1)}, u32[]{:S(2)}, u32[]{:S(2)}) collective-permute-start(bf16[256,1024]{1,0:T(8,128)(2,1)S(1)} %convert_bitcast_fusion), channel_id=1, source_target_pairs={{0,2},{2,0},{1,3},{3,1},{4,6},{6,4},{5,7},{7,5},{8,10},{10,8},{9,1... | collective-permute-start | bytes 1572872 | tf_op jit(solution)/shard_map/ppermute | solution.py:51
  17.0 21.8 %copy-start.3 = (bf16[768,1024]{1,0:T(8,128)(2,1)}, bf16[768,1024]{1,0:T(8,128)(2,1)S(1)}, u32[]{:S(2)}) copy-start(bf16[768,1024]{1,0:T(8,128)(2,1)S(1)} %pad_maximum_fusion.refs_0_) | copy-start | bytes 4718596
  17.0 21.8 %collective-permute-start.4 = (bf16[768,1024]{1,0:T(8,128)(2,1)S(1)}, bf16[768,1024]{1,0:T(8,128)(2,1)}, u32[]{:S(2)}, u32[]{:S(2)}) collective-permute-start(bf16[768,1024]{1,0:T(8,128)(2,1)S(1)} %pad_maximum_fusion.refs_0_), channel_id=1, source_target_pairs={{0,1},{1,0},{2,3},{3,2},{4,5},{5,4},{6,7},{7,6},{8,9},{9,8},{10,11... | collective-permute-start | bytes 4718600 | tf_op jit(solution)/shard_map/ppermute | solution.py:51
  17.1 14.4 %collective-permute-start.3 = (bf16[256,1024]{1,0:T(8,128)(2,1)S(1)}, bf16[256,1024]{1,0:T(8,128)(2,1)}, u32[]{:S(2)}, u32[]{:S(2)}) collective-permute-start(bf16[256,1024]{1,0:T(8,128)(2,1)S(1)} %collective-permute-done), channel_id=1, source_target_pairs={{0,2},{2,0},{1,3},{3,1},{4,6},{6,4},{5,7},{7,5},{8,10},{10,8},{9,1... | collective-permute-start | bytes 1572872 | tf_op jit(solution)/shard_map/ppermute | solution.py:51
  18.7 9.1 %collective-permute-start.2 = (bf16[128,1024]{1,0:T(8,128)(2,1)S(1)}, bf16[128,1024]{1,0:T(8,128)(2,1)S(1)}, u32[]{:S(2)}, u32[]{:S(2)}) collective-permute-start(bf16[128,1024]{1,0:T(8,128)(2,1)S(1)} %dynamic-slice_bitcast_fusion), channel_id=1, source_target_pairs={{0,4},{4,0},{1,5},{5,1},{2,6},{6,2},{3,7},{7,3},{8,12},{12,8},{9,1... | collective-permute-start | bytes 786440 | tf_op jit(solution)/shard_map/ppermute | solution.py:51
  19.2 19.1 %collective-permute-start.6 = (bf16[1024,256]{1,0:T(8,128)(2,1)}, bf16[1024,256]{1,0:T(8,128)(2,1)S(1)}, u32[]{:S(2)}, u32[]{:S(2)}) collective-permute-start(bf16[1024,256]{1,0:T(8,128)(2,1)} %get-tuple-element.60), channel_id=1, source_target_pairs={{0,4},{4,0},{1,5},{5,1},{2,6},{6,2},{3,7},{7,3},{8,12},{12,8},{9,1... | collective-permute-start | bytes 1572872 | tf_op jit(solution)/shard_map/ppermute | solution.py:51
  31.5 7.3 %collective-permute-start.5 = (bf16[256,1024]{1,0:T(8,128)(2,1)}, bf16[256,1024]{1,0:T(8,128)(2,1)}, u32[]{:S(2)}, u32[]{:S(2)}) collective-permute-start(bf16[256,1024]{1,0:T(8,128)(2,1)} %collective-permute-done.3.refs_1_), channel_id=1, source_target_pairs={{0,1},{1,0},{2,3},{3,2},{4,5},{5,4},{6,7},{7,6},{8,9},{9,8},{10,11... | collective-permute-start | bytes 1572872 | tf_op jit(solution)/shard_map/ppermute | solution.py:51
  38.3 20.9 %collective-permute-start.8 = (bf16[1024,256]{1,0:T(8,128)(2,1)}, bf16[1024,256]{1,0:T(8,128)(2,1)S(1)}, u32[]{:S(2)}, u32[]{:S(2)}) collective-permute-start(bf16[1024,256]{1,0:T(8,128)(2,1)} %get-tuple-element.67), channel_id=1, source_target_pairs={{0,4},{4,0},{1,5},{5,1},{2,6},{6,2},{3,7},{7,3},{8,12},{12,8},{9,1... | collective-permute-start | bytes 1572872 | tf_op jit(solution)/shard_map/ppermute | solution.py:51
  45.0 6.8 %copy-start.2 = (f32[1,256,1024]{2,1,0:T(8,128)S(1)}, f32[1,256,1024]{2,1,0:T(8,128)}, u32[]{:S(2)}) copy-start(f32[1,256,1024]{2,1,0:T(8,128)} %refs_5_.1) | copy-start | bytes 3145732
  49.2 17.0 %collective-permute-start.7 = (bf16[1024,256]{1,0:T(8,128)(2,1)}, bf16[1024,256]{1,0:T(8,128)(2,1)S(1)}, u32[]{:S(2)}, u32[]{:S(2)}) collective-permute-start(bf16[1024,256]{1,0:T(8,128)(2,1)} %get-tuple-element.66.refs_2_), channel_id=1, source_target_pairs={{24,16},{25,17},{26,18},{27,19},{28,20},{29,21},{30,22},{31,23}} | collective-permute-start | bytes 1572872 | tf_op jit(solution)/shard_map/ppermute | solution.py:411
  50.5 53.0 %collective-permute-start.10 = (bf16[512,1024]{1,0:T(8,128)(2,1)}, bf16[512,1024]{1,0:T(8,128)(2,1)}, u32[]{:S(2)}, u32[]{:S(2)}) collective-permute-start(bf16[512,1024]{1,0:T(8,128)(2,1)} %get-tuple-element.73), channel_id=1, source_target_pairs={{24,16},{8,0},{25,17},{9,1},{26,18},{10,2},{27,19},{11,3},{28,20},... | collective-permute-start | bytes 3145736 | tf_op jit(solution)/shard_map/ppermute | solution.py:434
  55.0 18.5 %all-to-all-start = ((bf16[8,256,128]{2,1,0:T(8,128)(2,1)}), bf16[8,256,128]{2,1,0:T(8,128)(2,1)}, u32[]{:S(2)}, u32[]{:S(2)}) async-start(bf16[8,256,128]{2,1,0:T(8,128)(2,1)} %get-tuple-element.69), calls=%async_computation | async-start | bytes 1048576 | tf_op jit(solution)/shard_map/all_to_all | solution.py:66
  66.2 5.4 %copy-start = (bf16[1024,256]{1,0:T(8,128)(2,1)}, bf16[1024,256]{1,0:T(8,128)(2,1)S(1)}, u32[]{:S(2)}) copy-start(bf16[1024,256]{1,0:T(8,128)(2,1)S(1)} %collective-permute-done.7.refs_1_.refs_3_) | copy-start | bytes 1572868
  71.6 31.9 %collective-permute-start.11 = (bf16[1024,256]{1,0:T(8,128)(2,1)}, bf16[1024,256]{1,0:T(8,128)(2,1)S(1)}, u32[]{:S(2)}, u32[]{:S(2)}) collective-permute-start(bf16[1024,256]{1,0:T(8,128)(2,1)} %get-tuple-element.74), channel_id=1, source_target_pairs={{24,16},{16,8},{25,17},{17,9},{26,18},{18,10},{27,19},{19,11},{28,... | collective-permute-start | bytes 1572872 | tf_op jit(solution)/shard_map/ppermute | solution.py:411
  77.8 25.7 %collective-permute-start.9 = (bf16[1024,128]{1,0:T(8,128)(2,1)}, bf16[1024,128]{1,0:T(8,128)(2,1)S(1)}, u32[]{:S(2)}, u32[]{:S(2)}) collective-permute-start(bf16[1024,128]{1,0:T(8,128)(2,1)} %get-tuple-element.72), channel_id=1, source_target_pairs={{24,16},{8,0},{25,17},{9,1},{26,18},{10,2},{27,19},{11,3},{28,20},... | collective-permute-start | bytes 786440 | tf_op jit(solution)/shard_map/ppermute | solution.py:450
  107.3 9.9 %collective-permute-start.12 = (bf16[512,1024]{1,0:T(8,128)(2,1)}, bf16[512,1024]{1,0:T(8,128)(2,1)}, u32[]{:S(2)}, u32[]{:S(2)}) collective-permute-start(bf16[512,1024]{1,0:T(8,128)(2,1)} %collective-permute-done.10.refs_3_), channel_id=1, source_target_pairs={{0,1},{1,0},{2,3},{3,2},{4,5},{5,4},{6,7},{7,6},{8,9},{9,8},{10,11... | collective-permute-start | bytes 3145736 | tf_op jit(solution)/shard_map/ppermute | solution.py:51
  107.3 9.9 %all-to-all-start.1 = ((bf16[8,128,128]{2,1,0:T(8,128)(2,1)}), bf16[8,128,128]{2,1,0:T(8,128)(2,1)S(1)}, u32[]{:S(2)}, u32[]{:S(2)}) async-start(bf16[8,128,128]{2,1,0:T(8,128)(2,1)} %bitcast.26), calls=%async_computation.1 | async-start | bytes 524288 | tf_op jit(solution)/shard_map/all_to_all | solution.py:66
  113.5 16.6 %collective-permute-start.13 = (bf16[1024,256]{1,0:T(8,128)(2,1)}, bf16[1024,256]{1,0:T(8,128)(2,1)}, u32[]{:S(2)}, u32[]{:S(2)}) collective-permute-start(bf16[1024,256]{1,0:T(8,128)(2,1)} %get-tuple-element.84), channel_id=1, source_target_pairs={{16,8},{8,0},{17,9},{9,1},{18,10},{10,2},{19,11},{11,3},{20,12},{1... | collective-permute-start | bytes 1572872 | tf_op jit(solution)/shard_map/ppermute | solution.py:411
  122.4 20.6 %collective-permute-start.15 = (bf16[1024,256]{1,0:T(8,128)(2,1)}, bf16[1024,256]{1,0:T(8,128)(2,1)}, u32[]{:S(2)}, u32[]{:S(2)}) collective-permute-start(bf16[1024,256]{1,0:T(8,128)(2,1)} %get-tuple-element.88), channel_id=1, source_target_pairs={{16,0},{17,1},{18,2},{19,3},{20,4},{21,5},{22,6},{23,7}} | collective-permute-start | bytes 1572872 | tf_op jit(solution)/shard_map/ppermute | solution.py:463
  124.5 25.2 %collective-permute-start.14 = (bf16[1024,256]{1,0:T(8,128)(2,1)}, bf16[1024,256]{1,0:T(8,128)(2,1)}, u32[]{:S(2)}, u32[]{:S(2)}) collective-permute-start(bf16[1024,256]{1,0:T(8,128)(2,1)} %get-tuple-element.88), channel_id=1, source_target_pairs={{16,8},{17,9},{18,10},{19,11},{20,12},{21,13},{22,14},{23,15}} | collective-permute-start | bytes 1572872 | tf_op jit(solution)/shard_map/ppermute | solution.py:463
  126.6 16.4 %all-to-all-start.2 = ((bf16[8,256,128]{2,1,0:T(8,128)(2,1)}), bf16[8,256,128]{2,1,0:T(8,128)(2,1)S(1)}, u32[]{:S(2)}, u32[]{:S(2)}) async-start(bf16[8,256,128]{2,1,0:T(8,128)(2,1)} %get-tuple-element.90), calls=%async_computation.2 | async-start | bytes 1048576 | tf_op jit(solution)/shard_map/all_to_all | solution.py:66
  130.1 1.0 copy-start.1
  136.3 23.2 %collective-permute-start.16 = (bf16[1024,256]{1,0:T(8,128)(2,1)}, bf16[1024,256]{1,0:T(8,128)(2,1)}, u32[]{:S(2)}, u32[]{:S(2)}) collective-permute-start(bf16[1024,256]{1,0:T(8,128)(2,1)} %get-tuple-element.92), channel_id=1, source_target_pairs={{0,4},{4,0},{1,5},{5,1},{2,6},{6,2},{3,7},{7,3},{8,12},{12,8},{9,1... | collective-permute-start | bytes 1572872 | tf_op jit(solution)/shard_map/ppermute | solution.py:51
  141.5 21.3 %collective-permute-start.17 = (bf16[1024,256]{1,0:T(8,128)(2,1)}, bf16[1024,256]{1,0:T(8,128)(2,1)}, u32[]{:S(2)}, u32[]{:S(2)}) collective-permute-start(bf16[1024,256]{1,0:T(8,128)(2,1)} %get-tuple-element.96), channel_id=1, source_target_pairs={{8,0},{9,1},{10,2},{11,3},{12,4},{13,5},{14,6},{15,7}} | collective-permute-start | bytes 1572872 | tf_op jit(solution)/shard_map/ppermute | solution.py:411
  155.2 19.2 %all-to-all-start.3 = ((bf16[8,256,256]{2,1,0:T(8,128)(2,1)}), bf16[8,256,256]{2,1,0:T(8,128)(2,1)}, u32[]{:S(2)}, u32[]{:S(2)}) async-start(bf16[8,256,256]{2,1,0:T(8,128)(2,1)} %get-tuple-element.100), calls=%async_computation.3 | async-start | bytes 2097152 | tf_op jit(solution)/shard_map/all_to_all | solution.py:66
  168.0 17.1 %collective-permute-start.18 = (bf16[1024,256]{1,0:T(8,128)(2,1)}, bf16[1024,256]{1,0:T(8,128)(2,1)S(1)}, u32[]{:S(2)}, u32[]{:S(2)}) collective-permute-start(bf16[1024,256]{1,0:T(8,128)(2,1)} %get-tuple-element.104), channel_id=1, source_target_pairs={{0,4},{4,0},{1,5},{5,1},{2,6},{6,2},{3,7},{7,3},{8,12},{12,8},{9,1... | collective-permute-start | bytes 1572872 | tf_op jit(solution)/shard_map/ppermute | solution.py:51

commit v17 on v13

--- a/solution.py
+++ b/solution.py
@@ -474,9 +474,9 @@
         far_in=(5,), scratch=[pltpu.VMEM((size_d, rows), LOW)],
     )
     m = exchange(m)
-    out_offset = add(0, other0, out_offset)
     out_offset, other1 = last(1, p1, [wave2, wave3, wave4], out_offset)
     other1 = swap(other1, "x")
+    out_offset = add(0, other0, out_offset)
     out_gain, out_spread = order.call(
         end_kernel, [pair, in_hbm(e1), in_hbm(following), near, in_hbm(prod), spread, m],
         [wide(rows, size_d), wide(rows, size_d)], 18, scratch=[slab_rows, slab_rows],

time: 184 us -> 196 us (1.065)
  waiting for transfers between devices: 64.9 us -> 79.1 us
  starting transfers between devices: 41.7 us -> 39.2 us
    ppermute x11, waiting for transfers between devices: 30.4 us -> 45.9 us  [swap(): return lax.ppermute(value, axis, [(0, 1), (1, 0)])]
    all_to_all x4, waiting for transfers between devices: 12 us -> 8.08 us  [exchange(): return lax.all_to_all(blocks, GROUP, 0, 0)]
    ppermute x1, waiting for transfers between devices: 7.24 us -> 9.9 us  [suffix(): lax.ppermute(far_slab, 'z', [(2, 1)])]
    ppermute x11, starting transfers between devices: 11.6 us -> 9.1 us  [swap(): return lax.ppermute(value, axis, [(0, 1), (1, 0)])]
  transfers between devices with their start and end apart: 23 -> 23, of which waited for: 12 -> 12; matrix products, arithmetic and copies ran while one was open for 3% -> 3% of each run, Pallas kernels for 33% -> 31%
where the time goes in v17:
time: 196 us; the launch traced here: 193 us
  waiting for transfers between devices  79.1 us (40%)
  Pallas kernels  65.9 us (34%)
  starting transfers between devices  39.2 us (20%)
  other arithmetic  4.08 us (2%)
  local copies, waits for them, and re-layouts  3.7 us (2%)
    pallas_call x15, Pallas kernels, call(): pl.pallas_call(body, in_specs=[SMEM, ANY] + [ANY if i in far_in else VMEM...  65.9 us
    ppermute x11, waiting for transfers between devices, swap(): return lax.ppermute(value, axis, [(0, 1), (1, 0)])  45.9 us
    all_to_all x4, starting transfers between devices, exchange(): return lax.all_to_all(blocks, GROUP, 0, 0)  15.7 us
    ppermute x4, waiting for transfers between devices, down(): lax.ppermute(value, 'z', [(source, source - 1) for source in sources])  15.3 us
    ppermute x1, waiting for transfers between devices, suffix(): lax.ppermute(far_slab, 'z', [(2, 1)])  9.9 us
    ppermute x11, starting transfers between devices, swap(): return lax.ppermute(value, axis, [(0, 1), (1, 0)])  9.1 us
    all_to_all x4, waiting for transfers between devices, exchange(): return lax.all_to_all(blocks, GROUP, 0, 0)  8.08 us
    ppermute x4, starting transfers between devices, down(): lax.ppermute(value, 'z', [(source, source - 1) for source in sources])  7.72 us
  transfers between devices with their start and end apart: 23, of which 12 were waited for; matrix products, arithmetic and copies ran while one was open for 3% of the time, Pallas kernels for 31%

profile of v17, /device:TPU:16, one launch (start us, length us, event | category | flops | bytes accessed | tf_op | source)
XLA Modules:
  0.0 193.1 jit_solution(15844468423908132196)
XLA Ops:
  0.6 1.3 convert_bitcast_fusion
  1.9 1.6 collective-permute-start
  3.5 1.5 collective-permute-start.1
  5.0 1.3 convert_element_type.25
  6.3 2.6 %fusion.1 = (bf16[1024,256]{1,0:T(8,128)(2,1)}, bf16[1024,256]{1,0:T(8,128)(2,1)}) fusion(f32[1,1024,1024]{2,1,0:T(8,128)} %param.5, s32[]{:T(128)S(6)} %select_n.11, s32[]{:T(128)S(6)} %select_n.10), kind=kLoop, calls=%fused_computation.4 | loop fusion | bytes 2097160 | tf_op jit(solution)/shard_map/convert_element_type | solution.py:386
  9.0 6.7 %collective-permute-done = bf16[256,1024]{1,0:T(8,128)(2,1)S(1)} collective-permute-done((bf16[256,1024]{1,0:T(8,128)(2,1)S(1)}, bf16[256,1024]{1,0:T(8,128)(2,1)S(1)}, u32[]{:S(2)}, u32[]{:S(2)}) %collective-permute-start) | collective-permute-done | bytes 524320 | tf_op jit(solution)/shard_map/ppermute | solution.py:51
  15.7 1.2 collective-permute-done.1
  17.1 1.6 collective-permute-start.3
  19.2 7.8 %collective-permute-done.2.refs_2_.refs_3_ = bf16[128,1024]{1,0:T(8,128)(2,1)S(1)} collective-permute-done((bf16[128,1024]{1,0:T(8,128)(2,1)S(1)}, bf16[128,1024]{1,0:T(8,128)(2,1)S(1)}, u32[]{:S(2)}, u32[]{:S(2)}) %collective-permute-start.2) | collective-permute-done | bytes 262176 | tf_op jit(solution)/shard_map/ppermute | solution.py:51
  27.0 4.4 %collective-permute-done.3.refs_1_ = bf16[256,1024]{1,0:T(8,128)(2,1)S(1)} collective-permute-done((bf16[256,1024]{1,0:T(8,128)(2,1)S(1)}, bf16[256,1024]{1,0:T(8,128)(2,1)S(1)}, u32[]{:S(2)}, u32[]{:S(2)}) %collective-permute-start.3) | collective-permute-done | bytes 524320 | tf_op jit(solution)/shard_map/ppermute | solution.py:51
  32.0 1.4 collective-permute-done.5.refs_3_
  33.5 6.1 %shard_map.58 = (bf16[1024,1024]{1,0:T(8,128)(2,1)}, bf16[1024,1024]{1,0:T(8,128)(2,1)}, bf16[1024,1024]{1,0:T(8,128)(2,1)S(1)}, bf16[512,1024]{1,0:T(8,128)(2,1)}, s32[8,128]{1,0:T(8,128)S(1)}) custom-call(s32[4]{0:T(128)S(1)} %pad_add_fusion.ids, s32[8,128]{1,0:T(8,128)S(1)} %broadcast_in_dim.12.token, ...), custom_call_target="tpu_custom_call", output_to_operand_aliasing={{4}: (1, {})} | custom-call | flops 1 | bytes 1 | tf_op jit(solution)/shard_map/pallas_call | solution.py:93
  39.6 1.3 collective-permute-start.9
  40.9 5.0 %collective-permute-done.6.refs_1_ = bf16[1024,256]{1,0:T(8,128)(2,1)S(1)} collective-permute-done((bf16[1024,256]{1,0:T(8,128)(2,1)}, bf16[1024,256]{1,0:T(8,128)(2,1)S(1)}, u32[]{:S(2)}, u32[]{:S(2)}) %collective-permute-start.6) | collective-permute-done | bytes 524320 | tf_op jit(solution)/shard_map/ppermute | solution.py:51
  46.5 1.3 convert_bitcast_fusion.1.refs_1_
  47.8 4.2 %shard_map.59 = (f32[1024,256]{1,0:T(8,128)}, bf16[1024,256]{1,0:T(8,128)(2,1)}, s32[8,128]{1,0:T(8,128)S(1)}) custom-call(s32[4]{0:T(128)S(1)} %pad_add_fusion.ids, s32[8,128]{1,0:T(8,128)S(1)} %get-tuple-element.58.token, bf16[1024,1024]{1,0:T(8,128)(2,1)} %get-tuple-element.59.refs_0_.refs_3_, ...), custom_call_target="tpu_custom_call", output_to_operand_aliasing={{2}: (1, {})} | custom-call | flops 1 | bytes 1 | tf_op jit(solution)/shard_map/pallas_call | solution.py:93
  52.0 3.1 %shard_map.60 = (bf16[8,256,128]{2,1,0:T(8,128)(2,1)}, s32[8,128]{1,0:T(8,128)S(1)}) custom-call(s32[4]{0:T(128)S(1)} %pad_add_fusion.ids, s32[8,128]{1,0:T(8,128)S(1)} %get-tuple-element.62.token, bf16[1024,1024]{1,0:T(8,128)(2,1)} %get-tuple-element.59.refs_0_.refs_3_, ...), custom_call_target="tpu_custom_call", output_to_operand_aliasing={{1}: (1, {})} | custom-call | flops 1 | bytes 1 | tf_op jit(solution)/shard_map/pallas_call | solution.py:93
  55.1 4.3 %all-to-all-start = ((bf16[8,256,128]{2,1,0:T(8,128)(2,1)}), bf16[8,256,128]{2,1,0:T(8,128)(2,1)}, u32[]{:S(2)}, u32[]{:S(2)}) async-start(bf16[8,256,128]{2,1,0:T(8,128)(2,1)} %get-tuple-element.65), calls=%async_computation | async-start | bytes 1048576 | tf_op jit(solution)/shard_map/all_to_all | solution.py:66
  59.4 1.3 collective-permute-start.8
  60.7 8.1 %all-to-all-done.refs_1_ = bf16[8,256,128]{2,1,0:T(8,128)(2,1)} async-done(((bf16[8,256,128]{2,1,0:T(8,128)(2,1)}), bf16[8,256,128]{2,1,0:T(8,128)(2,1)}, u32[]{:S(2)}, u32[]{:S(2)}) %all-to-all-start) | async-done | bytes 524320 | tf_op jit(solution)/shard_map/all_to_all | solution.py:66
  68.8 4.2 %shard_map.61 = (f32[256,1024]{1,0:T(8,128)}, f32[1024,128]{1,0:T(8,128)}, bf16[1024,128]{1,0:T(8,128)(2,1)}, s32[8,128]{1,0:T(8,128)S(1)}) custom-call(s32[4]{0:T(128)S(1)} %pad_add_fusion.ids, s32[8,128]{1,0:T(8,128)S(1)} %get-tuple-element.64.token, bf16[1024,1024]{1,0:T(8,128)(2,1)} %get-tuple-element.59.refs_0_.refs_3_, ...), custom_call_target="tpu_custom_call", output_to_operand_aliasing={{3}: (1, {})} | custom-call | flops 1 | bytes 1 | tf_op jit(solution)/shard_map/pallas_call | solution.py:93
  73.0 1.3 collective-permute-start.10
  74.3 4.6 %collective-permute-done.8.refs_1_.refs_3_ = bf16[1024,256]{1,0:T(8,128)(2,1)S(1)} collective-permute-done((bf16[1024,256]{1,0:T(8,128)(2,1)}, bf16[1024,256]{1,0:T(8,128)(2,1)S(1)}, u32[]{:S(2)}, u32[]{:S(2)}) %collective-permute-start.8) | collective-permute-done | bytes 524320 | tf_op jit(solution)/shard_map/ppermute | solution.py:411
  78.9 5.4 %shard_map.62 = (bf16[1024,256]{1,0:T(8,128)(2,1)}, f32[1024,256]{1,0:T(8,128)}, bf16[1024,256]{1,0:T(8,128)(2,1)}, s32[8,128]{1,0:T(8,128)S(1)}) custom-call(s32[4]{0:T(128)S(1)} %pad_add_fusion.ids, s32[8,128]{1,0:T(8,128)S(1)} %get-tuple-element.67.token, bf16[1024,1024]{1,0:T(8,128)(2,1)S(1)} %get-tuple-element.68.refs_0_, ...), custom_call_target="tpu_custom_call", output_to_operand_aliasing={{3}: (1, {})} | custom-call | flops 1 | bytes 1 | tf_op jit(solution)/shard_map/pallas_call | solution.py:93
  84.3 3.8 %shard_map.63 = (bf16[1024,128]{1,0:T(8,128)(2,1)}, bf16[8,256,128]{2,1,0:T(8,128)(2,1)}, s32[8,128]{1,0:T(8,128)S(1)}) custom-call(s32[4]{0:T(128)S(1)} %pad_add_fusion.ids, s32[8,128]{1,0:T(8,128)S(1)} %get-tuple-element.71.token, bf16[1024,1024]{1,0:T(8,128)(2,1)S(1)} %get-tuple-element.68.refs_0_, ...), custom_call_target="tpu_custom_call", output_to_operand_aliasing={{2}: (1, {})} | custom-call | flops 1 | bytes 1 | tf_op jit(solution)/shard_map/pallas_call | solution.py:93
  88.1 1.9 collective-permute-start.11
  90.1 3.6 %all-to-all-start.1 = ((bf16[8,128,128]{2,1,0:T(8,128)(2,1)}), bf16[8,128,128]{2,1,0:T(8,128)(2,1)S(1)}, u32[]{:S(2)}, u32[]{:S(2)}) async-start(bf16[8,128,128]{2,1,0:T(8,128)(2,1)} %bitcast.26), calls=%async_computation.1 | async-start | bytes 524288 | tf_op jit(solution)/shard_map/all_to_all | solution.py:66
  93.7 10.7 %collective-permute-done.11.refs_1_.refs_4_.refs_3_ = bf16[1024,256]{1,0:T(8,128)(2,1)S(1)} collective-permute-done((bf16[1024,256]{1,0:T(8,128)(2,1)S(1)}, bf16[1024,256]{1,0:T(8,128)(2,1)S(1)}, u32[]{:S(2)}, u32[]{:S(2)}) %collective-permute-start.11) | collective-permute-done | bytes 524320 | tf_op jit(solution)/shard_map/ppermute | solution.py:411
  104.4 2.8 %shard_map.64 = (bf16[1024,256]{1,0:T(8,128)(2,1)}, s32[8,128]{1,0:T(8,128)S(1)}) custom-call(s32[4]{0:T(128)S(1)} %pad_add_fusion.ids, s32[8,128]{1,0:T(8,128)S(1)} %get-tuple-element.74.token, bf16[1024,1024]{1,0:T(8,128)(2,1)S(1)} %get-tuple-element.68.refs_0_, ...), custom_call_target="tpu_custom_call", output_to_operand_aliasing={{1}: (1, {})} | custom-call | flops 1 | bytes 1 | tf_op jit(solution)/shard_map/pallas_call | solution.py:93
  107.2 3.0 %collective-permute-start.13 = (bf16[1024,256]{1,0:T(8,128)(2,1)}, bf16[1024,256]{1,0:T(8,128)(2,1)}, u32[]{:S(2)}, u32[]{:S(2)}) collective-permute-start(bf16[1024,256]{1,0:T(8,128)(2,1)} %get-tuple-element.84), channel_id=1, source_target_pairs={{16,8},{8,0},{17,9},{9,1},{18,10},{10,2},{19,11},{11,3},{20,12},{1... | collective-permute-start | bytes 1572872 | tf_op jit(solution)/shard_map/ppermute | solution.py:411
  110.2 5.2 %shard_map.65 = (bf16[1024,1024]{1,0:T(8,128)(2,1)}, bf16[1024,256]{1,0:T(8,128)(2,1)}, s32[8,128]{1,0:T(8,128)S(1)}) custom-call(s32[4]{0:T(128)S(1)} %pad_add_fusion.ids, s32[8,128]{1,0:T(8,128)S(1)} %get-tuple-element.77.token, bf16[1024,1024]{1,0:T(8,128)(2,1)S(1)} %get-tuple-element.68.refs_0_, ...), custom_call_target="tpu_custom_call", output_to_operand_aliasing={{2}: (1, {})} | custom-call | flops 1 | bytes 1 | tf_op jit(solution)/shard_map/pallas_call | solution.py:93
  115.4 2.1 %collective-permute-start.15 = (bf16[1024,256]{1,0:T(8,128)(2,1)}, bf16[1024,256]{1,0:T(8,128)(2,1)}, u32[]{:S(2)}, u32[]{:S(2)}) collective-permute-start(bf16[1024,256]{1,0:T(8,128)(2,1)} %get-tuple-element.88), channel_id=1, source_target_pairs={{16,0},{17,1},{18,2},{19,3},{20,4},{21,5},{22,6},{23,7}} | collective-permute-start | bytes 1572872 | tf_op jit(solution)/shard_map/ppermute | solution.py:464
  117.5 2.1 %collective-permute-start.14 = (bf16[1024,256]{1,0:T(8,128)(2,1)}, bf16[1024,256]{1,0:T(8,128)(2,1)}, u32[]{:S(2)}, u32[]{:S(2)}) collective-permute-start(bf16[1024,256]{1,0:T(8,128)(2,1)} %get-tuple-element.88), channel_id=1, source_target_pairs={{16,8},{17,9},{18,10},{19,11},{20,12},{21,13},{22,14},{23,15}} | collective-permute-start | bytes 1572872 | tf_op jit(solution)/shard_map/ppermute | solution.py:464
  119.6 3.5 %all-to-all-start.2 = ((bf16[8,256,128]{2,1,0:T(8,128)(2,1)}), bf16[8,256,128]{2,1,0:T(8,128)(2,1)S(1)}, u32[]{:S(2)}, u32[]{:S(2)}) async-start(bf16[8,256,128]{2,1,0:T(8,128)(2,1)} %get-tuple-element.90), calls=%async_computation.2 | async-start | bytes 1048576 | tf_op jit(solution)/shard_map/all_to_all | solution.py:66
  123.2 1.0 copy-done.1
  124.2 5.1 %shard_map.66 = (f32[1024,1024]{1,0:T(8,128)}, bf16[1024,256]{1,0:T(8,128)(2,1)}, s32[8,128]{1,0:T(8,128)S(1)}) custom-call(s32[4]{0:T(128)S(1)} %pad_add_fusion.ids, s32[8,128]{1,0:T(8,128)S(1)} %get-tuple-element.82.token, bf16[1024,1024]{1,0:T(8,128)(2,1)S(1)} %get-tuple-element.68.refs_0_, ...), custom_call_target="tpu_custom_call", output_to_operand_aliasing={{2}: (1, {})} | custom-call | flops 1 | bytes 1 | tf_op jit(solution)/shard_map/pallas_call | solution.py:93
  129.3 2.7 %shard_map.67 = (bf16[1024,256]{1,0:T(8,128)(2,1)}, s32[8,128]{1,0:T(8,128)S(1)}) custom-call(s32[4]{0:T(128)S(1)} %pad_add_fusion.ids, s32[8,128]{1,0:T(8,128)S(1)} %get-tuple-element.85.token, bf16[1024,1024]{1,0:T(8,128)(2,1)S(1)} %get-tuple-element.68.refs_0_, ...), custom_call_target="tpu_custom_call", output_to_operand_aliasing={{1}: (1, {})} | custom-call | flops 1 | bytes 1 | tf_op jit(solution)/shard_map/pallas_call | solution.py:93
  132.0 1.5 collective-permute-start.16
  133.5 9.9 %collective-permute-done.14.refs_3_ = bf16[1024,256]{1,0:T(8,128)(2,1)} collective-permute-done((bf16[1024,256]{1,0:T(8,128)(2,1)}, bf16[1024,256]{1,0:T(8,128)(2,1)}, u32[]{:S(2)}, u32[]{:S(2)}) %collective-permute-start.14) | collective-permute-done | bytes 524320 | tf_op jit(solution)/shard_map/ppermute | solution.py:464
  143.4 5.5 %shard_map.68 = (bf16[8,256,256]{2,1,0:T(8,128)(2,1)}, s32[8,128]{1,0:T(8,128)S(1)}) custom-call(s32[4]{0:T(128)S(1)} %pad_add_fusion.ids, s32[8,128]{1,0:T(8,128)S(1)} %get-tuple-element.86.token, bf16[1024,1024]{1,0:T(8,128)(2,1)S(1)} %get-tuple-element.68.refs_0_, bf16[1024,1024]{1,0:T(8,128)(2,1)} %get-tuple-element.72.refs_1_, ...), custom_call_target="tpu_custom_call", output_to_operand_aliasing={{1}: (1, {})} | custom-call | flops 1 | bytes 1 | tf_op jit(solution)/shard_map/pallas_call | solution.py:93
  148.9 4.2 %all-to-all-start.3 = ((bf16[8,256,256]{2,1,0:T(8,128)(2,1)}), bf16[8,256,256]{2,1,0:T(8,128)(2,1)}, u32[]{:S(2)}, u32[]{:S(2)}) async-start(bf16[8,256,256]{2,1,0:T(8,128)(2,1)} %get-tuple-element.100), calls=%async_computation.3 | async-start | bytes 2097152 | tf_op jit(solution)/shard_map/all_to_all | solution.py:66
  153.2 1.9 collective-permute-start.17
  155.1 5.1 %shard_map.69 = (f32[1024,1024]{1,0:T(8,128)}, bf16[1024,256]{1,0:T(8,128)(2,1)}, s32[8,128]{1,0:T(8,128)S(1)}) custom-call(s32[4]{0:T(128)S(1)} %pad_add_fusion.ids, s32[8,128]{1,0:T(8,128)S(1)} %get-tuple-element.91.token, bf16[1024,1024]{1,0:T(8,128)(2,1)S(1)} %get-tuple-element.68.refs_0_, ...), custom_call_target="tpu_custom_call", output_to_operand_aliasing={{2}: (1, {}), {0}: (9, {})} | custom-call | flops 1 | bytes 1 | tf_op jit(solution)/shard_map/pallas_call | solution.py:93
  161.0 18.2 %collective-permute-done.17.refs_0_ = bf16[1024,256]{1,0:T(8,128)(2,1)S(1)} collective-permute-done((bf16[1024,256]{1,0:T(8,128)(2,1)}, bf16[1024,256]{1,0:T(8,128)(2,1)S(1)}, u32[]{:S(2)}, u32[]{:S(2)}) %collective-permute-start.17) | collective-permute-done | bytes 524320 | tf_op jit(solution)/shard_map/ppermute | solution.py:51
  179.3 2.8 %shard_map.70 = (f32[1024,1024]{1,0:T(8,128)}, s32[8,128]{1,0:T(8,128)S(1)}) custom-call(s32[4]{0:T(128)S(1)} %pad_add_fusion.ids, s32[8,128]{1,0:T(8,128)S(1)} %get-tuple-element.95.token, bf16[1024,256]{1,0:T(8,128)(2,1)S(1)} %collective-permute-done.17.refs_0_, f32[1024,1024]{1,0:T(8,128)} %bitcast.23, ...), custom_call_target="tpu_custom_call", output_to_operand_aliasing={{1}: (1, {}), {0}: (4, {})} | custom-call | flops 1 | bytes 1 | tf_op jit(solution)/shard_map/pallas_call | solution.py:93
  182.1 6.9 %shard_map.71 = (f32[256,1024]{1,0:T(8,128)}, f32[256,1024]{1,0:T(8,128)}, s32[8,128]{1,0:T(8,128)S(1)}) custom-call(s32[4]{0:T(128)S(1)} %pad_add_fusion.ids, s32[8,128]{1,0:T(8,128)S(1)} %get-tuple-element.98.token, bf16[1024,1024]{1,0:T(8,128)(2,1)S(1)} %get-tuple-element.68.refs_0_, ...), custom_call_target="tpu_custom_call", output_to_operand_aliasing={{2}: (1, {})} | custom-call | flops 1 | bytes 1 | tf_op jit(solution)/shard_map/pallas_call | solution.py:93
  189.0 1.0 collective-permute-done.18.refs_0_
  190.0 2.9 %shard_map.72 = (f32[1024,1024]{1,0:T(8,128)}, s32[8,128]{1,0:T(8,128)S(1)}) custom-call(s32[4]{0:T(128)S(1)} %pad_add_fusion.ids, s32[8,128]{1,0:T(8,128)S(1)} %get-tuple-element.103.token, bf16[1024,256]{1,0:T(8,128)(2,1)S(1)} %collective-permute-done.18.refs_0_, f32[1024,1024]{1,0:T(8,128)} %bitcast.24, ...), custom_call_target="tpu_custom_call", output_to_operand_aliasing={{1}: (1, {}), {0}: (4, {})} | custom-call | flops 1 | bytes 1 | tf_op jit(solution)/shard_map/pallas_call | solution.py:93
  (31 shorter events, 2.8 us)
Async XLA Ops:
  1.9 13.7 %collective-permute-start = (bf16[256,1024]{1,0:T(8,128)(2,1)S(1)}, bf16[256,1024]{1,0:T(8,128)(2,1)S(1)}, u32[]{:S(2)}, u32[]{:S(2)}) collective-permute-start(bf16[256,1024]{1,0:T(8,128)(2,1)S(1)} %convert_bitcast_fusion), channel_id=1, source_target_pairs={{0,4},{4,0},{1,5},{5,1},{2,6},{6,2},{3,7},{7,3},{8,12},{12,8},{9,1... | collective-permute-start | bytes 1572872 | tf_op jit(solution)/shard_map/ppermute | solution.py:51
  3.5 13.4 %collective-permute-start.1 = (bf16[256,1024]{1,0:T(8,128)(2,1)S(1)}, bf16[256,1024]{1,0:T(8,128)(2,1)S(1)}, u32[]{:S(2)}, u32[]{:S(2)}) collective-permute-start(bf16[256,1024]{1,0:T(8,128)(2,1)S(1)} %convert_bitcast_fusion), channel_id=1, source_target_pairs={{0,2},{2,0},{1,3},{3,1},{4,6},{6,4},{5,7},{7,5},{8,10},{10,8},{9,1... | collective-permute-start | bytes 1572872 | tf_op jit(solution)/shard_map/ppermute | solution.py:51
  17.0 16.5 %copy-start.2 = (bf16[768,1024]{1,0:T(8,128)(2,1)}, bf16[768,1024]{1,0:T(8,128)(2,1)S(1)}, u32[]{:S(2)}) copy-start(bf16[768,1024]{1,0:T(8,128)(2,1)S(1)} %pad_maximum_fusion.refs_0_) | copy-start | bytes 4718596
  17.0 16.5 %collective-permute-start.4 = (bf16[768,1024]{1,0:T(8,128)(2,1)S(1)}, bf16[768,1024]{1,0:T(8,128)(2,1)}, u32[]{:S(2)}, u32[]{:S(2)}) collective-permute-start(bf16[768,1024]{1,0:T(8,128)(2,1)S(1)} %pad_maximum_fusion.refs_0_), channel_id=1, source_target_pairs={{0,1},{1,0},{2,3},{3,2},{4,5},{5,4},{6,7},{7,6},{8,9},{9,8},{10,11... | collective-permute-start | bytes 4718600 | tf_op jit(solution)/shard_map/ppermute | solution.py:51
  17.1 14.3 %collective-permute-start.3 = (bf16[256,1024]{1,0:T(8,128)(2,1)S(1)}, bf16[256,1024]{1,0:T(8,128)(2,1)S(1)}, u32[]{:S(2)}, u32[]{:S(2)}) collective-permute-start(bf16[256,1024]{1,0:T(8,128)(2,1)S(1)} %collective-permute-done), channel_id=1, source_target_pairs={{0,2},{2,0},{1,3},{3,1},{4,6},{6,4},{5,7},{7,5},{8,10},{10,8},{9,1... | collective-permute-start | bytes 1572872 | tf_op jit(solution)/shard_map/ppermute | solution.py:51
  18.7 8.4 %collective-permute-start.2 = (bf16[128,1024]{1,0:T(8,128)(2,1)S(1)}, bf16[128,1024]{1,0:T(8,128)(2,1)S(1)}, u32[]{:S(2)}, u32[]{:S(2)}) collective-permute-start(bf16[128,1024]{1,0:T(8,128)(2,1)S(1)} %dynamic-slice_bitcast_fusion), channel_id=1, source_target_pairs={{0,4},{4,0},{1,5},{5,1},{2,6},{6,2},{3,7},{7,3},{8,12},{12,8},{9,1... | collective-permute-start | bytes 786440 | tf_op jit(solution)/shard_map/ppermute | solution.py:51
  31.4 2.1 %copy-start.3 = (bf16[256,1024]{1,0:T(8,128)(2,1)}, bf16[256,1024]{1,0:T(8,128)(2,1)S(1)}, u32[]{:S(2)}) copy-start(bf16[256,1024]{1,0:T(8,128)(2,1)S(1)} %collective-permute-done.3.refs_1_) | copy-start | bytes 1572868
  31.4 2.0 %collective-permute-start.5 = (bf16[256,1024]{1,0:T(8,128)(2,1)S(1)}, bf16[256,1024]{1,0:T(8,128)(2,1)}, u32[]{:S(2)}, u32[]{:S(2)}) collective-permute-start(bf16[256,1024]{1,0:T(8,128)(2,1)S(1)} %collective-permute-done.3.refs_1_), channel_id=1, source_target_pairs={{0,1},{1,0},{2,3},{3,2},{4,5},{5,4},{6,7},{7,6},{8,9},{9,8},{10,11... | collective-permute-start | bytes 1572872 | tf_op jit(solution)/shard_map/ppermute | solution.py:51
  31.4 14.5 %collective-permute-start.6 = (bf16[1024,256]{1,0:T(8,128)(2,1)}, bf16[1024,256]{1,0:T(8,128)(2,1)S(1)}, u32[]{:S(2)}, u32[]{:S(2)}) collective-permute-start(bf16[1024,256]{1,0:T(8,128)(2,1)} %get-tuple-element.60), channel_id=1, source_target_pairs={{0,4},{4,0},{1,5},{5,1},{2,6},{6,2},{3,7},{7,3},{8,12},{12,8},{9,1... | collective-permute-start | bytes 1572872 | tf_op jit(solution)/shard_map/ppermute | solution.py:51
  39.6 39.3 %collective-permute-start.9 = (bf16[512,1024]{1,0:T(8,128)(2,1)}, bf16[512,1024]{1,0:T(8,128)(2,1)}, u32[]{:S(2)}, u32[]{:S(2)}) collective-permute-start(bf16[512,1024]{1,0:T(8,128)(2,1)} %get-tuple-element.70), channel_id=1, source_target_pairs={{24,16},{8,0},{25,17},{9,1},{26,18},{10,2},{27,19},{11,3},{28,20},... | collective-permute-start | bytes 3145736 | tf_op jit(solution)/shard_map/ppermute | solution.py:434
  46.0 14.7 %collective-permute-start.7 = (bf16[1024,256]{1,0:T(8,128)(2,1)}, bf16[1024,256]{1,0:T(8,128)(2,1)S(1)}, u32[]{:S(2)}, u32[]{:S(2)}) collective-permute-start(bf16[1024,256]{1,0:T(8,128)(2,1)} %get-tuple-element.66), channel_id=1, source_target_pairs={{0,4},{4,0},{1,5},{5,1},{2,6},{6,2},{3,7},{7,3},{8,12},{12,8},{9,1... | collective-permute-start | bytes 1572872 | tf_op jit(solution)/shard_map/ppermute | solution.py:51
  55.1 13.7 %all-to-all-start = ((bf16[8,256,128]{2,1,0:T(8,128)(2,1)}), bf16[8,256,128]{2,1,0:T(8,128)(2,1)}, u32[]{:S(2)}, u32[]{:S(2)}) async-start(bf16[8,256,128]{2,1,0:T(8,128)(2,1)} %get-tuple-element.65), calls=%async_computation | async-start | bytes 1048576 | tf_op jit(solution)/shard_map/all_to_all | solution.py:66
  59.4 19.5 %collective-permute-start.8 = (bf16[1024,256]{1,0:T(8,128)(2,1)}, bf16[1024,256]{1,0:T(8,128)(2,1)S(1)}, u32[]{:S(2)}, u32[]{:S(2)}) collective-permute-start(bf16[1024,256]{1,0:T(8,128)(2,1)} %get-tuple-element.69.refs_2_), channel_id=1, source_target_pairs={{24,16},{25,17},{26,18},{27,19},{28,20},{29,21},{30,22},{31,23}} | collective-permute-start | bytes 1572872 | tf_op jit(solution)/shard_map/ppermute | solution.py:411
  73.0 11.3 %collective-permute-start.10 = (bf16[1024,128]{1,0:T(8,128)(2,1)}, bf16[1024,128]{1,0:T(8,128)(2,1)S(1)}, u32[]{:S(2)}, u32[]{:S(2)}) collective-permute-start(bf16[1024,128]{1,0:T(8,128)(2,1)} %get-tuple-element.73), channel_id=1, source_target_pairs={{24,16},{8,0},{25,17},{9,1},{26,18},{10,2},{27,19},{11,3},{28,20},... | collective-permute-start | bytes 786440 | tf_op jit(solution)/shard_map/ppermute | solution.py:444
  78.9 5.4 %copy-start = (bf16[1024,256]{1,0:T(8,128)(2,1)}, bf16[1024,256]{1,0:T(8,128)(2,1)S(1)}, u32[]{:S(2)}) copy-start(bf16[1024,256]{1,0:T(8,128)(2,1)S(1)} %collective-permute-done.8.refs_1_.refs_3_) | copy-start | bytes 1572868
  84.3 3.9 %copy-start.4 = (bf16[1024,256]{1,0:T(8,128)(2,1)S(1)}, bf16[1024,256]{1,0:T(8,128)(2,1)}, u32[]{:S(2)}) copy-start(bf16[1024,256]{1,0:T(8,128)(2,1)} %get-tuple-element.75) | copy-start | bytes 1572868
  88.1 22.1 %collective-permute-start.12 = (bf16[512,1024]{1,0:T(8,128)(2,1)}, bf16[512,1024]{1,0:T(8,128)(2,1)}, u32[]{:S(2)}, u32[]{:S(2)}) collective-permute-start(bf16[512,1024]{1,0:T(8,128)(2,1)} %collective-permute-done.9.refs_6_.refs_3_), channel_id=1, source_target_pairs={{0,1},{1,0},{2,3},{3,2},{4,5},{5,4},{6,7},{7,6},{8,9},{9,8},{10,11... | collective-permute-start | bytes 3145736 | tf_op jit(solution)/shard_map/ppermute | solution.py:51
  88.1 16.2 %collective-permute-start.11 = (bf16[1024,256]{1,0:T(8,128)(2,1)S(1)}, bf16[1024,256]{1,0:T(8,128)(2,1)S(1)}, u32[]{:S(2)}, u32[]{:S(2)}) collective-permute-start(bf16[1024,256]{1,0:T(8,128)(2,1)S(1)} %copy-done.4), channel_id=1, source_target_pairs={{24,16},{16,8},{25,17},{17,9},{26,18},{18,10},{27,19},{19,11},{28,... | collective-permute-start | bytes 1572872 | tf_op jit(solution)/shard_map/ppermute | solution.py:411
  90.1 20.1 %all-to-all-start.1 = ((bf16[8,128,128]{2,1,0:T(8,128)(2,1)}), bf16[8,128,128]{2,1,0:T(8,128)(2,1)S(1)}, u32[]{:S(2)}, u32[]{:S(2)}) async-start(bf16[8,128,128]{2,1,0:T(8,128)(2,1)} %bitcast.26), calls=%async_computation.1 | async-start | bytes 524288 | tf_op jit(solution)/shard_map/all_to_all | solution.py:66
  107.2 16.0 %collective-permute-start.13 = (bf16[1024,256]{1,0:T(8,128)(2,1)}, bf16[1024,256]{1,0:T(8,128)(2,1)}, u32[]{:S(2)}, u32[]{:S(2)}) collective-permute-start(bf16[1024,256]{1,0:T(8,128)(2,1)} %get-tuple-element.84), channel_id=1, source_target_pairs={{16,8},{8,0},{17,9},{9,1},{18,10},{10,2},{19,11},{11,3},{20,12},{1... | collective-permute-start | bytes 1572872 | tf_op jit(solution)/shard_map/ppermute | solution.py:411
  115.4 18.1 %collective-permute-start.15 = (bf16[1024,256]{1,0:T(8,128)(2,1)}, bf16[1024,256]{1,0:T(8,128)(2,1)}, u32[]{:S(2)}, u32[]{:S(2)}) collective-permute-start(bf16[1024,256]{1,0:T(8,128)(2,1)} %get-tuple-element.88), channel_id=1, source_target_pairs={{16,0},{17,1},{18,2},{19,3},{20,4},{21,5},{22,6},{23,7}} | collective-permute-start | bytes 1572872 | tf_op jit(solution)/shard_map/ppermute | solution.py:464
  117.5 25.8 %collective-permute-start.14 = (bf16[1024,256]{1,0:T(8,128)(2,1)}, bf16[1024,256]{1,0:T(8,128)(2,1)}, u32[]{:S(2)}, u32[]{:S(2)}) collective-permute-start(bf16[1024,256]{1,0:T(8,128)(2,1)} %get-tuple-element.88), channel_id=1, source_target_pairs={{16,8},{17,9},{18,10},{19,11},{20,12},{21,13},{22,14},{23,15}} | collective-permute-start | bytes 1572872 | tf_op jit(solution)/shard_map/ppermute | solution.py:464
  119.6 13.9 %all-to-all-start.2 = ((bf16[8,256,128]{2,1,0:T(8,128)(2,1)}), bf16[8,256,128]{2,1,0:T(8,128)(2,1)S(1)}, u32[]{:S(2)}, u32[]{:S(2)}) async-start(bf16[8,256,128]{2,1,0:T(8,128)(2,1)} %get-tuple-element.90), calls=%async_computation.2 | async-start | bytes 1048576 | tf_op jit(solution)/shard_map/all_to_all | solution.py:66
  123.1 1.0 copy-start.1
  132.0 23.1 %collective-permute-start.16 = (bf16[1024,256]{1,0:T(8,128)(2,1)}, bf16[1024,256]{1,0:T(8,128)(2,1)}, u32[]{:S(2)}, u32[]{:S(2)}) collective-permute-start(bf16[1024,256]{1,0:T(8,128)(2,1)} %get-tuple-element.93), channel_id=1, source_target_pairs={{8,0},{9,1},{10,2},{11,3},{12,4},{13,5},{14,6},{15,7}} | collective-permute-start | bytes 1572872 | tf_op jit(solution)/shard_map/ppermute | solution.py:411
  148.9 33.2 %all-to-all-start.3 = ((bf16[8,256,256]{2,1,0:T(8,128)(2,1)}), bf16[8,256,256]{2,1,0:T(8,128)(2,1)}, u32[]{:S(2)}, u32[]{:S(2)}) async-start(bf16[8,256,256]{2,1,0:T(8,128)(2,1)} %get-tuple-element.100), calls=%async_computation.3 | async-start | bytes 2097152 | tf_op jit(solution)/shard_map/all_to_all | solution.py:66
  153.2 26.1 %collective-permute-start.17 = (bf16[1024,256]{1,0:T(8,128)(2,1)}, bf16[1024,256]{1,0:T(8,128)(2,1)S(1)}, u32[]{:S(2)}, u32[]{:S(2)}) collective-permute-start(bf16[1024,256]{1,0:T(8,128)(2,1)} %get-tuple-element.96), channel_id=1, source_target_pairs={{0,4},{4,0},{1,5},{5,1},{2,6},{6,2},{3,7},{7,3},{8,12},{12,8},{9,1... | collective-permute-start | bytes 1572872 | tf_op jit(solution)/shard_map/ppermute | solution.py:51
  160.2 29.9 %collective-permute-start.18 = (bf16[1024,256]{1,0:T(8,128)(2,1)}, bf16[1024,256]{1,0:T(8,128)(2,1)S(1)}, u32[]{:S(2)}, u32[]{:S(2)}) collective-permute-start(bf16[1024,256]{1,0:T(8,128)(2,1)} %get-tuple-element.104), channel_id=1, source_target_pairs={{0,4},{4,0},{1,5},{5,1},{2,6},{6,2},{3,7},{7,3},{8,12},{12,8},{9,1... | collective-permute-start | bytes 1572872 | tf_op jit(solution)/shard_map/ppermute | solution.py:51
